TPU v7x, 32 devices: a whole 2x2x4 slice. The times are simulated.
32 devices in a mesh: ctx: 16 (over z, y, x), head: 2 (over core).
Axes of the slice: x: 2, y: 2, z: 4, core: 2. Of those that a mesh axis runs over, the one named last changes fastest.
Arguments:
- inputs: bfloat16 [8192, 4096], P('ctx', 'head'), may hold values from -6 to 6
- w_in: bfloat16 [4096, 4096], P('ctx', 'head'), may hold values from -0.09375 to 0.09375
- b_rows: bfloat16 [8192, 128], P('ctx'), may hold values from -0.5 to 0.5
- c_rows: bfloat16 [8192, 128], P('ctx'), may hold values from -0.5 to 0.5
- log_decay: float32 [64, 8192], P('head', 'ctx'), may hold values from -2.09375 to 0, as said below
- skip_gain: float32 [64], P('head'), may hold values from 0.5 to 2
- grad_out: bfloat16 [8192, 4096], P('ctx', 'head'), may hold values from -6 to 6
Outputs:
- grad_inputs: bfloat16 [8192, 4096], P('ctx', 'head')
- grad_b: float32 [8192, 128], P('ctx')
- grad_c: float32 [8192, 128], P('ctx')
- grad_log_decay: float32 [64, 8192], P('head', 'ctx')
Inputs may be any that keep to these rules, and one draw needn't show every extreme that they name: log_decay is negative.
All inputs are finite; a program needn't handle non-finite values.
Results may differ from a plain program's by a relative error of at most 0.017.
Values may be sent and summed in bfloat16 or wider, within the bound.
No kernel may reach another device: no remote copies, remote signals or barrier semaphores. Data moves between devices by JAX's collectives and lax.ppermute only.
A program may use at most 128 MiB of HBM per device.

v0:
```python
import jax
import jax.numpy as jnp
from jax import lax
from jax.sharding import PartitionSpec as P

SPAN = 256
SPANS_DEV = 2


exact_precision = lax.Precision.HIGHEST


def entering(part, axis, combine, identity, reverse):
    count = lax.axis_size(axis)
    place = lax.axis_index(axis)
    ahead = count - 1 - place if reverse else place
    gathered = jax.tree.map(lambda a: lax.all_gather(a, axis), part)
    state = jax.tree.map(lambda a, e: jnp.zeros_like(a) + jnp.asarray(e, a.dtype), part, identity)

    def one(lap, state):
        source = count - 1 - lap if reverse else lap
        return combine(
            state, jax.tree.map(lambda a: lax.dynamic_index_in_dim(a, source, 0, False), gathered)
        )

    return lax.fori_loop(0, ahead, one, state)


def span_state(x_rows, b_rows, log_decay):
    length = x_rows.shape[0]
    heads = log_decay.shape[0]
    x_heads = x_rows.reshape(length, heads, -1)
    running = jnp.cumsum(log_decay, axis=1)
    to_end = jnp.exp(running[:, -1:] - running)
    own_state = jnp.einsum(
        "shp,sn->hpn", x_heads * to_end.T[:, :, None], b_rows, precision=exact_precision
    )
    return (jnp.exp(running[:, -1]), own_state)


def span_forward(x_rows, b_rows, c_rows, log_decay, state_in, skip_gain):
    length = x_rows.shape[0]
    heads = log_decay.shape[0]
    x_heads = x_rows.reshape(length, heads, -1)
    running = jnp.cumsum(log_decay, axis=1)
    later = lax.broadcasted_iota(jnp.int32, (length, length), 0)
    earlier = lax.broadcasted_iota(jnp.int32, (length, length), 1)
    causal = (later >= earlier)[None]
    spread = running[:, :, None] - running[:, None, :]
    kernel = jnp.where(causal, jnp.exp(jnp.where(causal, spread, 0.0)), 0.0)
    scores = jnp.dot(c_rows, b_rows.T, precision=exact_precision)
    inner = jnp.einsum("hts,shp->thp", kernel * scores[None], x_heads, precision=exact_precision)
    from_state = jnp.einsum("tn,hpn->thp", c_rows, state_in, precision=exact_precision)
    from_state = from_state * jnp.exp(running).T[:, :, None]
    outputs = inner + from_state + skip_gain[None, :, None] * x_heads
    retained, own_state = span_state(x_rows, b_rows, log_decay)
    state_out = retained[:, None, None] * state_in + own_state
    return (outputs.reshape(length, -1), state_out)


def boundary_grad(c_rows, log_decay, g_rows):
    length = g_rows.shape[0]
    heads = log_decay.shape[0]
    g_heads = g_rows.reshape(length, heads, -1)
    running = jnp.cumsum(log_decay, axis=1)
    return jnp.einsum(
        "thp,tn->hpn", g_heads * jnp.exp(running).T[:, :, None], c_rows, precision=exact_precision
    )


def combine_states(earlier, later):
    return (earlier[0] * later[0], later[0][:, None, None] * earlier[1] + later[1])


def local(inputs, w_in, b_rows, c_rows, log_decay, skip_gain, grad_out):
    weight = lax.all_gather(w_in, "ctx", axis=0, tiled=True)
    x_summed = jnp.dot(
        lax.all_gather(inputs, "head", axis=1, tiled=True),
        weight,
        preferred_element_type=jnp.float32,
    )
    x_rows = x_summed.astype(jnp.bfloat16)
    x_float = lax.optimization_barrier(x_rows).astype(jnp.float32)
    b_float = b_rows.astype(jnp.float32)
    c_float = c_rows.astype(jnp.float32)
    g_float = grad_out.astype(jnp.float32)
    heads = log_decay.shape[0]
    x_parts = [x_float[index * SPAN : (index + 1) * SPAN] for index in range(SPANS_DEV)]
    b_parts = [b_float[index * SPAN : (index + 1) * SPAN] for index in range(SPANS_DEV)]
    c_parts = [c_float[index * SPAN : (index + 1) * SPAN] for index in range(SPANS_DEV)]
    g_parts = [g_float[index * SPAN : (index + 1) * SPAN] for index in range(SPANS_DEV)]
    d_parts = [log_decay[:, index * SPAN : (index + 1) * SPAN] for index in range(SPANS_DEV)]
    span_states = [
        span_state(x_parts[index], b_parts[index], d_parts[index]) for index in range(SPANS_DEV)
    ]
    span_grads = [
        boundary_grad(c_parts[index], d_parts[index], g_parts[index]) for index in range(SPANS_DEV)
    ]
    forward_total = span_states[0]
    index = 1
    forward_total = combine_states(forward_total, span_states[index])
    backward_total = (span_states[SPANS_DEV - 1][0], span_grads[SPANS_DEV - 1])
    index = 0
    backward_total = combine_states(backward_total, (span_states[index][0], span_grads[index]))
    identity = (jnp.ones((heads,), jnp.float32), jnp.zeros(forward_total[1].shape, jnp.float32))
    device_state_in = entering(forward_total, "ctx", combine_states, identity, False)[1]
    device_grad_out = entering(backward_total, "ctx", combine_states, identity, True)[1]
    states_in = [device_state_in]
    index = 1
    previous = span_states[index - 1]
    states_in.append(previous[0][:, None, None] * states_in[index - 1] + previous[1])
    grads_out = [device_grad_out]
    index = 1
    grads_out.insert(0, span_grads[index] + span_states[index][0][:, None, None] * grads_out[0])
    grad_x_list = []
    grad_b_list = []
    grad_c_list = []
    grad_d_list = []
    for index in range(SPANS_DEV):
        state_here = states_in[index]

        def local_forward(x_value, b_value, c_value, d_value):
            return span_forward(x_value, b_value, c_value, d_value, state_here, skip_gain)

        _, pullback = jax.vjp(
            local_forward, x_parts[index], b_parts[index], c_parts[index], d_parts[index]
        )
        grad_x_part, grad_b_part, grad_c_part, grad_d_part = pullback(
            (g_parts[index], grads_out[index])
        )
        grad_x_list.append(grad_x_part)
        grad_b_list.append(grad_b_part)
        grad_c_list.append(grad_c_part)
        grad_d_list.append(grad_d_part)
    grad_x = jnp.concatenate(grad_x_list, axis=0)
    grad_b_local = jnp.concatenate(grad_b_list, axis=0)
    grad_c_local = jnp.concatenate(grad_c_list, axis=0)
    grad_log_decay = jnp.concatenate(grad_d_list, axis=1)
    grad_b, grad_c = (
        lax.psum(grad_b_local.astype(jnp.bfloat16), "head").astype(jnp.float32),
        lax.psum(grad_c_local.astype(jnp.bfloat16), "head").astype(jnp.float32),
    )
    grad_x_rows = grad_x.astype(jnp.bfloat16)
    partial_grads = lax.dot_general(
        grad_x_rows, weight, (((1,), (1,)), ((), ())), preferred_element_type=jnp.float32
    )
    grad_inputs = lax.psum_scatter(
        partial_grads.astype(jnp.bfloat16), "head", scatter_dimension=1, tiled=True
    )
    return (grad_inputs, grad_b, grad_c, grad_log_decay)


def solution(mesh):
    in_specs = (
        P("ctx", "head"),
        P("ctx", "head"),
        P("ctx", None),
        P("ctx", None),
        P("head", "ctx"),
        P("head"),
        P("ctx", "head"),
    )
    out_specs = (P("ctx", "head"), P("ctx", None), P("ctx", None), P("head", "ctx"))
    return jax.shard_map(local, mesh=mesh, in_specs=in_specs, out_specs=out_specs, check_vma=False)
```

profile of v0, /device:TPU:0, one launch (start us, length us, event | category | flops | bytes accessed | tf_op | source)
XLA Modules:
  0.0 738.2 jit_solution(16392328344785315927)
XLA Ops:
  10.5 4.1 fusion.137
  14.6 1.9 copy.89
  16.6 3.7 copy.94
  20.2 1.1 fusion.55
  21.8 2.1 fusion.61
  27.0 44.3 %all-reduce.4 = f32[512]{0:T(512)S(1)} all-reduce(f32[512]{0:T(512)S(1)} %dynamic-update-slice), channel_id=2, replica_groups=mesh['ctx'=16,'head'=2] {'ctx'}, use_global_device_ids=true, to_apply=%add.4 | all-reduce | flops 512 | bytes 4096
  71.4 147.5 %all-gather.12.cloned.1.call-done = f32[512,64,128]{2,1,0:T(8,128)} async-done(((f32[32,64,128]{2,1,0:T(8,128)}), f32[512,64,128]{2,1,0:T(8,128)}) %all-gather.12.cloned.1.call-update) | async-done | bytes 16777232 | tf_op jit(solution)/shard_map/all_gather | solution.py:17
  219.1 23.3 %while.26 = (s32[]{:T(128)}, f32[32,64,128]{2,1,0:T(8,128)S(1)}, s32[]{:T(128)}, f32[16,32]{1,0:T(8,128)S(1)}, f32[16,32,64,128]{3,2,1,0:T(8,128)}, /*index=5*/s32[]{:T(128)}, s32[]{:T(128)}, s32[]{:T(128)}, s32[]{:T(128)}) while((s32[]{:T(128)}, f32[32,64,128]{2,1,0:T(8,128)S(1)}, s32[]{:T(128)}, f32[16,32]{1,0:T(8,128)S(1)}, ...), condition=%wide.region_5.6_spmd, body=%wide.region_4.5_spmd.sunk | while | flops 524294 | bytes 3146259 | solution.py:26
  219.1 1.4 bitcast_add_fusion.6
  220.6 1.4 bitcast_add_fusion.6
  222.1 1.4 bitcast_add_fusion.6
  223.6 1.6 bitcast_add_fusion.6
  225.2 1.6 bitcast_add_fusion.6
  226.9 1.6 bitcast_add_fusion.6
  228.5 1.6 bitcast_add_fusion.6
  230.2 1.4 bitcast_add_fusion.6
  231.7 1.4 bitcast_add_fusion.6
  233.2 1.4 bitcast_add_fusion.6
  234.7 1.4 bitcast_add_fusion.6
  236.2 1.5 bitcast_add_fusion.6
  237.7 1.5 bitcast_add_fusion.6
  239.2 1.4 bitcast_add_fusion.6
  240.7 1.4 bitcast_add_fusion.6
  242.3 185.6 %all-gather.8.cloned.1.call-done = bf16[4096,2048]{1,0:T(8,128)(2,1)} async-done(((bf16[256,2048]{1,0:T(8,128)(2,1)}), bf16[4096,2048]{1,0:T(8,128)(2,1)}) %all-gather.8.cloned.1.call-update) | async-done | bytes 16777232 | tf_op jit(solution)/shard_map/all_gather | solution.py:76
  428.0 13.6 %convolution_convert_fusion.1 = bf16[512,2048]{1,0:T(8,128)(2,1)S(1)} fusion(bf16[512,4096]{1,0:T(8,128)(2,1)} %all-gather.10.cloned.1.call-done, bf16[4096,2048]{1,0:T(8,128)(2,1)} %all-gather.8.cloned.1.call-done), kind=kOutput, calls=%fused_computation.39 | convolution fusion | flops 8590983168 | bytes 23068672 | tf_op jit(solution)/shard_map/dot_general | solution.py:77
  441.6 2.7 fusion.136
  444.3 3.0 copy.103
  447.3 4.0 fusion.37
  451.9 2.9 copy.101
  454.9 2.8 fusion.45
  457.8 1.0 copy-done.8
  458.7 2.2 fusion.64
  461.2 3.2 fusion.135
  464.3 1.5 copy.99
  465.8 2.3 copy.96
  468.8 0.9 fusion.103
  469.7 0.9 fusion.108
  470.6 3.1 fusion.134
  473.7 2.3 copy.104
  476.0 2.3 copy.102
  478.2 5.1 fusion.76
  483.4 1.3 fusion.138
  485.0 10.7 %fusion.17 = (f32[32,256]{1,0:T(8,128)}, f32[32,256]{1,0:T(8,128)}, f32[256,256]{0,1:T(8,128)}, f32[256,256]{0,1:T(8,128)S(1)}, f32[32,256]{1,0:T(8,128)}, /*index=5*/f32[32,256]{1,0:T(8,128)}) fusion(f32[256,256]{0,1:T(8,128)S(1)} %copy-done.26, f32[32,256]{1,0:T(8,128)S(1)} %copy-done.34, pred[256,256]{0,1:T(8,128)(4,1)S(1)} %copy-done.37, ...), kind=kOutput, calls=%fused_computation.26 | convolution fusion | flops 314408960 | bytes 11796480 | tf_op jit(solution)/shard_map/transpose(jvp(hts,shp->thp))/dot_general | solution.py:52
  496.4 0.9 fusion.80
  497.3 7.7 %fusion.36 = bf16[256,32,64]{0,2,1:T(8,128)(2,1)} fusion(f32[32,64,256]{2,1,0:T(8,128)S(1)} %copy-done.12, f32[256,32,64]{0,2,1:T(8,128)S(1)} %bitcast.267, bf16[32,64,256]{2,1,0:T(8,128)(2,1)S(1)} %bitcast.279, f32[256,256]{0,1:T(8,128)S(1)} %copy-done.28, f32[32,256]{1,0:T(8,128)S(1)} %copy-done.31, pred[256,256]{0,1:T(8,128)(4,1)S(1)} %copy-done.37, ...), kind=kOutput, calls=%fused_computation.49 | convolution fusion | flops 1621622784 | bytes 6684800 | tf_op jit(solution)/shard_map/transpose(jvp(hts,shp->thp))/dot_general | solution.py:52
  505.0 145.8 %all-gather.14.cloned.1.call-done = f32[512,64,128]{2,1,0:T(8,128)} async-done(((f32[32,64,128]{2,1,0:T(8,128)}), f32[512,64,128]{2,1,0:T(8,128)}) %all-gather.14.cloned.1.call-update) | async-done | bytes 16777232 | tf_op jit(solution)/shard_map/all_gather | solution.py:17
  651.7 2.8 multiply_reduce_fusion
  654.4 3.4 fusion.70
  657.9 1.1 fusion.40
  659.0 3.5 fusion.73
  662.6 3.4 fusion.67
  667.2 7.8 %fusion.39 = bf16[256,32,64]{0,2,1:T(8,128)(2,1)} fusion(f32[32,64,256]{2,1,0:T(8,128)S(1)} %get-tuple-element.195, f32[256,32,64]{0,2,1:T(8,128)S(1)} %bitcast.273, bf16[32,64,256]{2,1,0:T(8,128)(2,1)S(1)} %bitcast.284, f32[256,256]{0,1:T(8,128)S(1)} %copy-done.27, f32[32,256]{1,0:T(8,128)S(1)} %copy-done.35, pred[256,256]{0,1:T(8,128)(4,1)S(1)} %copy-done.38, ...), kind=kOutput, calls=%fused_computation.55 | convolution fusion | flops 1621622784 | bytes 6684800 | tf_op jit(solution)/shard_map/transpose(jvp(hts,shp->thp))/dot_general | solution.py:52
  676.5 14.4 %convolution_convert_fusion = bf16[512,4096]{1,0:T(8,128)(2,1)} fusion(bf16[4096,2048]{1,0:T(8,128)(2,1)} %all-gather.8.cloned.1.call-done, bf16[256,2048]{0,1:T(8,128)(2,1)} %bitcast.294, bf16[256,2048]{0,1:T(8,128)(2,1)} %bitcast.295), kind=kOutput, calls=%fused_computation.24 | convolution fusion | flops 8596226048 | bytes 23068672 | tf_op jit(solution)/shard_map/dot_general | solution.py:144
  692.1 2.6 fusion.34
  694.8 0.9 add_bitcast_fusion.3
  695.6 2.5 reduce-window.46
  698.3 2.5 reduce-window.50
  701.7 2.3 fusion.33
  704.1 2.5 reduce-window.54
  706.8 2.5 reduce-window.56
  710.3 4.8 all-reduce.8.cloned.1.call-done
  715.1 1.6 convert_element_type.27
  716.7 1.6 convert_element_type.28
  718.3 12.8 %reduce-scatter.2.cloned.1.call-done = bf16[512,2048]{1,0:T(8,128)(2,1)} async-done(((bf16[512,4096]{1,0:T(8,128)(2,1)}), bf16[512,2048]{1,0:T(8,128)(2,1)}) %reduce-scatter.2.cloned.1.call-update) | async-done | bytes 2097168 | tf_op jit(solution)/shard_map/reduce_scatter | solution.py:147
  (201 shorter events, 15.9 us)
Async XLA Ops:
  7.2 211.8 %all-gather.12.cloned.1.call-start = ((), (), s32[]{:S(2)}) async-start(), calls=%async_computation.4 | async-start | bytes 17825792 | tf_op jit(solution)/shard_map/all_gather | solution.py:17
  8.8 5.8 copy-start.43
  8.9 5.7 copy-start.33
  9.7 441.6 %copy-start.41 = (f32[32,2]{0,1:T(2,128)}, f32[32,2]{0,1:T(2,128)S(1)}, u32[]{:S(2)}) copy-start(f32[32,2]{0,1:T(2,128)S(1)} %slice.89) | copy-start | bytes 772
  9.8 0.6 copy-start.30
  10.0 4.6 copy-start.45
  10.0 441.2 %copy-start.47 = (f32[32]{0:T(128)}, f32[32]{0:T(128)S(1)}, u32[]{:S(2)}) copy-start(f32[32]{0:T(128)S(1)} %get-tuple-element.143) | copy-start | bytes 388
  10.4 11.0 %copy-start.49 = (f32[32]{0:T(128)}, f32[32]{0:T(128)S(1)}, u32[]{:S(2)}) copy-start(f32[32]{0:T(128)S(1)} %exp.64) | copy-start | bytes 388
  10.5 9.8 %copy-start.22 = (f32[256,32]{0,1:T(8,128)}, f32[256,32]{0,1:T(8,128)S(1)}, u32[]{:S(2)}) copy-start(f32[256,32]{0,1:T(8,128)S(1)} %exponential_bitcast_fusion.1) | copy-start | bytes 98308
  16.5 3.7 copy-start
  16.6 3.7 copy-start.11
  20.2 1.6 copy-start.3
  23.9 1.6 copy-start.57
  23.9 218.4 %all-gather.10.cloned.1.call-start = ((), (), s32[]{:S(2)}) async-start(), calls=%async_computation.3 | async-start | bytes 6291456 | tf_op jit(solution)/shard_map/all_gather | solution.py:78
  24.7 403.3 %all-gather.8.cloned.1.call-start = ((), (), s32[]{:S(2)}) async-start(), calls=%async_computation.1 | async-start | bytes 17825792 | tf_op jit(solution)/shard_map/all_gather | solution.py:76
  25.4 625.4 %all-gather.14.cloned.1.call-start = ((), (), s32[]{:S(2)}) async-start(), calls=%async_computation.5 | async-start | bytes 17825792 | tf_op jit(solution)/shard_map/all_gather | solution.py:17
  71.4 386.3 %copy-start.51 = (f32[32]{0:T(128)}, f32[32]{0:T(128)S(1)}, u32[]{:S(2)}) copy-start(f32[32]{0:T(128)S(1)} %exp.61) | copy-start | bytes 388
  441.6 2.7 copy-start.7
  444.3 3.0 copy-start.13
  451.2 3.6 copy-start.24
  451.9 5.8 copy-start.20
  454.9 3.8 copy-start.6
  457.7 1.0 copy-start.8
  460.9 254.2 %all-reduce.8.cloned.1.call-start = ((), (), s32[]{:S(2)}) async-start(), calls=%async_computation.6 | async-start | bytes 524288 | tf_op jit(solution)/shard_map/psum | solution.py:140
  478.2 5.1 copy-start.10
  483.3 1.4 copy-start.14
  483.3 1.5 copy-start.16
  483.4 1.6 copy-start.26
  483.4 1.6 copy-start.28
  483.4 1.6 copy-start.31
  483.4 1.6 copy-start.34
  483.4 1.6 copy-start.37
  485.0 12.3 %copy-start.1 = (f32[256,2048]{0,1:T(8,128)S(1)}, f32[256,2048]{0,1:T(8,128)}, u32[]{:S(2)}) copy-start(f32[256,2048]{0,1:T(8,128)} %copy-done) | copy-start | bytes 6291460
  485.0 12.3 %copy-start.12 = (f32[32,64,256]{2,1,0:T(8,128)S(1)}, f32[32,64,256]{2,1,0:T(8,128)}, u32[]{:S(2)}) copy-start(f32[32,64,256]{2,1,0:T(8,128)} %get-tuple-element.193) | copy-start | bytes 6291460
  485.0 12.3 %copy-start.21 = (f32[256,32]{0,1:T(8,128)S(1)}, f32[256,32]{0,1:T(8,128)}, u32[]{:S(2)}) copy-start(f32[256,32]{0,1:T(8,128)} %copy-done.20) | copy-start | bytes 98308
  485.0 12.3 %copy-start.55 = (f32[32]{0:T(128)S(1)}, f32[32]{0:T(128)}, u32[]{:S(2)}) copy-start(f32[32]{0:T(128)} %param.16) | copy-start | bytes 388
  495.7 0.7 copy-start.18
  651.0 0.6 copy-start.50
  651.0 0.7 copy-start.52
  651.7 2.8 copy-start.4
  654.4 8.0 %copy-start.9 = (f32[32,64,128]{2,1,0:T(8,128)}, f32[32,64,128]{2,1,0:T(8,128)S(1)}, u32[]{:S(2)}) copy-start(f32[32,64,128]{2,1,0:T(8,128)S(1)} %get-tuple-element.171) | copy-start | bytes 3145732
  654.4 3.5 copy-start.5
  659.0 3.5 copy-start.2
  659.0 3.5 copy-start.23
  662.4 3.6 copy-start.19
  662.5 4.0 copy-start.17
  662.5 4.6 copy-start.15
  662.5 4.6 copy-start.27
  662.5 4.6 copy-start.35
  662.5 4.6 copy-start.38
  662.5 4.6 copy-start.56
  667.2 8.5 %copy-start.29 = (bf16[256,128]{1,0:T(8,128)(2,1)S(1)}, bf16[256,128]{1,0:T(8,128)(2,1)}, u32[]{:S(2)}) copy-start(bf16[256,128]{1,0:T(8,128)(2,1)} %fusion.80) | copy-start | bytes 196612
  676.3 54.8 %reduce-scatter.2.cloned.1.call-start = ((), (), s32[]{:S(2)}) async-start(), calls=%async_computation.2 | async-start | bytes 6291456 | tf_op jit(solution)/shard_map/reduce_scatter | solution.py:147
  690.9 0.6 copy-start.53
  690.9 0.7 copy-start.44
  690.9 0.7 copy-start.46
  690.9 1.0 copy-start.54
  691.0 1.1 copy-start.36
  691.0 10.6 %copy-start.32 = (f32[32,256]{1,0:T(8,128)S(1)}, f32[32,256]{1,0:T(8,128)}, u32[]{:S(2)}) copy-start(f32[32,256]{1,0:T(8,128)} %copy-done.30) | copy-start | bytes 98308
  694.7 9.3 %copy-start.25 = (f32[256,32]{0,1:T(8,128)S(1)}, f32[256,32]{0,1:T(8,128)}, u32[]{:S(2)}) copy-start(f32[256,32]{0,1:T(8,128)} %copy-done.24) | copy-start | bytes 98308
  694.7 9.3 %copy-start.39 = (f32[32,256]{1,0:T(8,128)S(1)}, f32[32,256]{1,0:T(8,128)}, u32[]{:S(2)}) copy-start(f32[32,256]{1,0:T(8,128)} %get-tuple-element.141) | copy-start | bytes 98308
  694.7 9.3 %copy-start.40 = (f32[32,256]{1,0:T(8,128)S(1)}, f32[32,256]{1,0:T(8,128)}, u32[]{:S(2)}) copy-start(f32[32,256]{1,0:T(8,128)} %get-tuple-element.142) | copy-start | bytes 98308
  694.7 9.3 %copy-start.42 = (f32[32,2]{0,1:T(2,128)S(1)}, f32[32,2]{0,1:T(2,128)}, u32[]{:S(2)}) copy-start(f32[32,2]{0,1:T(2,128)} %copy-done.41) | copy-start | bytes 772
  694.7 9.3 %copy-start.48 = (f32[32]{0:T(128)S(1)}, f32[32]{0:T(128)}, u32[]{:S(2)}) copy-start(f32[32]{0:T(128)} %copy-done.47) | copy-start | bytes 388
Sparse Core Ops, SparseCore 0:
  24.1 194.8 all-gather.11
  220.5 11.8 all-gather.9
  235.1 192.7 all-gather.7
  461.0 189.7 all-gather.13
  676.4 38.6 all-reduce.7
  717.9 13.1 reduce-scatter.1
where the time goes:
time: 744 us; the launch traced here: 738 us
  waiting for transfers between devices  498 us (67%)
  matrix products  92.8 us (12%)
  other arithmetic  45.2 us (6%)
  blocking collectives  44.3 us (6%)
  local copies, waits for them, and re-layouts  40.3 us (5%)
  between operations  15.7 us (2%)
    all_gather x2, waiting for transfers between devices, entering(): gathered = jax.tree.map(lambda a: lax.all_gather(a, axis), part)  293 us
    all_gather x1, waiting for transfers between devices, local(): weight = lax.all_gather(w_in, 'ctx', axis=0, tiled=True)  186 us
    unnamed x1, blocking collectives  44.3 us
    dot_general x4, matrix products, span_forward(): jnp.einsum('hts,shp->thp', kernel * scores[None], x_heads, precision=exac...  27.5 us
    add x15, other arithmetic, combine_states(): later[0][:, None, None] * earlier[1] + later[1]  22.3 us
    dot_general x6, matrix products, span_state(): jnp.einsum('shp,sn->hpn', x_heads * to_end.T[:, :, None], b_rows, precisi...  18.6 us
    slice x6, local copies, waits for them, and re-layouts, local(): g_float[index * SPAN:(index + 1) * SPAN]  16.7 us
    slice x6, local copies, waits for them, and re-layouts, local(): x_float[index * SPAN:(index + 1) * SPAN]  16.3 us
  transfers between devices with their start and end apart: 6, of which 5 were waited for; matrix products, arithmetic and copies ran while one was open for 14% of the time, Pallas kernels for 0%

commit v1 on v0

v1 whole, which is shorter than its diff:
```python
import functools

import jax
import jax.numpy as jnp
from jax import lax
from jax.experimental import pallas as pl
from jax.experimental.pallas import tpu as pltpu
from jax.sharding import PartitionSpec as P

SPAN = 256
HALF = SPAN // 2
P_SIZE = 64
GROUP = 8
WIDE = GROUP * P_SIZE
LOG2E = 1.4426950408889634
NEVER = -1e30

F32 = jnp.float32
BF16 = jnp.bfloat16
EXACT = lax.Precision.HIGHEST


def dot(a, b, dims, precision=None):
    return lax.dot_general(a, b, (dims, ((), ())), precision=precision, preferred_element_type=F32)


def mm(a, b, precision=None):
    return dot(a, b, ((1,), (0,)), precision)


def iota(shape, dim):
    return lax.broadcasted_iota(jnp.int32, shape, dim)


def one_hot(dtype):
    return (iota((GROUP, WIDE), 0) == iota((GROUP, WIDE), 1) // P_SIZE).astype(dtype)


def not_before():
    return (iota((SPAN, SPAN), 0) >= iota((SPAN, SPAN), 1)).astype(F32)


def before():
    return (iota((SPAN, SPAN), 0) < iota((SPAN, SPAN), 1)).astype(F32)


def same():
    return (iota((SPAN, SPAN), 0) == iota((SPAN, SPAN), 1)).astype(F32)


def first_head():
    return iota((SPAN, 2 * P_SIZE), 1) < P_SIZE


def pair_columns(columns, pair):
    shape = (columns.shape[0], 2 * P_SIZE)
    left = jnp.broadcast_to(columns[:, 2 * pair : 2 * pair + 1], shape)
    right = jnp.broadcast_to(columns[:, 2 * pair + 1 : 2 * pair + 2], shape)
    return jnp.where(iota(shape, 1) < P_SIZE, left, right)


def spread_columns(columns):
    return jnp.concatenate([pair_columns(columns, pair) for pair in range(GROUP // 2)], axis=1)


def thirds(value):
    high = value.astype(BF16).astype(F32)
    middle = (value - high).astype(BF16).astype(F32)
    return high, middle, value - high - middle


def sum_over(value, mask):
    rows = value.shape[0]
    parts = mm(jnp.concatenate(thirds(value), axis=0).astype(BF16), mask.astype(BF16))
    return parts[:rows] + parts[rows : 2 * rows] + parts[2 * rows :]


def decay_kernel(d_ref, g_ref, c_ref, r_ref, rt_ref, a_ref, gt_ref):
    row_sums = sum_over(d_ref[...] * LOG2E, 1.0 - not_before() + same())
    r_ref[...] = row_sums
    padded = jnp.concatenate([row_sums, jnp.zeros((2 * P_SIZE - GROUP, SPAN), F32)], axis=0)
    running = padded.T[:, :GROUP]
    rt_ref[0] = running
    growth = jnp.exp2(spread_columns(running))
    a_ref[0] = jnp.broadcast_to(growth[SPAN - 1 : SPAN], (8, WIDE))
    scaled = (g_ref[...].astype(F32) * growth).astype(BF16)
    gt_ref[0] = dot(c_ref[...], scaled, ((0,), (0,)))


def grad_x_kernel(r_ref, rt_ref, g_ref, b_ref, c_ref, q_ref, skip_ref, out_ref):
    b = b_ref[...]
    scores = dot(b, c_ref[...], ((1,), (1,)))
    running = r_ref[...]
    columns = rt_ref[0]
    top_keep = iota((HALF, SPAN), 1) >= iota((HALF, SPAN), 0)
    low_keep = iota((HALF, HALF), 1) >= iota((HALF, HALF), 0)
    to_end = jnp.exp2(spread_columns(columns[SPAN - 1 : SPAN] - columns))
    from_state = mm(b, q_ref[0]) * to_end
    for pair in range(GROUP // 2):
        lanes = slice(pair * 2 * P_SIZE, (pair + 1) * 2 * P_SIZE)
        g = g_ref[:, lanes]
        parts = []
        for head in (2 * pair, 2 * pair + 1):
            row = running[head : head + 1]
            top = jnp.where(top_keep, row - columns[:HALF, head : head + 1], NEVER)
            low = jnp.where(low_keep, row[:, HALF:] - columns[HALF:, head : head + 1], NEVER)
            top = (jnp.exp2(top) * scores[:HALF]).astype(BF16)
            low = (jnp.exp2(low) * scores[HALF:, HALF:]).astype(BF16)
            parts.append(jnp.concatenate([mm(top, g), mm(low, g[HALF:])], axis=0))
        inner = jnp.where(first_head(), parts[0], parts[1])
        total = inner + skip_ref[:, lanes] * g.astype(F32) + from_state[:, lanes]
        out_ref[:, lanes] = total.astype(BF16)


def arrange_kernel(unit, order_ref, f_ref, out_ref):
    for index in range(f_ref.shape[1] // unit):
        source = pl.ds(pl.multiple_of(order_ref[index] * unit, 128), unit)
        out_ref[:, index * unit : (index + 1) * unit] = f_ref[:, source]


def fetch(arrays, places, buffer, sems):
    copies = []
    at = 0
    for index, (ref, column) in enumerate(zip(arrays, places)):
        rows = ref.shape[0]
        source = ref.at[:, pl.ds(column, buffer.shape[1])]
        copy = pltpu.make_async_copy(source, buffer.at[pl.ds(at, rows)], sems.at[index])
        copy.start()
        copies.append(copy)
        at += rows
    return copies


def bundles(count):
    return [range(at, min(at + PLANE, count)) for at in range(0, count, PLANE)]


def forward_kernel(places, f_ref, rt_ref, b_ref, *refs):
    count = len(places)
    arrays, (x_ref, e_ref, buffer, sems) = refs[:count], refs[count:]
    copies = fetch(arrays, places, buffer, sems)
    rows = arrays[0].shape[0]
    total = None
    for bundle in bundles(count):
        for index in bundle:
            copies[index].wait()
        deep = slice(bundle[0] * rows, (bundle[-1] + 1) * rows)
        term = mm(f_ref[:, deep], buffer[deep])
        total = term if total is None else total + term
    x = total.astype(BF16)
    x_ref[...] = x
    for k in range(e_ref.shape[0]):
        rows = slice(k * SPAN, (k + 1) * SPAN)
        for group in range(rt_ref.shape[0]):
            lanes = slice(group * WIDE, (group + 1) * WIDE)
            columns = rt_ref[group, rows]
            to_end = jnp.exp2(spread_columns(columns[SPAN - 1 : SPAN] - columns))
            scaled = (x[rows, lanes].astype(F32) * to_end).astype(BF16)
            e_ref[k, :, lanes] = dot(b_ref[rows], scaled, ((0,), (0,)))


def product_kernel(places, has_before, order_ref, g_ref, *refs):
    count = len(places)
    arrays, refs = refs[:count], refs[count:]
    if has_before:
        before_ref, refs = refs[0], refs[1:]
    out_ref, buffer, slots, sems, out_sems = refs[:5]
    copies = fetch(arrays, places, buffer, sems)
    rows = arrays[0].shape[0]
    where = [pl.ds(pl.multiple_of(order_ref[index] * rows, 128), rows) for index in range(count)]
    if has_before:
        before_slots, before_sems = refs[5:]
        before = []
        for index in range(count):
            source = before_ref.at[:, where[index]]
            copy = pltpu.make_async_copy(source, before_slots.at[index], before_sems.at[index])
            copy.start()
            before.append(copy)
    g = g_ref[...]
    stores = []
    for bundle in bundles(count):
        for index in bundle:
            copies[index].wait()
        product = dot(g, buffer[bundle[0] * rows : (bundle[-1] + 1) * rows], ((1,), (1,)))
        for index in bundle:
            part = product[:, (index - bundle[0]) * rows : (index - bundle[0] + 1) * rows]
            if has_before:
                before[index].wait()
                part = part + before_slots[index].astype(F32)
            slots[index] = part.astype(BF16)
            store = pltpu.make_async_copy(
                slots.at[index], out_ref.at[:, where[index]], out_sems.at[index]
            )
            store.start()
            stores.append(store)
    for store in stores:
        store.wait()


def after_kernel(*refs):
    pass


def inner_kernel(
    r_ref, rt_ref, g_ref, x_ref, b_ref, c_ref, q_ref, *refs
):
    d_ref, grad_b_ref, grad_c_ref, sum_ref = refs[-4:]
    so_far = refs[:-4]
    step = pl.program_id(1)
    b = b_ref[...]
    c = c_ref[...]
    scores = dot(b, c, ((1,), (1,)))
    running = r_ref[...]
    columns = rt_ref[0]
    top_keep = iota((HALF, SPAN), 1) >= iota((HALF, SPAN), 0)
    low_keep = iota((HALF, HALF), 1) >= iota((HALF, HALF), 0)

    @pl.when(step == 0)
    def _():
        sum_ref[...] = jnp.zeros_like(sum_ref)
        grad_b_ref[...] = so_far[0][...] if so_far else jnp.zeros_like(grad_b_ref)

    rows = []
    across = jnp.zeros((SPAN, 2 * P_SIZE), F32)
    lane = iota((SPAN, 2 * P_SIZE), 1)
    top_sum = sum_ref[:HALF]
    low_sum = sum_ref[HALF:, HALF:]
    for pair in range(GROUP // 2):
        lanes = slice(pair * 2 * P_SIZE, (pair + 1) * 2 * P_SIZE)
        g = g_ref[:, lanes]
        x = x_ref[:, lanes]
        for head in (2 * pair, 2 * pair + 1):
            mine = (lane < P_SIZE) if head == 2 * pair else (lane >= P_SIZE)
            x_head = jnp.where(mine, x, jnp.zeros_like(x))
            row = running[head : head + 1]
            top = jnp.where(top_keep, row - columns[:HALF, head : head + 1], NEVER)
            low = jnp.where(low_keep, row[:, HALF:] - columns[HALF:, head : head + 1], NEVER)
            top = jnp.exp2(top) * dot(x_head[:HALF], g, ((1,), (1,)))
            low = jnp.exp2(low) * dot(x_head[HALF:], g[HALF:], ((1,), (1,)))
            top_sum = top_sum + top
            low_sum = low_sum + low
            top = top * scores[:HALF]
            low = low * scores[HALF:, HALF:]
            top_row = jnp.sum(top, axis=0, keepdims=True)
            low_row = jnp.sum(low, axis=0, keepdims=True)
            rows.append(jnp.concatenate([top_row[:, :HALF], top_row[:, HALF:] + low_row], axis=1))
            column = jnp.concatenate(
                [jnp.sum(top, axis=1, keepdims=True), jnp.sum(low, axis=1, keepdims=True)], axis=0
            )
            across = jnp.where(lane == head, column, across)
    sum_ref[:HALF] = top_sum
    sum_ref[HALF:, HALF:] = low_sum
    difference = jnp.concatenate(rows, axis=0) - across.T[:GROUP]
    to_end = jnp.exp2(spread_columns(columns[SPAN - 1 : SPAN] - columns))
    scaled = x_ref[...].astype(F32) * to_end
    ends = dot(one_hot(BF16), (scaled * mm(b, q_ref[0])).astype(BF16), ((1,), (1,)))
    d_ref[...] = sum_over(difference, not_before()) + sum_over(ends, before())
    grad_b_ref[...] += dot(scaled.astype(BF16), q_ref[0], ((1,), (1,)))

    @pl.when(step == pl.num_programs(1) - 1)
    def _():
        total = sum_ref[...].astype(BF16)
        grad_b_ref[...] += mm(total, c)
        part = dot(total, b, ((0,), (0,)))
        grad_c_ref[...] = part + so_far[1][...] if so_far else part


def state_kernel(
    rt_ref, g_ref, c_ref, s_ref, e_ref, q_ref, a_ref, d_part_ref, c_part_ref, d_ref, grad_c_ref, held
):
    span, group = pl.program_id(0), pl.program_id(1)

    @pl.when(group == 0)
    def _():
        grad_c_ref[...] = c_part_ref[...]

    @pl.when(span == 0)
    def _():
        held[group] = s_ref[...]

    state = held[group]
    low = state.astype(BF16)
    scaled = g_ref[...].astype(F32) * jnp.exp2(spread_columns(rt_ref[0]))
    ends = dot(one_hot(BF16), (scaled * mm(c_ref[...], low)).astype(BF16), ((1,), (1,)))
    grad_c_ref[...] += dot(scaled.astype(BF16), low, ((1,), (1,)))
    product = jnp.sum(q_ref[0].astype(F32) * state, axis=0, keepdims=True) * a_ref[0, :1]
    high, middle, last = thirds(product)
    row = iota((8, WIDE), 0)
    stacked = jnp.where(row == 0, high, jnp.where(row == 1, middle, jnp.where(row == 2, last, 0.0)))
    kept = dot(one_hot(BF16), stacked.astype(BF16), ((1,), (1,)))
    kept = jnp.sum(kept, axis=1, keepdims=True)
    d_ref[...] = d_part_ref[...] + sum_over(ends, not_before()) + kept
    held[group] = e_ref[0] + a_ref[0, :1] * state


def call(kernel, grid, in_specs, out_specs, out_shape, flops, size, scratch=()):
    return pl.pallas_call(
        kernel,
        grid=grid,
        in_specs=in_specs,
        out_specs=out_specs,
        out_shape=out_shape,
        scratch_shapes=list(scratch),
        cost_estimate=pl.CostEstimate(flops=flops, bytes_accessed=size, transcendentals=0),
        compiler_params=pltpu.CompilerParams(
            dimension_semantics=("arbitrary",) * len(grid), vmem_limit_bytes=56 * 2**20
        ),
    )


def run_spec(at=0):
    return pl.BlockSpec((GROUP, SPAN), lambda k, h: (h + at, k))


def run_t_spec(at=0):
    return pl.BlockSpec((1, SPAN, GROUP), lambda k, h: (h + at, k, 0))


def rows_spec(at=0):
    return pl.BlockSpec((SPAN, WIDE), lambda k, h: (k, h + at))


def state_spec(at=0):
    return pl.BlockSpec((1, 2 * P_SIZE, WIDE), lambda k, h: (k, 0, h + at))


def kept_spec(at=0):
    return pl.BlockSpec((1, 8, WIDE), lambda k, h: (k, 0, h + at))


SHARED = pl.BlockSpec((SPAN, 2 * P_SIZE), lambda k, h: (k, 0))
GAIN = pl.BlockSpec((1, WIDE), lambda k, h: (0, h))
ANYWHERE = pl.BlockSpec(memory_space=pl.ANY)
SCALARS = pl.BlockSpec(memory_space=pltpu.SMEM)


def shape(*dims, dtype=F32):
    return jax.ShapeDtypeStruct(dims, dtype)


def swap(value, axis, bit):
    count = lax.axis_size(axis)
    return lax.ppermute(value, axis, [(i, i ^ bit) for i in range(count)])


def block_products(kept):
    count = lax.axis_size("ctx")
    place = lax.axis_index("ctx")
    steps = []
    before_me = jnp.ones_like(kept)
    after_me = jnp.ones_like(kept)
    bit = 1
    while bit < count:
        other = swap(kept, "ctx", bit)
        upper = (place & bit) != 0
        steps.append((bit, upper, kept, other, before_me, after_me))
        before_me = jnp.where(upper, before_me * other, before_me)
        after_me = jnp.where(upper, after_me, after_me * other)
        kept = kept * other
        bit *= 2
    return steps


def scan_states(total, steps, reverse):
    entering = jnp.zeros_like(total)
    for bit, upper, kept, other, before_me, after_me in steps:
        got = swap(total.astype(BF16), "ctx", bit).astype(F32)
        if reverse:
            entering = entering + jnp.where(upper, 0.0, after_me) * got
            total = jnp.where(upper, got + other * total, total + kept * got)
        else:
            entering = entering + jnp.where(upper, before_me, 0.0) * got
            total = jnp.where(upper, kept * got + total, other * total + got)
    return entering


def head_sum(value):
    bit = 1
    while bit < lax.axis_size("head"):
        value = value.astype(BF16)
        value = value.astype(F32) + swap(value, "head", bit).astype(F32)
        bit *= 2
    return value


def head_scatter(product):
    count = lax.axis_size("head")
    if count != 2:
        return lax.psum_scatter(product, "head", scatter_dimension=1, tiled=True)
    half = product.shape[1] // 2
    got = swap(product[:, :half], "head", 1)
    return (product[:, half:].astype(F32) + got.astype(F32)).astype(BF16)


PLANE = 4


def after(value, *tokens):
    return pl.pallas_call(
        after_kernel,
        in_specs=[ANYWHERE] * (1 + len(tokens)),
        out_specs=ANYWHERE,
        out_shape=shape(*value.shape, dtype=value.dtype),
        input_output_aliases={0: 0},
        cost_estimate=pl.CostEstimate(flops=0, bytes_accessed=0, transcendentals=0),
    )(value, *tokens)


def shift(value, by):
    count = lax.axis_size("ctx")
    return lax.ppermute(value, "ctx", [(i, (i + PLANE * by) % count) for i in range(count)])


def gather_layered(w, sizes):
    place = lax.axis_index("ctx")
    layers = lax.axis_size("ctx") // PLANE
    layer, spot = place // PLANE, place % PLANE
    turns = (1, 3, 2)
    own_x = swap(w, "ctx", 1)
    own_y = swap(w, "ctx", 2)
    own_across = swap(own_y, "ctx", 1)
    chunks = []
    tokens = ()
    at = 0
    for size in sizes:
        part = w[:, at * P_SIZE : (at + size) * P_SIZE]
        if tokens:
            part = after(part, tokens[0])
        arrays = [w, own_x, own_y, own_across]
        places = [at * P_SIZE] * PLANE + [0] * (PLANE * len(turns))
        moved = [shift(part, by) for by in turns]
        if tokens:
            moved = [after(value, *tokens) for value in moved]
        for index, value in enumerate(moved):
            value_x = swap(value, "ctx", 1)
            value_y = swap(value, "ctx", 2)
            if index == 1:
                across = swap(value_y, "ctx", 1)
            else:
                across = swap(value_x, "ctx", 2)
            arrays += [value, value_x, value_y, across]
        tokens = (arrays[PLANE], arrays[-3], arrays[-2])
        chunks.append((arrays, places))
        at += size
    order = jnp.stack(
        [
            (layer + layers - k) % layers * PLANE + (spot ^ flip)
            for k in (0,) + turns
            for flip in range(PLANE)
        ]
    )
    return chunks, order.astype(jnp.int32)


def gather_plain(w, sizes):
    chunks = []
    at = 0
    for size in sizes:
        part = w[:, at * P_SIZE : (at + size) * P_SIZE]
        chunks.append(([lax.all_gather(part, "ctx", axis=0, tiled=True)], [0]))
        at += size
    return chunks, jnp.zeros((1,), jnp.int32)


def gather_weight(w, sizes):
    if lax.axis_size("ctx") == 4 * PLANE and w.shape[0] % 256 == 0:
        return gather_layered(w, sizes)
    return gather_plain(w, sizes)


def local(inputs, w_in, b_rows, c_rows, log_decay, skip_gain, grad_out):
    length, columns = grad_out.shape
    heads = log_decay.shape[0]
    spans = length // SPAN
    groups = heads // GROUP
    n = b_rows.shape[1]
    grid = (spans, groups)

    sizes = (heads // 2, heads // 2) if heads % (2 * GROUP) == 0 else (heads,)
    chunks, order = gather_weight(w_in, sizes)
    features = lax.all_gather(inputs, "head", axis=1, tiled=True)
    width = features.shape[1]
    unit = width // order.shape[0]
    features = call(
        functools.partial(arrange_kernel, unit),
        (1,),
        [SCALARS, pl.BlockSpec((length, width), lambda h: (0, 0))],
        pl.BlockSpec((length, width), lambda h: (0, 0)),
        shape(length, width, dtype=BF16),
        0,
        4 * length * width,
    )(order, features)

    running, running_t, kept, own_grads = call(
        decay_kernel,
        grid,
        [run_spec(), rows_spec(), SHARED],
        [run_spec(), run_t_spec(), kept_spec(), state_spec()],
        [
            shape(heads, length),
            shape(groups, length, GROUP),
            shape(spans, 8, columns),
            shape(spans, n, columns),
        ],
        2 * length * columns * n,
        6 * length * columns,
    )(log_decay, grad_out, c_rows)

    kept_total = kept[0, :1]
    for k in range(1, spans):
        kept_total = kept_total * kept[k, :1]
    steps = block_products(kept_total)

    total = own_grads[spans - 1]
    for k in range(spans - 2, -1, -1):
        total = own_grads[k] + kept[k, :1] * total
    leaving = [scan_states(total, steps, True)]
    for k in range(spans - 1, 0, -1):
        leaving.insert(0, own_grads[k] + kept[k, :1] * leaving[0])
    leaving = jnp.stack([value.astype(BF16) for value in leaving])

    skip = jnp.repeat(skip_gain, P_SIZE)[None]
    grad_x = call(
        grad_x_kernel,
        grid,
        [run_spec(), run_t_spec(), rows_spec(), SHARED, SHARED, state_spec(), GAIN],
        rows_spec(),
        shape(length, columns, dtype=BF16),
        8 * length * columns * SPAN,
        6 * length * columns,
    )(running, running_t, grad_out, b_rows, c_rows, leaving, skip)

    two = lax.axis_size("head") == 2
    product_order = order
    if two:
        blocks = order.shape[0]
        product_order = (order + (1 - lax.axis_index("head")) * (blocks // 2)) % blocks

    grad_b = grad_c = product = None
    decay_parts = []
    at = 0
    for index, size in enumerate(sizes):
        wide = size * P_SIZE
        here = at // GROUP
        count = size // GROUP
        arrays, places = chunks[index]
        pieces = len(arrays)
        x, own_states = call(
            functools.partial(forward_kernel, places),
            (1,),
            [
                pl.BlockSpec((length, width), lambda h: (0, 0)),
                pl.BlockSpec((count, length, GROUP), lambda h, here=here // count: (here, 0, 0)),
                pl.BlockSpec((length, n), lambda h: (0, 0)),
            ]
            + [ANYWHERE] * pieces,
            [
                pl.BlockSpec((length, wide), lambda h: (0, 0)),
                pl.BlockSpec((spans, n, wide), lambda h: (0, 0, 0)),
            ],
            [shape(length, wide, dtype=BF16), shape(spans, n, wide)],
            2 * length * wide * width,
            2 * wide * width,
            [pltpu.VMEM((width, wide), BF16), pltpu.SemaphoreType.DMA((pieces,))],
        )(features, running_t, b_rows, *arrays)

        chunk = slice(at * P_SIZE, at * P_SIZE + wide)
        total = own_states[0]
        for k in range(1, spans):
            total = kept[k, :1, chunk] * total + own_states[k]
        cut = [step[:2] + tuple(value[:, chunk] for value in step[2:]) for step in steps]
        entering = scan_states(total, cut, False)

        so_far = () if grad_b is None else (grad_b, grad_c)
        decay_part, grad_b, grad_c = call(
            inner_kernel,
            (spans, count),
            [
                run_spec(here),
                run_t_spec(here),
                rows_spec(here),
                rows_spec(),
                SHARED,
                SHARED,
                state_spec(here),
            ]
            + [SHARED] * len(so_far),
            [run_spec(), SHARED, SHARED],
            [shape(size, length), shape(length, n), shape(length, n)],
            12 * length * wide * SPAN,
            6 * length * wide,
            [pltpu.VMEM((SPAN, SPAN), F32)],
        )(running, running_t, grad_out, x, b_rows, c_rows, leaving, *so_far)
        decay_part, grad_c = call(
            state_kernel,
            (spans, count),
            [
                run_t_spec(here),
                rows_spec(here),
                SHARED,
                pl.BlockSpec((n, WIDE), lambda k, h: (0, h)),
                state_spec(),
                state_spec(here),
                kept_spec(here),
                run_spec(),
                SHARED,
            ],
            [run_spec(), SHARED],
            [shape(size, length), shape(length, n)],
            4 * length * wide * n,
            6 * length * wide,
            [pltpu.VMEM((count, n, WIDE), F32)],
        )(running_t, grad_out, c_rows, entering, own_states, leaving, kept, decay_part, grad_c)
        decay_parts.append(decay_part)

        scratch = [
            pltpu.VMEM((width, wide), BF16),
            pltpu.VMEM((pieces, length, unit), BF16),
            pltpu.SemaphoreType.DMA((pieces,)),
            pltpu.SemaphoreType.DMA((pieces,)),
        ]
        earlier = ()
        if product is not None:
            earlier = (product,)
            scratch += [
                pltpu.VMEM((pieces, length, unit), BF16),
                pltpu.SemaphoreType.DMA((pieces,)),
            ]
        product = call(
            functools.partial(product_kernel, places, product is not None),
            (1,),
            [SCALARS, pl.BlockSpec((length, wide), lambda h, index=at // size: (0, index))]
            + [ANYWHERE] * (pieces + len(earlier)),
            ANYWHERE,
            shape(length, width, dtype=BF16),
            2 * length * wide * width,
            2 * wide * width,
            scratch,
        )(product_order, grad_x, *arrays, *earlier)
        at += size

    if two and order.shape[0] == 1:
        product = jnp.roll(product, (1 - lax.axis_index("head")) * (width // 2), axis=1)
    grad_inputs = head_scatter(product)
    return (grad_inputs, head_sum(grad_b), head_sum(grad_c), jnp.concatenate(decay_parts, axis=0))


def solution(mesh):
    in_specs = (
        P("ctx", "head"),
        P("ctx", "head"),
        P("ctx", None),
        P("ctx", None),
        P("head", "ctx"),
        P("head"),
        P("ctx", "head"),
    )
    out_specs = (P("ctx", "head"), P("ctx", None), P("ctx", None), P("head", "ctx"))
    return jax.shard_map(local, mesh=mesh, in_specs=in_specs, out_specs=out_specs, check_vma=False)
```

time: 744 us -> 340 us (0.46)
  waiting for transfers between devices: 498 us -> 115 us
  Pallas kernels: 0 us -> 104 us
  matrix products: 92.8 us -> 0 us
  starting transfers between devices: 0.62 us -> 70.5 us
  blocking collectives: 44.3 us -> 0 us
  local copies, waits for them, and re-layouts: 40.3 us -> 9.96 us
  other arithmetic: 45.2 us -> 25.1 us
    all_gather x4 -> x1, waiting for transfers between devices: 479 us -> 0.01 us  [local(): features = lax.all_gather(inputs, 'head', axis=1, tiled=True)]
    ppermute x0 -> x45, waiting for transfers between devices: none -> 115 us  [the longest x39 104 us: swap(): return lax.ppermute(value, axis, [(i, i ^ bit) for i in range(count)])]
    pallas_call x0 -> x15, Pallas kernels: none -> 104 us  [the longest x2 27.3 us: local(): call(inner_kernel, (spans, count), [run_spec(here), run_t_spec(here), row...]
    dot_general x24 -> x0, matrix products: 92.8 us -> none  [the longest x4 27.5 us: span_forward(): jnp.einsum('hts,shp->thp', kernel * scores[None], x_heads, precision=exac...]
    ppermute x0 -> x45, starting transfers between devices: none -> 70.5 us  [the longest x39 49.1 us: swap(): return lax.ppermute(value, axis, [(i, i ^ bit) for i in range(count)])]
    unnamed x1 -> x0, blocking collectives: 44.3 us -> none
    slice x13 -> x9, local copies, waits for them, and re-layouts: 33.1 us -> 6.2 us  [the longest x1 3.16 us: head_scatter(): got = swap(product[:, :half], 'head', 1)]
    add x15 -> x4, other arithmetic: 22.3 us -> 3.44 us  [the longest x2 1.98 us: scan_states(): entering = entering + jnp.where(upper, before_me, 0.0) * got]
  transfers between devices with their start and end apart: 6 -> 46, of which waited for: 5 -> 17; matrix products, arithmetic and copies ran while one was open for 14% -> 9% of each run, Pallas kernels for 0% -> 31%
where the time goes in v1:
time: 340 us; the launch traced here: 339 us
  waiting for transfers between devices  115 us (34%)
  Pallas kernels  104 us (31%)
  starting transfers between devices  70.5 us (21%)
  other arithmetic  25.1 us (7%)
  between operations  14.5 us (4%)
  local copies, waits for them, and re-layouts  9.96 us (3%)
    ppermute x39, waiting for transfers between devices, swap(): return lax.ppermute(value, axis, [(i, i ^ bit) for i in range(count)])  104 us
    ppermute x39, starting transfers between devices, swap(): return lax.ppermute(value, axis, [(i, i ^ bit) for i in range(count)])  49.1 us
    pallas_call x2, Pallas kernels, local(): call(inner_kernel, (spans, count), [run_spec(here), run_t_spec(here), row...  27.3 us
    pallas_call x2, Pallas kernels, local(): call(functools.partial(forward_kernel, places), (1,), [pl.BlockSpec((leng...  21.8 us
    ppermute x6, starting transfers between devices, shift(): lax.ppermute(value, 'ctx', [(i, (i + PLANE * by) % count) for i in range(...  21.3 us
    pallas_call x2, Pallas kernels, local(): call(functools.partial(product_kernel, places, product is not None), (1,)...  19.5 us
    convert_element_type x12, other arithmetic, scan_states(): got = swap(total.astype(BF16), 'ctx', bit).astype(F32)  12 us
    pallas_call x2, Pallas kernels, local(): call(state_kernel, (spans, count), [run_t_spec(here), rows_spec(here), SH...  11.1 us
  transfers between devices with their start and end apart: 46, of which 17 were waited for; matrix products, arithmetic and copies ran while one was open for 9% of the time, Pallas kernels for 31%

profile of v1, /device:TPU:0, one launch (start us, length us, event | category | flops | bytes accessed | tf_op | source)
XLA Modules:
  0.0 339.3 jit_solution(16977687430902856236)
XLA Ops:
  7.2 2.3 fusion.45
  9.5 3.0 collective-permute-start.10
  12.5 9.1 %shard_map.102 = (f32[32,512]{1,0:T(8,128)}, f32[4,512,8]{2,1,0:T(8,128)}, f32[2,8,2048]{2,1,0:T(8,128)}, f32[2,128,2048]{2,1,0:T(8,128)}) custom-call(f32[32,512]{1,0:T(8,128)} %d_ref.1, bf16[512,2048]{1,0:T(8,128)(2,1)} %g_ref.11, bf16[512,128]{1,0:T(8,128)(2,1)} %c_ref.11), custom_call_target="tpu_custom_call" | custom-call | flops 268435456 | bytes 6291456 | tf_op jit(solution)/shard_map/pallas_call | solution.py:494
  22.5 2.5 fusion.33
  25.0 1.5 collective-permute-start
  26.4 2.6 collective-permute-start.12
  29.0 1.3 collective-permute-start.29
  31.8 6.9 %collective-permute-done.1 = f32[1,2048]{1,0:T(1,128)S(1)} collective-permute-done((f32[1,2048]{1,0:T(1,128)S(1)}, f32[1,2048]{1,0:T(1,128)S(1)}, u32[]{:S(2)}, u32[]{:S(2)}) %collective-permute-start.1) | collective-permute-done | bytes 8224 | tf_op jit(solution)/shard_map/ppermute | solution.py:343
  38.7 1.6 collective-permute-start.3
  41.1 1.6 collective-permute-start.11
  42.7 1.5 fusion.43
  44.8 1.6 collective-permute-start.5
  47.7 14.9 %collective-permute-done.5 = f32[1,2048]{1,0:T(1,128)S(1)} collective-permute-done((f32[1,2048]{1,0:T(1,128)S(1)}, f32[1,2048]{1,0:T(1,128)S(1)}, u32[]{:S(2)}, u32[]{:S(2)}) %collective-permute-start.5) | collective-permute-done | bytes 8224 | tf_op jit(solution)/shard_map/ppermute | solution.py:343
  62.6 1.5 collective-permute-start.8
  65.0 1.5 collective-permute-start.14
  66.5 12.8 %collective-permute-start.18 = (bf16[256,1024]{1,0:T(8,128)(2,1)}, bf16[256,1024]{1,0:T(8,128)(2,1)S(1)}, u32[]{:S(2)}, u32[]{:S(2)}) collective-permute-start(bf16[256,1024]{1,0:T(8,128)(2,1)} %shard_map.104), channel_id=1, source_target_pairs={{0,24},{2,26},{4,28},{6,30},{8,0},{10,2},{12,4},{14,6},{16,8},{18,... | collective-permute-start | bytes 1572872 | tf_op jit(solution)/shard_map/ppermute | solution.py:411
  79.3 2.4 fusion.32
  81.7 1.0 collective-permute-start.7
  82.7 14.8 %collective-permute-done.14.refs_3_.refs_14_ = bf16[256,1024]{1,0:T(8,128)(2,1)S(1)} collective-permute-done((bf16[256,1024]{1,0:T(8,128)(2,1)}, bf16[256,1024]{1,0:T(8,128)(2,1)S(1)}, u32[]{:S(2)}, u32[]{:S(2)}) %collective-permute-start.14) | collective-permute-done | bytes 524320 | tf_op jit(solution)/shard_map/ppermute | solution.py:343
  97.5 2.6 collective-permute-start.4
  100.7 10.6 %collective-permute-done.22.refs_0_ = bf16[256,1024]{1,0:T(8,128)(2,1)S(1)} collective-permute-done((bf16[256,1024]{1,0:T(8,128)(2,1)}, bf16[256,1024]{1,0:T(8,128)(2,1)S(1)}, u32[]{:S(2)}, u32[]{:S(2)}) %collective-permute-start.22) | collective-permute-done | bytes 524320 | tf_op jit(solution)/shard_map/ppermute | solution.py:411
  112.8 1.5 collective-permute-start.31
  114.4 4.8 %collective-permute-done.4 = bf16[128,2048]{1,0:T(8,128)(2,1)} collective-permute-done((bf16[128,2048]{1,0:T(8,128)(2,1)}, bf16[128,2048]{1,0:T(8,128)(2,1)}, u32[]{:S(2)}, u32[]{:S(2)}) %collective-permute-start.4) | collective-permute-done | bytes 524320 | tf_op jit(solution)/shard_map/ppermute | solution.py:343
  119.8 1.9 fusion.8
  121.7 1.5 collective-permute-start.15
  123.2 1.6 collective-permute-start.20
  124.8 1.5 collective-permute-done.27.refs_6_
  126.8 10.7 %collective-permute-done.31.refs_10_ = bf16[256,1024]{1,0:T(8,128)(2,1)} collective-permute-done((bf16[256,1024]{1,0:T(8,128)(2,1)}, bf16[256,1024]{1,0:T(8,128)(2,1)}, u32[]{:S(2)}, u32[]{:S(2)}) %collective-permute-start.31) | collective-permute-done | bytes 524320 | tf_op jit(solution)/shard_map/ppermute | solution.py:343
  137.5 3.1 collective-permute-start.6
  141.2 4.4 %collective-permute-done.15.refs_5_ = bf16[256,1024]{1,0:T(8,128)(2,1)} collective-permute-done((bf16[256,1024]{1,0:T(8,128)(2,1)}, bf16[256,1024]{1,0:T(8,128)(2,1)}, u32[]{:S(2)}, u32[]{:S(2)}) %collective-permute-start.15) | collective-permute-done | bytes 524320 | tf_op jit(solution)/shard_map/ppermute | solution.py:343
  145.6 1.6 collective-permute-start.16
  147.2 1.6 collective-permute-done.20.refs_10_
  148.8 8.0 %collective-permute-done.23.refs_13_ = bf16[256,1024]{1,0:T(8,128)(2,1)S(1)} collective-permute-done((bf16[256,1024]{1,0:T(8,128)(2,1)S(1)}, bf16[256,1024]{1,0:T(8,128)(2,1)S(1)}, u32[]{:S(2)}, u32[]{:S(2)}) %collective-permute-start.23) | collective-permute-done | bytes 524320 | tf_op jit(solution)/shard_map/ppermute | solution.py:343
  156.7 1.6 collective-permute-start.28
  159.5 1.7 fusion.31
  161.2 1.1 pad_maximum_fusion.q_ref
  162.3 1.7 collective-permute-start.19
  164.0 16.3 %collective-permute-done.28.refs_7_ = bf16[256,1024]{1,0:T(8,128)(2,1)S(1)} collective-permute-done((bf16[256,1024]{1,0:T(8,128)(2,1)}, bf16[256,1024]{1,0:T(8,128)(2,1)S(1)}, u32[]{:S(2)}, u32[]{:S(2)}) %collective-permute-start.28) | collective-permute-done | bytes 524320 | tf_op jit(solution)/shard_map/ppermute | solution.py:343
  181.1 1.3 collective-permute-start.17
  182.4 8.0 %collective-permute-done.32.refs_11_ = bf16[256,1024]{1,0:T(8,128)(2,1)S(1)} collective-permute-done((bf16[256,1024]{1,0:T(8,128)(2,1)}, bf16[256,1024]{1,0:T(8,128)(2,1)S(1)}, u32[]{:S(2)}, u32[]{:S(2)}) %collective-permute-start.32) | collective-permute-done | bytes 524320 | tf_op jit(solution)/shard_map/ppermute | solution.py:343
  191.0 1.3 collective-permute-start.25
  192.4 9.9 %shard_map.103.g_ref = bf16[512,2048]{1,0:T(8,128)(2,1)} custom-call(f32[32,512]{1,0:T(8,128)} %get-tuple-element.22.r_ref, f32[4,512,8]{2,1,0:T(8,128)} %get-tuple-element.23.rt_ref, bf16[512,2048]{1,0:T(8,128)(2,1)} %g_ref.11, bf16[512,128]{1,0:T(8,128)(2,1)} %b_ref.9, bf16[512,128]{1,0:T(8,128)(2,1)} %c_ref.11, ...), custom_call_target="tpu_custom_call" | custom-call | flops 2147483648 | bytes 6291456 | tf_op jit(solution)/shard_map/pallas_call | solution.py:523
  202.3 9.2 %shard_map.108.refs_16_ = bf16[512,4096]{1,0:T(8,128)(2,1)} custom-call(s32[16]{0:T(128)} %and_select_fusion.order_ref, bf16[512,2048]{1,0:T(8,128)(2,1)} %shard_map.103.g_ref, bf16[256,2048]{1,0:T(8,128)(2,1)} %refs_0_.7, bf16[256,2048]{1,0:T(8,128)(2,1)} %collective-permute-done.7.refs_1_, bf16[256,2048]{1,0:T(8,128)(2,1)} %copy-done.9, ...), custom_call_target="tpu_custom_call" | custom-call | flops 4294967296 | bytes 8388608 | tf_op jit(solution)/shard_map/pallas_call | solution.py:629
  211.6 1.1 collective-permute-done.25.refs_15_
  213.8 10.3 %shard_map.109 = bf16[512,4096]{1,0:T(8,128)(2,1)} custom-call(s32[16]{0:T(128)} %and_select_fusion.order_ref, bf16[512,2048]{1,0:T(8,128)(2,1)} %shard_map.103.g_ref, bf16[256,2048]{1,0:T(8,128)(2,1)} %refs_0_.7, bf16[256,2048]{1,0:T(8,128)(2,1)} %collective-permute-done.7.refs_1_, bf16[256,2048]{1,0:T(8,128)(2,1)} %copy-done.9, ...), custom_call_target="tpu_custom_call" | custom-call | flops 4294967296 | bytes 8388608 | tf_op jit(solution)/shard_map/pallas_call | solution.py:629
  224.1 3.2 slice.132
  227.3 5.0 %shard_map.110.f_ref = bf16[512,4096]{1,0:T(8,128)(2,1)} custom-call(s32[16]{0:T(128)} %copy-done.32, bf16[512,4096]{1,0:T(8,128)(2,1)} %all-gather.2.cloned.1.call-done.f_ref), custom_call_target="tpu_custom_call" | custom-call | bytes 8388608 | tf_op jit(solution)/shard_map/pallas_call | solution.py:484
  232.3 11.1 %shard_map.112 = (bf16[512,1024]{1,0:T(8,128)(2,1)}, f32[2,128,1024]{2,1,0:T(8,128)}) custom-call(bf16[512,4096]{1,0:T(8,128)(2,1)} %shard_map.110.f_ref, f32[4,512,8]{2,1,0:T(8,128)} %get-tuple-element.23.rt_ref, bf16[512,128]{1,0:T(8,128)(2,1)} %b_ref.9, bf16[256,2048]{1,0:T(8,128)(2,1)} %refs_0_.7, bf16[256,2048]{1,0:T(8,128)(2,1)} %collective-permute-done.7.refs_1_, ...), custom_call_target="tpu_custom_call" | custom-call | flops 4294967296 | bytes 8388608 | tf_op jit(solution)/shard_map/pallas_call | solution.py:548
  243.4 1.3 fusion.36
  244.7 1.6 collective-permute-start.35
  246.2 10.7 %shard_map.111 = (bf16[512,1024]{1,0:T(8,128)(2,1)}, f32[2,128,1024]{2,1,0:T(8,128)}) custom-call(bf16[512,4096]{1,0:T(8,128)(2,1)} %shard_map.110.f_ref, f32[4,512,8]{2,1,0:T(8,128)} %get-tuple-element.23.rt_ref, bf16[512,128]{1,0:T(8,128)(2,1)} %b_ref.9, bf16[256,2048]{1,0:T(8,128)(2,1)} %refs_0_.7, bf16[256,2048]{1,0:T(8,128)(2,1)} %collective-permute-done.7.refs_1_, ...), custom_call_target="tpu_custom_call" | custom-call | flops 4294967296 | bytes 8388608 | tf_op jit(solution)/shard_map/pallas_call | solution.py:548
  257.0 1.4 fusion.37
  259.7 7.2 %collective-permute-done.40 = bf16[128,1024]{1,0:T(8,128)(2,1)S(1)} collective-permute-done((bf16[128,1024]{1,0:T(8,128)(2,1)S(1)}, bf16[128,1024]{1,0:T(8,128)(2,1)S(1)}, u32[]{:S(2)}, u32[]{:S(2)}) %collective-permute-start.40) | collective-permute-done | bytes 262176 | tf_op jit(solution)/shard_map/ppermute | solution.py:343
  267.7 3.7 %collective-permute-start.37 = (bf16[128,1024]{1,0:T(8,128)(2,1)S(1)}, bf16[128,1024]{1,0:T(8,128)(2,1)S(1)}, u32[]{:S(2)}, u32[]{:S(2)}) collective-permute-start(bf16[128,1024]{1,0:T(8,128)(2,1)S(1)} %fusion.35), channel_id=1, source_target_pairs={{0,8},{2,10},{4,12},{6,14},{8,0},{10,2},{12,4},{14,6},{16,24},{18,... | collective-permute-start | bytes 786440 | tf_op jit(solution)/shard_map/ppermute | solution.py:343
  271.4 3.3 collective-permute-done.41
  274.8 2.9 collective-permute-start.42
  278.0 6.1 %collective-permute-start.38 = (bf16[128,1024]{1,0:T(8,128)(2,1)S(1)}, bf16[128,1024]{1,0:T(8,128)(2,1)S(1)}, u32[]{:S(2)}, u32[]{:S(2)}) collective-permute-start(bf16[128,1024]{1,0:T(8,128)(2,1)S(1)} %fusion.20), channel_id=1, source_target_pairs={{0,16},{2,18},{4,20},{6,22},{8,24},{10,26},{12,28},{14,30},{16,0},... | collective-permute-start | bytes 786440 | tf_op jit(solution)/shard_map/ppermute | solution.py:343
  284.1 13.4 %shard_map.113 = (f32[16,512]{1,0:T(8,128)}, f32[512,128]{1,0:T(8,128)}, f32[512,128]{1,0:T(8,128)}) custom-call(f32[32,512]{1,0:T(8,128)} %get-tuple-element.22.r_ref, f32[4,512,8]{2,1,0:T(8,128)} %get-tuple-element.23.rt_ref, bf16[512,2048]{1,0:T(8,128)(2,1)} %g_ref.11, bf16[512,1024]{1,0:T(8,128)(2,1)} %get-tuple-element.27.x_ref, ...), custom_call_target="tpu_custom_call" | custom-call | flops 1610612736 | bytes 3145728 | tf_op jit(solution)/shard_map/pallas_call | solution.py:575
  297.8 1.0 fusion.13.s_ref
  298.8 5.5 %shard_map.114 = (f32[16,512]{1,0:T(8,128)}, f32[512,128]{1,0:T(8,128)}) custom-call(f32[4,512,8]{2,1,0:T(8,128)} %get-tuple-element.23.rt_ref, bf16[512,2048]{1,0:T(8,128)(2,1)} %g_ref.11, bf16[512,128]{1,0:T(8,128)(2,1)} %c_ref.11, f32[128,1024]{1,0:T(8,128)} %fusion.13.s_ref, f32[2,128,1024]{2,1,0:T(8,128)} %get-tuple-element.29.e_ref, ...), custom_call_target="tpu_custom_call" | custom-call | flops 268435456 | bytes 3145728 | tf_op jit(solution)/shard_map/pallas_call | solution.py:594
  304.3 13.9 %shard_map.115 = (f32[16,512]{1,0:T(8,128)}, f32[512,128]{1,0:T(8,128)}, f32[512,128]{1,0:T(8,128)}) custom-call(f32[32,512]{1,0:T(8,128)} %get-tuple-element.22.r_ref, f32[4,512,8]{2,1,0:T(8,128)} %get-tuple-element.23.rt_ref, bf16[512,2048]{1,0:T(8,128)(2,1)} %g_ref.11, bf16[512,1024]{1,0:T(8,128)(2,1)} %get-tuple-element.26.x_ref, ...), custom_call_target="tpu_custom_call" | custom-call | flops 1610612736 | bytes 3145728 | tf_op jit(solution)/shard_map/pallas_call | solution.py:575
  318.2 1.0 fusion.23.s_ref
  319.2 5.7 %shard_map.116 = (f32[16,512]{1,0:T(8,128)}, f32[512,128]{1,0:T(8,128)}) custom-call(f32[4,512,8]{2,1,0:T(8,128)} %get-tuple-element.23.rt_ref, bf16[512,2048]{1,0:T(8,128)(2,1)} %g_ref.11, bf16[512,128]{1,0:T(8,128)(2,1)} %c_ref.11, f32[128,1024]{1,0:T(8,128)} %fusion.23.s_ref, f32[2,128,1024]{2,1,0:T(8,128)} %get-tuple-element.34.e_ref, ...), custom_call_target="tpu_custom_call" | custom-call | flops 268435456 | bytes 3145728 | tf_op jit(solution)/shard_map/pallas_call | solution.py:594
  326.0 3.9 %add_convert_fusion = bf16[512,2048]{1,0:T(8,128)(2,1)} fusion(bf16[512,2048]{1,0:T(8,128)(2,1)} %collective-permute-done.34, bf16[512,4096]{1,0:T(8,128)(2,1)S(1)} %copy-done), kind=kLoop, calls=%fused_computation | loop fusion | flops 4194304 | bytes 6291456 | tf_op jit(solution)/shard_map/convert_element_type | solution.py:392
  (154 shorter events, 19.8 us)
Async XLA Ops:
  7.2 220.1 %all-gather.2.cloned.1.call-start = ((), (), s32[]{:S(2)}) async-start(), calls=%async_computation | async-start | bytes 6291456 | tf_op jit(solution)/shard_map/all_gather | solution.py:481
  9.5 30.9 %collective-permute-start.10 = (bf16[256,1024]{1,0:T(8,128)(2,1)}, bf16[256,1024]{1,0:T(8,128)(2,1)S(1)}, u32[]{:S(2)}, u32[]{:S(2)}) collective-permute-start(bf16[256,1024]{1,0:T(8,128)(2,1)} %get-tuple-element.51), channel_id=1, source_target_pairs={{0,8},{2,10},{4,12},{6,14},{8,16},{10,18},{12,20},{14,22},{16,24},... | collective-permute-start | bytes 1572872 | tf_op jit(solution)/shard_map/ppermute | solution.py:411
  25.0 17.7 %copy-start.3 = (f32[2,128,2048]{2,1,0:T(8,128)S(1)}, f32[2,128,2048]{2,1,0:T(8,128)}, u32[]{:S(2)}) copy-start(f32[2,128,2048]{2,1,0:T(8,128)} %get-tuple-element.24) | copy-start | bytes 6291460
  25.0 17.7 %collective-permute-start = (bf16[128,2048]{1,0:T(8,128)(2,1)}, bf16[128,2048]{1,0:T(8,128)(2,1)S(1)}, u32[]{:S(2)}, u32[]{:S(2)}) collective-permute-start(bf16[128,2048]{1,0:T(8,128)(2,1)} %fusion.33), channel_id=1, source_target_pairs={{0,2},{2,0},{4,6},{6,4},{8,10},{10,8},{12,14},{14,12},{16,18},{18,... | collective-permute-start | bytes 1572872 | tf_op jit(solution)/shard_map/ppermute | solution.py:343
  26.4 38.0 %collective-permute-start.12 = (bf16[256,1024]{1,0:T(8,128)(2,1)}, bf16[256,1024]{1,0:T(8,128)(2,1)}, u32[]{:S(2)}, u32[]{:S(2)}) collective-permute-start(bf16[256,1024]{1,0:T(8,128)(2,1)} %get-tuple-element.51), channel_id=1, source_target_pairs={{0,16},{2,18},{4,20},{6,22},{8,24},{10,26},{12,28},{14,30},{16,0},... | collective-permute-start | bytes 1572872 | tf_op jit(solution)/shard_map/ppermute | solution.py:411
  29.0 36.0 %collective-permute-start.29 = (bf16[256,1024]{1,0:T(8,128)(2,1)}, bf16[256,1024]{1,0:T(8,128)(2,1)}, u32[]{:S(2)}, u32[]{:S(2)}) collective-permute-start(bf16[256,1024]{1,0:T(8,128)(2,1)} %get-tuple-element.51), channel_id=1, source_target_pairs={{0,24},{2,26},{4,28},{6,30},{8,0},{10,2},{12,4},{14,6},{16,8},{18,... | collective-permute-start | bytes 1572872 | tf_op jit(solution)/shard_map/ppermute | solution.py:411
  30.4 8.3 %collective-permute-start.1 = (f32[1,2048]{1,0:T(1,128)S(1)}, f32[1,2048]{1,0:T(1,128)S(1)}, u32[]{:S(2)}, u32[]{:S(2)}) collective-permute-start(f32[1,2048]{1,0:T(1,128)S(1)} %get-tuple-element.55), channel_id=1, source_target_pairs={{0,2},{2,0},{4,6},{6,4},{8,10},{10,8},{12,14},{14,12},{16,18},{18,... | collective-permute-start | bytes 24584 | tf_op jit(solution)/shard_map/ppermute | solution.py:343
  38.7 6.1 %collective-permute-start.3 = (f32[1,2048]{1,0:T(1,128)S(1)}, f32[1,2048]{1,0:T(1,128)S(1)}, u32[]{:S(2)}, u32[]{:S(2)}) collective-permute-start(f32[1,2048]{1,0:T(1,128)S(1)} %mul.415), channel_id=1, source_target_pairs={{0,4},{2,6},{4,0},{6,2},{8,12},{10,14},{12,8},{14,10},{16,20},{18,... | collective-permute-start | bytes 24584 | tf_op jit(solution)/shard_map/ppermute | solution.py:343
  41.1 25.4 %collective-permute-start.11 = (bf16[256,1024]{1,0:T(8,128)(2,1)}, bf16[256,1024]{1,0:T(8,128)(2,1)}, u32[]{:S(2)}, u32[]{:S(2)}) collective-permute-start(bf16[256,1024]{1,0:T(8,128)(2,1)} %shard_map.104), channel_id=1, source_target_pairs={{0,8},{2,10},{4,12},{6,14},{8,16},{10,18},{12,20},{14,22},{16,24},... | collective-permute-start | bytes 1572872 | tf_op jit(solution)/shard_map/ppermute | solution.py:411
  44.2 55.9 %copy-start.2 = (bf16[256,1024]{1,0:T(8,128)(2,1)S(1)}, bf16[256,1024]{1,0:T(8,128)(2,1)}, u32[]{:S(2)}) copy-start(bf16[256,1024]{1,0:T(8,128)(2,1)} %copy-done.1) | copy-start | bytes 1572868
  44.2 35.1 %collective-permute-start.2 = (bf16[128,2048]{1,0:T(8,128)(2,1)}, bf16[128,2048]{1,0:T(8,128)(2,1)}, u32[]{:S(2)}, u32[]{:S(2)}) collective-permute-start(bf16[128,2048]{1,0:T(8,128)(2,1)} %get-tuple-element.47), channel_id=1, source_target_pairs={{0,4},{2,6},{4,0},{6,2},{8,12},{10,14},{12,8},{14,10},{16,20},{18,... | collective-permute-start | bytes 1572872 | tf_op jit(solution)/shard_map/ppermute | solution.py:343
  44.8 69.6 %copy-start.32 = (s32[16]{0:T(128)}, s32[16]{0:T(128)S(1)}, u32[]{:S(2)}) copy-start(s32[16]{0:T(128)S(1)} %stack.76.order_ref) | copy-start | bytes 196
  44.8 17.8 %collective-permute-start.5 = (f32[1,2048]{1,0:T(1,128)S(1)}, f32[1,2048]{1,0:T(1,128)S(1)}, u32[]{:S(2)}, u32[]{:S(2)}) collective-permute-start(f32[1,2048]{1,0:T(1,128)S(1)} %mul.426), channel_id=1, source_target_pairs={{0,8},{2,10},{4,12},{6,14},{8,0},{10,2},{12,4},{14,6},{16,24},{18,... | collective-permute-start | bytes 24584 | tf_op jit(solution)/shard_map/ppermute | solution.py:343
  62.6 49.2 %collective-permute-start.8 = (bf16[256,2048]{1,0:T(8,128)(2,1)}, bf16[256,2048]{1,0:T(8,128)(2,1)S(1)}, u32[]{:S(2)}, u32[]{:S(2)}) collective-permute-start(bf16[256,2048]{1,0:T(8,128)(2,1)} %refs_0_.7), channel_id=1, source_target_pairs={{0,4},{2,6},{4,0},{6,2},{8,12},{10,14},{12,8},{14,10},{16,20},{18,... | collective-permute-start | bytes 3145736 | tf_op jit(solution)/shard_map/ppermute | solution.py:343
  64.5 17.3 %collective-permute-start.13 = (bf16[256,1024]{1,0:T(8,128)(2,1)}, bf16[256,1024]{1,0:T(8,128)(2,1)S(1)}, u32[]{:S(2)}, u32[]{:S(2)}) collective-permute-start(bf16[256,1024]{1,0:T(8,128)(2,1)} %collective-permute-done.12.refs_12_), channel_id=1, source_target_pairs={{0,2},{2,0},{4,6},{6,4},{8,10},{10,8},{12,14},{14,12},{16,18},{18,... | collective-permute-start | bytes 1572872 | tf_op jit(solution)/shard_map/ppermute | solution.py:343
  65.0 32.5 %collective-permute-start.14 = (bf16[256,1024]{1,0:T(8,128)(2,1)}, bf16[256,1024]{1,0:T(8,128)(2,1)S(1)}, u32[]{:S(2)}, u32[]{:S(2)}) collective-permute-start(bf16[256,1024]{1,0:T(8,128)(2,1)} %collective-permute-done.12.refs_12_), channel_id=1, source_target_pairs={{0,4},{2,6},{4,0},{6,2},{8,12},{10,14},{12,8},{14,10},{16,20},{18,... | collective-permute-start | bytes 1572872 | tf_op jit(solution)/shard_map/ppermute | solution.py:343
  66.5 33.6 %collective-permute-start.18 = (bf16[256,1024]{1,0:T(8,128)(2,1)}, bf16[256,1024]{1,0:T(8,128)(2,1)S(1)}, u32[]{:S(2)}, u32[]{:S(2)}) collective-permute-start(bf16[256,1024]{1,0:T(8,128)(2,1)} %shard_map.104), channel_id=1, source_target_pairs={{0,24},{2,26},{4,28},{6,30},{8,0},{10,2},{12,4},{14,6},{16,8},{18,... | collective-permute-start | bytes 1572872 | tf_op jit(solution)/shard_map/ppermute | solution.py:411
  79.3 32.0 %collective-permute-start.22 = (bf16[256,1024]{1,0:T(8,128)(2,1)}, bf16[256,1024]{1,0:T(8,128)(2,1)S(1)}, u32[]{:S(2)}, u32[]{:S(2)}) collective-permute-start(bf16[256,1024]{1,0:T(8,128)(2,1)} %shard_map.104), channel_id=1, source_target_pairs={{0,16},{2,18},{4,20},{6,22},{8,24},{10,26},{12,28},{14,30},{16,0},... | collective-permute-start | bytes 1572872 | tf_op jit(solution)/shard_map/ppermute | solution.py:411
  81.7 32.6 %copy-start.6 = (bf16[256,1024]{1,0:T(8,128)(2,1)}, bf16[256,1024]{1,0:T(8,128)(2,1)S(1)}, u32[]{:S(2)}) copy-start(bf16[256,1024]{1,0:T(8,128)(2,1)S(1)} %collective-permute-done.13.refs_2_.refs_13_) | copy-start | bytes 1572868
  81.7 40.0 %collective-permute-start.7 = (bf16[256,2048]{1,0:T(8,128)(2,1)}, bf16[256,2048]{1,0:T(8,128)(2,1)}, u32[]{:S(2)}, u32[]{:S(2)}) collective-permute-start(bf16[256,2048]{1,0:T(8,128)(2,1)} %refs_0_.7), channel_id=1, source_target_pairs={{0,2},{2,0},{4,6},{6,4},{8,10},{10,8},{12,14},{14,12},{16,18},{18,... | collective-permute-start | bytes 3145736 | tf_op jit(solution)/shard_map/ppermute | solution.py:343
  97.5 14.3 %copy-start.8 = (bf16[256,1024]{1,0:T(8,128)(2,1)}, bf16[256,1024]{1,0:T(8,128)(2,1)S(1)}, u32[]{:S(2)}) copy-start(bf16[256,1024]{1,0:T(8,128)(2,1)S(1)} %collective-permute-done.14.refs_3_.refs_14_) | copy-start | bytes 1572868
  97.5 21.7 %collective-permute-start.4 = (bf16[128,2048]{1,0:T(8,128)(2,1)}, bf16[128,2048]{1,0:T(8,128)(2,1)}, u32[]{:S(2)}, u32[]{:S(2)}) collective-permute-start(bf16[128,2048]{1,0:T(8,128)(2,1)} %fusion.32), channel_id=1, source_target_pairs={{0,8},{2,10},{4,12},{6,14},{8,0},{10,2},{12,4},{14,6},{16,24},{18,... | collective-permute-start | bytes 1572872 | tf_op jit(solution)/shard_map/ppermute | solution.py:343
  100.1 14.2 %copy-start.14 = (bf16[256,1024]{1,0:T(8,128)(2,1)}, bf16[256,1024]{1,0:T(8,128)(2,1)S(1)}, u32[]{:S(2)}) copy-start(bf16[256,1024]{1,0:T(8,128)(2,1)S(1)} %collective-permute-done.18.refs_0_) | copy-start | bytes 1572868
  100.1 23.1 %collective-permute-start.26 = (bf16[256,1024]{1,0:T(8,128)(2,1)S(1)}, bf16[256,1024]{1,0:T(8,128)(2,1)}, u32[]{:S(2)}, u32[]{:S(2)}) collective-permute-start(bf16[256,1024]{1,0:T(8,128)(2,1)S(1)} %copy-done.2), channel_id=1, source_target_pairs={{0,2},{2,0},{4,6},{6,4},{8,10},{10,8},{12,14},{14,12},{16,18},{18,... | collective-permute-start | bytes 1572872 | tf_op jit(solution)/shard_map/ppermute | solution.py:343
  111.3 15.0 %collective-permute-start.27 = (bf16[256,1024]{1,0:T(8,128)(2,1)S(1)}, bf16[256,1024]{1,0:T(8,128)(2,1)}, u32[]{:S(2)}, u32[]{:S(2)}) collective-permute-start(bf16[256,1024]{1,0:T(8,128)(2,1)S(1)} %copy-done.2), channel_id=1, source_target_pairs={{0,4},{2,6},{4,0},{6,2},{8,12},{10,14},{12,8},{14,10},{16,20},{18,... | collective-permute-start | bytes 1572872 | tf_op jit(solution)/shard_map/ppermute | solution.py:343
  112.8 24.7 %collective-permute-start.31 = (bf16[256,1024]{1,0:T(8,128)(2,1)}, bf16[256,1024]{1,0:T(8,128)(2,1)}, u32[]{:S(2)}, u32[]{:S(2)}) collective-permute-start(bf16[256,1024]{1,0:T(8,128)(2,1)} %collective-permute-done.29.refs_8_), channel_id=1, source_target_pairs={{0,4},{2,6},{4,0},{6,2},{8,12},{10,14},{12,8},{14,10},{16,20},{18,... | collective-permute-start | bytes 1572872 | tf_op jit(solution)/shard_map/ppermute | solution.py:343
  114.4 34.4 %copy-start.7 = (bf16[256,1024]{1,0:T(8,128)(2,1)S(1)}, bf16[256,1024]{1,0:T(8,128)(2,1)}, u32[]{:S(2)}) copy-start(bf16[256,1024]{1,0:T(8,128)(2,1)} %copy-done.6) | copy-start | bytes 1572868
  114.4 8.9 %copy-start.15 = (bf16[256,1024]{1,0:T(8,128)(2,1)S(1)}, bf16[256,1024]{1,0:T(8,128)(2,1)}, u32[]{:S(2)}) copy-start(bf16[256,1024]{1,0:T(8,128)(2,1)} %shard_map.106.refs_8_) | copy-start | bytes 1572868
  114.4 11.9 %copy-start.17 = (bf16[256,1024]{1,0:T(8,128)(2,1)S(1)}, bf16[256,1024]{1,0:T(8,128)(2,1)}, u32[]{:S(2)}) copy-start(bf16[256,1024]{1,0:T(8,128)(2,1)} %shard_map.107.refs_12_) | copy-start | bytes 1572868
  114.4 26.2 %copy-start.10 = (bf16[256,2048]{1,0:T(8,128)(2,1)S(1)}, bf16[256,2048]{1,0:T(8,128)(2,1)}, u32[]{:S(2)}) copy-start(bf16[256,2048]{1,0:T(8,128)(2,1)} %copy-done.9) | copy-start | bytes 3145732
  114.4 45.1 %copy-start.13 = (bf16[128,2048]{1,0:T(8,128)(2,1)S(1)}, bf16[128,2048]{1,0:T(8,128)(2,1)}, u32[]{:S(2)}) copy-start(bf16[128,2048]{1,0:T(8,128)(2,1)} %copy-done.12) | copy-start | bytes 1572868
  119.2 21.4 %collective-permute-start.30 = (bf16[256,1024]{1,0:T(8,128)(2,1)}, bf16[256,1024]{1,0:T(8,128)(2,1)}, u32[]{:S(2)}, u32[]{:S(2)}) collective-permute-start(bf16[256,1024]{1,0:T(8,128)(2,1)} %collective-permute-done.29.refs_8_), channel_id=1, source_target_pairs={{0,2},{2,0},{4,6},{6,4},{8,10},{10,8},{12,14},{14,12},{16,18},{18,... | collective-permute-start | bytes 1572872 | tf_op jit(solution)/shard_map/ppermute | solution.py:343
  121.7 23.9 %collective-permute-start.15 = (bf16[256,1024]{1,0:T(8,128)(2,1)}, bf16[256,1024]{1,0:T(8,128)(2,1)}, u32[]{:S(2)}, u32[]{:S(2)}) collective-permute-start(bf16[256,1024]{1,0:T(8,128)(2,1)} %shard_map.105.refs_4_), channel_id=1, source_target_pairs={{0,2},{2,0},{4,6},{6,4},{8,10},{10,8},{12,14},{14,12},{16,18},{18,... | collective-permute-start | bytes 1572872 | tf_op jit(solution)/shard_map/ppermute | solution.py:343
  123.2 25.5 %collective-permute-start.20 = (bf16[256,1024]{1,0:T(8,128)(2,1)S(1)}, bf16[256,1024]{1,0:T(8,128)(2,1)}, u32[]{:S(2)}, u32[]{:S(2)}) collective-permute-start(bf16[256,1024]{1,0:T(8,128)(2,1)S(1)} %copy-done.15), channel_id=1, source_target_pairs={{0,4},{2,6},{4,0},{6,2},{8,12},{10,14},{12,8},{14,10},{16,20},{18,... | collective-permute-start | bytes 1572872 | tf_op jit(solution)/shard_map/ppermute | solution.py:343
  126.3 30.4 %collective-permute-start.23 = (bf16[256,1024]{1,0:T(8,128)(2,1)S(1)}, bf16[256,1024]{1,0:T(8,128)(2,1)S(1)}, u32[]{:S(2)}, u32[]{:S(2)}) collective-permute-start(bf16[256,1024]{1,0:T(8,128)(2,1)S(1)} %copy-done.17), channel_id=1, source_target_pairs={{0,2},{2,0},{4,6},{6,4},{8,10},{10,8},{12,14},{14,12},{16,18},{18,... | collective-permute-start | bytes 1572872 | tf_op jit(solution)/shard_map/ppermute | solution.py:343
  137.5 21.7 %collective-permute-start.6 = (bf16[128,2048]{1,0:T(8,128)(2,1)S(1)}, bf16[128,2048]{1,0:T(8,128)(2,1)S(1)}, u32[]{:S(2)}, u32[]{:S(2)}) collective-permute-start(bf16[128,2048]{1,0:T(8,128)(2,1)S(1)} %fusion.8), channel_id=1, source_target_pairs={{0,16},{2,18},{4,20},{6,22},{8,24},{10,26},{12,28},{14,30},{16,0},... | collective-permute-start | bytes 1572872 | tf_op jit(solution)/shard_map/ppermute | solution.py:343
  140.6 50.4 %collective-permute-start.9 = (bf16[256,2048]{1,0:T(8,128)(2,1)S(1)}, bf16[256,2048]{1,0:T(8,128)(2,1)S(1)}, u32[]{:S(2)}, u32[]{:S(2)}) collective-permute-start(bf16[256,2048]{1,0:T(8,128)(2,1)S(1)} %copy-done.10), channel_id=1, source_target_pairs={{0,2},{2,0},{4,6},{6,4},{8,10},{10,8},{12,14},{14,12},{16,18},{18,... | collective-permute-start | bytes 3145736 | tf_op jit(solution)/shard_map/ppermute | solution.py:343
  145.6 16.7 %collective-permute-start.16 = (bf16[256,1024]{1,0:T(8,128)(2,1)}, bf16[256,1024]{1,0:T(8,128)(2,1)S(1)}, u32[]{:S(2)}, u32[]{:S(2)}) collective-permute-start(bf16[256,1024]{1,0:T(8,128)(2,1)} %shard_map.105.refs_4_), channel_id=1, source_target_pairs={{0,4},{2,6},{4,0},{6,2},{8,12},{10,14},{12,8},{14,10},{16,20},{18,... | collective-permute-start | bytes 1572872 | tf_op jit(solution)/shard_map/ppermute | solution.py:343
  148.8 32.4 %collective-permute-start.33 = (bf16[256,1024]{1,0:T(8,128)(2,1)S(1)}, bf16[256,1024]{1,0:T(8,128)(2,1)S(1)}, u32[]{:S(2)}, u32[]{:S(2)}) collective-permute-start(bf16[256,1024]{1,0:T(8,128)(2,1)S(1)} %copy-done.7), channel_id=1, source_target_pairs={{0,4},{2,6},{4,0},{6,2},{8,12},{10,14},{12,8},{14,10},{16,20},{18,... | collective-permute-start | bytes 1572872 | tf_op jit(solution)/shard_map/ppermute | solution.py:343
  156.7 34.3 %copy-start.20 = (bf16[256,1024]{1,0:T(8,128)(2,1)}, bf16[256,1024]{1,0:T(8,128)(2,1)S(1)}, u32[]{:S(2)}) copy-start(bf16[256,1024]{1,0:T(8,128)(2,1)S(1)} %collective-permute-done.23.refs_13_) | copy-start | bytes 1572868
  156.7 23.6 %collective-permute-start.28 = (bf16[256,1024]{1,0:T(8,128)(2,1)}, bf16[256,1024]{1,0:T(8,128)(2,1)S(1)}, u32[]{:S(2)}, u32[]{:S(2)}) collective-permute-start(bf16[256,1024]{1,0:T(8,128)(2,1)} %collective-permute-done.26.refs_5_), channel_id=1, source_target_pairs={{0,4},{2,6},{4,0},{6,2},{8,12},{10,14},{12,8},{14,10},{16,20},{18,... | collective-permute-start | bytes 1572872 | tf_op jit(solution)/shard_map/ppermute | solution.py:343
  159.2 31.2 %collective-permute-start.32 = (bf16[256,1024]{1,0:T(8,128)(2,1)}, bf16[256,1024]{1,0:T(8,128)(2,1)S(1)}, u32[]{:S(2)}, u32[]{:S(2)}) collective-permute-start(bf16[256,1024]{1,0:T(8,128)(2,1)} %collective-permute-done.31.refs_10_), channel_id=1, source_target_pairs={{0,2},{2,0},{4,6},{6,4},{8,10},{10,8},{12,14},{14,12},{16,18},{18,... | collective-permute-start | bytes 1572872 | tf_op jit(solution)/shard_map/ppermute | solution.py:343
  162.3 30.1 %copy-start.21 = (bf16[256,1024]{1,0:T(8,128)(2,1)}, bf16[256,1024]{1,0:T(8,128)(2,1)S(1)}, u32[]{:S(2)}) copy-start(bf16[256,1024]{1,0:T(8,128)(2,1)S(1)} %collective-permute-done.16.refs_6_) | copy-start | bytes 1572868
  162.3 49.2 %collective-permute-start.19 = (bf16[256,1024]{1,0:T(8,128)(2,1)S(1)}, bf16[256,1024]{1,0:T(8,128)(2,1)S(1)}, u32[]{:S(2)}, u32[]{:S(2)}) collective-permute-start(bf16[256,1024]{1,0:T(8,128)(2,1)S(1)} %copy-done.15), channel_id=1, source_target_pairs={{0,2},{2,0},{4,6},{6,4},{8,10},{10,8},{12,14},{14,12},{16,18},{18,... | collective-permute-start | bytes 1572872 | tf_op jit(solution)/shard_map/ppermute | solution.py:343
  180.4 12.0 %copy-start.23 = (bf16[256,1024]{1,0:T(8,128)(2,1)}, bf16[256,1024]{1,0:T(8,128)(2,1)S(1)}, u32[]{:S(2)}) copy-start(bf16[256,1024]{1,0:T(8,128)(2,1)S(1)} %collective-permute-done.28.refs_7_) | copy-start | bytes 1572868
  180.4 31.2 %collective-permute-start.24 = (bf16[256,1024]{1,0:T(8,128)(2,1)S(1)}, bf16[256,1024]{1,0:T(8,128)(2,1)S(1)}, u32[]{:S(2)}, u32[]{:S(2)}) collective-permute-start(bf16[256,1024]{1,0:T(8,128)(2,1)S(1)} %copy-done.17), channel_id=1, source_target_pairs={{0,4},{2,6},{4,0},{6,2},{8,12},{10,14},{12,8},{14,10},{16,20},{18,... | collective-permute-start | bytes 1572872 | tf_op jit(solution)/shard_map/ppermute | solution.py:343
  181.1 11.3 %copy-start.22 = (bf16[256,1024]{1,0:T(8,128)(2,1)}, bf16[256,1024]{1,0:T(8,128)(2,1)S(1)}, u32[]{:S(2)}) copy-start(bf16[256,1024]{1,0:T(8,128)(2,1)S(1)} %collective-permute-done.33.refs_15_) | copy-start | bytes 1572868
  181.1 30.4 %collective-permute-start.17 = (bf16[256,1024]{1,0:T(8,128)(2,1)}, bf16[256,1024]{1,0:T(8,128)(2,1)S(1)}, u32[]{:S(2)}, u32[]{:S(2)}) collective-permute-start(bf16[256,1024]{1,0:T(8,128)(2,1)} %collective-permute-done.15.refs_5_), channel_id=1, source_target_pairs={{0,4},{2,6},{4,0},{6,2},{8,12},{10,14},{12,8},{14,10},{16,20},{18,... | collective-permute-start | bytes 1572872 | tf_op jit(solution)/shard_map/ppermute | solution.py:343
  190.4 21.1 %collective-permute-start.21 = (bf16[256,1024]{1,0:T(8,128)(2,1)}, bf16[256,1024]{1,0:T(8,128)(2,1)S(1)}, u32[]{:S(2)}, u32[]{:S(2)}) collective-permute-start(bf16[256,1024]{1,0:T(8,128)(2,1)} %collective-permute-done.20.refs_10_), channel_id=1, source_target_pairs={{0,2},{2,0},{4,6},{6,4},{8,10},{10,8},{12,14},{14,12},{16,18},{18,... | collective-permute-start | bytes 1572872 | tf_op jit(solution)/shard_map/ppermute | solution.py:343
  191.0 11.3 %copy-start.11 = (bf16[256,2048]{1,0:T(8,128)(2,1)}, bf16[256,2048]{1,0:T(8,128)(2,1)S(1)}, u32[]{:S(2)}) copy-start(bf16[256,2048]{1,0:T(8,128)(2,1)S(1)} %collective-permute-done.9.refs_3_) | copy-start | bytes 3145732
  191.0 21.7 %collective-permute-start.25 = (bf16[256,1024]{1,0:T(8,128)(2,1)S(1)}, bf16[256,1024]{1,0:T(8,128)(2,1)S(1)}, u32[]{:S(2)}, u32[]{:S(2)}) collective-permute-start(bf16[256,1024]{1,0:T(8,128)(2,1)S(1)} %collective-permute-done.23.refs_13_), channel_id=1, source_target_pairs={{0,4},{2,6},{4,0},{6,2},{8,12},{10,14},{12,8},{14,10},{16,20},{18,... | collective-permute-start | bytes 1572872 | tf_op jit(solution)/shard_map/ppermute | solution.py:343
  227.3 98.7 %collective-permute-start.34 = (bf16[512,2048]{1,0:T(8,128)(2,1)}, bf16[512,2048]{1,0:T(8,128)(2,1)}, u32[]{:S(2)}, u32[]{:S(2)}) collective-permute-start(bf16[512,2048]{1,0:T(8,128)(2,1)} %slice.132), channel_id=1, source_target_pairs={{0,1},{1,0},{2,3},{3,2},{4,5},{5,4},{6,7},{7,6},{8,9},{9,8},{10,11... | collective-permute-start | bytes 6291464 | tf_op jit(solution)/shard_map/ppermute | solution.py:343
  244.7 14.3 %copy-start.5 = (f32[2,128,1024]{2,1,0:T(8,128)S(1)}, f32[2,128,1024]{2,1,0:T(8,128)}, u32[]{:S(2)}) copy-start(f32[2,128,1024]{2,1,0:T(8,128)} %get-tuple-element.29.e_ref) | copy-start | bytes 3145732
  244.7 14.3 %collective-permute-start.35 = (bf16[128,1024]{1,0:T(8,128)(2,1)S(1)}, bf16[128,1024]{1,0:T(8,128)(2,1)S(1)}, u32[]{:S(2)}, u32[]{:S(2)}) collective-permute-start(bf16[128,1024]{1,0:T(8,128)(2,1)S(1)} %fusion.36), channel_id=1, source_target_pairs={{0,2},{2,0},{4,6},{6,4},{8,10},{10,8},{12,14},{14,12},{16,18},{18,... | collective-permute-start | bytes 786440 | tf_op jit(solution)/shard_map/ppermute | solution.py:343
  257.0 9.9 %copy-start.4 = (f32[2,128,1024]{2,1,0:T(8,128)S(1)}, f32[2,128,1024]{2,1,0:T(8,128)}, u32[]{:S(2)}) copy-start(f32[2,128,1024]{2,1,0:T(8,128)} %get-tuple-element.34.e_ref) | copy-start | bytes 3145732
  258.4 8.5 %collective-permute-start.40 = (bf16[128,1024]{1,0:T(8,128)(2,1)S(1)}, bf16[128,1024]{1,0:T(8,128)(2,1)S(1)}, u32[]{:S(2)}, u32[]{:S(2)}) collective-permute-start(bf16[128,1024]{1,0:T(8,128)(2,1)S(1)} %fusion.37), channel_id=1, source_target_pairs={{0,2},{2,0},{4,6},{6,4},{8,10},{10,8},{12,14},{14,12},{16,18},{18,... | collective-permute-start | bytes 786440 | tf_op jit(solution)/shard_map/ppermute | solution.py:343
  259.1 8.4 %collective-permute-start.36 = (bf16[128,1024]{1,0:T(8,128)(2,1)S(1)}, bf16[128,1024]{1,0:T(8,128)(2,1)S(1)}, u32[]{:S(2)}, u32[]{:S(2)}) collective-permute-start(bf16[128,1024]{1,0:T(8,128)(2,1)S(1)} %get-tuple-element.45), channel_id=1, source_target_pairs={{0,4},{2,6},{4,0},{6,2},{8,12},{10,14},{12,8},{14,10},{16,20},{18,... | collective-permute-start | bytes 786440 | tf_op jit(solution)/shard_map/ppermute | solution.py:343
  267.0 7.7 %collective-permute-start.41 = (bf16[128,1024]{1,0:T(8,128)(2,1)S(1)}, bf16[128,1024]{1,0:T(8,128)(2,1)S(1)}, u32[]{:S(2)}, u32[]{:S(2)}) collective-permute-start(bf16[128,1024]{1,0:T(8,128)(2,1)S(1)} %get-tuple-element.40), channel_id=1, source_target_pairs={{0,4},{2,6},{4,0},{6,2},{8,12},{10,14},{12,8},{14,10},{16,20},{18,... | collective-permute-start | bytes 786440 | tf_op jit(solution)/shard_map/ppermute | solution.py:343
  267.7 10.1 %collective-permute-start.37 = (bf16[128,1024]{1,0:T(8,128)(2,1)S(1)}, bf16[128,1024]{1,0:T(8,128)(2,1)S(1)}, u32[]{:S(2)}, u32[]{:S(2)}) collective-permute-start(bf16[128,1024]{1,0:T(8,128)(2,1)S(1)} %fusion.35), channel_id=1, source_target_pairs={{0,8},{2,10},{4,12},{6,14},{8,0},{10,2},{12,4},{14,6},{16,24},{18,... | collective-permute-start | bytes 786440 | tf_op jit(solution)/shard_map/ppermute | solution.py:343
  274.8 22.7 %collective-permute-start.42 = (bf16[128,1024]{1,0:T(8,128)(2,1)S(1)}, bf16[128,1024]{1,0:T(8,128)(2,1)S(1)}, u32[]{:S(2)}, u32[]{:S(2)}) collective-permute-start(bf16[128,1024]{1,0:T(8,128)(2,1)S(1)} %fusion.34), channel_id=1, source_target_pairs={{0,8},{2,10},{4,12},{6,14},{8,0},{10,2},{12,4},{14,6},{16,24},{18,... | collective-permute-start | bytes 786440 | tf_op jit(solution)/shard_map/ppermute | solution.py:343
  278.0 19.8 %collective-permute-start.38 = (bf16[128,1024]{1,0:T(8,128)(2,1)S(1)}, bf16[128,1024]{1,0:T(8,128)(2,1)S(1)}, u32[]{:S(2)}, u32[]{:S(2)}) collective-permute-start(bf16[128,1024]{1,0:T(8,128)(2,1)S(1)} %fusion.20), channel_id=1, source_target_pairs={{0,16},{2,18},{4,20},{6,22},{8,24},{10,26},{12,28},{14,30},{16,0},... | collective-permute-start | bytes 786440 | tf_op jit(solution)/shard_map/ppermute | solution.py:343
  297.7 20.5 %collective-permute-start.43 = (bf16[128,1024]{1,0:T(8,128)(2,1)S(1)}, bf16[128,1024]{1,0:T(8,128)(2,1)S(1)}, u32[]{:S(2)}, u32[]{:S(2)}) collective-permute-start(bf16[128,1024]{1,0:T(8,128)(2,1)S(1)} %fusion.30), channel_id=1, source_target_pairs={{0,16},{2,18},{4,20},{6,22},{8,24},{10,26},{12,28},{14,30},{16,0},... | collective-permute-start | bytes 786440 | tf_op jit(solution)/shard_map/ppermute | solution.py:343
  325.9 5.1 %collective-permute-start.44 = (bf16[512,128]{1,0:T(8,128)(2,1)S(1)}, bf16[512,128]{1,0:T(8,128)(2,1)S(1)}, u32[]{:S(2)}, u32[]{:S(2)}) collective-permute-start(bf16[512,128]{1,0:T(8,128)(2,1)S(1)} %convert_element_type.137), channel_id=1, source_target_pairs={{0,1},{1,0},{2,3},{3,2},{4,5},{5,4},{6,7},{7,6},{8,9},{9,8},{10,11... | collective-permute-start | bytes 393224 | tf_op jit(solution)/shard_map/ppermute | solution.py:343
  329.9 1.9 collective-permute-start.39
  (16 other events, 43.1 us)
Sparse Core Ops, SparseCore 0:
  30.5 11.0 all-gather.1

commit v2 on v1

--- a/solution.py
+++ b/solution.py
@@ -112,89 +112,156 @@
         out_ref[:, lanes] = total.astype(BF16)
 
 
-def arrange_kernel(unit, order_ref, f_ref, out_ref):
-    for index in range(f_ref.shape[1] // unit):
+def forward_kernel(half_ref, own_ref, other_ref, w_ref, rt_ref, b_ref, x_ref, e_ref, total_ref):
+    step = pl.program_id(1)
+
+    @pl.when(step == 0)
+    def _():
+        total_ref[...] = jnp.zeros_like(total_ref)
+
+    half = pl.num_programs(1) // 2
+
+    @pl.when(step < half)
+    def _():
+        total_ref[...] += mm(own_ref[...], w_ref[...])
+
+    @pl.when(step >= half)
+    def _():
+        total_ref[...] += mm(other_ref[...], w_ref[...])
+
+    @pl.when(step == pl.num_programs(1) - 1)
+    def _():
+        x = total_ref[...].astype(BF16)
+        x_ref[...] = x
+        for k in range(e_ref.shape[0]):
+            rows = slice(k * SPAN, (k + 1) * SPAN)
+            columns = rt_ref[0, rows]
+            to_end = jnp.exp2(spread_columns(columns[SPAN - 1 : SPAN] - columns))
+            scaled = (x[rows].astype(F32) * to_end).astype(BF16)
+            e_ref[k] = dot(b_ref[rows], scaled, ((0,), (0,)))
+
+
+def product_kernel(has_before, has_other, half_ref, g_ref, w_ref, *refs):
+    refs = list(refs)
+    total = dot(g_ref[...], w_ref[...], ((1,), (1,)))
+    if has_before:
+        total = total + refs.pop(0)[...].astype(F32)
+    if has_other:
+        total = total.astype(BF16).astype(F32) + refs.pop(0)[...].astype(F32)
+    refs[0][...] = total.astype(BF16)
+
+
+def arrange_kernel(order_ref, own_ref, other_ref, out_ref, both_ref):
+    half = own_ref.shape[1]
+    both_ref[:, :half] = own_ref[...]
+    both_ref[:, half:] = other_ref[...]
+    unit = out_ref.shape[1] // order_ref.shape[0]
+    for index in range(order_ref.shape[0]):
         source = pl.ds(pl.multiple_of(order_ref[index] * unit, 128), unit)
-        out_ref[:, index * unit : (index + 1) * unit] = f_ref[:, source]
-
-
-def fetch(arrays, places, buffer, sems):
+        out_ref[:, index * unit : (index + 1) * unit] = both_ref[:, source]
+
+
+def fetch(arrays, columns, buffer, sems):
     copies = []
-    at = 0
-    for index, (ref, column) in enumerate(zip(arrays, places)):
+    for index, (ref, column) in enumerate(zip(arrays, columns)):
         rows = ref.shape[0]
         source = ref.at[:, pl.ds(column, buffer.shape[1])]
-        copy = pltpu.make_async_copy(source, buffer.at[pl.ds(at, rows)], sems.at[index])
+        target = buffer.at[pl.ds(index * rows, rows)]
+        copy = pltpu.make_async_copy(source, target, sems.at[index])
         copy.start()
         copies.append(copy)
-        at += rows
     return copies
 
 
 def bundles(count):
-    return [range(at, min(at + PLANE, count)) for at in range(0, count, PLANE)]
-
-
-def forward_kernel(places, f_ref, rt_ref, b_ref, *refs):
-    count = len(places)
-    arrays, (x_ref, e_ref, buffer, sems) = refs[:count], refs[count:]
-    copies = fetch(arrays, places, buffer, sems)
+    return [range(at, at + PLANE) for at in range(0, count, PLANE)]
+
+
+def pieces_forward_kernel(columns_at, here, f_ref, rt_ref, b_ref, *refs):
+    count = len(columns_at)
+    arrays, (x_ref, e_ref, buffer, total_ref, features, sems, f_sems) = refs[:count], refs[count:]
     rows = arrays[0].shape[0]
-    total = None
-    for bundle in bundles(count):
+    f_copies = []
+    for index, bundle in enumerate(bundles(count)):
+        deep = pl.ds(bundle[0] * rows, PLANE * rows)
+        copy = pltpu.make_async_copy(f_ref.at[:, deep], features.at[:, deep], f_sems.at[index])
+        copy.start()
+        f_copies.append(copy)
+    copies = fetch(arrays, columns_at, buffer, sems)
+    groups = x_ref.shape[1] // WIDE
+    for number, bundle in enumerate(bundles(count)):
+        f_copies[number].wait()
         for index in bundle:
             copies[index].wait()
         deep = slice(bundle[0] * rows, (bundle[-1] + 1) * rows)
-        term = mm(f_ref[:, deep], buffer[deep])
-        total = term if total is None else total + term
-    x = total.astype(BF16)
-    x_ref[...] = x
-    for k in range(e_ref.shape[0]):
-        rows = slice(k * SPAN, (k + 1) * SPAN)
-        for group in range(rt_ref.shape[0]):
+        for group in range(groups):
             lanes = slice(group * WIDE, (group + 1) * WIDE)
-            columns = rt_ref[group, rows]
+            term = mm(features[:, deep], buffer[deep, lanes])
+            if number == 0:
+                total_ref[:, lanes] = term
+            else:
+                total_ref[:, lanes] += term
+    for group in range(groups):
+        lanes = slice(group * WIDE, (group + 1) * WIDE)
+        x = total_ref[:, lanes].astype(BF16)
+        x_ref[:, lanes] = x
+        for k in range(e_ref.shape[0]):
+            part = slice(k * SPAN, (k + 1) * SPAN)
+            columns = rt_ref[here + group, part]
             to_end = jnp.exp2(spread_columns(columns[SPAN - 1 : SPAN] - columns))
-            scaled = (x[rows, lanes].astype(F32) * to_end).astype(BF16)
-            e_ref[k, :, lanes] = dot(b_ref[rows], scaled, ((0,), (0,)))
-
-
-def product_kernel(places, has_before, order_ref, g_ref, *refs):
-    count = len(places)
+            scaled = (x[part].astype(F32) * to_end).astype(BF16)
+            e_ref[k, :, lanes] = dot(b_ref[part], scaled, ((0,), (0,)))
+
+
+def pieces_product_kernel(columns_at, last, order_ref, g_ref, *refs):
+    count = len(columns_at)
     arrays, refs = refs[:count], refs[count:]
-    if has_before:
-        before_ref, refs = refs[0], refs[1:]
-    out_ref, buffer, slots, sems, out_sems = refs[:5]
-    copies = fetch(arrays, places, buffer, sems)
+    if last:
+        before_ref, away_ref, own_ref = refs[:3]
+        buffer, slots, sems, out_sems, before_slots, before_sems = refs[3:]
+    else:
+        away_ref, buffer, slots, sems, out_sems = refs
+    copies = fetch(arrays, columns_at, buffer, sems)
     rows = arrays[0].shape[0]
-    where = [pl.ds(pl.multiple_of(order_ref[index] * rows, 128), rows) for index in range(count)]
-    if has_before:
-        before_slots, before_sems = refs[5:]
-        before = []
+    half = count // 2
+    before = []
+    if last:
         for index in range(count):
-            source = before_ref.at[:, where[index]]
+            source = before_ref.at[:, pl.ds(pl.multiple_of(order_ref[index] * rows, 128), rows)]
             copy = pltpu.make_async_copy(source, before_slots.at[index], before_sems.at[index])
             copy.start()
             before.append(copy)
     g = g_ref[...]
-    stores = []
     for bundle in bundles(count):
         for index in bundle:
             copies[index].wait()
         product = dot(g, buffer[bundle[0] * rows : (bundle[-1] + 1) * rows], ((1,), (1,)))
         for index in bundle:
-            part = product[:, (index - bundle[0]) * rows : (index - bundle[0] + 1) * rows]
-            if has_before:
+            at = (index - bundle[0]) * rows
+            part = product[:, at : at + rows]
+            place = order_ref[index]
+            if last:
                 before[index].wait()
                 part = part + before_slots[index].astype(F32)
             slots[index] = part.astype(BF16)
-            store = pltpu.make_async_copy(
-                slots.at[index], out_ref.at[:, where[index]], out_sems.at[index]
-            )
-            store.start()
-            stores.append(store)
-    for store in stores:
-        store.wait()
+            if last:
+                lanes = pl.ds(pl.multiple_of(place % half * rows, 128), rows)
+
+                @pl.when(place < half)
+                def _():
+                    target = away_ref.at[:, lanes]
+                    pltpu.make_async_copy(slots.at[index], target, out_sems.at[index]).start()
+
+                @pl.when(place >= half)
+                def _():
+                    target = own_ref.at[:, lanes]
+                    pltpu.make_async_copy(slots.at[index], target, out_sems.at[index]).start()
+            else:
+                target = away_ref.at[:, pl.ds(pl.multiple_of(place * rows, 128), rows)]
+                pltpu.make_async_copy(slots.at[index], target, out_sems.at[index]).start()
+    for index in range(count):
+        target = away_ref.at[:, pl.ds(0, rows)]
+        pltpu.make_async_copy(slots.at[index], target, out_sems.at[index]).wait()
 
 
 def after_kernel(*refs):
@@ -303,7 +370,7 @@
         scratch_shapes=list(scratch),
         cost_estimate=pl.CostEstimate(flops=flops, bytes_accessed=size, transcendentals=0),
         compiler_params=pltpu.CompilerParams(
-            dimension_semantics=("arbitrary",) * len(grid), vmem_limit_bytes=56 * 2**20
+            dimension_semantics=("arbitrary",) * len(grid), vmem_limit_bytes=48 * 2**20
         ),
     )
 
@@ -361,6 +428,38 @@
     return steps
 
 
+def gathered_products(running, spans):
+    count = lax.axis_size("ctx")
+    place = lax.axis_index("ctx")
+    heads = running.shape[0]
+    last = jnp.sum(running.reshape(heads, spans, SPAN)[:, :, SPAN - 1], axis=1)
+    every = lax.all_gather(last, "ctx")
+    index = jnp.arange(count)
+    masks = []
+    bits = []
+    bit = 1
+    while bit < count:
+        start = place // bit * bit
+        upper = (place & bit) != 0
+        beside = jnp.where(upper, start - bit, start + bit)
+        for low, high in (
+            (start, start + bit),
+            (beside, beside + bit),
+            (start, place),
+            (place + 1, start + bit),
+        ):
+            masks.append((index >= low) & (index < high))
+        bits.append((bit, upper))
+        bit *= 2
+    products = jnp.exp2(mm(jnp.stack(masks).astype(F32), every, EXACT))
+    products = jnp.repeat(products, P_SIZE, axis=1)
+    steps = []
+    for number, (bit, upper) in enumerate(bits):
+        rows = [products[at : at + 1] for at in range(4 * number, 4 * number + 4)]
+        steps.append((bit, upper, *rows))
+    return steps
+
+
 def scan_states(total, steps, reverse):
     entering = jnp.zeros_like(total)
     for bit, upper, kept, other, before_me, after_me in steps:
@@ -383,27 +482,19 @@
     return value
 
 
-def head_scatter(product):
-    count = lax.axis_size("head")
-    if count != 2:
-        return lax.psum_scatter(product, "head", scatter_dimension=1, tiled=True)
-    half = product.shape[1] // 2
-    got = swap(product[:, :half], "head", 1)
-    return (product[:, half:].astype(F32) + got.astype(F32)).astype(BF16)
-
-
 PLANE = 4
 
 
-def after(value, *tokens):
-    return pl.pallas_call(
+def after(values, *tokens):
+    out = pl.pallas_call(
         after_kernel,
-        in_specs=[ANYWHERE] * (1 + len(tokens)),
-        out_specs=ANYWHERE,
-        out_shape=shape(*value.shape, dtype=value.dtype),
-        input_output_aliases={0: 0},
+        in_specs=[ANYWHERE] * (len(values) + len(tokens)),
+        out_specs=[ANYWHERE] * len(values),
+        out_shape=[shape(*value.shape, dtype=value.dtype) for value in values],
+        input_output_aliases={index: index for index in range(len(values))},
         cost_estimate=pl.CostEstimate(flops=0, bytes_accessed=0, transcendentals=0),
-    )(value, *tokens)
+    )(*values, *tokens)
+    return list(out)
 
 
 def shift(value, by):
@@ -411,64 +502,392 @@
     return lax.ppermute(value, "ctx", [(i, (i + PLANE * by) % count) for i in range(count)])
 
 
-def gather_layered(w, sizes):
+def swap_x(value):
+    return swap(value, "ctx", 1)
+
+
+def swap_y(value):
+    return swap(value, "ctx", 2)
+
+
+def block_order():
     place = lax.axis_index("ctx")
     layers = lax.axis_size("ctx") // PLANE
     layer, spot = place // PLANE, place % PLANE
-    turns = (1, 3, 2)
-    own_x = swap(w, "ctx", 1)
-    own_y = swap(w, "ctx", 2)
-    own_across = swap(own_y, "ctx", 1)
-    chunks = []
-    tokens = ()
-    at = 0
-    for size in sizes:
-        part = w[:, at * P_SIZE : (at + size) * P_SIZE]
-        if tokens:
-            part = after(part, tokens[0])
-        arrays = [w, own_x, own_y, own_across]
-        places = [at * P_SIZE] * PLANE + [0] * (PLANE * len(turns))
-        moved = [shift(part, by) for by in turns]
-        if tokens:
-            moved = [after(value, *tokens) for value in moved]
-        for index, value in enumerate(moved):
-            value_x = swap(value, "ctx", 1)
-            value_y = swap(value, "ctx", 2)
-            if index == 1:
-                across = swap(value_y, "ctx", 1)
-            else:
-                across = swap(value_x, "ctx", 2)
-            arrays += [value, value_x, value_y, across]
-        tokens = (arrays[PLANE], arrays[-3], arrays[-2])
-        chunks.append((arrays, places))
-        at += size
-    order = jnp.stack(
+    order = [
+        (layer + layers - k) % layers * PLANE + (spot ^ flip)
+        for k in (0, 1, 3, 2)
+        for flip in range(PLANE)
+    ]
+    return jnp.stack(order).astype(jnp.int32)
+
+
+def gather_weight(w, sizes):
+    ends = [sum(sizes[: j + 1]) * P_SIZE for j in range(len(sizes))]
+    parts = [w[:, end - size * P_SIZE : end] for end, size in zip(ends, sizes)]
+    return [lax.all_gather(part, "ctx", axis=0, tiled=True) for part in parts]
+
+
+def forward(features, first, weight, running_t, b_rows, here):
+    own, other = features
+    length = own.shape[0]
+    n = b_rows.shape[1]
+    width, wide = weight.shape
+    deep = width // 4
+    spans = length // SPAN
+
+    def depth(k, first_ref):
+        return (k // 2 ^ first_ref[0]) * 2 + k % 2
+
+    return pl.pallas_call(
+        forward_kernel,
+        grid_spec=pltpu.PrefetchScalarGridSpec(
+            num_scalar_prefetch=1,
+            grid=(wide // WIDE, 4),
+            in_specs=[
+                pl.BlockSpec((length, deep), lambda h, k, first_ref: (0, jnp.minimum(k, 1))),
+                pl.BlockSpec((length, deep), lambda h, k, first_ref: (0, jnp.maximum(k - 2, 0))),
+                pl.BlockSpec((deep, WIDE), lambda h, k, first_ref: (depth(k, first_ref), h)),
+                pl.BlockSpec((1, length, GROUP), lambda h, k, first_ref: (h + here, 0, 0)),
+                pl.BlockSpec((length, n), lambda h, k, first_ref: (0, 0)),
+            ],
+            out_specs=[
+                pl.BlockSpec((length, WIDE), lambda h, k, first_ref: (0, h)),
+                pl.BlockSpec((spans, n, WIDE), lambda h, k, first_ref: (0, 0, h)),
+            ],
+            scratch_shapes=[pltpu.VMEM((length, WIDE), F32)],
+        ),
+        out_shape=[shape(length, wide, dtype=BF16), shape(spans, n, wide)],
+        cost_estimate=pl.CostEstimate(
+            flops=2 * length * wide * width, bytes_accessed=2 * wide * width, transcendentals=0
+        ),
+        compiler_params=pltpu.CompilerParams(
+            dimension_semantics=("arbitrary", "arbitrary"), vmem_limit_bytes=48 * 2**20
+        ),
+    )(first, own, other, weight, running_t, b_rows)
+
+
+def multiply(grad_x, weight, at, half, halves, before=None, other=None):
+    length = grad_x.shape[0]
+    width, wide = weight.shape
+    tiles = width // halves // WIDE
+    tile = pl.BlockSpec((length, WIDE), lambda j, half_ref: (0, half_ref[0] * tiles + j))
+    plain = pl.BlockSpec((length, WIDE), lambda j, half_ref: (0, j))
+    in_specs = [
+        pl.BlockSpec((length, wide), lambda j, half_ref: (0, at)),
+        pl.BlockSpec((WIDE, wide), lambda j, half_ref: (half_ref[0] * tiles + j, 0)),
+    ]
+    operands = [grad_x, weight]
+    if before is not None:
+        in_specs.append(tile)
+        operands.append(before)
+    if other is not None:
+        in_specs.append(plain)
+        operands.append(other)
+    return pl.pallas_call(
+        functools.partial(product_kernel, before is not None, other is not None),
+        grid_spec=pltpu.PrefetchScalarGridSpec(
+            num_scalar_prefetch=1,
+            grid=(tiles,),
+            in_specs=in_specs,
+            out_specs=plain,
+        ),
+        out_shape=shape(length, width // halves, dtype=BF16),
+        cost_estimate=pl.CostEstimate(
+            flops=2 * length * wide * width // halves,
+            bytes_accessed=2 * wide * width // halves,
+            transcendentals=0,
+        ),
+        compiler_params=pltpu.CompilerParams(
+            dimension_semantics=("arbitrary",), vmem_limit_bytes=48 * 2**20
+        ),
+    )(half, *operands)
+
+
+def pieces_forward(features, arrays, columns_at, wide, running_t, b_rows, here):
+    length, width = features.shape
+    n = b_rows.shape[1]
+    spans = length // SPAN
+    count = len(arrays)
+    return call(
+        functools.partial(pieces_forward_kernel, columns_at, here),
+        (1,),
         [
-            (layer + layers - k) % layers * PLANE + (spot ^ flip)
-            for k in (0,) + turns
-            for flip in range(PLANE)
+            ANYWHERE,
+            pl.BlockSpec(running_t.shape, lambda h: (0, 0, 0)),
+            pl.BlockSpec((length, n), lambda h: (0, 0)),
         ]
-    )
-    return chunks, order.astype(jnp.int32)
-
-
-def gather_plain(w, sizes):
-    chunks = []
-    at = 0
-    for size in sizes:
-        part = w[:, at * P_SIZE : (at + size) * P_SIZE]
-        chunks.append(([lax.all_gather(part, "ctx", axis=0, tiled=True)], [0]))
-        at += size
-    return chunks, jnp.zeros((1,), jnp.int32)
-
-
-def gather_weight(w, sizes):
-    if lax.axis_size("ctx") == 4 * PLANE and w.shape[0] % 256 == 0:
-        return gather_layered(w, sizes)
-    return gather_plain(w, sizes)
+        + [ANYWHERE] * count,
+        [
+            pl.BlockSpec((length, wide), lambda h: (0, 0)),
+            pl.BlockSpec((spans, n, wide), lambda h: (0, 0, 0)),
+        ],
+        [shape(length, wide, dtype=BF16), shape(spans, n, wide)],
+        2 * length * wide * width,
+        2 * wide * width,
+        [
+            pltpu.VMEM((width, wide), BF16),
+            pltpu.VMEM((length, wide), F32),
+            pltpu.VMEM((length, width), BF16),
+            pltpu.SemaphoreType.DMA((count,)),
+            pltpu.SemaphoreType.DMA((count // PLANE,)),
+        ],
+    )(features, running_t, b_rows, *arrays)
+
+
+def pieces_product(order, grad_x, arrays, columns_at, wide, at, before=None):
+    length = grad_x.shape[0]
+    count = len(arrays)
+    rows = arrays[0].shape[0]
+    width = rows * count
+    last = before is not None
+    scratch = [
+        pltpu.VMEM((width, wide), BF16),
+        pltpu.VMEM((count, length, rows), BF16),
+        pltpu.SemaphoreType.DMA((count,)),
+        pltpu.SemaphoreType.DMA((count,)),
+    ]
+    if last:
+        scratch += [pltpu.VMEM((count, length, rows), BF16), pltpu.SemaphoreType.DMA((count,))]
+    half = shape(length, width // 2, dtype=BF16)
+    return call(
+        functools.partial(pieces_product_kernel, columns_at, last),
+        (1,),
+        [SCALARS, pl.BlockSpec((length, wide), lambda h: (0, at))] + [ANYWHERE] * (count + last),
+        [ANYWHERE, ANYWHERE] if last else ANYWHERE,
+        [half, half] if last else shape(length, width, dtype=BF16),
+        2 * length * wide * width,
+        2 * wide * width,
+        scratch,
+    )(order, grad_x, *arrays, *([before] if last else []))
 
 
 def local(inputs, w_in, b_rows, c_rows, log_decay, skip_gain, grad_out):
+    groups = log_decay.shape[0] // GROUP
+    layered = lax.axis_size("ctx") == 4 * PLANE and lax.axis_size("head") == 2
+    if layered and groups >= 2 and w_in.shape[0] == 256:
+        return local_layered(inputs, w_in, b_rows, c_rows, log_decay, skip_gain, grad_out)
+    return local_plain(inputs, w_in, b_rows, c_rows, log_decay, skip_gain, grad_out)
+
+
+def prepare(log_decay, grad_out, c_rows):
+    length, columns = grad_out.shape
+    heads = log_decay.shape[0]
+    spans = length // SPAN
+    groups = heads // GROUP
+    n = c_rows.shape[1]
+    return call(
+        decay_kernel,
+        (spans, groups),
+        [run_spec(), rows_spec(), SHARED],
+        [run_spec(), run_t_spec(), kept_spec(), state_spec()],
+        [
+            shape(heads, length),
+            shape(groups, length, GROUP),
+            shape(spans, 8, columns),
+            shape(spans, n, columns),
+        ],
+        2 * length * columns * n,
+        6 * length * columns,
+    )(log_decay, grad_out, c_rows)
+
+
+def scan_step(total, entering, step, reverse):
+    bit, upper, kept, other, before_me, after_me = step
+    got = swap(total.astype(BF16), "ctx", bit).astype(F32)
+    if reverse:
+        entering = entering + jnp.where(upper, 0.0, after_me) * got
+        total = jnp.where(upper, got + other * total, total + kept * got)
+    else:
+        entering = entering + jnp.where(upper, before_me, 0.0) * got
+        total = jnp.where(upper, kept * got + total, other * total + got)
+    return total, entering
+
+
+def inner(grid, here, wide, operands, so_far):
+    length = operands[2].shape[0]
+    n = operands[4].shape[1]
+    specs = [
+        run_spec(here),
+        run_t_spec(here),
+        rows_spec(here),
+        rows_spec(),
+        SHARED,
+        SHARED,
+        state_spec(here),
+    ]
+    return call(
+        inner_kernel,
+        grid,
+        specs + [SHARED] * len(so_far),
+        [run_spec(), SHARED, SHARED],
+        [shape(wide // P_SIZE, length), shape(length, n), shape(length, n)],
+        12 * length * wide * SPAN,
+        6 * length * wide,
+        [pltpu.VMEM((SPAN, SPAN), F32)],
+    )(*operands, *so_far)
+
+
+def state_terms(grid, here, wide, operands):
+    length = operands[1].shape[0]
+    n = operands[2].shape[1]
+    return call(
+        state_kernel,
+        grid,
+        [
+            run_t_spec(here),
+            rows_spec(here),
+            SHARED,
+            pl.BlockSpec((n, WIDE), lambda k, h: (0, h)),
+            state_spec(),
+            state_spec(here),
+            kept_spec(here),
+            run_spec(),
+            SHARED,
+        ],
+        [run_spec(), SHARED],
+        [shape(wide // P_SIZE, length), shape(length, n)],
+        4 * length * wide * n,
+        6 * length * wide,
+        [pltpu.VMEM((grid[1], n, WIDE), F32)],
+    )(*operands)
+
+
+def local_layered(inputs, w_in, b_rows, c_rows, log_decay, skip_gain, grad_out):
+    length, columns = grad_out.shape
+    heads = log_decay.shape[0]
+    spans = length // SPAN
+    groups = heads // GROUP
+    place = lax.axis_index("head").astype(jnp.int32)
+    cut = columns - WIDE
+    w_a, w_b = w_in[:, :cut], w_in[:, cut:]
+    order = block_order()
+    blocks = order.shape[0]
+    width = blocks * w_in.shape[0]
+
+    z1a, z3a = shift(w_a, 1), shift(w_a, 3)
+    own_x, own_y = swap_x(w_in), swap_y(w_in)
+    other = swap(inputs, "head", 1)
+    running, running_t, kept, own_grads = prepare(log_decay, grad_out, c_rows)
+    steps = gathered_products(running, spans)
+    back = own_grads[spans - 1]
+    for k in range(spans - 2, -1, -1):
+        back = own_grads[k] + kept[k, :1] * back
+    leaving = jnp.zeros_like(back)
+    back = after([back], z1a, z3a)[0]
+
+    w_a, z1a, z3a = after([w_a, z1a, z3a], own_x, own_y, back)
+    z2a = shift(w_a, 2)
+    x1a, y1a, x3a, y3a = swap_x(z1a), swap_y(z1a), swap_x(z3a), swap_y(z3a)
+    back, leaving = scan_step(back, leaving, steps[0], True)
+
+    z2a, x1a, y3a = after([z2a, x1a, y3a], y1a, x3a, back, other)
+    x2a, y2a = swap_x(z2a), swap_y(z2a)
+    d1a, d3a = swap_y(x1a), swap_x(y3a)
+    back, leaving = scan_step(back, leaving, steps[1], True)
+
+    own_y, x2a, w_b = after([own_y, x2a, w_b], y2a, d1a, d3a, back)
+    own_d, d2a = swap_x(own_y), swap_y(x2a)
+    z1b, z3b, z2b = shift(w_b, 1), shift(w_b, 3), shift(w_b, 2)
+    back, leaving = scan_step(back, leaving, steps[2], True)
+
+    order_own = (order + place * (blocks // 2)) % blocks
+    features = call(
+        arrange_kernel,
+        (1,),
+        [SCALARS] + [pl.BlockSpec((length, width // 2), lambda h: (0, 0))] * 2,
+        pl.BlockSpec((length, width), lambda h: (0, 0)),
+        shape(length, width, dtype=BF16),
+        0,
+        4 * length * width,
+        [pltpu.VMEM((length, width), BF16)],
+    )(order_own, inputs, other)
+
+    z1b, z3b, z2b, d2a = after([z1b, z3b, z2b, d2a], own_d, back, features)
+    x1b, x3b, x2b = swap_x(z1b), swap_x(z3b), swap_x(z2b)
+    y1b, y3b, y2b = swap_y(z1b), swap_y(z3b), swap_y(z2b)
+    back, leaving = scan_step(back, leaving, steps[3], True)
+    arrays_a = [w_in, own_x, own_y, own_d, z1a, x1a, y1a, d1a, z3a, x3a, y3a, d3a]
+    arrays_a += [z2a, x2a, y2a, d2a]
+    at_a = [0] * len(arrays_a)
+    x_a, states_a = pieces_forward(features, arrays_a, at_a, cut, running_t, b_rows, 0)
+
+    leaving_all = [leaving]
+    for k in range(spans - 1, 0, -1):
+        leaving_all.insert(0, own_grads[k] + kept[k, :1] * leaving_all[0])
+    leaving_all = jnp.stack([value.astype(BF16) for value in leaving_all])
+    skip = jnp.repeat(skip_gain, P_SIZE)[None]
+    grad_x = grad_rows(running, running_t, grad_out, b_rows, c_rows, leaving_all, skip)
+
+    def forward_total(states, lanes):
+        total = states[0]
+        for k in range(1, spans):
+            total = kept[k, :1, lanes] * total + states[k]
+        return total
+
+    def narrow(step, lanes):
+        return step[:2] + tuple(value[:, lanes] for value in step[2:])
+
+    lanes_a, lanes_b = slice(0, cut), slice(cut, columns)
+    steps_a = [narrow(step, lanes_a) for step in steps]
+    steps_b = [narrow(step, lanes_b) for step in steps]
+    total_a = forward_total(states_a, lanes_a)
+    entering_a = jnp.zeros_like(total_a)
+    total_a, entering_a = scan_step(total_a, entering_a, steps_a[0], False)
+
+    x1b, y3b, x2b, x_a, grad_x = after([x1b, y3b, x2b, x_a, grad_x], x3b, y1b, y2b, total_a)
+    d1b, d3b, d2b = swap_y(x1b), swap_x(y3b), swap_y(x2b)
+    total_a, entering_a = scan_step(total_a, entering_a, steps_a[1], False)
+
+    shared = (running, running_t, grad_out)
+    order_away = (order + (1 - place) * (blocks // 2)) % blocks
+    grid_a, grid_b = (spans, groups - 1), (spans, 1)
+    inner_a = shared + (x_a, b_rows, c_rows, leaving_all)
+    decay_a, grad_b, grad_c = inner(grid_a, 0, cut, inner_a, ())
+    product = pieces_product(order_away, grad_x, arrays_a, at_a, cut, 0)
+
+    d1b, d3b, d2b = after([d1b, d3b, d2b], product, grad_b, total_a)
+    arrays_b = [w_in, own_x, own_y, own_d, z1b, x1b, y1b, d1b, z3b, x3b, y3b, d3b]
+    arrays_b += [z2b, x2b, y2b, d2b]
+    at_b = [cut] * PLANE + [0] * (len(arrays_b) - PLANE)
+    here = groups - 1
+    x_b, states_b = pieces_forward(features, arrays_b, at_b, WIDE, running_t, b_rows, here)
+    total_b = forward_total(states_b, lanes_b)
+    entering_b = jnp.zeros_like(total_b)
+    for step_a, step_b in zip(steps_a[2:] + [None] * 2, steps_b):
+        if step_a is not None:
+            total_a, entering_a = scan_step(total_a, entering_a, step_a, False)
+        total_b, entering_b = scan_step(total_b, entering_b, step_b, False)
+    inner_b = shared + (x_b, b_rows, c_rows, leaving_all)
+    decay_b, grad_b, grad_c = inner(grid_b, here, WIDE, inner_b, (grad_b, grad_c))
+    away, own = pieces_product(order_away, grad_x, arrays_b, at_b, WIDE, here, product)
+    got = swap(away, "head", 1)
+    grad_b = head_sum(grad_b)
+
+    common = (running_t, grad_out, c_rows)
+    state_a = common + (entering_a, states_a, leaving_all, kept, decay_a, grad_c)
+    decay_a, grad_c = state_terms(grid_a, 0, cut, state_a)
+    state_b = common + (entering_b, states_b, leaving_all, kept, decay_b, grad_c)
+    decay_b, grad_c = state_terms(grid_b, here, WIDE, state_b)
+    grad_inputs = (own.astype(F32) + got.astype(F32)).astype(BF16)
+    grad_log_decay = jnp.concatenate([decay_a, decay_b], axis=0)
+    return (grad_inputs, grad_b, head_sum(grad_c), grad_log_decay)
+
+
+def grad_rows(running, running_t, grad_out, b_rows, c_rows, leaving, skip):
+    length, columns = grad_out.shape
+    return call(
+        grad_x_kernel,
+        (length // SPAN, running_t.shape[0]),
+        [run_spec(), run_t_spec(), rows_spec(), SHARED, SHARED, state_spec(), GAIN],
+        rows_spec(),
+        shape(length, columns, dtype=BF16),
+        8 * length * columns * SPAN,
+        6 * length * columns,
+    )(running, running_t, grad_out, b_rows, c_rows, leaving, skip)
+
+
+def local_plain(inputs, w_in, b_rows, c_rows, log_decay, skip_gain, grad_out):
     length, columns = grad_out.shape
     heads = log_decay.shape[0]
     spans = length // SPAN
@@ -476,20 +895,18 @@
     n = b_rows.shape[1]
     grid = (spans, groups)
 
-    sizes = (heads // 2, heads // 2) if heads % (2 * GROUP) == 0 else (heads,)
-    chunks, order = gather_weight(w_in, sizes)
-    features = lax.all_gather(inputs, "head", axis=1, tiled=True)
-    width = features.shape[1]
-    unit = width // order.shape[0]
-    features = call(
-        functools.partial(arrange_kernel, unit),
-        (1,),
-        [SCALARS, pl.BlockSpec((length, width), lambda h: (0, 0))],
-        pl.BlockSpec((length, width), lambda h: (0, 0)),
-        shape(length, width, dtype=BF16),
-        0,
-        4 * length * width,
-    )(order, features)
+    sizes = (heads // 2, heads // 4, heads // 4) if heads % (4 * GROUP) == 0 else (heads,)
+    weights = gather_weight(w_in, sizes)
+    two = lax.axis_size("head") == 2
+    place = lax.axis_index("head").astype(jnp.int32)[None]
+    width = weights[0].shape[0]
+    if two:
+        features = (inputs, swap(inputs, "head", 1))
+        first = place
+    else:
+        features = lax.all_gather(inputs, "head", axis=1, tiled=True)
+        features = (features[:, : width // 2], features[:, width // 2 :])
+        first = jnp.zeros((1,), jnp.int32)
 
     running, running_t, kept, own_grads = call(
         decay_kernel,
@@ -530,39 +947,18 @@
         6 * length * columns,
     )(running, running_t, grad_out, b_rows, c_rows, leaving, skip)
 
-    two = lax.axis_size("head") == 2
-    product_order = order
-    if two:
-        blocks = order.shape[0]
-        product_order = (order + (1 - lax.axis_index("head")) * (blocks // 2)) % blocks
-
     grad_b = grad_c = product = None
+    tokens = ()
     decay_parts = []
     at = 0
     for index, size in enumerate(sizes):
         wide = size * P_SIZE
         here = at // GROUP
         count = size // GROUP
-        arrays, places = chunks[index]
-        pieces = len(arrays)
-        x, own_states = call(
-            functools.partial(forward_kernel, places),
-            (1,),
-            [
-                pl.BlockSpec((length, width), lambda h: (0, 0)),
-                pl.BlockSpec((count, length, GROUP), lambda h, here=here // count: (here, 0, 0)),
-                pl.BlockSpec((length, n), lambda h: (0, 0)),
-            ]
-            + [ANYWHERE] * pieces,
-            [
-                pl.BlockSpec((length, wide), lambda h: (0, 0)),
-                pl.BlockSpec((spans, n, wide), lambda h: (0, 0, 0)),
-            ],
-            [shape(length, wide, dtype=BF16), shape(spans, n, wide)],
-            2 * length * wide * width,
-            2 * wide * width,
-            [pltpu.VMEM((width, wide), BF16), pltpu.SemaphoreType.DMA((pieces,))],
-        )(features, running_t, b_rows, *arrays)
+        weight = weights[index]
+        if tokens:
+            weight = after([weight], *tokens)[0]
+        x, own_states = forward(features, first, weight, running_t, b_rows, here)
 
         chunk = slice(at * P_SIZE, at * P_SIZE + wide)
         total = own_states[0]
@@ -613,35 +1009,20 @@
         )(running_t, grad_out, c_rows, entering, own_states, leaving, kept, decay_part, grad_c)
         decay_parts.append(decay_part)
 
-        scratch = [
-            pltpu.VMEM((width, wide), BF16),
-            pltpu.VMEM((pieces, length, unit), BF16),
-            pltpu.SemaphoreType.DMA((pieces,)),
-            pltpu.SemaphoreType.DMA((pieces,)),
-        ]
-        earlier = ()
-        if product is not None:
-            earlier = (product,)
-            scratch += [
-                pltpu.VMEM((pieces, length, unit), BF16),
-                pltpu.SemaphoreType.DMA((pieces,)),
-            ]
-        product = call(
-            functools.partial(product_kernel, places, product is not None),
-            (1,),
-            [SCALARS, pl.BlockSpec((length, wide), lambda h, index=at // size: (0, index))]
-            + [ANYWHERE] * (pieces + len(earlier)),
-            ANYWHERE,
-            shape(length, width, dtype=BF16),
-            2 * length * wide * width,
-            2 * wide * width,
-            scratch,
-        )(product_order, grad_x, *arrays, *earlier)
+        if index < len(sizes) - 1:
+            zero = jnp.zeros((1,), jnp.int32)
+            product = multiply(grad_x, weight, at // size, zero, 1, product)
+            tokens = (product, grad_b, entering)
+        elif two:
+            sent = multiply(grad_x, weight, at // size, 1 - place, 2, product)
+            got = swap(sent, "head", 1)
+            grad_inputs = multiply(grad_x, weight, at // size, place, 2, product, got)
+        else:
+            zero = jnp.zeros((1,), jnp.int32)
+            product = multiply(grad_x, weight, at // size, zero, 1, product)
+            grad_inputs = lax.psum_scatter(product, "head", scatter_dimension=1, tiled=True)
         at += size
 
-    if two and order.shape[0] == 1:
-        product = jnp.roll(product, (1 - lax.axis_index("head")) * (width // 2), axis=1)
-    grad_inputs = head_scatter(product)
     return (grad_inputs, head_sum(grad_b), head_sum(grad_c), jnp.concatenate(decay_parts, axis=0))
 
 

time: 340 us -> 376 us (1.11)
  blocking collectives: 0 us -> 50.5 us
  local copies, waits for them, and re-layouts: 9.96 us -> 52.9 us
  starting transfers between devices: 70.5 us -> 47 us
  Pallas kernels: 104 us -> 87.4 us
  waiting for transfers between devices: 115 us -> 101 us
  between operations: 14.5 us -> 2.5 us
  other arithmetic: 25.1 us -> 33.3 us
    unnamed x0 -> x1, blocking collectives: none -> 50.5 us
    unnamed x68 -> x233, local copies, waits for them, and re-layouts: 2.92 us -> 38.5 us
    ppermute x39 -> x37, waiting for transfers between devices: 104 us -> 87.9 us  [swap(): return lax.ppermute(value, axis, [(i, i ^ bit) for i in range(count)])]
    pallas_call x15 -> x18, Pallas kernels: 104 us -> 87.4 us  [the longest x2 23 us: inner(): call(inner_kernel, grid, specs + [SHARED] * len(so_far), [run_spec(), SHA...]
    ppermute x6, starting transfers between devices: 21.3 us -> 7.32 us  [shift(): lax.ppermute(value, 'ctx', [(i, (i + PLANE * by) % count) for i in range(...]
    ppermute x39 -> x37, starting transfers between devices: 49.1 us -> 39.7 us  [swap(): return lax.ppermute(value, axis, [(i, i ^ bit) for i in range(count)])]
    broadcast_in_dim x1 -> x31, local copies, waits for them, and re-layouts: 0.07 us -> 4.19 us  [the longest x30 4.12 us: gathered_products(): products = jnp.repeat(products, P_SIZE, axis=1)]
    select_n x4 -> x9, other arithmetic: 0.58 us -> 4.4 us  [the longest x8 4.39 us: scan_step(): entering = entering + jnp.where(upper, before_me, 0.0) * got]
  transfers between devices with their start and end apart: 46 -> 43, of which waited for: 17 -> 14; matrix products, arithmetic and copies ran while one was open for 9% -> 11% of each run, Pallas kernels for 31% -> 22%
where the time goes in v2:
time: 376 us; the launch traced here: 375 us
  waiting for transfers between devices  101 us (27%)
  Pallas kernels  87.4 us (23%)
  local copies, waits for them, and re-layouts  52.9 us (14%)
  blocking collectives  50.5 us (13%)
  starting transfers between devices  47 us (12%)
  other arithmetic  33.3 us (9%)
    ppermute x37, waiting for transfers between devices, swap(): return lax.ppermute(value, axis, [(i, i ^ bit) for i in range(count)])  87.9 us
    unnamed x1, blocking collectives  50.5 us
    ppermute x37, starting transfers between devices, swap(): return lax.ppermute(value, axis, [(i, i ^ bit) for i in range(count)])  39.7 us
    unnamed x233, local copies, waits for them, and re-layouts  38.5 us
    pallas_call x2, Pallas kernels, inner(): call(inner_kernel, grid, specs + [SHARED] * len(so_far), [run_spec(), SHA...  23 us
    pallas_call x2, Pallas kernels, pieces_product(): call(functools.partial(pieces_product_kernel, columns_at, last), (1,), [S...  19.4 us
    pallas_call x2, Pallas kernels, pieces_forward(): call(functools.partial(pieces_forward_kernel, columns_at, here), (1,), [A...  18.4 us
    convert_element_type x12, other arithmetic, scan_step(): got = swap(total.astype(BF16), 'ctx', bit).astype(F32)  16.9 us
  transfers between devices with their start and end apart: 43, of which 14 were waited for; matrix products, arithmetic and copies ran while one was open for 11% of the time, Pallas kernels for 22%

profile of v2, /device:TPU:0, one launch (start us, length us, event | category | flops | bytes accessed | tf_op | source)
XLA Modules:
  0.0 374.5 jit_solution(10801748848201090186)
XLA Ops:
  0.6 2.1 slice.190.refs_0_
  2.8 5.0 %collective-permute-start.2 = (bf16[256,1536]{1,0:T(8,128)(2,1)}, bf16[256,1536]{1,0:T(8,128)(2,1)}, u32[]{:S(2)}, u32[]{:S(2)}) collective-permute-start(bf16[256,1536]{1,0:T(8,128)(2,1)} %slice.190.refs_0_), channel_id=1, source_target_pairs={{0,24},{2,26},{4,28},{6,30},{8,0},{10,2},{12,4},{14,6},{16,8},{18,... | collective-permute-start | bytes 2359304 | tf_op jit(solution)/shard_map/ppermute | solution.py:502
  7.8 1.5 collective-permute-start.3
  9.3 1.5 collective-permute-start
  11.0 1.6 copy-done
  14.3 7.0 %shard_map.102 = (f32[32,512]{1,0:T(8,128)S(1)}, f32[4,512,8]{2,1,0:T(8,128)S(1)}, f32[2,8,2048]{2,1,0:T(8,128)S(1)}, f32[2,128,2048]{2,1,0:T(8,128)S(1)}) custom-call(f32[32,512]{1,0:T(8,128)S(1)} %copy-done.80, bf16[512,2048]{1,0:T(8,128)(2,1)S(1)} %copy-done, bf16[512,128]{1,0:T(8,128)(2,1)S(1)} %copy-done.55), custom_call_target="tpu_custom_call" | custom-call | flops 268435456 | bytes 6291456 | tf_op jit(solution)/shard_map/pallas_call | solution.py:679
  22.3 1.3 copy-done.13
  25.6 50.5 %all-reduce = f32[512]{0:T(512)S(1)} all-reduce(f32[512]{0:T(512)S(1)} %dynamic-update-slice), channel_id=2, replica_groups=mesh['ctx'=16,'head'=2] {'ctx'}, use_global_device_ids=true, to_apply=%add | all-reduce | flops 512 | bytes 4096
  76.2 2.7 fusion.10.refs_0_
  78.9 2.1 convert_element_type.106
  82.9 7.7 %collective-permute-done.9 = bf16[128,2048]{1,0:T(8,128)(2,1)} collective-permute-done((bf16[128,2048]{1,0:T(8,128)(2,1)}, bf16[128,2048]{1,0:T(8,128)(2,1)}, u32[]{:S(2)}, u32[]{:S(2)}) %collective-permute-start.9) | collective-permute-done | bytes 524320 | tf_op jit(solution)/shard_map/ppermute | solution.py:410
  90.5 2.8 fusion.56
  93.9 2.0 collective-permute-start.7
  97.3 9.8 %collective-permute-done.15 = bf16[128,2048]{1,0:T(8,128)(2,1)} collective-permute-done((bf16[128,2048]{1,0:T(8,128)(2,1)}, bf16[128,2048]{1,0:T(8,128)(2,1)}, u32[]{:S(2)}, u32[]{:S(2)}) %collective-permute-start.15) | collective-permute-done | bytes 524320 | tf_op jit(solution)/shard_map/ppermute | solution.py:410
  107.4 3.2 collective-permute-start.6
  111.7 2.8 fusion.54
  114.5 5.1 %collective-permute-done.7.refs_3_.refs_6_ = bf16[256,1536]{1,0:T(8,128)(2,1)S(1)} collective-permute-done((bf16[256,1536]{1,0:T(8,128)(2,1)}, bf16[256,1536]{1,0:T(8,128)(2,1)S(1)}, u32[]{:S(2)}, u32[]{:S(2)}) %collective-permute-start.7) | collective-permute-done | bytes 786464 | tf_op jit(solution)/shard_map/ppermute | solution.py:410
  119.6 5.0 %collective-permute-done.8.refs_4_.refs_9_ = bf16[256,1536]{1,0:T(8,128)(2,1)} collective-permute-done((bf16[256,1536]{1,0:T(8,128)(2,1)}, bf16[256,1536]{1,0:T(8,128)(2,1)}, u32[]{:S(2)}, u32[]{:S(2)}) %collective-permute-start.8) | collective-permute-done | bytes 786464 | tf_op jit(solution)/shard_map/ppermute | solution.py:410
  124.6 7.8 %collective-permute-done.6.refs_2_ = bf16[256,1536]{1,0:T(8,128)(2,1)} collective-permute-done((bf16[256,1536]{1,0:T(8,128)(2,1)}, bf16[256,1536]{1,0:T(8,128)(2,1)}, u32[]{:S(2)}, u32[]{:S(2)}) %collective-permute-start.6) | collective-permute-done | bytes 786464 | tf_op jit(solution)/shard_map/ppermute | solution.py:410
  132.4 1.3 copy-done.10
  134.3 1.7 collective-permute-start.13
  136.0 1.7 collective-permute-start.14
  138.4 1.7 slice.199.refs_2_
  141.2 2.9 fusion.52
  144.1 22.2 %collective-permute-done.13.refs_4_.refs_7_ = bf16[256,1536]{1,0:T(8,128)(2,1)S(1)} collective-permute-done((bf16[256,1536]{1,0:T(8,128)(2,1)}, bf16[256,1536]{1,0:T(8,128)(2,1)S(1)}, u32[]{:S(2)}, u32[]{:S(2)}) %collective-permute-start.13) | collective-permute-done | bytes 786464 | tf_op jit(solution)/shard_map/ppermute | solution.py:410
  166.3 2.0 collective-permute-done.14.refs_5_.refs_11_
  174.1 1.6 copy-done.57
  175.7 3.6 shard_map.107.refs_6_.f_ref
  179.3 1.8 collective-permute-start.17
  181.6 3.0 fusion.22
  184.6 12.8 %collective-permute-done.18.refs_2_ = bf16[256,512]{1,0:T(8,128)(2,1)S(1)} collective-permute-done((bf16[256,512]{1,0:T(8,128)(2,1)S(1)}, bf16[256,512]{1,0:T(8,128)(2,1)S(1)}, u32[]{:S(2)}, u32[]{:S(2)}) %collective-permute-start.18) | collective-permute-done | bytes 262176 | tf_op jit(solution)/shard_map/ppermute | solution.py:502
  199.2 1.1 copy-done.62
  201.4 13.1 %shard_map.109 = (bf16[512,1536]{1,0:T(8,128)(2,1)}, f32[2,128,1536]{2,1,0:T(8,128)}) custom-call(bf16[512,4096]{1,0:T(8,128)(2,1)} %shard_map.107.refs_6_.f_ref, f32[4,512,8]{2,1,0:T(8,128)} %copy-done.3, bf16[512,128]{1,0:T(8,128)(2,1)S(1)} %copy-done.69, bf16[256,2048]{1,0:T(8,128)(2,1)} %refs_0_.7, bf16[256,2048]{1,0:T(8,128)(2,1)} %copy-done.8, ...), custom_call_target="tpu_custom_call" | custom-call | flops 6442450944 | bytes 12582912 | tf_op jit(solution)/shard_map/pallas_call | solution.py:612
  214.5 1.6 fusion.33
  217.2 8.4 %shard_map.110.refs_4_ = bf16[512,2048]{1,0:T(8,128)(2,1)S(1)} custom-call(f32[32,512]{1,0:T(8,128)S(1)} %get-tuple-element.50.r_ref, f32[4,512,8]{2,1,0:T(8,128)S(1)} %copy-done.4, bf16[512,2048]{1,0:T(8,128)(2,1)} %g_ref.11, bf16[512,128]{1,0:T(8,128)(2,1)S(1)} %copy-done.69, bf16[512,128]{1,0:T(8,128)(2,1)S(1)} %copy-done.56, ...), custom_call_target="tpu_custom_call" | custom-call | flops 2147483648 | bytes 6291456 | tf_op jit(solution)/shard_map/pallas_call | solution.py:879
  225.6 1.3 collective-permute-start.22
  228.6 1.2 collective-permute-start.28
  229.8 1.2 collective-permute-start.24
  231.1 1.3 fusion.50
  232.4 2.6 collective-permute-done.22.refs_0_
  234.9 3.3 collective-permute-done.26.refs_5_.refs_9_
  238.3 3.4 collective-permute-done.24.refs_2_
  242.8 1.7 collective-permute-start.31
  244.5 1.7 collective-permute-start.32
  246.5 1.1 copy-done.63
  247.6 1.1 copy-done.66
  248.8 12.0 %shard_map.112.refs_3_.refs_16_ = bf16[512,4096]{1,0:T(8,128)(2,1)} custom-call(s32[16]{0:T(128)S(1)} %get-tuple-element.117.order_ref, bf16[512,2048]{1,0:T(8,128)(2,1)} %get-tuple-element.64.g_ref, bf16[256,2048]{1,0:T(8,128)(2,1)} %refs_0_.7, bf16[256,2048]{1,0:T(8,128)(2,1)} %copy-done.8, bf16[256,2048]{1,0:T(8,128)(2,1)} %get-tuple-element.56.refs_2_, ...), custom_call_target="tpu_custom_call" | custom-call | flops 6442450944 | bytes 12582912 | tf_op jit(solution)/shard_map/pallas_call | solution.py:653
  260.8 18.0 %shard_map.113 = (f32[24,512]{1,0:T(8,128)S(1)}, f32[512,128]{1,0:T(8,128)S(1)}, f32[512,128]{1,0:T(8,128)S(1)}) custom-call(f32[32,512]{1,0:T(8,128)S(1)} %copy-done.76, f32[4,512,8]{2,1,0:T(8,128)S(1)} %copy-done.4, bf16[512,2048]{1,0:T(8,128)(2,1)} %g_ref.11, bf16[512,1536]{1,0:T(8,128)(2,1)S(1)} %copy-done.58, bf16[512,128]{1,0:T(8,128)(2,1)S(1)} %copy-done.70, ...), custom_call_target="tpu_custom_call" | custom-call | flops 2415919104 | bytes 4718592 | tf_op jit(solution)/shard_map/pallas_call | solution.py:719
  278.8 1.3 fusion.46
  290.7 5.4 %shard_map.116 = (bf16[512,512]{1,0:T(8,128)(2,1)S(1)}, f32[2,128,512]{2,1,0:T(8,128)S(1)}) custom-call(bf16[512,4096]{1,0:T(8,128)(2,1)} %shard_map.107.refs_6_.f_ref, f32[4,512,8]{2,1,0:T(8,128)S(1)} %copy-done.4, bf16[512,128]{1,0:T(8,128)(2,1)S(1)} %copy-done.71, bf16[256,2048]{1,0:T(8,128)(2,1)} %refs_0_.7, bf16[256,2048]{1,0:T(8,128)(2,1)} %copy-done.8, ...), custom_call_target="tpu_custom_call" | custom-call | flops 2147483648 | bytes 4194304 | tf_op jit(solution)/shard_map/pallas_call | solution.py:612
  298.0 1.4 broadcast_in_dim.117
  300.8 2.1 collective-permute-done.36
  302.9 1.1 fusion.48
  304.0 1.8 collective-permute-start.37
  308.5 7.6 %collective-permute-start.40 = (bf16[128,1536]{1,0:T(8,128)(2,1)}, bf16[128,1536]{1,0:T(8,128)(2,1)S(1)}, u32[]{:S(2)}, u32[]{:S(2)}) collective-permute-start(bf16[128,1536]{1,0:T(8,128)(2,1)} %get-tuple-element.86), channel_id=1, source_target_pairs={{0,8},{2,10},{4,12},{6,14},{8,0},{10,2},{12,4},{14,6},{16,24},{18,... | collective-permute-start | bytes 1179656 | tf_op jit(solution)/shard_map/ppermute | solution.py:410
  327.8 7.4 %shard_map.115 = (bf16[512,2048]{1,0:T(8,128)(2,1)}, bf16[512,2048]{1,0:T(8,128)(2,1)}) custom-call(s32[16]{0:T(128)S(1)} %get-tuple-element.117.order_ref, bf16[512,2048]{1,0:T(8,128)(2,1)} %get-tuple-element.64.g_ref, bf16[256,2048]{1,0:T(8,128)(2,1)S(1)} %copy-done.7, bf16[256,2048]{1,0:T(8,128)(2,1)S(1)} %copy-done.9, ...), custom_call_target="tpu_custom_call" | custom-call | flops 2147483648 | bytes 4194304 | tf_op jit(solution)/shard_map/pallas_call | solution.py:653
  335.4 1.4 collective-permute-start.39
  337.0 1.7 collective-permute-start.41
  338.8 5.0 %shard_map.117 = (f32[8,512]{1,0:T(8,128)S(1)}, f32[512,128]{1,0:T(8,128)S(1)}, f32[512,128]{1,0:T(8,128)S(1)}) custom-call(f32[32,512]{1,0:T(8,128)S(1)} %copy-done.77, f32[4,512,8]{2,1,0:T(8,128)S(1)} %copy-done.4, bf16[512,2048]{1,0:T(8,128)(2,1)S(1)} %copy-done.1, bf16[512,512]{1,0:T(8,128)(2,1)S(1)} %copy-done.74, bf16[512,128]{1,0:T(8,128)(2,1)S(1)} %copy-done.72, ...), custom_call_target="tpu_custom_call" | custom-call | flops 805306368 | bytes 1572864 | tf_op jit(solution)/shard_map/pallas_call | solution.py:719
  344.0 9.9 %collective-permute-done.39 = bf16[128,512]{1,0:T(8,128)(2,1)S(1)} collective-permute-done((bf16[128,512]{1,0:T(8,128)(2,1)S(1)}, bf16[128,512]{1,0:T(8,128)(2,1)S(1)}, u32[]{:S(2)}, u32[]{:S(2)}) %collective-permute-start.39) | collective-permute-done | bytes 131104 | tf_op jit(solution)/shard_map/ppermute | solution.py:410
  355.0 7.0 %collective-permute-done.41 = bf16[128,1536]{1,0:T(8,128)(2,1)S(1)} collective-permute-done((bf16[128,1536]{1,0:T(8,128)(2,1)S(1)}, bf16[128,1536]{1,0:T(8,128)(2,1)S(1)}, u32[]{:S(2)}, u32[]{:S(2)}) %collective-permute-start.41) | collective-permute-done | bytes 393248 | tf_op jit(solution)/shard_map/ppermute | solution.py:410
  362.3 6.1 %shard_map.118 = (f32[24,512]{1,0:T(8,128)S(1)}, f32[512,128]{1,0:T(8,128)S(1)}) custom-call(f32[4,512,8]{2,1,0:T(8,128)S(1)} %copy-done.4, bf16[512,2048]{1,0:T(8,128)(2,1)} %g_ref.11, bf16[512,128]{1,0:T(8,128)(2,1)S(1)} %copy-done.56, f32[128,1536]{1,0:T(8,128)S(1)} %fusion.16.s_ref, f32[2,128,1536]{2,1,0:T(8,128)S(1)} %copy-done.6, ...), custom_call_target="tpu_custom_call" | custom-call | flops 402653184 | bytes 4718592 | tf_op jit(solution)/shard_map/pallas_call | solution.py:734
  368.5 1.6 shard_map.119
  372.3 2.2 add_convert_fusion
  (377 shorter events, 57.1 us)
Async XLA Ops:
  0.6 23.5 %copy-start.114 = (u32[32]{0:T(128)S(1)}, u32[32]{0:T(128)}, u32[]{:S(2)}) copy-start(u32[32]{0:T(128)} %constant.145) | copy-start | bytes 388
  2.8 76.2 %collective-permute-start.2 = (bf16[256,1536]{1,0:T(8,128)(2,1)}, bf16[256,1536]{1,0:T(8,128)(2,1)}, u32[]{:S(2)}, u32[]{:S(2)}) collective-permute-start(bf16[256,1536]{1,0:T(8,128)(2,1)} %slice.190.refs_0_), channel_id=1, source_target_pairs={{0,24},{2,26},{4,28},{6,30},{8,0},{10,2},{12,4},{14,6},{16,8},{18,... | collective-permute-start | bytes 2359304 | tf_op jit(solution)/shard_map/ppermute | solution.py:502
  7.8 71.1 %collective-permute-start.1 = (bf16[256,1536]{1,0:T(8,128)(2,1)}, bf16[256,1536]{1,0:T(8,128)(2,1)}, u32[]{:S(2)}, u32[]{:S(2)}) collective-permute-start(bf16[256,1536]{1,0:T(8,128)(2,1)} %slice.190.refs_0_), channel_id=1, source_target_pairs={{0,8},{2,10},{4,12},{6,14},{8,16},{10,18},{12,20},{14,22},{16,24},... | collective-permute-start | bytes 2359304 | tf_op jit(solution)/shard_map/ppermute | solution.py:502
  7.8 74.1 %collective-permute-start.3 = (bf16[256,2048]{1,0:T(8,128)(2,1)}, bf16[256,2048]{1,0:T(8,128)(2,1)S(1)}, u32[]{:S(2)}, u32[]{:S(2)}) collective-permute-start(bf16[256,2048]{1,0:T(8,128)(2,1)} %refs_0_.7), channel_id=1, source_target_pairs={{0,2},{2,0},{4,6},{6,4},{8,10},{10,8},{12,14},{14,12},{16,18},{18,... | collective-permute-start | bytes 3145736 | tf_op jit(solution)/shard_map/ppermute | solution.py:410
  9.3 72.6 %collective-permute-start = (bf16[256,2048]{1,0:T(8,128)(2,1)}, bf16[256,2048]{1,0:T(8,128)(2,1)}, u32[]{:S(2)}, u32[]{:S(2)}) collective-permute-start(bf16[256,2048]{1,0:T(8,128)(2,1)} %refs_0_.7), channel_id=1, source_target_pairs={{0,4},{2,6},{4,0},{6,2},{8,12},{10,14},{12,8},{14,10},{16,20},{18,... | collective-permute-start | bytes 3145736 | tf_op jit(solution)/shard_map/ppermute | solution.py:410
  10.8 121.6 %collective-permute-start.10 = (bf16[512,2048]{1,0:T(8,128)(2,1)}, bf16[512,2048]{1,0:T(8,128)(2,1)S(1)}, u32[]{:S(2)}, u32[]{:S(2)}) collective-permute-start(bf16[512,2048]{1,0:T(8,128)(2,1)} %own_ref.1), channel_id=1, source_target_pairs={{0,1},{1,0},{2,3},{3,2},{4,5},{5,4},{6,7},{7,6},{8,9},{9,8},{10,11... | collective-permute-start | bytes 6291464 | tf_op jit(solution)/shard_map/ppermute | solution.py:410
  23.6 147.8 %copy-start.67 = (f32[2,8,2048]{2,1,0:T(8,128)}, f32[2,8,2048]{2,1,0:T(8,128)S(1)}, u32[]{:S(2)}) copy-start(f32[2,8,2048]{2,1,0:T(8,128)S(1)} %get-tuple-element.46.a_ref) | copy-start | bytes 393220
  23.6 193.5 %copy-start.75 = (f32[32,512]{1,0:T(8,128)}, f32[32,512]{1,0:T(8,128)S(1)}, u32[]{:S(2)}) copy-start(f32[32,512]{1,0:T(8,128)S(1)} %get-tuple-element.50.r_ref) | copy-start | bytes 196612
  81.0 9.5 %collective-permute-start.9 = (bf16[128,2048]{1,0:T(8,128)(2,1)}, bf16[128,2048]{1,0:T(8,128)(2,1)}, u32[]{:S(2)}, u32[]{:S(2)}) collective-permute-start(bf16[128,2048]{1,0:T(8,128)(2,1)} %convert_element_type.106), channel_id=1, source_target_pairs={{0,2},{2,0},{4,6},{6,4},{8,10},{10,8},{12,14},{14,12},{16,18},{18,... | collective-permute-start | bytes 1572872 | tf_op jit(solution)/shard_map/ppermute | solution.py:410
  81.9 51.9 %copy-start.104 = (f32[1,2048]{1,0:T(1,128)}, f32[1,2048]{1,0:T(1,128)S(1)}, u32[]{:S(2)}) copy-start(f32[1,2048]{1,0:T(1,128)S(1)} %broadcast_in_dim.115) | copy-start | bytes 24580
  82.9 24.6 %collective-permute-start.4 = (bf16[256,1536]{1,0:T(8,128)(2,1)}, bf16[256,1536]{1,0:T(8,128)(2,1)}, u32[]{:S(2)}, u32[]{:S(2)}) collective-permute-start(bf16[256,1536]{1,0:T(8,128)(2,1)} %get-tuple-element.47), channel_id=1, source_target_pairs={{0,16},{2,18},{4,20},{6,22},{8,24},{10,26},{12,28},{14,30},{16,0},... | collective-permute-start | bytes 2359304 | tf_op jit(solution)/shard_map/ppermute | solution.py:502
  93.3 13.8 %collective-permute-start.15 = (bf16[128,2048]{1,0:T(8,128)(2,1)}, bf16[128,2048]{1,0:T(8,128)(2,1)}, u32[]{:S(2)}, u32[]{:S(2)}) collective-permute-start(bf16[128,2048]{1,0:T(8,128)(2,1)} %get-tuple-element.96), channel_id=1, source_target_pairs={{0,4},{2,6},{4,0},{6,2},{8,12},{10,14},{12,8},{14,10},{16,20},{18,... | collective-permute-start | bytes 1572872 | tf_op jit(solution)/shard_map/ppermute | solution.py:410
  93.9 25.7 %collective-permute-start.7 = (bf16[256,1536]{1,0:T(8,128)(2,1)}, bf16[256,1536]{1,0:T(8,128)(2,1)S(1)}, u32[]{:S(2)}, u32[]{:S(2)}) collective-permute-start(bf16[256,1536]{1,0:T(8,128)(2,1)} %get-tuple-element.48.refs_4_), channel_id=1, source_target_pairs={{0,4},{2,6},{4,0},{6,2},{8,12},{10,14},{12,8},{14,10},{16,20},{18,... | collective-permute-start | bytes 2359304 | tf_op jit(solution)/shard_map/ppermute | solution.py:410
  97.3 22.3 %collective-permute-start.5 = (bf16[256,1536]{1,0:T(8,128)(2,1)}, bf16[256,1536]{1,0:T(8,128)(2,1)}, u32[]{:S(2)}, u32[]{:S(2)}) collective-permute-start(bf16[256,1536]{1,0:T(8,128)(2,1)} %get-tuple-element.48.refs_4_), channel_id=1, source_target_pairs={{0,2},{2,0},{4,6},{6,4},{8,10},{10,8},{12,14},{14,12},{16,18},{18,... | collective-permute-start | bytes 2359304 | tf_op jit(solution)/shard_map/ppermute | solution.py:410
  107.1 17.5 %collective-permute-start.8 = (bf16[256,1536]{1,0:T(8,128)(2,1)}, bf16[256,1536]{1,0:T(8,128)(2,1)}, u32[]{:S(2)}, u32[]{:S(2)}) collective-permute-start(bf16[256,1536]{1,0:T(8,128)(2,1)} %get-tuple-element.49.refs_8_), channel_id=1, source_target_pairs={{0,2},{2,0},{4,6},{6,4},{8,10},{10,8},{12,14},{14,12},{16,18},{18,... | collective-permute-start | bytes 2359304 | tf_op jit(solution)/shard_map/ppermute | solution.py:410
  107.4 25.0 %collective-permute-start.6 = (bf16[256,1536]{1,0:T(8,128)(2,1)}, bf16[256,1536]{1,0:T(8,128)(2,1)}, u32[]{:S(2)}, u32[]{:S(2)}) collective-permute-start(bf16[256,1536]{1,0:T(8,128)(2,1)} %get-tuple-element.49.refs_8_), channel_id=1, source_target_pairs={{0,4},{2,6},{4,0},{6,2},{8,12},{10,14},{12,8},{14,10},{16,20},{18,... | collective-permute-start | bytes 2359304 | tf_op jit(solution)/shard_map/ppermute | solution.py:410
  111.5 26.3 %copy-start.100 = (f32[1,2048]{1,0:T(1,128)}, f32[1,2048]{1,0:T(1,128)S(1)}, u32[]{:S(2)}) copy-start(f32[1,2048]{1,0:T(1,128)S(1)} %broadcast_in_dim.106) | copy-start | bytes 24580
  119.6 21.6 %collective-permute-start.21 = (bf16[128,2048]{1,0:T(8,128)(2,1)}, bf16[128,2048]{1,0:T(8,128)(2,1)}, u32[]{:S(2)}, u32[]{:S(2)}) collective-permute-start(bf16[128,2048]{1,0:T(8,128)(2,1)} %get-tuple-element.94), channel_id=1, source_target_pairs={{0,8},{2,10},{4,12},{6,14},{8,0},{10,2},{12,4},{14,6},{16,24},{18,... | collective-permute-start | bytes 1572872 | tf_op jit(solution)/shard_map/ppermute | solution.py:410
  133.7 34.5 %collective-permute-start.12 = (bf16[256,1536]{1,0:T(8,128)(2,1)}, bf16[256,1536]{1,0:T(8,128)(2,1)}, u32[]{:S(2)}, u32[]{:S(2)}) collective-permute-start(bf16[256,1536]{1,0:T(8,128)(2,1)} %get-tuple-element.51.refs_12_), channel_id=1, source_target_pairs={{0,4},{2,6},{4,0},{6,2},{8,12},{10,14},{12,8},{14,10},{16,20},{18,... | collective-permute-start | bytes 2359304 | tf_op jit(solution)/shard_map/ppermute | solution.py:410
  134.0 34.3 %collective-permute-start.11 = (bf16[256,1536]{1,0:T(8,128)(2,1)}, bf16[256,1536]{1,0:T(8,128)(2,1)}, u32[]{:S(2)}, u32[]{:S(2)}) collective-permute-start(bf16[256,1536]{1,0:T(8,128)(2,1)} %get-tuple-element.51.refs_12_), channel_id=1, source_target_pairs={{0,2},{2,0},{4,6},{6,4},{8,10},{10,8},{12,14},{14,12},{16,18},{18,... | collective-permute-start | bytes 2359304 | tf_op jit(solution)/shard_map/ppermute | solution.py:410
  134.3 32.0 %collective-permute-start.13 = (bf16[256,1536]{1,0:T(8,128)(2,1)}, bf16[256,1536]{1,0:T(8,128)(2,1)S(1)}, u32[]{:S(2)}, u32[]{:S(2)}) collective-permute-start(bf16[256,1536]{1,0:T(8,128)(2,1)} %get-tuple-element.52.refs_5_), channel_id=1, source_target_pairs={{0,4},{2,6},{4,0},{6,2},{8,12},{10,14},{12,8},{14,10},{16,20},{18,... | collective-permute-start | bytes 2359304 | tf_op jit(solution)/shard_map/ppermute | solution.py:410
  136.0 32.2 %collective-permute-start.14 = (bf16[256,1536]{1,0:T(8,128)(2,1)}, bf16[256,1536]{1,0:T(8,128)(2,1)}, u32[]{:S(2)}, u32[]{:S(2)}) collective-permute-start(bf16[256,1536]{1,0:T(8,128)(2,1)} %get-tuple-element.53.refs_10_), channel_id=1, source_target_pairs={{0,2},{2,0},{4,6},{6,4},{8,10},{10,8},{12,14},{14,12},{16,18},{18,... | collective-permute-start | bytes 2359304 | tf_op jit(solution)/shard_map/ppermute | solution.py:410
  140.2 28.9 %copy-start.101 = (f32[1,2048]{1,0:T(1,128)}, f32[1,2048]{1,0:T(1,128)S(1)}, u32[]{:S(2)}) copy-start(f32[1,2048]{1,0:T(1,128)S(1)} %broadcast_in_dim.103) | copy-start | bytes 24580
  140.4 27.9 %copy-start.93 = (f32[32,64]{1,0:T(8,128)}, f32[32,64]{1,0:T(8,128)S(1)}, u32[]{:S(2)}) copy-start(f32[32,64]{1,0:T(8,128)S(1)} %broadcast_in_dim.93) | copy-start | bytes 24580
  140.6 27.7 %copy-start.107 = (f32[1,2048]{1,0:T(1,128)}, f32[1,2048]{1,0:T(1,128)S(1)}, u32[]{:S(2)}) copy-start(f32[1,2048]{1,0:T(1,128)S(1)} %broadcast_in_dim.113) | copy-start | bytes 24580
  144.1 28.6 %copy-start.113 = (f32[32]{0:T(128)S(1)}, f32[32]{0:T(128)}, u32[]{:S(2)}) copy-start(f32[32]{0:T(128)} %param.12) | copy-start | bytes 388
  144.1 30.1 %copy-start.11 = (bf16[512,2048]{1,0:T(8,128)(2,1)S(1)}, bf16[512,2048]{1,0:T(8,128)(2,1)}, u32[]{:S(2)}) copy-start(bf16[512,2048]{1,0:T(8,128)(2,1)} %copy-done.10) | copy-start | bytes 6291460
  144.1 37.0 %collective-permute-start.25 = (bf16[128,2048]{1,0:T(8,128)(2,1)}, bf16[128,2048]{1,0:T(8,128)(2,1)}, u32[]{:S(2)}, u32[]{:S(2)}) collective-permute-start(bf16[128,2048]{1,0:T(8,128)(2,1)} %get-tuple-element.92), channel_id=1, source_target_pairs={{0,16},{2,18},{4,20},{6,22},{8,24},{10,26},{12,28},{14,30},{16,0},... | collective-permute-start | bytes 1572872 | tf_op jit(solution)/shard_map/ppermute | solution.py:410
  168.3 29.1 %collective-permute-start.20 = (bf16[256,2048]{1,0:T(8,128)(2,1)}, bf16[256,2048]{1,0:T(8,128)(2,1)}, u32[]{:S(2)}, u32[]{:S(2)}) collective-permute-start(bf16[256,2048]{1,0:T(8,128)(2,1)} %get-tuple-element.56.refs_2_), channel_id=1, source_target_pairs={{0,2},{2,0},{4,6},{6,4},{8,10},{10,8},{12,14},{14,12},{16,18},{18,... | collective-permute-start | bytes 3145736 | tf_op jit(solution)/shard_map/ppermute | solution.py:410
  169.8 27.6 %collective-permute-start.19 = (bf16[256,1536]{1,0:T(8,128)(2,1)}, bf16[256,1536]{1,0:T(8,128)(2,1)}, u32[]{:S(2)}, u32[]{:S(2)}) collective-permute-start(bf16[256,1536]{1,0:T(8,128)(2,1)} %get-tuple-element.55.refs_13_), channel_id=1, source_target_pairs={{0,4},{2,6},{4,0},{6,2},{8,12},{10,14},{12,8},{14,10},{16,20},{18,... | collective-permute-start | bytes 2359304 | tf_op jit(solution)/shard_map/ppermute | solution.py:410
  179.3 18.0 %collective-permute-start.18 = (bf16[256,512]{1,0:T(8,128)(2,1)S(1)}, bf16[256,512]{1,0:T(8,128)(2,1)S(1)}, u32[]{:S(2)}, u32[]{:S(2)}) collective-permute-start(bf16[256,512]{1,0:T(8,128)(2,1)S(1)} %copy-done.92), channel_id=1, source_target_pairs={{0,16},{2,18},{4,20},{6,22},{8,24},{10,26},{12,28},{14,30},{16,0},... | collective-permute-start | bytes 786440 | tf_op jit(solution)/shard_map/ppermute | solution.py:502
  179.3 18.0 %collective-permute-start.17 = (bf16[256,512]{1,0:T(8,128)(2,1)S(1)}, bf16[256,512]{1,0:T(8,128)(2,1)S(1)}, u32[]{:S(2)}, u32[]{:S(2)}) collective-permute-start(bf16[256,512]{1,0:T(8,128)(2,1)S(1)} %copy-done.92), channel_id=1, source_target_pairs={{0,24},{2,26},{4,28},{6,30},{8,0},{10,2},{12,4},{14,6},{16,8},{18,... | collective-permute-start | bytes 786440 | tf_op jit(solution)/shard_map/ppermute | solution.py:502
  181.1 16.3 %collective-permute-start.16 = (bf16[256,512]{1,0:T(8,128)(2,1)S(1)}, bf16[256,512]{1,0:T(8,128)(2,1)S(1)}, u32[]{:S(2)}, u32[]{:S(2)}) collective-permute-start(bf16[256,512]{1,0:T(8,128)(2,1)S(1)} %copy-done.92), channel_id=1, source_target_pairs={{0,8},{2,10},{4,12},{6,14},{8,16},{10,18},{12,20},{14,22},{16,24},... | collective-permute-start | bytes 786440 | tf_op jit(solution)/shard_map/ppermute | solution.py:502
  198.3 30.4 %collective-permute-start.27 = (bf16[256,512]{1,0:T(8,128)(2,1)}, bf16[256,512]{1,0:T(8,128)(2,1)S(1)}, u32[]{:S(2)}, u32[]{:S(2)}) collective-permute-start(bf16[256,512]{1,0:T(8,128)(2,1)} %get-tuple-element.57.refs_4_), channel_id=1, source_target_pairs={{0,4},{2,6},{4,0},{6,2},{8,12},{10,14},{12,8},{14,10},{16,20},{18,... | collective-permute-start | bytes 786440 | tf_op jit(solution)/shard_map/ppermute | solution.py:410
  216.1 13.7 %collective-permute-start.29 = (bf16[128,1536]{1,0:T(8,128)(2,1)S(1)}, bf16[128,1536]{1,0:T(8,128)(2,1)S(1)}, u32[]{:S(2)}, u32[]{:S(2)}) collective-permute-start(bf16[128,1536]{1,0:T(8,128)(2,1)S(1)} %fusion.33), channel_id=1, source_target_pairs={{0,2},{2,0},{4,6},{6,4},{8,10},{10,8},{12,14},{14,12},{16,18},{18,... | collective-permute-start | bytes 1179656 | tf_op jit(solution)/shard_map/ppermute | solution.py:410
  225.6 9.3 %collective-permute-start.22 = (bf16[256,512]{1,0:T(8,128)(2,1)S(1)}, bf16[256,512]{1,0:T(8,128)(2,1)S(1)}, u32[]{:S(2)}, u32[]{:S(2)}) collective-permute-start(bf16[256,512]{1,0:T(8,128)(2,1)S(1)} %copy-done.49), channel_id=1, source_target_pairs={{0,2},{2,0},{4,6},{6,4},{8,10},{10,8},{12,14},{14,12},{16,18},{18,... | collective-permute-start | bytes 786440 | tf_op jit(solution)/shard_map/ppermute | solution.py:410
  226.9 11.3 %collective-permute-start.26 = (bf16[256,512]{1,0:T(8,128)(2,1)S(1)}, bf16[256,512]{1,0:T(8,128)(2,1)S(1)}, u32[]{:S(2)}, u32[]{:S(2)}) collective-permute-start(bf16[256,512]{1,0:T(8,128)(2,1)S(1)} %copy-done.42), channel_id=1, source_target_pairs={{0,2},{2,0},{4,6},{6,4},{8,10},{10,8},{12,14},{14,12},{16,18},{18,... | collective-permute-start | bytes 786440 | tf_op jit(solution)/shard_map/ppermute | solution.py:410
  227.7 10.6 %collective-permute-start.23 = (bf16[256,512]{1,0:T(8,128)(2,1)S(1)}, bf16[256,512]{1,0:T(8,128)(2,1)S(1)}, u32[]{:S(2)}, u32[]{:S(2)}) collective-permute-start(bf16[256,512]{1,0:T(8,128)(2,1)S(1)} %copy-done.42), channel_id=1, source_target_pairs={{0,4},{2,6},{4,0},{6,2},{8,12},{10,14},{12,8},{14,10},{16,20},{18,... | collective-permute-start | bytes 786440 | tf_op jit(solution)/shard_map/ppermute | solution.py:410
  228.6 9.7 %collective-permute-start.28 = (bf16[256,512]{1,0:T(8,128)(2,1)S(1)}, bf16[256,512]{1,0:T(8,128)(2,1)S(1)}, u32[]{:S(2)}, u32[]{:S(2)}) collective-permute-start(bf16[256,512]{1,0:T(8,128)(2,1)S(1)} %copy-done.35), channel_id=1, source_target_pairs={{0,4},{2,6},{4,0},{6,2},{8,12},{10,14},{12,8},{14,10},{16,20},{18,... | collective-permute-start | bytes 786440 | tf_op jit(solution)/shard_map/ppermute | solution.py:410
  229.8 11.8 %collective-permute-start.24 = (bf16[256,512]{1,0:T(8,128)(2,1)S(1)}, bf16[256,512]{1,0:T(8,128)(2,1)S(1)}, u32[]{:S(2)}, u32[]{:S(2)}) collective-permute-start(bf16[256,512]{1,0:T(8,128)(2,1)S(1)} %copy-done.35), channel_id=1, source_target_pairs={{0,2},{2,0},{4,6},{6,4},{8,10},{10,8},{12,14},{14,12},{16,18},{18,... | collective-permute-start | bytes 786440 | tf_op jit(solution)/shard_map/ppermute | solution.py:410
  242.4 37.7 %collective-permute-start.30 = (bf16[256,512]{1,0:T(8,128)(2,1)}, bf16[256,512]{1,0:T(8,128)(2,1)S(1)}, u32[]{:S(2)}, u32[]{:S(2)}) collective-permute-start(bf16[256,512]{1,0:T(8,128)(2,1)} %get-tuple-element.65.refs_5_), channel_id=1, source_target_pairs={{0,4},{2,6},{4,0},{6,2},{8,12},{10,14},{12,8},{14,10},{16,20},{18,... | collective-permute-start | bytes 786440 | tf_op jit(solution)/shard_map/ppermute | solution.py:410
  242.8 37.4 %collective-permute-start.31 = (bf16[256,512]{1,0:T(8,128)(2,1)}, bf16[256,512]{1,0:T(8,128)(2,1)S(1)}, u32[]{:S(2)}, u32[]{:S(2)}) collective-permute-start(bf16[256,512]{1,0:T(8,128)(2,1)} %get-tuple-element.66.refs_10_), channel_id=1, source_target_pairs={{0,2},{2,0},{4,6},{6,4},{8,10},{10,8},{12,14},{14,12},{16,18},{18,... | collective-permute-start | bytes 786440 | tf_op jit(solution)/shard_map/ppermute | solution.py:410
  244.5 35.7 %collective-permute-start.32 = (bf16[256,512]{1,0:T(8,128)(2,1)}, bf16[256,512]{1,0:T(8,128)(2,1)S(1)}, u32[]{:S(2)}, u32[]{:S(2)}) collective-permute-start(bf16[256,512]{1,0:T(8,128)(2,1)} %get-tuple-element.67.refs_13_), channel_id=1, source_target_pairs={{0,4},{2,6},{4,0},{6,2},{8,12},{10,14},{12,8},{14,10},{16,20},{18,... | collective-permute-start | bytes 786440 | tf_op jit(solution)/shard_map/ppermute | solution.py:410
  246.2 32.6 %collective-permute-start.33 = (bf16[128,1536]{1,0:T(8,128)(2,1)}, bf16[128,1536]{1,0:T(8,128)(2,1)S(1)}, u32[]{:S(2)}, u32[]{:S(2)}) collective-permute-start(bf16[128,1536]{1,0:T(8,128)(2,1)} %get-tuple-element.90), channel_id=1, source_target_pairs={{0,4},{2,6},{4,0},{6,2},{8,12},{10,14},{12,8},{14,10},{16,20},{18,... | collective-permute-start | bytes 1179656 | tf_op jit(solution)/shard_map/ppermute | solution.py:410
  260.8 18.0 %copy-start.84 = (f32[128,1536]{1,0:T(8,128)S(1)}, f32[128,1536]{1,0:T(8,128)}, u32[]{:S(2)}) copy-start(f32[128,1536]{1,0:T(8,128)} %get-tuple-element.91.refs_8_) | copy-start | bytes 2359300
  260.8 18.0 %copy-start.94 = (f32[1536]{0:T(1024)S(1)}, f32[1536]{0:T(1024)}, u32[]{:S(2)}) copy-start(f32[1536]{0:T(1024)} %slice_reduce_fusion.4) | copy-start | bytes 18436
  260.8 18.0 %copy-start.95 = (f32[1536]{0:T(1024)S(1)}, f32[1536]{0:T(1024)}, u32[]{:S(2)}) copy-start(f32[1536]{0:T(1024)} %slice_reduce_fusion.3) | copy-start | bytes 18436
  296.1 21.2 %copy-start.7 = (bf16[256,2048]{1,0:T(8,128)(2,1)S(1)}, bf16[256,2048]{1,0:T(8,128)(2,1)}, u32[]{:S(2)}) copy-start(bf16[256,2048]{1,0:T(8,128)(2,1)} %refs_0_.7) | copy-start | bytes 3145732
  297.6 5.3 %collective-permute-start.36 = (bf16[128,512]{1,0:T(8,128)(2,1)}, bf16[128,512]{1,0:T(8,128)(2,1)}, u32[]{:S(2)}, u32[]{:S(2)}) collective-permute-start(bf16[128,512]{1,0:T(8,128)(2,1)} %fusion.35), channel_id=1, source_target_pairs={{0,2},{2,0},{4,6},{6,4},{8,10},{10,8},{12,14},{14,12},{16,18},{18,... | collective-permute-start | bytes 393224 | tf_op jit(solution)/shard_map/ppermute | solution.py:410
  299.4 17.9 %copy-start.9 = (bf16[256,2048]{1,0:T(8,128)(2,1)S(1)}, bf16[256,2048]{1,0:T(8,128)(2,1)}, u32[]{:S(2)}) copy-start(bf16[256,2048]{1,0:T(8,128)(2,1)} %copy-done.8) | copy-start | bytes 3145732
  304.0 12.2 %collective-permute-start.37 = (bf16[128,512]{1,0:T(8,128)(2,1)S(1)}, bf16[128,512]{1,0:T(8,128)(2,1)S(1)}, u32[]{:S(2)}, u32[]{:S(2)}) collective-permute-start(bf16[128,512]{1,0:T(8,128)(2,1)S(1)} %get-tuple-element.88), channel_id=1, source_target_pairs={{0,4},{2,6},{4,0},{6,2},{8,12},{10,14},{12,8},{14,10},{16,20},{18,... | collective-permute-start | bytes 393224 | tf_op jit(solution)/shard_map/ppermute | solution.py:410
  308.5 28.3 %collective-permute-start.40 = (bf16[128,1536]{1,0:T(8,128)(2,1)}, bf16[128,1536]{1,0:T(8,128)(2,1)S(1)}, u32[]{:S(2)}, u32[]{:S(2)}) collective-permute-start(bf16[128,1536]{1,0:T(8,128)(2,1)} %get-tuple-element.86), channel_id=1, source_target_pairs={{0,8},{2,10},{4,12},{6,14},{8,0},{10,2},{12,4},{14,6},{16,24},{18,... | collective-permute-start | bytes 1179656 | tf_op jit(solution)/shard_map/ppermute | solution.py:410
  316.2 19.1 %collective-permute-start.38 = (bf16[128,512]{1,0:T(8,128)(2,1)S(1)}, bf16[128,512]{1,0:T(8,128)(2,1)S(1)}, u32[]{:S(2)}, u32[]{:S(2)}) collective-permute-start(bf16[128,512]{1,0:T(8,128)(2,1)S(1)} %fusion.34), channel_id=1, source_target_pairs={{0,8},{2,10},{4,12},{6,14},{8,0},{10,2},{12,4},{14,6},{16,24},{18,... | collective-permute-start | bytes 393224 | tf_op jit(solution)/shard_map/ppermute | solution.py:410
  335.2 37.1 %collective-permute-start.34 = (bf16[512,2048]{1,0:T(8,128)(2,1)}, bf16[512,2048]{1,0:T(8,128)(2,1)S(1)}, u32[]{:S(2)}, u32[]{:S(2)}) collective-permute-start(bf16[512,2048]{1,0:T(8,128)(2,1)} %get-tuple-element.74), channel_id=1, source_target_pairs={{0,1},{1,0},{2,3},{3,2},{4,5},{5,4},{6,7},{7,6},{8,9},{9,8},{10,11... | collective-permute-start | bytes 6291464 | tf_op jit(solution)/shard_map/ppermute | solution.py:410
  335.4 18.5 %collective-permute-start.39 = (bf16[128,512]{1,0:T(8,128)(2,1)S(1)}, bf16[128,512]{1,0:T(8,128)(2,1)S(1)}, u32[]{:S(2)}, u32[]{:S(2)}) collective-permute-start(bf16[128,512]{1,0:T(8,128)(2,1)S(1)} %fusion.32), channel_id=1, source_target_pairs={{0,16},{2,18},{4,20},{6,22},{8,24},{10,26},{12,28},{14,30},{16,0},... | collective-permute-start | bytes 393224 | tf_op jit(solution)/shard_map/ppermute | solution.py:410
  337.0 25.0 %collective-permute-start.41 = (bf16[128,1536]{1,0:T(8,128)(2,1)S(1)}, bf16[128,1536]{1,0:T(8,128)(2,1)S(1)}, u32[]{:S(2)}, u32[]{:S(2)}) collective-permute-start(bf16[128,1536]{1,0:T(8,128)(2,1)S(1)} %fusion.21), channel_id=1, source_target_pairs={{0,16},{2,18},{4,20},{6,22},{8,24},{10,26},{12,28},{14,30},{16,0},... | collective-permute-start | bytes 1179656 | tf_op jit(solution)/shard_map/ppermute | solution.py:410
  338.8 23.1 %copy-start.89 = (bf16[128,1536]{1,0:T(8,128)(2,1)S(1)}, bf16[128,1536]{1,0:T(8,128)(2,1)}, u32[]{:S(2)}) copy-start(bf16[128,1536]{1,0:T(8,128)(2,1)} %copy-done.88) | copy-start | bytes 1179652
  338.8 23.1 %copy-start.91 = (bf16[128,1536]{1,0:T(8,128)(2,1)S(1)}, bf16[128,1536]{1,0:T(8,128)(2,1)}, u32[]{:S(2)}) copy-start(bf16[128,1536]{1,0:T(8,128)(2,1)} %copy-done.90) | copy-start | bytes 1179652
  338.8 23.1 %copy-start.98 = (f32[1536]{0:T(1024)S(1)}, f32[1536]{0:T(1024)}, u32[]{:S(2)}) copy-start(f32[1536]{0:T(1024)} %fusion.36) | copy-start | bytes 18436
  343.9 18.4 %copy-start.6 = (f32[2,128,1536]{2,1,0:T(8,128)S(1)}, f32[2,128,1536]{2,1,0:T(8,128)}, u32[]{:S(2)}) copy-start(f32[2,128,1536]{2,1,0:T(8,128)} %get-tuple-element.63.e_ref) | copy-start | bytes 4718596
  343.9 18.4 %copy-start.68 = (f32[2,8,2048]{2,1,0:T(8,128)S(1)}, f32[2,8,2048]{2,1,0:T(8,128)}, u32[]{:S(2)}) copy-start(f32[2,8,2048]{2,1,0:T(8,128)} %copy-done.67) | copy-start | bytes 393220
  343.9 18.4 %copy-start.82 = (f32[24,512]{1,0:T(8,128)S(1)}, f32[24,512]{1,0:T(8,128)}, u32[]{:S(2)}) copy-start(f32[24,512]{1,0:T(8,128)} %copy-done.81) | copy-start | bytes 147460
  343.9 26.2 %collective-permute-start.35 = (bf16[512,128]{1,0:T(8,128)(2,1)S(1)}, bf16[512,128]{1,0:T(8,128)(2,1)S(1)}, u32[]{:S(2)}, u32[]{:S(2)}) collective-permute-start(bf16[512,128]{1,0:T(8,128)(2,1)S(1)} %convert_element_type.123), channel_id=1, source_target_pairs={{0,1},{1,0},{2,3},{3,2},{4,5},{5,4},{6,7},{7,6},{8,9},{9,8},{10,11... | collective-permute-start | bytes 393224 | tf_op jit(solution)/shard_map/ppermute | solution.py:410
  370.1 1.5 collective-permute-start.42
  (97 other events, 463.0 us)

commit v3 on v2

--- a/solution.py
+++ b/solution.py
@@ -14,6 +14,7 @@
 WIDE = GROUP * P_SIZE
 LOG2E = 1.4426950408889634
 NEVER = -1e30
+GRANT = 58 * 2**20
 
 F32 = jnp.float32
 BF16 = jnp.bfloat16
@@ -82,7 +83,8 @@
     running = padded.T[:, :GROUP]
     rt_ref[0] = running
     growth = jnp.exp2(spread_columns(running))
-    a_ref[0] = jnp.broadcast_to(growth[SPAN - 1 : SPAN], (8, WIDE))
+    last = spread_columns(running[SPAN - 1 : SPAN])
+    a_ref[0] = jnp.where(iota((8, WIDE), 0) < 4, jnp.exp2(last), last)
     scaled = (g_ref[...].astype(F32) * growth).astype(BF16)
     gt_ref[0] = dot(c_ref[...], scaled, ((0,), (0,)))
 
@@ -161,104 +163,118 @@
         out_ref[:, index * unit : (index + 1) * unit] = both_ref[:, source]
 
 
-def fetch(arrays, columns, buffer, sems):
+def coefficients_kernel(place_ref, every_ref, out_ref):
+    place = place_ref[0]
+    count = every_ref.shape[0]
+    parts = jnp.concatenate(thirds(every_ref[...]), axis=0).astype(BF16)
+    row = iota((8, count), 0)
+    column = iota((8, count), 1)
+    line = iota((8, every_ref.shape[1]), 0)
+    half = out_ref.shape[0] // 2
+    for step in range(half):
+        bit = 2**step
+        start = place // bit * bit
+        upper = place // bit % 2
+        beside = start + bit - 2 * bit * upper
+        low = jnp.where(row == 1, beside, jnp.where(row == 3, place + 1, start))
+        high = jnp.where(row == 1, beside + bit, jnp.where(row == 2, place, start + bit))
+        mask = ((column >= low) & (column < high)).astype(F32)
+        mask = jnp.concatenate([mask, mask, mask], axis=1).astype(BF16)
+        factors = jnp.exp2(mm(mask, parts))
+        kept, other, before_me, after_me = [factors[k : k + 1] for k in range(4)]
+        up = (upper + 0 * line) == 1
+        for way in range(2):
+            later = up if way == 0 else jnp.logical_not(up)
+            passed = before_me if way == 0 else after_me
+            first = jnp.where(later, 1.0, other)
+            second = jnp.where(later, kept, 1.0)
+            third = jnp.where(later, passed, 0.0)
+            out_ref[way * half + step] = jnp.where(
+                line == 0, first, jnp.where(line == 1, second, third)
+            )
+
+
+def scan_kernel(factor_ref, total_ref, got_ref, *refs):
+    entering_ref = refs[0] if len(refs) == 4 else None
+    total_out, entering_out, sent_out = refs[-3:]
+    factors = factor_ref[0]
+    got = got_ref[...].astype(F32)
+    total = factors[0:1] * total_ref[...] + factors[1:2] * got
+    total_out[...] = total
+    sent_out[...] = total.astype(BF16)
+    passed = factors[2:3] * got
+    entering_out[...] = passed if entering_ref is None else entering_ref[...] + passed
+
+
+def early_forward_kernel(count, f_ref, *refs):
+    pieces, (out_ref, buffer) = refs[:count], refs[count:]
+    rows = pieces[0].shape[0]
+    for index, piece in enumerate(pieces):
+        buffer[index * rows : (index + 1) * rows] = piece[...]
+    out_ref[...] = mm(f_ref[...], buffer[...])
+
+
+def late_forward_kernel(count, f_ref, part_ref, rt_ref, b_ref, kept_ref, *refs):
+    pieces, (x_ref, e_ref, total_ref, sent_ref, buffer) = refs[:count], refs[count:]
+    rows = pieces[0].shape[0]
+    for index, piece in enumerate(pieces):
+        buffer[index * rows : (index + 1) * rows] = piece[...]
+    x = (part_ref[...] + mm(f_ref[...], buffer[...])).astype(BF16)
+    x_ref[...] = x
+    total = None
+    for k in range(e_ref.shape[0]):
+        part = slice(k * SPAN, (k + 1) * SPAN)
+        columns = rt_ref[0, part]
+        to_end = jnp.exp2(spread_columns(columns[SPAN - 1 : SPAN] - columns))
+        scaled = (x[part].astype(F32) * to_end).astype(BF16)
+        state = dot(b_ref[part], scaled, ((0,), (0,)))
+        e_ref[k] = state
+        total = state if total is None else kept_ref[k, :1] * total + state
+    total_ref[...] = total
+    sent_ref[...] = total.astype(BF16)
+
+
+def blocks_kernel(halves, has_before, order_ref, g_ref, *refs):
+    count = len(halves)
+    number = sum(halves)
+    arrays, refs = refs[:number], refs[number:]
+    if has_before:
+        refs = refs[2:]
+    away_ref, own_ref, buffer, slots, sems, out_sems = refs
+    rows = arrays[0].shape[0]
+    wide = g_ref.shape[1]
     copies = []
-    for index, (ref, column) in enumerate(zip(arrays, columns)):
-        rows = ref.shape[0]
-        source = ref.at[:, pl.ds(column, buffer.shape[1])]
-        target = buffer.at[pl.ds(index * rows, rows)]
-        copy = pltpu.make_async_copy(source, target, sems.at[index])
-        copy.start()
-        copies.append(copy)
-    return copies
-
-
-def bundles(count):
-    return [range(at, at + PLANE) for at in range(0, count, PLANE)]
-
-
-def pieces_forward_kernel(columns_at, here, f_ref, rt_ref, b_ref, *refs):
-    count = len(columns_at)
-    arrays, (x_ref, e_ref, buffer, total_ref, features, sems, f_sems) = refs[:count], refs[count:]
-    rows = arrays[0].shape[0]
-    f_copies = []
-    for index, bundle in enumerate(bundles(count)):
-        deep = pl.ds(bundle[0] * rows, PLANE * rows)
-        copy = pltpu.make_async_copy(f_ref.at[:, deep], features.at[:, deep], f_sems.at[index])
-        copy.start()
-        f_copies.append(copy)
-    copies = fetch(arrays, columns_at, buffer, sems)
-    groups = x_ref.shape[1] // WIDE
-    for number, bundle in enumerate(bundles(count)):
-        f_copies[number].wait()
-        for index in bundle:
-            copies[index].wait()
-        deep = slice(bundle[0] * rows, (bundle[-1] + 1) * rows)
-        for group in range(groups):
-            lanes = slice(group * WIDE, (group + 1) * WIDE)
-            term = mm(features[:, deep], buffer[deep, lanes])
-            if number == 0:
-                total_ref[:, lanes] = term
-            else:
-                total_ref[:, lanes] += term
-    for group in range(groups):
-        lanes = slice(group * WIDE, (group + 1) * WIDE)
-        x = total_ref[:, lanes].astype(BF16)
-        x_ref[:, lanes] = x
-        for k in range(e_ref.shape[0]):
-            part = slice(k * SPAN, (k + 1) * SPAN)
-            columns = rt_ref[here + group, part]
-            to_end = jnp.exp2(spread_columns(columns[SPAN - 1 : SPAN] - columns))
-            scaled = (x[part].astype(F32) * to_end).astype(BF16)
-            e_ref[k, :, lanes] = dot(b_ref[part], scaled, ((0,), (0,)))
-
-
-def pieces_product_kernel(columns_at, last, order_ref, g_ref, *refs):
-    count = len(columns_at)
-    arrays, refs = refs[:count], refs[count:]
-    if last:
-        before_ref, away_ref, own_ref = refs[:3]
-        buffer, slots, sems, out_sems, before_slots, before_sems = refs[3:]
-    else:
-        away_ref, buffer, slots, sems, out_sems = refs
-    copies = fetch(arrays, columns_at, buffer, sems)
-    rows = arrays[0].shape[0]
-    half = count // 2
-    before = []
-    if last:
-        for index in range(count):
-            source = before_ref.at[:, pl.ds(pl.multiple_of(order_ref[index] * rows, 128), rows)]
-            copy = pltpu.make_async_copy(source, before_slots.at[index], before_sems.at[index])
+    at = 0
+    for index, parts in enumerate(halves):
+        mine = []
+        for part in range(parts):
+            lanes = pl.ds(part * (wide // parts), wide // parts)
+            target = buffer.at[pl.ds(index * rows, rows), lanes]
+            copy = pltpu.make_async_copy(arrays[at], target, sems.at[at])
             copy.start()
-            before.append(copy)
+            mine.append(copy)
+            at += 1
+        copies.append(mine)
     g = g_ref[...]
-    for bundle in bundles(count):
-        for index in bundle:
-            copies[index].wait()
-        product = dot(g, buffer[bundle[0] * rows : (bundle[-1] + 1) * rows], ((1,), (1,)))
-        for index in bundle:
-            at = (index - bundle[0]) * rows
-            part = product[:, at : at + rows]
-            place = order_ref[index]
-            if last:
-                before[index].wait()
-                part = part + before_slots[index].astype(F32)
-            slots[index] = part.astype(BF16)
-            if last:
-                lanes = pl.ds(pl.multiple_of(place % half * rows, 128), rows)
-
-                @pl.when(place < half)
-                def _():
-                    target = away_ref.at[:, lanes]
-                    pltpu.make_async_copy(slots.at[index], target, out_sems.at[index]).start()
-
-                @pl.when(place >= half)
-                def _():
-                    target = own_ref.at[:, lanes]
-                    pltpu.make_async_copy(slots.at[index], target, out_sems.at[index]).start()
-            else:
-                target = away_ref.at[:, pl.ds(pl.multiple_of(place * rows, 128), rows)]
-                pltpu.make_async_copy(slots.at[index], target, out_sems.at[index]).start()
+    half = away_ref.shape[1] // rows
+    for index in range(count):
+        for copy in copies[index]:
+            copy.wait()
+        product = dot(g, buffer[index * rows : (index + 1) * rows], ((1,), (1,)))
+        slots[index] = product.astype(BF16)
+        place = order_ref[index]
+        lanes = pl.ds(pl.multiple_of(place % half * rows, 128), rows)
+
+        @pl.when(place < half)
+        def _():
+            target = away_ref.at[:, lanes]
+            pltpu.make_async_copy(slots.at[index], target, out_sems.at[index]).start()
+
+        @pl.when(place >= half)
+        def _():
+            target = own_ref.at[:, lanes]
+            pltpu.make_async_copy(slots.at[index], target, out_sems.at[index]).start()
+
     for index in range(count):
         target = away_ref.at[:, pl.ds(0, rows)]
         pltpu.make_async_copy(slots.at[index], target, out_sems.at[index]).wait()
@@ -370,7 +386,7 @@
         scratch_shapes=list(scratch),
         cost_estimate=pl.CostEstimate(flops=flops, bytes_accessed=size, transcendentals=0),
         compiler_params=pltpu.CompilerParams(
-            dimension_semantics=("arbitrary",) * len(grid), vmem_limit_bytes=48 * 2**20
+            dimension_semantics=("arbitrary",) * len(grid), vmem_limit_bytes=GRANT
         ),
     )
 
@@ -428,38 +444,6 @@
     return steps
 
 
-def gathered_products(running, spans):
-    count = lax.axis_size("ctx")
-    place = lax.axis_index("ctx")
-    heads = running.shape[0]
-    last = jnp.sum(running.reshape(heads, spans, SPAN)[:, :, SPAN - 1], axis=1)
-    every = lax.all_gather(last, "ctx")
-    index = jnp.arange(count)
-    masks = []
-    bits = []
-    bit = 1
-    while bit < count:
-        start = place // bit * bit
-        upper = (place & bit) != 0
-        beside = jnp.where(upper, start - bit, start + bit)
-        for low, high in (
-            (start, start + bit),
-            (beside, beside + bit),
-            (start, place),
-            (place + 1, start + bit),
-        ):
-            masks.append((index >= low) & (index < high))
-        bits.append((bit, upper))
-        bit *= 2
-    products = jnp.exp2(mm(jnp.stack(masks).astype(F32), every, EXACT))
-    products = jnp.repeat(products, P_SIZE, axis=1)
-    steps = []
-    for number, (bit, upper) in enumerate(bits):
-        rows = [products[at : at + 1] for at in range(4 * number, 4 * number + 4)]
-        steps.append((bit, upper, *rows))
-    return steps
-
-
 def scan_states(total, steps, reverse):
     entering = jnp.zeros_like(total)
     for bit, upper, kept, other, before_me, after_me in steps:
@@ -510,15 +494,15 @@
     return swap(value, "ctx", 2)
 
 
+EARLY = [(k, flip) for k in (0, 1, 3) for flip in range(3)]
+LATE = [(0, 3), (1, 3), (3, 3), (2, 0), (2, 1), (2, 2), (2, 3)]
+
+
 def block_order():
     place = lax.axis_index("ctx")
     layers = lax.axis_size("ctx") // PLANE
     layer, spot = place // PLANE, place % PLANE
-    order = [
-        (layer + layers - k) % layers * PLANE + (spot ^ flip)
-        for k in (0, 1, 3, 2)
-        for flip in range(PLANE)
-    ]
+    order = [(layer + layers - k) % layers * PLANE + (spot ^ flip) for k, flip in EARLY + LATE]
     return jnp.stack(order).astype(jnp.int32)
 
 
@@ -562,7 +546,7 @@
             flops=2 * length * wide * width, bytes_accessed=2 * wide * width, transcendentals=0
         ),
         compiler_params=pltpu.CompilerParams(
-            dimension_semantics=("arbitrary", "arbitrary"), vmem_limit_bytes=48 * 2**20
+            dimension_semantics=("arbitrary", "arbitrary"), vmem_limit_bytes=GRANT
         ),
     )(first, own, other, weight, running_t, b_rows)
 
@@ -599,73 +583,133 @@
             transcendentals=0,
         ),
         compiler_params=pltpu.CompilerParams(
-            dimension_semantics=("arbitrary",), vmem_limit_bytes=48 * 2**20
+            dimension_semantics=("arbitrary",), vmem_limit_bytes=GRANT
         ),
     )(half, *operands)
 
 
-def pieces_forward(features, arrays, columns_at, wide, running_t, b_rows, here):
-    length, width = features.shape
+def early_forward(features, pieces):
+    length = features.shape[0]
+    rows, columns = pieces[0].shape
+    deep = rows * len(pieces)
+    return call(
+        functools.partial(early_forward_kernel, len(pieces)),
+        (columns // WIDE,),
+        [pl.BlockSpec((length, deep), lambda h: (0, 0))]
+        + [pl.BlockSpec((rows, WIDE), lambda h: (0, h))] * len(pieces),
+        pl.BlockSpec((length, WIDE), lambda h: (0, h)),
+        shape(length, columns),
+        2 * length * columns * deep,
+        2 * columns * deep,
+        [pltpu.VMEM((deep, WIDE), BF16)],
+    )(features, *pieces)
+
+
+def late_forward(features, part, pieces, running_t, b_rows, kept, here):
+    length = features.shape[0]
+    rows, columns = pieces[0].shape
+    deep = rows * len(pieces)
     n = b_rows.shape[1]
     spans = length // SPAN
-    count = len(arrays)
+    state = pl.BlockSpec((n, WIDE), lambda h: (0, h))
     return call(
-        functools.partial(pieces_forward_kernel, columns_at, here),
+        functools.partial(late_forward_kernel, len(pieces)),
+        (columns // WIDE,),
+        [
+            pl.BlockSpec((length, deep), lambda h: (0, 0)),
+            pl.BlockSpec((length, WIDE), lambda h: (0, h + here)),
+            pl.BlockSpec((1, length, GROUP), lambda h: (h + here, 0, 0)),
+            pl.BlockSpec((length, n), lambda h: (0, 0)),
+            pl.BlockSpec((spans, 8, WIDE), lambda h: (0, 0, h + here)),
+        ]
+        + [pl.BlockSpec((rows, WIDE), lambda h: (0, h))] * len(pieces),
+        [
+            pl.BlockSpec((length, WIDE), lambda h: (0, h)),
+            pl.BlockSpec((spans, n, WIDE), lambda h: (0, 0, h)),
+            state,
+            state,
+        ],
+        [
+            shape(length, columns, dtype=BF16),
+            shape(spans, n, columns),
+            shape(n, columns),
+            shape(n, columns, dtype=BF16),
+        ],
+        2 * length * columns * deep,
+        2 * columns * deep,
+        [pltpu.VMEM((deep, WIDE), BF16)],
+    )(features, part, running_t, b_rows, kept, *pieces)
+
+
+def multiply_blocks(order, grad_x, pieces, so_far):
+    length, columns = grad_x.shape
+    arrays = [array for piece in pieces for array in piece]
+    rows = arrays[0].shape[0]
+    count = len(pieces)
+    half = shape(length, lax.axis_size("ctx") * rows // 2, dtype=BF16)
+    first = 2 + len(arrays)
+    return pl.pallas_call(
+        functools.partial(blocks_kernel, [len(piece) for piece in pieces], bool(so_far)),
+        grid=(1,),
+        in_specs=[SCALARS, pl.BlockSpec((length, columns), lambda h: (0, 0))]
+        + [ANYWHERE] * (len(arrays) + len(so_far)),
+        out_specs=[ANYWHERE, ANYWHERE],
+        out_shape=[half, half],
+        input_output_aliases={first + k: k for k in range(len(so_far))},
+        scratch_shapes=[
+            pltpu.VMEM((rows * count, columns), BF16),
+            pltpu.VMEM((count, length, rows), BF16),
+            pltpu.SemaphoreType.DMA((len(arrays),)),
+            pltpu.SemaphoreType.DMA((count,)),
+        ],
+        cost_estimate=pl.CostEstimate(
+            flops=2 * length * columns * rows * count,
+            bytes_accessed=2 * columns * rows * count,
+            transcendentals=0,
+        ),
+        compiler_params=pltpu.CompilerParams(
+            dimension_semantics=("arbitrary",), vmem_limit_bytes=GRANT
+        ),
+    )(order, grad_x, *arrays, *so_far)
+
+
+def coefficients(logs):
+    count = lax.axis_size("ctx")
+    place = lax.axis_index("ctx").astype(jnp.int32)[None]
+    columns = logs.shape[1]
+    every = lax.all_gather(logs, "ctx").reshape(count, columns)
+    steps = count.bit_length() - 1
+    return call(
+        coefficients_kernel,
         (1,),
-        [
-            ANYWHERE,
-            pl.BlockSpec(running_t.shape, lambda h: (0, 0, 0)),
-            pl.BlockSpec((length, n), lambda h: (0, 0)),
-        ]
-        + [ANYWHERE] * count,
-        [
-            pl.BlockSpec((length, wide), lambda h: (0, 0)),
-            pl.BlockSpec((spans, n, wide), lambda h: (0, 0, 0)),
-        ],
-        [shape(length, wide, dtype=BF16), shape(spans, n, wide)],
-        2 * length * wide * width,
-        2 * wide * width,
-        [
-            pltpu.VMEM((width, wide), BF16),
-            pltpu.VMEM((length, wide), F32),
-            pltpu.VMEM((length, width), BF16),
-            pltpu.SemaphoreType.DMA((count,)),
-            pltpu.SemaphoreType.DMA((count // PLANE,)),
-        ],
-    )(features, running_t, b_rows, *arrays)
-
-
-def pieces_product(order, grad_x, arrays, columns_at, wide, at, before=None):
-    length = grad_x.shape[0]
-    count = len(arrays)
-    rows = arrays[0].shape[0]
-    width = rows * count
-    last = before is not None
-    scratch = [
-        pltpu.VMEM((width, wide), BF16),
-        pltpu.VMEM((count, length, rows), BF16),
-        pltpu.SemaphoreType.DMA((count,)),
-        pltpu.SemaphoreType.DMA((count,)),
-    ]
-    if last:
-        scratch += [pltpu.VMEM((count, length, rows), BF16), pltpu.SemaphoreType.DMA((count,))]
-    half = shape(length, width // 2, dtype=BF16)
+        [SCALARS, pl.BlockSpec((count, columns), lambda h: (0, 0))],
+        pl.BlockSpec((2 * steps, 8, columns), lambda h: (0, 0, 0)),
+        shape(2 * steps, 8, columns),
+        0,
+        256 * columns,
+    )(place, every)
+
+
+def scan_step(factors, number, here, total, sent, entering, bit):
+    got = swap(sent, "ctx", bit)
+    n, columns = total.shape
+    block = pl.BlockSpec((n, WIDE), lambda h: (0, h))
     return call(
-        functools.partial(pieces_product_kernel, columns_at, last),
-        (1,),
-        [SCALARS, pl.BlockSpec((length, wide), lambda h: (0, at))] + [ANYWHERE] * (count + last),
-        [ANYWHERE, ANYWHERE] if last else ANYWHERE,
-        [half, half] if last else shape(length, width, dtype=BF16),
-        2 * length * wide * width,
-        2 * wide * width,
-        scratch,
-    )(order, grad_x, *arrays, *([before] if last else []))
+        scan_kernel,
+        (columns // WIDE,),
+        [pl.BlockSpec((1, 8, WIDE), lambda h: (number, 0, h + here)), block, block]
+        + [block] * len(entering),
+        [block, block, block],
+        [shape(n, columns), shape(n, columns), shape(n, columns, dtype=BF16)],
+        0,
+        14 * n * columns,
+    )(factors, total, got, *entering)
 
 
 def local(inputs, w_in, b_rows, c_rows, log_decay, skip_gain, grad_out):
     groups = log_decay.shape[0] // GROUP
     layered = lax.axis_size("ctx") == 4 * PLANE and lax.axis_size("head") == 2
-    if layered and groups >= 2 and w_in.shape[0] == 256:
+    if layered and groups % 2 == 0 and w_in.shape[0] == 256:
         return local_layered(inputs, w_in, b_rows, c_rows, log_decay, skip_gain, grad_out)
     return local_plain(inputs, w_in, b_rows, c_rows, log_decay, skip_gain, grad_out)
 
@@ -690,18 +734,6 @@
         2 * length * columns * n,
         6 * length * columns,
     )(log_decay, grad_out, c_rows)
-
-
-def scan_step(total, entering, step, reverse):
-    bit, upper, kept, other, before_me, after_me = step
-    got = swap(total.astype(BF16), "ctx", bit).astype(F32)
-    if reverse:
-        entering = entering + jnp.where(upper, 0.0, after_me) * got
-        total = jnp.where(upper, got + other * total, total + kept * got)
-    else:
-        entering = entering + jnp.where(upper, before_me, 0.0) * got
-        total = jnp.where(upper, kept * got + total, other * total + got)
-    return total, entering
 
 
 def inner(grid, here, wide, operands, so_far):
@@ -759,38 +791,30 @@
     spans = length // SPAN
     groups = heads // GROUP
     place = lax.axis_index("head").astype(jnp.int32)
-    cut = columns - WIDE
-    w_a, w_b = w_in[:, :cut], w_in[:, cut:]
+    half = columns // 2
+    w_a, w_b = w_in[:, :half], w_in[:, half:]
     order = block_order()
     blocks = order.shape[0]
     width = blocks * w_in.shape[0]
 
-    z1a, z3a = shift(w_a, 1), shift(w_a, 3)
+    z1, z3 = shift(w_in, 1), shift(w_in, 3)
     own_x, own_y = swap_x(w_in), swap_y(w_in)
     other = swap(inputs, "head", 1)
     running, running_t, kept, own_grads = prepare(log_decay, grad_out, c_rows)
-    steps = gathered_products(running, spans)
+    factors = coefficients(jnp.sum(kept[:, 4:5], axis=0))
     back = own_grads[spans - 1]
     for k in range(spans - 2, -1, -1):
         back = own_grads[k] + kept[k, :1] * back
-    leaving = jnp.zeros_like(back)
-    back = after([back], z1a, z3a)[0]
-
-    w_a, z1a, z3a = after([w_a, z1a, z3a], own_x, own_y, back)
-    z2a = shift(w_a, 2)
-    x1a, y1a, x3a, y3a = swap_x(z1a), swap_y(z1a), swap_x(z3a), swap_y(z3a)
-    back, leaving = scan_step(back, leaving, steps[0], True)
-
-    z2a, x1a, y3a = after([z2a, x1a, y3a], y1a, x3a, back, other)
-    x2a, y2a = swap_x(z2a), swap_y(z2a)
-    d1a, d3a = swap_y(x1a), swap_x(y3a)
-    back, leaving = scan_step(back, leaving, steps[1], True)
-
-    own_y, x2a, w_b = after([own_y, x2a, w_b], y2a, d1a, d3a, back)
-    own_d, d2a = swap_x(own_y), swap_y(x2a)
-    z1b, z3b, z2b = shift(w_b, 1), shift(w_b, 3), shift(w_b, 2)
-    back, leaving = scan_step(back, leaving, steps[2], True)
-
+    sent = back.astype(BF16)
+    sent = after([sent], other)[0]
+    back, leaving, sent = scan_step(factors, 4, 0, back, sent, (), 1)
+
+    z1, w_a, w_b = after([z1, w_a, w_b], own_x, own_y, z3)
+    z2a, z2b = shift(w_a, 2), shift(w_b, 2)
+    x1, y1 = swap_x(z1), swap_y(z1)
+    z3 = after([z3], sent)[0]
+    x3, y3 = swap_x(z3), swap_y(z3)
+    back, leaving, sent = scan_step(factors, 5, 0, back, sent, (leaving,), 2)
     order_own = (order + place * (blocks // 2)) % blocks
     features = call(
         arrange_kernel,
@@ -802,73 +826,80 @@
         4 * length * width,
         [pltpu.VMEM((length, width), BF16)],
     )(order_own, inputs, other)
-
-    z1b, z3b, z2b, d2a = after([z1b, z3b, z2b, d2a], own_d, back, features)
-    x1b, x3b, x2b = swap_x(z1b), swap_x(z3b), swap_x(z2b)
-    y1b, y3b, y2b = swap_y(z1b), swap_y(z3b), swap_y(z2b)
-    back, leaving = scan_step(back, leaving, steps[3], True)
-    arrays_a = [w_in, own_x, own_y, own_d, z1a, x1a, y1a, d1a, z3a, x3a, y3a, d3a]
-    arrays_a += [z2a, x2a, y2a, d2a]
-    at_a = [0] * len(arrays_a)
-    x_a, states_a = pieces_forward(features, arrays_a, at_a, cut, running_t, b_rows, 0)
-
+    cut = len(EARLY) * w_in.shape[0]
+    early_features, late_features = features[:, :cut], features[:, cut:]
+
+    z2a, x1, y3, own_y = after(
+        [z2a, x1, y3, own_y], y1, x3, z2b, sent, early_features, late_features
+    )
+    x1_a, x1_b = x1[:, :half], x1[:, half:]
+    y3_a, y3_b = y3[:, :half], y3[:, half:]
+    own_y_a, own_y_b = own_y[:, :half], own_y[:, half:]
+    x2a, y2a = swap_x(z2a), swap_y(z2a)
+    d3a, d1a = swap_x(y3_a), swap_y(x1_a)
+    back, leaving, sent = scan_step(factors, 6, 0, back, sent, (leaving,), 4)
+    early = [w_in, own_x, own_y, z1, x1, y1, z3, x3, y3]
+    part = early_forward(early_features, early)
+
+    own_y_a, x2a, z2b, y3_b, x1_b = after(
+        [own_y_a, x2a, z2b, y3_b, x1_b], y2a, d3a, d1a, part, sent
+    )
+    d0a, d2a = swap_x(own_y_a), swap_y(x2a)
+    x2b, y2b = swap_x(z2b), swap_y(z2b)
+    d3b, d1b = swap_x(y3_b), swap_y(x1_b)
+    back, leaving, sent = scan_step(factors, 7, 0, back, sent, (leaving,), 8)
     leaving_all = [leaving]
     for k in range(spans - 1, 0, -1):
         leaving_all.insert(0, own_grads[k] + kept[k, :1] * leaving_all[0])
     leaving_all = jnp.stack([value.astype(BF16) for value in leaving_all])
     skip = jnp.repeat(skip_gain, P_SIZE)[None]
     grad_x = grad_rows(running, running_t, grad_out, b_rows, c_rows, leaving_all, skip)
-
-    def forward_total(states, lanes):
-        total = states[0]
-        for k in range(1, spans):
-            total = kept[k, :1, lanes] * total + states[k]
-        return total
-
-    def narrow(step, lanes):
-        return step[:2] + tuple(value[:, lanes] for value in step[2:])
-
-    lanes_a, lanes_b = slice(0, cut), slice(cut, columns)
-    steps_a = [narrow(step, lanes_a) for step in steps]
-    steps_b = [narrow(step, lanes_b) for step in steps]
-    total_a = forward_total(states_a, lanes_a)
-    entering_a = jnp.zeros_like(total_a)
-    total_a, entering_a = scan_step(total_a, entering_a, steps_a[0], False)
-
-    x1b, y3b, x2b, x_a, grad_x = after([x1b, y3b, x2b, x_a, grad_x], x3b, y1b, y2b, total_a)
-    d1b, d3b, d2b = swap_y(x1b), swap_x(y3b), swap_y(x2b)
-    total_a, entering_a = scan_step(total_a, entering_a, steps_a[1], False)
-
+    late_a = [d0a, d1a, d3a, z2a, x2a, y2a, d2a]
+    x_a, states_a, total_a, sent_a = late_forward(
+        late_features, part, late_a, running_t, b_rows, kept, 0
+    )
+
+    own_y_b, x2b, sent_a = after([own_y_b, x2b, sent_a], y2b, d3b, d1b, grad_x)
+    d0b, d2b = swap_x(own_y_b), swap_y(x2b)
+    total_a, entering_a, sent_a = scan_step(factors, 0, 0, total_a, sent_a, (), 1)
+    order_away = (order + (1 - place) * (blocks // 2)) % blocks
+    early_order, late_order = order_away[: len(EARLY)], order_away[len(EARLY) :]
+    product = multiply_blocks(early_order, grad_x, [[piece] for piece in early], ())
+
+    d0b, d2b = after([d0b, d2b], sent_a, product[0])
+    late_b = [d0b, d1b, d3b, z2b, x2b, y2b, d2b]
+    here = groups // 2
+    x_b, states_b, total_b, sent_b = late_forward(
+        late_features, part, late_b, running_t, b_rows, kept, here
+    )
+    pairs = list(zip(late_a, late_b))
+    product = after(list(product), sent_b)
+    away, own = multiply_blocks(late_order, grad_x, pairs, product)
+    got = swap(away, "head", 1)
+    entering_b = ()
+    for number, bit in enumerate((1, 2, 4, 8)):
+        if number > 0:
+            total_a, entering_a, sent_a = scan_step(
+                factors, number, 0, total_a, sent_a, (entering_a,), bit
+            )
+        total_b, entering_b, sent_b = scan_step(
+            factors, number, here, total_b, sent_b, entering_b, bit
+        )
+        entering_b = (entering_b,)
+    entering_b = entering_b[0]
     shared = (running, running_t, grad_out)
-    order_away = (order + (1 - place) * (blocks // 2)) % blocks
-    grid_a, grid_b = (spans, groups - 1), (spans, 1)
+    grid = (spans, here)
     inner_a = shared + (x_a, b_rows, c_rows, leaving_all)
-    decay_a, grad_b, grad_c = inner(grid_a, 0, cut, inner_a, ())
-    product = pieces_product(order_away, grad_x, arrays_a, at_a, cut, 0)
-
-    d1b, d3b, d2b = after([d1b, d3b, d2b], product, grad_b, total_a)
-    arrays_b = [w_in, own_x, own_y, own_d, z1b, x1b, y1b, d1b, z3b, x3b, y3b, d3b]
-    arrays_b += [z2b, x2b, y2b, d2b]
-    at_b = [cut] * PLANE + [0] * (len(arrays_b) - PLANE)
-    here = groups - 1
-    x_b, states_b = pieces_forward(features, arrays_b, at_b, WIDE, running_t, b_rows, here)
-    total_b = forward_total(states_b, lanes_b)
-    entering_b = jnp.zeros_like(total_b)
-    for step_a, step_b in zip(steps_a[2:] + [None] * 2, steps_b):
-        if step_a is not None:
-            total_a, entering_a = scan_step(total_a, entering_a, step_a, False)
-        total_b, entering_b = scan_step(total_b, entering_b, step_b, False)
+    decay_a, grad_b, grad_c = inner(grid, 0, half, inner_a, ())
     inner_b = shared + (x_b, b_rows, c_rows, leaving_all)
-    decay_b, grad_b, grad_c = inner(grid_b, here, WIDE, inner_b, (grad_b, grad_c))
-    away, own = pieces_product(order_away, grad_x, arrays_b, at_b, WIDE, here, product)
-    got = swap(away, "head", 1)
+    decay_b, grad_b, grad_c = inner(grid, here, half, inner_b, (grad_b, grad_c))
     grad_b = head_sum(grad_b)
 
     common = (running_t, grad_out, c_rows)
     state_a = common + (entering_a, states_a, leaving_all, kept, decay_a, grad_c)
-    decay_a, grad_c = state_terms(grid_a, 0, cut, state_a)
+    decay_a, grad_c = state_terms(grid, 0, half, state_a)
     state_b = common + (entering_b, states_b, leaving_all, kept, decay_b, grad_c)
-    decay_b, grad_c = state_terms(grid_b, here, WIDE, state_b)
+    decay_b, grad_c = state_terms(grid, here, half, state_b)
     grad_inputs = (own.astype(F32) + got.astype(F32)).astype(BF16)
     grad_log_decay = jnp.concatenate([decay_a, decay_b], axis=0)
     return (grad_inputs, grad_b, head_sum(grad_c), grad_log_decay)

time: 376 us -> 353 us (0.939)
  Pallas kernels: 87.4 us -> 148 us
  waiting for transfers between devices: 101 us -> 55.5 us
  local copies, waits for them, and re-layouts: 52.9 us -> 29.3 us
  other arithmetic: 33.3 us -> 15.3 us
  blocking collectives: 50.5 us -> 64.2 us
  starting transfers between devices: 47 us -> 38.4 us
    all_gather x0 -> x1, blocking collectives: none -> 64.2 us  [coefficients(): every = lax.all_gather(logs, 'ctx').reshape(count, columns)]
    unnamed x1 -> x0, blocking collectives: 50.5 us -> none
    ppermute x37 -> x34, waiting for transfers between devices: 87.9 us -> 39.7 us  [swap(): return lax.ppermute(value, axis, [(i, i ^ bit) for i in range(count)])]
    pallas_call x4 -> x18, Pallas kernels: 37.8 us -> 85.6 us  [the longest x12 33.6 us: scan_step(): call(scan_kernel, (columns // WIDE,), [pl.BlockSpec((1, 8, WIDE), lambda...]
    unnamed x233 -> x82, local copies, waits for them, and re-layouts: 38.5 us -> 15 us
    convert_element_type x12 -> x1, other arithmetic: 16.9 us -> 2.98 us  [local_layered(): sent = back.astype(BF16)]
    ppermute x37 -> x34, starting transfers between devices: 39.7 us -> 31.8 us  [swap(): return lax.ppermute(value, axis, [(i, i ^ bit) for i in range(count)])]
    select_n x8 -> x0, other arithmetic: 4.39 us -> none  [scan_step(): entering = entering + jnp.where(upper, before_me, 0.0) * got]
  transfers between devices with their start and end apart: 43 -> 38, of which waited for: 14 -> 8; matrix products, arithmetic and copies ran while one was open for 11% -> 8% of each run, Pallas kernels for 22% -> 37%
where the time goes in v3:
time: 353 us; the launch traced here: 352 us
  Pallas kernels  148 us (42%)
  blocking collectives  64.2 us (18%)
  waiting for transfers between devices  55.5 us (16%)
  starting transfers between devices  38.4 us (11%)
  local copies, waits for them, and re-layouts  29.3 us (8%)
  other arithmetic  15.3 us (4%)
    all_gather x1, blocking collectives, coefficients(): every = lax.all_gather(logs, 'ctx').reshape(count, columns)  64.2 us
    ppermute x34, waiting for transfers between devices, swap(): return lax.ppermute(value, axis, [(i, i ^ bit) for i in range(count)])  39.7 us
    pallas_call x12, Pallas kernels, scan_step(): call(scan_kernel, (columns // WIDE,), [pl.BlockSpec((1, 8, WIDE), lambda...  33.6 us
    ppermute x34, starting transfers between devices, swap(): return lax.ppermute(value, axis, [(i, i ^ bit) for i in range(count)])  31.8 us
    pallas_call x2, Pallas kernels, inner(): call(inner_kernel, grid, specs + [SHARED] * len(so_far), [run_spec(), SHA...  27.1 us
    pallas_call x2, Pallas kernels, multiply_blocks(): pl.pallas_call(functools.partial(blocks_kernel, [len(piece) for piece in...  26.7 us
    ppermute x4, waiting for transfers between devices, shift(): lax.ppermute(value, 'ctx', [(i, (i + PLANE * by) % count) for i in range(...  15.7 us
    unnamed x82, local copies, waits for them, and re-layouts  15 us
  transfers between devices with their start and end apart: 38, of which 8 were waited for; matrix products, arithmetic and copies ran while one was open for 8% of the time, Pallas kernels for 37%

profile of v3, /device:TPU:0, one launch (start us, length us, event | category | flops | bytes accessed | tf_op | source)
XLA Modules:
  0.0 351.7 jit_solution(8782431361839806501)
XLA Ops:
  1.1 2.6 collective-permute-start.7
  3.7 1.5 collective-permute-start.6
  5.2 3.6 %collective-permute-start.8 = (bf16[256,2048]{1,0:T(8,128)(2,1)}, bf16[256,2048]{1,0:T(8,128)(2,1)}, u32[]{:S(2)}, u32[]{:S(2)}) collective-permute-start(bf16[256,2048]{1,0:T(8,128)(2,1)} %refs_0_.3), channel_id=1, source_target_pairs={{0,24},{2,26},{4,28},{6,30},{8,0},{10,2},{12,4},{14,6},{16,8},{18,... | collective-permute-start | bytes 3145736 | tf_op jit(solution)/shard_map/ppermute | solution.py:486
  8.8 9.1 %shard_map.102 = (f32[32,512]{1,0:T(8,128)}, f32[4,512,8]{2,1,0:T(8,128)}, f32[2,8,2048]{2,1,0:T(8,128)}, f32[2,128,2048]{2,1,0:T(8,128)}) custom-call(f32[32,512]{1,0:T(8,128)} %d_ref.1, bf16[512,2048]{1,0:T(8,128)(2,1)} %g_ref.11, bf16[512,128]{1,0:T(8,128)(2,1)} %c_ref.11), custom_call_target="tpu_custom_call" | custom-call | flops 268435456 | bytes 6291456 | tf_op jit(solution)/shard_map/pallas_call | solution.py:723
  18.8 3.0 fusion.4
  21.8 1.3 copy-done.3
  24.6 64.2 %all-gather = f32[32768]{0:T(1024)S(1)} all-gather(f32[2048]{0:T(1024)S(1)} %slice_reduce_fusion), channel_id=2, replica_groups=mesh['ctx'=16,'head'=2] {'ctx'}, dimensions={0}, use_global_device_ids=true | all-gather | bytes 139264 | tf_op jit(solution)/shard_map/all_gather | solution.py:680
  89.4 2.1 shard_map.103.factor_ref
  91.5 2.2 fusion.8
  93.8 1.0 copy-done
  95.6 3.9 %shard_map.105 = (f32[128,2048]{1,0:T(8,128)}, f32[128,2048]{1,0:T(8,128)}, bf16[128,2048]{1,0:T(8,128)(2,1)}) custom-call(f32[8,8,2048]{2,1,0:T(8,128)} %shard_map.103.factor_ref, f32[128,2048]{1,0:T(8,128)} %get-tuple-element.155.total_ref, bf16[128,2048]{1,0:T(8,128)(2,1)} %copy-done.25), custom_call_target="tpu_custom_call" | custom-call | bytes 3670016 | tf_op jit(solution)/shard_map/pallas_call | solution.py:697
  99.4 2.0 collective-permute-start.12
  101.5 2.0 collective-permute-start.13
  103.5 4.9 %collective-permute-done.9.refs_0_ = bf16[256,1024]{1,0:T(8,128)(2,1)} collective-permute-done((bf16[256,1024]{1,0:T(8,128)(2,1)}, bf16[256,1024]{1,0:T(8,128)(2,1)}, u32[]{:S(2)}, u32[]{:S(2)}) %collective-permute-start.9) | collective-permute-done | bytes 524320 | tf_op jit(solution)/shard_map/ppermute | solution.py:486
  108.4 1.0 collective-permute-start.11
  109.4 5.2 %collective-permute-done.2.got_ref = bf16[128,2048]{1,0:T(8,128)(2,1)S(1)} collective-permute-done((bf16[128,2048]{1,0:T(8,128)(2,1)}, bf16[128,2048]{1,0:T(8,128)(2,1)S(1)}, u32[]{:S(2)}, u32[]{:S(2)}) %collective-permute-start.2) | collective-permute-done | bytes 524320 | tf_op jit(solution)/shard_map/ppermute | solution.py:426
  115.3 2.9 collective-permute-start.14
  118.2 4.1 %shard_map.106 = (f32[128,2048]{1,0:T(8,128)}, f32[128,2048]{1,0:T(8,128)}, bf16[128,2048]{1,0:T(8,128)(2,1)}) custom-call(f32[8,8,2048]{2,1,0:T(8,128)} %shard_map.103.factor_ref, f32[128,2048]{1,0:T(8,128)} %get-tuple-element.83.total_ref, bf16[128,2048]{1,0:T(8,128)(2,1)} %copy-done.26, f32[128,2048]{1,0:T(8,128)} %get-tuple-element.85.refs_0_), custom_call_target="tpu_custom_call" | custom-call | bytes 3670016 | tf_op jit(solution)/shard_map/pallas_call | solution.py:697
  122.3 10.8 %collective-permute-done.14.refs_6_.refs_2_ = bf16[256,1024]{1,0:T(8,128)(2,1)S(1)} collective-permute-done((bf16[256,1024]{1,0:T(8,128)(2,1)S(1)}, bf16[256,1024]{1,0:T(8,128)(2,1)S(1)}, u32[]{:S(2)}, u32[]{:S(2)}) %collective-permute-start.14) | collective-permute-done | bytes 524320 | tf_op jit(solution)/shard_map/ppermute | solution.py:486
  134.5 5.1 %shard_map.112 = bf16[512,4096]{1,0:T(8,128)(2,1)} custom-call(s32[16]{0:T(128)} %get-tuple-element.168.order_ref, bf16[512,2048]{1,0:T(8,128)(2,1)} %own_ref.1, bf16[512,2048]{1,0:T(8,128)(2,1)} %copy-done.3), custom_call_target="tpu_custom_call" | custom-call | bytes 8388608 | tf_op jit(solution)/shard_map/pallas_call | solution.py:819
  139.7 2.8 slice.70.refs_9_.f_ref
  142.5 3.2 slice.69.refs_8_.f_ref
  145.8 5.3 %collective-permute-done.11.refs_2_ = bf16[256,2048]{1,0:T(8,128)(2,1)S(1)} collective-permute-done((bf16[256,2048]{1,0:T(8,128)(2,1)}, bf16[256,2048]{1,0:T(8,128)(2,1)S(1)}, u32[]{:S(2)}, u32[]{:S(2)}) %collective-permute-start.11) | collective-permute-done | bytes 1048608 | tf_op jit(solution)/shard_map/ppermute | solution.py:426
  151.1 1.0 copy-done.8
  153.2 4.1 %shard_map.107 = (f32[128,2048]{1,0:T(8,128)}, f32[128,2048]{1,0:T(8,128)}, bf16[128,2048]{1,0:T(8,128)(2,1)}) custom-call(f32[8,8,2048]{2,1,0:T(8,128)} %shard_map.103.factor_ref, f32[128,2048]{1,0:T(8,128)} %get-tuple-element.86.total_ref, bf16[128,2048]{1,0:T(8,128)(2,1)} %copy-done.23, f32[128,2048]{1,0:T(8,128)} %get-tuple-element.88.refs_0_), custom_call_target="tpu_custom_call" | custom-call | bytes 3670016 | tf_op jit(solution)/shard_map/pallas_call | solution.py:697
  157.4 3.4 collective-permute-start.4
  161.7 2.0 collective-permute-start.17
  164.6 2.0 collective-permute-start.18
  166.6 1.1 fusion.5
  167.7 10.2 %shard_map.114.refs_8_.part_ref = f32[512,2048]{1,0:T(8,128)} custom-call(bf16[512,2304]{1,0:T(8,128)(2,1)} %slice.69.refs_8_.f_ref, bf16[256,2048]{1,0:T(8,128)(2,1)} %refs_0_.3, bf16[256,2048]{1,0:T(8,128)(2,1)} %collective-permute-done.6.refs_3_.refs_1_, bf16[256,2048]{1,0:T(8,128)(2,1)} %get-tuple-element.96.refs_2_, ...), custom_call_target="tpu_custom_call" | custom-call | flops 4831838208 | bytes 9437184 | tf_op jit(solution)/shard_map/pallas_call | solution.py:595
  179.3 2.0 collective-permute-start.19
  181.4 2.0 collective-permute-start.21
  183.4 4.1 %shard_map.108 = (f32[128,2048]{1,0:T(8,128)}, f32[128,2048]{1,0:T(8,128)}, bf16[128,2048]{1,0:T(8,128)(2,1)}) custom-call(f32[8,8,2048]{2,1,0:T(8,128)} %shard_map.103.factor_ref, f32[128,2048]{1,0:T(8,128)} %get-tuple-element.89.total_ref, bf16[128,2048]{1,0:T(8,128)(2,1)} %copy-done.24, f32[128,2048]{1,0:T(8,128)} %get-tuple-element.91.refs_0_), custom_call_target="tpu_custom_call" | custom-call | bytes 3670016 | tf_op jit(solution)/shard_map/pallas_call | solution.py:697
  187.5 1.8 fusion.1
  189.4 13.9 %collective-permute-done.19.refs_0_ = bf16[256,1024]{1,0:T(8,128)(2,1)S(1)} collective-permute-done((bf16[256,1024]{1,0:T(8,128)(2,1)}, bf16[256,1024]{1,0:T(8,128)(2,1)S(1)}, u32[]{:S(2)}, u32[]{:S(2)}) %collective-permute-start.19) | collective-permute-done | bytes 524320 | tf_op jit(solution)/shard_map/ppermute | solution.py:426
  204.2 1.1 pad_maximum_fusion.q_ref
  205.3 9.9 %shard_map.109.refs_6_.g_ref = bf16[512,2048]{1,0:T(8,128)(2,1)} custom-call(f32[32,512]{1,0:T(8,128)} %get-tuple-element.79.r_ref, f32[4,512,8]{2,1,0:T(8,128)} %get-tuple-element.80.rt_ref, bf16[512,2048]{1,0:T(8,128)(2,1)} %g_ref.11, bf16[512,128]{1,0:T(8,128)(2,1)} %b_ref.9, bf16[512,128]{1,0:T(8,128)(2,1)} %c_ref.11, ...), custom_call_target="tpu_custom_call" | custom-call | flops 2147483648 | bytes 6291456 | tf_op jit(solution)/shard_map/pallas_call | solution.py:910
  215.2 6.6 %shard_map.116 = (bf16[512,1024]{1,0:T(8,128)(2,1)}, f32[2,128,1024]{2,1,0:T(8,128)}, f32[128,1024]{1,0:T(8,128)}, bf16[128,1024]{1,0:T(8,128)(2,1)}) custom-call(bf16[512,1792]{1,0:T(8,128)(2,1)} %slice.70.refs_9_.f_ref, f32[512,2048]{1,0:T(8,128)} %shard_map.114.refs_8_.part_ref, f32[4,512,8]{2,1,0:T(8,128)} %get-tuple-element.80.rt_ref, ...), custom_call_target="tpu_custom_call" | custom-call | flops 1879048192 | bytes 3670016 | tf_op jit(solution)/shard_map/pallas_call | solution.py:615
  223.5 1.1 collective-permute-start.26
  225.3 1.7 collective-permute-start.27
  227.0 14.6 %shard_map.119 = (bf16[512,2048]{1,0:T(8,128)(2,1)}, bf16[512,2048]{1,0:T(8,128)(2,1)}) custom-call(s32[9]{0:T(128)} %bitcast.39, bf16[512,2048]{1,0:T(8,128)(2,1)} %shard_map.109.refs_6_.g_ref, bf16[256,2048]{1,0:T(8,128)(2,1)} %refs_0_.3, bf16[256,2048]{1,0:T(8,128)(2,1)} %collective-permute-done.6.refs_3_.refs_1_, ...), custom_call_target="tpu_custom_call" | custom-call | flops 4831838208 | bytes 9437184 | tf_op jit(solution)/shard_map/pallas_call | solution.py:651
  242.3 2.1 shard_map.118
  245.3 6.5 %shard_map.121 = (bf16[512,1024]{1,0:T(8,128)(2,1)}, f32[2,128,1024]{2,1,0:T(8,128)}, f32[128,1024]{1,0:T(8,128)}, bf16[128,1024]{1,0:T(8,128)(2,1)}) custom-call(bf16[512,1792]{1,0:T(8,128)(2,1)} %slice.70.refs_9_.f_ref, f32[512,2048]{1,0:T(8,128)} %shard_map.114.refs_8_.part_ref, f32[4,512,8]{2,1,0:T(8,128)} %get-tuple-element.80.rt_ref, ...), custom_call_target="tpu_custom_call" | custom-call | flops 1879048192 | bytes 3670016 | tf_op jit(solution)/shard_map/pallas_call | solution.py:615
  251.9 12.1 %shard_map.123 = (bf16[512,2048]{1,0:T(8,128)(2,1)}, bf16[512,2048]{1,0:T(8,128)(2,1)}) custom-call(s32[7]{0:T(128)} %slice.52.order_ref, bf16[512,2048]{1,0:T(8,128)(2,1)} %shard_map.109.refs_6_.g_ref, bf16[256,1024]{1,0:T(8,128)(2,1)} %copy-done.27, ...), custom_call_target="tpu_custom_call", output_to_operand_aliasing={{0}: (16, {}), {1}: (17, {})} | custom-call | flops 3758096384 | bytes 7340032 | tf_op jit(solution)/shard_map/pallas_call | solution.py:651
  265.4 7.4 %collective-permute-done.30.got_ref = bf16[128,1024]{1,0:T(8,128)(2,1)S(1)} collective-permute-done((bf16[128,1024]{1,0:T(8,128)(2,1)S(1)}, bf16[128,1024]{1,0:T(8,128)(2,1)S(1)}, u32[]{:S(2)}, u32[]{:S(2)}) %collective-permute-start.30) | collective-permute-done | bytes 262176 | tf_op jit(solution)/shard_map/ppermute | solution.py:426
  273.5 2.1 shard_map.126
  277.3 2.2 shard_map.130
  279.5 4.2 %collective-permute-done.31.got_ref = bf16[128,1024]{1,0:T(8,128)(2,1)S(1)} collective-permute-done((bf16[128,1024]{1,0:T(8,128)(2,1)}, bf16[128,1024]{1,0:T(8,128)(2,1)S(1)}, u32[]{:S(2)}, u32[]{:S(2)}) %collective-permute-start.31) | collective-permute-done | bytes 262176 | tf_op jit(solution)/shard_map/ppermute | solution.py:426
  284.4 2.2 shard_map.127
  288.0 2.2 shard_map.131
  290.2 2.0 collective-permute-start.36
  292.2 3.7 %collective-permute-done.32.got_ref = bf16[128,1024]{1,0:T(8,128)(2,1)S(1)} collective-permute-done((bf16[128,1024]{1,0:T(8,128)(2,1)}, bf16[128,1024]{1,0:T(8,128)(2,1)S(1)}, u32[]{:S(2)}, u32[]{:S(2)}) %collective-permute-start.32) | collective-permute-done | bytes 262176 | tf_op jit(solution)/shard_map/ppermute | solution.py:426
  296.5 2.2 shard_map.128
  299.0 13.4 %shard_map.124 = (f32[16,512]{1,0:T(8,128)}, f32[512,128]{1,0:T(8,128)}, f32[512,128]{1,0:T(8,128)}) custom-call(f32[32,512]{1,0:T(8,128)} %get-tuple-element.79.r_ref, f32[4,512,8]{2,1,0:T(8,128)} %get-tuple-element.80.rt_ref, bf16[512,2048]{1,0:T(8,128)(2,1)} %g_ref.11, bf16[512,1024]{1,0:T(8,128)(2,1)} %get-tuple-element.121.x_ref, ...), custom_call_target="tpu_custom_call" | custom-call | flops 1610612736 | bytes 3145728 | tf_op jit(solution)/shard_map/pallas_call | solution.py:751
  312.4 13.6 %shard_map.125 = (f32[16,512]{1,0:T(8,128)}, f32[512,128]{1,0:T(8,128)}, f32[512,128]{1,0:T(8,128)}) custom-call(f32[32,512]{1,0:T(8,128)} %get-tuple-element.79.r_ref, f32[4,512,8]{2,1,0:T(8,128)} %get-tuple-element.80.rt_ref, bf16[512,2048]{1,0:T(8,128)(2,1)} %g_ref.11, bf16[512,1024]{1,0:T(8,128)(2,1)} %get-tuple-element.120.x_ref, ...), custom_call_target="tpu_custom_call" | custom-call | flops 1610612736 | bytes 3145728 | tf_op jit(solution)/shard_map/pallas_call | solution.py:751
  326.0 1.0 convert_element_type.42
  327.8 2.2 shard_map.132
  330.0 5.5 %shard_map.133 = (f32[16,512]{1,0:T(8,128)}, f32[512,128]{1,0:T(8,128)}) custom-call(f32[4,512,8]{2,1,0:T(8,128)} %get-tuple-element.80.rt_ref, bf16[512,2048]{1,0:T(8,128)(2,1)} %g_ref.11, bf16[512,128]{1,0:T(8,128)(2,1)} %c_ref.11, f32[128,1024]{1,0:T(8,128)} %get-tuple-element.146.s_ref, f32[2,128,1024]{2,1,0:T(8,128)} %get-tuple-element.147.e_ref, ...), custom_call_target="tpu_custom_call" | custom-call | flops 268435456 | bytes 3145728 | tf_op jit(solution)/shard_map/pallas_call | solution.py:766
  336.2 2.2 shard_map.129
  338.4 5.7 %shard_map.134 = (f32[16,512]{1,0:T(8,128)}, f32[512,128]{1,0:T(8,128)}) custom-call(f32[4,512,8]{2,1,0:T(8,128)} %get-tuple-element.80.rt_ref, bf16[512,2048]{1,0:T(8,128)(2,1)} %g_ref.11, bf16[512,128]{1,0:T(8,128)(2,1)} %c_ref.11, f32[128,1024]{1,0:T(8,128)} %get-tuple-element.135.s_ref, f32[2,128,1024]{2,1,0:T(8,128)} %get-tuple-element.136.e_ref, ...), custom_call_target="tpu_custom_call" | custom-call | flops 268435456 | bytes 3145728 | tf_op jit(solution)/shard_map/pallas_call | solution.py:766
  344.1 1.0 convert_element_type.45
  346.3 1.4 pad_maximum_fusion.1
  347.7 1.7 convert_add_fusion
  349.4 2.2 add_convert_fusion
  (151 shorter events, 25.4 us)
Async XLA Ops:
  0.6 21.2 %collective-permute-start = (bf16[512,2048]{1,0:T(8,128)(2,1)}, bf16[512,2048]{1,0:T(8,128)(2,1)S(1)}, u32[]{:S(2)}, u32[]{:S(2)}) collective-permute-start(bf16[512,2048]{1,0:T(8,128)(2,1)} %own_ref.1), channel_id=1, source_target_pairs={{0,1},{1,0},{2,3},{3,2},{4,5},{5,4},{6,7},{7,6},{8,9},{9,8},{10,11... | collective-permute-start | bytes 6291464 | tf_op jit(solution)/shard_map/ppermute | solution.py:426
  1.1 92.6 %collective-permute-start.7 = (bf16[256,2048]{1,0:T(8,128)(2,1)}, bf16[256,2048]{1,0:T(8,128)(2,1)S(1)}, u32[]{:S(2)}, u32[]{:S(2)}) collective-permute-start(bf16[256,2048]{1,0:T(8,128)(2,1)} %refs_0_.3), channel_id=1, source_target_pairs={{0,4},{2,6},{4,0},{6,2},{8,12},{10,14},{12,8},{14,10},{16,20},{18,... | collective-permute-start | bytes 3145736 | tf_op jit(solution)/shard_map/ppermute | solution.py:426
  3.7 90.0 %collective-permute-start.6 = (bf16[256,2048]{1,0:T(8,128)(2,1)}, bf16[256,2048]{1,0:T(8,128)(2,1)}, u32[]{:S(2)}, u32[]{:S(2)}) collective-permute-start(bf16[256,2048]{1,0:T(8,128)(2,1)} %refs_0_.3), channel_id=1, source_target_pairs={{0,2},{2,0},{4,6},{6,4},{8,10},{10,8},{12,14},{14,12},{16,18},{18,... | collective-permute-start | bytes 3145736 | tf_op jit(solution)/shard_map/ppermute | solution.py:426
  5.2 88.5 %collective-permute-start.8 = (bf16[256,2048]{1,0:T(8,128)(2,1)}, bf16[256,2048]{1,0:T(8,128)(2,1)}, u32[]{:S(2)}, u32[]{:S(2)}) collective-permute-start(bf16[256,2048]{1,0:T(8,128)(2,1)} %refs_0_.3), channel_id=1, source_target_pairs={{0,24},{2,26},{4,28},{6,30},{8,0},{10,2},{12,4},{14,6},{16,8},{18,... | collective-permute-start | bytes 3145736 | tf_op jit(solution)/shard_map/ppermute | solution.py:486
  8.8 84.9 %collective-permute-start.5 = (bf16[256,2048]{1,0:T(8,128)(2,1)}, bf16[256,2048]{1,0:T(8,128)(2,1)}, u32[]{:S(2)}, u32[]{:S(2)}) collective-permute-start(bf16[256,2048]{1,0:T(8,128)(2,1)} %refs_0_.3), channel_id=1, source_target_pairs={{0,8},{2,10},{4,12},{6,14},{8,16},{10,18},{12,20},{14,22},{16,24},... | collective-permute-start | bytes 3145736 | tf_op jit(solution)/shard_map/ppermute | solution.py:486
  21.8 1.3 copy-start.3
  23.1 71.6 %collective-permute-start.1 = (bf16[128,2048]{1,0:T(8,128)(2,1)}, bf16[128,2048]{1,0:T(8,128)(2,1)S(1)}, u32[]{:S(2)}, u32[]{:S(2)}) collective-permute-start(bf16[128,2048]{1,0:T(8,128)(2,1)} %shard_map.104), channel_id=1, source_target_pairs={{0,2},{2,0},{4,6},{6,4},{8,10},{10,8},{12,14},{14,12},{16,18},{18,... | collective-permute-start | bytes 1572872 | tf_op jit(solution)/shard_map/ppermute | solution.py:426
  93.7 1.0 copy-start
  94.8 13.6 %collective-permute-start.9 = (bf16[256,1024]{1,0:T(8,128)(2,1)}, bf16[256,1024]{1,0:T(8,128)(2,1)}, u32[]{:S(2)}, u32[]{:S(2)}) collective-permute-start(bf16[256,1024]{1,0:T(8,128)(2,1)} %get-tuple-element.93), channel_id=1, source_target_pairs={{0,16},{2,18},{4,20},{6,22},{8,24},{10,26},{12,28},{14,30},{16,0},... | collective-permute-start | bytes 1572872 | tf_op jit(solution)/shard_map/ppermute | solution.py:486
  95.6 19.7 %copy-start.11 = (bf16[256,1024]{1,0:T(8,128)(2,1)S(1)}, bf16[256,1024]{1,0:T(8,128)(2,1)}, u32[]{:S(2)}) copy-start(bf16[256,1024]{1,0:T(8,128)(2,1)} %get-tuple-element.95) | copy-start | bytes 1572868
  99.4 15.1 %collective-permute-start.2 = (bf16[128,2048]{1,0:T(8,128)(2,1)}, bf16[128,2048]{1,0:T(8,128)(2,1)S(1)}, u32[]{:S(2)}, u32[]{:S(2)}) collective-permute-start(bf16[128,2048]{1,0:T(8,128)(2,1)} %get-tuple-element.84.refs_1_), channel_id=1, source_target_pairs={{0,4},{2,6},{4,0},{6,2},{8,12},{10,14},{12,8},{14,10},{16,20},{18,... | collective-permute-start | bytes 1572872 | tf_op jit(solution)/shard_map/ppermute | solution.py:426
  99.4 46.3 %collective-permute-start.12 = (bf16[256,2048]{1,0:T(8,128)(2,1)}, bf16[256,2048]{1,0:T(8,128)(2,1)}, u32[]{:S(2)}, u32[]{:S(2)}) collective-permute-start(bf16[256,2048]{1,0:T(8,128)(2,1)} %get-tuple-element.94.refs_3_), channel_id=1, source_target_pairs={{0,4},{2,6},{4,0},{6,2},{8,12},{10,14},{12,8},{14,10},{16,20},{18,... | collective-permute-start | bytes 3145736 | tf_op jit(solution)/shard_map/ppermute | solution.py:426
  101.5 44.3 %collective-permute-start.10 = (bf16[256,2048]{1,0:T(8,128)(2,1)}, bf16[256,2048]{1,0:T(8,128)(2,1)S(1)}, u32[]{:S(2)}, u32[]{:S(2)}) collective-permute-start(bf16[256,2048]{1,0:T(8,128)(2,1)} %get-tuple-element.94.refs_3_), channel_id=1, source_target_pairs={{0,2},{2,0},{4,6},{6,4},{8,10},{10,8},{12,14},{14,12},{16,18},{18,... | collective-permute-start | bytes 3145736 | tf_op jit(solution)/shard_map/ppermute | solution.py:426
  101.5 31.7 %copy-start.39 = (f32[32]{0:T(128)S(1)}, f32[32]{0:T(128)}, u32[]{:S(2)}) copy-start(f32[32]{0:T(128)} %param.12) | copy-start | bytes 388
  101.5 44.3 %collective-permute-start.13 = (bf16[256,2048]{1,0:T(8,128)(2,1)}, bf16[256,2048]{1,0:T(8,128)(2,1)}, u32[]{:S(2)}, u32[]{:S(2)}) collective-permute-start(bf16[256,2048]{1,0:T(8,128)(2,1)} %shard_map.111.refs_6_), channel_id=1, source_target_pairs={{0,2},{2,0},{4,6},{6,4},{8,10},{10,8},{12,14},{14,12},{16,18},{18,... | collective-permute-start | bytes 3145736 | tf_op jit(solution)/shard_map/ppermute | solution.py:426
  108.4 42.7 %collective-permute-start.11 = (bf16[256,2048]{1,0:T(8,128)(2,1)}, bf16[256,2048]{1,0:T(8,128)(2,1)S(1)}, u32[]{:S(2)}, u32[]{:S(2)}) collective-permute-start(bf16[256,2048]{1,0:T(8,128)(2,1)} %shard_map.111.refs_6_), channel_id=1, source_target_pairs={{0,4},{2,6},{4,0},{6,2},{8,12},{10,14},{12,8},{14,10},{16,20},{18,... | collective-permute-start | bytes 3145736 | tf_op jit(solution)/shard_map/ppermute | solution.py:426
  115.3 17.8 %collective-permute-start.14 = (bf16[256,1024]{1,0:T(8,128)(2,1)S(1)}, bf16[256,1024]{1,0:T(8,128)(2,1)S(1)}, u32[]{:S(2)}, u32[]{:S(2)}) collective-permute-start(bf16[256,1024]{1,0:T(8,128)(2,1)S(1)} %copy-done.11), channel_id=1, source_target_pairs={{0,16},{2,18},{4,20},{6,22},{8,24},{10,26},{12,28},{14,30},{16,0},... | collective-permute-start | bytes 1572872 | tf_op jit(solution)/shard_map/ppermute | solution.py:486
  133.1 6.5 %copy-start.5 = (bf16[256,1024]{1,0:T(8,128)(2,1)}, bf16[256,1024]{1,0:T(8,128)(2,1)S(1)}, u32[]{:S(2)}) copy-start(bf16[256,1024]{1,0:T(8,128)(2,1)S(1)} %collective-permute-done.14.refs_6_.refs_2_) | copy-start | bytes 1572868
  133.2 19.2 %collective-permute-start.3 = (bf16[128,2048]{1,0:T(8,128)(2,1)}, bf16[128,2048]{1,0:T(8,128)(2,1)S(1)}, u32[]{:S(2)}, u32[]{:S(2)}) collective-permute-start(bf16[128,2048]{1,0:T(8,128)(2,1)} %get-tuple-element.87.refs_7_), channel_id=1, source_target_pairs={{0,8},{2,10},{4,12},{6,14},{8,0},{10,2},{12,4},{14,6},{16,24},{18,... | collective-permute-start | bytes 1572872 | tf_op jit(solution)/shard_map/ppermute | solution.py:426
  134.5 90.1 %copy-start.40 = (s32[16]{0:T(128)}, s32[16]{0:T(128)S(1)}, u32[]{:S(2)}) copy-start(s32[16]{0:T(128)S(1)} %get-tuple-element.169) | copy-start | bytes 196
  145.8 5.3 %copy-start.6 = (bf16[256,2048]{1,0:T(8,128)(2,1)}, bf16[256,2048]{1,0:T(8,128)(2,1)S(1)}, u32[]{:S(2)}) copy-start(bf16[256,2048]{1,0:T(8,128)(2,1)S(1)} %collective-permute-done.10.refs_1_) | copy-start | bytes 3145732
  151.1 1.0 copy-start.8
  152.1 8.7 %copy-start.9 = (bf16[256,2048]{1,0:T(8,128)(2,1)S(1)}, bf16[256,2048]{1,0:T(8,128)(2,1)}, u32[]{:S(2)}) copy-start(bf16[256,2048]{1,0:T(8,128)(2,1)} %get-tuple-element.98.refs_8_) | copy-start | bytes 3145732
  152.1 25.8 %collective-permute-start.16 = (bf16[256,1024]{1,0:T(8,128)(2,1)}, bf16[256,1024]{1,0:T(8,128)(2,1)S(1)}, u32[]{:S(2)}, u32[]{:S(2)}) collective-permute-start(bf16[256,1024]{1,0:T(8,128)(2,1)} %get-tuple-element.97.refs_3_.refs_6_), channel_id=1, source_target_pairs={{0,4},{2,6},{4,0},{6,2},{8,12},{10,14},{12,8},{14,10},{16,20},{18,... | collective-permute-start | bytes 1572872 | tf_op jit(solution)/shard_map/ppermute | solution.py:426
  152.4 25.6 %collective-permute-start.15 = (bf16[256,1024]{1,0:T(8,128)(2,1)}, bf16[256,1024]{1,0:T(8,128)(2,1)S(1)}, u32[]{:S(2)}, u32[]{:S(2)}) collective-permute-start(bf16[256,1024]{1,0:T(8,128)(2,1)} %get-tuple-element.97.refs_3_.refs_6_), channel_id=1, source_target_pairs={{0,2},{2,0},{4,6},{6,4},{8,10},{10,8},{12,14},{14,12},{16,18},{18,... | collective-permute-start | bytes 1572872 | tf_op jit(solution)/shard_map/ppermute | solution.py:426
  153.2 10.5 %copy-start.7 = (bf16[256,2048]{1,0:T(8,128)(2,1)S(1)}, bf16[256,2048]{1,0:T(8,128)(2,1)}, u32[]{:S(2)}) copy-start(bf16[256,2048]{1,0:T(8,128)(2,1)} %get-tuple-element.99.refs_4_) | copy-start | bytes 3145732
  157.4 24.1 %collective-permute-start.4 = (bf16[128,2048]{1,0:T(8,128)(2,1)}, bf16[128,2048]{1,0:T(8,128)(2,1)S(1)}, u32[]{:S(2)}, u32[]{:S(2)}) collective-permute-start(bf16[128,2048]{1,0:T(8,128)(2,1)} %get-tuple-element.90.refs_9_), channel_id=1, source_target_pairs={{0,16},{2,18},{4,20},{6,22},{8,24},{10,26},{12,28},{14,30},{16,0},... | collective-permute-start | bytes 1572872 | tf_op jit(solution)/shard_map/ppermute | solution.py:426
  160.7 5.9 %copy-start.1 = (bf16[256,2048]{1,0:T(8,128)(2,1)S(1)}, bf16[256,2048]{1,0:T(8,128)(2,1)}, u32[]{:S(2)}) copy-start(bf16[256,2048]{1,0:T(8,128)(2,1)} %get-tuple-element.96.refs_2_) | copy-start | bytes 3145732
  161.7 16.2 %collective-permute-start.17 = (bf16[256,1024]{1,0:T(8,128)(2,1)S(1)}, bf16[256,1024]{1,0:T(8,128)(2,1)S(1)}, u32[]{:S(2)}, u32[]{:S(2)}) collective-permute-start(bf16[256,1024]{1,0:T(8,128)(2,1)S(1)} %get-tuple-element.160), channel_id=1, source_target_pairs={{0,2},{2,0},{4,6},{6,4},{8,10},{10,8},{12,14},{14,12},{16,18},{18,... | collective-permute-start | bytes 1572872 | tf_op jit(solution)/shard_map/ppermute | solution.py:426
  164.6 13.4 %collective-permute-start.18 = (bf16[256,1024]{1,0:T(8,128)(2,1)S(1)}, bf16[256,1024]{1,0:T(8,128)(2,1)S(1)}, u32[]{:S(2)}, u32[]{:S(2)}) collective-permute-start(bf16[256,1024]{1,0:T(8,128)(2,1)S(1)} %get-tuple-element.158), channel_id=1, source_target_pairs={{0,4},{2,6},{4,0},{6,2},{8,12},{10,14},{12,8},{14,10},{16,20},{18,... | collective-permute-start | bytes 1572872 | tf_op jit(solution)/shard_map/ppermute | solution.py:426
  177.9 1.0 copy-start.19
  177.9 1.2 copy-start.13
  178.0 1.3 copy-start.14
  179.3 8.2 %copy-start.4 = (f32[2,128,2048]{2,1,0:T(8,128)S(1)}, f32[2,128,2048]{2,1,0:T(8,128)}, u32[]{:S(2)}) copy-start(f32[2,128,2048]{2,1,0:T(8,128)} %get-tuple-element.81) | copy-start | bytes 6291460
  179.3 42.5 %collective-permute-start.22 = (bf16[256,1024]{1,0:T(8,128)(2,1)}, bf16[256,1024]{1,0:T(8,128)(2,1)S(1)}, u32[]{:S(2)}, u32[]{:S(2)}) collective-permute-start(bf16[256,1024]{1,0:T(8,128)(2,1)} %get-tuple-element.101.refs_3_.refs_7_), channel_id=1, source_target_pairs={{0,4},{2,6},{4,0},{6,2},{8,12},{10,14},{12,8},{14,10},{16,20},{18,... | collective-permute-start | bytes 1572872 | tf_op jit(solution)/shard_map/ppermute | solution.py:426
  179.3 42.6 %collective-permute-start.20 = (bf16[256,1024]{1,0:T(8,128)(2,1)}, bf16[256,1024]{1,0:T(8,128)(2,1)S(1)}, u32[]{:S(2)}, u32[]{:S(2)}) collective-permute-start(bf16[256,1024]{1,0:T(8,128)(2,1)} %get-tuple-element.101.refs_3_.refs_7_), channel_id=1, source_target_pairs={{0,2},{2,0},{4,6},{6,4},{8,10},{10,8},{12,14},{14,12},{16,18},{18,... | collective-permute-start | bytes 1572872 | tf_op jit(solution)/shard_map/ppermute | solution.py:426
  179.3 24.0 %collective-permute-start.19 = (bf16[256,1024]{1,0:T(8,128)(2,1)}, bf16[256,1024]{1,0:T(8,128)(2,1)S(1)}, u32[]{:S(2)}, u32[]{:S(2)}) collective-permute-start(bf16[256,1024]{1,0:T(8,128)(2,1)} %get-tuple-element.100), channel_id=1, source_target_pairs={{0,2},{2,0},{4,6},{6,4},{8,10},{10,8},{12,14},{14,12},{16,18},{18,... | collective-permute-start | bytes 1572872 | tf_op jit(solution)/shard_map/ppermute | solution.py:426
  181.3 40.5 %collective-permute-start.23 = (bf16[256,1024]{1,0:T(8,128)(2,1)}, bf16[256,1024]{1,0:T(8,128)(2,1)S(1)}, u32[]{:S(2)}, u32[]{:S(2)}) collective-permute-start(bf16[256,1024]{1,0:T(8,128)(2,1)} %get-tuple-element.104), channel_id=1, source_target_pairs={{0,2},{2,0},{4,6},{6,4},{8,10},{10,8},{12,14},{14,12},{16,18},{18,... | collective-permute-start | bytes 1572872 | tf_op jit(solution)/shard_map/ppermute | solution.py:426
  181.4 2.0 copy-start.24
  181.4 33.8 %collective-permute-start.21 = (bf16[256,1024]{1,0:T(8,128)(2,1)}, bf16[256,1024]{1,0:T(8,128)(2,1)}, u32[]{:S(2)}, u32[]{:S(2)}) collective-permute-start(bf16[256,1024]{1,0:T(8,128)(2,1)} %get-tuple-element.102.refs_4_.refs_8_), channel_id=1, source_target_pairs={{0,4},{2,6},{4,0},{6,2},{8,12},{10,14},{12,8},{14,10},{16,20},{18,... | collective-permute-start | bytes 1572872 | tf_op jit(solution)/shard_map/ppermute | solution.py:426
  187.5 15.8 %copy-start.10 = (bf16[256,1024]{1,0:T(8,128)(2,1)S(1)}, bf16[256,1024]{1,0:T(8,128)(2,1)}, u32[]{:S(2)}) copy-start(bf16[256,1024]{1,0:T(8,128)(2,1)} %get-tuple-element.105) | copy-start | bytes 1572868
  203.3 11.9 %copy-start.27 = (bf16[256,1024]{1,0:T(8,128)(2,1)}, bf16[256,1024]{1,0:T(8,128)(2,1)S(1)}, u32[]{:S(2)}) copy-start(bf16[256,1024]{1,0:T(8,128)(2,1)S(1)} %collective-permute-done.19.refs_0_) | copy-start | bytes 1572868
  203.3 18.5 %collective-permute-start.24 = (bf16[256,1024]{1,0:T(8,128)(2,1)S(1)}, bf16[256,1024]{1,0:T(8,128)(2,1)S(1)}, u32[]{:S(2)}, u32[]{:S(2)}) collective-permute-start(bf16[256,1024]{1,0:T(8,128)(2,1)S(1)} %copy-done.10), channel_id=1, source_target_pairs={{0,4},{2,6},{4,0},{6,2},{8,12},{10,14},{12,8},{14,10},{16,20},{18,... | collective-permute-start | bytes 1572872 | tf_op jit(solution)/shard_map/ppermute | solution.py:426
  221.8 1.0 copy-start.17
  221.9 1.2 copy-start.15
  221.9 1.3 copy-start.18
  223.2 21.1 %collective-permute-start.25 = (bf16[256,1024]{1,0:T(8,128)(2,1)}, bf16[256,1024]{1,0:T(8,128)(2,1)S(1)}, u32[]{:S(2)}, u32[]{:S(2)}) collective-permute-start(bf16[256,1024]{1,0:T(8,128)(2,1)} %get-tuple-element.106), channel_id=1, source_target_pairs={{0,2},{2,0},{4,6},{6,4},{8,10},{10,8},{12,14},{14,12},{16,18},{18,... | collective-permute-start | bytes 1572872 | tf_op jit(solution)/shard_map/ppermute | solution.py:426
  223.5 20.8 %collective-permute-start.26 = (bf16[256,1024]{1,0:T(8,128)(2,1)}, bf16[256,1024]{1,0:T(8,128)(2,1)S(1)}, u32[]{:S(2)}, u32[]{:S(2)}) collective-permute-start(bf16[256,1024]{1,0:T(8,128)(2,1)} %get-tuple-element.107.refs_4_.refs_9_), channel_id=1, source_target_pairs={{0,4},{2,6},{4,0},{6,2},{8,12},{10,14},{12,8},{14,10},{16,20},{18,... | collective-permute-start | bytes 1572872 | tf_op jit(solution)/shard_map/ppermute | solution.py:426
  225.3 16.3 %collective-permute-start.27 = (bf16[128,1024]{1,0:T(8,128)(2,1)}, bf16[128,1024]{1,0:T(8,128)(2,1)S(1)}, u32[]{:S(2)}, u32[]{:S(2)}) collective-permute-start(bf16[128,1024]{1,0:T(8,128)(2,1)} %get-tuple-element.109), channel_id=1, source_target_pairs={{0,2},{2,0},{4,6},{6,4},{8,10},{10,8},{12,14},{14,12},{16,18},{18,... | collective-permute-start | bytes 786440 | tf_op jit(solution)/shard_map/ppermute | solution.py:426
  251.9 12.3 %copy-start.29 = (bf16[128,1024]{1,0:T(8,128)(2,1)S(1)}, bf16[128,1024]{1,0:T(8,128)(2,1)}, u32[]{:S(2)}) copy-start(bf16[128,1024]{1,0:T(8,128)(2,1)} %get-tuple-element.115.refs_2_) | copy-start | bytes 786436
  251.9 12.6 %copy-start.37 = (bf16[128,1024]{1,0:T(8,128)(2,1)S(1)}, bf16[128,1024]{1,0:T(8,128)(2,1)}, u32[]{:S(2)}) copy-start(bf16[128,1024]{1,0:T(8,128)(2,1)} %get-tuple-element.110.refs_2_) | copy-start | bytes 786436
  264.0 85.4 %collective-permute-start.28 = (bf16[512,2048]{1,0:T(8,128)(2,1)}, bf16[512,2048]{1,0:T(8,128)(2,1)S(1)}, u32[]{:S(2)}, u32[]{:S(2)}) collective-permute-start(bf16[512,2048]{1,0:T(8,128)(2,1)} %get-tuple-element.119), channel_id=1, source_target_pairs={{0,1},{1,0},{2,3},{3,2},{4,5},{5,4},{6,7},{7,6},{8,9},{9,8},{10,11... | collective-permute-start | bytes 6291464 | tf_op jit(solution)/shard_map/ppermute | solution.py:426
  264.1 8.7 %collective-permute-start.30 = (bf16[128,1024]{1,0:T(8,128)(2,1)S(1)}, bf16[128,1024]{1,0:T(8,128)(2,1)S(1)}, u32[]{:S(2)}, u32[]{:S(2)}) collective-permute-start(bf16[128,1024]{1,0:T(8,128)(2,1)S(1)} %copy-done.29), channel_id=1, source_target_pairs={{0,2},{2,0},{4,6},{6,4},{8,10},{10,8},{12,14},{14,12},{16,18},{18,... | collective-permute-start | bytes 786440 | tf_op jit(solution)/shard_map/ppermute | solution.py:426
  264.5 12.0 %collective-permute-start.34 = (bf16[128,1024]{1,0:T(8,128)(2,1)S(1)}, bf16[128,1024]{1,0:T(8,128)(2,1)S(1)}, u32[]{:S(2)}, u32[]{:S(2)}) collective-permute-start(bf16[128,1024]{1,0:T(8,128)(2,1)S(1)} %copy-done.37), channel_id=1, source_target_pairs={{0,4},{2,6},{4,0},{6,2},{8,12},{10,14},{12,8},{14,10},{16,20},{18,... | collective-permute-start | bytes 786440 | tf_op jit(solution)/shard_map/ppermute | solution.py:426
  275.6 8.1 %collective-permute-start.31 = (bf16[128,1024]{1,0:T(8,128)(2,1)}, bf16[128,1024]{1,0:T(8,128)(2,1)S(1)}, u32[]{:S(2)}, u32[]{:S(2)}) collective-permute-start(bf16[128,1024]{1,0:T(8,128)(2,1)} %get-tuple-element.127), channel_id=1, source_target_pairs={{0,4},{2,6},{4,0},{6,2},{8,12},{10,14},{12,8},{14,10},{16,20},{18,... | collective-permute-start | bytes 786440 | tf_op jit(solution)/shard_map/ppermute | solution.py:426
  279.5 7.8 %collective-permute-start.35 = (bf16[128,1024]{1,0:T(8,128)(2,1)}, bf16[128,1024]{1,0:T(8,128)(2,1)S(1)}, u32[]{:S(2)}, u32[]{:S(2)}) collective-permute-start(bf16[128,1024]{1,0:T(8,128)(2,1)} %get-tuple-element.141), channel_id=1, source_target_pairs={{0,8},{2,10},{4,12},{6,14},{8,0},{10,2},{12,4},{14,6},{16,24},{18,... | collective-permute-start | bytes 786440 | tf_op jit(solution)/shard_map/ppermute | solution.py:426
  286.6 9.3 %collective-permute-start.32 = (bf16[128,1024]{1,0:T(8,128)(2,1)}, bf16[128,1024]{1,0:T(8,128)(2,1)S(1)}, u32[]{:S(2)}, u32[]{:S(2)}) collective-permute-start(bf16[128,1024]{1,0:T(8,128)(2,1)} %get-tuple-element.130), channel_id=1, source_target_pairs={{0,8},{2,10},{4,12},{6,14},{8,0},{10,2},{12,4},{14,6},{16,24},{18,... | collective-permute-start | bytes 786440 | tf_op jit(solution)/shard_map/ppermute | solution.py:426
  290.2 36.9 %collective-permute-start.36 = (bf16[128,1024]{1,0:T(8,128)(2,1)}, bf16[128,1024]{1,0:T(8,128)(2,1)S(1)}, u32[]{:S(2)}, u32[]{:S(2)}) collective-permute-start(bf16[128,1024]{1,0:T(8,128)(2,1)} %get-tuple-element.144), channel_id=1, source_target_pairs={{0,16},{2,18},{4,20},{6,22},{8,24},{10,26},{12,28},{14,30},{16,0},... | collective-permute-start | bytes 786440 | tf_op jit(solution)/shard_map/ppermute | solution.py:426
  298.8 36.7 %collective-permute-start.33 = (bf16[128,1024]{1,0:T(8,128)(2,1)}, bf16[128,1024]{1,0:T(8,128)(2,1)S(1)}, u32[]{:S(2)}, u32[]{:S(2)}) collective-permute-start(bf16[128,1024]{1,0:T(8,128)(2,1)} %get-tuple-element.133), channel_id=1, source_target_pairs={{0,16},{2,18},{4,20},{6,22},{8,24},{10,26},{12,28},{14,30},{16,0},... | collective-permute-start | bytes 786440 | tf_op jit(solution)/shard_map/ppermute | solution.py:426
  327.0 18.6 %collective-permute-start.29 = (bf16[512,128]{1,0:T(8,128)(2,1)S(1)}, bf16[512,128]{1,0:T(8,128)(2,1)S(1)}, u32[]{:S(2)}, u32[]{:S(2)}) collective-permute-start(bf16[512,128]{1,0:T(8,128)(2,1)S(1)} %convert_element_type.42), channel_id=1, source_target_pairs={{0,1},{1,0},{2,3},{3,2},{4,5},{5,4},{6,7},{7,6},{8,9},{9,8},{10,11... | collective-permute-start | bytes 393224 | tf_op jit(solution)/shard_map/ppermute | solution.py:426
  338.4 7.2 %copy-start.22 = (f32[512,128]{1,0:T(8,128)S(1)}, f32[512,128]{1,0:T(8,128)}, u32[]{:S(2)}) copy-start(f32[512,128]{1,0:T(8,128)} %get-tuple-element.124) | copy-start | bytes 786436
  338.4 7.9 %copy-start.38 = (f32[16,512]{1,0:T(8,128)S(1)}, f32[16,512]{1,0:T(8,128)}, u32[]{:S(2)}) copy-start(f32[16,512]{1,0:T(8,128)} %get-tuple-element.152) | copy-start | bytes 98308
  338.4 11.0 %copy-start.2 = (bf16[512,2048]{1,0:T(8,128)(2,1)S(1)}, bf16[512,2048]{1,0:T(8,128)(2,1)}, u32[]{:S(2)}) copy-start(bf16[512,2048]{1,0:T(8,128)(2,1)} %get-tuple-element.118) | copy-start | bytes 6291460
  345.0 2.7 collective-permute-start.37
  (15 other events, 11.5 us)

commit v4 on v3

--- a/solution.py
+++ b/solution.py
@@ -14,7 +14,7 @@
 WIDE = GROUP * P_SIZE
 LOG2E = 1.4426950408889634
 NEVER = -1e30
-GRANT = 58 * 2**20
+GRANT = 62 * 2**20
 
 F32 = jnp.float32
 BF16 = jnp.bfloat16
@@ -89,7 +89,7 @@
     gt_ref[0] = dot(c_ref[...], scaled, ((0,), (0,)))
 
 
-def grad_x_kernel(r_ref, rt_ref, g_ref, b_ref, c_ref, q_ref, skip_ref, out_ref):
+def grad_x_kernel(transposed, r_ref, rt_ref, g_ref, b_ref, c_ref, q_ref, skip_ref, out_ref):
     b = b_ref[...]
     scores = dot(b, c_ref[...], ((1,), (1,)))
     running = r_ref[...]
@@ -111,7 +111,10 @@
             parts.append(jnp.concatenate([mm(top, g), mm(low, g[HALF:])], axis=0))
         inner = jnp.where(first_head(), parts[0], parts[1])
         total = inner + skip_ref[:, lanes] * g.astype(F32) + from_state[:, lanes]
-        out_ref[:, lanes] = total.astype(BF16)
+        if transposed:
+            out_ref[lanes, :] = total.T.astype(BF16)
+        else:
+            out_ref[:, lanes] = total.astype(BF16)
 
 
 def forward_kernel(half_ref, own_ref, other_ref, w_ref, rt_ref, b_ref, x_ref, e_ref, total_ref):
@@ -153,51 +156,75 @@
     refs[0][...] = total.astype(BF16)
 
 
-def arrange_kernel(order_ref, own_ref, other_ref, out_ref, both_ref):
+def arrange_kernel(order_ref, own_ref, other_ref, early_ref, late_ref, both_ref):
     half = own_ref.shape[1]
     both_ref[:, :half] = own_ref[...]
     both_ref[:, half:] = other_ref[...]
-    unit = out_ref.shape[1] // order_ref.shape[0]
+    unit = 2 * half // order_ref.shape[0]
+    cut = early_ref.shape[1]
     for index in range(order_ref.shape[0]):
         source = pl.ds(pl.multiple_of(order_ref[index] * unit, 128), unit)
-        out_ref[:, index * unit : (index + 1) * unit] = both_ref[:, source]
-
-
-def coefficients_kernel(place_ref, every_ref, out_ref):
-    place = place_ref[0]
-    count = every_ref.shape[0]
-    parts = jnp.concatenate(thirds(every_ref[...]), axis=0).astype(BF16)
-    row = iota((8, count), 0)
-    column = iota((8, count), 1)
-    line = iota((8, every_ref.shape[1]), 0)
-    half = out_ref.shape[0] // 2
-    for step in range(half):
-        bit = 2**step
-        start = place // bit * bit
-        upper = place // bit % 2
-        beside = start + bit - 2 * bit * upper
-        low = jnp.where(row == 1, beside, jnp.where(row == 3, place + 1, start))
-        high = jnp.where(row == 1, beside + bit, jnp.where(row == 2, place, start + bit))
-        mask = ((column >= low) & (column < high)).astype(F32)
-        mask = jnp.concatenate([mask, mask, mask], axis=1).astype(BF16)
-        factors = jnp.exp2(mm(mask, parts))
-        kept, other, before_me, after_me = [factors[k : k + 1] for k in range(4)]
-        up = (upper + 0 * line) == 1
-        for way in range(2):
-            later = up if way == 0 else jnp.logical_not(up)
-            passed = before_me if way == 0 else after_me
-            first = jnp.where(later, 1.0, other)
-            second = jnp.where(later, kept, 1.0)
-            third = jnp.where(later, passed, 0.0)
-            out_ref[way * half + step] = jnp.where(
-                line == 0, first, jnp.where(line == 1, second, third)
-            )
+        at = index * unit
+        if at < cut:
+            early_ref[:, at : at + unit] = both_ref[:, source]
+        else:
+            late_ref[:, at - cut : at - cut + unit] = both_ref[:, source]
+
+
+TAIL = 16
+
+
+def message(total, log):
+    high, middle, last = thirds(log)
+    line = iota((TAIL, total.shape[1]), 0)
+    tail = jnp.where(line == 0, high, jnp.where(line == 1, middle, jnp.where(line == 2, last, 0.0)))
+    return total.astype(BF16), tail.astype(BF16)
+
+
+def start_kernel(own_ref, kept_ref, total_ref, log_ref, sent_ref):
+    spans = own_ref.shape[0]
+    total = own_ref[spans - 1]
+    log = kept_ref[spans - 1, 4:5]
+    for k in range(spans - 2, -1, -1):
+        total = own_ref[k] + kept_ref[k, :1] * total
+        log = log + kept_ref[k, 4:5]
+    total_ref[...] = total
+    line = iota(log_ref.shape, 0)
+    log_ref[...] = jnp.where(line == 0, log, 0.0)
+    n = total.shape[0]
+    sent_ref[:n], sent_ref[n:] = message(total, log)
+
+
+def back_kernel(bit, place_ref, log_ref, total_ref, got_ref, *refs):
+    entering_ref = refs[0] if len(refs) == 6 else None
+    total_out, entering_out, sent_out, log_out, factor_out = refs[-5:]
+    n = total_ref.shape[0]
+    got = got_ref[:n].astype(F32)
+    tail = got_ref[n:].astype(F32)
+    other_log = tail[0:1] + tail[1:2] + tail[2:3]
+    log, before_me, after_me = log_ref[0:1], log_ref[1:2], log_ref[2:3]
+    line = iota(log_ref.shape, 0)
+    upper = (place_ref[0] // bit % 2 + 0 * line[0:1]) == 1
+    kept, other = jnp.exp2(log), jnp.exp2(other_log)
+    total = jnp.where(upper, other, 1.0) * total_ref[...] + jnp.where(upper, 1.0, kept) * got
+    passed = jnp.where(upper, 0.0, jnp.exp2(after_me)) * got
+    total_out[...] = total
+    entering_out[...] = passed if entering_ref is None else entering_ref[...] + passed
+    first = jnp.where(upper, 1.0, other)
+    second = jnp.where(upper, kept, 1.0)
+    third = jnp.where(upper, jnp.exp2(before_me), 0.0)
+    factor_out[...] = jnp.where(line == 0, first, jnp.where(line == 1, second, third))
+    log = log + other_log
+    before_me = jnp.where(upper, before_me + other_log, before_me)
+    after_me = jnp.where(upper, after_me, after_me + other_log)
+    log_out[...] = jnp.where(line == 0, log, jnp.where(line == 1, before_me, after_me))
+    sent_out[:n], sent_out[n:] = message(total, log)
 
 
 def scan_kernel(factor_ref, total_ref, got_ref, *refs):
     entering_ref = refs[0] if len(refs) == 4 else None
     total_out, entering_out, sent_out = refs[-3:]
-    factors = factor_ref[0]
+    factors = factor_ref[...]
     got = got_ref[...].astype(F32)
     total = factors[0:1] * total_ref[...] + factors[1:2] * got
     total_out[...] = total
@@ -242,7 +269,7 @@
         refs = refs[2:]
     away_ref, own_ref, buffer, slots, sems, out_sems = refs
     rows = arrays[0].shape[0]
-    wide = g_ref.shape[1]
+    wide = g_ref.shape[0]
     copies = []
     at = 0
     for index, parts in enumerate(halves):
@@ -257,23 +284,29 @@
         copies.append(mine)
     g = g_ref[...]
     half = away_ref.shape[1] // rows
+    bundle = 3 if count % 3 == 0 else count
     for index in range(count):
         for copy in copies[index]:
             copy.wait()
-        product = dot(g, buffer[index * rows : (index + 1) * rows], ((1,), (1,)))
-        slots[index] = product.astype(BF16)
-        place = order_ref[index]
-        lanes = pl.ds(pl.multiple_of(place % half * rows, 128), rows)
-
-        @pl.when(place < half)
-        def _():
-            target = away_ref.at[:, lanes]
-            pltpu.make_async_copy(slots.at[index], target, out_sems.at[index]).start()
-
-        @pl.when(place >= half)
-        def _():
-            target = own_ref.at[:, lanes]
-            pltpu.make_async_copy(slots.at[index], target, out_sems.at[index]).start()
+        if (index + 1) % bundle:
+            continue
+        start = index + 1 - bundle
+        product = mm(buffer[start * rows : (index + 1) * rows], g)
+        for done in range(start, index + 1):
+            part = product[(done - start) * rows : (done - start + 1) * rows]
+            slots[done] = part.T.astype(BF16)
+            place = order_ref[done]
+            lanes = pl.ds(pl.multiple_of(place % half * rows, 128), rows)
+
+            @pl.when(place < half)
+            def _():
+                target = away_ref.at[:, lanes]
+                pltpu.make_async_copy(slots.at[done], target, out_sems.at[done]).start()
+
+            @pl.when(place >= half)
+            def _():
+                target = own_ref.at[:, lanes]
+                pltpu.make_async_copy(slots.at[done], target, out_sems.at[done]).start()
 
     for index in range(count):
         target = away_ref.at[:, pl.ds(0, rows)]
@@ -304,13 +337,15 @@
         grad_b_ref[...] = so_far[0][...] if so_far else jnp.zeros_like(grad_b_ref)
 
     rows = []
-    across = jnp.zeros((SPAN, 2 * P_SIZE), F32)
     lane = iota((SPAN, 2 * P_SIZE), 1)
+    later = not_before().astype(BF16)
+    top_less = iota((HALF, SPAN), 1) > iota((HALF, SPAN), 0)
+    low_less = iota((HALF, HALF), 1) > iota((HALF, HALF), 0)
     top_sum = sum_ref[:HALF]
     low_sum = sum_ref[HALF:, HALF:]
     for pair in range(GROUP // 2):
         lanes = slice(pair * 2 * P_SIZE, (pair + 1) * 2 * P_SIZE)
-        g = g_ref[:, lanes]
+        g = g_ref[:, lanes].T
         x = x_ref[:, lanes]
         for head in (2 * pair, 2 * pair + 1):
             mine = (lane < P_SIZE) if head == 2 * pair else (lane >= P_SIZE)
@@ -318,26 +353,21 @@
             row = running[head : head + 1]
             top = jnp.where(top_keep, row - columns[:HALF, head : head + 1], NEVER)
             low = jnp.where(low_keep, row[:, HALF:] - columns[HALF:, head : head + 1], NEVER)
-            top = jnp.exp2(top) * dot(x_head[:HALF], g, ((1,), (1,)))
-            low = jnp.exp2(low) * dot(x_head[HALF:], g[HALF:], ((1,), (1,)))
+            top = jnp.exp2(top) * mm(x_head[:HALF], g)
+            low = jnp.exp2(low) * mm(x_head[HALF:], g[:, HALF:])
             top_sum = top_sum + top
             low_sum = low_sum + low
-            top = top * scores[:HALF]
-            low = low * scores[HALF:, HALF:]
-            top_row = jnp.sum(top, axis=0, keepdims=True)
-            low_row = jnp.sum(low, axis=0, keepdims=True)
+            top = mm((top * scores[:HALF]).astype(BF16), later)
+            low = mm((low * scores[HALF:, HALF:]).astype(BF16), later[HALF:, HALF:])
+            top_row = jnp.sum(jnp.where(top_less, top, 0.0), axis=0, keepdims=True)
+            low_row = jnp.sum(jnp.where(low_less, low, 0.0), axis=0, keepdims=True)
             rows.append(jnp.concatenate([top_row[:, :HALF], top_row[:, HALF:] + low_row], axis=1))
-            column = jnp.concatenate(
-                [jnp.sum(top, axis=1, keepdims=True), jnp.sum(low, axis=1, keepdims=True)], axis=0
-            )
-            across = jnp.where(lane == head, column, across)
     sum_ref[:HALF] = top_sum
     sum_ref[HALF:, HALF:] = low_sum
-    difference = jnp.concatenate(rows, axis=0) - across.T[:GROUP]
     to_end = jnp.exp2(spread_columns(columns[SPAN - 1 : SPAN] - columns))
     scaled = x_ref[...].astype(F32) * to_end
     ends = dot(one_hot(BF16), (scaled * mm(b, q_ref[0])).astype(BF16), ((1,), (1,)))
-    d_ref[...] = sum_over(difference, not_before()) + sum_over(ends, before())
+    d_ref[...] = jnp.concatenate(rows, axis=0) + sum_over(ends, before())
     grad_b_ref[...] += dot(scaled.astype(BF16), q_ref[0], ((1,), (1,)))
 
     @pl.when(step == pl.num_programs(1) - 1)
@@ -642,7 +672,7 @@
 
 
 def multiply_blocks(order, grad_x, pieces, so_far):
-    length, columns = grad_x.shape
+    columns, length = grad_x.shape
     arrays = [array for piece in pieces for array in piece]
     rows = arrays[0].shape[0]
     count = len(pieces)
@@ -651,7 +681,7 @@
     return pl.pallas_call(
         functools.partial(blocks_kernel, [len(piece) for piece in pieces], bool(so_far)),
         grid=(1,),
-        in_specs=[SCALARS, pl.BlockSpec((length, columns), lambda h: (0, 0))]
+        in_specs=[SCALARS, pl.BlockSpec((columns, length), lambda h: (0, 0))]
         + [ANYWHERE] * (len(arrays) + len(so_far)),
         out_specs=[ANYWHERE, ANYWHERE],
         out_shape=[half, half],
@@ -673,31 +703,51 @@
     )(order, grad_x, *arrays, *so_far)
 
 
-def coefficients(logs):
-    count = lax.axis_size("ctx")
-    place = lax.axis_index("ctx").astype(jnp.int32)[None]
-    columns = logs.shape[1]
-    every = lax.all_gather(logs, "ctx").reshape(count, columns)
-    steps = count.bit_length() - 1
+def back_start(own_grads, kept):
+    spans, n, columns = own_grads.shape
     return call(
-        coefficients_kernel,
-        (1,),
-        [SCALARS, pl.BlockSpec((count, columns), lambda h: (0, 0))],
-        pl.BlockSpec((2 * steps, 8, columns), lambda h: (0, 0, 0)),
-        shape(2 * steps, 8, columns),
+        start_kernel,
+        (columns // WIDE,),
+        [
+            pl.BlockSpec((spans, n, WIDE), lambda h: (0, 0, h)),
+            pl.BlockSpec((spans, 8, WIDE), lambda h: (0, 0, h)),
+        ],
+        [pl.BlockSpec((rows, WIDE), lambda h: (0, h)) for rows in (n, 8, n + TAIL)],
+        [shape(n, columns), shape(8, columns), shape(n + TAIL, columns, dtype=BF16)],
         0,
-        256 * columns,
-    )(place, every)
-
-
-def scan_step(factors, number, here, total, sent, entering, bit):
+        14 * n * columns,
+    )(own_grads, kept)
+
+
+def back_step(place, log, total, sent, entering, bit):
+    got = swap(sent, "ctx", bit)
+    n, columns = total.shape
+    tall = [pl.BlockSpec((rows, WIDE), lambda h: (0, h)) for rows in (8, n, n + TAIL)]
+    return call(
+        functools.partial(back_kernel, bit),
+        (columns // WIDE,),
+        [SCALARS] + tall + [tall[1]] * len(entering),
+        [tall[1], tall[1], tall[2], tall[0], tall[0]],
+        [
+            shape(n, columns),
+            shape(n, columns),
+            shape(n + TAIL, columns, dtype=BF16),
+            shape(8, columns),
+            shape(8, columns),
+        ],
+        0,
+        18 * n * columns,
+    )(place, log, total, got, *entering)
+
+
+def scan_step(factors, here, total, sent, entering, bit):
     got = swap(sent, "ctx", bit)
     n, columns = total.shape
     block = pl.BlockSpec((n, WIDE), lambda h: (0, h))
     return call(
         scan_kernel,
         (columns // WIDE,),
-        [pl.BlockSpec((1, 8, WIDE), lambda h: (number, 0, h + here)), block, block]
+        [pl.BlockSpec((8, WIDE), lambda h: (0, h + here)), block, block]
         + [block] * len(entering),
         [block, block, block],
         [shape(n, columns), shape(n, columns), shape(n, columns, dtype=BF16)],
@@ -801,33 +851,29 @@
     own_x, own_y = swap_x(w_in), swap_y(w_in)
     other = swap(inputs, "head", 1)
     running, running_t, kept, own_grads = prepare(log_decay, grad_out, c_rows)
-    factors = coefficients(jnp.sum(kept[:, 4:5], axis=0))
-    back = own_grads[spans - 1]
-    for k in range(spans - 2, -1, -1):
-        back = own_grads[k] + kept[k, :1] * back
-    sent = back.astype(BF16)
+    spot = lax.axis_index("ctx").astype(jnp.int32)[None]
+    back, log, sent = back_start(own_grads, kept)
     sent = after([sent], other)[0]
-    back, leaving, sent = scan_step(factors, 4, 0, back, sent, (), 1)
+    back, leaving, sent, log, factors_1 = back_step(spot, log, back, sent, (), 1)
 
     z1, w_a, w_b = after([z1, w_a, w_b], own_x, own_y, z3)
     z2a, z2b = shift(w_a, 2), shift(w_b, 2)
     x1, y1 = swap_x(z1), swap_y(z1)
     z3 = after([z3], sent)[0]
     x3, y3 = swap_x(z3), swap_y(z3)
-    back, leaving, sent = scan_step(factors, 5, 0, back, sent, (leaving,), 2)
+    back, leaving, sent, log, factors_2 = back_step(spot, log, back, sent, (leaving,), 2)
     order_own = (order + place * (blocks // 2)) % blocks
-    features = call(
+    cut = len(EARLY) * w_in.shape[0]
+    early_features, late_features = call(
         arrange_kernel,
         (1,),
         [SCALARS] + [pl.BlockSpec((length, width // 2), lambda h: (0, 0))] * 2,
-        pl.BlockSpec((length, width), lambda h: (0, 0)),
-        shape(length, width, dtype=BF16),
+        [pl.BlockSpec((length, wide), lambda h: (0, 0)) for wide in (cut, width - cut)],
+        [shape(length, wide, dtype=BF16) for wide in (cut, width - cut)],
         0,
         4 * length * width,
         [pltpu.VMEM((length, width), BF16)],
     )(order_own, inputs, other)
-    cut = len(EARLY) * w_in.shape[0]
-    early_features, late_features = features[:, :cut], features[:, cut:]
 
     z2a, x1, y3, own_y = after(
         [z2a, x1, y3, own_y], y1, x3, z2b, sent, early_features, late_features
@@ -837,7 +883,7 @@
     own_y_a, own_y_b = own_y[:, :half], own_y[:, half:]
     x2a, y2a = swap_x(z2a), swap_y(z2a)
     d3a, d1a = swap_x(y3_a), swap_y(x1_a)
-    back, leaving, sent = scan_step(factors, 6, 0, back, sent, (leaving,), 4)
+    back, leaving, sent, log, factors_4 = back_step(spot, log, back, sent, (leaving,), 4)
     early = [w_in, own_x, own_y, z1, x1, y1, z3, x3, y3]
     part = early_forward(early_features, early)
 
@@ -847,13 +893,13 @@
     d0a, d2a = swap_x(own_y_a), swap_y(x2a)
     x2b, y2b = swap_x(z2b), swap_y(z2b)
     d3b, d1b = swap_x(y3_b), swap_y(x1_b)
-    back, leaving, sent = scan_step(factors, 7, 0, back, sent, (leaving,), 8)
+    back, leaving, sent, log, factors_8 = back_step(spot, log, back, sent, (leaving,), 8)
     leaving_all = [leaving]
     for k in range(spans - 1, 0, -1):
         leaving_all.insert(0, own_grads[k] + kept[k, :1] * leaving_all[0])
     leaving_all = jnp.stack([value.astype(BF16) for value in leaving_all])
     skip = jnp.repeat(skip_gain, P_SIZE)[None]
-    grad_x = grad_rows(running, running_t, grad_out, b_rows, c_rows, leaving_all, skip)
+    grad_x = grad_rows(running, running_t, grad_out, b_rows, c_rows, leaving_all, skip, True)
     late_a = [d0a, d1a, d3a, z2a, x2a, y2a, d2a]
     x_a, states_a, total_a, sent_a = late_forward(
         late_features, part, late_a, running_t, b_rows, kept, 0
@@ -861,7 +907,7 @@
 
     own_y_b, x2b, sent_a = after([own_y_b, x2b, sent_a], y2b, d3b, d1b, grad_x)
     d0b, d2b = swap_x(own_y_b), swap_y(x2b)
-    total_a, entering_a, sent_a = scan_step(factors, 0, 0, total_a, sent_a, (), 1)
+    total_a, entering_a, sent_a = scan_step(factors_1, 0, total_a, sent_a, (), 1)
     order_away = (order + (1 - place) * (blocks // 2)) % blocks
     early_order, late_order = order_away[: len(EARLY)], order_away[len(EARLY) :]
     product = multiply_blocks(early_order, grad_x, [[piece] for piece in early], ())
@@ -873,26 +919,33 @@
         late_features, part, late_b, running_t, b_rows, kept, here
     )
     pairs = list(zip(late_a, late_b))
-    product = after(list(product), sent_b)
-    away, own = multiply_blocks(late_order, grad_x, pairs, product)
-    got = swap(away, "head", 1)
-    entering_b = ()
-    for number, bit in enumerate((1, 2, 4, 8)):
-        if number > 0:
-            total_a, entering_a, sent_a = scan_step(
-                factors, number, 0, total_a, sent_a, (entering_a,), bit
-            )
-        total_b, entering_b, sent_b = scan_step(
-            factors, number, here, total_b, sent_b, entering_b, bit
-        )
-        entering_b = (entering_b,)
-    entering_b = entering_b[0]
     shared = (running, running_t, grad_out)
     grid = (spans, here)
-    inner_a = shared + (x_a, b_rows, c_rows, leaving_all)
-    decay_a, grad_b, grad_c = inner(grid, 0, half, inner_a, ())
-    inner_b = shared + (x_b, b_rows, c_rows, leaving_all)
-    decay_b, grad_b, grad_c = inner(grid, here, half, inner_b, (grad_b, grad_c))
+    entering_b = ()
+    for factors, bit in ((factors_1, 1), (factors_2, 2), (factors_4, 4), (factors_8, 8)):
+        if bit > 1:
+            total_a, entering_a, sent_a = scan_step(
+                factors, 0, total_a, sent_a, (entering_a,), bit
+            )
+        if bit == 4:
+            sent_b = after([sent_b], away)[0]
+        if bit == 8:
+            sent_b = after([sent_b], grad_b)[0]
+        total_b, entering_b, sent_b = scan_step(factors, here, total_b, sent_b, entering_b, bit)
+        entering_b = (entering_b,)
+        if bit == 1:
+            product = after(list(product), sent_b)
+            away, own = multiply_blocks(late_order, grad_x, pairs, product)
+            got = swap(away, "head", 1)
+        if bit == 2:
+            x_a = after([x_a], sent_b)[0]
+            inner_a = shared + (x_a, b_rows, c_rows, leaving_all)
+            decay_a, grad_b, grad_c = inner(grid, 0, half, inner_a, ())
+        if bit == 4:
+            x_b = after([x_b], sent_b)[0]
+            inner_b = shared + (x_b, b_rows, c_rows, leaving_all)
+            decay_b, grad_b, grad_c = inner(grid, here, half, inner_b, (grad_b, grad_c))
+    entering_b = entering_b[0]
     grad_b = head_sum(grad_b)
 
     common = (running_t, grad_out, c_rows)
@@ -905,14 +958,17 @@
     return (grad_inputs, grad_b, head_sum(grad_c), grad_log_decay)
 
 
-def grad_rows(running, running_t, grad_out, b_rows, c_rows, leaving, skip):
+def grad_rows(running, running_t, grad_out, b_rows, c_rows, leaving, skip, transposed):
     length, columns = grad_out.shape
+    spec, dims = rows_spec(), (length, columns)
+    if transposed:
+        spec, dims = pl.BlockSpec((WIDE, SPAN), lambda k, h: (h, k)), (columns, length)
     return call(
-        grad_x_kernel,
+        functools.partial(grad_x_kernel, transposed),
         (length // SPAN, running_t.shape[0]),
         [run_spec(), run_t_spec(), rows_spec(), SHARED, SHARED, state_spec(), GAIN],
-        rows_spec(),
-        shape(length, columns, dtype=BF16),
+        spec,
+        shape(*dims, dtype=BF16),
         8 * length * columns * SPAN,
         6 * length * columns,
     )(running, running_t, grad_out, b_rows, c_rows, leaving, skip)
@@ -968,15 +1024,7 @@
     leaving = jnp.stack([value.astype(BF16) for value in leaving])
 
     skip = jnp.repeat(skip_gain, P_SIZE)[None]
-    grad_x = call(
-        grad_x_kernel,
-        grid,
-        [run_spec(), run_t_spec(), rows_spec(), SHARED, SHARED, state_spec(), GAIN],
-        rows_spec(),
-        shape(length, columns, dtype=BF16),
-        8 * length * columns * SPAN,
-        6 * length * columns,
-    )(running, running_t, grad_out, b_rows, c_rows, leaving, skip)
+    grad_x = grad_rows(running, running_t, grad_out, b_rows, c_rows, leaving, skip, False)
 
     grad_b = grad_c = product = None
     tokens = ()

time: 353 us -> 317 us (0.90)
  blocking collectives: 64.2 us -> 0 us
  waiting for transfers between devices: 55.5 us -> 106 us
  local copies, waits for them, and re-layouts: 29.3 us -> 17.8 us
  Pallas kernels: 148 us -> 140 us
    all_gather x1 -> x0, blocking collectives: 64.2 us -> none  [coefficients(): every = lax.all_gather(logs, 'ctx').reshape(count, columns)]
    ppermute x4, waiting for transfers between devices: 15.7 us -> 62.1 us  [shift(): lax.ppermute(value, 'ctx', [(i, (i + PLANE * by) % count) for i in range(...]
    pallas_call x2, Pallas kernels: 26.7 us -> 19.9 us  [multiply_blocks(): pl.pallas_call(functools.partial(blocks_kernel, [len(piece) for piece in...]
    slice x2 -> x0, local copies, waits for them, and re-layouts: 6.08 us -> none  [local_layered(): early_features, late_features = (features[:, :cut], features[:, cut:])]
    unnamed x82 -> x56, local copies, waits for them, and re-layouts: 15 us -> 10 us
    pallas_call x2, Pallas kernels: 27.1 us -> 23.3 us  [inner(): call(inner_kernel, grid, specs + [SHARED] * len(so_far), [run_spec(), SHA...]
    ppermute x34, waiting for transfers between devices: 39.7 us -> 43.4 us  [swap(): return lax.ppermute(value, axis, [(i, i ^ bit) for i in range(count)])]
  transfers between devices with their start and end apart: 38 -> 38, of which waited for: 8 -> 14; matrix products, arithmetic and copies ran while one was open for 8% -> 5% of each run, Pallas kernels for 37% -> 38%
where the time goes in v4:
time: 317 us; the launch traced here: 315 us
  Pallas kernels  140 us (44%)
  waiting for transfers between devices  106 us (33%)
  starting transfers between devices  37.6 us (12%)
  local copies, waits for them, and re-layouts  17.8 us (6%)
  other arithmetic  14 us (4%)
    ppermute x4, waiting for transfers between devices, shift(): lax.ppermute(value, 'ctx', [(i, (i + PLANE * by) % count) for i in range(...  62.1 us
    ppermute x34, waiting for transfers between devices, swap(): return lax.ppermute(value, axis, [(i, i ^ bit) for i in range(count)])  43.4 us
    ppermute x34, starting transfers between devices, swap(): return lax.ppermute(value, axis, [(i, i ^ bit) for i in range(count)])  33.3 us
    pallas_call x2, Pallas kernels, inner(): call(inner_kernel, grid, specs + [SHARED] * len(so_far), [run_spec(), SHA...  23.3 us
    pallas_call x2, Pallas kernels, multiply_blocks(): pl.pallas_call(functools.partial(blocks_kernel, [len(piece) for piece in...  19.9 us
    pallas_call x8, Pallas kernels, scan_step(): call(scan_kernel, (columns // WIDE,), [pl.BlockSpec((8, WIDE), lambda h:...  17.4 us
    pallas_call x4, Pallas kernels, back_step(): call(functools.partial(back_kernel, bit), (columns // WIDE,), [SCALARS] +...  16.1 us
    pallas_call x2, Pallas kernels, late_forward(): call(functools.partial(late_forward_kernel, len(pieces)), (columns // WID...  13.4 us
  transfers between devices with their start and end apart: 38, of which 14 were waited for; matrix products, arithmetic and copies ran while one was open for 5% of the time, Pallas kernels for 38%

profile of v4, /device:TPU:0, one launch (start us, length us, event | category | flops | bytes accessed | tf_op | source)
XLA Modules:
  0.0 315.5 jit_solution(15384378522770652006)
XLA Ops:
  1.1 2.6 collective-permute-start.7
  3.7 1.5 collective-permute-start.6
  5.2 3.6 %collective-permute-start.8 = (bf16[256,2048]{1,0:T(8,128)(2,1)}, bf16[256,2048]{1,0:T(8,128)(2,1)}, u32[]{:S(2)}, u32[]{:S(2)}) collective-permute-start(bf16[256,2048]{1,0:T(8,128)(2,1)} %refs_0_.3), channel_id=1, source_target_pairs={{0,24},{2,26},{4,28},{6,30},{8,0},{10,2},{12,4},{14,6},{16,8},{18,... | collective-permute-start | bytes 3145736 | tf_op jit(solution)/shard_map/ppermute | solution.py:516
  8.8 9.1 %shard_map.102 = (f32[32,512]{1,0:T(8,128)}, f32[4,512,8]{2,1,0:T(8,128)}, f32[2,8,2048]{2,1,0:T(8,128)}, f32[2,128,2048]{2,1,0:T(8,128)}) custom-call(f32[32,512]{1,0:T(8,128)} %d_ref.1, bf16[512,2048]{1,0:T(8,128)(2,1)} %g_ref.11, bf16[512,128]{1,0:T(8,128)(2,1)} %c_ref.11), custom_call_target="tpu_custom_call" | custom-call | flops 268435456 | bytes 6291456 | tf_op jit(solution)/shard_map/pallas_call | solution.py:773
  17.9 3.7 %shard_map.103 = (f32[128,2048]{1,0:T(8,128)}, f32[8,2048]{1,0:T(8,128)}, bf16[144,2048]{1,0:T(8,128)(2,1)}) custom-call(f32[2,128,2048]{2,1,0:T(8,128)} %get-tuple-element.93.own_ref, f32[2,8,2048]{2,1,0:T(8,128)} %get-tuple-element.94.kept_ref.a_ref), custom_call_target="tpu_custom_call" | custom-call | bytes 3670016 | tf_op jit(solution)/shard_map/pallas_call | solution.py:708
  22.9 1.1 fusion.7
  24.0 3.7 %collective-permute-done.7.refs_4_.refs_3_ = bf16[256,2048]{1,0:T(8,128)(2,1)S(1)} collective-permute-done((bf16[256,2048]{1,0:T(8,128)(2,1)}, bf16[256,2048]{1,0:T(8,128)(2,1)S(1)}, u32[]{:S(2)}, u32[]{:S(2)}) %collective-permute-start.7) | collective-permute-done | bytes 1048608 | tf_op jit(solution)/shard_map/ppermute | solution.py:456
  27.7 2.4 collective-permute-done.6.refs_3_.refs_1_
  30.1 2.6 collective-permute-done.8.refs_5_.refs_0_
  32.7 22.3 %collective-permute-done.5.refs_0_ = bf16[256,2048]{1,0:T(8,128)(2,1)} collective-permute-done((bf16[256,2048]{1,0:T(8,128)(2,1)}, bf16[256,2048]{1,0:T(8,128)(2,1)}, u32[]{:S(2)}, u32[]{:S(2)}) %collective-permute-start.5) | collective-permute-done | bytes 1048608 | tf_op jit(solution)/shard_map/ppermute | solution.py:516
  55.7 3.8 %shard_map.105 = (f32[128,2048]{1,0:T(8,128)}, f32[128,2048]{1,0:T(8,128)}, bf16[144,2048]{1,0:T(8,128)(2,1)}, f32[8,2048]{1,0:T(8,128)}, f32[8,2048]{1,0:T(8,128)}) custom-call(s32[1]{0:T(128)} %bitcast.18.place_ref, f32[8,2048]{1,0:T(8,128)} %get-tuple-element.95.log_ref, f32[128,2048]{1,0:T(8,128)} %get-tuple-element.96.total_ref, ...), custom_call_target="tpu_custom_call" | custom-call | bytes 4718592 | tf_op jit(solution)/shard_map/pallas_call | solution.py:726
  60.1 1.5 collective-permute-start.12
  62.2 1.5 collective-permute-start.13
  63.7 16.5 %collective-permute-done.9.refs_0_ = bf16[256,1024]{1,0:T(8,128)(2,1)S(1)} collective-permute-done((bf16[256,1024]{1,0:T(8,128)(2,1)}, bf16[256,1024]{1,0:T(8,128)(2,1)S(1)}, u32[]{:S(2)}, u32[]{:S(2)}) %collective-permute-start.9) | collective-permute-done | bytes 524320 | tf_op jit(solution)/shard_map/ppermute | solution.py:516
  81.9 4.1 %shard_map.106 = (f32[128,2048]{1,0:T(8,128)}, f32[128,2048]{1,0:T(8,128)}, bf16[144,2048]{1,0:T(8,128)(2,1)}, f32[8,2048]{1,0:T(8,128)}, f32[8,2048]{1,0:T(8,128)}) custom-call(s32[1]{0:T(128)} %bitcast.18.place_ref, f32[8,2048]{1,0:T(8,128)} %get-tuple-element.98.log_ref, f32[128,2048]{1,0:T(8,128)} %get-tuple-element.99.total_ref, ...), custom_call_target="tpu_custom_call" | custom-call | bytes 4718592 | tf_op jit(solution)/shard_map/pallas_call | solution.py:726
  86.0 20.7 %collective-permute-done.14.refs_6_.refs_2_ = bf16[256,1024]{1,0:T(8,128)(2,1)S(1)} collective-permute-done((bf16[256,1024]{1,0:T(8,128)(2,1)}, bf16[256,1024]{1,0:T(8,128)(2,1)S(1)}, u32[]{:S(2)}, u32[]{:S(2)}) %collective-permute-start.14) | collective-permute-done | bytes 524320 | tf_op jit(solution)/shard_map/ppermute | solution.py:516
  108.9 5.1 %shard_map.112 = (bf16[512,2304]{1,0:T(8,128)(2,1)}, bf16[512,1792]{1,0:T(8,128)(2,1)}) custom-call(s32[16]{0:T(128)} %get-tuple-element.188.order_ref, bf16[512,2048]{1,0:T(8,128)(2,1)} %own_ref.1, bf16[512,2048]{1,0:T(8,128)(2,1)} %collective-permute-done.refs_1_.other_ref), custom_call_target="tpu_custom_call" | custom-call | bytes 8388608 | tf_op jit(solution)/shard_map/pallas_call | solution.py:867
  114.0 4.5 %collective-permute-done.11.refs_2_ = bf16[256,2048]{1,0:T(8,128)(2,1)} collective-permute-done((bf16[256,2048]{1,0:T(8,128)(2,1)}, bf16[256,2048]{1,0:T(8,128)(2,1)}, u32[]{:S(2)}, u32[]{:S(2)}) %collective-permute-start.11) | collective-permute-done | bytes 1048608 | tf_op jit(solution)/shard_map/ppermute | solution.py:456
  119.6 2.3 fusion.6
  121.9 1.5 collective-permute-start.17
  123.3 1.1 fusion.5
  124.4 1.5 collective-permute-start.18
  125.9 4.1 %shard_map.107 = (f32[128,2048]{1,0:T(8,128)}, f32[128,2048]{1,0:T(8,128)}, bf16[144,2048]{1,0:T(8,128)(2,1)}, f32[8,2048]{1,0:T(8,128)}, f32[8,2048]{1,0:T(8,128)}) custom-call(s32[1]{0:T(128)} %bitcast.18.place_ref, f32[8,2048]{1,0:T(8,128)} %get-tuple-element.102.log_ref, f32[128,2048]{1,0:T(8,128)} %get-tuple-element.103.total_ref, ...), custom_call_target="tpu_custom_call" | custom-call | bytes 4718592 | tf_op jit(solution)/shard_map/pallas_call | solution.py:726
  130.0 2.6 collective-permute-start.4
  132.6 1.1 fusion.4
  133.7 10.2 %shard_map.114.refs_8_.part_ref = f32[512,2048]{1,0:T(8,128)} custom-call(bf16[512,2304]{1,0:T(8,128)(2,1)} %get-tuple-element.114.refs_8_.f_ref, bf16[256,2048]{1,0:T(8,128)(2,1)} %refs_0_.3, bf16[256,2048]{1,0:T(8,128)(2,1)} %collective-permute-done.6.refs_3_.refs_1_, bf16[256,2048]{1,0:T(8,128)(2,1)} %get-tuple-element.116.refs_2_, ...), custom_call_target="tpu_custom_call" | custom-call | flops 4831838208 | bytes 9437184 | tf_op jit(solution)/shard_map/pallas_call | solution.py:625
  145.7 1.5 collective-permute-start.19
  147.7 8.0 %collective-permute-done.4.got_ref = bf16[144,2048]{1,0:T(8,128)(2,1)} collective-permute-done((bf16[144,2048]{1,0:T(8,128)(2,1)}, bf16[144,2048]{1,0:T(8,128)(2,1)}, u32[]{:S(2)}, u32[]{:S(2)}) %collective-permute-start.4) | collective-permute-done | bytes 589856 | tf_op jit(solution)/shard_map/ppermute | solution.py:456
  156.3 4.1 %shard_map.108 = (f32[128,2048]{1,0:T(8,128)}, f32[128,2048]{1,0:T(8,128)}, bf16[144,2048]{1,0:T(8,128)(2,1)}, f32[8,2048]{1,0:T(8,128)}, f32[8,2048]{1,0:T(8,128)}) custom-call(s32[1]{0:T(128)} %bitcast.18.place_ref, f32[8,2048]{1,0:T(8,128)} %get-tuple-element.106.log_ref, f32[128,2048]{1,0:T(8,128)} %get-tuple-element.107.total_ref, ...), custom_call_target="tpu_custom_call" | custom-call | bytes 4718592 | tf_op jit(solution)/shard_map/pallas_call | solution.py:726
  160.3 2.1 fusion.1
  162.5 9.1 %collective-permute-done.19.refs_0_ = bf16[256,1024]{1,0:T(8,128)(2,1)} collective-permute-done((bf16[256,1024]{1,0:T(8,128)(2,1)}, bf16[256,1024]{1,0:T(8,128)(2,1)}, u32[]{:S(2)}, u32[]{:S(2)}) %collective-permute-start.19) | collective-permute-done | bytes 524320 | tf_op jit(solution)/shard_map/ppermute | solution.py:456
  171.6 1.5 collective-permute-start.24
  173.1 1.1 pad_maximum_fusion.q_ref
  174.2 10.3 %shard_map.109.refs_6_.g_ref = bf16[2048,512]{1,0:T(8,128)(2,1)} custom-call(f32[32,512]{1,0:T(8,128)} %get-tuple-element.91.r_ref, f32[4,512,8]{2,1,0:T(8,128)} %get-tuple-element.92.rt_ref, bf16[512,2048]{1,0:T(8,128)(2,1)} %g_ref.11, bf16[512,128]{1,0:T(8,128)(2,1)} %b_ref.9, bf16[512,128]{1,0:T(8,128)(2,1)} %c_ref.11, ...), custom_call_target="tpu_custom_call" | custom-call | flops 2147483648 | bytes 6291456 | tf_op jit(solution)/shard_map/pallas_call | solution.py:966
  184.5 6.6 %shard_map.116 = (bf16[512,1024]{1,0:T(8,128)(2,1)}, f32[2,128,1024]{2,1,0:T(8,128)}, f32[128,1024]{1,0:T(8,128)}, bf16[128,1024]{1,0:T(8,128)(2,1)}) custom-call(bf16[512,1792]{1,0:T(8,128)(2,1)} %get-tuple-element.115.refs_9_.f_ref, f32[512,2048]{1,0:T(8,128)} %shard_map.114.refs_8_.part_ref, f32[4,512,8]{2,1,0:T(8,128)} %get-tuple-element.92.rt_ref, ...), custom_call_target="tpu_custom_call" | custom-call | flops 1879048192 | bytes 3670016 | tf_op jit(solution)/shard_map/pallas_call | solution.py:645
  193.1 1.5 collective-permute-start.27
  194.6 10.0 %shard_map.119 = (bf16[512,2048]{1,0:T(8,128)(2,1)}, bf16[512,2048]{1,0:T(8,128)(2,1)}) custom-call(s32[9]{0:T(128)} %bitcast.30, bf16[2048,512]{1,0:T(8,128)(2,1)} %shard_map.109.refs_6_.g_ref, bf16[256,2048]{1,0:T(8,128)(2,1)} %refs_0_.3, bf16[256,2048]{1,0:T(8,128)(2,1)} %collective-permute-done.6.refs_3_.refs_1_, ...), custom_call_target="tpu_custom_call" | custom-call | flops 4831838208 | bytes 9437184 | tf_op jit(solution)/shard_map/pallas_call | solution.py:681
  205.3 2.1 shard_map.118
  208.4 6.8 %shard_map.121 = (bf16[512,1024]{1,0:T(8,128)(2,1)}, f32[2,128,1024]{2,1,0:T(8,128)}, f32[128,1024]{1,0:T(8,128)}, bf16[128,1024]{1,0:T(8,128)(2,1)}) custom-call(bf16[512,1792]{1,0:T(8,128)(2,1)} %get-tuple-element.115.refs_9_.f_ref, f32[512,2048]{1,0:T(8,128)} %shard_map.114.refs_8_.part_ref, f32[4,512,8]{2,1,0:T(8,128)} %get-tuple-element.92.rt_ref, ...), custom_call_target="tpu_custom_call" | custom-call | flops 1879048192 | bytes 3670016 | tf_op jit(solution)/shard_map/pallas_call | solution.py:645
  216.5 5.4 %collective-permute-done.28.got_ref = bf16[128,1024]{1,0:T(8,128)(2,1)S(1)} collective-permute-done((bf16[128,1024]{1,0:T(8,128)(2,1)}, bf16[128,1024]{1,0:T(8,128)(2,1)S(1)}, u32[]{:S(2)}, u32[]{:S(2)}) %collective-permute-start.28) | collective-permute-done | bytes 262176 | tf_op jit(solution)/shard_map/ppermute | solution.py:456
  222.5 2.1 shard_map.122
  224.6 9.9 %shard_map.124 = (bf16[512,2048]{1,0:T(8,128)(2,1)}, bf16[512,2048]{1,0:T(8,128)(2,1)}) custom-call(s32[7]{0:T(128)} %slice.36.order_ref, bf16[2048,512]{1,0:T(8,128)(2,1)} %shard_map.109.refs_6_.g_ref, bf16[256,1024]{1,0:T(8,128)(2,1)} %collective-permute-done.19.refs_0_, ...), custom_call_target="tpu_custom_call", output_to_operand_aliasing={{0}: (16, {}), {1}: (17, {})} | custom-call | flops 3758096384 | bytes 7340032 | tf_op jit(solution)/shard_map/pallas_call | solution.py:681
  234.6 1.6 collective-permute-start.34
  236.7 7.1 %collective-permute-done.34.got_ref = bf16[128,1024]{1,0:T(8,128)(2,1)S(1)} collective-permute-done((bf16[128,1024]{1,0:T(8,128)(2,1)S(1)}, bf16[128,1024]{1,0:T(8,128)(2,1)S(1)}, u32[]{:S(2)}, u32[]{:S(2)}) %collective-permute-start.34) | collective-permute-done | bytes 262176 | tf_op jit(solution)/shard_map/ppermute | solution.py:456
  244.5 2.2 shard_map.134
  246.8 1.6 collective-permute-start.35
  249.7 2.2 shard_map.125
  251.9 1.7 collective-permute-start.31
  255.1 2.2 shard_map.135
  257.3 0.9 collective-permute-start.36
  258.2 11.6 %shard_map.130 = (f32[16,512]{1,0:T(8,128)}, f32[512,128]{1,0:T(8,128)}, f32[512,128]{1,0:T(8,128)}) custom-call(f32[32,512]{1,0:T(8,128)} %get-tuple-element.91.r_ref, f32[4,512,8]{2,1,0:T(8,128)} %get-tuple-element.92.rt_ref, bf16[512,2048]{1,0:T(8,128)(2,1)} %g_ref.11, bf16[512,1024]{1,0:T(8,128)(2,1)} %shard_map.129.x_ref, bf16[512,128]{1,0:T(8,128)(2,1)} %b_ref.9, ...), custom_call_target="tpu_custom_call" | custom-call | flops 1610612736 | bytes 3145728 | tf_op jit(solution)/shard_map/pallas_call | solution.py:801
  270.4 2.2 shard_map.127
  272.6 11.7 %shard_map.131 = (f32[16,512]{1,0:T(8,128)}, f32[512,128]{1,0:T(8,128)}, f32[512,128]{1,0:T(8,128)}) custom-call(f32[32,512]{1,0:T(8,128)} %get-tuple-element.91.r_ref, f32[4,512,8]{2,1,0:T(8,128)} %get-tuple-element.92.rt_ref, bf16[512,2048]{1,0:T(8,128)(2,1)} %g_ref.11, bf16[512,1024]{1,0:T(8,128)(2,1)} %shard_map.128.x_ref, bf16[512,128]{1,0:T(8,128)(2,1)} %b_ref.9, ...), custom_call_target="tpu_custom_call" | custom-call | flops 1610612736 | bytes 3145728 | tf_op jit(solution)/shard_map/pallas_call | solution.py:801
  284.4 2.1 collective-permute-start.33
  286.5 1.0 convert_element_type.38
  288.2 2.2 shard_map.136
  290.4 5.5 %shard_map.137 = (f32[16,512]{1,0:T(8,128)}, f32[512,128]{1,0:T(8,128)}) custom-call(f32[4,512,8]{2,1,0:T(8,128)} %get-tuple-element.92.rt_ref, bf16[512,2048]{1,0:T(8,128)(2,1)} %g_ref.11, bf16[512,128]{1,0:T(8,128)(2,1)} %c_ref.11, f32[128,1024]{1,0:T(8,128)} %get-tuple-element.170.s_ref, f32[2,128,1024]{2,1,0:T(8,128)} %get-tuple-element.171.e_ref, ...), custom_call_target="tpu_custom_call" | custom-call | flops 268435456 | bytes 3145728 | tf_op jit(solution)/shard_map/pallas_call | solution.py:816
  295.9 1.8 collective-permute-done.33.got_ref
  298.4 2.2 shard_map.133
  300.6 5.5 %shard_map.138 = (f32[16,512]{1,0:T(8,128)}, f32[512,128]{1,0:T(8,128)}) custom-call(f32[4,512,8]{2,1,0:T(8,128)} %get-tuple-element.92.rt_ref, bf16[512,2048]{1,0:T(8,128)(2,1)} %g_ref.11, bf16[512,128]{1,0:T(8,128)(2,1)} %c_ref.11, f32[128,1024]{1,0:T(8,128)} %get-tuple-element.159.s_ref, f32[2,128,1024]{2,1,0:T(8,128)} %get-tuple-element.160.e_ref, ...), custom_call_target="tpu_custom_call" | custom-call | flops 268435456 | bytes 3145728 | tf_op jit(solution)/shard_map/pallas_call | solution.py:816
  306.2 1.0 convert_element_type.41
  308.0 1.4 pad_maximum_fusion.1
  309.4 1.7 convert_add_fusion
  311.1 4.4 %add_convert_fusion = bf16[512,2048]{1,0:T(8,128)(2,1)} fusion(bf16[512,2048]{1,0:T(8,128)(2,1)} %collective-permute-done.29, bf16[512,2048]{1,0:T(8,128)(2,1)} %get-tuple-element.141), kind=kLoop, calls=%fused_computation | loop fusion | flops 4194304 | bytes 6291456 | tf_op jit(solution)/shard_map/convert_element_type | solution.py:956
  (123 shorter events, 24.1 us)
Async XLA Ops:
  0.6 21.1 %collective-permute-start = (bf16[512,2048]{1,0:T(8,128)(2,1)}, bf16[512,2048]{1,0:T(8,128)(2,1)}, u32[]{:S(2)}, u32[]{:S(2)}) collective-permute-start(bf16[512,2048]{1,0:T(8,128)(2,1)} %own_ref.1), channel_id=1, source_target_pairs={{0,1},{1,0},{2,3},{3,2},{4,5},{5,4},{6,7},{7,6},{8,9},{9,8},{10,11... | collective-permute-start | bytes 6291464 | tf_op jit(solution)/shard_map/ppermute | solution.py:456
  1.1 26.6 %collective-permute-start.7 = (bf16[256,2048]{1,0:T(8,128)(2,1)}, bf16[256,2048]{1,0:T(8,128)(2,1)S(1)}, u32[]{:S(2)}, u32[]{:S(2)}) collective-permute-start(bf16[256,2048]{1,0:T(8,128)(2,1)} %refs_0_.3), channel_id=1, source_target_pairs={{0,4},{2,6},{4,0},{6,2},{8,12},{10,14},{12,8},{14,10},{16,20},{18,... | collective-permute-start | bytes 3145736 | tf_op jit(solution)/shard_map/ppermute | solution.py:456
  3.7 26.3 %collective-permute-start.6 = (bf16[256,2048]{1,0:T(8,128)(2,1)}, bf16[256,2048]{1,0:T(8,128)(2,1)}, u32[]{:S(2)}, u32[]{:S(2)}) collective-permute-start(bf16[256,2048]{1,0:T(8,128)(2,1)} %refs_0_.3), channel_id=1, source_target_pairs={{0,2},{2,0},{4,6},{6,4},{8,10},{10,8},{12,14},{14,12},{16,18},{18,... | collective-permute-start | bytes 3145736 | tf_op jit(solution)/shard_map/ppermute | solution.py:456
  5.2 27.5 %collective-permute-start.8 = (bf16[256,2048]{1,0:T(8,128)(2,1)}, bf16[256,2048]{1,0:T(8,128)(2,1)}, u32[]{:S(2)}, u32[]{:S(2)}) collective-permute-start(bf16[256,2048]{1,0:T(8,128)(2,1)} %refs_0_.3), channel_id=1, source_target_pairs={{0,24},{2,26},{4,28},{6,30},{8,0},{10,2},{12,4},{14,6},{16,8},{18,... | collective-permute-start | bytes 3145736 | tf_op jit(solution)/shard_map/ppermute | solution.py:516
  8.8 46.2 %collective-permute-start.5 = (bf16[256,2048]{1,0:T(8,128)(2,1)}, bf16[256,2048]{1,0:T(8,128)(2,1)}, u32[]{:S(2)}, u32[]{:S(2)}) collective-permute-start(bf16[256,2048]{1,0:T(8,128)(2,1)} %refs_0_.3), channel_id=1, source_target_pairs={{0,8},{2,10},{4,12},{6,14},{8,16},{10,18},{12,20},{14,22},{16,24},... | collective-permute-start | bytes 3145736 | tf_op jit(solution)/shard_map/ppermute | solution.py:516
  21.7 1.2 copy-start.13
  21.7 34.0 %collective-permute-start.1 = (bf16[144,2048]{1,0:T(8,128)(2,1)}, bf16[144,2048]{1,0:T(8,128)(2,1)}, u32[]{:S(2)}, u32[]{:S(2)}) collective-permute-start(bf16[144,2048]{1,0:T(8,128)(2,1)} %shard_map.104), channel_id=1, source_target_pairs={{0,2},{2,0},{4,6},{6,4},{8,10},{10,8},{12,14},{14,12},{16,18},{18,... | collective-permute-start | bytes 1769480 | tf_op jit(solution)/shard_map/ppermute | solution.py:456
  27.7 27.3 %copy-start = (bf16[256,2048]{1,0:T(8,128)(2,1)}, bf16[256,2048]{1,0:T(8,128)(2,1)S(1)}, u32[]{:S(2)}) copy-start(bf16[256,2048]{1,0:T(8,128)(2,1)S(1)} %collective-permute-done.7.refs_4_.refs_3_) | copy-start | bytes 3145732
  55.0 25.2 %collective-permute-start.9 = (bf16[256,1024]{1,0:T(8,128)(2,1)}, bf16[256,1024]{1,0:T(8,128)(2,1)S(1)}, u32[]{:S(2)}, u32[]{:S(2)}) collective-permute-start(bf16[256,1024]{1,0:T(8,128)(2,1)} %get-tuple-element.111), channel_id=1, source_target_pairs={{0,16},{2,18},{4,20},{6,22},{8,24},{10,26},{12,28},{14,30},{16,0},... | collective-permute-start | bytes 1572872 | tf_op jit(solution)/shard_map/ppermute | solution.py:516
  59.6 21.1 %collective-permute-start.2 = (bf16[144,2048]{1,0:T(8,128)(2,1)}, bf16[144,2048]{1,0:T(8,128)(2,1)S(1)}, u32[]{:S(2)}, u32[]{:S(2)}) collective-permute-start(bf16[144,2048]{1,0:T(8,128)(2,1)} %get-tuple-element.100.refs_1_), channel_id=1, source_target_pairs={{0,4},{2,6},{4,0},{6,2},{8,12},{10,14},{12,8},{14,10},{16,20},{18,... | collective-permute-start | bytes 1769480 | tf_op jit(solution)/shard_map/ppermute | solution.py:456
  60.1 53.9 %collective-permute-start.12 = (bf16[256,2048]{1,0:T(8,128)(2,1)}, bf16[256,2048]{1,0:T(8,128)(2,1)}, u32[]{:S(2)}, u32[]{:S(2)}) collective-permute-start(bf16[256,2048]{1,0:T(8,128)(2,1)} %get-tuple-element.112.refs_3_), channel_id=1, source_target_pairs={{0,4},{2,6},{4,0},{6,2},{8,12},{10,14},{12,8},{14,10},{16,20},{18,... | collective-permute-start | bytes 3145736 | tf_op jit(solution)/shard_map/ppermute | solution.py:456
  61.7 52.4 %collective-permute-start.10 = (bf16[256,2048]{1,0:T(8,128)(2,1)}, bf16[256,2048]{1,0:T(8,128)(2,1)S(1)}, u32[]{:S(2)}, u32[]{:S(2)}) collective-permute-start(bf16[256,2048]{1,0:T(8,128)(2,1)} %get-tuple-element.112.refs_3_), channel_id=1, source_target_pairs={{0,2},{2,0},{4,6},{6,4},{8,10},{10,8},{12,14},{14,12},{16,18},{18,... | collective-permute-start | bytes 3145736 | tf_op jit(solution)/shard_map/ppermute | solution.py:456
  62.2 45.9 %copy-start.26 = (f32[32]{0:T(128)S(1)}, f32[32]{0:T(128)}, u32[]{:S(2)}) copy-start(f32[32]{0:T(128)} %param.12) | copy-start | bytes 388
  62.2 51.8 %collective-permute-start.13 = (bf16[256,2048]{1,0:T(8,128)(2,1)}, bf16[256,2048]{1,0:T(8,128)(2,1)}, u32[]{:S(2)}, u32[]{:S(2)}) collective-permute-start(bf16[256,2048]{1,0:T(8,128)(2,1)} %shard_map.111.refs_6_), channel_id=1, source_target_pairs={{0,2},{2,0},{4,6},{6,4},{8,10},{10,8},{12,14},{14,12},{16,18},{18,... | collective-permute-start | bytes 3145736 | tf_op jit(solution)/shard_map/ppermute | solution.py:456
  80.2 0.8 copy-start.12
  80.2 38.4 %collective-permute-start.11 = (bf16[256,2048]{1,0:T(8,128)(2,1)}, bf16[256,2048]{1,0:T(8,128)(2,1)}, u32[]{:S(2)}, u32[]{:S(2)}) collective-permute-start(bf16[256,2048]{1,0:T(8,128)(2,1)} %shard_map.111.refs_6_), channel_id=1, source_target_pairs={{0,4},{2,6},{4,0},{6,2},{8,12},{10,14},{12,8},{14,10},{16,20},{18,... | collective-permute-start | bytes 3145736 | tf_op jit(solution)/shard_map/ppermute | solution.py:456
  81.0 0.8 copy-start.14
  81.8 24.9 %collective-permute-start.14 = (bf16[256,1024]{1,0:T(8,128)(2,1)}, bf16[256,1024]{1,0:T(8,128)(2,1)S(1)}, u32[]{:S(2)}, u32[]{:S(2)}) collective-permute-start(bf16[256,1024]{1,0:T(8,128)(2,1)} %get-tuple-element.113), channel_id=1, source_target_pairs={{0,16},{2,18},{4,20},{6,22},{8,24},{10,26},{12,28},{14,30},{16,0},... | collective-permute-start | bytes 1572872 | tf_op jit(solution)/shard_map/ppermute | solution.py:516
  106.7 7.3 %copy-start.2 = (bf16[256,1024]{1,0:T(8,128)(2,1)}, bf16[256,1024]{1,0:T(8,128)(2,1)S(1)}, u32[]{:S(2)}) copy-start(bf16[256,1024]{1,0:T(8,128)(2,1)S(1)} %collective-permute-done.14.refs_6_.refs_2_) | copy-start | bytes 1572868
  106.7 19.3 %collective-permute-start.3 = (bf16[144,2048]{1,0:T(8,128)(2,1)}, bf16[144,2048]{1,0:T(8,128)(2,1)}, u32[]{:S(2)}, u32[]{:S(2)}) collective-permute-start(bf16[144,2048]{1,0:T(8,128)(2,1)} %get-tuple-element.104.refs_7_), channel_id=1, source_target_pairs={{0,8},{2,10},{4,12},{6,14},{8,0},{10,2},{12,4},{14,6},{16,24},{18,... | collective-permute-start | bytes 1769480 | tf_op jit(solution)/shard_map/ppermute | solution.py:456
  114.0 4.5 %copy-start.3 = (bf16[256,2048]{1,0:T(8,128)(2,1)}, bf16[256,2048]{1,0:T(8,128)(2,1)S(1)}, u32[]{:S(2)}) copy-start(bf16[256,2048]{1,0:T(8,128)(2,1)S(1)} %collective-permute-done.10.refs_1_) | copy-start | bytes 3145732
  118.5 4.8 %copy-start.4 = (bf16[256,2048]{1,0:T(8,128)(2,1)S(1)}, bf16[256,2048]{1,0:T(8,128)(2,1)}, u32[]{:S(2)}) copy-start(bf16[256,2048]{1,0:T(8,128)(2,1)} %get-tuple-element.119.refs_4_) | copy-start | bytes 3145732
  118.5 25.3 %collective-permute-start.16 = (bf16[256,1024]{1,0:T(8,128)(2,1)}, bf16[256,1024]{1,0:T(8,128)(2,1)S(1)}, u32[]{:S(2)}, u32[]{:S(2)}) collective-permute-start(bf16[256,1024]{1,0:T(8,128)(2,1)} %get-tuple-element.117.refs_3_.refs_6_), channel_id=1, source_target_pairs={{0,4},{2,6},{4,0},{6,2},{8,12},{10,14},{12,8},{14,10},{16,20},{18,... | collective-permute-start | bytes 1572872 | tf_op jit(solution)/shard_map/ppermute | solution.py:456
  119.1 24.8 %collective-permute-start.15 = (bf16[256,1024]{1,0:T(8,128)(2,1)}, bf16[256,1024]{1,0:T(8,128)(2,1)}, u32[]{:S(2)}, u32[]{:S(2)}) collective-permute-start(bf16[256,1024]{1,0:T(8,128)(2,1)} %get-tuple-element.117.refs_3_.refs_6_), channel_id=1, source_target_pairs={{0,2},{2,0},{4,6},{6,4},{8,10},{10,8},{12,14},{14,12},{16,18},{18,... | collective-permute-start | bytes 1572872 | tf_op jit(solution)/shard_map/ppermute | solution.py:456
  121.9 22.0 %collective-permute-start.17 = (bf16[256,1024]{1,0:T(8,128)(2,1)}, bf16[256,1024]{1,0:T(8,128)(2,1)}, u32[]{:S(2)}, u32[]{:S(2)}) collective-permute-start(bf16[256,1024]{1,0:T(8,128)(2,1)} %get-tuple-element.182), channel_id=1, source_target_pairs={{0,2},{2,0},{4,6},{6,4},{8,10},{10,8},{12,14},{14,12},{16,18},{18,... | collective-permute-start | bytes 1572872 | tf_op jit(solution)/shard_map/ppermute | solution.py:456
  123.3 9.3 %copy-start.1 = (bf16[256,2048]{1,0:T(8,128)(2,1)S(1)}, bf16[256,2048]{1,0:T(8,128)(2,1)}, u32[]{:S(2)}) copy-start(bf16[256,2048]{1,0:T(8,128)(2,1)} %get-tuple-element.116.refs_2_) | copy-start | bytes 3145732
  124.4 19.5 %collective-permute-start.18 = (bf16[256,1024]{1,0:T(8,128)(2,1)}, bf16[256,1024]{1,0:T(8,128)(2,1)}, u32[]{:S(2)}, u32[]{:S(2)}) collective-permute-start(bf16[256,1024]{1,0:T(8,128)(2,1)} %get-tuple-element.180), channel_id=1, source_target_pairs={{0,4},{2,6},{4,0},{6,2},{8,12},{10,14},{12,8},{14,10},{16,20},{18,... | collective-permute-start | bytes 1572872 | tf_op jit(solution)/shard_map/ppermute | solution.py:456
  130.0 25.7 %collective-permute-start.4 = (bf16[144,2048]{1,0:T(8,128)(2,1)}, bf16[144,2048]{1,0:T(8,128)(2,1)}, u32[]{:S(2)}, u32[]{:S(2)}) collective-permute-start(bf16[144,2048]{1,0:T(8,128)(2,1)} %get-tuple-element.108.refs_9_), channel_id=1, source_target_pairs={{0,16},{2,18},{4,20},{6,22},{8,24},{10,26},{12,28},{14,30},{16,0},... | collective-permute-start | bytes 1769480 | tf_op jit(solution)/shard_map/ppermute | solution.py:456
  143.9 0.8 copy-start.7
  144.7 46.5 %collective-permute-start.22 = (bf16[256,1024]{1,0:T(8,128)(2,1)}, bf16[256,1024]{1,0:T(8,128)(2,1)S(1)}, u32[]{:S(2)}, u32[]{:S(2)}) collective-permute-start(bf16[256,1024]{1,0:T(8,128)(2,1)} %get-tuple-element.121.refs_3_.refs_7_), channel_id=1, source_target_pairs={{0,4},{2,6},{4,0},{6,2},{8,12},{10,14},{12,8},{14,10},{16,20},{18,... | collective-permute-start | bytes 1572872 | tf_op jit(solution)/shard_map/ppermute | solution.py:456
  145.2 46.0 %collective-permute-start.20 = (bf16[256,1024]{1,0:T(8,128)(2,1)}, bf16[256,1024]{1,0:T(8,128)(2,1)}, u32[]{:S(2)}, u32[]{:S(2)}) collective-permute-start(bf16[256,1024]{1,0:T(8,128)(2,1)} %get-tuple-element.121.refs_3_.refs_7_), channel_id=1, source_target_pairs={{0,2},{2,0},{4,6},{6,4},{8,10},{10,8},{12,14},{14,12},{16,18},{18,... | collective-permute-start | bytes 1572872 | tf_op jit(solution)/shard_map/ppermute | solution.py:456
  145.7 25.9 %collective-permute-start.19 = (bf16[256,1024]{1,0:T(8,128)(2,1)}, bf16[256,1024]{1,0:T(8,128)(2,1)}, u32[]{:S(2)}, u32[]{:S(2)}) collective-permute-start(bf16[256,1024]{1,0:T(8,128)(2,1)} %get-tuple-element.120), channel_id=1, source_target_pairs={{0,2},{2,0},{4,6},{6,4},{8,10},{10,8},{12,14},{14,12},{16,18},{18,... | collective-permute-start | bytes 1572872 | tf_op jit(solution)/shard_map/ppermute | solution.py:456
  147.2 43.9 %collective-permute-start.23 = (bf16[256,1024]{1,0:T(8,128)(2,1)}, bf16[256,1024]{1,0:T(8,128)(2,1)S(1)}, u32[]{:S(2)}, u32[]{:S(2)}) collective-permute-start(bf16[256,1024]{1,0:T(8,128)(2,1)} %get-tuple-element.124), channel_id=1, source_target_pairs={{0,2},{2,0},{4,6},{6,4},{8,10},{10,8},{12,14},{14,12},{16,18},{18,... | collective-permute-start | bytes 1572872 | tf_op jit(solution)/shard_map/ppermute | solution.py:456
  155.8 28.8 %collective-permute-start.21 = (bf16[256,1024]{1,0:T(8,128)(2,1)}, bf16[256,1024]{1,0:T(8,128)(2,1)}, u32[]{:S(2)}, u32[]{:S(2)}) collective-permute-start(bf16[256,1024]{1,0:T(8,128)(2,1)} %get-tuple-element.122.refs_4_.refs_8_), channel_id=1, source_target_pairs={{0,4},{2,6},{4,0},{6,2},{8,12},{10,14},{12,8},{14,10},{16,20},{18,... | collective-permute-start | bytes 1572872 | tf_op jit(solution)/shard_map/ppermute | solution.py:456
  160.3 11.3 %copy-start.6 = (bf16[256,1024]{1,0:T(8,128)(2,1)S(1)}, bf16[256,1024]{1,0:T(8,128)(2,1)}, u32[]{:S(2)}) copy-start(bf16[256,1024]{1,0:T(8,128)(2,1)} %get-tuple-element.125) | copy-start | bytes 1572868
  171.6 19.5 %collective-permute-start.24 = (bf16[256,1024]{1,0:T(8,128)(2,1)S(1)}, bf16[256,1024]{1,0:T(8,128)(2,1)}, u32[]{:S(2)}, u32[]{:S(2)}) collective-permute-start(bf16[256,1024]{1,0:T(8,128)(2,1)S(1)} %copy-done.6), channel_id=1, source_target_pairs={{0,4},{2,6},{4,0},{6,2},{8,12},{10,14},{12,8},{14,10},{16,20},{18,... | collective-permute-start | bytes 1572872 | tf_op jit(solution)/shard_map/ppermute | solution.py:456
  191.1 0.8 copy-start.9
  191.1 0.9 copy-start.8
  192.1 15.3 %collective-permute-start.25 = (bf16[256,1024]{1,0:T(8,128)(2,1)}, bf16[256,1024]{1,0:T(8,128)(2,1)S(1)}, u32[]{:S(2)}, u32[]{:S(2)}) collective-permute-start(bf16[256,1024]{1,0:T(8,128)(2,1)} %get-tuple-element.126), channel_id=1, source_target_pairs={{0,2},{2,0},{4,6},{6,4},{8,10},{10,8},{12,14},{14,12},{16,18},{18,... | collective-permute-start | bytes 1572872 | tf_op jit(solution)/shard_map/ppermute | solution.py:456
  192.6 14.8 %collective-permute-start.26 = (bf16[256,1024]{1,0:T(8,128)(2,1)}, bf16[256,1024]{1,0:T(8,128)(2,1)S(1)}, u32[]{:S(2)}, u32[]{:S(2)}) collective-permute-start(bf16[256,1024]{1,0:T(8,128)(2,1)} %get-tuple-element.127.refs_4_.refs_9_), channel_id=1, source_target_pairs={{0,4},{2,6},{4,0},{6,2},{8,12},{10,14},{12,8},{14,10},{16,20},{18,... | collective-permute-start | bytes 1572872 | tf_op jit(solution)/shard_map/ppermute | solution.py:456
  193.1 11.5 %collective-permute-start.27 = (bf16[128,1024]{1,0:T(8,128)(2,1)}, bf16[128,1024]{1,0:T(8,128)(2,1)S(1)}, u32[]{:S(2)}, u32[]{:S(2)}) collective-permute-start(bf16[128,1024]{1,0:T(8,128)(2,1)} %get-tuple-element.130), channel_id=1, source_target_pairs={{0,2},{2,0},{4,6},{6,4},{8,10},{10,8},{12,14},{14,12},{16,18},{18,... | collective-permute-start | bytes 786440 | tf_op jit(solution)/shard_map/ppermute | solution.py:456
  204.6 0.7 copy-start.16
  207.4 0.8 copy-start.10
  207.4 1.0 copy-start.11
  208.4 7.4 %copy-start.27 = (s32[16]{0:T(128)S(1)}, s32[16]{0:T(128)}, u32[]{:S(2)}) copy-start(s32[16]{0:T(128)} %get-tuple-element.189) | copy-start | bytes 196
  215.2 6.6 %collective-permute-start.28 = (bf16[128,1024]{1,0:T(8,128)(2,1)}, bf16[128,1024]{1,0:T(8,128)(2,1)S(1)}, u32[]{:S(2)}, u32[]{:S(2)}) collective-permute-start(bf16[128,1024]{1,0:T(8,128)(2,1)} %get-tuple-element.137), channel_id=1, source_target_pairs={{0,2},{2,0},{4,6},{6,4},{8,10},{10,8},{12,14},{14,12},{16,18},{18,... | collective-permute-start | bytes 786440 | tf_op jit(solution)/shard_map/ppermute | solution.py:456
  221.8 0.7 copy-start.17
  224.6 10.0 %copy-start.24 = (bf16[128,1024]{1,0:T(8,128)(2,1)S(1)}, bf16[128,1024]{1,0:T(8,128)(2,1)}, u32[]{:S(2)}) copy-start(bf16[128,1024]{1,0:T(8,128)(2,1)} %get-tuple-element.131.refs_2_) | copy-start | bytes 786436
  224.6 11.6 %copy-start.15 = (bf16[128,1024]{1,0:T(8,128)(2,1)S(1)}, bf16[128,1024]{1,0:T(8,128)(2,1)}, u32[]{:S(2)}) copy-start(bf16[128,1024]{1,0:T(8,128)(2,1)} %get-tuple-element.138.refs_2_) | copy-start | bytes 786436
  234.6 76.5 %collective-permute-start.29 = (bf16[512,2048]{1,0:T(8,128)(2,1)}, bf16[512,2048]{1,0:T(8,128)(2,1)}, u32[]{:S(2)}, u32[]{:S(2)}) collective-permute-start(bf16[512,2048]{1,0:T(8,128)(2,1)} %get-tuple-element.142.refs_1_), channel_id=1, source_target_pairs={{0,1},{1,0},{2,3},{3,2},{4,5},{5,4},{6,7},{7,6},{8,9},{9,8},{10,11... | collective-permute-start | bytes 6291464 | tf_op jit(solution)/shard_map/ppermute | solution.py:456
  234.6 9.2 %collective-permute-start.34 = (bf16[128,1024]{1,0:T(8,128)(2,1)S(1)}, bf16[128,1024]{1,0:T(8,128)(2,1)S(1)}, u32[]{:S(2)}, u32[]{:S(2)}) collective-permute-start(bf16[128,1024]{1,0:T(8,128)(2,1)S(1)} %copy-done.24), channel_id=1, source_target_pairs={{0,4},{2,6},{4,0},{6,2},{8,12},{10,14},{12,8},{14,10},{16,20},{18,... | collective-permute-start | bytes 786440 | tf_op jit(solution)/shard_map/ppermute | solution.py:456
  236.2 12.8 %collective-permute-start.30 = (bf16[128,1024]{1,0:T(8,128)(2,1)S(1)}, bf16[128,1024]{1,0:T(8,128)(2,1)S(1)}, u32[]{:S(2)}, u32[]{:S(2)}) collective-permute-start(bf16[128,1024]{1,0:T(8,128)(2,1)S(1)} %copy-done.15), channel_id=1, source_target_pairs={{0,4},{2,6},{4,0},{6,2},{8,12},{10,14},{12,8},{14,10},{16,20},{18,... | collective-permute-start | bytes 786440 | tf_op jit(solution)/shard_map/ppermute | solution.py:456
  243.8 0.7 copy-start.23
  246.8 7.6 %collective-permute-start.35 = (bf16[128,1024]{1,0:T(8,128)(2,1)}, bf16[128,1024]{1,0:T(8,128)(2,1)S(1)}, u32[]{:S(2)}, u32[]{:S(2)}) collective-permute-start(bf16[128,1024]{1,0:T(8,128)(2,1)} %get-tuple-element.165), channel_id=1, source_target_pairs={{0,8},{2,10},{4,12},{6,14},{8,0},{10,2},{12,4},{14,6},{16,24},{18,... | collective-permute-start | bytes 786440 | tf_op jit(solution)/shard_map/ppermute | solution.py:456
  249.0 0.7 copy-start.22
  251.9 17.9 %collective-permute-start.31 = (bf16[128,1024]{1,0:T(8,128)(2,1)}, bf16[128,1024]{1,0:T(8,128)(2,1)S(1)}, u32[]{:S(2)}, u32[]{:S(2)}) collective-permute-start(bf16[128,1024]{1,0:T(8,128)(2,1)} %shard_map.126), channel_id=1, source_target_pairs={{0,8},{2,10},{4,12},{6,14},{8,0},{10,2},{12,4},{14,6},{16,24},{18,... | collective-permute-start | bytes 786440 | tf_op jit(solution)/shard_map/ppermute | solution.py:456
  257.3 30.2 %collective-permute-start.36 = (bf16[128,1024]{1,0:T(8,128)(2,1)}, bf16[128,1024]{1,0:T(8,128)(2,1)S(1)}, u32[]{:S(2)}, u32[]{:S(2)}) collective-permute-start(bf16[128,1024]{1,0:T(8,128)(2,1)} %get-tuple-element.168), channel_id=1, source_target_pairs={{0,16},{2,18},{4,20},{6,22},{8,24},{10,26},{12,28},{14,30},{16,0},... | collective-permute-start | bytes 786440 | tf_op jit(solution)/shard_map/ppermute | solution.py:456
  269.7 0.7 copy-start.20
  284.4 13.4 %collective-permute-start.33 = (bf16[128,1024]{1,0:T(8,128)(2,1)}, bf16[128,1024]{1,0:T(8,128)(2,1)S(1)}, u32[]{:S(2)}, u32[]{:S(2)}) collective-permute-start(bf16[128,1024]{1,0:T(8,128)(2,1)} %shard_map.132), channel_id=1, source_target_pairs={{0,16},{2,18},{4,20},{6,22},{8,24},{10,26},{12,28},{14,30},{16,0},... | collective-permute-start | bytes 786440 | tf_op jit(solution)/shard_map/ppermute | solution.py:456
  287.4 19.8 %collective-permute-start.32 = (bf16[512,128]{1,0:T(8,128)(2,1)S(1)}, bf16[512,128]{1,0:T(8,128)(2,1)S(1)}, u32[]{:S(2)}, u32[]{:S(2)}) collective-permute-start(bf16[512,128]{1,0:T(8,128)(2,1)S(1)} %convert_element_type.38), channel_id=1, source_target_pairs={{0,1},{1,0},{2,3},{3,2},{4,5},{5,4},{6,7},{7,6},{8,9},{9,8},{10,11... | collective-permute-start | bytes 393224 | tf_op jit(solution)/shard_map/ppermute | solution.py:456
  287.5 0.7 copy-start.18
  300.6 6.6 %copy-start.5 = (f32[512,128]{1,0:T(8,128)S(1)}, f32[512,128]{1,0:T(8,128)}, u32[]{:S(2)}) copy-start(f32[512,128]{1,0:T(8,128)} %get-tuple-element.155.refs_1_) | copy-start | bytes 786436
  300.6 7.4 %copy-start.25 = (f32[16,512]{1,0:T(8,128)S(1)}, f32[16,512]{1,0:T(8,128)}, u32[]{:S(2)}) copy-start(f32[16,512]{1,0:T(8,128)} %get-tuple-element.176) | copy-start | bytes 98308
  307.2 2.2 collective-permute-start.37
  (2 other events, 1.4 us)

commit v5 on v4

--- a/solution.py
+++ b/solution.py
@@ -106,9 +106,11 @@
             row = running[head : head + 1]
             top = jnp.where(top_keep, row - columns[:HALF, head : head + 1], NEVER)
             low = jnp.where(low_keep, row[:, HALF:] - columns[HALF:, head : head + 1], NEVER)
-            top = (jnp.exp2(top) * scores[:HALF]).astype(BF16)
+            parts.append((jnp.exp2(top) * scores[:HALF]).astype(BF16))
             low = (jnp.exp2(low) * scores[HALF:, HALF:]).astype(BF16)
-            parts.append(jnp.concatenate([mm(top, g), mm(low, g[HALF:])], axis=0))
+            parts.append(jnp.concatenate([jnp.zeros((HALF, HALF), BF16), low], axis=1))
+        product = mm(jnp.concatenate(parts, axis=0), g)
+        parts = [product[:SPAN], product[SPAN:]]
         inner = jnp.where(first_head(), parts[0], parts[1])
         total = inner + skip_ref[:, lanes] * g.astype(F32) + from_state[:, lanes]
         if transposed:
@@ -320,8 +322,8 @@
 def inner_kernel(
     r_ref, rt_ref, g_ref, x_ref, b_ref, c_ref, q_ref, *refs
 ):
-    d_ref, grad_b_ref, grad_c_ref, sum_ref = refs[-4:]
-    so_far = refs[:-4]
+    d_ref, grad_b_ref, grad_c_ref, sum_ref, top_ref, low_ref = refs[-6:]
+    so_far = refs[:-6]
     step = pl.program_id(1)
     b = b_ref[...]
     c = c_ref[...]
@@ -341,29 +343,35 @@
     later = not_before().astype(BF16)
     top_less = iota((HALF, SPAN), 1) > iota((HALF, SPAN), 0)
     low_less = iota((HALF, HALF), 1) > iota((HALF, HALF), 0)
-    top_sum = sum_ref[:HALF]
-    low_sum = sum_ref[HALF:, HALF:]
     for pair in range(GROUP // 2):
         lanes = slice(pair * 2 * P_SIZE, (pair + 1) * 2 * P_SIZE)
-        g = g_ref[:, lanes].T
         x = x_ref[:, lanes]
-        for head in (2 * pair, 2 * pair + 1):
-            mine = (lane < P_SIZE) if head == 2 * pair else (lane >= P_SIZE)
-            x_head = jnp.where(mine, x, jnp.zeros_like(x))
+        none = jnp.zeros_like(x)
+        x = [jnp.where(lane < P_SIZE, x, none), jnp.where(lane < P_SIZE, none, x)]
+        product = mm(jnp.concatenate(x, axis=0), g_ref[:, lanes].T)
+        top_sum = low_sum = None
+        for number in range(2):
+            head = 2 * pair + number
             row = running[head : head + 1]
+            at = number * SPAN
             top = jnp.where(top_keep, row - columns[:HALF, head : head + 1], NEVER)
             low = jnp.where(low_keep, row[:, HALF:] - columns[HALF:, head : head + 1], NEVER)
-            top = jnp.exp2(top) * mm(x_head[:HALF], g)
-            low = jnp.exp2(low) * mm(x_head[HALF:], g[:, HALF:])
-            top_sum = top_sum + top
-            low_sum = low_sum + low
-            top = mm((top * scores[:HALF]).astype(BF16), later)
-            low = mm((low * scores[HALF:, HALF:]).astype(BF16), later[HALF:, HALF:])
-            top_row = jnp.sum(jnp.where(top_less, top, 0.0), axis=0, keepdims=True)
-            low_row = jnp.sum(jnp.where(low_less, low, 0.0), axis=0, keepdims=True)
-            rows.append(jnp.concatenate([top_row[:, :HALF], top_row[:, HALF:] + low_row], axis=1))
-    sum_ref[:HALF] = top_sum
-    sum_ref[HALF:, HALF:] = low_sum
+            top = jnp.exp2(top) * product[at : at + HALF]
+            low = jnp.exp2(low) * product[at + HALF : at + SPAN, HALF:]
+            top_sum = top if number == 0 else top_sum + top
+            low_sum = low if number == 0 else low_sum + low
+            part = slice(head * HALF, (head + 1) * HALF)
+            top_ref[part] = (top * scores[:HALF]).astype(BF16)
+            low_ref[part] = (low * scores[HALF:, HALF:]).astype(BF16)
+        sum_ref[:HALF] += top_sum
+        sum_ref[HALF:, HALF:] += low_sum
+    top = mm(top_ref[...], later)
+    low = mm(low_ref[...], later[HALF:, HALF:])
+    for head in range(GROUP):
+        part = slice(head * HALF, (head + 1) * HALF)
+        top_row = jnp.sum(jnp.where(top_less, top[part], 0.0), axis=0, keepdims=True)
+        low_row = jnp.sum(jnp.where(low_less, low[part], 0.0), axis=0, keepdims=True)
+        rows.append(jnp.concatenate([top_row[:, :HALF], top_row[:, HALF:] + low_row], axis=1))
     to_end = jnp.exp2(spread_columns(columns[SPAN - 1 : SPAN] - columns))
     scaled = x_ref[...].astype(F32) * to_end
     ends = dot(one_hot(BF16), (scaled * mm(b, q_ref[0])).astype(BF16), ((1,), (1,)))
@@ -444,6 +452,11 @@
 SHARED = pl.BlockSpec((SPAN, 2 * P_SIZE), lambda k, h: (k, 0))
 GAIN = pl.BlockSpec((1, WIDE), lambda k, h: (0, h))
 ANYWHERE = pl.BlockSpec(memory_space=pl.ANY)
+INNER_SCRATCH = [
+    pltpu.VMEM((SPAN, SPAN), F32),
+    pltpu.VMEM((GROUP * HALF, SPAN), BF16),
+    pltpu.VMEM((GROUP * HALF, HALF), BF16),
+]
 SCALARS = pl.BlockSpec(memory_space=pltpu.SMEM)
 
 
@@ -511,9 +524,10 @@
     return list(out)
 
 
-def shift(value, by):
+def along_z(value, by):
     count = lax.axis_size("ctx")
-    return lax.ppermute(value, "ctx", [(i, (i + PLANE * by) % count) for i in range(count)])
+    pairs = [(i, i + PLANE * by) for i in range(count) if 0 <= i + PLANE * by < count]
+    return lax.ppermute(value, "ctx", pairs)
 
 
 def swap_x(value):
@@ -524,15 +538,16 @@
     return swap(value, "ctx", 2)
 
 
-EARLY = [(k, flip) for k in (0, 1, 3) for flip in range(3)]
-LATE = [(0, 3), (1, 3), (3, 3), (2, 0), (2, 1), (2, 2), (2, 3)]
+LAYERS = ((0, 1, 2, 3), (1, 0, 1, 2), (2, 2, 3, 1), (3, 3, 0, 0))
+EARLY = [(k, flip) for k in (0, 1, 2) for flip in range(3)]
+LATE = [(0, 3), (1, 3), (2, 3), (3, 0), (3, 1), (3, 2), (3, 3)]
 
 
 def block_order():
     place = lax.axis_index("ctx")
-    layers = lax.axis_size("ctx") // PLANE
     layer, spot = place // PLANE, place % PLANE
-    order = [(layer + layers - k) % layers * PLANE + (spot ^ flip) for k, flip in EARLY + LATE]
+    layers = jnp.array(LAYERS, jnp.int32)[:, layer]
+    order = [layers[k] * PLANE + (spot ^ flip) for k, flip in EARLY + LATE]
     return jnp.stack(order).astype(jnp.int32)
 
 
@@ -806,7 +821,7 @@
         [shape(wide // P_SIZE, length), shape(length, n), shape(length, n)],
         12 * length * wide * SPAN,
         6 * length * wide,
-        [pltpu.VMEM((SPAN, SPAN), F32)],
+        INNER_SCRATCH,
     )(*operands, *so_far)
 
 
@@ -842,12 +857,12 @@
     groups = heads // GROUP
     place = lax.axis_index("head").astype(jnp.int32)
     half = columns // 2
-    w_a, w_b = w_in[:, :half], w_in[:, half:]
     order = block_order()
     blocks = order.shape[0]
     width = blocks * w_in.shape[0]
 
-    z1, z3 = shift(w_in, 1), shift(w_in, 3)
+    layer = lax.axis_index("ctx") // PLANE
+    up1, down1 = along_z(w_in, 1), along_z(w_in, -1)
     own_x, own_y = swap_x(w_in), swap_y(w_in)
     other = swap(inputs, "head", 1)
     running, running_t, kept, own_grads = prepare(log_decay, grad_out, c_rows)
@@ -856,10 +871,13 @@
     sent = after([sent], other)[0]
     back, leaving, sent, log, factors_1 = back_step(spot, log, back, sent, (), 1)
 
-    z1, w_a, w_b = after([z1, w_a, w_b], own_x, own_y, z3)
-    z2a, z2b = shift(w_a, 2), shift(w_b, 2)
+    up1, down1 = after([up1, down1], own_x, own_y)
+    up2, down2 = along_z(up1, 1), along_z(down1, -1)
+    z1 = jnp.where(layer == 0, down1, up1)
     x1, y1 = swap_x(z1), swap_y(z1)
-    z3 = after([z3], sent)[0]
+    z3 = jnp.where(layer == 0, down2, jnp.where(layer == 3, up2, down1))
+    up2, down2, z3 = after([up2, down2, z3], sent)
+    up3, down3 = along_z(up2, 1), along_z(down2, -1)
     x3, y3 = swap_x(z3), swap_y(z3)
     back, leaving, sent, log, factors_2 = back_step(spot, log, back, sent, (leaving,), 2)
     order_own = (order + place * (blocks // 2)) % blocks
@@ -875,6 +893,8 @@
         [pltpu.VMEM((length, width), BF16)],
     )(order_own, inputs, other)
 
+    z2 = jnp.where(layer == 1, down2, jnp.where(layer == 2, up2, up3 + down3))
+    z2a, z2b = z2[:, :half], z2[:, half:]
     z2a, x1, y3, own_y = after(
         [z2a, x1, y3, own_y], y1, x3, z2b, sent, early_features, late_features
     )
@@ -1064,7 +1084,7 @@
             [shape(size, length), shape(length, n), shape(length, n)],
             12 * length * wide * SPAN,
             6 * length * wide,
-            [pltpu.VMEM((SPAN, SPAN), F32)],
+            INNER_SCRATCH,
         )(running, running_t, grad_out, x, b_rows, c_rows, leaving, *so_far)
         decay_part, grad_c = call(
             state_kernel,

time: 317 us -> 333 us (1.050)
  starting transfers between devices: 37.6 us -> 49.7 us
  Pallas kernels: 140 us -> 134 us
  other arithmetic: 14 us -> 18.5 us
    ppermute x4 -> x6, waiting for transfers between devices: 62.1 us -> 19.9 us  [along_z(): return lax.ppermute(value, 'ctx', pairs)]
    ppermute x34, waiting for transfers between devices: 43.4 us -> 85.4 us  [swap(): return lax.ppermute(value, axis, [(i, i ^ bit) for i in range(count)])]
    ppermute x4 -> x6, starting transfers between devices: 4.34 us -> 18.6 us  [along_z(): return lax.ppermute(value, 'ctx', pairs)]
    pallas_call x2, Pallas kernels: 23.3 us -> 17.8 us  [inner(): call(inner_kernel, grid, specs + [SHARED] * len(so_far), [run_spec(), SHA...]
    select_n x0 -> x2, other arithmetic: none -> 4.55 us  [the longest x1 2.83 us: local_layered(): z1 = jnp.where(layer == 0, down1, up1)]
    unnamed x56 -> x64, local copies, waits for them, and re-layouts: 10 us -> 10.2 us
  transfers between devices with their start and end apart: 38 -> 40, of which waited for: 14 -> 18; matrix products, arithmetic and copies ran while one was open for 5% -> 7% of each run, Pallas kernels for 38% -> 34%
where the time goes in v5:
time: 333 us; the launch traced here: 331 us
  Pallas kernels  134 us (40%)
  waiting for transfers between devices  105 us (32%)
  starting transfers between devices  49.7 us (15%)
  local copies, waits for them, and re-layouts  19.9 us (6%)
  other arithmetic  18.5 us (6%)
  between operations  3.6 us (1%)
    ppermute x34, waiting for transfers between devices, swap(): return lax.ppermute(value, axis, [(i, i ^ bit) for i in range(count)])  85.4 us
    ppermute x34, starting transfers between devices, swap(): return lax.ppermute(value, axis, [(i, i ^ bit) for i in range(count)])  31.2 us
    ppermute x6, waiting for transfers between devices, along_z(): return lax.ppermute(value, 'ctx', pairs)  19.9 us
    pallas_call x2, Pallas kernels, multiply_blocks(): pl.pallas_call(functools.partial(blocks_kernel, [len(piece) for piece in...  19.9 us
    ppermute x6, starting transfers between devices, along_z(): return lax.ppermute(value, 'ctx', pairs)  18.6 us
    pallas_call x2, Pallas kernels, inner(): call(inner_kernel, grid, specs + [SHARED] * len(so_far), [run_spec(), SHA...  17.8 us
    pallas_call x8, Pallas kernels, scan_step(): call(scan_kernel, (columns // WIDE,), [pl.BlockSpec((8, WIDE), lambda h:...  17.5 us
    pallas_call x4, Pallas kernels, back_step(): call(functools.partial(back_kernel, bit), (columns // WIDE,), [SCALARS] +...  16.2 us
  transfers between devices with their start and end apart: 40, of which 18 were waited for; matrix products, arithmetic and copies ran while one was open for 7% of the time, Pallas kernels for 34%

profile of v5, /device:TPU:0, one launch (start us, length us, event | category | flops | bytes accessed | tf_op | source)
XLA Modules:
  0.0 331.1 jit_solution(7087827838425714539)
XLA Ops:
  0.6 3.0 collective-permute-start.8
  3.7 1.5 collective-permute-start.7
  6.5 4.6 %collective-permute-start.5 = (bf16[256,2048]{1,0:T(8,128)(2,1)}, bf16[256,2048]{1,0:T(8,128)(2,1)S(1)}, u32[]{:S(2)}, u32[]{:S(2)}) collective-permute-start(bf16[256,2048]{1,0:T(8,128)(2,1)} %refs_0_.3), channel_id=1, source_target_pairs={{0,8},{2,10},{4,12},{6,14},{8,16},{10,18},{12,20},{14,22},{16,24},... | collective-permute-start | bytes 3145736 | tf_op jit(solution)/shard_map/ppermute | solution.py:530
  11.1 15.9 %collective-permute-done.8.refs_3_ = bf16[256,2048]{1,0:T(8,128)(2,1)S(1)} collective-permute-done((bf16[256,2048]{1,0:T(8,128)(2,1)}, bf16[256,2048]{1,0:T(8,128)(2,1)S(1)}, u32[]{:S(2)}, u32[]{:S(2)}) %collective-permute-start.8) | collective-permute-done | bytes 1048608 | tf_op jit(solution)/shard_map/ppermute | solution.py:469
  27.0 1.5 collective-permute-done.7.refs_2_.refs_1_
  28.5 3.1 collective-permute-done.6.refs_1_
  31.6 2.9 collective-permute-done.5.refs_0_
  35.5 4.3 %collective-permute-start.9 = (bf16[256,2048]{1,0:T(8,128)(2,1)}, bf16[256,2048]{1,0:T(8,128)(2,1)S(1)}, u32[]{:S(2)}, u32[]{:S(2)}) collective-permute-start(bf16[256,2048]{1,0:T(8,128)(2,1)} %get-tuple-element.113), channel_id=1, source_target_pairs={{0,8},{2,10},{4,12},{6,14},{8,16},{10,18},{12,20},{14,22},{16,24},... | collective-permute-start | bytes 3145736 | tf_op jit(solution)/shard_map/ppermute | solution.py:530
  41.1 9.1 %shard_map.111 = (f32[32,512]{1,0:T(8,128)}, f32[4,512,8]{2,1,0:T(8,128)}, f32[2,8,2048]{2,1,0:T(8,128)}, f32[2,128,2048]{2,1,0:T(8,128)}) custom-call(f32[32,512]{1,0:T(8,128)} %d_ref.1, bf16[512,2048]{1,0:T(8,128)(2,1)} %g_ref.11, bf16[512,128]{1,0:T(8,128)(2,1)} %c_ref.11), custom_call_target="tpu_custom_call" | custom-call | flops 268435456 | bytes 6291456 | tf_op jit(solution)/shard_map/pallas_call | solution.py:788
  50.2 3.7 %shard_map.112 = (f32[128,2048]{1,0:T(8,128)}, f32[8,2048]{1,0:T(8,128)}, bf16[144,2048]{1,0:T(8,128)(2,1)}) custom-call(f32[2,128,2048]{2,1,0:T(8,128)} %get-tuple-element.95.own_ref, f32[2,8,2048]{2,1,0:T(8,128)} %get-tuple-element.96.kept_ref.a_ref), custom_call_target="tpu_custom_call" | custom-call | bytes 3670016 | tf_op jit(solution)/shard_map/pallas_call | solution.py:723
  54.6 7.7 %collective-permute-done.9.refs_0_ = bf16[256,2048]{1,0:T(8,128)(2,1)S(1)} collective-permute-done((bf16[256,2048]{1,0:T(8,128)(2,1)}, bf16[256,2048]{1,0:T(8,128)(2,1)S(1)}, u32[]{:S(2)}, u32[]{:S(2)}) %collective-permute-start.9) | collective-permute-done | bytes 1048608 | tf_op jit(solution)/shard_map/ppermute | solution.py:530
  62.3 4.2 %collective-permute-done.10.refs_1_ = bf16[256,2048]{1,0:T(8,128)(2,1)} collective-permute-done((bf16[256,2048]{1,0:T(8,128)(2,1)}, bf16[256,2048]{1,0:T(8,128)(2,1)}, u32[]{:S(2)}, u32[]{:S(2)}) %collective-permute-start.10) | collective-permute-done | bytes 1048608 | tf_op jit(solution)/shard_map/ppermute | solution.py:530
  66.5 2.8 broadcast_select_fusion
  70.2 3.9 %shard_map.114 = (f32[128,2048]{1,0:T(8,128)}, f32[128,2048]{1,0:T(8,128)}, bf16[144,2048]{1,0:T(8,128)(2,1)}, f32[8,2048]{1,0:T(8,128)}, f32[8,2048]{1,0:T(8,128)}) custom-call(s32[1]{0:T(128)} %bitcast.22.place_ref, f32[8,2048]{1,0:T(8,128)} %get-tuple-element.97.log_ref, f32[128,2048]{1,0:T(8,128)} %get-tuple-element.98.total_ref, ...), custom_call_target="tpu_custom_call" | custom-call | bytes 4718592 | tf_op jit(solution)/shard_map/pallas_call | solution.py:741
  75.5 5.6 %collective-permute-start.11 = (bf16[256,2048]{1,0:T(8,128)(2,1)}, bf16[256,2048]{1,0:T(8,128)(2,1)}, u32[]{:S(2)}, u32[]{:S(2)}) collective-permute-start(bf16[256,2048]{1,0:T(8,128)(2,1)} %get-tuple-element.116), channel_id=1, source_target_pairs={{0,8},{2,10},{4,12},{6,14},{8,16},{10,18},{12,20},{14,22},{16,24},... | collective-permute-start | bytes 3145736 | tf_op jit(solution)/shard_map/ppermute | solution.py:530
  86.5 1.6 collective-permute-start.15
  88.6 8.8 %collective-permute-done.2.got_ref = bf16[144,2048]{1,0:T(8,128)(2,1)S(1)} collective-permute-done((bf16[144,2048]{1,0:T(8,128)(2,1)S(1)}, bf16[144,2048]{1,0:T(8,128)(2,1)S(1)}, u32[]{:S(2)}, u32[]{:S(2)}) %collective-permute-start.2) | collective-permute-done | bytes 589856 | tf_op jit(solution)/shard_map/ppermute | solution.py:469
  97.9 2.0 collective-permute-done.12
  101.0 5.1 %shard_map.121 = (bf16[512,2304]{1,0:T(8,128)(2,1)}, bf16[512,1792]{1,0:T(8,128)(2,1)}) custom-call(s32[16]{0:T(128)} %get-tuple-element.198.order_ref, bf16[512,2048]{1,0:T(8,128)(2,1)} %own_ref.1, bf16[512,2048]{1,0:T(8,128)(2,1)} %collective-permute-done.refs_1_.other_ref), custom_call_target="tpu_custom_call" | custom-call | bytes 8388608 | tf_op jit(solution)/shard_map/pallas_call | solution.py:885
  106.1 4.2 %shard_map.115 = (f32[128,2048]{1,0:T(8,128)}, f32[128,2048]{1,0:T(8,128)}, bf16[144,2048]{1,0:T(8,128)(2,1)}, f32[8,2048]{1,0:T(8,128)}, f32[8,2048]{1,0:T(8,128)}) custom-call(s32[1]{0:T(128)} %bitcast.22.place_ref, f32[8,2048]{1,0:T(8,128)} %get-tuple-element.100.log_ref, f32[128,2048]{1,0:T(8,128)} %get-tuple-element.101.total_ref, ...), custom_call_target="tpu_custom_call" | custom-call | bytes 4718592 | tf_op jit(solution)/shard_map/pallas_call | solution.py:741
  110.3 1.7 collective-permute-start.3
  112.0 1.7 select_select_fusion
  114.9 5.1 %collective-permute-done.15.refs_4_.refs_5_ = bf16[256,2048]{1,0:T(8,128)(2,1)} collective-permute-done((bf16[256,2048]{1,0:T(8,128)(2,1)}, bf16[256,2048]{1,0:T(8,128)(2,1)}, u32[]{:S(2)}, u32[]{:S(2)}) %collective-permute-start.15) | collective-permute-done | bytes 1048608 | tf_op jit(solution)/shard_map/ppermute | solution.py:469
  120.0 13.4 %collective-permute-done.16.refs_5_.refs_7_ = bf16[256,2048]{1,0:T(8,128)(2,1)} collective-permute-done((bf16[256,2048]{1,0:T(8,128)(2,1)}, bf16[256,2048]{1,0:T(8,128)(2,1)}, u32[]{:S(2)}, u32[]{:S(2)}) %collective-permute-start.16) | collective-permute-done | bytes 1048608 | tf_op jit(solution)/shard_map/ppermute | solution.py:469
  133.3 6.0 %collective-permute-done.14.refs_2_ = bf16[256,2048]{1,0:T(8,128)(2,1)} collective-permute-done((bf16[256,2048]{1,0:T(8,128)(2,1)}, bf16[256,2048]{1,0:T(8,128)(2,1)}, u32[]{:S(2)}, u32[]{:S(2)}) %collective-permute-start.14) | collective-permute-done | bytes 1048608 | tf_op jit(solution)/shard_map/ppermute | solution.py:469
  140.4 2.2 fusion.6
  142.6 1.5 collective-permute-start.19
  144.1 2.4 fusion.5
  146.4 1.5 collective-permute-start.20
  148.0 4.1 %shard_map.116 = (f32[128,2048]{1,0:T(8,128)}, f32[128,2048]{1,0:T(8,128)}, bf16[144,2048]{1,0:T(8,128)(2,1)}, f32[8,2048]{1,0:T(8,128)}, f32[8,2048]{1,0:T(8,128)}) custom-call(s32[1]{0:T(128)} %bitcast.22.place_ref, f32[8,2048]{1,0:T(8,128)} %get-tuple-element.104.log_ref, f32[128,2048]{1,0:T(8,128)} %get-tuple-element.105.total_ref, ...), custom_call_target="tpu_custom_call" | custom-call | bytes 4718592 | tf_op jit(solution)/shard_map/pallas_call | solution.py:741
  152.0 2.9 collective-permute-start.4
  156.0 10.2 %shard_map.123.refs_8_.part_ref = f32[512,2048]{1,0:T(8,128)} custom-call(bf16[512,2304]{1,0:T(8,128)(2,1)} %get-tuple-element.118.refs_8_.f_ref, bf16[256,2048]{1,0:T(8,128)(2,1)} %refs_0_.3, bf16[256,2048]{1,0:T(8,128)(2,1)} %copy-done.14, bf16[256,2048]{1,0:T(8,128)(2,1)} %get-tuple-element.120.refs_2_, bf16[256,2048]{1,0:T(8,128)(2,1)} %get-tuple-element.190.refs_3_, ...), custom_call_target="tpu_custom_call" | custom-call | flops 4831838208 | bytes 9437184 | tf_op jit(solution)/shard_map/pallas_call | solution.py:640
  168.1 1.5 collective-permute-start.21
  170.1 6.8 %collective-permute-done.4.got_ref = bf16[144,2048]{1,0:T(8,128)(2,1)} collective-permute-done((bf16[144,2048]{1,0:T(8,128)(2,1)}, bf16[144,2048]{1,0:T(8,128)(2,1)}, u32[]{:S(2)}, u32[]{:S(2)}) %collective-permute-start.4) | collective-permute-done | bytes 589856 | tf_op jit(solution)/shard_map/ppermute | solution.py:469
  177.4 4.1 %shard_map.117 = (f32[128,2048]{1,0:T(8,128)}, f32[128,2048]{1,0:T(8,128)}, bf16[144,2048]{1,0:T(8,128)(2,1)}, f32[8,2048]{1,0:T(8,128)}, f32[8,2048]{1,0:T(8,128)}) custom-call(s32[1]{0:T(128)} %bitcast.22.place_ref, f32[8,2048]{1,0:T(8,128)} %get-tuple-element.108.log_ref, f32[128,2048]{1,0:T(8,128)} %get-tuple-element.109.total_ref, ...), custom_call_target="tpu_custom_call" | custom-call | bytes 4718592 | tf_op jit(solution)/shard_map/pallas_call | solution.py:741
  181.5 2.1 fusion.1
  183.6 10.0 %collective-permute-done.21.refs_0_ = bf16[256,1024]{1,0:T(8,128)(2,1)} collective-permute-done((bf16[256,1024]{1,0:T(8,128)(2,1)}, bf16[256,1024]{1,0:T(8,128)(2,1)}, u32[]{:S(2)}, u32[]{:S(2)}) %collective-permute-start.21) | collective-permute-done | bytes 524320 | tf_op jit(solution)/shard_map/ppermute | solution.py:469
  193.7 1.5 collective-permute-start.26
  196.3 10.4 %shard_map.118.refs_6_.g_ref = bf16[2048,512]{1,0:T(8,128)(2,1)} custom-call(f32[32,512]{1,0:T(8,128)} %get-tuple-element.93.r_ref, f32[4,512,8]{2,1,0:T(8,128)} %get-tuple-element.94.rt_ref, bf16[512,2048]{1,0:T(8,128)(2,1)} %g_ref.11, bf16[512,128]{1,0:T(8,128)(2,1)} %b_ref.9, bf16[512,128]{1,0:T(8,128)(2,1)} %c_ref.11, ...), custom_call_target="tpu_custom_call" | custom-call | flops 2147483648 | bytes 6291456 | tf_op jit(solution)/shard_map/pallas_call | solution.py:986
  206.6 6.6 %shard_map.125 = (bf16[512,1024]{1,0:T(8,128)(2,1)}, f32[2,128,1024]{2,1,0:T(8,128)}, f32[128,1024]{1,0:T(8,128)}, bf16[128,1024]{1,0:T(8,128)(2,1)}) custom-call(bf16[512,1792]{1,0:T(8,128)(2,1)} %get-tuple-element.119.refs_9_.f_ref, f32[512,2048]{1,0:T(8,128)} %shard_map.123.refs_8_.part_ref, f32[4,512,8]{2,1,0:T(8,128)} %get-tuple-element.94.rt_ref, ...), custom_call_target="tpu_custom_call" | custom-call | flops 1879048192 | bytes 3670016 | tf_op jit(solution)/shard_map/pallas_call | solution.py:660
  215.3 1.5 collective-permute-start.29
  216.8 10.0 %shard_map.128 = (bf16[512,2048]{1,0:T(8,128)(2,1)}, bf16[512,2048]{1,0:T(8,128)(2,1)}) custom-call(s32[9]{0:T(128)} %bitcast.34, bf16[2048,512]{1,0:T(8,128)(2,1)} %shard_map.118.refs_6_.g_ref, bf16[256,2048]{1,0:T(8,128)(2,1)} %refs_0_.3, bf16[256,2048]{1,0:T(8,128)(2,1)} %copy-done.14, bf16[256,2048]{1,0:T(8,128)(2,1)} %get-tuple-element.120.refs_2_, ...), custom_call_target="tpu_custom_call" | custom-call | flops 4831838208 | bytes 9437184 | tf_op jit(solution)/shard_map/pallas_call | solution.py:696
  227.5 2.1 shard_map.127
  230.6 6.6 %shard_map.130 = (bf16[512,1024]{1,0:T(8,128)(2,1)}, f32[2,128,1024]{2,1,0:T(8,128)}, f32[128,1024]{1,0:T(8,128)}, bf16[128,1024]{1,0:T(8,128)(2,1)}) custom-call(bf16[512,1792]{1,0:T(8,128)(2,1)} %get-tuple-element.119.refs_9_.f_ref, f32[512,2048]{1,0:T(8,128)} %shard_map.123.refs_8_.part_ref, f32[4,512,8]{2,1,0:T(8,128)} %get-tuple-element.94.rt_ref, ...), custom_call_target="tpu_custom_call" | custom-call | flops 1879048192 | bytes 3670016 | tf_op jit(solution)/shard_map/pallas_call | solution.py:660
  238.4 5.4 %collective-permute-done.30.got_ref = bf16[128,1024]{1,0:T(8,128)(2,1)S(1)} collective-permute-done((bf16[128,1024]{1,0:T(8,128)(2,1)}, bf16[128,1024]{1,0:T(8,128)(2,1)S(1)}, u32[]{:S(2)}, u32[]{:S(2)}) %collective-permute-start.30) | collective-permute-done | bytes 262176 | tf_op jit(solution)/shard_map/ppermute | solution.py:469
  244.5 2.1 shard_map.131
  246.6 9.9 %shard_map.133 = (bf16[512,2048]{1,0:T(8,128)(2,1)}, bf16[512,2048]{1,0:T(8,128)(2,1)}) custom-call(s32[7]{0:T(128)} %slice.68.order_ref, bf16[2048,512]{1,0:T(8,128)(2,1)} %shard_map.118.refs_6_.g_ref, bf16[256,1024]{1,0:T(8,128)(2,1)} %collective-permute-done.21.refs_0_, ...), custom_call_target="tpu_custom_call", output_to_operand_aliasing={{0}: (16, {}), {1}: (17, {})} | custom-call | flops 3758096384 | bytes 7340032 | tf_op jit(solution)/shard_map/pallas_call | solution.py:696
  256.6 1.6 collective-permute-start.36
  258.7 7.1 %collective-permute-done.36.got_ref = bf16[128,1024]{1,0:T(8,128)(2,1)S(1)} collective-permute-done((bf16[128,1024]{1,0:T(8,128)(2,1)S(1)}, bf16[128,1024]{1,0:T(8,128)(2,1)S(1)}, u32[]{:S(2)}, u32[]{:S(2)}) %collective-permute-start.36) | collective-permute-done | bytes 262176 | tf_op jit(solution)/shard_map/ppermute | solution.py:469
  266.5 2.3 shard_map.143
  268.8 2.2 collective-permute-done.32.got_ref
  271.7 2.2 shard_map.134
  273.9 2.5 collective-permute-done.37.got_ref
  277.1 2.2 shard_map.144
  279.6 8.8 %shard_map.139 = (f32[16,512]{1,0:T(8,128)}, f32[512,128]{1,0:T(8,128)}, f32[512,128]{1,0:T(8,128)}) custom-call(f32[32,512]{1,0:T(8,128)} %get-tuple-element.93.r_ref, f32[4,512,8]{2,1,0:T(8,128)} %get-tuple-element.94.rt_ref, bf16[512,2048]{1,0:T(8,128)(2,1)} %g_ref.11, bf16[512,1024]{1,0:T(8,128)(2,1)} %shard_map.138.x_ref, bf16[512,128]{1,0:T(8,128)(2,1)} %b_ref.9, ...), custom_call_target="tpu_custom_call" | custom-call | flops 1610612736 | bytes 3145728 | tf_op jit(solution)/shard_map/pallas_call | solution.py:816
  289.1 2.2 shard_map.136
  291.3 9.0 %shard_map.140 = (f32[16,512]{1,0:T(8,128)}, f32[512,128]{1,0:T(8,128)}, f32[512,128]{1,0:T(8,128)}) custom-call(f32[32,512]{1,0:T(8,128)} %get-tuple-element.93.r_ref, f32[4,512,8]{2,1,0:T(8,128)} %get-tuple-element.94.rt_ref, bf16[512,2048]{1,0:T(8,128)(2,1)} %g_ref.11, bf16[512,1024]{1,0:T(8,128)(2,1)} %shard_map.137.x_ref, bf16[512,128]{1,0:T(8,128)(2,1)} %b_ref.9, ...), custom_call_target="tpu_custom_call" | custom-call | flops 1610612736 | bytes 3145728 | tf_op jit(solution)/shard_map/pallas_call | solution.py:816
  300.3 2.7 collective-permute-start.35
  304.8 2.2 shard_map.145
  307.0 5.5 %shard_map.146 = (f32[16,512]{1,0:T(8,128)}, f32[512,128]{1,0:T(8,128)}) custom-call(f32[4,512,8]{2,1,0:T(8,128)} %get-tuple-element.94.rt_ref, bf16[512,2048]{1,0:T(8,128)(2,1)} %g_ref.11, bf16[512,128]{1,0:T(8,128)(2,1)} %c_ref.11, f32[128,1024]{1,0:T(8,128)} %get-tuple-element.174.s_ref, f32[2,128,1024]{2,1,0:T(8,128)} %get-tuple-element.175.e_ref, ...), custom_call_target="tpu_custom_call" | custom-call | flops 268435456 | bytes 3145728 | tf_op jit(solution)/shard_map/pallas_call | solution.py:831
  314.1 2.2 shard_map.142
  316.3 5.6 %shard_map.147 = (f32[16,512]{1,0:T(8,128)}, f32[512,128]{1,0:T(8,128)}) custom-call(f32[4,512,8]{2,1,0:T(8,128)} %get-tuple-element.94.rt_ref, bf16[512,2048]{1,0:T(8,128)(2,1)} %g_ref.11, bf16[512,128]{1,0:T(8,128)(2,1)} %c_ref.11, f32[128,1024]{1,0:T(8,128)} %get-tuple-element.163.s_ref, f32[2,128,1024]{2,1,0:T(8,128)} %get-tuple-element.164.e_ref, ...), custom_call_target="tpu_custom_call" | custom-call | flops 268435456 | bytes 3145728 | tf_op jit(solution)/shard_map/pallas_call | solution.py:831
  325.0 1.7 convert_add_fusion
  326.7 4.4 %add_convert_fusion = bf16[512,2048]{1,0:T(8,128)(2,1)} fusion(bf16[512,2048]{1,0:T(8,128)(2,1)} %collective-permute-done.31, bf16[512,2048]{1,0:T(8,128)(2,1)} %get-tuple-element.145), kind=kLoop, calls=%fused_computation | loop fusion | flops 4194304 | bytes 6291456 | tf_op jit(solution)/shard_map/convert_element_type | solution.py:976
  (139 shorter events, 34.6 us)
Async XLA Ops:
  0.6 26.4 %collective-permute-start.8 = (bf16[256,2048]{1,0:T(8,128)(2,1)}, bf16[256,2048]{1,0:T(8,128)(2,1)S(1)}, u32[]{:S(2)}, u32[]{:S(2)}) collective-permute-start(bf16[256,2048]{1,0:T(8,128)(2,1)} %refs_0_.3), channel_id=1, source_target_pairs={{0,4},{2,6},{4,0},{6,2},{8,12},{10,14},{12,8},{14,10},{16,20},{18,... | collective-permute-start | bytes 3145736 | tf_op jit(solution)/shard_map/ppermute | solution.py:469
  3.7 24.8 %collective-permute-start.7 = (bf16[256,2048]{1,0:T(8,128)(2,1)}, bf16[256,2048]{1,0:T(8,128)(2,1)S(1)}, u32[]{:S(2)}, u32[]{:S(2)}) collective-permute-start(bf16[256,2048]{1,0:T(8,128)(2,1)} %refs_0_.3), channel_id=1, source_target_pairs={{0,2},{2,0},{4,6},{6,4},{8,10},{10,8},{12,14},{14,12},{16,18},{18,... | collective-permute-start | bytes 3145736 | tf_op jit(solution)/shard_map/ppermute | solution.py:469
  5.2 26.4 %collective-permute-start.6 = (bf16[256,2048]{1,0:T(8,128)(2,1)}, bf16[256,2048]{1,0:T(8,128)(2,1)S(1)}, u32[]{:S(2)}, u32[]{:S(2)}) collective-permute-start(bf16[256,2048]{1,0:T(8,128)(2,1)} %refs_0_.3), channel_id=1, source_target_pairs={{8,0},{10,2},{12,4},{14,6},{16,8},{18,10},{20,12},{22,14},{24,16},... | collective-permute-start | bytes 3145736 | tf_op jit(solution)/shard_map/ppermute | solution.py:530
  6.4 47.5 %collective-permute-start = (bf16[512,2048]{1,0:T(8,128)(2,1)}, bf16[512,2048]{1,0:T(8,128)(2,1)}, u32[]{:S(2)}, u32[]{:S(2)}) collective-permute-start(bf16[512,2048]{1,0:T(8,128)(2,1)} %own_ref.1), channel_id=1, source_target_pairs={{0,1},{1,0},{2,3},{3,2},{4,5},{5,4},{6,7},{7,6},{8,9},{9,8},{10,11... | collective-permute-start | bytes 6291464 | tf_op jit(solution)/shard_map/ppermute | solution.py:469
  6.5 27.9 %collective-permute-start.5 = (bf16[256,2048]{1,0:T(8,128)(2,1)}, bf16[256,2048]{1,0:T(8,128)(2,1)S(1)}, u32[]{:S(2)}, u32[]{:S(2)}) collective-permute-start(bf16[256,2048]{1,0:T(8,128)(2,1)} %refs_0_.3), channel_id=1, source_target_pairs={{0,8},{2,10},{4,12},{6,14},{8,16},{10,18},{12,20},{14,22},{16,24},... | collective-permute-start | bytes 3145736 | tf_op jit(solution)/shard_map/ppermute | solution.py:530
  27.0 7.4 %copy-start.2 = (bf16[256,2048]{1,0:T(8,128)(2,1)}, bf16[256,2048]{1,0:T(8,128)(2,1)S(1)}, u32[]{:S(2)}) copy-start(bf16[256,2048]{1,0:T(8,128)(2,1)S(1)} %collective-permute-done.8.refs_3_) | copy-start | bytes 3145732
  28.5 3.1 copy-start.14
  31.6 2.9 copy-start.4
  34.5 1.0 copy-start.6
  35.5 26.8 %collective-permute-start.9 = (bf16[256,2048]{1,0:T(8,128)(2,1)}, bf16[256,2048]{1,0:T(8,128)(2,1)S(1)}, u32[]{:S(2)}, u32[]{:S(2)}) collective-permute-start(bf16[256,2048]{1,0:T(8,128)(2,1)} %get-tuple-element.113), channel_id=1, source_target_pairs={{0,8},{2,10},{4,12},{6,14},{8,16},{10,18},{12,20},{14,22},{16,24},... | collective-permute-start | bytes 3145736 | tf_op jit(solution)/shard_map/ppermute | solution.py:530
  39.8 26.7 %collective-permute-start.10 = (bf16[256,2048]{1,0:T(8,128)(2,1)}, bf16[256,2048]{1,0:T(8,128)(2,1)}, u32[]{:S(2)}, u32[]{:S(2)}) collective-permute-start(bf16[256,2048]{1,0:T(8,128)(2,1)} %get-tuple-element.114), channel_id=1, source_target_pairs={{8,0},{10,2},{12,4},{14,6},{16,8},{18,10},{20,12},{22,14},{24,16},... | collective-permute-start | bytes 3145736 | tf_op jit(solution)/shard_map/ppermute | solution.py:530
  54.0 12.5 %copy-start.5 = (bf16[256,2048]{1,0:T(8,128)(2,1)S(1)}, bf16[256,2048]{1,0:T(8,128)(2,1)}, u32[]{:S(2)}) copy-start(bf16[256,2048]{1,0:T(8,128)(2,1)} %get-tuple-element.114) | copy-start | bytes 3145732
  54.0 15.3 %collective-permute-start.1 = (bf16[144,2048]{1,0:T(8,128)(2,1)}, bf16[144,2048]{1,0:T(8,128)(2,1)S(1)}, u32[]{:S(2)}, u32[]{:S(2)}) collective-permute-start(bf16[144,2048]{1,0:T(8,128)(2,1)} %shard_map.113), channel_id=1, source_target_pairs={{0,2},{2,0},{4,6},{6,4},{8,10},{10,8},{12,14},{14,12},{16,18},{18,... | collective-permute-start | bytes 1769480 | tf_op jit(solution)/shard_map/ppermute | solution.py:469
  62.3 7.0 %copy-start = (bf16[256,2048]{1,0:T(8,128)(2,1)}, bf16[256,2048]{1,0:T(8,128)(2,1)S(1)}, u32[]{:S(2)}) copy-start(bf16[256,2048]{1,0:T(8,128)(2,1)S(1)} %collective-permute-done.9.refs_0_) | copy-start | bytes 3145732
  69.3 0.8 copy-start.16
  74.0 7.1 %copy-start.15 = (bf16[144,2048]{1,0:T(8,128)(2,1)S(1)}, bf16[144,2048]{1,0:T(8,128)(2,1)}, u32[]{:S(2)}) copy-start(bf16[144,2048]{1,0:T(8,128)(2,1)} %get-tuple-element.102.refs_3_) | copy-start | bytes 1769476
  74.0 7.6 %copy-start.29 = (s32[4,4]{1,0:T(4,128)S(1)}, s32[4,4]{1,0:T(4,128)}, u32[]{:S(2)}) copy-start(s32[4,4]{1,0:T(4,128)} %constant.68.clone) | copy-start | bytes 196
  74.0 11.6 %copy-start.30 = (f32[32]{0:T(128)S(1)}, f32[32]{0:T(128)}, u32[]{:S(2)}) copy-start(f32[32]{0:T(128)} %param.13) | copy-start | bytes 388
  74.1 25.9 %collective-permute-start.12 = (bf16[256,2048]{1,0:T(8,128)(2,1)}, bf16[256,2048]{1,0:T(8,128)(2,1)}, u32[]{:S(2)}, u32[]{:S(2)}) collective-permute-start(bf16[256,2048]{1,0:T(8,128)(2,1)} %get-tuple-element.115), channel_id=1, source_target_pairs={{8,0},{10,2},{12,4},{14,6},{16,8},{18,10},{20,12},{22,14},{24,16},... | collective-permute-start | bytes 3145736 | tf_op jit(solution)/shard_map/ppermute | solution.py:530
  75.5 34.8 %collective-permute-start.11 = (bf16[256,2048]{1,0:T(8,128)(2,1)}, bf16[256,2048]{1,0:T(8,128)(2,1)}, u32[]{:S(2)}, u32[]{:S(2)}) collective-permute-start(bf16[256,2048]{1,0:T(8,128)(2,1)} %get-tuple-element.116), channel_id=1, source_target_pairs={{0,8},{2,10},{4,12},{6,14},{8,16},{10,18},{12,20},{14,22},{16,24},... | collective-permute-start | bytes 3145736 | tf_op jit(solution)/shard_map/ppermute | solution.py:530
  81.1 16.3 %collective-permute-start.2 = (bf16[144,2048]{1,0:T(8,128)(2,1)S(1)}, bf16[144,2048]{1,0:T(8,128)(2,1)S(1)}, u32[]{:S(2)}, u32[]{:S(2)}) collective-permute-start(bf16[144,2048]{1,0:T(8,128)(2,1)S(1)} %copy-done.15), channel_id=1, source_target_pairs={{0,4},{2,6},{4,0},{6,2},{8,12},{10,14},{12,8},{14,10},{16,20},{18,... | collective-permute-start | bytes 1769480 | tf_op jit(solution)/shard_map/ppermute | solution.py:469
  86.5 33.4 %collective-permute-start.15 = (bf16[256,2048]{1,0:T(8,128)(2,1)}, bf16[256,2048]{1,0:T(8,128)(2,1)}, u32[]{:S(2)}, u32[]{:S(2)}) collective-permute-start(bf16[256,2048]{1,0:T(8,128)(2,1)} %get-tuple-element.190.refs_3_), channel_id=1, source_target_pairs={{0,4},{2,6},{4,0},{6,2},{8,12},{10,14},{12,8},{14,10},{16,20},{18,... | collective-permute-start | bytes 3145736 | tf_op jit(solution)/shard_map/ppermute | solution.py:469
  88.1 31.9 %collective-permute-start.13 = (bf16[256,2048]{1,0:T(8,128)(2,1)}, bf16[256,2048]{1,0:T(8,128)(2,1)}, u32[]{:S(2)}, u32[]{:S(2)}) collective-permute-start(bf16[256,2048]{1,0:T(8,128)(2,1)} %get-tuple-element.190.refs_3_), channel_id=1, source_target_pairs={{0,2},{2,0},{4,6},{6,4},{8,10},{10,8},{12,14},{14,12},{16,18},{18,... | collective-permute-start | bytes 3145736 | tf_op jit(solution)/shard_map/ppermute | solution.py:469
  97.4 8.8 %copy-start.17 = (bf16[144,2048]{1,0:T(8,128)(2,1)}, bf16[144,2048]{1,0:T(8,128)(2,1)S(1)}, u32[]{:S(2)}) copy-start(bf16[144,2048]{1,0:T(8,128)(2,1)S(1)} %collective-permute-done.2.got_ref) | copy-start | bytes 1769476
  97.4 35.9 %collective-permute-start.16 = (bf16[256,2048]{1,0:T(8,128)(2,1)}, bf16[256,2048]{1,0:T(8,128)(2,1)}, u32[]{:S(2)}, u32[]{:S(2)}) collective-permute-start(bf16[256,2048]{1,0:T(8,128)(2,1)} %get-tuple-element.117.refs_6_), channel_id=1, source_target_pairs={{0,2},{2,0},{4,6},{6,4},{8,10},{10,8},{12,14},{14,12},{16,18},{18,... | collective-permute-start | bytes 3145736 | tf_op jit(solution)/shard_map/ppermute | solution.py:469
  99.9 39.4 %collective-permute-start.14 = (bf16[256,2048]{1,0:T(8,128)(2,1)}, bf16[256,2048]{1,0:T(8,128)(2,1)}, u32[]{:S(2)}, u32[]{:S(2)}) collective-permute-start(bf16[256,2048]{1,0:T(8,128)(2,1)} %get-tuple-element.117.refs_6_), channel_id=1, source_target_pairs={{0,4},{2,6},{4,0},{6,2},{8,12},{10,14},{12,8},{14,10},{16,20},{18,... | collective-permute-start | bytes 3145736 | tf_op jit(solution)/shard_map/ppermute | solution.py:469
  106.1 5.9 %copy-start.1 = (bf16[256,2048]{1,0:T(8,128)(2,1)S(1)}, bf16[256,2048]{1,0:T(8,128)(2,1)}, u32[]{:S(2)}) copy-start(bf16[256,2048]{1,0:T(8,128)(2,1)} %get-tuple-element.116) | copy-start | bytes 3145732
  110.3 37.7 %collective-permute-start.3 = (bf16[144,2048]{1,0:T(8,128)(2,1)}, bf16[144,2048]{1,0:T(8,128)(2,1)}, u32[]{:S(2)}, u32[]{:S(2)}) collective-permute-start(bf16[144,2048]{1,0:T(8,128)(2,1)} %get-tuple-element.106.refs_7_), channel_id=1, source_target_pairs={{0,8},{2,10},{4,12},{6,14},{8,0},{10,2},{12,4},{14,6},{16,24},{18,... | collective-permute-start | bytes 1769480 | tf_op jit(solution)/shard_map/ppermute | solution.py:469
  139.3 26.9 %collective-permute-start.18 = (bf16[256,1024]{1,0:T(8,128)(2,1)}, bf16[256,1024]{1,0:T(8,128)(2,1)S(1)}, u32[]{:S(2)}, u32[]{:S(2)}) collective-permute-start(bf16[256,1024]{1,0:T(8,128)(2,1)} %get-tuple-element.121.refs_3_.refs_6_), channel_id=1, source_target_pairs={{0,4},{2,6},{4,0},{6,2},{8,12},{10,14},{12,8},{14,10},{16,20},{18,... | collective-permute-start | bytes 1572872 | tf_op jit(solution)/shard_map/ppermute | solution.py:469
  139.8 26.4 %collective-permute-start.17 = (bf16[256,1024]{1,0:T(8,128)(2,1)}, bf16[256,1024]{1,0:T(8,128)(2,1)}, u32[]{:S(2)}, u32[]{:S(2)}) collective-permute-start(bf16[256,1024]{1,0:T(8,128)(2,1)} %get-tuple-element.121.refs_3_.refs_6_), channel_id=1, source_target_pairs={{0,2},{2,0},{4,6},{6,4},{8,10},{10,8},{12,14},{14,12},{16,18},{18,... | collective-permute-start | bytes 1572872 | tf_op jit(solution)/shard_map/ppermute | solution.py:469
  142.6 23.7 %collective-permute-start.19 = (bf16[256,1024]{1,0:T(8,128)(2,1)}, bf16[256,1024]{1,0:T(8,128)(2,1)}, u32[]{:S(2)}, u32[]{:S(2)}) collective-permute-start(bf16[256,1024]{1,0:T(8,128)(2,1)} %get-tuple-element.186), channel_id=1, source_target_pairs={{0,2},{2,0},{4,6},{6,4},{8,10},{10,8},{12,14},{14,12},{16,18},{18,... | collective-permute-start | bytes 1572872 | tf_op jit(solution)/shard_map/ppermute | solution.py:469
  144.1 10.9 %copy-start.3 = (bf16[256,2048]{1,0:T(8,128)(2,1)S(1)}, bf16[256,2048]{1,0:T(8,128)(2,1)}, u32[]{:S(2)}) copy-start(bf16[256,2048]{1,0:T(8,128)(2,1)} %get-tuple-element.120.refs_2_) | copy-start | bytes 3145732
  146.4 19.8 %collective-permute-start.20 = (bf16[256,1024]{1,0:T(8,128)(2,1)}, bf16[256,1024]{1,0:T(8,128)(2,1)}, u32[]{:S(2)}, u32[]{:S(2)}) collective-permute-start(bf16[256,1024]{1,0:T(8,128)(2,1)} %get-tuple-element.184), channel_id=1, source_target_pairs={{0,4},{2,6},{4,0},{6,2},{8,12},{10,14},{12,8},{14,10},{16,20},{18,... | collective-permute-start | bytes 1572872 | tf_op jit(solution)/shard_map/ppermute | solution.py:469
  152.0 24.9 %collective-permute-start.4 = (bf16[144,2048]{1,0:T(8,128)(2,1)}, bf16[144,2048]{1,0:T(8,128)(2,1)}, u32[]{:S(2)}, u32[]{:S(2)}) collective-permute-start(bf16[144,2048]{1,0:T(8,128)(2,1)} %get-tuple-element.110.refs_9_), channel_id=1, source_target_pairs={{0,16},{2,18},{4,20},{6,22},{8,24},{10,26},{12,28},{14,30},{16,0},... | collective-permute-start | bytes 1769480 | tf_op jit(solution)/shard_map/ppermute | solution.py:469
  166.2 0.8 copy-start.9
  167.0 46.2 %collective-permute-start.24 = (bf16[256,1024]{1,0:T(8,128)(2,1)}, bf16[256,1024]{1,0:T(8,128)(2,1)S(1)}, u32[]{:S(2)}, u32[]{:S(2)}) collective-permute-start(bf16[256,1024]{1,0:T(8,128)(2,1)} %get-tuple-element.125.refs_3_.refs_7_), channel_id=1, source_target_pairs={{0,4},{2,6},{4,0},{6,2},{8,12},{10,14},{12,8},{14,10},{16,20},{18,... | collective-permute-start | bytes 1572872 | tf_op jit(solution)/shard_map/ppermute | solution.py:469
  167.5 45.7 %collective-permute-start.22 = (bf16[256,1024]{1,0:T(8,128)(2,1)}, bf16[256,1024]{1,0:T(8,128)(2,1)}, u32[]{:S(2)}, u32[]{:S(2)}) collective-permute-start(bf16[256,1024]{1,0:T(8,128)(2,1)} %get-tuple-element.125.refs_3_.refs_7_), channel_id=1, source_target_pairs={{0,2},{2,0},{4,6},{6,4},{8,10},{10,8},{12,14},{14,12},{16,18},{18,... | collective-permute-start | bytes 1572872 | tf_op jit(solution)/shard_map/ppermute | solution.py:469
  168.1 25.6 %collective-permute-start.21 = (bf16[256,1024]{1,0:T(8,128)(2,1)}, bf16[256,1024]{1,0:T(8,128)(2,1)}, u32[]{:S(2)}, u32[]{:S(2)}) collective-permute-start(bf16[256,1024]{1,0:T(8,128)(2,1)} %get-tuple-element.124), channel_id=1, source_target_pairs={{0,2},{2,0},{4,6},{6,4},{8,10},{10,8},{12,14},{14,12},{16,18},{18,... | collective-permute-start | bytes 1572872 | tf_op jit(solution)/shard_map/ppermute | solution.py:469
  169.6 43.7 %collective-permute-start.25 = (bf16[256,1024]{1,0:T(8,128)(2,1)}, bf16[256,1024]{1,0:T(8,128)(2,1)S(1)}, u32[]{:S(2)}, u32[]{:S(2)}) collective-permute-start(bf16[256,1024]{1,0:T(8,128)(2,1)} %get-tuple-element.128), channel_id=1, source_target_pairs={{0,2},{2,0},{4,6},{6,4},{8,10},{10,8},{12,14},{14,12},{16,18},{18,... | collective-permute-start | bytes 1572872 | tf_op jit(solution)/shard_map/ppermute | solution.py:469
  176.9 29.8 %collective-permute-start.23 = (bf16[256,1024]{1,0:T(8,128)(2,1)}, bf16[256,1024]{1,0:T(8,128)(2,1)}, u32[]{:S(2)}, u32[]{:S(2)}) collective-permute-start(bf16[256,1024]{1,0:T(8,128)(2,1)} %get-tuple-element.126.refs_4_.refs_8_), channel_id=1, source_target_pairs={{0,4},{2,6},{4,0},{6,2},{8,12},{10,14},{12,8},{14,10},{16,20},{18,... | collective-permute-start | bytes 1572872 | tf_op jit(solution)/shard_map/ppermute | solution.py:469
  181.5 12.2 %copy-start.8 = (bf16[256,1024]{1,0:T(8,128)(2,1)S(1)}, bf16[256,1024]{1,0:T(8,128)(2,1)}, u32[]{:S(2)}) copy-start(bf16[256,1024]{1,0:T(8,128)(2,1)} %get-tuple-element.129) | copy-start | bytes 1572868
  193.7 19.6 %collective-permute-start.26 = (bf16[256,1024]{1,0:T(8,128)(2,1)S(1)}, bf16[256,1024]{1,0:T(8,128)(2,1)}, u32[]{:S(2)}, u32[]{:S(2)}) collective-permute-start(bf16[256,1024]{1,0:T(8,128)(2,1)S(1)} %copy-done.8), channel_id=1, source_target_pairs={{0,4},{2,6},{4,0},{6,2},{8,12},{10,14},{12,8},{14,10},{16,20},{18,... | collective-permute-start | bytes 1572872 | tf_op jit(solution)/shard_map/ppermute | solution.py:469
  213.2 0.8 copy-start.11
  213.3 1.0 copy-start.10
  214.2 15.3 %collective-permute-start.27 = (bf16[256,1024]{1,0:T(8,128)(2,1)}, bf16[256,1024]{1,0:T(8,128)(2,1)S(1)}, u32[]{:S(2)}, u32[]{:S(2)}) collective-permute-start(bf16[256,1024]{1,0:T(8,128)(2,1)} %get-tuple-element.130), channel_id=1, source_target_pairs={{0,2},{2,0},{4,6},{6,4},{8,10},{10,8},{12,14},{14,12},{16,18},{18,... | collective-permute-start | bytes 1572872 | tf_op jit(solution)/shard_map/ppermute | solution.py:469
  214.8 14.8 %collective-permute-start.28 = (bf16[256,1024]{1,0:T(8,128)(2,1)}, bf16[256,1024]{1,0:T(8,128)(2,1)S(1)}, u32[]{:S(2)}, u32[]{:S(2)}) collective-permute-start(bf16[256,1024]{1,0:T(8,128)(2,1)} %get-tuple-element.131.refs_4_.refs_9_), channel_id=1, source_target_pairs={{0,4},{2,6},{4,0},{6,2},{8,12},{10,14},{12,8},{14,10},{16,20},{18,... | collective-permute-start | bytes 1572872 | tf_op jit(solution)/shard_map/ppermute | solution.py:469
  215.3 11.5 %collective-permute-start.29 = (bf16[128,1024]{1,0:T(8,128)(2,1)}, bf16[128,1024]{1,0:T(8,128)(2,1)S(1)}, u32[]{:S(2)}, u32[]{:S(2)}) collective-permute-start(bf16[128,1024]{1,0:T(8,128)(2,1)} %get-tuple-element.134), channel_id=1, source_target_pairs={{0,2},{2,0},{4,6},{6,4},{8,10},{10,8},{12,14},{14,12},{16,18},{18,... | collective-permute-start | bytes 786440 | tf_op jit(solution)/shard_map/ppermute | solution.py:469
  229.5 0.8 copy-start.12
  229.6 1.0 copy-start.13
  230.6 7.2 %copy-start.31 = (s32[16]{0:T(128)S(1)}, s32[16]{0:T(128)}, u32[]{:S(2)}) copy-start(s32[16]{0:T(128)} %get-tuple-element.199) | copy-start | bytes 196
  237.1 6.6 %collective-permute-start.30 = (bf16[128,1024]{1,0:T(8,128)(2,1)}, bf16[128,1024]{1,0:T(8,128)(2,1)S(1)}, u32[]{:S(2)}, u32[]{:S(2)}) collective-permute-start(bf16[128,1024]{1,0:T(8,128)(2,1)} %get-tuple-element.141), channel_id=1, source_target_pairs={{0,2},{2,0},{4,6},{6,4},{8,10},{10,8},{12,14},{14,12},{16,18},{18,... | collective-permute-start | bytes 786440 | tf_op jit(solution)/shard_map/ppermute | solution.py:469
  246.6 10.0 %copy-start.27 = (bf16[128,1024]{1,0:T(8,128)(2,1)S(1)}, bf16[128,1024]{1,0:T(8,128)(2,1)}, u32[]{:S(2)}) copy-start(bf16[128,1024]{1,0:T(8,128)(2,1)} %get-tuple-element.135.refs_2_) | copy-start | bytes 786436
  246.6 11.6 %copy-start.18 = (bf16[128,1024]{1,0:T(8,128)(2,1)S(1)}, bf16[128,1024]{1,0:T(8,128)(2,1)}, u32[]{:S(2)}) copy-start(bf16[128,1024]{1,0:T(8,128)(2,1)} %get-tuple-element.142.refs_2_) | copy-start | bytes 786436
  256.5 70.1 %collective-permute-start.31 = (bf16[512,2048]{1,0:T(8,128)(2,1)}, bf16[512,2048]{1,0:T(8,128)(2,1)}, u32[]{:S(2)}, u32[]{:S(2)}) collective-permute-start(bf16[512,2048]{1,0:T(8,128)(2,1)} %get-tuple-element.146.refs_1_), channel_id=1, source_target_pairs={{0,1},{1,0},{2,3},{3,2},{4,5},{5,4},{6,7},{7,6},{8,9},{9,8},{10,11... | collective-permute-start | bytes 6291464 | tf_op jit(solution)/shard_map/ppermute | solution.py:469
  256.6 9.2 %collective-permute-start.36 = (bf16[128,1024]{1,0:T(8,128)(2,1)S(1)}, bf16[128,1024]{1,0:T(8,128)(2,1)S(1)}, u32[]{:S(2)}, u32[]{:S(2)}) collective-permute-start(bf16[128,1024]{1,0:T(8,128)(2,1)S(1)} %copy-done.27), channel_id=1, source_target_pairs={{0,4},{2,6},{4,0},{6,2},{8,12},{10,14},{12,8},{14,10},{16,20},{18,... | collective-permute-start | bytes 786440 | tf_op jit(solution)/shard_map/ppermute | solution.py:469
  258.2 12.8 %collective-permute-start.32 = (bf16[128,1024]{1,0:T(8,128)(2,1)S(1)}, bf16[128,1024]{1,0:T(8,128)(2,1)S(1)}, u32[]{:S(2)}, u32[]{:S(2)}) collective-permute-start(bf16[128,1024]{1,0:T(8,128)(2,1)S(1)} %copy-done.18), channel_id=1, source_target_pairs={{0,4},{2,6},{4,0},{6,2},{8,12},{10,14},{12,8},{14,10},{16,20},{18,... | collective-permute-start | bytes 786440 | tf_op jit(solution)/shard_map/ppermute | solution.py:469
  268.8 7.6 %collective-permute-start.37 = (bf16[128,1024]{1,0:T(8,128)(2,1)}, bf16[128,1024]{1,0:T(8,128)(2,1)S(1)}, u32[]{:S(2)}, u32[]{:S(2)}) collective-permute-start(bf16[128,1024]{1,0:T(8,128)(2,1)} %get-tuple-element.169), channel_id=1, source_target_pairs={{0,8},{2,10},{4,12},{6,14},{8,0},{10,2},{12,4},{14,6},{16,24},{18,... | collective-permute-start | bytes 786440 | tf_op jit(solution)/shard_map/ppermute | solution.py:469
  273.8 14.6 %collective-permute-start.33 = (bf16[128,1024]{1,0:T(8,128)(2,1)}, bf16[128,1024]{1,0:T(8,128)(2,1)S(1)}, u32[]{:S(2)}, u32[]{:S(2)}) collective-permute-start(bf16[128,1024]{1,0:T(8,128)(2,1)} %shard_map.135), channel_id=1, source_target_pairs={{0,8},{2,10},{4,12},{6,14},{8,0},{10,2},{12,4},{14,6},{16,24},{18,... | collective-permute-start | bytes 786440 | tf_op jit(solution)/shard_map/ppermute | solution.py:469
  279.3 24.8 %collective-permute-start.38 = (bf16[128,1024]{1,0:T(8,128)(2,1)}, bf16[128,1024]{1,0:T(8,128)(2,1)S(1)}, u32[]{:S(2)}, u32[]{:S(2)}) collective-permute-start(bf16[128,1024]{1,0:T(8,128)(2,1)} %get-tuple-element.172), channel_id=1, source_target_pairs={{0,16},{2,18},{4,20},{6,22},{8,24},{10,26},{12,28},{14,30},{16,0},... | collective-permute-start | bytes 786440 | tf_op jit(solution)/shard_map/ppermute | solution.py:469
  300.3 13.0 %collective-permute-start.35 = (bf16[128,1024]{1,0:T(8,128)(2,1)}, bf16[128,1024]{1,0:T(8,128)(2,1)S(1)}, u32[]{:S(2)}, u32[]{:S(2)}) collective-permute-start(bf16[128,1024]{1,0:T(8,128)(2,1)} %shard_map.141), channel_id=1, source_target_pairs={{0,16},{2,18},{4,20},{6,22},{8,24},{10,26},{12,28},{14,30},{16,0},... | collective-permute-start | bytes 786440 | tf_op jit(solution)/shard_map/ppermute | solution.py:469
  304.0 18.9 %collective-permute-start.34 = (bf16[512,128]{1,0:T(8,128)(2,1)S(1)}, bf16[512,128]{1,0:T(8,128)(2,1)S(1)}, u32[]{:S(2)}, u32[]{:S(2)}) collective-permute-start(bf16[512,128]{1,0:T(8,128)(2,1)S(1)} %convert_element_type.38), channel_id=1, source_target_pairs={{0,1},{1,0},{2,3},{3,2},{4,5},{5,4},{6,7},{7,6},{8,9},{9,8},{10,11... | collective-permute-start | bytes 393224 | tf_op jit(solution)/shard_map/ppermute | solution.py:469
  316.2 6.6 %copy-start.7 = (f32[512,128]{1,0:T(8,128)S(1)}, f32[512,128]{1,0:T(8,128)}, u32[]{:S(2)}) copy-start(f32[512,128]{1,0:T(8,128)} %get-tuple-element.159.refs_1_) | copy-start | bytes 786436
  316.2 7.4 %copy-start.28 = (f32[16,512]{1,0:T(8,128)S(1)}, f32[16,512]{1,0:T(8,128)}, u32[]{:S(2)}) copy-start(f32[16,512]{1,0:T(8,128)} %get-tuple-element.180) | copy-start | bytes 98308
  322.8 2.2 collective-permute-start.39
  (8 other events, 5.6 us)

commit v6 on v5

--- a/solution.py
+++ b/solution.py
@@ -224,13 +224,15 @@
 
 
 def scan_kernel(factor_ref, total_ref, got_ref, *refs):
-    entering_ref = refs[0] if len(refs) == 4 else None
-    total_out, entering_out, sent_out = refs[-3:]
+    refs = list(refs)
+    entering_ref = refs.pop(0) if len(refs) % 2 == 0 else None
     factors = factor_ref[...]
     got = got_ref[...].astype(F32)
-    total = factors[0:1] * total_ref[...] + factors[1:2] * got
-    total_out[...] = total
-    sent_out[...] = total.astype(BF16)
+    entering_out = refs[0]
+    if len(refs) == 3:
+        total = factors[0:1] * total_ref[...] + factors[1:2] * got
+        refs[1][...] = total
+        refs[2][...] = total.astype(BF16)
     passed = factors[2:3] * got
     entering_out[...] = passed if entering_ref is None else entering_ref[...] + passed
 
@@ -387,8 +389,9 @@
 
 
 def state_kernel(
-    rt_ref, g_ref, c_ref, s_ref, e_ref, q_ref, a_ref, d_part_ref, c_part_ref, d_ref, grad_c_ref, held
+    rt_ref, g_ref, c_ref, s_ref, e_ref, q_ref, a_ref, d_part_ref, c_part_ref, *refs
 ):
+    d_ref, grad_c_ref, held = refs[-3:]
     span, group = pl.program_id(0), pl.program_id(1)
 
     @pl.when(group == 0)
@@ -755,20 +758,22 @@
     )(place, log, total, got, *entering)
 
 
-def scan_step(factors, here, total, sent, entering, bit):
+def scan_step(factors, here, total, sent, entering, bit, last=False):
     got = swap(sent, "ctx", bit)
     n, columns = total.shape
     block = pl.BlockSpec((n, WIDE), lambda h: (0, h))
-    return call(
+    outs = [shape(n, columns), shape(n, columns), shape(n, columns, dtype=BF16)]
+    outs = outs[:1] if last else outs
+    out = call(
         scan_kernel,
         (columns // WIDE,),
-        [pl.BlockSpec((8, WIDE), lambda h: (0, h + here)), block, block]
-        + [block] * len(entering),
-        [block, block, block],
-        [shape(n, columns), shape(n, columns), shape(n, columns, dtype=BF16)],
+        [pl.BlockSpec((8, WIDE), lambda h: (0, h + here)), block, block] + [block] * len(entering),
+        [block] * len(outs),
+        outs,
         0,
         14 * n * columns,
     )(factors, total, got, *entering)
+    return out if last else (out[1], out[0], out[2])
 
 
 def local(inputs, w_in, b_rows, c_rows, log_decay, skip_gain, grad_out):
@@ -825,13 +830,16 @@
     )(*operands, *so_far)
 
 
-def state_terms(grid, here, wide, operands):
+def state_terms(grid, here, wide, operands, heads=None, so_far=None):
     length = operands[1].shape[0]
     n = operands[2].shape[1]
-    return call(
+    heads = heads or wide // P_SIZE
+    at = here if heads > wide // P_SIZE else 0
+    extra = () if so_far is None else (so_far,)
+    return pl.pallas_call(
         state_kernel,
-        grid,
-        [
+        grid=grid,
+        in_specs=[
             run_t_spec(here),
             rows_spec(here),
             SHARED,
@@ -841,13 +849,19 @@
             kept_spec(here),
             run_spec(),
             SHARED,
-        ],
-        [run_spec(), SHARED],
-        [shape(wide // P_SIZE, length), shape(length, n)],
-        4 * length * wide * n,
-        6 * length * wide,
-        [pltpu.VMEM((grid[1], n, WIDE), F32)],
-    )(*operands)
+        ]
+        + [ANYWHERE] * len(extra),
+        out_specs=[run_spec(at), SHARED],
+        out_shape=[shape(heads, length), shape(length, n)],
+        scratch_shapes=[pltpu.VMEM((grid[1], n, WIDE), F32)],
+        input_output_aliases={len(operands): 0} if extra else {},
+        cost_estimate=pl.CostEstimate(
+            flops=4 * length * wide * n, bytes_accessed=6 * length * wide, transcendentals=0
+        ),
+        compiler_params=pltpu.CompilerParams(
+            dimension_semantics=("arbitrary", "arbitrary"), vmem_limit_bytes=GRANT
+        ),
+    )(*operands, *extra)
 
 
 def local_layered(inputs, w_in, b_rows, c_rows, log_decay, skip_gain, grad_out):
@@ -871,14 +885,10 @@
     sent = after([sent], other)[0]
     back, leaving, sent, log, factors_1 = back_step(spot, log, back, sent, (), 1)
 
-    up1, down1 = after([up1, down1], own_x, own_y)
+    up1, down1, sent = after([up1, down1, sent], own_x, own_y)
     up2, down2 = along_z(up1, 1), along_z(down1, -1)
     z1 = jnp.where(layer == 0, down1, up1)
     x1, y1 = swap_x(z1), swap_y(z1)
-    z3 = jnp.where(layer == 0, down2, jnp.where(layer == 3, up2, down1))
-    up2, down2, z3 = after([up2, down2, z3], sent)
-    up3, down3 = along_z(up2, 1), along_z(down2, -1)
-    x3, y3 = swap_x(z3), swap_y(z3)
     back, leaving, sent, log, factors_2 = back_step(spot, log, back, sent, (leaving,), 2)
     order_own = (order + place * (blocks // 2)) % blocks
     cut = len(EARLY) * w_in.shape[0]
@@ -893,89 +903,87 @@
         [pltpu.VMEM((length, width), BF16)],
     )(order_own, inputs, other)
 
+    up2, down2, down1, sent = after([up2, down2, down1, sent], x1, y1, early_features)
+    z3 = jnp.where(layer == 0, down2, jnp.where(layer == 3, up2, down1))
+    up3, down3 = along_z(up2, 1), along_z(down2, -1)
+    x3, y3 = swap_x(z3), swap_y(z3)
+    back, leaving, sent, log, factors_4 = back_step(spot, log, back, sent, (leaving,), 4)
     z2 = jnp.where(layer == 1, down2, jnp.where(layer == 2, up2, up3 + down3))
     z2a, z2b = z2[:, :half], z2[:, half:]
-    z2a, x1, y3, own_y = after(
-        [z2a, x1, y3, own_y], y1, x3, z2b, sent, early_features, late_features
-    )
+
+    z2a, x1, y3, own_y, sent = after([z2a, x1, y3, own_y, sent], x3, z2b)
     x1_a, x1_b = x1[:, :half], x1[:, half:]
     y3_a, y3_b = y3[:, :half], y3[:, half:]
     own_y_a, own_y_b = own_y[:, :half], own_y[:, half:]
     x2a, y2a = swap_x(z2a), swap_y(z2a)
     d3a, d1a = swap_x(y3_a), swap_y(x1_a)
-    back, leaving, sent, log, factors_4 = back_step(spot, log, back, sent, (leaving,), 4)
+    back, leaving, sent, log, factors_8 = back_step(spot, log, back, sent, (leaving,), 8)
     early = [w_in, own_x, own_y, z1, x1, y1, z3, x3, y3]
     part = early_forward(early_features, early)
 
-    own_y_a, x2a, z2b, y3_b, x1_b = after(
-        [own_y_a, x2a, z2b, y3_b, x1_b], y2a, d3a, d1a, part, sent
+    own_y_a, x2a, z2b, y3_b, x1_b, leaving = after(
+        [own_y_a, x2a, z2b, y3_b, x1_b, leaving], y2a, d3a, d1a, part
     )
     d0a, d2a = swap_x(own_y_a), swap_y(x2a)
     x2b, y2b = swap_x(z2b), swap_y(z2b)
     d3b, d1b = swap_x(y3_b), swap_y(x1_b)
-    back, leaving, sent, log, factors_8 = back_step(spot, log, back, sent, (leaving,), 8)
     leaving_all = [leaving]
     for k in range(spans - 1, 0, -1):
         leaving_all.insert(0, own_grads[k] + kept[k, :1] * leaving_all[0])
     leaving_all = jnp.stack([value.astype(BF16) for value in leaving_all])
     skip = jnp.repeat(skip_gain, P_SIZE)[None]
     grad_x = grad_rows(running, running_t, grad_out, b_rows, c_rows, leaving_all, skip, True)
+    order_away = (order + (1 - place) * (blocks // 2)) % blocks
+    early_order, late_order = order_away[: len(EARLY)], order_away[len(EARLY) :]
+    product = multiply_blocks(early_order, grad_x, [[piece] for piece in early], ())
     late_a = [d0a, d1a, d3a, z2a, x2a, y2a, d2a]
     x_a, states_a, total_a, sent_a = late_forward(
         late_features, part, late_a, running_t, b_rows, kept, 0
     )
 
-    own_y_b, x2b, sent_a = after([own_y_b, x2b, sent_a], y2b, d3b, d1b, grad_x)
+    own_y_b, x2b, sent_a, x_a = after(
+        [own_y_b, x2b, sent_a, x_a], y2b, d3b, d1b, product[0]
+    )
     d0b, d2b = swap_x(own_y_b), swap_y(x2b)
     total_a, entering_a, sent_a = scan_step(factors_1, 0, total_a, sent_a, (), 1)
-    order_away = (order + (1 - place) * (blocks // 2)) % blocks
-    early_order, late_order = order_away[: len(EARLY)], order_away[len(EARLY) :]
-    product = multiply_blocks(early_order, grad_x, [[piece] for piece in early], ())
-
-    d0b, d2b = after([d0b, d2b], sent_a, product[0])
+    shared = (running, running_t, grad_out)
+    here = groups // 2
+    grid = (spans, here)
+    inner_a = shared + (x_a, b_rows, c_rows, leaving_all)
+    decay_a, grad_b, grad_c = inner(grid, 0, half, inner_a, ())
+
+    d0b, d2b = after([d0b, d2b], sent_a, grad_b)
     late_b = [d0b, d1b, d3b, z2b, x2b, y2b, d2b]
-    here = groups // 2
     x_b, states_b, total_b, sent_b = late_forward(
         late_features, part, late_b, running_t, b_rows, kept, here
     )
     pairs = list(zip(late_a, late_b))
-    shared = (running, running_t, grad_out)
-    grid = (spans, here)
-    entering_b = ()
-    for factors, bit in ((factors_1, 1), (factors_2, 2), (factors_4, 4), (factors_8, 8)):
-        if bit > 1:
-            total_a, entering_a, sent_a = scan_step(
-                factors, 0, total_a, sent_a, (entering_a,), bit
-            )
-        if bit == 4:
-            sent_b = after([sent_b], away)[0]
-        if bit == 8:
-            sent_b = after([sent_b], grad_b)[0]
-        total_b, entering_b, sent_b = scan_step(factors, here, total_b, sent_b, entering_b, bit)
-        entering_b = (entering_b,)
-        if bit == 1:
-            product = after(list(product), sent_b)
-            away, own = multiply_blocks(late_order, grad_x, pairs, product)
-            got = swap(away, "head", 1)
-        if bit == 2:
-            x_a = after([x_a], sent_b)[0]
-            inner_a = shared + (x_a, b_rows, c_rows, leaving_all)
-            decay_a, grad_b, grad_c = inner(grid, 0, half, inner_a, ())
-        if bit == 4:
-            x_b = after([x_b], sent_b)[0]
-            inner_b = shared + (x_b, b_rows, c_rows, leaving_all)
-            decay_b, grad_b, grad_c = inner(grid, here, half, inner_b, (grad_b, grad_c))
-    entering_b = entering_b[0]
+    sent_a, sent_b, *product = after([sent_a, sent_b, *product])
+    total_b, entering_b, sent_b = scan_step(factors_1, here, total_b, sent_b, (), 1)
+    total_a, entering_a, sent_a = scan_step(factors_2, 0, total_a, sent_a, (entering_a,), 2)
+    away, own = multiply_blocks(late_order, grad_x, pairs, product)
+
+    sent_a, sent_b, x_b, away = after([sent_a, sent_b, x_b, away])
+    total_b, entering_b, sent_b = scan_step(factors_2, here, total_b, sent_b, (entering_b,), 2)
+    total_a, entering_a, sent_a = scan_step(factors_4, 0, total_a, sent_a, (entering_a,), 4)
+    got = swap(away, "head", 1)
+    inner_b = shared + (x_b, b_rows, c_rows, leaving_all)
+    decay_b, grad_b, grad_c = inner(grid, here, half, inner_b, (grad_b, grad_c))
+
+    sent_a, sent_b, got, grad_b = after([sent_a, sent_b, got, grad_b])
+    total_b, entering_b, sent_b = scan_step(factors_4, here, total_b, sent_b, (entering_b,), 4)
+    (entering_a,) = scan_step(factors_8, 0, total_a, sent_a, (entering_a,), 8, True)
+    grad_inputs = (own.astype(F32) + got.astype(F32)).astype(BF16)
     grad_b = head_sum(grad_b)
 
+    sent_b, entering_a = after([sent_b, entering_a], grad_inputs, grad_b)
+    (entering_b,) = scan_step(factors_8, here, total_b, sent_b, (entering_b,), 8, True)
     common = (running_t, grad_out, c_rows)
     state_a = common + (entering_a, states_a, leaving_all, kept, decay_a, grad_c)
-    decay_a, grad_c = state_terms(grid, 0, half, state_a)
+    decays, grad_c = state_terms(grid, 0, half, state_a, heads)
     state_b = common + (entering_b, states_b, leaving_all, kept, decay_b, grad_c)
-    decay_b, grad_c = state_terms(grid, here, half, state_b)
-    grad_inputs = (own.astype(F32) + got.astype(F32)).astype(BF16)
-    grad_log_decay = jnp.concatenate([decay_a, decay_b], axis=0)
-    return (grad_inputs, grad_b, head_sum(grad_c), grad_log_decay)
+    decays, grad_c = state_terms(grid, here, half, state_b, heads, decays)
+    return (grad_inputs, grad_b, head_sum(grad_c), decays)
 
 
 def grad_rows(running, running_t, grad_out, b_rows, c_rows, leaving, skip, transposed):

time: 333 us -> 332 us (level)
  waiting for transfers between devices: 105 us -> 96.4 us
  starting transfers between devices: 49.7 us -> 56 us
  local copies, waits for them, and re-layouts: 19.9 us -> 23.4 us
    ppermute x34, waiting for transfers between devices: 85.4 us -> 72.2 us  [swap(): return lax.ppermute(value, axis, [(i, i ^ bit) for i in range(count)])]
    ppermute x34, starting transfers between devices: 31.2 us -> 38.6 us  [swap(): return lax.ppermute(value, axis, [(i, i ^ bit) for i in range(count)])]
    ppermute x6, waiting for transfers between devices: 19.9 us -> 24.2 us  [along_z(): return lax.ppermute(value, 'ctx', pairs)]
    unnamed x64 -> x58, local copies, waits for them, and re-layouts: 10.2 us -> 11.2 us
  transfers between devices with their start and end apart: 40 -> 40, of which waited for: 18 -> 13; matrix products, arithmetic and copies ran while one was open for 7% -> 6% of each run, Pallas kernels for 34% -> 35%
where the time goes in v6:
time: 332 us; the launch traced here: 331 us
  Pallas kernels  134 us (40%)
  waiting for transfers between devices  96.4 us (29%)
  starting transfers between devices  56 us (17%)
  local copies, waits for them, and re-layouts  23.4 us (7%)
  other arithmetic  17.4 us (5%)
  between operations  3.56 us (1%)
    ppermute x34, waiting for transfers between devices, swap(): return lax.ppermute(value, axis, [(i, i ^ bit) for i in range(count)])  72.2 us
    ppermute x34, starting transfers between devices, swap(): return lax.ppermute(value, axis, [(i, i ^ bit) for i in range(count)])  38.6 us
    ppermute x6, waiting for transfers between devices, along_z(): return lax.ppermute(value, 'ctx', pairs)  24.2 us
    pallas_call x2, Pallas kernels, multiply_blocks(): pl.pallas_call(functools.partial(blocks_kernel, [len(piece) for piece in...  19.8 us
    pallas_call x2, Pallas kernels, inner(): call(inner_kernel, grid, specs + [SHARED] * len(so_far), [run_spec(), SHA...  17.9 us
    ppermute x6, starting transfers between devices, along_z(): return lax.ppermute(value, 'ctx', pairs)  17.5 us
    pallas_call x8, Pallas kernels, scan_step(): call(scan_kernel, (columns // WIDE,), [pl.BlockSpec((8, WIDE), lambda h:...  17.4 us
    pallas_call x4, Pallas kernels, back_step(): call(functools.partial(back_kernel, bit), (columns // WIDE,), [SCALARS] +...  16 us
  transfers between devices with their start and end apart: 40, of which 13 were waited for; matrix products, arithmetic and copies ran while one was open for 6% of the time, Pallas kernels for 35%

profile of v6, /device:TPU:0, one launch (start us, length us, event | category | flops | bytes accessed | tf_op | source)
XLA Modules:
  0.0 330.5 jit_solution(2236021412088151235)
XLA Ops:
  1.1 2.6 collective-permute-start.4
  3.7 1.5 collective-permute-start.5
  5.2 4.5 %collective-permute-start = (bf16[256,2048]{1,0:T(8,128)(2,1)}, bf16[256,2048]{1,0:T(8,128)(2,1)}, u32[]{:S(2)}, u32[]{:S(2)}) collective-permute-start(bf16[256,2048]{1,0:T(8,128)(2,1)} %refs_0_.3), channel_id=1, source_target_pairs={{0,8},{2,10},{4,12},{6,14},{8,16},{10,18},{12,20},{14,22},{16,24},... | collective-permute-start | bytes 3145736 | tf_op jit(solution)/shard_map/ppermute | solution.py:533
  11.0 9.1 %shard_map.111 = (f32[32,512]{1,0:T(8,128)}, f32[4,512,8]{2,1,0:T(8,128)}, f32[2,8,2048]{2,1,0:T(8,128)}, f32[2,128,2048]{2,1,0:T(8,128)}) custom-call(f32[32,512]{1,0:T(8,128)} %d_ref.1, bf16[512,2048]{1,0:T(8,128)(2,1)} %g_ref.11, bf16[512,128]{1,0:T(8,128)(2,1)} %c_ref.11), custom_call_target="tpu_custom_call" | custom-call | flops 268435456 | bytes 6291456 | tf_op jit(solution)/shard_map/pallas_call | solution.py:793
  20.1 3.7 %shard_map.112 = (f32[128,2048]{1,0:T(8,128)}, f32[8,2048]{1,0:T(8,128)}, bf16[144,2048]{1,0:T(8,128)(2,1)}) custom-call(f32[2,128,2048]{2,1,0:T(8,128)} %get-tuple-element.110.own_ref, f32[2,8,2048]{2,1,0:T(8,128)} %get-tuple-element.111.kept_ref.a_ref), custom_call_target="tpu_custom_call" | custom-call | bytes 3670016 | tf_op jit(solution)/shard_map/pallas_call | solution.py:726
  24.5 15.9 %collective-permute-done.3.got_ref = bf16[144,2048]{1,0:T(8,128)(2,1)S(1)} collective-permute-done((bf16[144,2048]{1,0:T(8,128)(2,1)}, bf16[144,2048]{1,0:T(8,128)(2,1)S(1)}, u32[]{:S(2)}, u32[]{:S(2)}) %collective-permute-start.3) | collective-permute-done | bytes 589856 | tf_op jit(solution)/shard_map/ppermute | solution.py:472
  41.1 3.9 %shard_map.114 = (f32[128,2048]{1,0:T(8,128)}, f32[128,2048]{1,0:T(8,128)}, bf16[144,2048]{1,0:T(8,128)(2,1)}, f32[8,2048]{1,0:T(8,128)}, f32[8,2048]{1,0:T(8,128)}) custom-call(s32[1]{0:T(128)} %bitcast.22.place_ref, f32[8,2048]{1,0:T(8,128)} %get-tuple-element.112.log_ref, f32[128,2048]{1,0:T(8,128)} %get-tuple-element.113.total_ref, ...), custom_call_target="tpu_custom_call" | custom-call | bytes 4718592 | tf_op jit(solution)/shard_map/pallas_call | solution.py:744
  46.0 2.4 broadcast_select_fusion.refs_3_
  48.4 1.8 collective-permute-start.10
  50.2 1.5 collective-permute-start.9
  53.0 5.5 %collective-permute-start.6 = (bf16[256,2048]{1,0:T(8,128)(2,1)}, bf16[256,2048]{1,0:T(8,128)(2,1)}, u32[]{:S(2)}, u32[]{:S(2)}) collective-permute-start(bf16[256,2048]{1,0:T(8,128)(2,1)} %get-tuple-element.116), channel_id=1, source_target_pairs={{0,8},{2,10},{4,12},{6,14},{8,16},{10,18},{12,20},{14,22},{16,24},... | collective-permute-start | bytes 3145736 | tf_op jit(solution)/shard_map/ppermute | solution.py:533
  62.8 5.1 %shard_map.117 = (bf16[512,2304]{1,0:T(8,128)(2,1)}, bf16[512,1792]{1,0:T(8,128)(2,1)}) custom-call(s32[16]{0:T(128)} %get-tuple-element.229.order_ref, bf16[512,2048]{1,0:T(8,128)(2,1)} %own_ref.1, bf16[512,2048]{1,0:T(8,128)(2,1)} %collective-permute-done.2.refs_1_.other_ref), custom_call_target="tpu_custom_call" | custom-call | bytes 8388608 | tf_op jit(solution)/shard_map/pallas_call | solution.py:895
  67.9 18.4 %collective-permute-done.8.got_ref = bf16[144,2048]{1,0:T(8,128)(2,1)} collective-permute-done((bf16[144,2048]{1,0:T(8,128)(2,1)S(1)}, bf16[144,2048]{1,0:T(8,128)(2,1)}, u32[]{:S(2)}, u32[]{:S(2)}) %collective-permute-start.8) | collective-permute-done | bytes 589856 | tf_op jit(solution)/shard_map/ppermute | solution.py:472
  86.3 4.0 %shard_map.116 = (f32[128,2048]{1,0:T(8,128)}, f32[128,2048]{1,0:T(8,128)}, bf16[144,2048]{1,0:T(8,128)(2,1)}, f32[8,2048]{1,0:T(8,128)}, f32[8,2048]{1,0:T(8,128)}) custom-call(s32[1]{0:T(128)} %bitcast.22.place_ref, f32[8,2048]{1,0:T(8,128)} %get-tuple-element.118.log_ref, f32[128,2048]{1,0:T(8,128)} %get-tuple-element.119.total_ref, ...), custom_call_target="tpu_custom_call" | custom-call | bytes 4718592 | tf_op jit(solution)/shard_map/pallas_call | solution.py:744
  90.4 3.4 %collective-permute-start.11 = (bf16[256,2048]{1,0:T(8,128)(2,1)}, bf16[256,2048]{1,0:T(8,128)(2,1)S(1)}, u32[]{:S(2)}, u32[]{:S(2)}) collective-permute-start(bf16[256,2048]{1,0:T(8,128)(2,1)} %get-tuple-element.125), channel_id=1, source_target_pairs={{0,8},{2,10},{4,12},{6,14},{8,16},{10,18},{12,20},{14,22},{16,24},... | collective-permute-start | bytes 3145736 | tf_op jit(solution)/shard_map/ppermute | solution.py:533
  95.3 19.8 %collective-permute-done.11 = bf16[256,2048]{1,0:T(8,128)(2,1)S(1)} collective-permute-done((bf16[256,2048]{1,0:T(8,128)(2,1)}, bf16[256,2048]{1,0:T(8,128)(2,1)S(1)}, u32[]{:S(2)}, u32[]{:S(2)}) %collective-permute-start.11) | collective-permute-done | bytes 1048608 | tf_op jit(solution)/shard_map/ppermute | solution.py:533
  115.1 4.3 %collective-permute-done.12 = bf16[256,2048]{1,0:T(8,128)(2,1)S(1)} collective-permute-done((bf16[256,2048]{1,0:T(8,128)(2,1)}, bf16[256,2048]{1,0:T(8,128)(2,1)S(1)}, u32[]{:S(2)}, u32[]{:S(2)}) %collective-permute-start.12) | collective-permute-done | bytes 1048608 | tf_op jit(solution)/shard_map/ppermute | solution.py:533
  119.4 3.6 %select_select_fusion = (bf16[256,2048]{1,0:T(8,128)(2,1)}, bf16[256,2048]{1,0:T(8,128)(2,1)}) fusion(bf16[256,2048]{1,0:T(8,128)(2,1)} %get-tuple-element.124, bf16[256,2048]{1,0:T(8,128)(2,1)} %get-tuple-element.125, bf16[256,2048]{1,0:T(8,128)(2,1)} %get-tuple-element.126, pred[]{:T(512)S(6)} %eq.21, pred[]{:T(512)S(6)} %eq.19, ...), kind=kLoop, calls=%fused_computation.4 | loop fusion | flops 2621440 | bytes 7340036 | tf_op jit(solution)/shard_map/jit(_where)/select_n | solution.py:907
  123.0 1.7 collective-permute-start.13
  124.7 1.5 collective-permute-start.15
  126.2 1.5 collective-permute-start.14
  129.3 9.1 %collective-permute-done.14.got_ref = bf16[144,2048]{1,0:T(8,128)(2,1)S(1)} collective-permute-done((bf16[144,2048]{1,0:T(8,128)(2,1)S(1)}, bf16[144,2048]{1,0:T(8,128)(2,1)S(1)}, u32[]{:S(2)}, u32[]{:S(2)}) %collective-permute-start.14) | collective-permute-done | bytes 589856 | tf_op jit(solution)/shard_map/ppermute | solution.py:472
  139.3 4.1 %shard_map.119 = (f32[128,2048]{1,0:T(8,128)}, f32[128,2048]{1,0:T(8,128)}, bf16[144,2048]{1,0:T(8,128)(2,1)}, f32[8,2048]{1,0:T(8,128)}, f32[8,2048]{1,0:T(8,128)}) custom-call(s32[1]{0:T(128)} %bitcast.22.place_ref, f32[8,2048]{1,0:T(8,128)} %get-tuple-element.127.log_ref, f32[128,2048]{1,0:T(8,128)} %get-tuple-element.128.total_ref, ...), custom_call_target="tpu_custom_call" | custom-call | bytes 4718592 | tf_op jit(solution)/shard_map/pallas_call | solution.py:744
  143.3 2.2 fusion.7
  145.8 2.2 collective-permute-done.15.refs_5_.refs_7_
  150.1 2.5 collective-permute-start.17
  152.6 2.3 fusion.6
  155.4 2.3 fusion.5
  157.7 1.5 collective-permute-start.20
  159.2 2.3 fusion.4
  161.5 10.2 %shard_map.122.refs_9_.part_ref = f32[512,2048]{1,0:T(8,128)} custom-call(bf16[512,2304]{1,0:T(8,128)(2,1)} %get-tuple-element.123.refs_6_.f_ref, bf16[256,2048]{1,0:T(8,128)(2,1)} %refs_0_.3, bf16[256,2048]{1,0:T(8,128)(2,1)} %collective-permute-done.4.refs_3_.refs_1_, bf16[256,2048]{1,0:T(8,128)(2,1)} %get-tuple-element.132.refs_2_, ...), custom_call_target="tpu_custom_call" | custom-call | flops 4831838208 | bytes 9437184 | tf_op jit(solution)/shard_map/pallas_call | solution.py:643
  171.7 3.6 %collective-permute-done.17.got_ref = bf16[144,2048]{1,0:T(8,128)(2,1)} collective-permute-done((bf16[144,2048]{1,0:T(8,128)(2,1)}, bf16[144,2048]{1,0:T(8,128)(2,1)}, u32[]{:S(2)}, u32[]{:S(2)}) %collective-permute-start.17) | collective-permute-done | bytes 589856 | tf_op jit(solution)/shard_map/ppermute | solution.py:472
  175.3 4.1 %shard_map.121 = (f32[128,2048]{1,0:T(8,128)}, f32[128,2048]{1,0:T(8,128)}, bf16[144,2048]{1,0:T(8,128)(2,1)}, f32[8,2048]{1,0:T(8,128)}, f32[8,2048]{1,0:T(8,128)}) custom-call(s32[1]{0:T(128)} %bitcast.22.place_ref, f32[8,2048]{1,0:T(8,128)} %get-tuple-element.136.log_ref, f32[128,2048]{1,0:T(8,128)} %get-tuple-element.137.total_ref, ...), custom_call_target="tpu_custom_call" | custom-call | bytes 4718592 | tf_op jit(solution)/shard_map/pallas_call | solution.py:744
  181.6 1.5 collective-permute-start.21
  183.1 1.5 collective-permute-start.23
  185.1 1.8 fusion.1
  188.0 10.4 %shard_map.124.g_ref = bf16[2048,512]{1,0:T(8,128)(2,1)} custom-call(f32[32,512]{1,0:T(8,128)} %get-tuple-element.108.r_ref, f32[4,512,8]{2,1,0:T(8,128)} %get-tuple-element.109.rt_ref, bf16[512,2048]{1,0:T(8,128)(2,1)} %g_ref.11, bf16[512,128]{1,0:T(8,128)(2,1)} %b_ref.9, bf16[512,128]{1,0:T(8,128)(2,1)} %c_ref.11, ...), custom_call_target="tpu_custom_call" | custom-call | flops 2147483648 | bytes 6291456 | tf_op jit(solution)/shard_map/pallas_call | solution.py:994
  198.4 8.6 %collective-permute-done.21.refs_0_ = bf16[256,1024]{1,0:T(8,128)(2,1)} collective-permute-done((bf16[256,1024]{1,0:T(8,128)(2,1)}, bf16[256,1024]{1,0:T(8,128)(2,1)}, u32[]{:S(2)}, u32[]{:S(2)}) %collective-permute-start.21) | collective-permute-done | bytes 524320 | tf_op jit(solution)/shard_map/ppermute | solution.py:472
  207.5 10.0 %shard_map.126 = (bf16[512,2048]{1,0:T(8,128)(2,1)}, bf16[512,2048]{1,0:T(8,128)(2,1)}) custom-call(s32[9]{0:T(128)} %bitcast.34, bf16[2048,512]{1,0:T(8,128)(2,1)} %shard_map.124.g_ref, bf16[256,2048]{1,0:T(8,128)(2,1)} %refs_0_.3, bf16[256,2048]{1,0:T(8,128)(2,1)} %collective-permute-done.4.refs_3_.refs_1_, bf16[256,2048]{1,0:T(8,128)(2,1)} %get-tuple-element.132.refs_2_, ...), custom_call_target="tpu_custom_call" | custom-call | flops 4831838208 | bytes 9437184 | tf_op jit(solution)/shard_map/pallas_call | solution.py:699
  217.5 6.6 %shard_map.125 = (bf16[512,1024]{1,0:T(8,128)(2,1)}, f32[2,128,1024]{2,1,0:T(8,128)}, f32[128,1024]{1,0:T(8,128)}, bf16[128,1024]{1,0:T(8,128)(2,1)}) custom-call(bf16[512,1792]{1,0:T(8,128)(2,1)} %get-tuple-element.144.f_ref, f32[512,2048]{1,0:T(8,128)} %shard_map.122.refs_9_.part_ref, f32[4,512,8]{2,1,0:T(8,128)} %get-tuple-element.109.rt_ref, ...), custom_call_target="tpu_custom_call" | custom-call | flops 1879048192 | bytes 3670016 | tf_op jit(solution)/shard_map/pallas_call | solution.py:663
  225.6 1.5 collective-permute-start.28
  227.1 1.5 collective-permute-start.29
  229.3 8.8 %shard_map.129 = (f32[16,512]{1,0:T(8,128)}, f32[512,128]{1,0:T(8,128)}, f32[512,128]{1,0:T(8,128)}) custom-call(f32[32,512]{1,0:T(8,128)} %get-tuple-element.108.r_ref, f32[4,512,8]{2,1,0:T(8,128)} %get-tuple-element.109.rt_ref, bf16[512,2048]{1,0:T(8,128)(2,1)} %g_ref.11, bf16[512,1024]{1,0:T(8,128)(2,1)} %get-tuple-element.157.x_ref, ...), custom_call_target="tpu_custom_call" | custom-call | flops 1610612736 | bytes 3145728 | tf_op jit(solution)/shard_map/pallas_call | solution.py:821
  238.1 2.4 collective-permute-done.29.got_ref
  241.2 2.1 shard_map.128
  244.3 6.5 %shard_map.131 = (bf16[512,1024]{1,0:T(8,128)(2,1)}, f32[2,128,1024]{2,1,0:T(8,128)}, f32[128,1024]{1,0:T(8,128)}, bf16[128,1024]{1,0:T(8,128)(2,1)}) custom-call(bf16[512,1792]{1,0:T(8,128)(2,1)} %get-tuple-element.144.f_ref, f32[512,2048]{1,0:T(8,128)} %shard_map.122.refs_9_.part_ref, f32[4,512,8]{2,1,0:T(8,128)} %get-tuple-element.109.rt_ref, ...), custom_call_target="tpu_custom_call" | custom-call | flops 1879048192 | bytes 3670016 | tf_op jit(solution)/shard_map/pallas_call | solution.py:663
  251.3 1.7 collective-permute-start.30
  253.0 9.8 %shard_map.133 = (bf16[512,2048]{1,0:T(8,128)(2,1)}, bf16[512,2048]{1,0:T(8,128)(2,1)}) custom-call(s32[7]{0:T(128)} %slice.68.order_ref, bf16[2048,512]{1,0:T(8,128)(2,1)} %shard_map.124.g_ref, bf16[256,1024]{1,0:T(8,128)(2,1)} %collective-permute-done.21.refs_0_, ...), custom_call_target="tpu_custom_call", output_to_operand_aliasing={{0}: (16, {}), {1}: (17, {})} | custom-call | flops 3758096384 | bytes 7340032 | tf_op jit(solution)/shard_map/pallas_call | solution.py:699
  263.5 2.1 shard_map.135
  266.4 2.2 shard_map.134
  269.1 9.0 %shard_map.139 = (f32[16,512]{1,0:T(8,128)}, f32[512,128]{1,0:T(8,128)}, f32[512,128]{1,0:T(8,128)}) custom-call(f32[32,512]{1,0:T(8,128)} %get-tuple-element.108.r_ref, f32[4,512,8]{2,1,0:T(8,128)} %get-tuple-element.109.rt_ref, bf16[512,2048]{1,0:T(8,128)(2,1)} %g_ref.11, bf16[512,1024]{1,0:T(8,128)(2,1)} %get-tuple-element.186.x_ref, ...), custom_call_target="tpu_custom_call" | custom-call | flops 1610612736 | bytes 3145728 | tf_op jit(solution)/shard_map/pallas_call | solution.py:821
  278.8 2.2 shard_map.138
  281.8 2.3 shard_map.137
  284.4 1.9 collective-permute-start.36
  287.3 3.7 %add_convert_fusion.refs_2_ = bf16[512,2048]{1,0:T(8,128)(2,1)} fusion(bf16[512,2048]{1,0:T(8,128)(2,1)} %get-tuple-element.189, bf16[512,2048]{1,0:T(8,128)(2,1)S(1)} %copy-done.2), kind=kLoop, calls=%fused_computation | loop fusion | flops 4194304 | bytes 6291456 | tf_op jit(solution)/shard_map/convert_element_type | solution.py:976
  291.8 4.5 %collective-permute-done.36.got_ref = bf16[128,1024]{1,0:T(8,128)(2,1)S(1)} collective-permute-done((bf16[128,1024]{1,0:T(8,128)(2,1)}, bf16[128,1024]{1,0:T(8,128)(2,1)S(1)}, u32[]{:S(2)}, u32[]{:S(2)}) %collective-permute-start.36) | collective-permute-done | bytes 262176 | tf_op jit(solution)/shard_map/ppermute | solution.py:472
  297.0 2.3 shard_map.141
  300.0 2.1 shard_map.142.refs_1_
  302.1 4.7 %collective-permute-start.38 = (bf16[128,1024]{1,0:T(8,128)(2,1)}, bf16[128,1024]{1,0:T(8,128)(2,1)S(1)}, u32[]{:S(2)}, u32[]{:S(2)}) collective-permute-start(bf16[128,1024]{1,0:T(8,128)(2,1)} %get-tuple-element.200), channel_id=1, source_target_pairs={{0,16},{2,18},{4,20},{6,22},{8,24},{10,26},{12,28},{14,30},{16,0},... | collective-permute-start | bytes 786440 | tf_op jit(solution)/shard_map/ppermute | solution.py:472
  306.8 5.5 %shard_map.145 = (f32[32,512]{1,0:T(8,128)}, f32[512,128]{1,0:T(8,128)}) custom-call(f32[4,512,8]{2,1,0:T(8,128)} %get-tuple-element.109.rt_ref, bf16[512,2048]{1,0:T(8,128)(2,1)} %g_ref.11, bf16[512,128]{1,0:T(8,128)(2,1)} %c_ref.11, f32[128,1024]{1,0:T(8,128)} %get-tuple-element.204.s_ref, f32[2,128,1024]{2,1,0:T(8,128)} %get-tuple-element.205.e_ref, ...), custom_call_target="tpu_custom_call" | custom-call | flops 268435456 | bytes 3145728 | tf_op jit(solution)/shard_map/pallas_call | solution.py:839
  312.3 5.9 %collective-permute-done.38.got_ref = bf16[128,1024]{1,0:T(8,128)(2,1)S(1)} collective-permute-done((bf16[128,1024]{1,0:T(8,128)(2,1)}, bf16[128,1024]{1,0:T(8,128)(2,1)S(1)}, u32[]{:S(2)}, u32[]{:S(2)}) %collective-permute-start.38) | collective-permute-done | bytes 262176 | tf_op jit(solution)/shard_map/ppermute | solution.py:472
  318.8 2.1 shard_map.144.s_ref
  320.9 5.5 %shard_map.146 = (f32[32,512]{1,0:T(8,128)}, f32[512,128]{1,0:T(8,128)}) custom-call(f32[4,512,8]{2,1,0:T(8,128)} %get-tuple-element.109.rt_ref, bf16[512,2048]{1,0:T(8,128)(2,1)} %g_ref.11, bf16[512,128]{1,0:T(8,128)(2,1)} %c_ref.11, f32[128,1024]{1,0:T(8,128)} %shard_map.144.s_ref, ...), custom_call_target="tpu_custom_call", output_to_operand_aliasing={{0}: (9, {})} | custom-call | flops 268435456 | bytes 3145728 | tf_op jit(solution)/shard_map/pallas_call | solution.py:839
  328.8 1.7 convert_add_fusion
  (131 shorter events, 32.3 us)
Async XLA Ops:
  0.6 23.2 %collective-permute-start.2 = (bf16[512,2048]{1,0:T(8,128)(2,1)}, bf16[512,2048]{1,0:T(8,128)(2,1)}, u32[]{:S(2)}, u32[]{:S(2)}) collective-permute-start(bf16[512,2048]{1,0:T(8,128)(2,1)} %own_ref.1), channel_id=1, source_target_pairs={{0,1},{1,0},{2,3},{3,2},{4,5},{5,4},{6,7},{7,6},{8,9},{9,8},{10,11... | collective-permute-start | bytes 6291464 | tf_op jit(solution)/shard_map/ppermute | solution.py:472
  1.1 43.9 %collective-permute-start.4 = (bf16[256,2048]{1,0:T(8,128)(2,1)}, bf16[256,2048]{1,0:T(8,128)(2,1)}, u32[]{:S(2)}, u32[]{:S(2)}) collective-permute-start(bf16[256,2048]{1,0:T(8,128)(2,1)} %refs_0_.3), channel_id=1, source_target_pairs={{0,2},{2,0},{4,6},{6,4},{8,10},{10,8},{12,14},{14,12},{16,18},{18,... | collective-permute-start | bytes 3145736 | tf_op jit(solution)/shard_map/ppermute | solution.py:472
  3.7 41.3 %collective-permute-start.5 = (bf16[256,2048]{1,0:T(8,128)(2,1)}, bf16[256,2048]{1,0:T(8,128)(2,1)}, u32[]{:S(2)}, u32[]{:S(2)}) collective-permute-start(bf16[256,2048]{1,0:T(8,128)(2,1)} %refs_0_.3), channel_id=1, source_target_pairs={{0,4},{2,6},{4,0},{6,2},{8,12},{10,14},{12,8},{14,10},{16,20},{18,... | collective-permute-start | bytes 3145736 | tf_op jit(solution)/shard_map/ppermute | solution.py:472
  5.2 39.8 %collective-permute-start = (bf16[256,2048]{1,0:T(8,128)(2,1)}, bf16[256,2048]{1,0:T(8,128)(2,1)}, u32[]{:S(2)}, u32[]{:S(2)}) collective-permute-start(bf16[256,2048]{1,0:T(8,128)(2,1)} %refs_0_.3), channel_id=1, source_target_pairs={{0,8},{2,10},{4,12},{6,14},{8,16},{10,18},{12,20},{14,22},{16,24},... | collective-permute-start | bytes 3145736 | tf_op jit(solution)/shard_map/ppermute | solution.py:533
  9.7 35.3 %collective-permute-start.1 = (bf16[256,2048]{1,0:T(8,128)(2,1)}, bf16[256,2048]{1,0:T(8,128)(2,1)S(1)}, u32[]{:S(2)}, u32[]{:S(2)}) collective-permute-start(bf16[256,2048]{1,0:T(8,128)(2,1)} %refs_0_.3), channel_id=1, source_target_pairs={{8,0},{10,2},{12,4},{14,6},{16,8},{18,10},{20,12},{22,14},{24,16},... | collective-permute-start | bytes 3145736 | tf_op jit(solution)/shard_map/ppermute | solution.py:533
  23.9 16.5 %collective-permute-start.3 = (bf16[144,2048]{1,0:T(8,128)(2,1)}, bf16[144,2048]{1,0:T(8,128)(2,1)S(1)}, u32[]{:S(2)}, u32[]{:S(2)}) collective-permute-start(bf16[144,2048]{1,0:T(8,128)(2,1)} %shard_map.113), channel_id=1, source_target_pairs={{0,2},{2,0},{4,6},{6,4},{8,10},{10,8},{12,14},{14,12},{16,18},{18,... | collective-permute-start | bytes 1769480 | tf_op jit(solution)/shard_map/ppermute | solution.py:472
  40.3 0.8 copy-start.16
  45.0 1.0 copy-start
  46.0 5.7 %copy-start.1 = (bf16[256,2048]{1,0:T(8,128)(2,1)S(1)}, bf16[256,2048]{1,0:T(8,128)(2,1)}, u32[]{:S(2)}) copy-start(bf16[256,2048]{1,0:T(8,128)(2,1)} %get-tuple-element.117.refs_2_) | copy-start | bytes 3145732
  46.0 12.6 %copy-start.15 = (bf16[144,2048]{1,0:T(8,128)(2,1)S(1)}, bf16[144,2048]{1,0:T(8,128)(2,1)}, u32[]{:S(2)}) copy-start(bf16[144,2048]{1,0:T(8,128)(2,1)} %get-tuple-element.120) | copy-start | bytes 1769476
  46.0 13.1 %copy-start.26 = (s32[4,4]{1,0:T(4,128)S(1)}, s32[4,4]{1,0:T(4,128)}, u32[]{:S(2)}) copy-start(s32[4,4]{1,0:T(4,128)} %constant.68.clone) | copy-start | bytes 196
  48.4 41.9 %collective-permute-start.10 = (bf16[256,2048]{1,0:T(8,128)(2,1)}, bf16[256,2048]{1,0:T(8,128)(2,1)}, u32[]{:S(2)}, u32[]{:S(2)}) collective-permute-start(bf16[256,2048]{1,0:T(8,128)(2,1)} %broadcast_select_fusion.refs_3_), channel_id=1, source_target_pairs={{0,4},{2,6},{4,0},{6,2},{8,12},{10,14},{12,8},{14,10},{16,20},{18,... | collective-permute-start | bytes 3145736 | tf_op jit(solution)/shard_map/ppermute | solution.py:472
  50.2 40.1 %collective-permute-start.9 = (bf16[256,2048]{1,0:T(8,128)(2,1)}, bf16[256,2048]{1,0:T(8,128)(2,1)}, u32[]{:S(2)}, u32[]{:S(2)}) collective-permute-start(bf16[256,2048]{1,0:T(8,128)(2,1)} %broadcast_select_fusion.refs_3_), channel_id=1, source_target_pairs={{0,2},{2,0},{4,6},{6,4},{8,10},{10,8},{12,14},{14,12},{16,18},{18,... | collective-permute-start | bytes 3145736 | tf_op jit(solution)/shard_map/ppermute | solution.py:472
  51.7 38.6 %collective-permute-start.7 = (bf16[256,2048]{1,0:T(8,128)(2,1)S(1)}, bf16[256,2048]{1,0:T(8,128)(2,1)}, u32[]{:S(2)}, u32[]{:S(2)}) collective-permute-start(bf16[256,2048]{1,0:T(8,128)(2,1)S(1)} %copy-done.1), channel_id=1, source_target_pairs={{8,0},{10,2},{12,4},{14,6},{16,8},{18,10},{20,12},{22,14},{24,16},... | collective-permute-start | bytes 3145736 | tf_op jit(solution)/shard_map/ppermute | solution.py:533
  53.0 37.4 %collective-permute-start.6 = (bf16[256,2048]{1,0:T(8,128)(2,1)}, bf16[256,2048]{1,0:T(8,128)(2,1)}, u32[]{:S(2)}, u32[]{:S(2)}) collective-permute-start(bf16[256,2048]{1,0:T(8,128)(2,1)} %get-tuple-element.116), channel_id=1, source_target_pairs={{0,8},{2,10},{4,12},{6,14},{8,16},{10,18},{12,20},{14,22},{16,24},... | collective-permute-start | bytes 3145736 | tf_op jit(solution)/shard_map/ppermute | solution.py:533
  58.6 27.7 %collective-permute-start.8 = (bf16[144,2048]{1,0:T(8,128)(2,1)S(1)}, bf16[144,2048]{1,0:T(8,128)(2,1)}, u32[]{:S(2)}, u32[]{:S(2)}) collective-permute-start(bf16[144,2048]{1,0:T(8,128)(2,1)S(1)} %copy-done.15), channel_id=1, source_target_pairs={{0,4},{2,6},{4,0},{6,2},{8,12},{10,14},{12,8},{14,10},{16,20},{18,... | collective-permute-start | bytes 1769480 | tf_op jit(solution)/shard_map/ppermute | solution.py:472
  90.4 24.7 %collective-permute-start.11 = (bf16[256,2048]{1,0:T(8,128)(2,1)}, bf16[256,2048]{1,0:T(8,128)(2,1)S(1)}, u32[]{:S(2)}, u32[]{:S(2)}) collective-permute-start(bf16[256,2048]{1,0:T(8,128)(2,1)} %get-tuple-element.125), channel_id=1, source_target_pairs={{0,8},{2,10},{4,12},{6,14},{8,16},{10,18},{12,20},{14,22},{16,24},... | collective-permute-start | bytes 3145736 | tf_op jit(solution)/shard_map/ppermute | solution.py:533
  93.8 25.6 %collective-permute-start.12 = (bf16[256,2048]{1,0:T(8,128)(2,1)}, bf16[256,2048]{1,0:T(8,128)(2,1)S(1)}, u32[]{:S(2)}, u32[]{:S(2)}) collective-permute-start(bf16[256,2048]{1,0:T(8,128)(2,1)} %get-tuple-element.124), channel_id=1, source_target_pairs={{8,0},{10,2},{12,4},{14,6},{16,8},{18,10},{20,12},{22,14},{24,16},... | collective-permute-start | bytes 3145736 | tf_op jit(solution)/shard_map/ppermute | solution.py:533
  119.4 6.8 %copy-start.14 = (bf16[144,2048]{1,0:T(8,128)(2,1)S(1)}, bf16[144,2048]{1,0:T(8,128)(2,1)}, u32[]{:S(2)}) copy-start(bf16[144,2048]{1,0:T(8,128)(2,1)} %get-tuple-element.129) | copy-start | bytes 1769476
  119.4 9.2 %copy-start.27 = (f32[32]{0:T(128)S(1)}, f32[32]{0:T(128)}, u32[]{:S(2)}) copy-start(f32[32]{0:T(128)} %param.13) | copy-start | bytes 388
  123.0 22.8 %collective-permute-start.13 = (bf16[256,2048]{1,0:T(8,128)(2,1)}, bf16[256,2048]{1,0:T(8,128)(2,1)S(1)}, u32[]{:S(2)}, u32[]{:S(2)}) collective-permute-start(bf16[256,2048]{1,0:T(8,128)(2,1)} %get-tuple-element.212.refs_6_), channel_id=1, source_target_pairs={{0,4},{2,6},{4,0},{6,2},{8,12},{10,14},{12,8},{14,10},{16,20},{18,... | collective-permute-start | bytes 3145736 | tf_op jit(solution)/shard_map/ppermute | solution.py:472
  124.7 23.3 %collective-permute-start.15 = (bf16[256,2048]{1,0:T(8,128)(2,1)}, bf16[256,2048]{1,0:T(8,128)(2,1)}, u32[]{:S(2)}, u32[]{:S(2)}) collective-permute-start(bf16[256,2048]{1,0:T(8,128)(2,1)} %get-tuple-element.212.refs_6_), channel_id=1, source_target_pairs={{0,2},{2,0},{4,6},{6,4},{8,10},{10,8},{12,14},{14,12},{16,18},{18,... | collective-permute-start | bytes 3145736 | tf_op jit(solution)/shard_map/ppermute | solution.py:472
  126.2 12.2 %collective-permute-start.14 = (bf16[144,2048]{1,0:T(8,128)(2,1)S(1)}, bf16[144,2048]{1,0:T(8,128)(2,1)S(1)}, u32[]{:S(2)}, u32[]{:S(2)}) collective-permute-start(bf16[144,2048]{1,0:T(8,128)(2,1)S(1)} %copy-done.14), channel_id=1, source_target_pairs={{0,8},{2,10},{4,12},{6,14},{8,0},{10,2},{12,4},{14,6},{16,24},{18,... | collective-permute-start | bytes 1769480 | tf_op jit(solution)/shard_map/ppermute | solution.py:472
  138.4 0.8 copy-start.17
  145.8 2.2 copy-start.4
  148.1 31.4 %collective-permute-start.16 = (bf16[256,1024]{1,0:T(8,128)(2,1)}, bf16[256,1024]{1,0:T(8,128)(2,1)}, u32[]{:S(2)}, u32[]{:S(2)}) collective-permute-start(bf16[256,1024]{1,0:T(8,128)(2,1)} %get-tuple-element.133.refs_3_.refs_6_), channel_id=1, source_target_pairs={{0,2},{2,0},{4,6},{6,4},{8,10},{10,8},{12,14},{14,12},{16,18},{18,... | collective-permute-start | bytes 1572872 | tf_op jit(solution)/shard_map/ppermute | solution.py:472
  149.5 29.9 %collective-permute-start.18 = (bf16[256,1024]{1,0:T(8,128)(2,1)}, bf16[256,1024]{1,0:T(8,128)(2,1)S(1)}, u32[]{:S(2)}, u32[]{:S(2)}) collective-permute-start(bf16[256,1024]{1,0:T(8,128)(2,1)} %get-tuple-element.133.refs_3_.refs_6_), channel_id=1, source_target_pairs={{0,4},{2,6},{4,0},{6,2},{8,12},{10,14},{12,8},{14,10},{16,20},{18,... | collective-permute-start | bytes 1572872 | tf_op jit(solution)/shard_map/ppermute | solution.py:472
  150.1 25.3 %collective-permute-start.17 = (bf16[144,2048]{1,0:T(8,128)(2,1)}, bf16[144,2048]{1,0:T(8,128)(2,1)}, u32[]{:S(2)}, u32[]{:S(2)}) collective-permute-start(bf16[144,2048]{1,0:T(8,128)(2,1)} %get-tuple-element.138), channel_id=1, source_target_pairs={{0,16},{2,18},{4,20},{6,22},{8,24},{10,26},{12,28},{14,30},{16,0},... | collective-permute-start | bytes 1769480 | tf_op jit(solution)/shard_map/ppermute | solution.py:472
  154.9 24.5 %collective-permute-start.19 = (bf16[256,1024]{1,0:T(8,128)(2,1)}, bf16[256,1024]{1,0:T(8,128)(2,1)S(1)}, u32[]{:S(2)}, u32[]{:S(2)}) collective-permute-start(bf16[256,1024]{1,0:T(8,128)(2,1)} %get-tuple-element.220), channel_id=1, source_target_pairs={{0,2},{2,0},{4,6},{6,4},{8,10},{10,8},{12,14},{14,12},{16,18},{18,... | collective-permute-start | bytes 1572872 | tf_op jit(solution)/shard_map/ppermute | solution.py:472
  157.7 21.7 %collective-permute-start.20 = (bf16[256,1024]{1,0:T(8,128)(2,1)}, bf16[256,1024]{1,0:T(8,128)(2,1)S(1)}, u32[]{:S(2)}, u32[]{:S(2)}) collective-permute-start(bf16[256,1024]{1,0:T(8,128)(2,1)} %get-tuple-element.218), channel_id=1, source_target_pairs={{0,4},{2,6},{4,0},{6,2},{8,12},{10,14},{12,8},{14,10},{16,20},{18,... | collective-permute-start | bytes 1572872 | tf_op jit(solution)/shard_map/ppermute | solution.py:472
  179.4 1.0 copy-start.8
  179.4 0.9 copy-start.9
  179.4 1.1 copy-start.7
  180.6 4.6 %copy-start.3 = (f32[2,128,2048]{2,1,0:T(8,128)S(1)}, f32[2,128,2048]{2,1,0:T(8,128)}, u32[]{:S(2)}) copy-start(f32[2,128,2048]{2,1,0:T(8,128)} %get-tuple-element.110.own_ref) | copy-start | bytes 6291460
  180.6 43.5 %collective-permute-start.22 = (bf16[256,1024]{1,0:T(8,128)(2,1)}, bf16[256,1024]{1,0:T(8,128)(2,1)}, u32[]{:S(2)}, u32[]{:S(2)}) collective-permute-start(bf16[256,1024]{1,0:T(8,128)(2,1)} %get-tuple-element.143.refs_3_.refs_7_), channel_id=1, source_target_pairs={{0,2},{2,0},{4,6},{6,4},{8,10},{10,8},{12,14},{14,12},{16,18},{18,... | collective-permute-start | bytes 1572872 | tf_op jit(solution)/shard_map/ppermute | solution.py:472
  181.1 43.0 %collective-permute-start.24 = (bf16[256,1024]{1,0:T(8,128)(2,1)}, bf16[256,1024]{1,0:T(8,128)(2,1)S(1)}, u32[]{:S(2)}, u32[]{:S(2)}) collective-permute-start(bf16[256,1024]{1,0:T(8,128)(2,1)} %get-tuple-element.143.refs_3_.refs_7_), channel_id=1, source_target_pairs={{0,4},{2,6},{4,0},{6,2},{8,12},{10,14},{12,8},{14,10},{16,20},{18,... | collective-permute-start | bytes 1572872 | tf_op jit(solution)/shard_map/ppermute | solution.py:472
  181.6 25.4 %collective-permute-start.21 = (bf16[256,1024]{1,0:T(8,128)(2,1)}, bf16[256,1024]{1,0:T(8,128)(2,1)}, u32[]{:S(2)}, u32[]{:S(2)}) collective-permute-start(bf16[256,1024]{1,0:T(8,128)(2,1)} %get-tuple-element.142), channel_id=1, source_target_pairs={{0,2},{2,0},{4,6},{6,4},{8,10},{10,8},{12,14},{14,12},{16,18},{18,... | collective-permute-start | bytes 1572872 | tf_op jit(solution)/shard_map/ppermute | solution.py:472
  183.1 34.4 %collective-permute-start.23 = (bf16[256,1024]{1,0:T(8,128)(2,1)}, bf16[256,1024]{1,0:T(8,128)(2,1)}, u32[]{:S(2)}, u32[]{:S(2)}) collective-permute-start(bf16[256,1024]{1,0:T(8,128)(2,1)} %get-tuple-element.145.refs_4_.refs_8_), channel_id=1, source_target_pairs={{0,4},{2,6},{4,0},{6,2},{8,12},{10,14},{12,8},{14,10},{16,20},{18,... | collective-permute-start | bytes 1572872 | tf_op jit(solution)/shard_map/ppermute | solution.py:472
  184.6 39.5 %collective-permute-start.25 = (bf16[256,1024]{1,0:T(8,128)(2,1)}, bf16[256,1024]{1,0:T(8,128)(2,1)S(1)}, u32[]{:S(2)}, u32[]{:S(2)}) collective-permute-start(bf16[256,1024]{1,0:T(8,128)(2,1)} %get-tuple-element.148), channel_id=1, source_target_pairs={{0,2},{2,0},{4,6},{6,4},{8,10},{10,8},{12,14},{14,12},{16,18},{18,... | collective-permute-start | bytes 1572872 | tf_op jit(solution)/shard_map/ppermute | solution.py:472
  188.0 19.0 %copy-start.6 = (bf16[256,1024]{1,0:T(8,128)(2,1)S(1)}, bf16[256,1024]{1,0:T(8,128)(2,1)}, u32[]{:S(2)}) copy-start(bf16[256,1024]{1,0:T(8,128)(2,1)} %get-tuple-element.149) | copy-start | bytes 1572868
  207.0 17.1 %collective-permute-start.26 = (bf16[256,1024]{1,0:T(8,128)(2,1)S(1)}, bf16[256,1024]{1,0:T(8,128)(2,1)}, u32[]{:S(2)}, u32[]{:S(2)}) collective-permute-start(bf16[256,1024]{1,0:T(8,128)(2,1)S(1)} %copy-done.6), channel_id=1, source_target_pairs={{0,4},{2,6},{4,0},{6,2},{8,12},{10,14},{12,8},{14,10},{16,20},{18,... | collective-permute-start | bytes 1572872 | tf_op jit(solution)/shard_map/ppermute | solution.py:472
  224.1 0.8 copy-start.10
  224.1 1.0 copy-start.11
  225.1 3.6 %copy-start.28 = (s32[16]{0:T(128)S(1)}, s32[16]{0:T(128)}, u32[]{:S(2)}) copy-start(s32[16]{0:T(128)} %get-tuple-element.228) | copy-start | bytes 196
  225.1 18.2 %collective-permute-start.27 = (bf16[256,1024]{1,0:T(8,128)(2,1)}, bf16[256,1024]{1,0:T(8,128)(2,1)S(1)}, u32[]{:S(2)}, u32[]{:S(2)}) collective-permute-start(bf16[256,1024]{1,0:T(8,128)(2,1)} %get-tuple-element.151), channel_id=1, source_target_pairs={{0,2},{2,0},{4,6},{6,4},{8,10},{10,8},{12,14},{14,12},{16,18},{18,... | collective-permute-start | bytes 1572872 | tf_op jit(solution)/shard_map/ppermute | solution.py:472
  225.6 17.7 %collective-permute-start.28 = (bf16[256,1024]{1,0:T(8,128)(2,1)}, bf16[256,1024]{1,0:T(8,128)(2,1)S(1)}, u32[]{:S(2)}, u32[]{:S(2)}) collective-permute-start(bf16[256,1024]{1,0:T(8,128)(2,1)} %get-tuple-element.152.refs_4_.refs_9_), channel_id=1, source_target_pairs={{0,4},{2,6},{4,0},{6,2},{8,12},{10,14},{12,8},{14,10},{16,20},{18,... | collective-permute-start | bytes 1572872 | tf_op jit(solution)/shard_map/ppermute | solution.py:472
  227.1 13.3 %collective-permute-start.29 = (bf16[128,1024]{1,0:T(8,128)(2,1)}, bf16[128,1024]{1,0:T(8,128)(2,1)S(1)}, u32[]{:S(2)}, u32[]{:S(2)}) collective-permute-start(bf16[128,1024]{1,0:T(8,128)(2,1)} %get-tuple-element.155), channel_id=1, source_target_pairs={{0,2},{2,0},{4,6},{6,4},{8,10},{10,8},{12,14},{14,12},{16,18},{18,... | collective-permute-start | bytes 786440 | tf_op jit(solution)/shard_map/ppermute | solution.py:472
  243.3 0.8 copy-start.12
  243.3 0.9 copy-start.13
  250.8 12.0 %collective-permute-start.31 = (bf16[128,1024]{1,0:T(8,128)(2,1)}, bf16[128,1024]{1,0:T(8,128)(2,1)S(1)}, u32[]{:S(2)}, u32[]{:S(2)}) collective-permute-start(bf16[128,1024]{1,0:T(8,128)(2,1)} %get-tuple-element.174), channel_id=1, source_target_pairs={{0,2},{2,0},{4,6},{6,4},{8,10},{10,8},{12,14},{14,12},{16,18},{18,... | collective-permute-start | bytes 786440 | tf_op jit(solution)/shard_map/ppermute | solution.py:472
  251.3 14.3 %collective-permute-start.30 = (bf16[128,1024]{1,0:T(8,128)(2,1)}, bf16[128,1024]{1,0:T(8,128)(2,1)S(1)}, u32[]{:S(2)}, u32[]{:S(2)}) collective-permute-start(bf16[128,1024]{1,0:T(8,128)(2,1)} %get-tuple-element.169), channel_id=1, source_target_pairs={{0,4},{2,6},{4,0},{6,2},{8,12},{10,14},{12,8},{14,10},{16,20},{18,... | collective-permute-start | bytes 786440 | tf_op jit(solution)/shard_map/ppermute | solution.py:472
  262.8 0.7 copy-start.18
  265.7 0.7 copy-start.20
  268.6 15.5 %collective-permute-start.34 = (bf16[512,2048]{1,0:T(8,128)(2,1)}, bf16[512,2048]{1,0:T(8,128)(2,1)}, u32[]{:S(2)}, u32[]{:S(2)}) collective-permute-start(bf16[512,2048]{1,0:T(8,128)(2,1)} %get-tuple-element.185), channel_id=1, source_target_pairs={{0,1},{1,0},{2,3},{3,2},{4,5},{5,4},{6,7},{7,6},{8,9},{9,8},{10,11... | collective-permute-start | bytes 6291464 | tf_op jit(solution)/shard_map/ppermute | solution.py:472
  268.6 9.5 %collective-permute-start.33 = (bf16[128,1024]{1,0:T(8,128)(2,1)}, bf16[128,1024]{1,0:T(8,128)(2,1)S(1)}, u32[]{:S(2)}, u32[]{:S(2)}) collective-permute-start(bf16[128,1024]{1,0:T(8,128)(2,1)} %get-tuple-element.182), channel_id=1, source_target_pairs={{0,4},{2,6},{4,0},{6,2},{8,12},{10,14},{12,8},{14,10},{16,20},{18,... | collective-permute-start | bytes 786440 | tf_op jit(solution)/shard_map/ppermute | solution.py:472
  269.1 12.0 %collective-permute-start.32 = (bf16[128,1024]{1,0:T(8,128)(2,1)}, bf16[128,1024]{1,0:T(8,128)(2,1)S(1)}, u32[]{:S(2)}, u32[]{:S(2)}) collective-permute-start(bf16[128,1024]{1,0:T(8,128)(2,1)} %get-tuple-element.178), channel_id=1, source_target_pairs={{0,8},{2,10},{4,12},{6,14},{8,0},{10,2},{12,4},{14,6},{16,24},{18,... | collective-permute-start | bytes 786440 | tf_op jit(solution)/shard_map/ppermute | solution.py:472
  278.1 0.7 copy-start.23
  284.1 3.2 copy-start.2
  284.1 15.2 %collective-permute-start.37 = (bf16[128,1024]{1,0:T(8,128)(2,1)}, bf16[128,1024]{1,0:T(8,128)(2,1)S(1)}, u32[]{:S(2)}, u32[]{:S(2)}) collective-permute-start(bf16[128,1024]{1,0:T(8,128)(2,1)} %get-tuple-element.198), channel_id=1, source_target_pairs={{0,16},{2,18},{4,20},{6,22},{8,24},{10,26},{12,28},{14,30},{16,0},... | collective-permute-start | bytes 786440 | tf_op jit(solution)/shard_map/ppermute | solution.py:472
  284.4 11.9 %collective-permute-start.36 = (bf16[128,1024]{1,0:T(8,128)(2,1)}, bf16[128,1024]{1,0:T(8,128)(2,1)S(1)}, u32[]{:S(2)}, u32[]{:S(2)}) collective-permute-start(bf16[128,1024]{1,0:T(8,128)(2,1)} %get-tuple-element.193), channel_id=1, source_target_pairs={{0,8},{2,10},{4,12},{6,14},{8,0},{10,2},{12,4},{14,6},{16,24},{18,... | collective-permute-start | bytes 786440 | tf_op jit(solution)/shard_map/ppermute | solution.py:472
  287.2 3.8 %collective-permute-start.35 = (bf16[512,128]{1,0:T(8,128)(2,1)S(1)}, bf16[512,128]{1,0:T(8,128)(2,1)S(1)}, u32[]{:S(2)}, u32[]{:S(2)}) collective-permute-start(bf16[512,128]{1,0:T(8,128)(2,1)S(1)} %convert_element_type.38), channel_id=1, source_target_pairs={{0,1},{1,0},{2,3},{3,2},{4,5},{5,4},{6,7},{7,6},{8,9},{9,8},{10,11... | collective-permute-start | bytes 393224 | tf_op jit(solution)/shard_map/ppermute | solution.py:472
  287.3 3.7 %copy-start.5 = (f32[512,128]{1,0:T(8,128)S(1)}, f32[512,128]{1,0:T(8,128)}, u32[]{:S(2)}) copy-start(f32[512,128]{1,0:T(8,128)} %get-tuple-element.190) | copy-start | bytes 786436
  302.1 16.1 %collective-permute-start.38 = (bf16[128,1024]{1,0:T(8,128)(2,1)}, bf16[128,1024]{1,0:T(8,128)(2,1)S(1)}, u32[]{:S(2)}, u32[]{:S(2)}) collective-permute-start(bf16[128,1024]{1,0:T(8,128)(2,1)} %get-tuple-element.200), channel_id=1, source_target_pairs={{0,16},{2,18},{4,20},{6,22},{8,24},{10,26},{12,28},{14,30},{16,0},... | collective-permute-start | bytes 786440 | tf_op jit(solution)/shard_map/ppermute | solution.py:472
  327.4 1.4 collective-permute-start.39
  (5 other events, 3.5 us)

commit v7 on v6

--- a/solution.py
+++ b/solution.py
@@ -14,7 +14,8 @@
 WIDE = GROUP * P_SIZE
 LOG2E = 1.4426950408889634
 NEVER = -1e30
-GRANT = 62 * 2**20
+GRANT = 24 * 2**20
+LARGE = 30 * 2**20
 
 F32 = jnp.float32
 BF16 = jnp.bfloat16
@@ -527,10 +528,13 @@
     return list(out)
 
 
-def along_z(value, by):
-    count = lax.axis_size("ctx")
-    pairs = [(i, i + PLANE * by) for i in range(count) if 0 <= i + PLANE * by < count]
+def along_z(value, moves):
+    pairs = [(a * PLANE + i, b * PLANE + i) for a, b in moves for i in range(PLANE)]
     return lax.ppermute(value, "ctx", pairs)
+
+
+MIDDLE = ((1, 2), (2, 1))
+OUTWARD = ((1, 0), (2, 3))
 
 
 def swap_x(value):
@@ -541,7 +545,7 @@
     return swap(value, "ctx", 2)
 
 
-LAYERS = ((0, 1, 2, 3), (1, 0, 1, 2), (2, 2, 3, 1), (3, 3, 0, 0))
+LAYERS = ((0, 1, 2, 3), (1, 0, 3, 2), (2, 2, 1, 1), (3, 3, 0, 0))
 EARLY = [(k, flip) for k in (0, 1, 2) for flip in range(3)]
 LATE = [(0, 3), (1, 3), (2, 3), (3, 0), (3, 1), (3, 2), (3, 3)]
 
@@ -716,7 +720,7 @@
             transcendentals=0,
         ),
         compiler_params=pltpu.CompilerParams(
-            dimension_semantics=("arbitrary",), vmem_limit_bytes=GRANT
+            dimension_semantics=("arbitrary",), vmem_limit_bytes=LARGE
         ),
     )(order, grad_x, *arrays, *so_far)
 
@@ -875,8 +879,7 @@
     blocks = order.shape[0]
     width = blocks * w_in.shape[0]
 
-    layer = lax.axis_index("ctx") // PLANE
-    up1, down1 = along_z(w_in, 1), along_z(w_in, -1)
+    z1, inner2 = swap(w_in, "ctx", PLANE), along_z(w_in, MIDDLE)
     own_x, own_y = swap_x(w_in), swap_y(w_in)
     other = swap(inputs, "head", 1)
     running, running_t, kept, own_grads = prepare(log_decay, grad_out, c_rows)
@@ -885,10 +888,10 @@
     sent = after([sent], other)[0]
     back, leaving, sent, log, factors_1 = back_step(spot, log, back, sent, (), 1)
 
-    up1, down1, sent = after([up1, down1, sent], own_x, own_y)
-    up2, down2 = along_z(up1, 1), along_z(down1, -1)
-    z1 = jnp.where(layer == 0, down1, up1)
+    z1, inner2, own_y, sent = after([z1, inner2, own_y, sent], own_x)
     x1, y1 = swap_x(z1), swap_y(z1)
+    inner3, outer2 = along_z(z1, MIDDLE), along_z(inner2, OUTWARD)
+    own_y_a, own_y_b = own_y[:, :half], own_y[:, half:]
     back, leaving, sent, log, factors_2 = back_step(spot, log, back, sent, (leaving,), 2)
     order_own = (order + place * (blocks // 2)) % blocks
     cut = len(EARLY) * w_in.shape[0]
@@ -903,18 +906,19 @@
         [pltpu.VMEM((length, width), BF16)],
     )(order_own, inputs, other)
 
-    up2, down2, down1, sent = after([up2, down2, down1, sent], x1, y1, early_features)
-    z3 = jnp.where(layer == 0, down2, jnp.where(layer == 3, up2, down1))
-    up3, down3 = along_z(up2, 1), along_z(down2, -1)
+    inner2, inner3, outer2, x1, sent, own_y_a, own_y_b = after(
+        [inner2, inner3, outer2, x1, sent, own_y_a, own_y_b], y1, early_features
+    )
+    z3 = inner2 + outer2
     x3, y3 = swap_x(z3), swap_y(z3)
+    outer3 = along_z(inner3, OUTWARD)
+    x1_a, x1_b = x1[:, :half], x1[:, half:]
     back, leaving, sent, log, factors_4 = back_step(spot, log, back, sent, (leaving,), 4)
-    z2 = jnp.where(layer == 1, down2, jnp.where(layer == 2, up2, up3 + down3))
-    z2a, z2b = z2[:, :half], z2[:, half:]
-
-    z2a, x1, y3, own_y, sent = after([z2a, x1, y3, own_y, sent], x3, z2b)
-    x1_a, x1_b = x1[:, :half], x1[:, half:]
+
+    inner3, outer3, y3, x1_a, x1_b, sent = after([inner3, outer3, y3, x1_a, x1_b, sent], x3)
+    z2a = inner3[:, :half] + outer3[:, :half]
+    z2b = inner3[:, half:] + outer3[:, half:]
     y3_a, y3_b = y3[:, :half], y3[:, half:]
-    own_y_a, own_y_b = own_y[:, :half], own_y[:, half:]
     x2a, y2a = swap_x(z2a), swap_y(z2a)
     d3a, d1a = swap_x(y3_a), swap_y(x1_a)
     back, leaving, sent, log, factors_8 = back_step(spot, log, back, sent, (leaving,), 8)

time: 332 us -> 348 us (1.048)
  local copies, waits for them, and re-layouts: 23.4 us -> 97.2 us
  Pallas kernels: 134 us -> 84.2 us
  starting transfers between devices: 56 us -> 46.4 us
    unnamed x58 -> x308, local copies, waits for them, and re-layouts: 11.2 us -> 89.3 us
    ppermute x34 -> x35, waiting for transfers between devices: 72.2 us -> 99.6 us  [swap(): return lax.ppermute(value, axis, [(i, i ^ bit) for i in range(count)])]
    ppermute x6 -> x4, waiting for transfers between devices: 24.2 us -> 0.01 us  [along_z(): return lax.ppermute(value, 'ctx', pairs)]
    pallas_call x8, Pallas kernels: 17.4 us -> 2.68 us  [scan_step(): call(scan_kernel, (columns // WIDE,), [pl.BlockSpec((8, WIDE), lambda h:...]
    ppermute x6 -> x4, starting transfers between devices: 17.5 us -> 5.82 us  [along_z(): return lax.ppermute(value, 'ctx', pairs)]
    pallas_call x4, Pallas kernels: 16 us -> 8.64 us  [back_step(): call(functools.partial(back_kernel, bit), (columns // WIDE,), [SCALARS] +...]
    select_n x2 -> x0, other arithmetic: 5.99 us -> none  [the longest x1 3.55 us: local_layered(): z3 = jnp.where(layer == 0, down2, jnp.where(layer == 3, up2, down1))]
    add x0 -> x2, other arithmetic: none -> 4.77 us  [the longest x1 2.68 us: local_layered(): z2b = inner3[:, half:] + outer3[:, half:]]
  transfers between devices with their start and end apart: 40 -> 39, of which waited for: 13 -> 9; matrix products, arithmetic and copies ran while one was open for 6% -> 5% of each run, Pallas kernels for 35% -> 22%
where the time goes in v7:
time: 348 us; the launch traced here: 346 us
  waiting for transfers between devices  99.7 us (29%)
  local copies, waits for them, and re-layouts  97.2 us (28%)
  Pallas kernels  84.2 us (24%)
  starting transfers between devices  46.4 us (13%)
  other arithmetic  14.1 us (4%)
  between operations  4.37 us (1%)
    ppermute x35, waiting for transfers between devices, swap(): return lax.ppermute(value, axis, [(i, i ^ bit) for i in range(count)])  99.6 us
    unnamed x308, local copies, waits for them, and re-layouts  89.3 us
    ppermute x35, starting transfers between devices, swap(): return lax.ppermute(value, axis, [(i, i ^ bit) for i in range(count)])  40.6 us
    pallas_call x2, Pallas kernels, multiply_blocks(): pl.pallas_call(functools.partial(blocks_kernel, [len(piece) for piece in...  17.6 us
    pallas_call x2, Pallas kernels, inner(): call(inner_kernel, grid, specs + [SHARED] * len(so_far), [run_spec(), SHA...  13.9 us
    pallas_call x2, Pallas kernels, late_forward(): call(functools.partial(late_forward_kernel, len(pieces)), (columns // WID...  9.06 us
    pallas_call x4, Pallas kernels, back_step(): call(functools.partial(back_kernel, bit), (columns // WIDE,), [SCALARS] +...  8.64 us
    pallas_call x1, Pallas kernels, grad_rows(): call(functools.partial(grad_x_kernel, transposed), (length // SPAN, runni...  8.02 us
  transfers between devices with their start and end apart: 39, of which 9 were waited for; matrix products, arithmetic and copies ran while one was open for 5% of the time, Pallas kernels for 22%

profile of v7, /device:TPU:0, one launch (start us, length us, event | category | flops | bytes accessed | tf_op | source)
XLA Modules:
  0.0 345.9 jit_solution(7387038304363406016)
XLA Ops:
  1.1 2.6 collective-permute-start.5
  3.7 1.6 collective-permute-start
  5.3 1.6 collective-permute-start.1
  6.9 1.5 collective-permute-start.2
  8.4 1.6 copy-done.3
  11.8 7.0 %shard_map.111 = (f32[32,512]{1,0:T(8,128)S(1)}, f32[4,512,8]{2,1,0:T(8,128)S(1)}, f32[2,8,2048]{2,1,0:T(8,128)S(1)}, f32[2,128,2048]{2,1,0:T(8,128)S(1)}) custom-call(f32[32,512]{1,0:T(8,128)S(1)} %copy-done.140, bf16[512,2048]{1,0:T(8,128)(2,1)S(1)} %copy-done.3, bf16[512,128]{1,0:T(8,128)(2,1)S(1)} %copy-done.36), custom_call_target="tpu_custom_call" | custom-call | flops 268435456 | bytes 6291456 | tf_op jit(solution)/shard_map/pallas_call | solution.py:797
  21.4 1.3 copy-done.16
  23.2 17.1 %collective-permute-done.4.got_ref = bf16[144,2048]{1,0:T(8,128)(2,1)S(1)} collective-permute-done((bf16[144,2048]{1,0:T(8,128)(2,1)}, bf16[144,2048]{1,0:T(8,128)(2,1)S(1)}, u32[]{:S(2)}, u32[]{:S(2)}) %collective-permute-start.4) | collective-permute-done | bytes 589856 | tf_op jit(solution)/shard_map/ppermute | solution.py:473
  45.8 1.9 collective-permute-start.10
  47.6 1.6 collective-permute-start.6
  49.3 1.5 collective-permute-start.8
  56.1 1.6 copy-done.38
  57.7 1.4 shard_map.117
  59.1 1.4 copy-done.32
  60.5 3.0 fusion.6
  63.5 20.2 %collective-permute-done.9.got_ref = bf16[144,2048]{1,0:T(8,128)(2,1)} collective-permute-done((bf16[144,2048]{1,0:T(8,128)(2,1)}, bf16[144,2048]{1,0:T(8,128)(2,1)}, u32[]{:S(2)}, u32[]{:S(2)}) %collective-permute-start.9) | collective-permute-done | bytes 589856 | tf_op jit(solution)/shard_map/ppermute | solution.py:473
  83.7 2.4 shard_map.116
  89.6 2.1 add.123.refs_6_
  91.7 1.7 collective-permute-start.12
  93.4 1.5 collective-permute-start.14
  96.2 2.8 collective-permute-start.13
  98.9 2.3 fusion.5
  101.2 31.7 %collective-permute-done.13.got_ref = bf16[144,2048]{1,0:T(8,128)(2,1)S(1)} collective-permute-done((bf16[144,2048]{1,0:T(8,128)(2,1)S(1)}, bf16[144,2048]{1,0:T(8,128)(2,1)S(1)}, u32[]{:S(2)}, u32[]{:S(2)}) %collective-permute-start.13) | collective-permute-done | bytes 589856 | tf_op jit(solution)/shard_map/ppermute | solution.py:473
  132.9 2.0 shard_map.119
  139.4 2.7 slice_add_fusion
  143.3 1.5 collective-permute-start.16
  146.0 1.5 collective-permute-start.18
  147.5 1.5 collective-permute-start.19
  149.7 1.7 copy-done.33
  155.1 7.4 %shard_map.122.refs_9_.part_ref = f32[512,2048]{1,0:T(8,128)S(1)} custom-call(bf16[512,2304]{1,0:T(8,128)(2,1)S(1)} %copy-done.33, bf16[256,2048]{1,0:T(8,128)(2,1)S(1)} %copy-done.145, bf16[256,2048]{1,0:T(8,128)(2,1)} %collective-permute-done.5.refs_4_.refs_1_, bf16[256,2048]{1,0:T(8,128)(2,1)} %get-tuple-element.128.refs_2_, ...), custom_call_target="tpu_custom_call" | custom-call | flops 4831838208 | bytes 9437184 | tf_op jit(solution)/shard_map/pallas_call | solution.py:647
  162.6 2.0 copy-done
  164.5 4.8 %collective-permute-done.16.got_ref = bf16[144,2048]{1,0:T(8,128)(2,1)} collective-permute-done((bf16[144,2048]{1,0:T(8,128)(2,1)}, bf16[144,2048]{1,0:T(8,128)(2,1)}, u32[]{:S(2)}, u32[]{:S(2)}) %collective-permute-start.16) | collective-permute-done | bytes 589856 | tf_op jit(solution)/shard_map/ppermute | solution.py:473
  169.3 3.6 %shard_map.121 = (f32[128,2048]{1,0:T(8,128)}, f32[128,2048]{1,0:T(8,128)S(1)}, bf16[144,2048]{1,0:T(8,128)(2,1)}, f32[8,2048]{1,0:T(8,128)}, f32[8,2048]{1,0:T(8,128)S(1)}) custom-call(s32[1]{0:T(128)} %bitcast.22.place_ref, f32[8,2048]{1,0:T(8,128)S(1)} %get-tuple-element.144.log_ref, f32[128,2048]{1,0:T(8,128)S(1)} %copy-done.61, ...), custom_call_target="tpu_custom_call" | custom-call | bytes 4718592 | tf_op jit(solution)/shard_map/pallas_call | solution.py:748
  176.6 1.5 collective-permute-start.23
  180.7 2.2 fusion.1
  183.3 8.0 %shard_map.124.g_ref = bf16[2048,512]{1,0:T(8,128)(2,1)S(1)} custom-call(f32[32,512]{1,0:T(8,128)S(1)} %copy-done.137, f32[4,512,8]{2,1,0:T(8,128)S(1)} %get-tuple-element.114.rt_ref, bf16[512,2048]{1,0:T(8,128)(2,1)S(1)} %copy-done.4, bf16[512,128]{1,0:T(8,128)(2,1)S(1)} %copy-done.48, bf16[512,128]{1,0:T(8,128)(2,1)S(1)} %copy-done.37, ...), custom_call_target="tpu_custom_call" | custom-call | flops 2147483648 | bytes 6291456 | tf_op jit(solution)/shard_map/pallas_call | solution.py:998
  191.3 10.5 %collective-permute-done.20.refs_0_ = bf16[256,1024]{1,0:T(8,128)(2,1)S(1)} collective-permute-done((bf16[256,1024]{1,0:T(8,128)(2,1)}, bf16[256,1024]{1,0:T(8,128)(2,1)S(1)}, u32[]{:S(2)}, u32[]{:S(2)}) %collective-permute-start.20) | collective-permute-done | bytes 524320 | tf_op jit(solution)/shard_map/ppermute | solution.py:473
  203.0 9.3 %shard_map.126 = (bf16[512,2048]{1,0:T(8,128)(2,1)S(1)}, bf16[512,2048]{1,0:T(8,128)(2,1)S(1)}) custom-call(s32[9]{0:T(128)S(1)} %bitcast.33, bf16[2048,512]{1,0:T(8,128)(2,1)S(1)} %shard_map.124.g_ref, bf16[256,2048]{1,0:T(8,128)(2,1)S(1)} %copy-done.146, bf16[256,2048]{1,0:T(8,128)(2,1)} %collective-permute-done.5.refs_4_.refs_1_, ...), custom_call_target="tpu_custom_call" | custom-call | flops 4831838208 | bytes 9437184 | tf_op jit(solution)/shard_map/pallas_call | solution.py:703
  212.4 1.3 copy-done.13
  213.7 4.8 %shard_map.125 = (bf16[512,1024]{1,0:T(8,128)(2,1)S(1)}, f32[2,128,1024]{2,1,0:T(8,128)S(1)}, f32[128,1024]{1,0:T(8,128)S(1)}, bf16[128,1024]{1,0:T(8,128)(2,1)S(1)}) custom-call(bf16[512,1792]{1,0:T(8,128)(2,1)S(1)} %copy-done.19, f32[512,2048]{1,0:T(8,128)S(1)} %copy-done.1, f32[4,512,8]{2,1,0:T(8,128)S(1)} %get-tuple-element.114.rt_ref, ...), custom_call_target="tpu_custom_call" | custom-call | flops 1879048192 | bytes 3670016 | tf_op jit(solution)/shard_map/pallas_call | solution.py:667
  222.8 1.6 collective-permute-start.26
  229.1 6.9 %shard_map.129 = (f32[16,512]{1,0:T(8,128)S(1)}, f32[512,128]{1,0:T(8,128)S(1)}, f32[512,128]{1,0:T(8,128)S(1)}) custom-call(f32[32,512]{1,0:T(8,128)S(1)} %copy-done.138, f32[4,512,8]{2,1,0:T(8,128)S(1)} %get-tuple-element.114.rt_ref, bf16[512,2048]{1,0:T(8,128)(2,1)S(1)} %copy-done.4, bf16[512,1024]{1,0:T(8,128)(2,1)S(1)} %copy-done.77, ...), custom_call_target="tpu_custom_call" | custom-call | flops 1610612736 | bytes 3145728 | tf_op jit(solution)/shard_map/pallas_call | solution.py:825
  236.7 1.5 collective-permute-done.28.got_ref
  240.9 2.2 copy-done.2
  243.1 1.5 copy-done.20
  246.7 4.3 %shard_map.131 = (bf16[512,1024]{1,0:T(8,128)(2,1)S(1)}, f32[2,128,1024]{2,1,0:T(8,128)S(1)}, f32[128,1024]{1,0:T(8,128)S(1)}, bf16[128,1024]{1,0:T(8,128)(2,1)S(1)}) custom-call(bf16[512,1792]{1,0:T(8,128)(2,1)S(1)} %copy-done.20, f32[512,2048]{1,0:T(8,128)S(1)} %copy-done.2, f32[4,512,8]{2,1,0:T(8,128)S(1)} %get-tuple-element.114.rt_ref, ...), custom_call_target="tpu_custom_call" | custom-call | flops 1879048192 | bytes 3670016 | tf_op jit(solution)/shard_map/pallas_call | solution.py:667
  254.5 1.5 collective-permute-start.30
  256.5 1.6 copy-done.6
  258.1 1.6 copy-done.14
  266.0 1.6 copy-done.148
  267.6 8.3 %shard_map.133 = (bf16[512,2048]{1,0:T(8,128)(2,1)S(1)}, bf16[512,2048]{1,0:T(8,128)(2,1)S(1)}) custom-call(s32[7]{0:T(128)S(1)} %slice.74.order_ref, bf16[2048,512]{1,0:T(8,128)(2,1)S(1)} %copy-done.148, bf16[256,1024]{1,0:T(8,128)(2,1)S(1)} %copy-done.111, ...), custom_call_target="tpu_custom_call", output_to_operand_aliasing={{0}: (16, {}), {1}: (17, {})} | custom-call | flops 3758096384 | bytes 7340032 | tf_op jit(solution)/shard_map/pallas_call | solution.py:703
  275.8 1.3 copy-done.7
  277.1 1.3 copy-done.15
  282.8 1.5 collective-permute-start.32
  284.3 1.9 collective-permute-start.31
  291.4 6.9 %shard_map.139 = (f32[16,512]{1,0:T(8,128)S(1)}, f32[512,128]{1,0:T(8,128)S(1)}, f32[512,128]{1,0:T(8,128)S(1)}) custom-call(f32[32,512]{1,0:T(8,128)S(1)} %copy-done.139, f32[4,512,8]{2,1,0:T(8,128)S(1)} %get-tuple-element.114.rt_ref, bf16[512,2048]{1,0:T(8,128)(2,1)S(1)} %copy-done.4, bf16[512,1024]{1,0:T(8,128)(2,1)S(1)} %copy-done.28, ...), custom_call_target="tpu_custom_call" | custom-call | flops 1610612736 | bytes 3145728 | tf_op jit(solution)/shard_map/pallas_call | solution.py:825
  303.9 1.3 copy-done.149
  305.2 3.4 collective-permute-start.36
  309.7 4.5 %add_convert_fusion.refs_2_ = bf16[512,2048]{1,0:T(8,128)(2,1)} fusion(bf16[512,2048]{1,0:T(8,128)(2,1)} %get-tuple-element.199, bf16[512,2048]{1,0:T(8,128)(2,1)} %copy-done.15), kind=kLoop, calls=%fused_computation | loop fusion | flops 4194304 | bytes 6291456 | tf_op jit(solution)/shard_map/convert_element_type | solution.py:980
  315.0 7.2 %collective-permute-done.35.got_ref = bf16[128,1024]{1,0:T(8,128)(2,1)S(1)} collective-permute-done((bf16[128,1024]{1,0:T(8,128)(2,1)}, bf16[128,1024]{1,0:T(8,128)(2,1)S(1)}, u32[]{:S(2)}, u32[]{:S(2)}) %collective-permute-start.35) | collective-permute-done | bytes 262176 | tf_op jit(solution)/shard_map/ppermute | solution.py:473
  330.2 4.0 %shard_map.145 = (f32[32,512]{1,0:T(8,128)}, f32[512,128]{1,0:T(8,128)S(1)}) custom-call(f32[4,512,8]{2,1,0:T(8,128)S(1)} %get-tuple-element.114.rt_ref, bf16[512,2048]{1,0:T(8,128)(2,1)S(1)} %copy-done.4, bf16[512,128]{1,0:T(8,128)(2,1)S(1)} %copy-done.37, f32[128,1024]{1,0:T(8,128)S(1)} %copy-done.23, f32[2,128,1024]{2,1,0:T(8,128)S(1)} %copy-done.72, ...), custom_call_target="tpu_custom_call" | custom-call | flops 268435456 | bytes 3145728 | tf_op jit(solution)/shard_map/pallas_call | solution.py:843
  334.2 5.3 %collective-permute-done.37.got_ref = bf16[128,1024]{1,0:T(8,128)(2,1)S(1)} collective-permute-done((bf16[128,1024]{1,0:T(8,128)(2,1)}, bf16[128,1024]{1,0:T(8,128)(2,1)S(1)}, u32[]{:S(2)}, u32[]{:S(2)}) %collective-permute-start.37) | collective-permute-done | bytes 262176 | tf_op jit(solution)/shard_map/ppermute | solution.py:473
  339.8 4.0 %shard_map.146 = (f32[32,512]{1,0:T(8,128)}, f32[512,128]{1,0:T(8,128)S(1)}) custom-call(f32[4,512,8]{2,1,0:T(8,128)S(1)} %get-tuple-element.114.rt_ref, bf16[512,2048]{1,0:T(8,128)(2,1)S(1)} %copy-done.4, bf16[512,128]{1,0:T(8,128)(2,1)S(1)} %copy-done.37, f32[128,1024]{1,0:T(8,128)S(1)} %shard_map.144.s_ref, ...), custom_call_target="tpu_custom_call", output_to_operand_aliasing={{0}: (9, {})} | custom-call | flops 268435456 | bytes 3145728 | tf_op jit(solution)/shard_map/pallas_call | solution.py:843
  343.8 1.3 collective-permute-done.38
  (378 shorter events, 87.6 us)
Async XLA Ops:
  0.6 20.7 %collective-permute-start.3 = (bf16[512,2048]{1,0:T(8,128)(2,1)}, bf16[512,2048]{1,0:T(8,128)(2,1)S(1)}, u32[]{:S(2)}, u32[]{:S(2)}) collective-permute-start(bf16[512,2048]{1,0:T(8,128)(2,1)} %own_ref.1), channel_id=1, source_target_pairs={{0,1},{1,0},{2,3},{3,2},{4,5},{5,4},{6,7},{7,6},{8,9},{9,8},{10,11... | collective-permute-start | bytes 6291464 | tf_op jit(solution)/shard_map/ppermute | solution.py:473
  1.1 44.6 %collective-permute-start.5 = (bf16[256,2048]{1,0:T(8,128)(2,1)}, bf16[256,2048]{1,0:T(8,128)(2,1)}, u32[]{:S(2)}, u32[]{:S(2)}) collective-permute-start(bf16[256,2048]{1,0:T(8,128)(2,1)} %refs_0_.3), channel_id=1, source_target_pairs={{0,2},{2,0},{4,6},{6,4},{8,10},{10,8},{12,14},{14,12},{16,18},{18,... | collective-permute-start | bytes 3145736 | tf_op jit(solution)/shard_map/ppermute | solution.py:473
  3.7 42.0 %collective-permute-start = (bf16[256,2048]{1,0:T(8,128)(2,1)}, bf16[256,2048]{1,0:T(8,128)(2,1)}, u32[]{:S(2)}, u32[]{:S(2)}) collective-permute-start(bf16[256,2048]{1,0:T(8,128)(2,1)} %refs_0_.3), channel_id=1, source_target_pairs={{0,8},{2,10},{4,12},{6,14},{8,0},{10,2},{12,4},{14,6},{16,24},{18,... | collective-permute-start | bytes 3145736 | tf_op jit(solution)/shard_map/ppermute | solution.py:473
  5.3 40.4 %collective-permute-start.1 = (bf16[256,2048]{1,0:T(8,128)(2,1)}, bf16[256,2048]{1,0:T(8,128)(2,1)}, u32[]{:S(2)}, u32[]{:S(2)}) collective-permute-start(bf16[256,2048]{1,0:T(8,128)(2,1)} %refs_0_.3), channel_id=1, source_target_pairs={{8,16},{10,18},{12,20},{14,22},{16,8},{18,10},{20,12},{22,14},{9,1... | collective-permute-start | bytes 3145736 | tf_op jit(solution)/shard_map/ppermute | solution.py:533
  6.9 38.8 %collective-permute-start.2 = (bf16[256,2048]{1,0:T(8,128)(2,1)}, bf16[256,2048]{1,0:T(8,128)(2,1)}, u32[]{:S(2)}, u32[]{:S(2)}) collective-permute-start(bf16[256,2048]{1,0:T(8,128)(2,1)} %refs_0_.3), channel_id=1, source_target_pairs={{0,4},{2,6},{4,0},{6,2},{8,12},{10,14},{12,8},{14,10},{16,20},{18,... | collective-permute-start | bytes 3145736 | tf_op jit(solution)/shard_map/ppermute | solution.py:473
  22.7 17.6 %collective-permute-start.4 = (bf16[144,2048]{1,0:T(8,128)(2,1)}, bf16[144,2048]{1,0:T(8,128)(2,1)S(1)}, u32[]{:S(2)}, u32[]{:S(2)}) collective-permute-start(bf16[144,2048]{1,0:T(8,128)(2,1)} %shard_map.113), channel_id=1, source_target_pairs={{0,2},{2,0},{4,6},{6,4},{8,10},{10,8},{12,14},{14,12},{16,18},{18,... | collective-permute-start | bytes 1769480 | tf_op jit(solution)/shard_map/ppermute | solution.py:473
  45.8 43.8 %collective-permute-start.10 = (bf16[256,2048]{1,0:T(8,128)(2,1)}, bf16[256,2048]{1,0:T(8,128)(2,1)}, u32[]{:S(2)}, u32[]{:S(2)}) collective-permute-start(bf16[256,2048]{1,0:T(8,128)(2,1)} %get-tuple-element.122.refs_3_), channel_id=1, source_target_pairs={{0,4},{2,6},{4,0},{6,2},{8,12},{10,14},{12,8},{14,10},{16,20},{18,... | collective-permute-start | bytes 3145736 | tf_op jit(solution)/shard_map/ppermute | solution.py:473
  47.6 41.9 %collective-permute-start.6 = (bf16[256,2048]{1,0:T(8,128)(2,1)}, bf16[256,2048]{1,0:T(8,128)(2,1)}, u32[]{:S(2)}, u32[]{:S(2)}) collective-permute-start(bf16[256,2048]{1,0:T(8,128)(2,1)} %get-tuple-element.122.refs_3_), channel_id=1, source_target_pairs={{8,16},{10,18},{12,20},{14,22},{16,8},{18,10},{20,12},{22,14},{9,1... | collective-permute-start | bytes 3145736 | tf_op jit(solution)/shard_map/ppermute | solution.py:533
  49.3 40.3 %collective-permute-start.8 = (bf16[256,2048]{1,0:T(8,128)(2,1)}, bf16[256,2048]{1,0:T(8,128)(2,1)}, u32[]{:S(2)}, u32[]{:S(2)}) collective-permute-start(bf16[256,2048]{1,0:T(8,128)(2,1)} %get-tuple-element.122.refs_3_), channel_id=1, source_target_pairs={{0,2},{2,0},{4,6},{6,4},{8,10},{10,8},{12,14},{14,12},{16,18},{18,... | collective-permute-start | bytes 3145736 | tf_op jit(solution)/shard_map/ppermute | solution.py:473
  50.8 38.8 %collective-permute-start.7 = (bf16[256,2048]{1,0:T(8,128)(2,1)}, bf16[256,2048]{1,0:T(8,128)(2,1)}, u32[]{:S(2)}, u32[]{:S(2)}) collective-permute-start(bf16[256,2048]{1,0:T(8,128)(2,1)} %get-tuple-element.121.refs_0_), channel_id=1, source_target_pairs={{8,0},{10,2},{12,4},{14,6},{16,24},{18,26},{20,28},{22,30},{9,1},{... | collective-permute-start | bytes 3145736 | tf_op jit(solution)/shard_map/ppermute | solution.py:533
  52.2 31.5 %collective-permute-start.9 = (bf16[144,2048]{1,0:T(8,128)(2,1)}, bf16[144,2048]{1,0:T(8,128)(2,1)}, u32[]{:S(2)}, u32[]{:S(2)}) collective-permute-start(bf16[144,2048]{1,0:T(8,128)(2,1)} %get-tuple-element.125), channel_id=1, source_target_pairs={{0,4},{2,6},{4,0},{6,2},{8,12},{10,14},{12,8},{14,10},{16,20},{18,... | collective-permute-start | bytes 1769480 | tf_op jit(solution)/shard_map/ppermute | solution.py:473
  60.5 25.6 %copy-start.18 = (bf16[512,1792]{1,0:T(8,128)(2,1)}, bf16[512,1792]{1,0:T(8,128)(2,1)S(1)}, u32[]{:S(2)}) copy-start(bf16[512,1792]{1,0:T(8,128)(2,1)S(1)} %get-tuple-element.154.f_ref) | copy-start | bytes 5505028
  60.5 23.2 %copy-start.57 = (f32[128,2048]{1,0:T(8,128)S(1)}, f32[128,2048]{1,0:T(8,128)}, u32[]{:S(2)}) copy-start(f32[128,2048]{1,0:T(8,128)} %copy-done.56) | copy-start | bytes 3145732
  60.5 23.2 %copy-start.59 = (f32[128,2048]{1,0:T(8,128)S(1)}, f32[128,2048]{1,0:T(8,128)}, u32[]{:S(2)}) copy-start(f32[128,2048]{1,0:T(8,128)} %copy-done.58) | copy-start | bytes 3145732
  89.6 43.3 %copy-start.65 = (f32[128,2048]{1,0:T(8,128)S(1)}, f32[128,2048]{1,0:T(8,128)}, u32[]{:S(2)}) copy-start(f32[128,2048]{1,0:T(8,128)} %copy-done.64) | copy-start | bytes 3145732
  89.6 43.3 %copy-start.67 = (f32[128,2048]{1,0:T(8,128)S(1)}, f32[128,2048]{1,0:T(8,128)}, u32[]{:S(2)}) copy-start(f32[128,2048]{1,0:T(8,128)} %copy-done.66) | copy-start | bytes 3145732
  91.7 43.1 %copy-start.51 = (bf16[256,2048]{1,0:T(8,128)(2,1)}, bf16[256,2048]{1,0:T(8,128)(2,1)S(1)}, u32[]{:S(2)}) copy-start(bf16[256,2048]{1,0:T(8,128)(2,1)S(1)} %add.123.refs_6_) | copy-start | bytes 3145732
  91.7 45.7 %collective-permute-start.12 = (bf16[256,2048]{1,0:T(8,128)(2,1)S(1)}, bf16[256,2048]{1,0:T(8,128)(2,1)S(1)}, u32[]{:S(2)}, u32[]{:S(2)}) collective-permute-start(bf16[256,2048]{1,0:T(8,128)(2,1)S(1)} %add.123.refs_6_), channel_id=1, source_target_pairs={{0,4},{2,6},{4,0},{6,2},{8,12},{10,14},{12,8},{14,10},{16,20},{18,... | collective-permute-start | bytes 3145736 | tf_op jit(solution)/shard_map/ppermute | solution.py:473
  93.4 44.0 %collective-permute-start.14 = (bf16[256,2048]{1,0:T(8,128)(2,1)S(1)}, bf16[256,2048]{1,0:T(8,128)(2,1)S(1)}, u32[]{:S(2)}, u32[]{:S(2)}) collective-permute-start(bf16[256,2048]{1,0:T(8,128)(2,1)S(1)} %add.123.refs_6_), channel_id=1, source_target_pairs={{0,2},{2,0},{4,6},{6,4},{8,10},{10,8},{12,14},{14,12},{16,18},{18,... | collective-permute-start | bytes 3145736 | tf_op jit(solution)/shard_map/ppermute | solution.py:473
  94.9 43.6 %collective-permute-start.11 = (bf16[256,2048]{1,0:T(8,128)(2,1)}, bf16[256,2048]{1,0:T(8,128)(2,1)S(1)}, u32[]{:S(2)}, u32[]{:S(2)}) collective-permute-start(bf16[256,2048]{1,0:T(8,128)(2,1)} %get-tuple-element.131.refs_0_), channel_id=1, source_target_pairs={{8,0},{10,2},{12,4},{14,6},{16,24},{18,26},{20,28},{22,30},{9,1},{... | collective-permute-start | bytes 3145736 | tf_op jit(solution)/shard_map/ppermute | solution.py:533
  96.2 36.7 %collective-permute-start.13 = (bf16[144,2048]{1,0:T(8,128)(2,1)S(1)}, bf16[144,2048]{1,0:T(8,128)(2,1)S(1)}, u32[]{:S(2)}, u32[]{:S(2)}) collective-permute-start(bf16[144,2048]{1,0:T(8,128)(2,1)S(1)} %copy-done.79), channel_id=1, source_target_pairs={{0,8},{2,10},{4,12},{6,14},{8,0},{10,2},{12,4},{14,6},{16,24},{18,... | collective-permute-start | bytes 1769480 | tf_op jit(solution)/shard_map/ppermute | solution.py:473
  142.1 32.4 %collective-permute-start.15 = (bf16[256,1024]{1,0:T(8,128)(2,1)}, bf16[256,1024]{1,0:T(8,128)(2,1)}, u32[]{:S(2)}, u32[]{:S(2)}) collective-permute-start(bf16[256,1024]{1,0:T(8,128)(2,1)} %get-tuple-element.223.refs_3_.refs_6_), channel_id=1, source_target_pairs={{0,2},{2,0},{4,6},{6,4},{8,10},{10,8},{12,14},{14,12},{16,18},{18,... | collective-permute-start | bytes 1572872 | tf_op jit(solution)/shard_map/ppermute | solution.py:473
  142.7 31.8 %collective-permute-start.17 = (bf16[256,1024]{1,0:T(8,128)(2,1)}, bf16[256,1024]{1,0:T(8,128)(2,1)S(1)}, u32[]{:S(2)}, u32[]{:S(2)}) collective-permute-start(bf16[256,1024]{1,0:T(8,128)(2,1)} %get-tuple-element.223.refs_3_.refs_6_), channel_id=1, source_target_pairs={{0,4},{2,6},{4,0},{6,2},{8,12},{10,14},{12,8},{14,10},{16,20},{18,... | collective-permute-start | bytes 1572872 | tf_op jit(solution)/shard_map/ppermute | solution.py:473
  143.3 26.0 %collective-permute-start.16 = (bf16[144,2048]{1,0:T(8,128)(2,1)}, bf16[144,2048]{1,0:T(8,128)(2,1)}, u32[]{:S(2)}, u32[]{:S(2)}) collective-permute-start(bf16[144,2048]{1,0:T(8,128)(2,1)} %get-tuple-element.146), channel_id=1, source_target_pairs={{0,16},{2,18},{4,20},{6,22},{8,24},{10,26},{12,28},{14,30},{16,0},... | collective-permute-start | bytes 1769480 | tf_op jit(solution)/shard_map/ppermute | solution.py:473
  146.0 28.5 %collective-permute-start.18 = (bf16[256,1024]{1,0:T(8,128)(2,1)}, bf16[256,1024]{1,0:T(8,128)(2,1)S(1)}, u32[]{:S(2)}, u32[]{:S(2)}) collective-permute-start(bf16[256,1024]{1,0:T(8,128)(2,1)} %get-tuple-element.226), channel_id=1, source_target_pairs={{0,2},{2,0},{4,6},{6,4},{8,10},{10,8},{12,14},{14,12},{16,18},{18,... | collective-permute-start | bytes 1572872 | tf_op jit(solution)/shard_map/ppermute | solution.py:473
  147.5 27.0 %collective-permute-start.19 = (bf16[256,1024]{1,0:T(8,128)(2,1)}, bf16[256,1024]{1,0:T(8,128)(2,1)}, u32[]{:S(2)}, u32[]{:S(2)}) collective-permute-start(bf16[256,1024]{1,0:T(8,128)(2,1)} %get-tuple-element.149), channel_id=1, source_target_pairs={{0,4},{2,6},{4,0},{6,2},{8,12},{10,14},{12,8},{14,10},{16,20},{18,... | collective-permute-start | bytes 1572872 | tf_op jit(solution)/shard_map/ppermute | solution.py:473
  155.1 14.2 %copy-start.61 = (f32[128,2048]{1,0:T(8,128)S(1)}, f32[128,2048]{1,0:T(8,128)}, u32[]{:S(2)}) copy-start(f32[128,2048]{1,0:T(8,128)} %copy-done.60) | copy-start | bytes 3145732
  155.1 14.2 %copy-start.63 = (f32[128,2048]{1,0:T(8,128)S(1)}, f32[128,2048]{1,0:T(8,128)}, u32[]{:S(2)}) copy-start(f32[128,2048]{1,0:T(8,128)} %copy-done.62) | copy-start | bytes 3145732
  175.5 46.5 %collective-permute-start.21 = (bf16[256,1024]{1,0:T(8,128)(2,1)}, bf16[256,1024]{1,0:T(8,128)(2,1)S(1)}, u32[]{:S(2)}, u32[]{:S(2)}) collective-permute-start(bf16[256,1024]{1,0:T(8,128)(2,1)} %get-tuple-element.153.refs_3_.refs_7_), channel_id=1, source_target_pairs={{0,2},{2,0},{4,6},{6,4},{8,10},{10,8},{12,14},{14,12},{16,18},{18,... | collective-permute-start | bytes 1572872 | tf_op jit(solution)/shard_map/ppermute | solution.py:473
  176.6 46.1 %collective-permute-start.23 = (bf16[256,1024]{1,0:T(8,128)(2,1)}, bf16[256,1024]{1,0:T(8,128)(2,1)}, u32[]{:S(2)}, u32[]{:S(2)}) collective-permute-start(bf16[256,1024]{1,0:T(8,128)(2,1)} %get-tuple-element.153.refs_3_.refs_7_), channel_id=1, source_target_pairs={{0,4},{2,6},{4,0},{6,2},{8,12},{10,14},{12,8},{14,10},{16,20},{18,... | collective-permute-start | bytes 1572872 | tf_op jit(solution)/shard_map/ppermute | solution.py:473
  178.2 23.6 %collective-permute-start.20 = (bf16[256,1024]{1,0:T(8,128)(2,1)}, bf16[256,1024]{1,0:T(8,128)(2,1)S(1)}, u32[]{:S(2)}, u32[]{:S(2)}) collective-permute-start(bf16[256,1024]{1,0:T(8,128)(2,1)} %get-tuple-element.151), channel_id=1, source_target_pairs={{0,2},{2,0},{4,6},{6,4},{8,10},{10,8},{12,14},{14,12},{16,18},{18,... | collective-permute-start | bytes 1572872 | tf_op jit(solution)/shard_map/ppermute | solution.py:473
  178.7 35.0 %collective-permute-start.22 = (bf16[256,1024]{1,0:T(8,128)(2,1)}, bf16[256,1024]{1,0:T(8,128)(2,1)S(1)}, u32[]{:S(2)}, u32[]{:S(2)}) collective-permute-start(bf16[256,1024]{1,0:T(8,128)(2,1)} %get-tuple-element.155.refs_4_.refs_8_), channel_id=1, source_target_pairs={{0,4},{2,6},{4,0},{6,2},{8,12},{10,14},{12,8},{14,10},{16,20},{18,... | collective-permute-start | bytes 1572872 | tf_op jit(solution)/shard_map/ppermute | solution.py:473
  179.5 43.2 %collective-permute-start.24 = (bf16[256,1024]{1,0:T(8,128)(2,1)}, bf16[256,1024]{1,0:T(8,128)(2,1)}, u32[]{:S(2)}, u32[]{:S(2)}) collective-permute-start(bf16[256,1024]{1,0:T(8,128)(2,1)} %get-tuple-element.158), channel_id=1, source_target_pairs={{0,2},{2,0},{4,6},{6,4},{8,10},{10,8},{12,14},{14,12},{16,18},{18,... | collective-permute-start | bytes 1572872 | tf_op jit(solution)/shard_map/ppermute | solution.py:473
  183.2 18.6 %copy-start.150 = (bf16[256,1024]{1,0:T(8,128)(2,1)S(1)}, bf16[256,1024]{1,0:T(8,128)(2,1)}, u32[]{:S(2)}) copy-start(bf16[256,1024]{1,0:T(8,128)(2,1)} %get-tuple-element.159) | copy-start | bytes 1572868
  183.3 19.7 %copy-start.31 = (bf16[256,2048]{1,0:T(8,128)(2,1)S(1)}, bf16[256,2048]{1,0:T(8,128)(2,1)}, u32[]{:S(2)}) copy-start(bf16[256,2048]{1,0:T(8,128)(2,1)} %get-tuple-element.142.refs_8_) | copy-start | bytes 3145732
  183.3 19.7 %copy-start.53 = (bf16[256,2048]{1,0:T(8,128)(2,1)S(1)}, bf16[256,2048]{1,0:T(8,128)(2,1)}, u32[]{:S(2)}) copy-start(bf16[256,2048]{1,0:T(8,128)(2,1)} %copy-done.51) | copy-start | bytes 3145732
  183.3 19.7 %copy-start.75 = (bf16[256,2048]{1,0:T(8,128)(2,1)S(1)}, bf16[256,2048]{1,0:T(8,128)(2,1)}, u32[]{:S(2)}) copy-start(bf16[256,2048]{1,0:T(8,128)(2,1)} %copy-done.73) | copy-start | bytes 3145732
  183.3 19.7 %copy-start.146 = (bf16[256,2048]{1,0:T(8,128)(2,1)S(1)}, bf16[256,2048]{1,0:T(8,128)(2,1)}, u32[]{:S(2)}) copy-start(bf16[256,2048]{1,0:T(8,128)(2,1)} %refs_0_.3) | copy-start | bytes 3145732
  191.3 21.0 %copy-start.147 = (bf16[2048,512]{1,0:T(8,128)(2,1)}, bf16[2048,512]{1,0:T(8,128)(2,1)S(1)}, u32[]{:S(2)}) copy-start(bf16[2048,512]{1,0:T(8,128)(2,1)S(1)} %shard_map.124.g_ref) | copy-start | bytes 6291460
  201.8 11.9 %copy-start.110 = (bf16[256,1024]{1,0:T(8,128)(2,1)}, bf16[256,1024]{1,0:T(8,128)(2,1)S(1)}, u32[]{:S(2)}) copy-start(bf16[256,1024]{1,0:T(8,128)(2,1)S(1)} %collective-permute-done.20.refs_0_) | copy-start | bytes 1572868
  201.8 21.0 %collective-permute-start.25 = (bf16[256,1024]{1,0:T(8,128)(2,1)S(1)}, bf16[256,1024]{1,0:T(8,128)(2,1)}, u32[]{:S(2)}, u32[]{:S(2)}) collective-permute-start(bf16[256,1024]{1,0:T(8,128)(2,1)S(1)} %copy-done.150), channel_id=1, source_target_pairs={{0,4},{2,6},{4,0},{6,2},{8,12},{10,14},{12,8},{14,10},{16,20},{18,... | collective-permute-start | bytes 1572872 | tf_op jit(solution)/shard_map/ppermute | solution.py:473
  203.0 10.7 %copy-start.1 = (f32[512,2048]{1,0:T(8,128)S(1)}, f32[512,2048]{1,0:T(8,128)}, u32[]{:S(2)}) copy-start(f32[512,2048]{1,0:T(8,128)} %copy-done) | copy-start | bytes 12582916
  222.8 18.1 %collective-permute-start.26 = (bf16[256,1024]{1,0:T(8,128)(2,1)}, bf16[256,1024]{1,0:T(8,128)(2,1)}, u32[]{:S(2)}, u32[]{:S(2)}) collective-permute-start(bf16[256,1024]{1,0:T(8,128)(2,1)} %get-tuple-element.161), channel_id=1, source_target_pairs={{0,2},{2,0},{4,6},{6,4},{8,10},{10,8},{12,14},{14,12},{16,18},{18,... | collective-permute-start | bytes 1572872 | tf_op jit(solution)/shard_map/ppermute | solution.py:473
  224.3 16.6 %collective-permute-start.27 = (bf16[256,1024]{1,0:T(8,128)(2,1)}, bf16[256,1024]{1,0:T(8,128)(2,1)}, u32[]{:S(2)}, u32[]{:S(2)}) collective-permute-start(bf16[256,1024]{1,0:T(8,128)(2,1)} %get-tuple-element.162.refs_4_.refs_9_), channel_id=1, source_target_pairs={{0,4},{2,6},{4,0},{6,2},{8,12},{10,14},{12,8},{14,10},{16,20},{18,... | collective-permute-start | bytes 1572872 | tf_op jit(solution)/shard_map/ppermute | solution.py:473
  224.9 13.4 %collective-permute-start.28 = (bf16[128,1024]{1,0:T(8,128)(2,1)}, bf16[128,1024]{1,0:T(8,128)(2,1)S(1)}, u32[]{:S(2)}, u32[]{:S(2)}) collective-permute-start(bf16[128,1024]{1,0:T(8,128)(2,1)} %get-tuple-element.165), channel_id=1, source_target_pairs={{0,2},{2,0},{4,6},{6,4},{8,10},{10,8},{12,14},{14,12},{16,18},{18,... | collective-permute-start | bytes 786440 | tf_op jit(solution)/shard_map/ppermute | solution.py:473
  254.5 24.0 %collective-permute-start.30 = (bf16[128,1024]{1,0:T(8,128)(2,1)}, bf16[128,1024]{1,0:T(8,128)(2,1)S(1)}, u32[]{:S(2)}, u32[]{:S(2)}) collective-permute-start(bf16[128,1024]{1,0:T(8,128)(2,1)} %get-tuple-element.184), channel_id=1, source_target_pairs={{0,2},{2,0},{4,6},{6,4},{8,10},{10,8},{12,14},{14,12},{16,18},{18,... | collective-permute-start | bytes 786440 | tf_op jit(solution)/shard_map/ppermute | solution.py:473
  256.0 23.6 %collective-permute-start.29 = (bf16[128,1024]{1,0:T(8,128)(2,1)}, bf16[128,1024]{1,0:T(8,128)(2,1)S(1)}, u32[]{:S(2)}, u32[]{:S(2)}) collective-permute-start(bf16[128,1024]{1,0:T(8,128)(2,1)} %get-tuple-element.179), channel_id=1, source_target_pairs={{0,4},{2,6},{4,0},{6,2},{8,12},{10,14},{12,8},{14,10},{16,20},{18,... | collective-permute-start | bytes 786440 | tf_op jit(solution)/shard_map/ppermute | solution.py:473
  267.5 11.0 %copy-start.101 = (f32[128,1024]{1,0:T(8,128)S(1)}, f32[128,1024]{1,0:T(8,128)}, u32[]{:S(2)}) copy-start(f32[128,1024]{1,0:T(8,128)} %copy-done.100) | copy-start | bytes 1572868
  267.5 11.0 %copy-start.127 = (f32[8,2048]{1,0:T(8,128)S(1)}, f32[8,2048]{1,0:T(8,128)}, u32[]{:S(2)}) copy-start(f32[8,2048]{1,0:T(8,128)} %copy-done.125) | copy-start | bytes 196612
  267.5 12.1 %copy-start.83 = (f32[128,1024]{1,0:T(8,128)S(1)}, f32[128,1024]{1,0:T(8,128)}, u32[]{:S(2)}) copy-start(f32[128,1024]{1,0:T(8,128)} %copy-done.82) | copy-start | bytes 1572868
  267.5 12.1 %copy-start.85 = (f32[128,1024]{1,0:T(8,128)S(1)}, f32[128,1024]{1,0:T(8,128)}, u32[]{:S(2)}) copy-start(f32[128,1024]{1,0:T(8,128)} %copy-done.84) | copy-start | bytes 1572868
  267.6 12.1 %copy-start.129 = (f32[8,2048]{1,0:T(8,128)S(1)}, f32[8,2048]{1,0:T(8,128)}, u32[]{:S(2)}) copy-start(f32[8,2048]{1,0:T(8,128)} %copy-done.128) | copy-start | bytes 196612
  282.8 21.1 %collective-permute-start.33 = (bf16[512,2048]{1,0:T(8,128)(2,1)}, bf16[512,2048]{1,0:T(8,128)(2,1)S(1)}, u32[]{:S(2)}, u32[]{:S(2)}) collective-permute-start(bf16[512,2048]{1,0:T(8,128)(2,1)} %get-tuple-element.195), channel_id=1, source_target_pairs={{0,1},{1,0},{2,3},{3,2},{4,5},{5,4},{6,7},{7,6},{8,9},{9,8},{10,11... | collective-permute-start | bytes 6291464 | tf_op jit(solution)/shard_map/ppermute | solution.py:473
  282.8 16.3 %collective-permute-start.32 = (bf16[128,1024]{1,0:T(8,128)(2,1)}, bf16[128,1024]{1,0:T(8,128)(2,1)S(1)}, u32[]{:S(2)}, u32[]{:S(2)}) collective-permute-start(bf16[128,1024]{1,0:T(8,128)(2,1)} %get-tuple-element.192), channel_id=1, source_target_pairs={{0,4},{2,6},{4,0},{6,2},{8,12},{10,14},{12,8},{14,10},{16,20},{18,... | collective-permute-start | bytes 786440 | tf_op jit(solution)/shard_map/ppermute | solution.py:473
  284.3 16.8 %collective-permute-start.31 = (bf16[128,1024]{1,0:T(8,128)(2,1)}, bf16[128,1024]{1,0:T(8,128)(2,1)S(1)}, u32[]{:S(2)}, u32[]{:S(2)}) collective-permute-start(bf16[128,1024]{1,0:T(8,128)(2,1)} %get-tuple-element.188), channel_id=1, source_target_pairs={{0,8},{2,10},{4,12},{6,14},{8,0},{10,2},{12,4},{14,6},{16,24},{18,... | collective-permute-start | bytes 786440 | tf_op jit(solution)/shard_map/ppermute | solution.py:473
  305.2 19.0 %collective-permute-start.36 = (bf16[128,1024]{1,0:T(8,128)(2,1)}, bf16[128,1024]{1,0:T(8,128)(2,1)S(1)}, u32[]{:S(2)}, u32[]{:S(2)}) collective-permute-start(bf16[128,1024]{1,0:T(8,128)(2,1)} %get-tuple-element.208), channel_id=1, source_target_pairs={{0,16},{2,18},{4,20},{6,22},{8,24},{10,26},{12,28},{14,30},{16,0},... | collective-permute-start | bytes 786440 | tf_op jit(solution)/shard_map/ppermute | solution.py:473
  308.6 13.6 %collective-permute-start.35 = (bf16[128,1024]{1,0:T(8,128)(2,1)}, bf16[128,1024]{1,0:T(8,128)(2,1)S(1)}, u32[]{:S(2)}, u32[]{:S(2)}) collective-permute-start(bf16[128,1024]{1,0:T(8,128)(2,1)} %get-tuple-element.203), channel_id=1, source_target_pairs={{0,8},{2,10},{4,12},{6,14},{8,0},{10,2},{12,4},{14,6},{16,24},{18,... | collective-permute-start | bytes 786440 | tf_op jit(solution)/shard_map/ppermute | solution.py:473
  309.6 4.7 %collective-permute-start.34 = (bf16[512,128]{1,0:T(8,128)(2,1)S(1)}, bf16[512,128]{1,0:T(8,128)(2,1)S(1)}, u32[]{:S(2)}, u32[]{:S(2)}) collective-permute-start(bf16[512,128]{1,0:T(8,128)(2,1)S(1)} %convert_element_type.38), channel_id=1, source_target_pairs={{0,1},{1,0},{2,3},{3,2},{4,5},{5,4},{6,7},{7,6},{8,9},{9,8},{10,11... | collective-permute-start | bytes 393224 | tf_op jit(solution)/shard_map/ppermute | solution.py:473
  309.7 12.6 %copy-start.87 = (f32[128,1024]{1,0:T(8,128)S(1)}, f32[128,1024]{1,0:T(8,128)}, u32[]{:S(2)}) copy-start(f32[128,1024]{1,0:T(8,128)} %copy-done.86) | copy-start | bytes 1572868
  309.7 12.5 %copy-start.89 = (f32[128,1024]{1,0:T(8,128)S(1)}, f32[128,1024]{1,0:T(8,128)}, u32[]{:S(2)}) copy-start(f32[128,1024]{1,0:T(8,128)} %copy-done.88) | copy-start | bytes 1572868
  309.7 12.5 %copy-start.133 = (f32[8,2048]{1,0:T(8,128)S(1)}, f32[8,2048]{1,0:T(8,128)}, u32[]{:S(2)}) copy-start(f32[8,2048]{1,0:T(8,128)} %copy-done.131) | copy-start | bytes 196612
  309.7 14.6 %copy-start.135 = (f32[8,2048]{1,0:T(8,128)S(1)}, f32[8,2048]{1,0:T(8,128)}, u32[]{:S(2)}) copy-start(f32[8,2048]{1,0:T(8,128)} %copy-done.134) | copy-start | bytes 196612
  325.8 13.7 %collective-permute-start.37 = (bf16[128,1024]{1,0:T(8,128)(2,1)}, bf16[128,1024]{1,0:T(8,128)(2,1)S(1)}, u32[]{:S(2)}, u32[]{:S(2)}) collective-permute-start(bf16[128,1024]{1,0:T(8,128)(2,1)} %get-tuple-element.210), channel_id=1, source_target_pairs={{0,16},{2,18},{4,20},{6,22},{8,24},{10,26},{12,28},{14,30},{16,0},... | collective-permute-start | bytes 786440 | tf_op jit(solution)/shard_map/ppermute | solution.py:473
  343.8 1.4 collective-permute-start.38
  (129 other events, 355.9 us)

commit v8 on v7

--- a/solution.py
+++ b/solution.py
@@ -14,8 +14,7 @@
 WIDE = GROUP * P_SIZE
 LOG2E = 1.4426950408889634
 NEVER = -1e30
-GRANT = 24 * 2**20
-LARGE = 30 * 2**20
+GRANT = 64 * 2**20
 
 F32 = jnp.float32
 BF16 = jnp.bfloat16
@@ -524,6 +523,7 @@
         out_shape=[shape(*value.shape, dtype=value.dtype) for value in values],
         input_output_aliases={index: index for index in range(len(values))},
         cost_estimate=pl.CostEstimate(flops=0, bytes_accessed=0, transcendentals=0),
+        compiler_params=pltpu.CompilerParams(vmem_limit_bytes=GRANT),
     )(*values, *tokens)
     return list(out)
 
@@ -720,7 +720,7 @@
             transcendentals=0,
         ),
         compiler_params=pltpu.CompilerParams(
-            dimension_semantics=("arbitrary",), vmem_limit_bytes=LARGE
+            dimension_semantics=("arbitrary",), vmem_limit_bytes=GRANT
         ),
     )(order, grad_x, *arrays, *so_far)
 

time: 348 us -> 320 us (0.920)
  local copies, waits for them, and re-layouts: 97.2 us -> 12.4 us
  Pallas kernels: 84.2 us -> 134 us
  other arithmetic: 14.1 us -> 18.2 us
    unnamed x308 -> x8, local copies, waits for them, and re-layouts: 89.3 us -> 0.85 us
    pallas_call x8, Pallas kernels: 2.68 us -> 17.5 us  [scan_step(): call(scan_kernel, (columns // WIDE,), [pl.BlockSpec((8, WIDE), lambda h:...]
    pallas_call x4, Pallas kernels: 8.64 us -> 16 us  [back_step(): call(functools.partial(back_kernel, bit), (columns // WIDE,), [SCALARS] +...]
    pallas_call x2, Pallas kernels: 9.06 us -> 13.2 us  [late_forward(): call(functools.partial(late_forward_kernel, len(pieces)), (columns // WID...]
    pallas_call x2, Pallas kernels: 13.9 us -> 17.8 us  [inner(): call(inner_kernel, grid, specs + [SHARED] * len(so_far), [run_spec(), SHA...]
    pallas_call x1, Pallas kernels: 1.39 us -> 5.13 us  [local_layered(): call(arrange_kernel, (1,), [SCALARS] + [pl.BlockSpec((length, width // 2)...]
  transfers between devices with their start and end apart: 39 -> 39, of which waited for: 9 -> 9; matrix products, arithmetic and copies ran while one was open for 5% -> 7% of each run, Pallas kernels for 22% -> 36%
where the time goes in v8:
time: 320 us; the launch traced here: 318 us
  Pallas kernels  134 us (42%)
  waiting for transfers between devices  103 us (32%)
  starting transfers between devices  47.5 us (15%)
  other arithmetic  18.2 us (6%)
  local copies, waits for them, and re-layouts  12.4 us (4%)
  between operations  3.42 us (1%)
    ppermute x35, waiting for transfers between devices, swap(): return lax.ppermute(value, axis, [(i, i ^ bit) for i in range(count)])  103 us
    ppermute x35, starting transfers between devices, swap(): return lax.ppermute(value, axis, [(i, i ^ bit) for i in range(count)])  41.4 us
    pallas_call x2, Pallas kernels, multiply_blocks(): pl.pallas_call(functools.partial(blocks_kernel, [len(piece) for piece in...  19.8 us
    pallas_call x2, Pallas kernels, inner(): call(inner_kernel, grid, specs + [SHARED] * len(so_far), [run_spec(), SHA...  17.8 us
    pallas_call x8, Pallas kernels, scan_step(): call(scan_kernel, (columns // WIDE,), [pl.BlockSpec((8, WIDE), lambda h:...  17.5 us
    pallas_call x4, Pallas kernels, back_step(): call(functools.partial(back_kernel, bit), (columns // WIDE,), [SCALARS] +...  16 us
    pallas_call x2, Pallas kernels, late_forward(): call(functools.partial(late_forward_kernel, len(pieces)), (columns // WID...  13.2 us
    pallas_call x2, Pallas kernels, state_terms(): pl.pallas_call(state_kernel, grid=grid, in_specs=[run_t_spec(here), rows_...  11 us
  transfers between devices with their start and end apart: 39, of which 9 were waited for; matrix products, arithmetic and copies ran while one was open for 7% of the time, Pallas kernels for 36%

profile of v8, /device:TPU:0, one launch (start us, length us, event | category | flops | bytes accessed | tf_op | source)
XLA Modules:
  0.0 318.3 jit_solution(15905319232331376078)
XLA Ops:
  1.1 2.6 collective-permute-start.5
  3.7 1.6 collective-permute-start
  5.3 1.7 collective-permute-start.1
  6.9 1.5 collective-permute-start.2
  8.5 9.1 %shard_map.111 = (f32[32,512]{1,0:T(8,128)}, f32[4,512,8]{2,1,0:T(8,128)}, f32[2,8,2048]{2,1,0:T(8,128)}, f32[2,128,2048]{2,1,0:T(8,128)}) custom-call(f32[32,512]{1,0:T(8,128)} %d_ref.1, bf16[512,2048]{1,0:T(8,128)(2,1)} %g_ref.11, bf16[512,128]{1,0:T(8,128)(2,1)} %c_ref.11), custom_call_target="tpu_custom_call" | custom-call | flops 268435456 | bytes 6291456 | tf_op jit(solution)/shard_map/pallas_call | solution.py:797
  17.6 3.7 %shard_map.112 = (f32[128,2048]{1,0:T(8,128)}, f32[8,2048]{1,0:T(8,128)}, bf16[144,2048]{1,0:T(8,128)(2,1)}) custom-call(f32[2,128,2048]{2,1,0:T(8,128)} %get-tuple-element.115.own_ref, f32[2,8,2048]{2,1,0:T(8,128)} %get-tuple-element.116.kept_ref.a_ref), custom_call_target="tpu_custom_call" | custom-call | bytes 3670016 | tf_op jit(solution)/shard_map/pallas_call | solution.py:730
  21.9 18.5 %collective-permute-done.4.got_ref = bf16[144,2048]{1,0:T(8,128)(2,1)} collective-permute-done((bf16[144,2048]{1,0:T(8,128)(2,1)}, bf16[144,2048]{1,0:T(8,128)(2,1)}, u32[]{:S(2)}, u32[]{:S(2)}) %collective-permute-start.4) | collective-permute-done | bytes 589856 | tf_op jit(solution)/shard_map/ppermute | solution.py:472
  40.4 3.8 %shard_map.114 = (f32[128,2048]{1,0:T(8,128)}, f32[128,2048]{1,0:T(8,128)}, bf16[144,2048]{1,0:T(8,128)(2,1)}, f32[8,2048]{1,0:T(8,128)}, f32[8,2048]{1,0:T(8,128)}) custom-call(s32[1]{0:T(128)} %bitcast.22.place_ref, f32[8,2048]{1,0:T(8,128)} %get-tuple-element.117.log_ref, f32[128,2048]{1,0:T(8,128)} %get-tuple-element.118.total_ref, ...), custom_call_target="tpu_custom_call" | custom-call | bytes 4718592 | tf_op jit(solution)/shard_map/pallas_call | solution.py:748
  44.3 1.9 collective-permute-start.10
  46.2 1.6 collective-permute-start.6
  47.8 1.5 collective-permute-start.8
  49.3 1.3 collective-permute-start.7
  55.4 5.1 %shard_map.117 = (bf16[512,2304]{1,0:T(8,128)(2,1)}, bf16[512,1792]{1,0:T(8,128)(2,1)}) custom-call(s32[16]{0:T(128)} %get-tuple-element.237.order_ref, bf16[512,2048]{1,0:T(8,128)(2,1)} %own_ref.1, bf16[512,2048]{1,0:T(8,128)(2,1)} %collective-permute-done.3.refs_1_.other_ref), custom_call_target="tpu_custom_call" | custom-call | bytes 8388608 | tf_op jit(solution)/shard_map/pallas_call | solution.py:898
  60.5 2.2 fusion.6
  62.8 19.5 %collective-permute-done.9.got_ref = bf16[144,2048]{1,0:T(8,128)(2,1)} collective-permute-done((bf16[144,2048]{1,0:T(8,128)(2,1)}, bf16[144,2048]{1,0:T(8,128)(2,1)}, u32[]{:S(2)}, u32[]{:S(2)}) %collective-permute-start.9) | collective-permute-done | bytes 589856 | tf_op jit(solution)/shard_map/ppermute | solution.py:472
  82.3 4.1 %shard_map.116 = (f32[128,2048]{1,0:T(8,128)}, f32[128,2048]{1,0:T(8,128)}, bf16[144,2048]{1,0:T(8,128)(2,1)}, f32[8,2048]{1,0:T(8,128)}, f32[8,2048]{1,0:T(8,128)}) custom-call(s32[1]{0:T(128)} %bitcast.22.place_ref, f32[8,2048]{1,0:T(8,128)} %get-tuple-element.123.log_ref, f32[128,2048]{1,0:T(8,128)} %get-tuple-element.124.total_ref, ...), custom_call_target="tpu_custom_call" | custom-call | bytes 4718592 | tf_op jit(solution)/shard_map/pallas_call | solution.py:748
  86.4 3.0 add.123.refs_6_
  89.4 1.6 collective-permute-start.12
  91.0 1.5 collective-permute-start.14
  92.4 1.5 collective-permute-start.11
  93.9 3.5 %collective-permute-start.13 = (bf16[144,2048]{1,0:T(8,128)(2,1)S(1)}, bf16[144,2048]{1,0:T(8,128)(2,1)S(1)}, u32[]{:S(2)}, u32[]{:S(2)}) collective-permute-start(bf16[144,2048]{1,0:T(8,128)(2,1)S(1)} %copy-done.1), channel_id=1, source_target_pairs={{0,8},{2,10},{4,12},{6,14},{8,0},{10,2},{12,4},{14,6},{16,24},{18,... | collective-permute-start | bytes 1769480 | tf_op jit(solution)/shard_map/ppermute | solution.py:472
  97.4 2.3 fusion.5
  99.6 30.8 %collective-permute-done.13.got_ref = bf16[144,2048]{1,0:T(8,128)(2,1)S(1)} collective-permute-done((bf16[144,2048]{1,0:T(8,128)(2,1)S(1)}, bf16[144,2048]{1,0:T(8,128)(2,1)S(1)}, u32[]{:S(2)}, u32[]{:S(2)}) %collective-permute-start.13) | collective-permute-done | bytes 589856 | tf_op jit(solution)/shard_map/ppermute | solution.py:472
  131.3 4.1 %shard_map.119 = (f32[128,2048]{1,0:T(8,128)}, f32[128,2048]{1,0:T(8,128)}, bf16[144,2048]{1,0:T(8,128)(2,1)}, f32[8,2048]{1,0:T(8,128)}, f32[8,2048]{1,0:T(8,128)}) custom-call(s32[1]{0:T(128)} %bitcast.22.place_ref, f32[8,2048]{1,0:T(8,128)} %get-tuple-element.135.log_ref, f32[128,2048]{1,0:T(8,128)} %get-tuple-element.136.total_ref, ...), custom_call_target="tpu_custom_call" | custom-call | bytes 4718592 | tf_op jit(solution)/shard_map/pallas_call | solution.py:748
  135.4 2.6 slice_add_fusion
  139.2 1.5 collective-permute-start.16
  140.7 2.2 fusion.4
  143.0 1.5 collective-permute-start.18
  144.5 1.5 collective-permute-start.19
  146.0 1.4 slice.76
  148.2 10.2 %shard_map.122.refs_9_.part_ref = f32[512,2048]{1,0:T(8,128)} custom-call(bf16[512,2304]{1,0:T(8,128)(2,1)} %get-tuple-element.129.refs_8_.f_ref, bf16[256,2048]{1,0:T(8,128)(2,1)} %refs_0_.3, bf16[256,2048]{1,0:T(8,128)(2,1)} %collective-permute-done.5.refs_4_.refs_1_, bf16[256,2048]{1,0:T(8,128)(2,1)} %get-tuple-element.128.refs_2_, ...), custom_call_target="tpu_custom_call" | custom-call | flops 4831838208 | bytes 9437184 | tf_op jit(solution)/shard_map/pallas_call | solution.py:647
  158.3 6.9 %collective-permute-done.16.got_ref = bf16[144,2048]{1,0:T(8,128)(2,1)} collective-permute-done((bf16[144,2048]{1,0:T(8,128)(2,1)}, bf16[144,2048]{1,0:T(8,128)(2,1)}, u32[]{:S(2)}, u32[]{:S(2)}) %collective-permute-start.16) | collective-permute-done | bytes 589856 | tf_op jit(solution)/shard_map/ppermute | solution.py:472
  165.2 4.1 %shard_map.121 = (f32[128,2048]{1,0:T(8,128)}, f32[128,2048]{1,0:T(8,128)}, bf16[144,2048]{1,0:T(8,128)(2,1)}, f32[8,2048]{1,0:T(8,128)}, f32[8,2048]{1,0:T(8,128)}) custom-call(s32[1]{0:T(128)} %bitcast.22.place_ref, f32[8,2048]{1,0:T(8,128)} %get-tuple-element.144.log_ref, f32[128,2048]{1,0:T(8,128)} %get-tuple-element.145.total_ref, ...), custom_call_target="tpu_custom_call" | custom-call | bytes 4718592 | tf_op jit(solution)/shard_map/pallas_call | solution.py:748
  170.5 1.5 collective-permute-start.23
  174.5 2.2 fusion.1
  177.8 10.4 %shard_map.124.g_ref = bf16[2048,512]{1,0:T(8,128)(2,1)} custom-call(f32[32,512]{1,0:T(8,128)} %get-tuple-element.113.r_ref, f32[4,512,8]{2,1,0:T(8,128)} %get-tuple-element.114.rt_ref, bf16[512,2048]{1,0:T(8,128)(2,1)} %g_ref.11, bf16[512,128]{1,0:T(8,128)(2,1)} %b_ref.9, bf16[512,128]{1,0:T(8,128)(2,1)} %c_ref.11, ...), custom_call_target="tpu_custom_call" | custom-call | flops 2147483648 | bytes 6291456 | tf_op jit(solution)/shard_map/pallas_call | solution.py:998
  188.2 7.6 %collective-permute-done.20.refs_0_ = bf16[256,1024]{1,0:T(8,128)(2,1)} collective-permute-done((bf16[256,1024]{1,0:T(8,128)(2,1)}, bf16[256,1024]{1,0:T(8,128)(2,1)}, u32[]{:S(2)}, u32[]{:S(2)}) %collective-permute-start.20) | collective-permute-done | bytes 524320 | tf_op jit(solution)/shard_map/ppermute | solution.py:472
  196.9 10.0 %shard_map.126 = (bf16[512,2048]{1,0:T(8,128)(2,1)}, bf16[512,2048]{1,0:T(8,128)(2,1)}) custom-call(s32[9]{0:T(128)} %bitcast.34, bf16[2048,512]{1,0:T(8,128)(2,1)} %shard_map.124.g_ref, bf16[256,2048]{1,0:T(8,128)(2,1)} %refs_0_.3, bf16[256,2048]{1,0:T(8,128)(2,1)} %collective-permute-done.5.refs_4_.refs_1_, bf16[256,2048]{1,0:T(8,128)(2,1)} %get-tuple-element.128.refs_2_, ...), custom_call_target="tpu_custom_call" | custom-call | flops 4831838208 | bytes 9437184 | tf_op jit(solution)/shard_map/pallas_call | solution.py:703
  206.9 6.6 %shard_map.125 = (bf16[512,1024]{1,0:T(8,128)(2,1)}, f32[2,128,1024]{2,1,0:T(8,128)}, f32[128,1024]{1,0:T(8,128)}, bf16[128,1024]{1,0:T(8,128)(2,1)}) custom-call(bf16[512,1792]{1,0:T(8,128)(2,1)} %get-tuple-element.154.f_ref, f32[512,2048]{1,0:T(8,128)} %shard_map.122.refs_9_.part_ref, f32[4,512,8]{2,1,0:T(8,128)} %get-tuple-element.114.rt_ref, ...), custom_call_target="tpu_custom_call" | custom-call | flops 1879048192 | bytes 3670016 | tf_op jit(solution)/shard_map/pallas_call | solution.py:667
  213.6 1.5 collective-permute-start.26
  217.8 8.8 %shard_map.129 = (f32[16,512]{1,0:T(8,128)}, f32[512,128]{1,0:T(8,128)}, f32[512,128]{1,0:T(8,128)}) custom-call(f32[32,512]{1,0:T(8,128)} %get-tuple-element.113.r_ref, f32[4,512,8]{2,1,0:T(8,128)} %get-tuple-element.114.rt_ref, bf16[512,2048]{1,0:T(8,128)(2,1)} %g_ref.11, bf16[512,1024]{1,0:T(8,128)(2,1)} %get-tuple-element.167.x_ref, ...), custom_call_target="tpu_custom_call" | custom-call | flops 1610612736 | bytes 3145728 | tf_op jit(solution)/shard_map/pallas_call | solution.py:825
  226.6 2.6 collective-permute-done.28.got_ref
  229.2 2.1 shard_map.128
  231.3 6.6 %shard_map.131 = (bf16[512,1024]{1,0:T(8,128)(2,1)}, f32[2,128,1024]{2,1,0:T(8,128)}, f32[128,1024]{1,0:T(8,128)}, bf16[128,1024]{1,0:T(8,128)(2,1)}) custom-call(bf16[512,1792]{1,0:T(8,128)(2,1)} %get-tuple-element.154.f_ref, f32[512,2048]{1,0:T(8,128)} %shard_map.122.refs_9_.part_ref, f32[4,512,8]{2,1,0:T(8,128)} %get-tuple-element.114.rt_ref, ...), custom_call_target="tpu_custom_call" | custom-call | flops 1879048192 | bytes 3670016 | tf_op jit(solution)/shard_map/pallas_call | solution.py:667
  238.0 1.5 collective-permute-start.30
  240.0 9.8 %shard_map.133 = (bf16[512,2048]{1,0:T(8,128)(2,1)}, bf16[512,2048]{1,0:T(8,128)(2,1)}) custom-call(s32[7]{0:T(128)} %slice.74.order_ref, bf16[2048,512]{1,0:T(8,128)(2,1)} %shard_map.124.g_ref, bf16[256,1024]{1,0:T(8,128)(2,1)} %collective-permute-done.20.refs_0_, ...), custom_call_target="tpu_custom_call", output_to_operand_aliasing={{0}: (16, {}), {1}: (17, {})} | custom-call | flops 3758096384 | bytes 7340032 | tf_op jit(solution)/shard_map/pallas_call | solution.py:703
  249.8 2.1 shard_map.135
  251.9 2.2 shard_map.134
  254.2 1.6 collective-permute-start.32
  255.8 1.9 collective-permute-start.31
  257.8 9.0 %shard_map.139 = (f32[16,512]{1,0:T(8,128)}, f32[512,128]{1,0:T(8,128)}, f32[512,128]{1,0:T(8,128)}) custom-call(f32[32,512]{1,0:T(8,128)} %get-tuple-element.113.r_ref, f32[4,512,8]{2,1,0:T(8,128)} %get-tuple-element.114.rt_ref, bf16[512,2048]{1,0:T(8,128)(2,1)} %g_ref.11, bf16[512,1024]{1,0:T(8,128)(2,1)} %get-tuple-element.196.x_ref, ...), custom_call_target="tpu_custom_call" | custom-call | flops 1610612736 | bytes 3145728 | tf_op jit(solution)/shard_map/pallas_call | solution.py:825
  266.8 2.3 shard_map.138
  269.1 2.2 shard_map.137
  271.3 3.4 %collective-permute-start.36 = (bf16[128,1024]{1,0:T(8,128)(2,1)}, bf16[128,1024]{1,0:T(8,128)(2,1)}, u32[]{:S(2)}, u32[]{:S(2)}) collective-permute-start(bf16[128,1024]{1,0:T(8,128)(2,1)} %get-tuple-element.208), channel_id=1, source_target_pairs={{0,16},{2,18},{4,20},{6,22},{8,24},{10,26},{12,28},{14,30},{16,0},... | collective-permute-start | bytes 786440 | tf_op jit(solution)/shard_map/ppermute | solution.py:472
  275.9 4.5 %add_convert_fusion.refs_2_ = bf16[512,2048]{1,0:T(8,128)(2,1)} fusion(bf16[512,2048]{1,0:T(8,128)(2,1)} %get-tuple-element.199, bf16[512,2048]{1,0:T(8,128)(2,1)} %get-tuple-element.175), kind=kLoop, calls=%fused_computation | loop fusion | flops 4194304 | bytes 6291456 | tf_op jit(solution)/shard_map/convert_element_type | solution.py:980
  281.1 7.4 %collective-permute-done.35.got_ref = bf16[128,1024]{1,0:T(8,128)(2,1)} collective-permute-done((bf16[128,1024]{1,0:T(8,128)(2,1)}, bf16[128,1024]{1,0:T(8,128)(2,1)}, u32[]{:S(2)}, u32[]{:S(2)}) %collective-permute-start.35) | collective-permute-done | bytes 262176 | tf_op jit(solution)/shard_map/ppermute | solution.py:472
  288.5 2.3 shard_map.141
  290.7 2.1 shard_map.142.refs_1_
  292.9 5.5 %shard_map.145 = (f32[32,512]{1,0:T(8,128)}, f32[512,128]{1,0:T(8,128)}) custom-call(f32[4,512,8]{2,1,0:T(8,128)} %get-tuple-element.114.rt_ref, bf16[512,2048]{1,0:T(8,128)(2,1)} %g_ref.11, bf16[512,128]{1,0:T(8,128)(2,1)} %c_ref.11, f32[128,1024]{1,0:T(8,128)} %get-tuple-element.214.s_ref, f32[2,128,1024]{2,1,0:T(8,128)} %get-tuple-element.215.e_ref, ...), custom_call_target="tpu_custom_call" | custom-call | flops 268435456 | bytes 3145728 | tf_op jit(solution)/shard_map/pallas_call | solution.py:843
  298.4 8.2 %collective-permute-done.37.got_ref = bf16[128,1024]{1,0:T(8,128)(2,1)} collective-permute-done((bf16[128,1024]{1,0:T(8,128)(2,1)}, bf16[128,1024]{1,0:T(8,128)(2,1)}, u32[]{:S(2)}, u32[]{:S(2)}) %collective-permute-start.37) | collective-permute-done | bytes 262176 | tf_op jit(solution)/shard_map/ppermute | solution.py:472
  306.6 2.1 shard_map.144.s_ref
  308.7 5.5 %shard_map.146 = (f32[32,512]{1,0:T(8,128)}, f32[512,128]{1,0:T(8,128)}) custom-call(f32[4,512,8]{2,1,0:T(8,128)} %get-tuple-element.114.rt_ref, bf16[512,2048]{1,0:T(8,128)(2,1)} %g_ref.11, bf16[512,128]{1,0:T(8,128)(2,1)} %c_ref.11, f32[128,1024]{1,0:T(8,128)} %shard_map.144.s_ref, ...), custom_call_target="tpu_custom_call", output_to_operand_aliasing={{0}: (9, {})} | custom-call | flops 268435456 | bytes 3145728 | tf_op jit(solution)/shard_map/pallas_call | solution.py:843
  315.3 1.3 collective-permute-done.38
  316.6 1.7 convert_add_fusion
  (78 shorter events, 18.4 us)
Async XLA Ops:
  0.6 20.7 %collective-permute-start.3 = (bf16[512,2048]{1,0:T(8,128)(2,1)}, bf16[512,2048]{1,0:T(8,128)(2,1)}, u32[]{:S(2)}, u32[]{:S(2)}) collective-permute-start(bf16[512,2048]{1,0:T(8,128)(2,1)} %own_ref.1), channel_id=1, source_target_pairs={{0,1},{1,0},{2,3},{3,2},{4,5},{5,4},{6,7},{7,6},{8,9},{9,8},{10,11... | collective-permute-start | bytes 6291464 | tf_op jit(solution)/shard_map/ppermute | solution.py:472
  1.1 43.1 %collective-permute-start.5 = (bf16[256,2048]{1,0:T(8,128)(2,1)}, bf16[256,2048]{1,0:T(8,128)(2,1)}, u32[]{:S(2)}, u32[]{:S(2)}) collective-permute-start(bf16[256,2048]{1,0:T(8,128)(2,1)} %refs_0_.3), channel_id=1, source_target_pairs={{0,2},{2,0},{4,6},{6,4},{8,10},{10,8},{12,14},{14,12},{16,18},{18,... | collective-permute-start | bytes 3145736 | tf_op jit(solution)/shard_map/ppermute | solution.py:472
  3.7 40.6 %collective-permute-start = (bf16[256,2048]{1,0:T(8,128)(2,1)}, bf16[256,2048]{1,0:T(8,128)(2,1)}, u32[]{:S(2)}, u32[]{:S(2)}) collective-permute-start(bf16[256,2048]{1,0:T(8,128)(2,1)} %refs_0_.3), channel_id=1, source_target_pairs={{0,8},{2,10},{4,12},{6,14},{8,0},{10,2},{12,4},{14,6},{16,24},{18,... | collective-permute-start | bytes 3145736 | tf_op jit(solution)/shard_map/ppermute | solution.py:472
  5.3 39.0 %collective-permute-start.1 = (bf16[256,2048]{1,0:T(8,128)(2,1)}, bf16[256,2048]{1,0:T(8,128)(2,1)}, u32[]{:S(2)}, u32[]{:S(2)}) collective-permute-start(bf16[256,2048]{1,0:T(8,128)(2,1)} %refs_0_.3), channel_id=1, source_target_pairs={{8,16},{10,18},{12,20},{14,22},{16,8},{18,10},{20,12},{22,14},{9,1... | collective-permute-start | bytes 3145736 | tf_op jit(solution)/shard_map/ppermute | solution.py:533
  6.9 37.4 %collective-permute-start.2 = (bf16[256,2048]{1,0:T(8,128)(2,1)}, bf16[256,2048]{1,0:T(8,128)(2,1)}, u32[]{:S(2)}, u32[]{:S(2)}) collective-permute-start(bf16[256,2048]{1,0:T(8,128)(2,1)} %refs_0_.3), channel_id=1, source_target_pairs={{0,4},{2,6},{4,0},{6,2},{8,12},{10,14},{12,8},{14,10},{16,20},{18,... | collective-permute-start | bytes 3145736 | tf_op jit(solution)/shard_map/ppermute | solution.py:472
  21.3 19.1 %collective-permute-start.4 = (bf16[144,2048]{1,0:T(8,128)(2,1)}, bf16[144,2048]{1,0:T(8,128)(2,1)}, u32[]{:S(2)}, u32[]{:S(2)}) collective-permute-start(bf16[144,2048]{1,0:T(8,128)(2,1)} %shard_map.113), channel_id=1, source_target_pairs={{0,2},{2,0},{4,6},{6,4},{8,10},{10,8},{12,14},{14,12},{16,18},{18,... | collective-permute-start | bytes 1769480 | tf_op jit(solution)/shard_map/ppermute | solution.py:472
  44.3 42.0 %collective-permute-start.10 = (bf16[256,2048]{1,0:T(8,128)(2,1)}, bf16[256,2048]{1,0:T(8,128)(2,1)}, u32[]{:S(2)}, u32[]{:S(2)}) collective-permute-start(bf16[256,2048]{1,0:T(8,128)(2,1)} %get-tuple-element.122.refs_3_), channel_id=1, source_target_pairs={{0,4},{2,6},{4,0},{6,2},{8,12},{10,14},{12,8},{14,10},{16,20},{18,... | collective-permute-start | bytes 3145736 | tf_op jit(solution)/shard_map/ppermute | solution.py:472
  46.2 40.2 %collective-permute-start.6 = (bf16[256,2048]{1,0:T(8,128)(2,1)}, bf16[256,2048]{1,0:T(8,128)(2,1)}, u32[]{:S(2)}, u32[]{:S(2)}) collective-permute-start(bf16[256,2048]{1,0:T(8,128)(2,1)} %get-tuple-element.122.refs_3_), channel_id=1, source_target_pairs={{8,16},{10,18},{12,20},{14,22},{16,8},{18,10},{20,12},{22,14},{9,1... | collective-permute-start | bytes 3145736 | tf_op jit(solution)/shard_map/ppermute | solution.py:533
  47.8 38.5 %collective-permute-start.8 = (bf16[256,2048]{1,0:T(8,128)(2,1)}, bf16[256,2048]{1,0:T(8,128)(2,1)}, u32[]{:S(2)}, u32[]{:S(2)}) collective-permute-start(bf16[256,2048]{1,0:T(8,128)(2,1)} %get-tuple-element.122.refs_3_), channel_id=1, source_target_pairs={{0,2},{2,0},{4,6},{6,4},{8,10},{10,8},{12,14},{14,12},{16,18},{18,... | collective-permute-start | bytes 3145736 | tf_op jit(solution)/shard_map/ppermute | solution.py:472
  49.3 37.0 %collective-permute-start.7 = (bf16[256,2048]{1,0:T(8,128)(2,1)}, bf16[256,2048]{1,0:T(8,128)(2,1)}, u32[]{:S(2)}, u32[]{:S(2)}) collective-permute-start(bf16[256,2048]{1,0:T(8,128)(2,1)} %get-tuple-element.121.refs_0_), channel_id=1, source_target_pairs={{8,0},{10,2},{12,4},{14,6},{16,24},{18,26},{20,28},{22,30},{9,1},{... | collective-permute-start | bytes 3145736 | tf_op jit(solution)/shard_map/ppermute | solution.py:533
  51.4 30.9 %collective-permute-start.9 = (bf16[144,2048]{1,0:T(8,128)(2,1)}, bf16[144,2048]{1,0:T(8,128)(2,1)}, u32[]{:S(2)}, u32[]{:S(2)}) collective-permute-start(bf16[144,2048]{1,0:T(8,128)(2,1)} %get-tuple-element.125), channel_id=1, source_target_pairs={{0,4},{2,6},{4,0},{6,2},{8,12},{10,14},{12,8},{14,10},{16,20},{18,... | collective-permute-start | bytes 1769480 | tf_op jit(solution)/shard_map/ppermute | solution.py:472
  86.4 7.6 %copy-start.1 = (bf16[144,2048]{1,0:T(8,128)(2,1)S(1)}, bf16[144,2048]{1,0:T(8,128)(2,1)}, u32[]{:S(2)}) copy-start(bf16[144,2048]{1,0:T(8,128)(2,1)} %get-tuple-element.137) | copy-start | bytes 1769476
  89.4 46.0 %collective-permute-start.12 = (bf16[256,2048]{1,0:T(8,128)(2,1)}, bf16[256,2048]{1,0:T(8,128)(2,1)}, u32[]{:S(2)}, u32[]{:S(2)}) collective-permute-start(bf16[256,2048]{1,0:T(8,128)(2,1)} %add.123.refs_6_), channel_id=1, source_target_pairs={{0,4},{2,6},{4,0},{6,2},{8,12},{10,14},{12,8},{14,10},{16,20},{18,... | collective-permute-start | bytes 3145736 | tf_op jit(solution)/shard_map/ppermute | solution.py:472
  91.0 44.4 %collective-permute-start.14 = (bf16[256,2048]{1,0:T(8,128)(2,1)}, bf16[256,2048]{1,0:T(8,128)(2,1)}, u32[]{:S(2)}, u32[]{:S(2)}) collective-permute-start(bf16[256,2048]{1,0:T(8,128)(2,1)} %add.123.refs_6_), channel_id=1, source_target_pairs={{0,2},{2,0},{4,6},{6,4},{8,10},{10,8},{12,14},{14,12},{16,18},{18,... | collective-permute-start | bytes 3145736 | tf_op jit(solution)/shard_map/ppermute | solution.py:472
  92.4 42.9 %collective-permute-start.11 = (bf16[256,2048]{1,0:T(8,128)(2,1)}, bf16[256,2048]{1,0:T(8,128)(2,1)}, u32[]{:S(2)}, u32[]{:S(2)}) collective-permute-start(bf16[256,2048]{1,0:T(8,128)(2,1)} %get-tuple-element.131.refs_0_), channel_id=1, source_target_pairs={{8,0},{10,2},{12,4},{14,6},{16,24},{18,26},{20,28},{22,30},{9,1},{... | collective-permute-start | bytes 3145736 | tf_op jit(solution)/shard_map/ppermute | solution.py:533
  93.9 36.5 %collective-permute-start.13 = (bf16[144,2048]{1,0:T(8,128)(2,1)S(1)}, bf16[144,2048]{1,0:T(8,128)(2,1)S(1)}, u32[]{:S(2)}, u32[]{:S(2)}) collective-permute-start(bf16[144,2048]{1,0:T(8,128)(2,1)S(1)} %copy-done.1), channel_id=1, source_target_pairs={{0,8},{2,10},{4,12},{6,14},{8,0},{10,2},{12,4},{14,6},{16,24},{18,... | collective-permute-start | bytes 1769480 | tf_op jit(solution)/shard_map/ppermute | solution.py:472
  130.4 0.8 copy-start.2
  135.4 12.0 %copy-start.3 = (f32[32]{0:T(128)S(1)}, f32[32]{0:T(128)}, u32[]{:S(2)}) copy-start(f32[32]{0:T(128)} %param.13) | copy-start | bytes 388
  138.0 31.3 %collective-permute-start.15 = (bf16[256,1024]{1,0:T(8,128)(2,1)}, bf16[256,1024]{1,0:T(8,128)(2,1)}, u32[]{:S(2)}, u32[]{:S(2)}) collective-permute-start(bf16[256,1024]{1,0:T(8,128)(2,1)} %get-tuple-element.223.refs_3_.refs_6_), channel_id=1, source_target_pairs={{0,2},{2,0},{4,6},{6,4},{8,10},{10,8},{12,14},{14,12},{16,18},{18,... | collective-permute-start | bytes 1572872 | tf_op jit(solution)/shard_map/ppermute | solution.py:472
  138.5 30.7 %collective-permute-start.17 = (bf16[256,1024]{1,0:T(8,128)(2,1)}, bf16[256,1024]{1,0:T(8,128)(2,1)}, u32[]{:S(2)}, u32[]{:S(2)}) collective-permute-start(bf16[256,1024]{1,0:T(8,128)(2,1)} %get-tuple-element.223.refs_3_.refs_6_), channel_id=1, source_target_pairs={{0,4},{2,6},{4,0},{6,2},{8,12},{10,14},{12,8},{14,10},{16,20},{18,... | collective-permute-start | bytes 1572872 | tf_op jit(solution)/shard_map/ppermute | solution.py:472
  139.2 26.0 %collective-permute-start.16 = (bf16[144,2048]{1,0:T(8,128)(2,1)}, bf16[144,2048]{1,0:T(8,128)(2,1)}, u32[]{:S(2)}, u32[]{:S(2)}) collective-permute-start(bf16[144,2048]{1,0:T(8,128)(2,1)} %get-tuple-element.146), channel_id=1, source_target_pairs={{0,16},{2,18},{4,20},{6,22},{8,24},{10,26},{12,28},{14,30},{16,0},... | collective-permute-start | bytes 1769480 | tf_op jit(solution)/shard_map/ppermute | solution.py:472
  143.0 26.3 %collective-permute-start.18 = (bf16[256,1024]{1,0:T(8,128)(2,1)}, bf16[256,1024]{1,0:T(8,128)(2,1)}, u32[]{:S(2)}, u32[]{:S(2)}) collective-permute-start(bf16[256,1024]{1,0:T(8,128)(2,1)} %get-tuple-element.226), channel_id=1, source_target_pairs={{0,2},{2,0},{4,6},{6,4},{8,10},{10,8},{12,14},{14,12},{16,18},{18,... | collective-permute-start | bytes 1572872 | tf_op jit(solution)/shard_map/ppermute | solution.py:472
  144.5 24.8 %collective-permute-start.19 = (bf16[256,1024]{1,0:T(8,128)(2,1)}, bf16[256,1024]{1,0:T(8,128)(2,1)}, u32[]{:S(2)}, u32[]{:S(2)}) collective-permute-start(bf16[256,1024]{1,0:T(8,128)(2,1)} %get-tuple-element.149), channel_id=1, source_target_pairs={{0,4},{2,6},{4,0},{6,2},{8,12},{10,14},{12,8},{14,10},{16,20},{18,... | collective-permute-start | bytes 1572872 | tf_op jit(solution)/shard_map/ppermute | solution.py:472
  169.3 44.2 %collective-permute-start.21 = (bf16[256,1024]{1,0:T(8,128)(2,1)}, bf16[256,1024]{1,0:T(8,128)(2,1)}, u32[]{:S(2)}, u32[]{:S(2)}) collective-permute-start(bf16[256,1024]{1,0:T(8,128)(2,1)} %get-tuple-element.153.refs_3_.refs_7_), channel_id=1, source_target_pairs={{0,2},{2,0},{4,6},{6,4},{8,10},{10,8},{12,14},{14,12},{16,18},{18,... | collective-permute-start | bytes 1572872 | tf_op jit(solution)/shard_map/ppermute | solution.py:472
  170.5 43.0 %collective-permute-start.23 = (bf16[256,1024]{1,0:T(8,128)(2,1)}, bf16[256,1024]{1,0:T(8,128)(2,1)}, u32[]{:S(2)}, u32[]{:S(2)}) collective-permute-start(bf16[256,1024]{1,0:T(8,128)(2,1)} %get-tuple-element.153.refs_3_.refs_7_), channel_id=1, source_target_pairs={{0,4},{2,6},{4,0},{6,2},{8,12},{10,14},{12,8},{14,10},{16,20},{18,... | collective-permute-start | bytes 1572872 | tf_op jit(solution)/shard_map/ppermute | solution.py:472
  172.0 23.8 %collective-permute-start.20 = (bf16[256,1024]{1,0:T(8,128)(2,1)}, bf16[256,1024]{1,0:T(8,128)(2,1)}, u32[]{:S(2)}, u32[]{:S(2)}) collective-permute-start(bf16[256,1024]{1,0:T(8,128)(2,1)} %get-tuple-element.151), channel_id=1, source_target_pairs={{0,2},{2,0},{4,6},{6,4},{8,10},{10,8},{12,14},{14,12},{16,18},{18,... | collective-permute-start | bytes 1572872 | tf_op jit(solution)/shard_map/ppermute | solution.py:472
  172.5 34.4 %collective-permute-start.22 = (bf16[256,1024]{1,0:T(8,128)(2,1)}, bf16[256,1024]{1,0:T(8,128)(2,1)}, u32[]{:S(2)}, u32[]{:S(2)}) collective-permute-start(bf16[256,1024]{1,0:T(8,128)(2,1)} %get-tuple-element.155.refs_4_.refs_8_), channel_id=1, source_target_pairs={{0,4},{2,6},{4,0},{6,2},{8,12},{10,14},{12,8},{14,10},{16,20},{18,... | collective-permute-start | bytes 1572872 | tf_op jit(solution)/shard_map/ppermute | solution.py:472
  173.4 40.1 %collective-permute-start.24 = (bf16[256,1024]{1,0:T(8,128)(2,1)}, bf16[256,1024]{1,0:T(8,128)(2,1)}, u32[]{:S(2)}, u32[]{:S(2)}) collective-permute-start(bf16[256,1024]{1,0:T(8,128)(2,1)} %get-tuple-element.158), channel_id=1, source_target_pairs={{0,2},{2,0},{4,6},{6,4},{8,10},{10,8},{12,14},{14,12},{16,18},{18,... | collective-permute-start | bytes 1572872 | tf_op jit(solution)/shard_map/ppermute | solution.py:472
  195.8 17.8 %collective-permute-start.25 = (bf16[256,1024]{1,0:T(8,128)(2,1)}, bf16[256,1024]{1,0:T(8,128)(2,1)}, u32[]{:S(2)}, u32[]{:S(2)}) collective-permute-start(bf16[256,1024]{1,0:T(8,128)(2,1)} %get-tuple-element.159), channel_id=1, source_target_pairs={{0,4},{2,6},{4,0},{6,2},{8,12},{10,14},{12,8},{14,10},{16,20},{18,... | collective-permute-start | bytes 1572872 | tf_op jit(solution)/shard_map/ppermute | solution.py:472
  213.6 17.7 %collective-permute-start.26 = (bf16[256,1024]{1,0:T(8,128)(2,1)}, bf16[256,1024]{1,0:T(8,128)(2,1)}, u32[]{:S(2)}, u32[]{:S(2)}) collective-permute-start(bf16[256,1024]{1,0:T(8,128)(2,1)} %get-tuple-element.161), channel_id=1, source_target_pairs={{0,2},{2,0},{4,6},{6,4},{8,10},{10,8},{12,14},{14,12},{16,18},{18,... | collective-permute-start | bytes 1572872 | tf_op jit(solution)/shard_map/ppermute | solution.py:472
  215.1 16.2 %collective-permute-start.27 = (bf16[256,1024]{1,0:T(8,128)(2,1)}, bf16[256,1024]{1,0:T(8,128)(2,1)}, u32[]{:S(2)}, u32[]{:S(2)}) collective-permute-start(bf16[256,1024]{1,0:T(8,128)(2,1)} %get-tuple-element.162.refs_4_.refs_9_), channel_id=1, source_target_pairs={{0,4},{2,6},{4,0},{6,2},{8,12},{10,14},{12,8},{14,10},{16,20},{18,... | collective-permute-start | bytes 1572872 | tf_op jit(solution)/shard_map/ppermute | solution.py:472
  215.7 13.5 %collective-permute-start.28 = (bf16[128,1024]{1,0:T(8,128)(2,1)}, bf16[128,1024]{1,0:T(8,128)(2,1)}, u32[]{:S(2)}, u32[]{:S(2)}) collective-permute-start(bf16[128,1024]{1,0:T(8,128)(2,1)} %get-tuple-element.165), channel_id=1, source_target_pairs={{0,2},{2,0},{4,6},{6,4},{8,10},{10,8},{12,14},{14,12},{16,18},{18,... | collective-permute-start | bytes 786440 | tf_op jit(solution)/shard_map/ppermute | solution.py:472
  238.0 11.8 %collective-permute-start.30 = (bf16[128,1024]{1,0:T(8,128)(2,1)}, bf16[128,1024]{1,0:T(8,128)(2,1)}, u32[]{:S(2)}, u32[]{:S(2)}) collective-permute-start(bf16[128,1024]{1,0:T(8,128)(2,1)} %get-tuple-element.184), channel_id=1, source_target_pairs={{0,2},{2,0},{4,6},{6,4},{8,10},{10,8},{12,14},{14,12},{16,18},{18,... | collective-permute-start | bytes 786440 | tf_op jit(solution)/shard_map/ppermute | solution.py:472
  239.5 12.5 %collective-permute-start.29 = (bf16[128,1024]{1,0:T(8,128)(2,1)}, bf16[128,1024]{1,0:T(8,128)(2,1)}, u32[]{:S(2)}, u32[]{:S(2)}) collective-permute-start(bf16[128,1024]{1,0:T(8,128)(2,1)} %get-tuple-element.179), channel_id=1, source_target_pairs={{0,4},{2,6},{4,0},{6,2},{8,12},{10,14},{12,8},{14,10},{16,20},{18,... | collective-permute-start | bytes 786440 | tf_op jit(solution)/shard_map/ppermute | solution.py:472
  254.2 17.2 %collective-permute-start.33 = (bf16[512,2048]{1,0:T(8,128)(2,1)}, bf16[512,2048]{1,0:T(8,128)(2,1)}, u32[]{:S(2)}, u32[]{:S(2)}) collective-permute-start(bf16[512,2048]{1,0:T(8,128)(2,1)} %get-tuple-element.195), channel_id=1, source_target_pairs={{0,1},{1,0},{2,3},{3,2},{4,5},{5,4},{6,7},{7,6},{8,9},{9,8},{10,11... | collective-permute-start | bytes 6291464 | tf_op jit(solution)/shard_map/ppermute | solution.py:472
  254.2 12.5 %collective-permute-start.32 = (bf16[128,1024]{1,0:T(8,128)(2,1)}, bf16[128,1024]{1,0:T(8,128)(2,1)}, u32[]{:S(2)}, u32[]{:S(2)}) collective-permute-start(bf16[128,1024]{1,0:T(8,128)(2,1)} %get-tuple-element.192), channel_id=1, source_target_pairs={{0,4},{2,6},{4,0},{6,2},{8,12},{10,14},{12,8},{14,10},{16,20},{18,... | collective-permute-start | bytes 786440 | tf_op jit(solution)/shard_map/ppermute | solution.py:472
  255.8 13.2 %collective-permute-start.31 = (bf16[128,1024]{1,0:T(8,128)(2,1)}, bf16[128,1024]{1,0:T(8,128)(2,1)}, u32[]{:S(2)}, u32[]{:S(2)}) collective-permute-start(bf16[128,1024]{1,0:T(8,128)(2,1)} %get-tuple-element.188), channel_id=1, source_target_pairs={{0,8},{2,10},{4,12},{6,14},{8,0},{10,2},{12,4},{14,6},{16,24},{18,... | collective-permute-start | bytes 786440 | tf_op jit(solution)/shard_map/ppermute | solution.py:472
  271.3 19.4 %collective-permute-start.36 = (bf16[128,1024]{1,0:T(8,128)(2,1)}, bf16[128,1024]{1,0:T(8,128)(2,1)}, u32[]{:S(2)}, u32[]{:S(2)}) collective-permute-start(bf16[128,1024]{1,0:T(8,128)(2,1)} %get-tuple-element.208), channel_id=1, source_target_pairs={{0,16},{2,18},{4,20},{6,22},{8,24},{10,26},{12,28},{14,30},{16,0},... | collective-permute-start | bytes 786440 | tf_op jit(solution)/shard_map/ppermute | solution.py:472
  274.8 13.7 %collective-permute-start.35 = (bf16[128,1024]{1,0:T(8,128)(2,1)}, bf16[128,1024]{1,0:T(8,128)(2,1)}, u32[]{:S(2)}, u32[]{:S(2)}) collective-permute-start(bf16[128,1024]{1,0:T(8,128)(2,1)} %get-tuple-element.203), channel_id=1, source_target_pairs={{0,8},{2,10},{4,12},{6,14},{8,0},{10,2},{12,4},{14,6},{16,24},{18,... | collective-permute-start | bytes 786440 | tf_op jit(solution)/shard_map/ppermute | solution.py:472
  275.8 4.6 %collective-permute-start.34 = (bf16[512,128]{1,0:T(8,128)(2,1)S(1)}, bf16[512,128]{1,0:T(8,128)(2,1)S(1)}, u32[]{:S(2)}, u32[]{:S(2)}) collective-permute-start(bf16[512,128]{1,0:T(8,128)(2,1)S(1)} %convert_element_type.38), channel_id=1, source_target_pairs={{0,1},{1,0},{2,3},{3,2},{4,5},{5,4},{6,7},{7,6},{8,9},{9,8},{10,11... | collective-permute-start | bytes 393224 | tf_op jit(solution)/shard_map/ppermute | solution.py:472
  275.9 4.5 %copy-start = (f32[512,128]{1,0:T(8,128)S(1)}, f32[512,128]{1,0:T(8,128)}, u32[]{:S(2)}) copy-start(f32[512,128]{1,0:T(8,128)} %get-tuple-element.200) | copy-start | bytes 786436
  292.9 13.8 %collective-permute-start.37 = (bf16[128,1024]{1,0:T(8,128)(2,1)}, bf16[128,1024]{1,0:T(8,128)(2,1)}, u32[]{:S(2)}, u32[]{:S(2)}) collective-permute-start(bf16[128,1024]{1,0:T(8,128)(2,1)} %get-tuple-element.210), channel_id=1, source_target_pairs={{0,16},{2,18},{4,20},{6,22},{8,24},{10,26},{12,28},{14,30},{16,0},... | collective-permute-start | bytes 786440 | tf_op jit(solution)/shard_map/ppermute | solution.py:472
  315.2 1.4 collective-permute-start.38

commit v9 on v8

--- a/solution.py
+++ b/solution.py
@@ -183,24 +183,23 @@
     return total.astype(BF16), tail.astype(BF16)
 
 
-def start_kernel(own_ref, kept_ref, total_ref, log_ref, sent_ref):
+def start_kernel(own_ref, kept_ref, log_ref, sent_ref):
     spans = own_ref.shape[0]
     total = own_ref[spans - 1]
     log = kept_ref[spans - 1, 4:5]
     for k in range(spans - 2, -1, -1):
         total = own_ref[k] + kept_ref[k, :1] * total
         log = log + kept_ref[k, 4:5]
-    total_ref[...] = total
     line = iota(log_ref.shape, 0)
     log_ref[...] = jnp.where(line == 0, log, 0.0)
     n = total.shape[0]
     sent_ref[:n], sent_ref[n:] = message(total, log)
 
 
-def back_kernel(bit, place_ref, log_ref, total_ref, got_ref, *refs):
-    entering_ref = refs[0] if len(refs) == 6 else None
-    total_out, entering_out, sent_out, log_out, factor_out = refs[-5:]
-    n = total_ref.shape[0]
+def back_kernel(bit, place_ref, log_ref, mine_ref, got_ref, *refs):
+    entering_ref = refs[0] if len(refs) == 5 else None
+    entering_out, sent_out, log_out, factor_out = refs[-4:]
+    n = entering_out.shape[0]
     got = got_ref[:n].astype(F32)
     tail = got_ref[n:].astype(F32)
     other_log = tail[0:1] + tail[1:2] + tail[2:3]
@@ -208,9 +207,9 @@
     line = iota(log_ref.shape, 0)
     upper = (place_ref[0] // bit % 2 + 0 * line[0:1]) == 1
     kept, other = jnp.exp2(log), jnp.exp2(other_log)
-    total = jnp.where(upper, other, 1.0) * total_ref[...] + jnp.where(upper, 1.0, kept) * got
+    mine = mine_ref[:n].astype(F32)
+    total = jnp.where(upper, other, 1.0) * mine + jnp.where(upper, 1.0, kept) * got
     passed = jnp.where(upper, 0.0, jnp.exp2(after_me)) * got
-    total_out[...] = total
     entering_out[...] = passed if entering_ref is None else entering_ref[...] + passed
     first = jnp.where(upper, 1.0, other)
     second = jnp.where(upper, kept, 1.0)
@@ -223,18 +222,16 @@
     sent_out[:n], sent_out[n:] = message(total, log)
 
 
-def scan_kernel(factor_ref, total_ref, got_ref, *refs):
+def scan_kernel(last, factor_ref, mine_ref, got_ref, *refs):
     refs = list(refs)
-    entering_ref = refs.pop(0) if len(refs) % 2 == 0 else None
+    entering_ref = refs.pop(0) if len(refs) == 3 - last else None
     factors = factor_ref[...]
     got = got_ref[...].astype(F32)
-    entering_out = refs[0]
-    if len(refs) == 3:
-        total = factors[0:1] * total_ref[...] + factors[1:2] * got
-        refs[1][...] = total
-        refs[2][...] = total.astype(BF16)
+    if not last:
+        total = factors[0:1] * mine_ref[...].astype(F32) + factors[1:2] * got
+        refs[1][...] = total.astype(BF16)
     passed = factors[2:3] * got
-    entering_out[...] = passed if entering_ref is None else entering_ref[...] + passed
+    refs[0][...] = passed if entering_ref is None else entering_ref[...] + passed
 
 
 def early_forward_kernel(count, f_ref, *refs):
@@ -246,7 +243,7 @@
 
 
 def late_forward_kernel(count, f_ref, part_ref, rt_ref, b_ref, kept_ref, *refs):
-    pieces, (x_ref, e_ref, total_ref, sent_ref, buffer) = refs[:count], refs[count:]
+    pieces, (x_ref, e_ref, sent_ref, buffer) = refs[:count], refs[count:]
     rows = pieces[0].shape[0]
     for index, piece in enumerate(pieces):
         buffer[index * rows : (index + 1) * rows] = piece[...]
@@ -261,7 +258,6 @@
         state = dot(b_ref[part], scaled, ((0,), (0,)))
         e_ref[k] = state
         total = state if total is None else kept_ref[k, :1] * total + state
-    total_ref[...] = total
     sent_ref[...] = total.astype(BF16)
 
 
@@ -288,13 +284,15 @@
         copies.append(mine)
     g = g_ref[...]
     half = away_ref.shape[1] // rows
-    bundle = 3 if count % 3 == 0 else count
+    starts = [0]
+    while starts[-1] < count:
+        starts.append(starts[-1] + (2 if count - starts[-1] in (2, 4) else 3))
     for index in range(count):
         for copy in copies[index]:
             copy.wait()
-        if (index + 1) % bundle:
+        if index + 1 not in starts:
             continue
-        start = index + 1 - bundle
+        start = starts[starts.index(index + 1) - 1]
         product = mm(buffer[start * rows : (index + 1) * rows], g)
         for done in range(start, index + 1):
             part = product[(done - start) * rows : (done - start + 1) * rows]
@@ -679,12 +677,10 @@
             pl.BlockSpec((length, WIDE), lambda h: (0, h)),
             pl.BlockSpec((spans, n, WIDE), lambda h: (0, 0, h)),
             state,
-            state,
         ],
         [
             shape(length, columns, dtype=BF16),
             shape(spans, n, columns),
-            shape(n, columns),
             shape(n, columns, dtype=BF16),
         ],
         2 * length * columns * deep,
@@ -734,50 +730,51 @@
             pl.BlockSpec((spans, n, WIDE), lambda h: (0, 0, h)),
             pl.BlockSpec((spans, 8, WIDE), lambda h: (0, 0, h)),
         ],
-        [pl.BlockSpec((rows, WIDE), lambda h: (0, h)) for rows in (n, 8, n + TAIL)],
-        [shape(n, columns), shape(8, columns), shape(n + TAIL, columns, dtype=BF16)],
+        [pl.BlockSpec((rows, WIDE), lambda h: (0, h)) for rows in (8, n + TAIL)],
+        [shape(8, columns), shape(n + TAIL, columns, dtype=BF16)],
         0,
         14 * n * columns,
     )(own_grads, kept)
 
 
-def back_step(place, log, total, sent, entering, bit):
+def back_step(place, log, sent, entering, bit):
     got = swap(sent, "ctx", bit)
-    n, columns = total.shape
-    tall = [pl.BlockSpec((rows, WIDE), lambda h: (0, h)) for rows in (8, n, n + TAIL)]
+    columns = sent.shape[1]
+    n = sent.shape[0] - TAIL
+    short, state, tall = [
+        pl.BlockSpec((rows, 2 * WIDE), lambda h: (0, h)) for rows in (8, n, n + TAIL)
+    ]
     return call(
         functools.partial(back_kernel, bit),
-        (columns // WIDE,),
-        [SCALARS] + tall + [tall[1]] * len(entering),
-        [tall[1], tall[1], tall[2], tall[0], tall[0]],
+        (columns // (2 * WIDE),),
+        [SCALARS, short, tall, tall] + [state] * len(entering),
+        [state, tall, short, short],
         [
-            shape(n, columns),
             shape(n, columns),
             shape(n + TAIL, columns, dtype=BF16),
             shape(8, columns),
             shape(8, columns),
         ],
         0,
-        18 * n * columns,
-    )(place, log, total, got, *entering)
-
-
-def scan_step(factors, here, total, sent, entering, bit, last=False):
+        14 * n * columns,
+    )(place, log, sent, got, *entering)
+
+
+def scan_step(factors, here, sent, entering, bit, last=False):
     got = swap(sent, "ctx", bit)
-    n, columns = total.shape
-    block = pl.BlockSpec((n, WIDE), lambda h: (0, h))
-    outs = [shape(n, columns), shape(n, columns), shape(n, columns, dtype=BF16)]
-    outs = outs[:1] if last else outs
-    out = call(
-        scan_kernel,
-        (columns // WIDE,),
-        [pl.BlockSpec((8, WIDE), lambda h: (0, h + here)), block, block] + [block] * len(entering),
+    n, columns = sent.shape
+    block = pl.BlockSpec((n, columns), lambda h: (0, 0))
+    at = here * WIDE // columns
+    outs = [shape(n, columns), shape(n, columns, dtype=BF16)][: 2 - last]
+    return call(
+        functools.partial(scan_kernel, last),
+        (1,),
+        [pl.BlockSpec((8, columns), lambda h: (0, at)), block, block] + [block] * len(entering),
         [block] * len(outs),
         outs,
         0,
-        14 * n * columns,
-    )(factors, total, got, *entering)
-    return out if last else (out[1], out[0], out[2])
+        10 * n * columns,
+    )(factors, sent, got, *entering)
 
 
 def local(inputs, w_in, b_rows, c_rows, log_decay, skip_gain, grad_out):
@@ -884,15 +881,16 @@
     other = swap(inputs, "head", 1)
     running, running_t, kept, own_grads = prepare(log_decay, grad_out, c_rows)
     spot = lax.axis_index("ctx").astype(jnp.int32)[None]
-    back, log, sent = back_start(own_grads, kept)
+    log, sent = back_start(own_grads, kept)
     sent = after([sent], other)[0]
-    back, leaving, sent, log, factors_1 = back_step(spot, log, back, sent, (), 1)
-
-    z1, inner2, own_y, sent = after([z1, inner2, own_y, sent], own_x)
+    leaving, moved, log, factors_1 = back_step(spot, log, sent, (), 1)
+
+    z1, inner2, own_y = after([z1, inner2, own_y], own_x, sent)
+    sent = moved
     x1, y1 = swap_x(z1), swap_y(z1)
     inner3, outer2 = along_z(z1, MIDDLE), along_z(inner2, OUTWARD)
     own_y_a, own_y_b = own_y[:, :half], own_y[:, half:]
-    back, leaving, sent, log, factors_2 = back_step(spot, log, back, sent, (leaving,), 2)
+    leaving, sent, log, factors_2 = back_step(spot, log, sent, (leaving,), 2)
     order_own = (order + place * (blocks // 2)) % blocks
     cut = len(EARLY) * w_in.shape[0]
     early_features, late_features = call(
@@ -913,24 +911,21 @@
     x3, y3 = swap_x(z3), swap_y(z3)
     outer3 = along_z(inner3, OUTWARD)
     x1_a, x1_b = x1[:, :half], x1[:, half:]
-    back, leaving, sent, log, factors_4 = back_step(spot, log, back, sent, (leaving,), 4)
-
-    inner3, outer3, y3, x1_a, x1_b, sent = after([inner3, outer3, y3, x1_a, x1_b, sent], x3)
+    leaving, sent, log, factors_4 = back_step(spot, log, sent, (leaving,), 4)
+
+    inner3, outer3, y3, x1_a, x1_b = after([inner3, outer3, y3, x1_a, x1_b], x3)
     z2a = inner3[:, :half] + outer3[:, :half]
     z2b = inner3[:, half:] + outer3[:, half:]
     y3_a, y3_b = y3[:, :half], y3[:, half:]
     x2a, y2a = swap_x(z2a), swap_y(z2a)
     d3a, d1a = swap_x(y3_a), swap_y(x1_a)
-    back, leaving, sent, log, factors_8 = back_step(spot, log, back, sent, (leaving,), 8)
+    leaving, sent, log, factors_8 = back_step(spot, log, sent, (leaving,), 8)
     early = [w_in, own_x, own_y, z1, x1, y1, z3, x3, y3]
     part = early_forward(early_features, early)
 
-    own_y_a, x2a, z2b, y3_b, x1_b, leaving = after(
-        [own_y_a, x2a, z2b, y3_b, x1_b, leaving], y2a, d3a, d1a, part
-    )
+    own_y_a, x2a, z2b, leaving = after([own_y_a, x2a, z2b, leaving], y2a, d3a, d1a, part)
     d0a, d2a = swap_x(own_y_a), swap_y(x2a)
     x2b, y2b = swap_x(z2b), swap_y(z2b)
-    d3b, d1b = swap_x(y3_b), swap_y(x1_b)
     leaving_all = [leaving]
     for k in range(spans - 1, 0, -1):
         leaving_all.insert(0, own_grads[k] + kept[k, :1] * leaving_all[0])
@@ -939,52 +934,54 @@
     grad_x = grad_rows(running, running_t, grad_out, b_rows, c_rows, leaving_all, skip, True)
     order_away = (order + (1 - place) * (blocks // 2)) % blocks
     early_order, late_order = order_away[: len(EARLY)], order_away[len(EARLY) :]
-    product = multiply_blocks(early_order, grad_x, [[piece] for piece in early], ())
     late_a = [d0a, d1a, d3a, z2a, x2a, y2a, d2a]
-    x_a, states_a, total_a, sent_a = late_forward(
+    x_a, states_a, sent_a = late_forward(
         late_features, part, late_a, running_t, b_rows, kept, 0
     )
 
-    own_y_b, x2b, sent_a, x_a = after(
-        [own_y_b, x2b, sent_a, x_a], y2b, d3b, d1b, product[0]
+    own_y_b, x2b, y3_b, x1_b, sent_a, x_a, grad_x = after(
+        [own_y_b, x2b, y3_b, x1_b, sent_a, x_a, grad_x], y2b
     )
     d0b, d2b = swap_x(own_y_b), swap_y(x2b)
-    total_a, entering_a, sent_a = scan_step(factors_1, 0, total_a, sent_a, (), 1)
+    d3b, d1b = swap_x(y3_b), swap_y(x1_b)
+    entering_a, sent_a = scan_step(factors_1, 0, sent_a, (), 1)
+    product = multiply_blocks(early_order, grad_x, [[piece] for piece in early], ())
     shared = (running, running_t, grad_out)
     here = groups // 2
     grid = (spans, here)
     inner_a = shared + (x_a, b_rows, c_rows, leaving_all)
     decay_a, grad_b, grad_c = inner(grid, 0, half, inner_a, ())
 
-    d0b, d2b = after([d0b, d2b], sent_a, grad_b)
+    d0b, d2b = after([d0b, d2b], d3b, d1b, sent_a, grad_b, product[0])
     late_b = [d0b, d1b, d3b, z2b, x2b, y2b, d2b]
-    x_b, states_b, total_b, sent_b = late_forward(
+    x_b, states_b, sent_b = late_forward(
         late_features, part, late_b, running_t, b_rows, kept, here
     )
     pairs = list(zip(late_a, late_b))
     sent_a, sent_b, *product = after([sent_a, sent_b, *product])
-    total_b, entering_b, sent_b = scan_step(factors_1, here, total_b, sent_b, (), 1)
-    total_a, entering_a, sent_a = scan_step(factors_2, 0, total_a, sent_a, (entering_a,), 2)
+    entering_b, sent_b = scan_step(factors_1, here, sent_b, (), 1)
+    entering_a, sent_a = scan_step(factors_2, 0, sent_a, (entering_a,), 2)
     away, own = multiply_blocks(late_order, grad_x, pairs, product)
 
     sent_a, sent_b, x_b, away = after([sent_a, sent_b, x_b, away])
-    total_b, entering_b, sent_b = scan_step(factors_2, here, total_b, sent_b, (entering_b,), 2)
-    total_a, entering_a, sent_a = scan_step(factors_4, 0, total_a, sent_a, (entering_a,), 4)
+    entering_b, sent_b = scan_step(factors_2, here, sent_b, (entering_b,), 2)
+    entering_a, sent_a = scan_step(factors_4, 0, sent_a, (entering_a,), 4)
     got = swap(away, "head", 1)
     inner_b = shared + (x_b, b_rows, c_rows, leaving_all)
     decay_b, grad_b, grad_c = inner(grid, here, half, inner_b, (grad_b, grad_c))
 
     sent_a, sent_b, got, grad_b = after([sent_a, sent_b, got, grad_b])
-    total_b, entering_b, sent_b = scan_step(factors_4, here, total_b, sent_b, (entering_b,), 4)
-    (entering_a,) = scan_step(factors_8, 0, total_a, sent_a, (entering_a,), 8, True)
+    entering_b, sent_b = scan_step(factors_4, here, sent_b, (entering_b,), 4)
+    (entering_a,) = scan_step(factors_8, 0, sent_a, (entering_a,), 8, True)
+    grad_b = head_sum(grad_b)
+
+    sent_b, entering_a, got = after([sent_b, entering_a, got], grad_b)
     grad_inputs = (own.astype(F32) + got.astype(F32)).astype(BF16)
-    grad_b = head_sum(grad_b)
-
-    sent_b, entering_a = after([sent_b, entering_a], grad_inputs, grad_b)
-    (entering_b,) = scan_step(factors_8, here, total_b, sent_b, (entering_b,), 8, True)
+    (entering_b,) = scan_step(factors_8, here, sent_b, (entering_b,), 8, True)
     common = (running_t, grad_out, c_rows)
     state_a = common + (entering_a, states_a, leaving_all, kept, decay_a, grad_c)
     decays, grad_c = state_terms(grid, 0, half, state_a, heads)
+    (entering_b,) = after([entering_b], grad_inputs, grad_c)
     state_b = common + (entering_b, states_b, leaving_all, kept, decay_b, grad_c)
     decays, grad_c = state_terms(grid, here, half, state_b, heads, decays)
     return (grad_inputs, grad_b, head_sum(grad_c), decays)

time: 320 us -> 291 us (0.909)
  waiting for transfers between devices: 103 us -> 84.8 us
  Pallas kernels: 134 us -> 127 us
  starting transfers between devices: 47.5 us -> 42.6 us
    ppermute x35, waiting for transfers between devices: 103 us -> 84.8 us  [swap(): return lax.ppermute(value, axis, [(i, i ^ bit) for i in range(count)])]
    pallas_call x12, Pallas kernels: 33.5 us -> 27.6 us  [the longest x8 17.1 us: scan_step(): call(functools.partial(scan_kernel, last), (1,), [pl.BlockSpec((8, column...]
    ppermute x35, starting transfers between devices: 41.4 us -> 36.3 us  [swap(): return lax.ppermute(value, axis, [(i, i ^ bit) for i in range(count)])]
  transfers between devices with their start and end apart: 39 -> 39, of which waited for: 9 -> 14; matrix products, arithmetic and copies ran while one was open for 7% -> 10% of each run, Pallas kernels for 36% -> 37%
where the time goes in v9:
time: 291 us; the launch traced here: 290 us
  Pallas kernels  127 us (44%)
  waiting for transfers between devices  84.8 us (29%)
  starting transfers between devices  42.6 us (15%)
  other arithmetic  19 us (7%)
  local copies, waits for them, and re-layouts  13.2 us (5%)
  between operations  3.57 us (1%)
    ppermute x35, waiting for transfers between devices, swap(): return lax.ppermute(value, axis, [(i, i ^ bit) for i in range(count)])  84.8 us
    ppermute x35, starting transfers between devices, swap(): return lax.ppermute(value, axis, [(i, i ^ bit) for i in range(count)])  36.3 us
    pallas_call x2, Pallas kernels, multiply_blocks(): pl.pallas_call(functools.partial(blocks_kernel, [len(piece) for piece in...  18.9 us
    pallas_call x2, Pallas kernels, inner(): call(inner_kernel, grid, specs + [SHARED] * len(so_far), [run_spec(), SHA...  17.8 us
    pallas_call x8, Pallas kernels, scan_step(): call(functools.partial(scan_kernel, last), (1,), [pl.BlockSpec((8, column...  17.1 us
    pallas_call x2, Pallas kernels, late_forward(): call(functools.partial(late_forward_kernel, len(pieces)), (columns // WID...  12.9 us
    pallas_call x2, Pallas kernels, state_terms(): pl.pallas_call(state_kernel, grid=grid, in_specs=[run_t_spec(here), rows_...  11 us
    pallas_call x4, Pallas kernels, back_step(): call(functools.partial(back_kernel, bit), (columns // (2 * WIDE),), [SCAL...  10.5 us
  transfers between devices with their start and end apart: 39, of which 14 were waited for; matrix products, arithmetic and copies ran while one was open for 10% of the time, Pallas kernels for 37%

profile of v9, /device:TPU:0, one launch (start us, length us, event | category | flops | bytes accessed | tf_op | source)
XLA Modules:
  0.0 289.8 jit_solution(11574395885547719319)
XLA Ops:
  1.1 2.7 collective-permute-start
  3.8 1.6 collective-permute-start.1
  5.5 1.5 collective-permute-start.2
  7.0 1.5 collective-permute-start.3
  8.5 9.1 %shard_map.111 = (f32[32,512]{1,0:T(8,128)}, f32[4,512,8]{2,1,0:T(8,128)}, f32[2,8,2048]{2,1,0:T(8,128)}, f32[2,128,2048]{2,1,0:T(8,128)}) custom-call(f32[32,512]{1,0:T(8,128)} %d_ref.1, bf16[512,2048]{1,0:T(8,128)(2,1)} %g_ref.11, bf16[512,128]{1,0:T(8,128)(2,1)} %c_ref.11), custom_call_target="tpu_custom_call" | custom-call | flops 268435456 | bytes 6291456 | tf_op jit(solution)/shard_map/pallas_call | solution.py:794
  17.5 3.6 %shard_map.112 = (f32[8,2048]{1,0:T(8,128)}, bf16[144,2048]{1,0:T(8,128)(2,1)}) custom-call(f32[2,128,2048]{2,1,0:T(8,128)} %get-tuple-element.101.own_ref, f32[2,8,2048]{2,1,0:T(8,128)} %get-tuple-element.102.kept_ref.a_ref), custom_call_target="tpu_custom_call" | custom-call | bytes 3670016 | tf_op jit(solution)/shard_map/pallas_call | solution.py:726
  21.7 6.1 %collective-permute-done.refs_0_ = bf16[256,2048]{1,0:T(8,128)(2,1)} collective-permute-done((bf16[256,2048]{1,0:T(8,128)(2,1)}, bf16[256,2048]{1,0:T(8,128)(2,1)}, u32[]{:S(2)}, u32[]{:S(2)}) %collective-permute-start) | collective-permute-done | bytes 1048608 | tf_op jit(solution)/shard_map/ppermute | solution.py:470
  27.9 3.1 %collective-permute-done.2.refs_2_ = bf16[256,2048]{1,0:T(8,128)(2,1)} collective-permute-done((bf16[256,2048]{1,0:T(8,128)(2,1)}, bf16[256,2048]{1,0:T(8,128)(2,1)}, u32[]{:S(2)}, u32[]{:S(2)}) %collective-permute-start.2) | collective-permute-done | bytes 1048608 | tf_op jit(solution)/shard_map/ppermute | solution.py:470
  31.0 2.3 collective-permute-done.3.refs_3_.refs_1_
  33.3 1.7 collective-permute-start.5
  36.3 1.6 collective-permute-start.7
  38.4 1.3 constant_dynamic-slice_fusion
  39.7 6.2 %collective-permute-done.8.got_ref = bf16[144,2048]{1,0:T(8,128)(2,1)} collective-permute-done((bf16[144,2048]{1,0:T(8,128)(2,1)}, bf16[144,2048]{1,0:T(8,128)(2,1)}, u32[]{:S(2)}, u32[]{:S(2)}) %collective-permute-start.8) | collective-permute-done | bytes 589856 | tf_op jit(solution)/shard_map/ppermute | solution.py:470
  46.0 2.4 shard_map.115
  49.0 1.4 fusion.7
  53.6 5.1 %shard_map.117 = (bf16[512,2304]{1,0:T(8,128)(2,1)}, bf16[512,1792]{1,0:T(8,128)(2,1)}) custom-call(s32[16]{0:T(128)} %get-tuple-element.213.order_ref, bf16[512,2048]{1,0:T(8,128)(2,1)} %own_ref.1, bf16[512,2048]{1,0:T(8,128)(2,1)} %collective-permute-done.4.refs_1_.other_ref), custom_call_target="tpu_custom_call" | custom-call | bytes 8388608 | tf_op jit(solution)/shard_map/pallas_call | solution.py:896
  58.8 2.3 fusion.6
  61.1 12.5 %collective-permute-done.9.got_ref = bf16[144,2048]{1,0:T(8,128)(2,1)} collective-permute-done((bf16[144,2048]{1,0:T(8,128)(2,1)}, bf16[144,2048]{1,0:T(8,128)(2,1)}, u32[]{:S(2)}, u32[]{:S(2)}) %collective-permute-start.9) | collective-permute-done | bytes 589856 | tf_op jit(solution)/shard_map/ppermute | solution.py:470
  73.6 2.7 shard_map.116
  76.3 1.6 collective-permute-start.11
  77.9 2.9 %add.123.refs_6_ = bf16[256,2048]{1,0:T(8,128)(2,1)} add(bf16[256,2048]{1,0:T(8,128)(2,1)} %get-tuple-element.116, bf16[256,2048]{1,0:T(8,128)(2,1)} %get-tuple-element.117) | non-fusion elementwise | flops 524288 | bytes 3145728 | tf_op jit(solution)/shard_map/add | solution.py:910
  82.0 5.1 %collective-permute-start.15 = (bf16[144,2048]{1,0:T(8,128)(2,1)S(1)}, bf16[144,2048]{1,0:T(8,128)(2,1)S(1)}, u32[]{:S(2)}, u32[]{:S(2)}) collective-permute-start(bf16[144,2048]{1,0:T(8,128)(2,1)S(1)} %copy-done), channel_id=1, source_target_pairs={{0,8},{2,10},{4,12},{6,14},{8,0},{10,2},{12,4},{14,6},{16,24},{18,... | collective-permute-start | bytes 1769480 | tf_op jit(solution)/shard_map/ppermute | solution.py:470
  87.2 2.2 fusion.5
  89.4 25.3 %collective-permute-done.15.got_ref = bf16[144,2048]{1,0:T(8,128)(2,1)S(1)} collective-permute-done((bf16[144,2048]{1,0:T(8,128)(2,1)S(1)}, bf16[144,2048]{1,0:T(8,128)(2,1)S(1)}, u32[]{:S(2)}, u32[]{:S(2)}) %collective-permute-start.15) | collective-permute-done | bytes 589856 | tf_op jit(solution)/shard_map/ppermute | solution.py:470
  115.5 2.7 shard_map.120
  118.3 2.6 slice_add_fusion
  122.1 2.3 fusion.4
  124.4 1.5 collective-permute-start.18
  125.9 1.3 collective-permute-start.19
  127.3 1.4 slice.86
  130.0 10.2 %shard_map.122.refs_7_.part_ref = f32[512,2048]{1,0:T(8,128)} custom-call(bf16[512,2304]{1,0:T(8,128)(2,1)} %get-tuple-element.112.refs_8_.f_ref, bf16[256,2048]{1,0:T(8,128)(2,1)} %refs_0_.3, bf16[256,2048]{1,0:T(8,128)(2,1)} %collective-permute-done.3.refs_3_.refs_1_, bf16[256,2048]{1,0:T(8,128)(2,1)} %get-tuple-element.111.refs_2_, ...), custom_call_target="tpu_custom_call" | custom-call | flops 4831838208 | bytes 9437184 | tf_op jit(solution)/shard_map/pallas_call | solution.py:645
  140.2 1.9 collective-permute-done.16.got_ref
  142.0 2.7 shard_map.121
  146.2 1.5 collective-permute-start.21
  148.9 2.1 fusion.1
  152.1 10.4 %shard_map.125.refs_6_ = bf16[2048,512]{1,0:T(8,128)(2,1)} custom-call(f32[32,512]{1,0:T(8,128)} %get-tuple-element.138.r_ref, f32[4,512,8]{2,1,0:T(8,128)} %get-tuple-element.133.rt_ref, bf16[512,2048]{1,0:T(8,128)(2,1)} %g_ref.11, bf16[512,128]{1,0:T(8,128)(2,1)} %b_ref.9, bf16[512,128]{1,0:T(8,128)(2,1)} %c_ref.11, ...), custom_call_target="tpu_custom_call" | custom-call | flops 2147483648 | bytes 6291456 | tf_op jit(solution)/shard_map/pallas_call | solution.py:995
  162.5 7.8 %collective-permute-done.21.refs_0_ = bf16[256,1024]{1,0:T(8,128)(2,1)} collective-permute-done((bf16[256,1024]{1,0:T(8,128)(2,1)}, bf16[256,1024]{1,0:T(8,128)(2,1)}, u32[]{:S(2)}, u32[]{:S(2)}) %collective-permute-start.21) | collective-permute-done | bytes 524320 | tf_op jit(solution)/shard_map/ppermute | solution.py:470
  170.5 6.5 %shard_map.124 = (bf16[512,1024]{1,0:T(8,128)(2,1)}, f32[2,128,1024]{2,1,0:T(8,128)}, bf16[128,1024]{1,0:T(8,128)(2,1)}) custom-call(bf16[512,1792]{1,0:T(8,128)(2,1)} %get-tuple-element.132.f_ref, f32[512,2048]{1,0:T(8,128)} %shard_map.122.refs_7_.part_ref, f32[4,512,8]{2,1,0:T(8,128)} %get-tuple-element.133.rt_ref, bf16[512,128]{1,0:T(8,128)(2,1)} %b_ref.9, ...), custom_call_target="tpu_custom_call" | custom-call | flops 1879048192 | bytes 3670016 | tf_op jit(solution)/shard_map/pallas_call | solution.py:665
  177.0 1.6 collective-permute-start.28
  179.9 1.5 collective-permute-start.26
  182.7 10.0 %shard_map.129 = (bf16[512,2048]{1,0:T(8,128)(2,1)}, bf16[512,2048]{1,0:T(8,128)(2,1)}) custom-call(s32[9]{0:T(128)} %bitcast.34, bf16[2048,512]{1,0:T(8,128)(2,1)} %get-tuple-element.140.g_ref, bf16[256,2048]{1,0:T(8,128)(2,1)} %refs_0_.3, bf16[256,2048]{1,0:T(8,128)(2,1)} %collective-permute-done.3.refs_3_.refs_1_, ...), custom_call_target="tpu_custom_call" | custom-call | flops 4831838208 | bytes 9437184 | tf_op jit(solution)/shard_map/pallas_call | solution.py:699
  192.7 8.8 %shard_map.128 = (f32[16,512]{1,0:T(8,128)}, f32[512,128]{1,0:T(8,128)}, f32[512,128]{1,0:T(8,128)}) custom-call(f32[32,512]{1,0:T(8,128)} %get-tuple-element.138.r_ref, f32[4,512,8]{2,1,0:T(8,128)} %get-tuple-element.133.rt_ref, bf16[512,2048]{1,0:T(8,128)(2,1)} %g_ref.11, bf16[512,1024]{1,0:T(8,128)(2,1)} %get-tuple-element.148.x_ref, ...), custom_call_target="tpu_custom_call" | custom-call | flops 1610612736 | bytes 3145728 | tf_op jit(solution)/shard_map/pallas_call | solution.py:822
  201.5 2.0 shard_map.127
  203.5 3.5 %collective-permute-done.26.refs_2_.refs_5_ = bf16[256,1024]{1,0:T(8,128)(2,1)} collective-permute-done((bf16[256,1024]{1,0:T(8,128)(2,1)}, bf16[256,1024]{1,0:T(8,128)(2,1)}, u32[]{:S(2)}, u32[]{:S(2)}) %collective-permute-start.26) | collective-permute-done | bytes 524320 | tf_op jit(solution)/shard_map/ppermute | solution.py:470
  207.0 6.4 %shard_map.131 = (bf16[512,1024]{1,0:T(8,128)(2,1)}, f32[2,128,1024]{2,1,0:T(8,128)}, bf16[128,1024]{1,0:T(8,128)(2,1)}) custom-call(bf16[512,1792]{1,0:T(8,128)(2,1)} %get-tuple-element.132.f_ref, f32[512,2048]{1,0:T(8,128)} %shard_map.122.refs_7_.part_ref, f32[4,512,8]{2,1,0:T(8,128)} %get-tuple-element.133.rt_ref, bf16[512,128]{1,0:T(8,128)(2,1)} %b_ref.9, ...), custom_call_target="tpu_custom_call" | custom-call | flops 1879048192 | bytes 3670016 | tf_op jit(solution)/shard_map/pallas_call | solution.py:665
  214.3 1.4 collective-permute-start.30
  215.8 8.9 %shard_map.133 = (bf16[512,2048]{1,0:T(8,128)(2,1)}, bf16[512,2048]{1,0:T(8,128)(2,1)}) custom-call(s32[7]{0:T(128)} %slice.74.order_ref, bf16[2048,512]{1,0:T(8,128)(2,1)} %get-tuple-element.140.g_ref, bf16[256,1024]{1,0:T(8,128)(2,1)} %collective-permute-done.21.refs_0_, ...), custom_call_target="tpu_custom_call", output_to_operand_aliasing={{0}: (16, {}), {1}: (17, {})} | custom-call | flops 3758096384 | bytes 7340032 | tf_op jit(solution)/shard_map/pallas_call | solution.py:699
  224.7 2.1 shard_map.135
  226.8 2.2 shard_map.134
  230.3 9.0 %shard_map.139 = (f32[16,512]{1,0:T(8,128)}, f32[512,128]{1,0:T(8,128)}, f32[512,128]{1,0:T(8,128)}) custom-call(f32[32,512]{1,0:T(8,128)} %get-tuple-element.138.r_ref, f32[4,512,8]{2,1,0:T(8,128)} %get-tuple-element.133.rt_ref, bf16[512,2048]{1,0:T(8,128)(2,1)} %g_ref.11, bf16[512,1024]{1,0:T(8,128)(2,1)} %get-tuple-element.174.x_ref, ...), custom_call_target="tpu_custom_call" | custom-call | flops 1610612736 | bytes 3145728 | tf_op jit(solution)/shard_map/pallas_call | solution.py:822
  239.3 2.2 shard_map.138
  241.5 2.2 shard_map.137
  245.0 1.9 collective-permute-start.34
  247.5 1.7 convert_add_fusion.1.refs_3_
  249.2 9.9 %collective-permute-done.34.got_ref = bf16[128,1024]{1,0:T(8,128)(2,1)} collective-permute-done((bf16[128,1024]{1,0:T(8,128)(2,1)}, bf16[128,1024]{1,0:T(8,128)(2,1)}, u32[]{:S(2)}, u32[]{:S(2)}) %collective-permute-start.34) | collective-permute-done | bytes 262176 | tf_op jit(solution)/shard_map/ppermute | solution.py:470
  259.1 2.2 shard_map.141
  262.1 2.1 shard_map.142.refs_1_
  264.5 4.4 %add_convert_fusion.refs_1_ = bf16[512,2048]{1,0:T(8,128)(2,1)} fusion(bf16[512,2048]{1,0:T(8,128)(2,1)} %get-tuple-element.185, bf16[512,2048]{1,0:T(8,128)(2,1)} %get-tuple-element.157), kind=kLoop, calls=%fused_computation | loop fusion | flops 4194304 | bytes 6291456 | tf_op jit(solution)/shard_map/convert_element_type | solution.py:979
  268.9 5.5 %shard_map.145 = (f32[32,512]{1,0:T(8,128)}, f32[512,128]{1,0:T(8,128)}) custom-call(f32[4,512,8]{2,1,0:T(8,128)} %get-tuple-element.133.rt_ref, bf16[512,2048]{1,0:T(8,128)(2,1)} %g_ref.11, bf16[512,128]{1,0:T(8,128)(2,1)} %c_ref.11, f32[128,1024]{1,0:T(8,128)} %get-tuple-element.188.s_ref, f32[2,128,1024]{2,1,0:T(8,128)} %get-tuple-element.189.e_ref, ...), custom_call_target="tpu_custom_call" | custom-call | flops 268435456 | bytes 3145728 | tf_op jit(solution)/shard_map/pallas_call | solution.py:840
  274.4 3.7 %collective-permute-done.37.got_ref = bf16[128,1024]{1,0:T(8,128)(2,1)} collective-permute-done((bf16[128,1024]{1,0:T(8,128)(2,1)}, bf16[128,1024]{1,0:T(8,128)(2,1)}, u32[]{:S(2)}, u32[]{:S(2)}) %collective-permute-start.37) | collective-permute-done | bytes 262176 | tf_op jit(solution)/shard_map/ppermute | solution.py:470
  278.1 2.1 shard_map.144.refs_0_
  280.2 5.5 %shard_map.147 = (f32[32,512]{1,0:T(8,128)}, f32[512,128]{1,0:T(8,128)}) custom-call(f32[4,512,8]{2,1,0:T(8,128)} %get-tuple-element.133.rt_ref, bf16[512,2048]{1,0:T(8,128)(2,1)} %g_ref.11, bf16[512,128]{1,0:T(8,128)(2,1)} %c_ref.11, f32[128,1024]{1,0:T(8,128)} %shard_map.146.s_ref, ...), custom_call_target="tpu_custom_call", output_to_operand_aliasing={{0}: (9, {})} | custom-call | flops 268435456 | bytes 3145728 | tf_op jit(solution)/shard_map/pallas_call | solution.py:840
  286.8 1.3 collective-permute-done.38
  288.1 1.7 convert_add_fusion
  (79 shorter events, 21.5 us)
Async XLA Ops:
  0.6 20.5 %collective-permute-start.4 = (bf16[512,2048]{1,0:T(8,128)(2,1)}, bf16[512,2048]{1,0:T(8,128)(2,1)}, u32[]{:S(2)}, u32[]{:S(2)}) collective-permute-start(bf16[512,2048]{1,0:T(8,128)(2,1)} %own_ref.1), channel_id=1, source_target_pairs={{0,1},{1,0},{2,3},{3,2},{4,5},{5,4},{6,7},{7,6},{8,9},{9,8},{10,11... | collective-permute-start | bytes 6291464 | tf_op jit(solution)/shard_map/ppermute | solution.py:470
  1.1 26.7 %collective-permute-start = (bf16[256,2048]{1,0:T(8,128)(2,1)}, bf16[256,2048]{1,0:T(8,128)(2,1)}, u32[]{:S(2)}, u32[]{:S(2)}) collective-permute-start(bf16[256,2048]{1,0:T(8,128)(2,1)} %refs_0_.3), channel_id=1, source_target_pairs={{0,8},{2,10},{4,12},{6,14},{8,0},{10,2},{12,4},{14,6},{16,24},{18,... | collective-permute-start | bytes 3145736 | tf_op jit(solution)/shard_map/ppermute | solution.py:470
  3.8 24.1 %collective-permute-start.1 = (bf16[256,2048]{1,0:T(8,128)(2,1)}, bf16[256,2048]{1,0:T(8,128)(2,1)}, u32[]{:S(2)}, u32[]{:S(2)}) collective-permute-start(bf16[256,2048]{1,0:T(8,128)(2,1)} %refs_0_.3), channel_id=1, source_target_pairs={{8,16},{10,18},{12,20},{14,22},{16,8},{18,10},{20,12},{22,14},{9,1... | collective-permute-start | bytes 3145736 | tf_op jit(solution)/shard_map/ppermute | solution.py:531
  5.5 25.5 %collective-permute-start.2 = (bf16[256,2048]{1,0:T(8,128)(2,1)}, bf16[256,2048]{1,0:T(8,128)(2,1)}, u32[]{:S(2)}, u32[]{:S(2)}) collective-permute-start(bf16[256,2048]{1,0:T(8,128)(2,1)} %refs_0_.3), channel_id=1, source_target_pairs={{0,4},{2,6},{4,0},{6,2},{8,12},{10,14},{12,8},{14,10},{16,20},{18,... | collective-permute-start | bytes 3145736 | tf_op jit(solution)/shard_map/ppermute | solution.py:470
  7.0 26.4 %collective-permute-start.3 = (bf16[256,2048]{1,0:T(8,128)(2,1)}, bf16[256,2048]{1,0:T(8,128)(2,1)}, u32[]{:S(2)}, u32[]{:S(2)}) collective-permute-start(bf16[256,2048]{1,0:T(8,128)(2,1)} %refs_0_.3), channel_id=1, source_target_pairs={{0,2},{2,0},{4,6},{6,4},{8,10},{10,8},{12,14},{14,12},{16,18},{18,... | collective-permute-start | bytes 3145736 | tf_op jit(solution)/shard_map/ppermute | solution.py:470
  21.1 24.9 %collective-permute-start.8 = (bf16[144,2048]{1,0:T(8,128)(2,1)}, bf16[144,2048]{1,0:T(8,128)(2,1)}, u32[]{:S(2)}, u32[]{:S(2)}) collective-permute-start(bf16[144,2048]{1,0:T(8,128)(2,1)} %shard_map.113.refs_4_.mine_ref), channel_id=1, source_target_pairs={{0,2},{2,0},{4,6},{6,4},{8,10},{10,8},{12,14},{14,12},{16,18},{18,... | collective-permute-start | bytes 1769480 | tf_op jit(solution)/shard_map/ppermute | solution.py:470
  33.3 42.9 %collective-permute-start.5 = (bf16[256,2048]{1,0:T(8,128)(2,1)}, bf16[256,2048]{1,0:T(8,128)(2,1)}, u32[]{:S(2)}, u32[]{:S(2)}) collective-permute-start(bf16[256,2048]{1,0:T(8,128)(2,1)} %get-tuple-element.105.refs_3_), channel_id=1, source_target_pairs={{8,16},{10,18},{12,20},{14,22},{16,8},{18,10},{20,12},{22,14},{9,1... | collective-permute-start | bytes 3145736 | tf_op jit(solution)/shard_map/ppermute | solution.py:531
  35.1 41.2 %collective-permute-start.6 = (bf16[256,2048]{1,0:T(8,128)(2,1)}, bf16[256,2048]{1,0:T(8,128)(2,1)}, u32[]{:S(2)}, u32[]{:S(2)}) collective-permute-start(bf16[256,2048]{1,0:T(8,128)(2,1)} %get-tuple-element.104.refs_0_), channel_id=1, source_target_pairs={{8,0},{10,2},{12,4},{14,6},{16,24},{18,26},{20,28},{22,30},{9,1},{... | collective-permute-start | bytes 3145736 | tf_op jit(solution)/shard_map/ppermute | solution.py:531
  36.3 39.9 %collective-permute-start.7 = (bf16[256,2048]{1,0:T(8,128)(2,1)}, bf16[256,2048]{1,0:T(8,128)(2,1)}, u32[]{:S(2)}, u32[]{:S(2)}) collective-permute-start(bf16[256,2048]{1,0:T(8,128)(2,1)} %get-tuple-element.105.refs_3_), channel_id=1, source_target_pairs={{0,2},{2,0},{4,6},{6,4},{8,10},{10,8},{12,14},{14,12},{16,18},{18,... | collective-permute-start | bytes 3145736 | tf_op jit(solution)/shard_map/ppermute | solution.py:470
  37.9 38.4 %collective-permute-start.10 = (bf16[256,2048]{1,0:T(8,128)(2,1)}, bf16[256,2048]{1,0:T(8,128)(2,1)}, u32[]{:S(2)}, u32[]{:S(2)}) collective-permute-start(bf16[256,2048]{1,0:T(8,128)(2,1)} %get-tuple-element.105.refs_3_), channel_id=1, source_target_pairs={{0,4},{2,6},{4,0},{6,2},{8,12},{10,14},{12,8},{14,10},{16,20},{18,... | collective-permute-start | bytes 3145736 | tf_op jit(solution)/shard_map/ppermute | solution.py:470
  48.4 25.2 %collective-permute-start.9 = (bf16[144,2048]{1,0:T(8,128)(2,1)}, bf16[144,2048]{1,0:T(8,128)(2,1)}, u32[]{:S(2)}, u32[]{:S(2)}) collective-permute-start(bf16[144,2048]{1,0:T(8,128)(2,1)} %get-tuple-element.108.mine_ref), channel_id=1, source_target_pairs={{0,4},{2,6},{4,0},{6,2},{8,12},{10,14},{12,8},{14,10},{16,20},{18,... | collective-permute-start | bytes 1769480 | tf_op jit(solution)/shard_map/ppermute | solution.py:470
  76.3 5.7 %copy-start = (bf16[144,2048]{1,0:T(8,128)(2,1)S(1)}, bf16[144,2048]{1,0:T(8,128)(2,1)}, u32[]{:S(2)}) copy-start(bf16[144,2048]{1,0:T(8,128)(2,1)} %get-tuple-element.122.mine_ref) | copy-start | bytes 1769476
  76.3 41.9 %collective-permute-start.11 = (bf16[256,2048]{1,0:T(8,128)(2,1)}, bf16[256,2048]{1,0:T(8,128)(2,1)}, u32[]{:S(2)}, u32[]{:S(2)}) collective-permute-start(bf16[256,2048]{1,0:T(8,128)(2,1)} %get-tuple-element.115.refs_0_), channel_id=1, source_target_pairs={{8,0},{10,2},{12,4},{14,6},{16,24},{18,26},{20,28},{22,30},{9,1},{... | collective-permute-start | bytes 3145736 | tf_op jit(solution)/shard_map/ppermute | solution.py:531
  80.9 37.4 %collective-permute-start.12 = (bf16[256,2048]{1,0:T(8,128)(2,1)}, bf16[256,2048]{1,0:T(8,128)(2,1)}, u32[]{:S(2)}, u32[]{:S(2)}) collective-permute-start(bf16[256,2048]{1,0:T(8,128)(2,1)} %add.123.refs_6_), channel_id=1, source_target_pairs={{0,4},{2,6},{4,0},{6,2},{8,12},{10,14},{12,8},{14,10},{16,20},{18,... | collective-permute-start | bytes 3145736 | tf_op jit(solution)/shard_map/ppermute | solution.py:470
  81.5 36.8 %collective-permute-start.13 = (bf16[256,2048]{1,0:T(8,128)(2,1)}, bf16[256,2048]{1,0:T(8,128)(2,1)}, u32[]{:S(2)}, u32[]{:S(2)}) collective-permute-start(bf16[256,2048]{1,0:T(8,128)(2,1)} %add.123.refs_6_), channel_id=1, source_target_pairs={{0,2},{2,0},{4,6},{6,4},{8,10},{10,8},{12,14},{14,12},{16,18},{18,... | collective-permute-start | bytes 3145736 | tf_op jit(solution)/shard_map/ppermute | solution.py:470
  82.0 32.6 %collective-permute-start.15 = (bf16[144,2048]{1,0:T(8,128)(2,1)S(1)}, bf16[144,2048]{1,0:T(8,128)(2,1)S(1)}, u32[]{:S(2)}, u32[]{:S(2)}) collective-permute-start(bf16[144,2048]{1,0:T(8,128)(2,1)S(1)} %copy-done), channel_id=1, source_target_pairs={{0,8},{2,10},{4,12},{6,14},{8,0},{10,2},{12,4},{14,6},{16,24},{18,... | collective-permute-start | bytes 1769480 | tf_op jit(solution)/shard_map/ppermute | solution.py:470
  114.6 0.8 copy-start.1
  118.1 23.9 %collective-permute-start.16 = (bf16[144,2048]{1,0:T(8,128)(2,1)}, bf16[144,2048]{1,0:T(8,128)(2,1)}, u32[]{:S(2)}, u32[]{:S(2)}) collective-permute-start(bf16[144,2048]{1,0:T(8,128)(2,1)} %get-tuple-element.125.mine_ref), channel_id=1, source_target_pairs={{0,16},{2,18},{4,20},{6,22},{8,24},{10,26},{12,28},{14,30},{16,0},... | collective-permute-start | bytes 1769480 | tf_op jit(solution)/shard_map/ppermute | solution.py:470
  118.3 10.4 %copy-start.2 = (f32[32]{0:T(128)S(1)}, f32[32]{0:T(128)}, u32[]{:S(2)}) copy-start(f32[32]{0:T(128)} %param.13) | copy-start | bytes 388
  118.3 11.2 %copy-start.3 = (s32[16]{0:T(128)S(1)}, s32[16]{0:T(128)}, u32[]{:S(2)}) copy-start(s32[16]{0:T(128)} %get-tuple-element.212) | copy-start | bytes 196
  120.9 23.8 %collective-permute-start.14 = (bf16[256,1024]{1,0:T(8,128)(2,1)}, bf16[256,1024]{1,0:T(8,128)(2,1)}, u32[]{:S(2)}, u32[]{:S(2)}) collective-permute-start(bf16[256,1024]{1,0:T(8,128)(2,1)} %get-tuple-element.199.refs_3_.refs_6_), channel_id=1, source_target_pairs={{0,2},{2,0},{4,6},{6,4},{8,10},{10,8},{12,14},{14,12},{16,18},{18,... | collective-permute-start | bytes 1572872 | tf_op jit(solution)/shard_map/ppermute | solution.py:470
  121.4 23.3 %collective-permute-start.17 = (bf16[256,1024]{1,0:T(8,128)(2,1)}, bf16[256,1024]{1,0:T(8,128)(2,1)}, u32[]{:S(2)}, u32[]{:S(2)}) collective-permute-start(bf16[256,1024]{1,0:T(8,128)(2,1)} %get-tuple-element.199.refs_3_.refs_6_), channel_id=1, source_target_pairs={{0,4},{2,6},{4,0},{6,2},{8,12},{10,14},{12,8},{14,10},{16,20},{18,... | collective-permute-start | bytes 1572872 | tf_op jit(solution)/shard_map/ppermute | solution.py:470
  124.4 20.3 %collective-permute-start.18 = (bf16[256,1024]{1,0:T(8,128)(2,1)}, bf16[256,1024]{1,0:T(8,128)(2,1)}, u32[]{:S(2)}, u32[]{:S(2)}) collective-permute-start(bf16[256,1024]{1,0:T(8,128)(2,1)} %get-tuple-element.203), channel_id=1, source_target_pairs={{0,2},{2,0},{4,6},{6,4},{8,10},{10,8},{12,14},{14,12},{16,18},{18,... | collective-permute-start | bytes 1572872 | tf_op jit(solution)/shard_map/ppermute | solution.py:470
  125.9 18.8 %collective-permute-start.19 = (bf16[256,1024]{1,0:T(8,128)(2,1)}, bf16[256,1024]{1,0:T(8,128)(2,1)}, u32[]{:S(2)}, u32[]{:S(2)}) collective-permute-start(bf16[256,1024]{1,0:T(8,128)(2,1)} %get-tuple-element.129), channel_id=1, source_target_pairs={{0,4},{2,6},{4,0},{6,2},{8,12},{10,14},{12,8},{14,10},{16,20},{18,... | collective-permute-start | bytes 1572872 | tf_op jit(solution)/shard_map/ppermute | solution.py:470
  144.8 32.2 %collective-permute-start.20 = (bf16[256,1024]{1,0:T(8,128)(2,1)}, bf16[256,1024]{1,0:T(8,128)(2,1)}, u32[]{:S(2)}, u32[]{:S(2)}) collective-permute-start(bf16[256,1024]{1,0:T(8,128)(2,1)} %get-tuple-element.130.refs_3_.refs_7_), channel_id=1, source_target_pairs={{0,2},{2,0},{4,6},{6,4},{8,10},{10,8},{12,14},{14,12},{16,18},{18,... | collective-permute-start | bytes 1572872 | tf_op jit(solution)/shard_map/ppermute | solution.py:470
  145.4 31.6 %collective-permute-start.23 = (bf16[256,1024]{1,0:T(8,128)(2,1)}, bf16[256,1024]{1,0:T(8,128)(2,1)}, u32[]{:S(2)}, u32[]{:S(2)}) collective-permute-start(bf16[256,1024]{1,0:T(8,128)(2,1)} %get-tuple-element.130.refs_3_.refs_7_), channel_id=1, source_target_pairs={{0,4},{2,6},{4,0},{6,2},{8,12},{10,14},{12,8},{14,10},{16,20},{18,... | collective-permute-start | bytes 1572872 | tf_op jit(solution)/shard_map/ppermute | solution.py:470
  146.2 24.1 %collective-permute-start.21 = (bf16[256,1024]{1,0:T(8,128)(2,1)}, bf16[256,1024]{1,0:T(8,128)(2,1)}, u32[]{:S(2)}, u32[]{:S(2)}) collective-permute-start(bf16[256,1024]{1,0:T(8,128)(2,1)} %get-tuple-element.134), channel_id=1, source_target_pairs={{0,2},{2,0},{4,6},{6,4},{8,10},{10,8},{12,14},{14,12},{16,18},{18,... | collective-permute-start | bytes 1572872 | tf_op jit(solution)/shard_map/ppermute | solution.py:470
  147.7 22.8 %collective-permute-start.22 = (bf16[256,1024]{1,0:T(8,128)(2,1)}, bf16[256,1024]{1,0:T(8,128)(2,1)}, u32[]{:S(2)}, u32[]{:S(2)}) collective-permute-start(bf16[256,1024]{1,0:T(8,128)(2,1)} %get-tuple-element.135.refs_4_.refs_8_), channel_id=1, source_target_pairs={{0,4},{2,6},{4,0},{6,2},{8,12},{10,14},{12,8},{14,10},{16,20},{18,... | collective-permute-start | bytes 1572872 | tf_op jit(solution)/shard_map/ppermute | solution.py:470
  177.0 24.5 %collective-permute-start.28 = (bf16[128,1024]{1,0:T(8,128)(2,1)}, bf16[128,1024]{1,0:T(8,128)(2,1)}, u32[]{:S(2)}, u32[]{:S(2)}) collective-permute-start(bf16[128,1024]{1,0:T(8,128)(2,1)} %get-tuple-element.146.mine_ref), channel_id=1, source_target_pairs={{0,2},{2,0},{4,6},{6,4},{8,10},{10,8},{12,14},{14,12},{16,18},{18,... | collective-permute-start | bytes 786440 | tf_op jit(solution)/shard_map/ppermute | solution.py:470
  178.6 24.9 %collective-permute-start.24 = (bf16[256,1024]{1,0:T(8,128)(2,1)}, bf16[256,1024]{1,0:T(8,128)(2,1)}, u32[]{:S(2)}, u32[]{:S(2)}) collective-permute-start(bf16[256,1024]{1,0:T(8,128)(2,1)} %get-tuple-element.141), channel_id=1, source_target_pairs={{0,2},{2,0},{4,6},{6,4},{8,10},{10,8},{12,14},{14,12},{16,18},{18,... | collective-permute-start | bytes 1572872 | tf_op jit(solution)/shard_map/ppermute | solution.py:470
  179.1 24.4 %collective-permute-start.25 = (bf16[256,1024]{1,0:T(8,128)(2,1)}, bf16[256,1024]{1,0:T(8,128)(2,1)}, u32[]{:S(2)}, u32[]{:S(2)}) collective-permute-start(bf16[256,1024]{1,0:T(8,128)(2,1)} %get-tuple-element.142.refs_4_.refs_9_), channel_id=1, source_target_pairs={{0,4},{2,6},{4,0},{6,2},{8,12},{10,14},{12,8},{14,10},{16,20},{18,... | collective-permute-start | bytes 1572872 | tf_op jit(solution)/shard_map/ppermute | solution.py:470
  179.9 27.1 %collective-permute-start.26 = (bf16[256,1024]{1,0:T(8,128)(2,1)}, bf16[256,1024]{1,0:T(8,128)(2,1)}, u32[]{:S(2)}, u32[]{:S(2)}) collective-permute-start(bf16[256,1024]{1,0:T(8,128)(2,1)} %get-tuple-element.143), channel_id=1, source_target_pairs={{0,2},{2,0},{4,6},{6,4},{8,10},{10,8},{12,14},{14,12},{16,18},{18,... | collective-permute-start | bytes 1572872 | tf_op jit(solution)/shard_map/ppermute | solution.py:470
  181.4 25.6 %collective-permute-start.27 = (bf16[256,1024]{1,0:T(8,128)(2,1)}, bf16[256,1024]{1,0:T(8,128)(2,1)}, u32[]{:S(2)}, u32[]{:S(2)}) collective-permute-start(bf16[256,1024]{1,0:T(8,128)(2,1)} %get-tuple-element.144), channel_id=1, source_target_pairs={{0,4},{2,6},{4,0},{6,2},{8,12},{10,14},{12,8},{14,10},{16,20},{18,... | collective-permute-start | bytes 1572872 | tf_op jit(solution)/shard_map/ppermute | solution.py:470
  213.5 13.3 %collective-permute-start.29 = (bf16[128,1024]{1,0:T(8,128)(2,1)}, bf16[128,1024]{1,0:T(8,128)(2,1)}, u32[]{:S(2)}, u32[]{:S(2)}) collective-permute-start(bf16[128,1024]{1,0:T(8,128)(2,1)} %get-tuple-element.160.mine_ref), channel_id=1, source_target_pairs={{0,4},{2,6},{4,0},{6,2},{8,12},{10,14},{12,8},{14,10},{16,20},{18,... | collective-permute-start | bytes 786440 | tf_op jit(solution)/shard_map/ppermute | solution.py:470
  214.3 10.3 %collective-permute-start.30 = (bf16[128,1024]{1,0:T(8,128)(2,1)}, bf16[128,1024]{1,0:T(8,128)(2,1)}, u32[]{:S(2)}, u32[]{:S(2)}) collective-permute-start(bf16[128,1024]{1,0:T(8,128)(2,1)} %get-tuple-element.163.mine_ref), channel_id=1, source_target_pairs={{0,2},{2,0},{4,6},{6,4},{8,10},{10,8},{12,14},{14,12},{16,18},{18,... | collective-permute-start | bytes 786440 | tf_op jit(solution)/shard_map/ppermute | solution.py:470
  229.0 14.7 %collective-permute-start.33 = (bf16[512,2048]{1,0:T(8,128)(2,1)}, bf16[512,2048]{1,0:T(8,128)(2,1)}, u32[]{:S(2)}, u32[]{:S(2)}) collective-permute-start(bf16[512,2048]{1,0:T(8,128)(2,1)} %get-tuple-element.173), channel_id=1, source_target_pairs={{0,1},{1,0},{2,3},{3,2},{4,5},{5,4},{6,7},{7,6},{8,9},{9,8},{10,11... | collective-permute-start | bytes 6291464 | tf_op jit(solution)/shard_map/ppermute | solution.py:470
  229.0 10.3 %collective-permute-start.32 = (bf16[128,1024]{1,0:T(8,128)(2,1)}, bf16[128,1024]{1,0:T(8,128)(2,1)}, u32[]{:S(2)}, u32[]{:S(2)}) collective-permute-start(bf16[128,1024]{1,0:T(8,128)(2,1)} %get-tuple-element.170.mine_ref), channel_id=1, source_target_pairs={{0,4},{2,6},{4,0},{6,2},{8,12},{10,14},{12,8},{14,10},{16,20},{18,... | collective-permute-start | bytes 786440 | tf_op jit(solution)/shard_map/ppermute | solution.py:470
  230.3 11.2 %collective-permute-start.31 = (bf16[128,1024]{1,0:T(8,128)(2,1)}, bf16[128,1024]{1,0:T(8,128)(2,1)}, u32[]{:S(2)}, u32[]{:S(2)}) collective-permute-start(bf16[128,1024]{1,0:T(8,128)(2,1)} %get-tuple-element.167.mine_ref), channel_id=1, source_target_pairs={{0,8},{2,10},{4,12},{6,14},{8,0},{10,2},{12,4},{14,6},{16,24},{18,... | collective-permute-start | bytes 786440 | tf_op jit(solution)/shard_map/ppermute | solution.py:470
  244.7 2.8 collective-permute-start.36
  245.0 14.1 %collective-permute-start.34 = (bf16[128,1024]{1,0:T(8,128)(2,1)}, bf16[128,1024]{1,0:T(8,128)(2,1)}, u32[]{:S(2)}, u32[]{:S(2)}) collective-permute-start(bf16[128,1024]{1,0:T(8,128)(2,1)} %get-tuple-element.177.mine_ref), channel_id=1, source_target_pairs={{0,8},{2,10},{4,12},{6,14},{8,0},{10,2},{12,4},{14,6},{16,24},{18,... | collective-permute-start | bytes 786440 | tf_op jit(solution)/shard_map/ppermute | solution.py:470
  246.8 15.3 %collective-permute-start.35 = (bf16[128,1024]{1,0:T(8,128)(2,1)}, bf16[128,1024]{1,0:T(8,128)(2,1)}, u32[]{:S(2)}, u32[]{:S(2)}) collective-permute-start(bf16[128,1024]{1,0:T(8,128)(2,1)} %get-tuple-element.181.mine_ref), channel_id=1, source_target_pairs={{0,16},{2,18},{4,20},{6,22},{8,24},{10,26},{12,28},{14,30},{16,0},... | collective-permute-start | bytes 786440 | tf_op jit(solution)/shard_map/ppermute | solution.py:470
  264.1 14.0 %collective-permute-start.37 = (bf16[128,1024]{1,0:T(8,128)(2,1)}, bf16[128,1024]{1,0:T(8,128)(2,1)}, u32[]{:S(2)}, u32[]{:S(2)}) collective-permute-start(bf16[128,1024]{1,0:T(8,128)(2,1)} %get-tuple-element.186.mine_ref), channel_id=1, source_target_pairs={{0,16},{2,18},{4,20},{6,22},{8,24},{10,26},{12,28},{14,30},{16,0},... | collective-permute-start | bytes 786440 | tf_op jit(solution)/shard_map/ppermute | solution.py:470
  286.7 1.4 collective-permute-start.38

commit v10 on v9

--- a/solution.py
+++ b/solution.py
@@ -232,6 +232,12 @@
         refs[1][...] = total.astype(BF16)
     passed = factors[2:3] * got
     refs[0][...] = passed if entering_ref is None else entering_ref[...] + passed
+
+
+def scan_pair_kernel(number, last, *refs):
+    first, second, outs = refs[:number], refs[number : number + 4], refs[number + 4 :]
+    scan_kernel(False, *first, *outs[:2])
+    scan_kernel(last, *second, *outs[2:])
 
 
 def early_forward_kernel(count, f_ref, *refs):
@@ -777,6 +783,29 @@
     )(factors, sent, got, *entering)
 
 
+def scan_pair(first, second, last=False):
+    operands, specs, outs = [], [], []
+    for factors, here, sent, entering, bit in (first, second):
+        got = swap(sent, "ctx", bit)
+        n, columns = sent.shape
+        block = pl.BlockSpec((n, columns), lambda h: (0, 0))
+        at = here * WIDE // columns
+        operands += [factors, sent, got, *entering]
+        specs += [pl.BlockSpec((8, columns), lambda h, at=at: (0, at))]
+        specs += [block] * (2 + len(entering))
+        outs += [shape(n, columns), shape(n, columns, dtype=BF16)]
+    outs = outs[: 4 - last]
+    return call(
+        functools.partial(scan_pair_kernel, 3 + len(first[3]), last),
+        (1,),
+        specs,
+        [block] * len(outs),
+        outs,
+        0,
+        20 * n * columns,
+    )(*operands)
+
+
 def local(inputs, w_in, b_rows, c_rows, log_decay, skip_gain, grad_out):
     groups = log_decay.shape[0] // GROUP
     layered = lax.axis_size("ctx") == 4 * PLANE and lax.axis_size("head") == 2
@@ -904,8 +933,8 @@
         [pltpu.VMEM((length, width), BF16)],
     )(order_own, inputs, other)
 
-    inner2, inner3, outer2, x1, sent, own_y_a, own_y_b = after(
-        [inner2, inner3, outer2, x1, sent, own_y_a, own_y_b], y1, early_features
+    inner2, inner3, outer2, x1, own_y_a, own_y_b = after(
+        [inner2, inner3, outer2, x1, own_y_a, own_y_b], y1, early_features, moved
     )
     z3 = inner2 + outer2
     x3, y3 = swap_x(z3), swap_y(z3)
@@ -925,11 +954,12 @@
 
     own_y_a, x2a, z2b, leaving = after([own_y_a, x2a, z2b, leaving], y2a, d3a, d1a, part)
     d0a, d2a = swap_x(own_y_a), swap_y(x2a)
-    x2b, y2b = swap_x(z2b), swap_y(z2b)
     leaving_all = [leaving]
     for k in range(spans - 1, 0, -1):
         leaving_all.insert(0, own_grads[k] + kept[k, :1] * leaving_all[0])
     leaving_all = jnp.stack([value.astype(BF16) for value in leaving_all])
+    (z2b,) = after([z2b], leaving_all)
+    x2b, y2b = swap_x(z2b), swap_y(z2b)
     skip = jnp.repeat(skip_gain, P_SIZE)[None]
     grad_x = grad_rows(running, running_t, grad_out, b_rows, c_rows, leaving_all, skip, True)
     order_away = (order + (1 - place) * (blocks // 2)) % blocks
@@ -959,23 +989,28 @@
     )
     pairs = list(zip(late_a, late_b))
     sent_a, sent_b, *product = after([sent_a, sent_b, *product])
-    entering_b, sent_b = scan_step(factors_1, here, sent_b, (), 1)
-    entering_a, sent_a = scan_step(factors_2, 0, sent_a, (entering_a,), 2)
+    entering_b, sent_b, entering_a, sent_a = scan_pair(
+        (factors_1, here, sent_b, (), 1), (factors_2, 0, sent_a, (entering_a,), 2)
+    )
     away, own = multiply_blocks(late_order, grad_x, pairs, product)
 
     sent_a, sent_b, x_b, away = after([sent_a, sent_b, x_b, away])
-    entering_b, sent_b = scan_step(factors_2, here, sent_b, (entering_b,), 2)
-    entering_a, sent_a = scan_step(factors_4, 0, sent_a, (entering_a,), 4)
+    entering_b, sent_b, entering_a, sent_a = scan_pair(
+        (factors_2, here, sent_b, (entering_b,), 2), (factors_4, 0, sent_a, (entering_a,), 4)
+    )
     got = swap(away, "head", 1)
+
+    sent_a, sent_b, x_b = after([sent_a, sent_b, x_b])
+    entering_b, sent_b, entering_a = scan_pair(
+        (factors_4, here, sent_b, (entering_b,), 4),
+        (factors_8, 0, sent_a, (entering_a,), 8),
+        True,
+    )
     inner_b = shared + (x_b, b_rows, c_rows, leaving_all)
     decay_b, grad_b, grad_c = inner(grid, here, half, inner_b, (grad_b, grad_c))
 
-    sent_a, sent_b, got, grad_b = after([sent_a, sent_b, got, grad_b])
-    entering_b, sent_b = scan_step(factors_4, here, sent_b, (entering_b,), 4)
-    (entering_a,) = scan_step(factors_8, 0, sent_a, (entering_a,), 8, True)
+    sent_b, entering_a, got, grad_b = after([sent_b, entering_a, got, grad_b])
     grad_b = head_sum(grad_b)
-
-    sent_b, entering_a, got = after([sent_b, entering_a, got], grad_b)
     grad_inputs = (own.astype(F32) + got.astype(F32)).astype(BF16)
     (entering_b,) = scan_step(factors_8, here, sent_b, (entering_b,), 8, True)
     common = (running_t, grad_out, c_rows)

time: 291 us -> 291 us (level)
  Pallas kernels: 127 us -> 122 us
    pallas_call x8 -> x2, Pallas kernels: 17.1 us -> 4.11 us  [scan_step(): call(functools.partial(scan_kernel, last), (1,), [pl.BlockSpec((8, column...]
    pallas_call x0 -> x3, Pallas kernels: none -> 8.17 us  [scan_pair(): call(functools.partial(scan_pair_kernel, 3 + len(first[3]), last), (1,),...]
  transfers between devices with their start and end apart: 39 -> 39, of which waited for: 14 -> 12; matrix products, arithmetic and copies ran while one was open for 10% -> 10% of each run, Pallas kernels for 37% -> 39%
where the time goes in v10:
time: 291 us; the launch traced here: 289 us
  Pallas kernels  122 us (42%)
  waiting for transfers between devices  87.6 us (30%)
  starting transfers between devices  44.5 us (15%)
  other arithmetic  19.8 us (7%)
  local copies, waits for them, and re-layouts  12.3 us (4%)
  between operations  3.38 us (1%)
    ppermute x35, waiting for transfers between devices, swap(): return lax.ppermute(value, axis, [(i, i ^ bit) for i in range(count)])  87.6 us
    ppermute x35, starting transfers between devices, swap(): return lax.ppermute(value, axis, [(i, i ^ bit) for i in range(count)])  38.4 us
    pallas_call x2, Pallas kernels, multiply_blocks(): pl.pallas_call(functools.partial(blocks_kernel, [len(piece) for piece in...  18.9 us
    pallas_call x2, Pallas kernels, inner(): call(inner_kernel, grid, specs + [SHARED] * len(so_far), [run_spec(), SHA...  17.9 us
    pallas_call x2, Pallas kernels, late_forward(): call(functools.partial(late_forward_kernel, len(pieces)), (columns // WID...  13 us
    pallas_call x2, Pallas kernels, state_terms(): pl.pallas_call(state_kernel, grid=grid, in_specs=[run_t_spec(here), rows_...  11 us
    pallas_call x4, Pallas kernels, back_step(): call(functools.partial(back_kernel, bit), (columns // (2 * WIDE),), [SCAL...  10.5 us
    pallas_call x1, Pallas kernels, grad_rows(): call(functools.partial(grad_x_kernel, transposed), (length // SPAN, runni...  10.4 us
  transfers between devices with their start and end apart: 39, of which 12 were waited for; matrix products, arithmetic and copies ran while one was open for 10% of the time, Pallas kernels for 39%

profile of v10, /device:TPU:0, one launch (start us, length us, event | category | flops | bytes accessed | tf_op | source)
XLA Modules:
  0.0 289.5 jit_solution(2528709971020397424)
XLA Ops:
  1.1 2.7 collective-permute-start
  3.8 1.6 collective-permute-start.1
  5.4 1.5 collective-permute-start.2
  7.0 1.5 collective-permute-start.3
  8.4 9.1 %shard_map.111 = (f32[32,512]{1,0:T(8,128)}, f32[4,512,8]{2,1,0:T(8,128)}, f32[2,8,2048]{2,1,0:T(8,128)}, f32[2,128,2048]{2,1,0:T(8,128)}) custom-call(f32[32,512]{1,0:T(8,128)} %d_ref.1, bf16[512,2048]{1,0:T(8,128)(2,1)} %g_ref.11, bf16[512,128]{1,0:T(8,128)(2,1)} %c_ref.11), custom_call_target="tpu_custom_call" | custom-call | flops 268435456 | bytes 6291456 | tf_op jit(solution)/shard_map/pallas_call | solution.py:823
  17.5 3.5 %shard_map.112 = (f32[8,2048]{1,0:T(8,128)}, bf16[144,2048]{1,0:T(8,128)(2,1)}) custom-call(f32[2,128,2048]{2,1,0:T(8,128)} %get-tuple-element.101.own_ref, f32[2,8,2048]{2,1,0:T(8,128)} %get-tuple-element.102.kept_ref.a_ref), custom_call_target="tpu_custom_call" | custom-call | bytes 3670016 | tf_op jit(solution)/shard_map/pallas_call | solution.py:732
  21.1 6.8 %collective-permute-done.refs_0_ = bf16[256,2048]{1,0:T(8,128)(2,1)} collective-permute-done((bf16[256,2048]{1,0:T(8,128)(2,1)}, bf16[256,2048]{1,0:T(8,128)(2,1)}, u32[]{:S(2)}, u32[]{:S(2)}) %collective-permute-start) | collective-permute-done | bytes 1048608 | tf_op jit(solution)/shard_map/ppermute | solution.py:476
  27.9 3.1 %collective-permute-done.2.refs_2_ = bf16[256,2048]{1,0:T(8,128)(2,1)} collective-permute-done((bf16[256,2048]{1,0:T(8,128)(2,1)}, bf16[256,2048]{1,0:T(8,128)(2,1)}, u32[]{:S(2)}, u32[]{:S(2)}) %collective-permute-start.2) | collective-permute-done | bytes 1048608 | tf_op jit(solution)/shard_map/ppermute | solution.py:476
  31.0 1.2 collective-permute-done.3.refs_3_.refs_1_
  32.2 1.7 collective-permute-start.5
  34.0 1.3 collective-permute-start.6
  35.2 1.6 collective-permute-start.7
  42.4 30.0 %collective-permute-done.9.got_ref = bf16[144,2048]{1,0:T(8,128)(2,1)} collective-permute-done((bf16[144,2048]{1,0:T(8,128)(2,1)}, bf16[144,2048]{1,0:T(8,128)(2,1)}, u32[]{:S(2)}, u32[]{:S(2)}) %collective-permute-start.9) | collective-permute-done | bytes 589856 | tf_op jit(solution)/shard_map/ppermute | solution.py:476
  72.3 2.4 shard_map.116
  75.4 2.3 fusion.6
  77.7 5.1 %shard_map.115 = (bf16[512,2304]{1,0:T(8,128)(2,1)}, bf16[512,1792]{1,0:T(8,128)(2,1)}) custom-call(s32[16]{0:T(128)} %get-tuple-element.213.order_ref, bf16[512,2048]{1,0:T(8,128)(2,1)} %own_ref.1, bf16[512,2048]{1,0:T(8,128)(2,1)} %collective-permute-done.4.refs_1_.other_ref), custom_call_target="tpu_custom_call" | custom-call | bytes 8388608 | tf_op jit(solution)/shard_map/pallas_call | solution.py:925
  82.9 1.5 collective-permute-start.10
  84.3 2.9 %add.123.refs_6_ = bf16[256,2048]{1,0:T(8,128)(2,1)} add(bf16[256,2048]{1,0:T(8,128)(2,1)} %get-tuple-element.113, bf16[256,2048]{1,0:T(8,128)(2,1)} %get-tuple-element.114) | non-fusion elementwise | flops 524288 | bytes 3145728 | tf_op jit(solution)/shard_map/add | solution.py:939
  87.2 1.4 collective-permute-start.11
  88.7 1.5 collective-permute-start.12
  90.2 2.7 shard_map.119
  92.9 5.2 %collective-permute-start.15 = (bf16[144,2048]{1,0:T(8,128)(2,1)}, bf16[144,2048]{1,0:T(8,128)(2,1)}, u32[]{:S(2)}, u32[]{:S(2)}) collective-permute-start(bf16[144,2048]{1,0:T(8,128)(2,1)} %get-tuple-element.121.mine_ref), channel_id=1, source_target_pairs={{0,8},{2,10},{4,12},{6,14},{8,0},{10,2},{12,4},{14,6},{16,24},{18,... | collective-permute-start | bytes 1769480 | tf_op jit(solution)/shard_map/ppermute | solution.py:476
  98.1 2.3 fusion.5
  100.4 22.0 %collective-permute-done.15.got_ref = bf16[144,2048]{1,0:T(8,128)(2,1)} collective-permute-done((bf16[144,2048]{1,0:T(8,128)(2,1)}, bf16[144,2048]{1,0:T(8,128)(2,1)}, u32[]{:S(2)}, u32[]{:S(2)}) %collective-permute-start.15) | collective-permute-done | bytes 589856 | tf_op jit(solution)/shard_map/ppermute | solution.py:476
  122.4 2.7 shard_map.120
  125.2 2.6 slice_add_fusion
  127.9 1.5 collective-permute-start.13
  129.4 1.3 collective-permute-start.17
  130.7 2.3 fusion.4
  134.2 1.4 slice.85
  135.6 10.2 %shard_map.122.refs_7_.part_ref = f32[512,2048]{1,0:T(8,128)} custom-call(bf16[512,2304]{1,0:T(8,128)(2,1)} %get-tuple-element.107.refs_7_.f_ref, bf16[256,2048]{1,0:T(8,128)(2,1)} %refs_0_.3, bf16[256,2048]{1,0:T(8,128)(2,1)} %collective-permute-done.3.refs_3_.refs_1_, bf16[256,2048]{1,0:T(8,128)(2,1)} %get-tuple-element.106.refs_2_, ...), custom_call_target="tpu_custom_call" | custom-call | flops 4831838208 | bytes 9437184 | tf_op jit(solution)/shard_map/pallas_call | solution.py:651
  145.8 4.5 %collective-permute-done.16.got_ref = bf16[144,2048]{1,0:T(8,128)(2,1)} collective-permute-done((bf16[144,2048]{1,0:T(8,128)(2,1)}, bf16[144,2048]{1,0:T(8,128)(2,1)}, u32[]{:S(2)}, u32[]{:S(2)}) %collective-permute-start.16) | collective-permute-done | bytes 589856 | tf_op jit(solution)/shard_map/ppermute | solution.py:476
  150.3 2.7 shard_map.121
  153.0 1.6 collective-permute-start.21
  155.8 2.2 fusion.1
  163.0 10.4 %shard_map.126.refs_6_ = bf16[2048,512]{1,0:T(8,128)(2,1)} custom-call(f32[32,512]{1,0:T(8,128)} %get-tuple-element.138.r_ref, f32[4,512,8]{2,1,0:T(8,128)} %get-tuple-element.133.rt_ref, bf16[512,2048]{1,0:T(8,128)(2,1)} %g_ref.11, bf16[512,128]{1,0:T(8,128)(2,1)} %b_ref.9, bf16[512,128]{1,0:T(8,128)(2,1)} %c_ref.11, ...), custom_call_target="tpu_custom_call" | custom-call | flops 2147483648 | bytes 6291456 | tf_op jit(solution)/shard_map/pallas_call | solution.py:1030
  173.4 6.5 %shard_map.125 = (bf16[512,1024]{1,0:T(8,128)(2,1)}, f32[2,128,1024]{2,1,0:T(8,128)}, bf16[128,1024]{1,0:T(8,128)(2,1)}) custom-call(bf16[512,1792]{1,0:T(8,128)(2,1)} %get-tuple-element.132.f_ref, f32[512,2048]{1,0:T(8,128)} %shard_map.122.refs_7_.part_ref, f32[4,512,8]{2,1,0:T(8,128)} %get-tuple-element.133.rt_ref, bf16[512,128]{1,0:T(8,128)(2,1)} %b_ref.9, ...), custom_call_target="tpu_custom_call" | custom-call | flops 1879048192 | bytes 3670016 | tf_op jit(solution)/shard_map/pallas_call | solution.py:671
  179.9 1.6 collective-permute-start.28
  182.0 1.2 collective-permute-start.25
  183.3 1.5 collective-permute-start.26
  185.5 10.0 %shard_map.130 = (bf16[512,2048]{1,0:T(8,128)(2,1)}, bf16[512,2048]{1,0:T(8,128)(2,1)}) custom-call(s32[9]{0:T(128)} %bitcast.34, bf16[2048,512]{1,0:T(8,128)(2,1)} %get-tuple-element.139.g_ref, bf16[256,2048]{1,0:T(8,128)(2,1)} %refs_0_.3, bf16[256,2048]{1,0:T(8,128)(2,1)} %collective-permute-done.3.refs_3_.refs_1_, ...), custom_call_target="tpu_custom_call" | custom-call | flops 4831838208 | bytes 9437184 | tf_op jit(solution)/shard_map/pallas_call | solution.py:705
  195.5 8.9 %shard_map.129 = (f32[16,512]{1,0:T(8,128)}, f32[512,128]{1,0:T(8,128)}, f32[512,128]{1,0:T(8,128)}) custom-call(f32[32,512]{1,0:T(8,128)} %get-tuple-element.138.r_ref, f32[4,512,8]{2,1,0:T(8,128)} %get-tuple-element.133.rt_ref, bf16[512,2048]{1,0:T(8,128)(2,1)} %g_ref.11, bf16[512,1024]{1,0:T(8,128)(2,1)} %get-tuple-element.147.x_ref, ...), custom_call_target="tpu_custom_call" | custom-call | flops 1610612736 | bytes 3145728 | tf_op jit(solution)/shard_map/pallas_call | solution.py:851
  204.4 2.0 shard_map.128
  206.4 3.4 %collective-permute-done.26.refs_2_.refs_5_ = bf16[256,1024]{1,0:T(8,128)(2,1)} collective-permute-done((bf16[256,1024]{1,0:T(8,128)(2,1)}, bf16[256,1024]{1,0:T(8,128)(2,1)}, u32[]{:S(2)}, u32[]{:S(2)}) %collective-permute-start.26) | collective-permute-done | bytes 524320 | tf_op jit(solution)/shard_map/ppermute | solution.py:476
  209.9 6.4 %shard_map.132 = (bf16[512,1024]{1,0:T(8,128)(2,1)}, f32[2,128,1024]{2,1,0:T(8,128)}, bf16[128,1024]{1,0:T(8,128)(2,1)}) custom-call(bf16[512,1792]{1,0:T(8,128)(2,1)} %get-tuple-element.132.f_ref, f32[512,2048]{1,0:T(8,128)} %shard_map.122.refs_7_.part_ref, f32[4,512,8]{2,1,0:T(8,128)} %get-tuple-element.133.rt_ref, bf16[512,128]{1,0:T(8,128)(2,1)} %b_ref.9, ...), custom_call_target="tpu_custom_call" | custom-call | flops 1879048192 | bytes 3670016 | tf_op jit(solution)/shard_map/pallas_call | solution.py:671
  216.3 1.5 collective-permute-start.29
  217.9 1.2 collective-permute-start.30
  219.1 8.9 %shard_map.134 = (bf16[512,2048]{1,0:T(8,128)(2,1)}, bf16[512,2048]{1,0:T(8,128)(2,1)}) custom-call(s32[7]{0:T(128)} %slice.74.order_ref, bf16[2048,512]{1,0:T(8,128)(2,1)} %get-tuple-element.139.g_ref, bf16[256,1024]{1,0:T(8,128)(2,1)} %collective-permute-done.21.refs_0_, ...), custom_call_target="tpu_custom_call", output_to_operand_aliasing={{0}: (16, {}), {1}: (17, {})} | custom-call | flops 3758096384 | bytes 7340032 | tf_op jit(solution)/shard_map/pallas_call | solution.py:705
  228.1 2.7 shard_map.135
  231.6 8.1 %collective-permute-done.31.refs_2_ = bf16[128,1024]{1,0:T(8,128)(2,1)} collective-permute-done((bf16[128,1024]{1,0:T(8,128)(2,1)}, bf16[128,1024]{1,0:T(8,128)(2,1)}, u32[]{:S(2)}, u32[]{:S(2)}) %collective-permute-start.31) | collective-permute-done | bytes 262176 | tf_op jit(solution)/shard_map/ppermute | solution.py:476
  240.3 2.8 shard_map.137
  243.4 2.4 collective-permute-start.34
  245.8 9.0 %shard_map.140 = (f32[16,512]{1,0:T(8,128)}, f32[512,128]{1,0:T(8,128)}, f32[512,128]{1,0:T(8,128)}) custom-call(f32[32,512]{1,0:T(8,128)} %get-tuple-element.138.r_ref, f32[4,512,8]{2,1,0:T(8,128)} %get-tuple-element.133.rt_ref, bf16[512,2048]{1,0:T(8,128)(2,1)} %g_ref.11, bf16[512,1024]{1,0:T(8,128)(2,1)} %get-tuple-element.181.x_ref, ...), custom_call_target="tpu_custom_call" | custom-call | flops 1610612736 | bytes 3145728 | tf_op jit(solution)/shard_map/pallas_call | solution.py:851
  254.8 1.3 collective-permute-done.33.refs_2_
  256.1 1.7 collective-permute-done.34.refs_6_
  257.8 2.7 shard_map.139
  260.6 1.6 convert_element_type.38
  262.5 4.4 %add_convert_fusion.refs_1_ = bf16[512,2048]{1,0:T(8,128)(2,1)} fusion(bf16[512,2048]{1,0:T(8,128)(2,1)} %get-tuple-element.184, bf16[512,2048]{1,0:T(8,128)(2,1)} %get-tuple-element.156), kind=kLoop, calls=%fused_computation | loop fusion | flops 4194304 | bytes 6291456 | tf_op jit(solution)/shard_map/convert_element_type | solution.py:1014
  267.0 5.5 %shard_map.143 = (f32[32,512]{1,0:T(8,128)}, f32[512,128]{1,0:T(8,128)}) custom-call(f32[4,512,8]{2,1,0:T(8,128)} %get-tuple-element.133.rt_ref, bf16[512,2048]{1,0:T(8,128)(2,1)} %g_ref.11, bf16[512,128]{1,0:T(8,128)(2,1)} %c_ref.11, f32[128,1024]{1,0:T(8,128)} %get-tuple-element.188.s_ref, f32[2,128,1024]{2,1,0:T(8,128)} %get-tuple-element.189.e_ref, ...), custom_call_target="tpu_custom_call" | custom-call | flops 268435456 | bytes 3145728 | tf_op jit(solution)/shard_map/pallas_call | solution.py:869
  272.5 4.9 %collective-permute-done.37.got_ref = bf16[128,1024]{1,0:T(8,128)(2,1)} collective-permute-done((bf16[128,1024]{1,0:T(8,128)(2,1)}, bf16[128,1024]{1,0:T(8,128)(2,1)}, u32[]{:S(2)}, u32[]{:S(2)}) %collective-permute-start.37) | collective-permute-done | bytes 262176 | tf_op jit(solution)/shard_map/ppermute | solution.py:476
  277.3 2.1 shard_map.142.refs_0_
  279.4 5.5 %shard_map.145 = (f32[32,512]{1,0:T(8,128)}, f32[512,128]{1,0:T(8,128)}) custom-call(f32[4,512,8]{2,1,0:T(8,128)} %get-tuple-element.133.rt_ref, bf16[512,2048]{1,0:T(8,128)(2,1)} %g_ref.11, bf16[512,128]{1,0:T(8,128)(2,1)} %c_ref.11, f32[128,1024]{1,0:T(8,128)} %shard_map.144.s_ref, ...), custom_call_target="tpu_custom_call", output_to_operand_aliasing={{0}: (9, {})} | custom-call | flops 268435456 | bytes 3145728 | tf_op jit(solution)/shard_map/pallas_call | solution.py:869
  286.0 1.7 convert_add_fusion.1
  287.8 1.7 convert_add_fusion
  (69 shorter events, 16.4 us)
Async XLA Ops:
  0.6 20.4 %collective-permute-start.4 = (bf16[512,2048]{1,0:T(8,128)(2,1)}, bf16[512,2048]{1,0:T(8,128)(2,1)}, u32[]{:S(2)}, u32[]{:S(2)}) collective-permute-start(bf16[512,2048]{1,0:T(8,128)(2,1)} %own_ref.1), channel_id=1, source_target_pairs={{0,1},{1,0},{2,3},{3,2},{4,5},{5,4},{6,7},{7,6},{8,9},{9,8},{10,11... | collective-permute-start | bytes 6291464 | tf_op jit(solution)/shard_map/ppermute | solution.py:476
  1.1 26.7 %collective-permute-start = (bf16[256,2048]{1,0:T(8,128)(2,1)}, bf16[256,2048]{1,0:T(8,128)(2,1)}, u32[]{:S(2)}, u32[]{:S(2)}) collective-permute-start(bf16[256,2048]{1,0:T(8,128)(2,1)} %refs_0_.3), channel_id=1, source_target_pairs={{0,8},{2,10},{4,12},{6,14},{8,0},{10,2},{12,4},{14,6},{16,24},{18,... | collective-permute-start | bytes 3145736 | tf_op jit(solution)/shard_map/ppermute | solution.py:476
  3.8 24.1 %collective-permute-start.1 = (bf16[256,2048]{1,0:T(8,128)(2,1)}, bf16[256,2048]{1,0:T(8,128)(2,1)}, u32[]{:S(2)}, u32[]{:S(2)}) collective-permute-start(bf16[256,2048]{1,0:T(8,128)(2,1)} %refs_0_.3), channel_id=1, source_target_pairs={{8,16},{10,18},{12,20},{14,22},{16,8},{18,10},{20,12},{22,14},{9,1... | collective-permute-start | bytes 3145736 | tf_op jit(solution)/shard_map/ppermute | solution.py:537
  5.4 25.5 %collective-permute-start.2 = (bf16[256,2048]{1,0:T(8,128)(2,1)}, bf16[256,2048]{1,0:T(8,128)(2,1)}, u32[]{:S(2)}, u32[]{:S(2)}) collective-permute-start(bf16[256,2048]{1,0:T(8,128)(2,1)} %refs_0_.3), channel_id=1, source_target_pairs={{0,4},{2,6},{4,0},{6,2},{8,12},{10,14},{12,8},{14,10},{16,20},{18,... | collective-permute-start | bytes 3145736 | tf_op jit(solution)/shard_map/ppermute | solution.py:476
  7.0 25.3 %collective-permute-start.3 = (bf16[256,2048]{1,0:T(8,128)(2,1)}, bf16[256,2048]{1,0:T(8,128)(2,1)}, u32[]{:S(2)}, u32[]{:S(2)}) collective-permute-start(bf16[256,2048]{1,0:T(8,128)(2,1)} %refs_0_.3), channel_id=1, source_target_pairs={{0,2},{2,0},{4,6},{6,4},{8,10},{10,8},{12,14},{14,12},{16,18},{18,... | collective-permute-start | bytes 3145736 | tf_op jit(solution)/shard_map/ppermute | solution.py:476
  32.2 50.6 %collective-permute-start.5 = (bf16[256,2048]{1,0:T(8,128)(2,1)}, bf16[256,2048]{1,0:T(8,128)(2,1)}, u32[]{:S(2)}, u32[]{:S(2)}) collective-permute-start(bf16[256,2048]{1,0:T(8,128)(2,1)} %get-tuple-element.105.refs_3_), channel_id=1, source_target_pairs={{8,16},{10,18},{12,20},{14,22},{16,8},{18,10},{20,12},{22,14},{9,1... | collective-permute-start | bytes 3145736 | tf_op jit(solution)/shard_map/ppermute | solution.py:537
  34.0 48.9 %collective-permute-start.6 = (bf16[256,2048]{1,0:T(8,128)(2,1)}, bf16[256,2048]{1,0:T(8,128)(2,1)}, u32[]{:S(2)}, u32[]{:S(2)}) collective-permute-start(bf16[256,2048]{1,0:T(8,128)(2,1)} %get-tuple-element.104.refs_0_), channel_id=1, source_target_pairs={{8,0},{10,2},{12,4},{14,6},{16,24},{18,26},{20,28},{22,30},{9,1},{... | collective-permute-start | bytes 3145736 | tf_op jit(solution)/shard_map/ppermute | solution.py:537
  35.2 47.6 %collective-permute-start.7 = (bf16[256,2048]{1,0:T(8,128)(2,1)}, bf16[256,2048]{1,0:T(8,128)(2,1)}, u32[]{:S(2)}, u32[]{:S(2)}) collective-permute-start(bf16[256,2048]{1,0:T(8,128)(2,1)} %get-tuple-element.105.refs_3_), channel_id=1, source_target_pairs={{0,2},{2,0},{4,6},{6,4},{8,10},{10,8},{12,14},{14,12},{16,18},{18,... | collective-permute-start | bytes 3145736 | tf_op jit(solution)/shard_map/ppermute | solution.py:476
  36.8 46.0 %collective-permute-start.8 = (bf16[256,2048]{1,0:T(8,128)(2,1)}, bf16[256,2048]{1,0:T(8,128)(2,1)}, u32[]{:S(2)}, u32[]{:S(2)}) collective-permute-start(bf16[256,2048]{1,0:T(8,128)(2,1)} %get-tuple-element.105.refs_3_), channel_id=1, source_target_pairs={{0,4},{2,6},{4,0},{6,2},{8,12},{10,14},{12,8},{14,10},{16,20},{18,... | collective-permute-start | bytes 3145736 | tf_op jit(solution)/shard_map/ppermute | solution.py:476
  37.3 35.0 %collective-permute-start.9 = (bf16[144,2048]{1,0:T(8,128)(2,1)}, bf16[144,2048]{1,0:T(8,128)(2,1)}, u32[]{:S(2)}, u32[]{:S(2)}) collective-permute-start(bf16[144,2048]{1,0:T(8,128)(2,1)} %shard_map.113.refs_4_.mine_ref), channel_id=1, source_target_pairs={{0,2},{2,0},{4,6},{6,4},{8,10},{10,8},{12,14},{14,12},{16,18},{18,... | collective-permute-start | bytes 1769480 | tf_op jit(solution)/shard_map/ppermute | solution.py:476
  74.8 15.4 %collective-permute-start.14 = (bf16[144,2048]{1,0:T(8,128)(2,1)}, bf16[144,2048]{1,0:T(8,128)(2,1)}, u32[]{:S(2)}, u32[]{:S(2)}) collective-permute-start(bf16[144,2048]{1,0:T(8,128)(2,1)} %get-tuple-element.109.refs_8_.mine_ref), channel_id=1, source_target_pairs={{0,4},{2,6},{4,0},{6,2},{8,12},{10,14},{12,8},{14,10},{16,20},{18,... | collective-permute-start | bytes 1769480 | tf_op jit(solution)/shard_map/ppermute | solution.py:476
  82.9 42.4 %collective-permute-start.10 = (bf16[256,2048]{1,0:T(8,128)(2,1)}, bf16[256,2048]{1,0:T(8,128)(2,1)}, u32[]{:S(2)}, u32[]{:S(2)}) collective-permute-start(bf16[256,2048]{1,0:T(8,128)(2,1)} %get-tuple-element.112.refs_0_), channel_id=1, source_target_pairs={{8,0},{10,2},{12,4},{14,6},{16,24},{18,26},{20,28},{22,30},{9,1},{... | collective-permute-start | bytes 3145736 | tf_op jit(solution)/shard_map/ppermute | solution.py:537
  87.2 38.0 %collective-permute-start.11 = (bf16[256,2048]{1,0:T(8,128)(2,1)}, bf16[256,2048]{1,0:T(8,128)(2,1)}, u32[]{:S(2)}, u32[]{:S(2)}) collective-permute-start(bf16[256,2048]{1,0:T(8,128)(2,1)} %add.123.refs_6_), channel_id=1, source_target_pairs={{0,4},{2,6},{4,0},{6,2},{8,12},{10,14},{12,8},{14,10},{16,20},{18,... | collective-permute-start | bytes 3145736 | tf_op jit(solution)/shard_map/ppermute | solution.py:476
  88.7 36.6 %collective-permute-start.12 = (bf16[256,2048]{1,0:T(8,128)(2,1)}, bf16[256,2048]{1,0:T(8,128)(2,1)}, u32[]{:S(2)}, u32[]{:S(2)}) collective-permute-start(bf16[256,2048]{1,0:T(8,128)(2,1)} %add.123.refs_6_), channel_id=1, source_target_pairs={{0,2},{2,0},{4,6},{6,4},{8,10},{10,8},{12,14},{14,12},{16,18},{18,... | collective-permute-start | bytes 3145736 | tf_op jit(solution)/shard_map/ppermute | solution.py:476
  92.9 29.5 %collective-permute-start.15 = (bf16[144,2048]{1,0:T(8,128)(2,1)}, bf16[144,2048]{1,0:T(8,128)(2,1)}, u32[]{:S(2)}, u32[]{:S(2)}) collective-permute-start(bf16[144,2048]{1,0:T(8,128)(2,1)} %get-tuple-element.121.mine_ref), channel_id=1, source_target_pairs={{0,8},{2,10},{4,12},{6,14},{8,0},{10,2},{12,4},{14,6},{16,24},{18,... | collective-permute-start | bytes 1769480 | tf_op jit(solution)/shard_map/ppermute | solution.py:476
  125.1 25.2 %collective-permute-start.16 = (bf16[144,2048]{1,0:T(8,128)(2,1)}, bf16[144,2048]{1,0:T(8,128)(2,1)}, u32[]{:S(2)}, u32[]{:S(2)}) collective-permute-start(bf16[144,2048]{1,0:T(8,128)(2,1)} %get-tuple-element.124.mine_ref), channel_id=1, source_target_pairs={{0,16},{2,18},{4,20},{6,22},{8,24},{10,26},{12,28},{14,30},{16,0},... | collective-permute-start | bytes 1769480 | tf_op jit(solution)/shard_map/ppermute | solution.py:476
  127.9 25.1 %collective-permute-start.13 = (bf16[256,1024]{1,0:T(8,128)(2,1)}, bf16[256,1024]{1,0:T(8,128)(2,1)}, u32[]{:S(2)}, u32[]{:S(2)}) collective-permute-start(bf16[256,1024]{1,0:T(8,128)(2,1)} %get-tuple-element.199.refs_3_.refs_6_), channel_id=1, source_target_pairs={{0,2},{2,0},{4,6},{6,4},{8,10},{10,8},{12,14},{14,12},{16,18},{18,... | collective-permute-start | bytes 1572872 | tf_op jit(solution)/shard_map/ppermute | solution.py:476
  129.4 23.6 %collective-permute-start.17 = (bf16[256,1024]{1,0:T(8,128)(2,1)}, bf16[256,1024]{1,0:T(8,128)(2,1)}, u32[]{:S(2)}, u32[]{:S(2)}) collective-permute-start(bf16[256,1024]{1,0:T(8,128)(2,1)} %get-tuple-element.199.refs_3_.refs_6_), channel_id=1, source_target_pairs={{0,4},{2,6},{4,0},{6,2},{8,12},{10,14},{12,8},{14,10},{16,20},{18,... | collective-permute-start | bytes 1572872 | tf_op jit(solution)/shard_map/ppermute | solution.py:476
  132.9 20.0 %collective-permute-start.18 = (bf16[256,1024]{1,0:T(8,128)(2,1)}, bf16[256,1024]{1,0:T(8,128)(2,1)}, u32[]{:S(2)}, u32[]{:S(2)}) collective-permute-start(bf16[256,1024]{1,0:T(8,128)(2,1)} %get-tuple-element.201), channel_id=1, source_target_pairs={{0,2},{2,0},{4,6},{6,4},{8,10},{10,8},{12,14},{14,12},{16,18},{18,... | collective-permute-start | bytes 1572872 | tf_op jit(solution)/shard_map/ppermute | solution.py:476
  133.5 19.5 %collective-permute-start.19 = (bf16[256,1024]{1,0:T(8,128)(2,1)}, bf16[256,1024]{1,0:T(8,128)(2,1)}, u32[]{:S(2)}, u32[]{:S(2)}) collective-permute-start(bf16[256,1024]{1,0:T(8,128)(2,1)} %get-tuple-element.128), channel_id=1, source_target_pairs={{0,4},{2,6},{4,0},{6,2},{8,12},{10,14},{12,8},{14,10},{16,20},{18,... | collective-permute-start | bytes 1572872 | tf_op jit(solution)/shard_map/ppermute | solution.py:476
  153.0 20.4 %collective-permute-start.21 = (bf16[256,1024]{1,0:T(8,128)(2,1)}, bf16[256,1024]{1,0:T(8,128)(2,1)}, u32[]{:S(2)}, u32[]{:S(2)}) collective-permute-start(bf16[256,1024]{1,0:T(8,128)(2,1)} %get-tuple-element.134), channel_id=1, source_target_pairs={{0,2},{2,0},{4,6},{6,4},{8,10},{10,8},{12,14},{14,12},{16,18},{18,... | collective-permute-start | bytes 1572872 | tf_op jit(solution)/shard_map/ppermute | solution.py:476
  154.6 18.8 %collective-permute-start.22 = (bf16[256,1024]{1,0:T(8,128)(2,1)}, bf16[256,1024]{1,0:T(8,128)(2,1)}, u32[]{:S(2)}, u32[]{:S(2)}) collective-permute-start(bf16[256,1024]{1,0:T(8,128)(2,1)} %get-tuple-element.135.refs_4_.refs_8_), channel_id=1, source_target_pairs={{0,4},{2,6},{4,0},{6,2},{8,12},{10,14},{12,8},{14,10},{16,20},{18,... | collective-permute-start | bytes 1572872 | tf_op jit(solution)/shard_map/ppermute | solution.py:476
  159.0 20.9 %collective-permute-start.20 = (bf16[256,1024]{1,0:T(8,128)(2,1)}, bf16[256,1024]{1,0:T(8,128)(2,1)}, u32[]{:S(2)}, u32[]{:S(2)}) collective-permute-start(bf16[256,1024]{1,0:T(8,128)(2,1)} %shard_map.124.refs_3_.refs_7_), channel_id=1, source_target_pairs={{0,2},{2,0},{4,6},{6,4},{8,10},{10,8},{12,14},{14,12},{16,18},{18,... | collective-permute-start | bytes 1572872 | tf_op jit(solution)/shard_map/ppermute | solution.py:476
  159.6 20.3 %collective-permute-start.23 = (bf16[256,1024]{1,0:T(8,128)(2,1)}, bf16[256,1024]{1,0:T(8,128)(2,1)}, u32[]{:S(2)}, u32[]{:S(2)}) collective-permute-start(bf16[256,1024]{1,0:T(8,128)(2,1)} %shard_map.124.refs_3_.refs_7_), channel_id=1, source_target_pairs={{0,4},{2,6},{4,0},{6,2},{8,12},{10,14},{12,8},{14,10},{16,20},{18,... | collective-permute-start | bytes 1572872 | tf_op jit(solution)/shard_map/ppermute | solution.py:476
  179.9 24.5 %collective-permute-start.28 = (bf16[128,1024]{1,0:T(8,128)(2,1)}, bf16[128,1024]{1,0:T(8,128)(2,1)}, u32[]{:S(2)}, u32[]{:S(2)}) collective-permute-start(bf16[128,1024]{1,0:T(8,128)(2,1)} %get-tuple-element.145.mine_ref), channel_id=1, source_target_pairs={{0,2},{2,0},{4,6},{6,4},{8,10},{10,8},{12,14},{14,12},{16,18},{18,... | collective-permute-start | bytes 786440 | tf_op jit(solution)/shard_map/ppermute | solution.py:476
  181.5 25.0 %collective-permute-start.24 = (bf16[256,1024]{1,0:T(8,128)(2,1)}, bf16[256,1024]{1,0:T(8,128)(2,1)}, u32[]{:S(2)}, u32[]{:S(2)}) collective-permute-start(bf16[256,1024]{1,0:T(8,128)(2,1)} %get-tuple-element.140), channel_id=1, source_target_pairs={{0,2},{2,0},{4,6},{6,4},{8,10},{10,8},{12,14},{14,12},{16,18},{18,... | collective-permute-start | bytes 1572872 | tf_op jit(solution)/shard_map/ppermute | solution.py:476
  182.0 24.4 %collective-permute-start.25 = (bf16[256,1024]{1,0:T(8,128)(2,1)}, bf16[256,1024]{1,0:T(8,128)(2,1)}, u32[]{:S(2)}, u32[]{:S(2)}) collective-permute-start(bf16[256,1024]{1,0:T(8,128)(2,1)} %get-tuple-element.141.refs_4_.refs_9_), channel_id=1, source_target_pairs={{0,4},{2,6},{4,0},{6,2},{8,12},{10,14},{12,8},{14,10},{16,20},{18,... | collective-permute-start | bytes 1572872 | tf_op jit(solution)/shard_map/ppermute | solution.py:476
  183.3 26.6 %collective-permute-start.26 = (bf16[256,1024]{1,0:T(8,128)(2,1)}, bf16[256,1024]{1,0:T(8,128)(2,1)}, u32[]{:S(2)}, u32[]{:S(2)}) collective-permute-start(bf16[256,1024]{1,0:T(8,128)(2,1)} %get-tuple-element.142), channel_id=1, source_target_pairs={{0,2},{2,0},{4,6},{6,4},{8,10},{10,8},{12,14},{14,12},{16,18},{18,... | collective-permute-start | bytes 1572872 | tf_op jit(solution)/shard_map/ppermute | solution.py:476
  184.7 25.1 %collective-permute-start.27 = (bf16[256,1024]{1,0:T(8,128)(2,1)}, bf16[256,1024]{1,0:T(8,128)(2,1)}, u32[]{:S(2)}, u32[]{:S(2)}) collective-permute-start(bf16[256,1024]{1,0:T(8,128)(2,1)} %get-tuple-element.143), channel_id=1, source_target_pairs={{0,4},{2,6},{4,0},{6,2},{8,12},{10,14},{12,8},{14,10},{16,20},{18,... | collective-permute-start | bytes 1572872 | tf_op jit(solution)/shard_map/ppermute | solution.py:476
  216.3 11.7 %collective-permute-start.29 = (bf16[128,1024]{1,0:T(8,128)(2,1)}, bf16[128,1024]{1,0:T(8,128)(2,1)}, u32[]{:S(2)}, u32[]{:S(2)}) collective-permute-start(bf16[128,1024]{1,0:T(8,128)(2,1)} %get-tuple-element.159.refs_1_), channel_id=1, source_target_pairs={{0,2},{2,0},{4,6},{6,4},{8,10},{10,8},{12,14},{14,12},{16,18},{18,... | collective-permute-start | bytes 786440 | tf_op jit(solution)/shard_map/ppermute | solution.py:476
  217.9 10.2 %collective-permute-start.30 = (bf16[128,1024]{1,0:T(8,128)(2,1)}, bf16[128,1024]{1,0:T(8,128)(2,1)}, u32[]{:S(2)}, u32[]{:S(2)}) collective-permute-start(bf16[128,1024]{1,0:T(8,128)(2,1)} %get-tuple-element.160.refs_4_), channel_id=1, source_target_pairs={{0,4},{2,6},{4,0},{6,2},{8,12},{10,14},{12,8},{14,10},{16,20},{18,... | collective-permute-start | bytes 786440 | tf_op jit(solution)/shard_map/ppermute | solution.py:476
  230.7 29.8 %collective-permute-start.35 = (bf16[512,2048]{1,0:T(8,128)(2,1)}, bf16[512,2048]{1,0:T(8,128)(2,1)}, u32[]{:S(2)}, u32[]{:S(2)}) collective-permute-start(bf16[512,2048]{1,0:T(8,128)(2,1)} %get-tuple-element.180), channel_id=1, source_target_pairs={{0,1},{1,0},{2,3},{3,2},{4,5},{5,4},{6,7},{7,6},{8,9},{9,8},{10,11... | collective-permute-start | bytes 6291464 | tf_op jit(solution)/shard_map/ppermute | solution.py:476
  230.7 9.0 %collective-permute-start.31 = (bf16[128,1024]{1,0:T(8,128)(2,1)}, bf16[128,1024]{1,0:T(8,128)(2,1)}, u32[]{:S(2)}, u32[]{:S(2)}) collective-permute-start(bf16[128,1024]{1,0:T(8,128)(2,1)} %get-tuple-element.166.refs_1_), channel_id=1, source_target_pairs={{0,4},{2,6},{4,0},{6,2},{8,12},{10,14},{12,8},{14,10},{16,20},{18,... | collective-permute-start | bytes 786440 | tf_op jit(solution)/shard_map/ppermute | solution.py:476
  231.6 8.7 %collective-permute-start.32 = (bf16[128,1024]{1,0:T(8,128)(2,1)}, bf16[128,1024]{1,0:T(8,128)(2,1)}, u32[]{:S(2)}, u32[]{:S(2)}) collective-permute-start(bf16[128,1024]{1,0:T(8,128)(2,1)} %get-tuple-element.168.refs_5_), channel_id=1, source_target_pairs={{0,8},{2,10},{4,12},{6,14},{8,0},{10,2},{12,4},{14,6},{16,24},{18,... | collective-permute-start | bytes 786440 | tf_op jit(solution)/shard_map/ppermute | solution.py:476
  243.1 13.1 %collective-permute-start.33 = (bf16[128,1024]{1,0:T(8,128)(2,1)}, bf16[128,1024]{1,0:T(8,128)(2,1)}, u32[]{:S(2)}, u32[]{:S(2)}) collective-permute-start(bf16[128,1024]{1,0:T(8,128)(2,1)} %get-tuple-element.173.refs_1_), channel_id=1, source_target_pairs={{0,8},{2,10},{4,12},{6,14},{8,0},{10,2},{12,4},{14,6},{16,24},{18,... | collective-permute-start | bytes 786440 | tf_op jit(solution)/shard_map/ppermute | solution.py:476
  243.4 14.5 %collective-permute-start.34 = (bf16[128,1024]{1,0:T(8,128)(2,1)}, bf16[128,1024]{1,0:T(8,128)(2,1)}, u32[]{:S(2)}, u32[]{:S(2)}) collective-permute-start(bf16[128,1024]{1,0:T(8,128)(2,1)} %get-tuple-element.176.refs_5_), channel_id=1, source_target_pairs={{0,16},{2,18},{4,20},{6,22},{8,24},{10,26},{12,28},{14,30},{16,0},... | collective-permute-start | bytes 786440 | tf_op jit(solution)/shard_map/ppermute | solution.py:476
  262.2 23.8 %collective-permute-start.36 = (bf16[512,128]{1,0:T(8,128)(2,1)}, bf16[512,128]{1,0:T(8,128)(2,1)}, u32[]{:S(2)}, u32[]{:S(2)}) collective-permute-start(bf16[512,128]{1,0:T(8,128)(2,1)} %convert_element_type.38), channel_id=1, source_target_pairs={{0,1},{1,0},{2,3},{3,2},{4,5},{5,4},{6,7},{7,6},{8,9},{9,8},{10,11... | collective-permute-start | bytes 393224 | tf_op jit(solution)/shard_map/ppermute | solution.py:476
  262.2 15.1 %collective-permute-start.37 = (bf16[128,1024]{1,0:T(8,128)(2,1)}, bf16[128,1024]{1,0:T(8,128)(2,1)}, u32[]{:S(2)}, u32[]{:S(2)}) collective-permute-start(bf16[128,1024]{1,0:T(8,128)(2,1)} %get-tuple-element.186.mine_ref), channel_id=1, source_target_pairs={{0,16},{2,18},{4,20},{6,22},{8,24},{10,26},{12,28},{14,30},{16,0},... | collective-permute-start | bytes 786440 | tf_op jit(solution)/shard_map/ppermute | solution.py:476
  285.9 1.9 collective-permute-start.38

commit v11 on v10

--- a/solution.py
+++ b/solution.py
@@ -933,8 +933,8 @@
         [pltpu.VMEM((length, width), BF16)],
     )(order_own, inputs, other)
 
-    inner2, inner3, outer2, x1, own_y_a, own_y_b = after(
-        [inner2, inner3, outer2, x1, own_y_a, own_y_b], y1, early_features, moved
+    inner2, inner3, outer2, x1, sent, own_y_a, own_y_b = after(
+        [inner2, inner3, outer2, x1, sent, own_y_a, own_y_b], y1, early_features
     )
     z3 = inner2 + outer2
     x3, y3 = swap_x(z3), swap_y(z3)
@@ -969,20 +969,16 @@
         late_features, part, late_a, running_t, b_rows, kept, 0
     )
 
-    own_y_b, x2b, y3_b, x1_b, sent_a, x_a, grad_x = after(
-        [own_y_b, x2b, y3_b, x1_b, sent_a, x_a, grad_x], y2b
-    )
+    own_y_b, x2b, y3_b, x1_b, grad_x = after([own_y_b, x2b, y3_b, x1_b, grad_x], y2b, sent_a)
     d0b, d2b = swap_x(own_y_b), swap_y(x2b)
     d3b, d1b = swap_x(y3_b), swap_y(x1_b)
-    entering_a, sent_a = scan_step(factors_1, 0, sent_a, (), 1)
     product = multiply_blocks(early_order, grad_x, [[piece] for piece in early], ())
     shared = (running, running_t, grad_out)
     here = groups // 2
     grid = (spans, here)
-    inner_a = shared + (x_a, b_rows, c_rows, leaving_all)
-    decay_a, grad_b, grad_c = inner(grid, 0, half, inner_a, ())
-
-    d0b, d2b = after([d0b, d2b], d3b, d1b, sent_a, grad_b, product[0])
+
+    d0b, d2b, sent_a = after([d0b, d2b, sent_a], d3b, d1b, product[0])
+    entering_a, sent_a = scan_step(factors_1, 0, sent_a, (), 1)
     late_b = [d0b, d1b, d3b, z2b, x2b, y2b, d2b]
     x_b, states_b, sent_b = late_forward(
         late_features, part, late_b, running_t, b_rows, kept, here
@@ -994,13 +990,15 @@
     )
     away, own = multiply_blocks(late_order, grad_x, pairs, product)
 
-    sent_a, sent_b, x_b, away = after([sent_a, sent_b, x_b, away])
+    sent_a, sent_b, x_a, away = after([sent_a, sent_b, x_a, away])
     entering_b, sent_b, entering_a, sent_a = scan_pair(
         (factors_2, here, sent_b, (entering_b,), 2), (factors_4, 0, sent_a, (entering_a,), 4)
     )
     got = swap(away, "head", 1)
-
-    sent_a, sent_b, x_b = after([sent_a, sent_b, x_b])
+    inner_a = shared + (x_a, b_rows, c_rows, leaving_all)
+    decay_a, grad_b, grad_c = inner(grid, 0, half, inner_a, ())
+
+    sent_a, sent_b, x_b, grad_b = after([sent_a, sent_b, x_b, grad_b])
     entering_b, sent_b, entering_a = scan_pair(
         (factors_4, here, sent_b, (entering_b,), 4),
         (factors_8, 0, sent_a, (entering_a,), 8),

time: 291 us -> 280 us (0.962)
  waiting for transfers between devices: 87.6 us -> 76.5 us
    ppermute x35, waiting for transfers between devices: 87.6 us -> 76.5 us  [swap(): return lax.ppermute(value, axis, [(i, i ^ bit) for i in range(count)])]
  transfers between devices with their start and end apart: 39 -> 39, of which waited for: 12 -> 14; matrix products, arithmetic and copies ran while one was open for 10% -> 10% of each run, Pallas kernels for 39% -> 42%
where the time goes in v11:
time: 280 us; the launch traced here: 279 us
  Pallas kernels  122 us (44%)
  waiting for transfers between devices  76.5 us (27%)
  starting transfers between devices  42.7 us (15%)
  other arithmetic  19.8 us (7%)
  local copies, waits for them, and re-layouts  14.3 us (5%)
  between operations  3.35 us (1%)
    ppermute x35, waiting for transfers between devices, swap(): return lax.ppermute(value, axis, [(i, i ^ bit) for i in range(count)])  76.5 us
    ppermute x35, starting transfers between devices, swap(): return lax.ppermute(value, axis, [(i, i ^ bit) for i in range(count)])  36.5 us
    pallas_call x2, Pallas kernels, multiply_blocks(): pl.pallas_call(functools.partial(blocks_kernel, [len(piece) for piece in...  18.9 us
    pallas_call x2, Pallas kernels, inner(): call(inner_kernel, grid, specs + [SHARED] * len(so_far), [run_spec(), SHA...  17.9 us
    pallas_call x2, Pallas kernels, late_forward(): call(functools.partial(late_forward_kernel, len(pieces)), (columns // WID...  13 us
    pallas_call x2, Pallas kernels, state_terms(): pl.pallas_call(state_kernel, grid=grid, in_specs=[run_t_spec(here), rows_...  11 us
    pallas_call x4, Pallas kernels, back_step(): call(functools.partial(back_kernel, bit), (columns // (2 * WIDE),), [SCAL...  10.5 us
    pallas_call x1, Pallas kernels, grad_rows(): call(functools.partial(grad_x_kernel, transposed), (length // SPAN, runni...  10.4 us
  transfers between devices with their start and end apart: 39, of which 14 were waited for; matrix products, arithmetic and copies ran while one was open for 10% of the time, Pallas kernels for 42%

profile of v11, /device:TPU:0, one launch (start us, length us, event | category | flops | bytes accessed | tf_op | source)
XLA Modules:
  0.0 278.5 jit_solution(4101293395329350952)
XLA Ops:
  1.1 2.6 collective-permute-start.3
  3.7 1.6 collective-permute-start
  5.3 1.6 collective-permute-start.1
  6.9 1.5 collective-permute-start.2
  8.4 9.1 %shard_map.111 = (f32[32,512]{1,0:T(8,128)}, f32[4,512,8]{2,1,0:T(8,128)}, f32[2,8,2048]{2,1,0:T(8,128)}, f32[2,128,2048]{2,1,0:T(8,128)}) custom-call(f32[32,512]{1,0:T(8,128)} %d_ref.1, bf16[512,2048]{1,0:T(8,128)(2,1)} %g_ref.11, bf16[512,128]{1,0:T(8,128)(2,1)} %c_ref.11), custom_call_target="tpu_custom_call" | custom-call | flops 268435456 | bytes 6291456 | tf_op jit(solution)/shard_map/pallas_call | solution.py:823
  17.5 3.6 %shard_map.112 = (f32[8,2048]{1,0:T(8,128)}, bf16[144,2048]{1,0:T(8,128)(2,1)}) custom-call(f32[2,128,2048]{2,1,0:T(8,128)} %get-tuple-element.102.own_ref, f32[2,8,2048]{2,1,0:T(8,128)} %get-tuple-element.103.kept_ref.a_ref), custom_call_target="tpu_custom_call" | custom-call | bytes 3670016 | tf_op jit(solution)/shard_map/pallas_call | solution.py:732
  21.7 6.3 %collective-permute-done.3.refs_3_.refs_1_ = bf16[256,2048]{1,0:T(8,128)(2,1)} collective-permute-done((bf16[256,2048]{1,0:T(8,128)(2,1)}, bf16[256,2048]{1,0:T(8,128)(2,1)}, u32[]{:S(2)}, u32[]{:S(2)}) %collective-permute-start.3) | collective-permute-done | bytes 1048608 | tf_op jit(solution)/shard_map/ppermute | solution.py:476
  29.3 2.9 %collective-permute-done.2.refs_2_ = bf16[256,2048]{1,0:T(8,128)(2,1)} collective-permute-done((bf16[256,2048]{1,0:T(8,128)(2,1)}, bf16[256,2048]{1,0:T(8,128)(2,1)}, u32[]{:S(2)}, u32[]{:S(2)}) %collective-permute-start.2) | collective-permute-done | bytes 1048608 | tf_op jit(solution)/shard_map/ppermute | solution.py:476
  32.2 1.5 collective-permute-start.10
  33.7 1.7 collective-permute-start.5
  36.0 1.3 collective-permute-start.6
  37.3 1.3 constant_dynamic-slice_fusion
  38.6 2.1 collective-permute-done.8.got_ref
  40.7 2.4 shard_map.115
  43.1 2.0 collective-permute-start.9
  45.2 1.3 fusion.7
  49.6 5.1 %shard_map.117 = (bf16[512,2304]{1,0:T(8,128)(2,1)}, bf16[512,1792]{1,0:T(8,128)(2,1)}) custom-call(s32[16]{0:T(128)} %get-tuple-element.215.order_ref, bf16[512,2048]{1,0:T(8,128)(2,1)} %own_ref.1, bf16[512,2048]{1,0:T(8,128)(2,1)} %collective-permute-done.4.refs_1_.other_ref), custom_call_target="tpu_custom_call" | custom-call | bytes 8388608 | tf_op jit(solution)/shard_map/pallas_call | solution.py:925
  54.7 2.2 fusion.6
  56.9 12.3 %collective-permute-done.9.got_ref = bf16[144,2048]{1,0:T(8,128)(2,1)} collective-permute-done((bf16[144,2048]{1,0:T(8,128)(2,1)}, bf16[144,2048]{1,0:T(8,128)(2,1)}, u32[]{:S(2)}, u32[]{:S(2)}) %collective-permute-start.9) | collective-permute-done | bytes 589856 | tf_op jit(solution)/shard_map/ppermute | solution.py:476
  69.2 2.7 shard_map.116
  72.0 3.0 %add.123.refs_6_ = bf16[256,2048]{1,0:T(8,128)(2,1)} add(bf16[256,2048]{1,0:T(8,128)(2,1)} %get-tuple-element.117, bf16[256,2048]{1,0:T(8,128)(2,1)} %get-tuple-element.118) | non-fusion elementwise | flops 524288 | bytes 3145728 | tf_op jit(solution)/shard_map/add | solution.py:939
  75.0 1.5 collective-permute-start.12
  77.0 1.5 collective-permute-start.11
  78.5 3.7 %collective-permute-start.15 = (bf16[144,2048]{1,0:T(8,128)(2,1)S(1)}, bf16[144,2048]{1,0:T(8,128)(2,1)S(1)}, u32[]{:S(2)}, u32[]{:S(2)}) collective-permute-start(bf16[144,2048]{1,0:T(8,128)(2,1)S(1)} %copy-done), channel_id=1, source_target_pairs={{0,8},{2,10},{4,12},{6,14},{8,0},{10,2},{12,4},{14,6},{16,24},{18,... | collective-permute-start | bytes 1769480 | tf_op jit(solution)/shard_map/ppermute | solution.py:476
  82.2 2.2 fusion.5
  84.4 30.2 %collective-permute-done.15.got_ref = bf16[144,2048]{1,0:T(8,128)(2,1)S(1)} collective-permute-done((bf16[144,2048]{1,0:T(8,128)(2,1)S(1)}, bf16[144,2048]{1,0:T(8,128)(2,1)S(1)}, u32[]{:S(2)}, u32[]{:S(2)}) %collective-permute-start.15) | collective-permute-done | bytes 589856 | tf_op jit(solution)/shard_map/ppermute | solution.py:476
  115.4 2.7 shard_map.120
  118.5 2.6 slice_add_fusion
  121.1 1.5 collective-permute-start.14
  123.1 2.3 fusion.4
  125.9 1.5 collective-permute-start.19
  127.5 1.4 slice.85
  128.9 10.2 %shard_map.122.refs_7_.part_ref = f32[512,2048]{1,0:T(8,128)} custom-call(bf16[512,2304]{1,0:T(8,128)(2,1)} %get-tuple-element.113.refs_8_.f_ref, bf16[256,2048]{1,0:T(8,128)(2,1)} %refs_0_.3, bf16[256,2048]{1,0:T(8,128)(2,1)} %collective-permute-done.3.refs_3_.refs_1_, bf16[256,2048]{1,0:T(8,128)(2,1)} %get-tuple-element.112.refs_2_, ...), custom_call_target="tpu_custom_call" | custom-call | flops 4831838208 | bytes 9437184 | tf_op jit(solution)/shard_map/pallas_call | solution.py:651
  139.1 4.4 %collective-permute-done.16.got_ref = bf16[144,2048]{1,0:T(8,128)(2,1)} collective-permute-done((bf16[144,2048]{1,0:T(8,128)(2,1)}, bf16[144,2048]{1,0:T(8,128)(2,1)}, u32[]{:S(2)}, u32[]{:S(2)}) %collective-permute-start.16) | collective-permute-done | bytes 589856 | tf_op jit(solution)/shard_map/ppermute | solution.py:476
  143.5 2.7 shard_map.121
  146.2 1.6 collective-permute-start.22
  148.3 2.1 fusion.1
  152.0 1.5 collective-permute-start.21
  154.9 10.4 %shard_map.125.refs_4_ = bf16[2048,512]{1,0:T(8,128)(2,1)} custom-call(f32[32,512]{1,0:T(8,128)} %get-tuple-element.134.r_ref, f32[4,512,8]{2,1,0:T(8,128)} %get-tuple-element.135.rt_ref, bf16[512,2048]{1,0:T(8,128)(2,1)} %g_ref.11, bf16[512,128]{1,0:T(8,128)(2,1)} %b_ref.9, bf16[512,128]{1,0:T(8,128)(2,1)} %c_ref.11, ...), custom_call_target="tpu_custom_call" | custom-call | flops 2147483648 | bytes 6291456 | tf_op jit(solution)/shard_map/pallas_call | solution.py:1028
  165.3 6.5 %shard_map.126 = (bf16[512,1024]{1,0:T(8,128)(2,1)}, f32[2,128,1024]{2,1,0:T(8,128)}, bf16[128,1024]{1,0:T(8,128)(2,1)}) custom-call(bf16[512,1792]{1,0:T(8,128)(2,1)} %get-tuple-element.136.f_ref, f32[512,2048]{1,0:T(8,128)} %shard_map.122.refs_7_.part_ref, f32[4,512,8]{2,1,0:T(8,128)} %get-tuple-element.135.rt_ref, bf16[512,128]{1,0:T(8,128)(2,1)} %b_ref.9, ...), custom_call_target="tpu_custom_call" | custom-call | flops 1879048192 | bytes 3670016 | tf_op jit(solution)/shard_map/pallas_call | solution.py:671
  173.9 1.5 collective-permute-start.26
  175.4 1.5 collective-permute-start.27
  176.9 10.0 %shard_map.128 = (bf16[512,2048]{1,0:T(8,128)(2,1)}, bf16[512,2048]{1,0:T(8,128)(2,1)}) custom-call(s32[9]{0:T(128)} %bitcast.34, bf16[2048,512]{1,0:T(8,128)(2,1)} %get-tuple-element.140.g_ref, bf16[256,2048]{1,0:T(8,128)(2,1)} %refs_0_.3, bf16[256,2048]{1,0:T(8,128)(2,1)} %collective-permute-done.3.refs_3_.refs_1_, ...), custom_call_target="tpu_custom_call" | custom-call | flops 4831838208 | bytes 9437184 | tf_op jit(solution)/shard_map/pallas_call | solution.py:705
  188.6 8.5 %collective-permute-done.26.refs_3_.refs_2_.refs_5_ = bf16[256,1024]{1,0:T(8,128)(2,1)} collective-permute-done((bf16[256,1024]{1,0:T(8,128)(2,1)}, bf16[256,1024]{1,0:T(8,128)(2,1)}, u32[]{:S(2)}, u32[]{:S(2)}) %collective-permute-start.26) | collective-permute-done | bytes 524320 | tf_op jit(solution)/shard_map/ppermute | solution.py:476
  197.5 1.4 collective-permute-start.28
  200.1 6.5 %shard_map.131 = (bf16[512,1024]{1,0:T(8,128)(2,1)}, f32[2,128,1024]{2,1,0:T(8,128)}, bf16[128,1024]{1,0:T(8,128)(2,1)}) custom-call(bf16[512,1792]{1,0:T(8,128)(2,1)} %get-tuple-element.136.f_ref, f32[512,2048]{1,0:T(8,128)} %shard_map.122.refs_7_.part_ref, f32[4,512,8]{2,1,0:T(8,128)} %get-tuple-element.135.rt_ref, bf16[512,128]{1,0:T(8,128)(2,1)} %b_ref.9, ...), custom_call_target="tpu_custom_call" | custom-call | flops 1879048192 | bytes 3670016 | tf_op jit(solution)/shard_map/pallas_call | solution.py:671
  206.6 2.0 shard_map.130
  209.8 8.9 %shard_map.133 = (bf16[512,2048]{1,0:T(8,128)(2,1)}, bf16[512,2048]{1,0:T(8,128)(2,1)}) custom-call(s32[7]{0:T(128)} %slice.74.order_ref, bf16[2048,512]{1,0:T(8,128)(2,1)} %get-tuple-element.140.g_ref, bf16[256,1024]{1,0:T(8,128)(2,1)} %collective-permute-done.22.refs_0_, ...), custom_call_target="tpu_custom_call", output_to_operand_aliasing={{0}: (16, {}), {1}: (17, {})} | custom-call | flops 3758096384 | bytes 7340032 | tf_op jit(solution)/shard_map/pallas_call | solution.py:705
  218.7 2.7 shard_map.134
  221.4 1.6 collective-permute-start.31
  223.0 8.8 %shard_map.137 = (f32[16,512]{1,0:T(8,128)}, f32[512,128]{1,0:T(8,128)}, f32[512,128]{1,0:T(8,128)}) custom-call(f32[32,512]{1,0:T(8,128)} %get-tuple-element.134.r_ref, f32[4,512,8]{2,1,0:T(8,128)} %get-tuple-element.135.rt_ref, bf16[512,2048]{1,0:T(8,128)(2,1)} %g_ref.11, bf16[512,1024]{1,0:T(8,128)(2,1)} %get-tuple-element.172.x_ref, ...), custom_call_target="tpu_custom_call" | custom-call | flops 1610612736 | bytes 3145728 | tf_op jit(solution)/shard_map/pallas_call | solution.py:851
  231.8 2.8 %shard_map.136 = (f32[128,1024]{1,0:T(8,128)}, bf16[128,1024]{1,0:T(8,128)(2,1)}, f32[128,1024]{1,0:T(8,128)}, bf16[128,1024]{1,0:T(8,128)(2,1)}) custom-call(f32[8,2048]{1,0:T(8,128)} %get-tuple-element.157.refs_3_.refs_0_, bf16[128,1024]{1,0:T(8,128)(2,1)} %get-tuple-element.165.refs_1_, bf16[128,1024]{1,0:T(8,128)(2,1)} %collective-permute-done.31.refs_2_, ...), custom_call_target="tpu_custom_call" | custom-call | bytes 2621440 | tf_op jit(solution)/shard_map/pallas_call | solution.py:798
  234.6 2.0 collective-permute-start.33
  236.9 9.0 %shard_map.140 = (f32[16,512]{1,0:T(8,128)}, f32[512,128]{1,0:T(8,128)}, f32[512,128]{1,0:T(8,128)}) custom-call(f32[32,512]{1,0:T(8,128)} %get-tuple-element.134.r_ref, f32[4,512,8]{2,1,0:T(8,128)} %get-tuple-element.135.rt_ref, bf16[512,2048]{1,0:T(8,128)(2,1)} %g_ref.11, bf16[512,1024]{1,0:T(8,128)(2,1)} %get-tuple-element.182.x_ref, ...), custom_call_target="tpu_custom_call" | custom-call | flops 1610612736 | bytes 3145728 | tf_op jit(solution)/shard_map/pallas_call | solution.py:851
  245.9 2.1 collective-permute-done.33.refs_2_
  248.0 3.3 %collective-permute-done.34.refs_6_ = bf16[128,1024]{1,0:T(8,128)(2,1)} collective-permute-done((bf16[128,1024]{1,0:T(8,128)(2,1)}, bf16[128,1024]{1,0:T(8,128)(2,1)}, u32[]{:S(2)}, u32[]{:S(2)}) %collective-permute-start.34) | collective-permute-done | bytes 262176 | tf_op jit(solution)/shard_map/ppermute | solution.py:476
  251.3 2.7 shard_map.139
  254.4 1.6 convert_element_type.38
  256.0 4.4 %add_convert_fusion.refs_1_ = bf16[512,2048]{1,0:T(8,128)(2,1)} fusion(bf16[512,2048]{1,0:T(8,128)(2,1)} %get-tuple-element.186, bf16[512,2048]{1,0:T(8,128)(2,1)} %get-tuple-element.155), kind=kLoop, calls=%fused_computation | loop fusion | flops 4194304 | bytes 6291456 | tf_op jit(solution)/shard_map/convert_element_type | solution.py:1012
  260.4 5.5 %shard_map.143 = (f32[32,512]{1,0:T(8,128)}, f32[512,128]{1,0:T(8,128)}) custom-call(f32[4,512,8]{2,1,0:T(8,128)} %get-tuple-element.135.rt_ref, bf16[512,2048]{1,0:T(8,128)(2,1)} %g_ref.11, bf16[512,128]{1,0:T(8,128)(2,1)} %c_ref.11, f32[128,1024]{1,0:T(8,128)} %get-tuple-element.190.s_ref, f32[2,128,1024]{2,1,0:T(8,128)} %get-tuple-element.191.e_ref, ...), custom_call_target="tpu_custom_call" | custom-call | flops 268435456 | bytes 3145728 | tf_op jit(solution)/shard_map/pallas_call | solution.py:869
  266.0 2.1 shard_map.142.refs_0_
  268.0 5.5 %shard_map.145 = (f32[32,512]{1,0:T(8,128)}, f32[512,128]{1,0:T(8,128)}) custom-call(f32[4,512,8]{2,1,0:T(8,128)} %get-tuple-element.135.rt_ref, bf16[512,2048]{1,0:T(8,128)(2,1)} %g_ref.11, bf16[512,128]{1,0:T(8,128)(2,1)} %c_ref.11, f32[128,1024]{1,0:T(8,128)} %shard_map.144.s_ref, ...), custom_call_target="tpu_custom_call", output_to_operand_aliasing={{0}: (9, {})} | custom-call | flops 268435456 | bytes 3145728 | tf_op jit(solution)/shard_map/pallas_call | solution.py:869
  275.1 1.7 convert_add_fusion.1
  276.8 1.7 convert_add_fusion
  (73 shorter events, 18.6 us)
Async XLA Ops:
  0.6 20.5 %collective-permute-start.4 = (bf16[512,2048]{1,0:T(8,128)(2,1)}, bf16[512,2048]{1,0:T(8,128)(2,1)}, u32[]{:S(2)}, u32[]{:S(2)}) collective-permute-start(bf16[512,2048]{1,0:T(8,128)(2,1)} %own_ref.1), channel_id=1, source_target_pairs={{0,1},{1,0},{2,3},{3,2},{4,5},{5,4},{6,7},{7,6},{8,9},{9,8},{10,11... | collective-permute-start | bytes 6291464 | tf_op jit(solution)/shard_map/ppermute | solution.py:476
  1.1 26.9 %collective-permute-start.3 = (bf16[256,2048]{1,0:T(8,128)(2,1)}, bf16[256,2048]{1,0:T(8,128)(2,1)}, u32[]{:S(2)}, u32[]{:S(2)}) collective-permute-start(bf16[256,2048]{1,0:T(8,128)(2,1)} %refs_0_.3), channel_id=1, source_target_pairs={{0,2},{2,0},{4,6},{6,4},{8,10},{10,8},{12,14},{14,12},{16,18},{18,... | collective-permute-start | bytes 3145736 | tf_op jit(solution)/shard_map/ppermute | solution.py:476
  3.7 25.5 %collective-permute-start = (bf16[256,2048]{1,0:T(8,128)(2,1)}, bf16[256,2048]{1,0:T(8,128)(2,1)}, u32[]{:S(2)}, u32[]{:S(2)}) collective-permute-start(bf16[256,2048]{1,0:T(8,128)(2,1)} %refs_0_.3), channel_id=1, source_target_pairs={{0,8},{2,10},{4,12},{6,14},{8,0},{10,2},{12,4},{14,6},{16,24},{18,... | collective-permute-start | bytes 3145736 | tf_op jit(solution)/shard_map/ppermute | solution.py:476
  5.3 24.0 %collective-permute-start.1 = (bf16[256,2048]{1,0:T(8,128)(2,1)}, bf16[256,2048]{1,0:T(8,128)(2,1)}, u32[]{:S(2)}, u32[]{:S(2)}) collective-permute-start(bf16[256,2048]{1,0:T(8,128)(2,1)} %refs_0_.3), channel_id=1, source_target_pairs={{8,16},{10,18},{12,20},{14,22},{16,8},{18,10},{20,12},{22,14},{9,1... | collective-permute-start | bytes 3145736 | tf_op jit(solution)/shard_map/ppermute | solution.py:537
  6.9 25.3 %collective-permute-start.2 = (bf16[256,2048]{1,0:T(8,128)(2,1)}, bf16[256,2048]{1,0:T(8,128)(2,1)}, u32[]{:S(2)}, u32[]{:S(2)}) collective-permute-start(bf16[256,2048]{1,0:T(8,128)(2,1)} %refs_0_.3), channel_id=1, source_target_pairs={{0,4},{2,6},{4,0},{6,2},{8,12},{10,14},{12,8},{14,10},{16,20},{18,... | collective-permute-start | bytes 3145736 | tf_op jit(solution)/shard_map/ppermute | solution.py:476
  21.1 19.6 %collective-permute-start.8 = (bf16[144,2048]{1,0:T(8,128)(2,1)}, bf16[144,2048]{1,0:T(8,128)(2,1)}, u32[]{:S(2)}, u32[]{:S(2)}) collective-permute-start(bf16[144,2048]{1,0:T(8,128)(2,1)} %shard_map.113.refs_4_.mine_ref), channel_id=1, source_target_pairs={{0,2},{2,0},{4,6},{6,4},{8,10},{10,8},{12,14},{14,12},{16,18},{18,... | collective-permute-start | bytes 1769480 | tf_op jit(solution)/shard_map/ppermute | solution.py:476
  32.2 39.7 %collective-permute-start.10 = (bf16[256,2048]{1,0:T(8,128)(2,1)}, bf16[256,2048]{1,0:T(8,128)(2,1)}, u32[]{:S(2)}, u32[]{:S(2)}) collective-permute-start(bf16[256,2048]{1,0:T(8,128)(2,1)} %get-tuple-element.106.refs_3_), channel_id=1, source_target_pairs={{0,4},{2,6},{4,0},{6,2},{8,12},{10,14},{12,8},{14,10},{16,20},{18,... | collective-permute-start | bytes 3145736 | tf_op jit(solution)/shard_map/ppermute | solution.py:476
  33.7 38.2 %collective-permute-start.5 = (bf16[256,2048]{1,0:T(8,128)(2,1)}, bf16[256,2048]{1,0:T(8,128)(2,1)}, u32[]{:S(2)}, u32[]{:S(2)}) collective-permute-start(bf16[256,2048]{1,0:T(8,128)(2,1)} %get-tuple-element.106.refs_3_), channel_id=1, source_target_pairs={{8,16},{10,18},{12,20},{14,22},{16,8},{18,10},{20,12},{22,14},{9,1... | collective-permute-start | bytes 3145736 | tf_op jit(solution)/shard_map/ppermute | solution.py:537
  35.5 36.5 %collective-permute-start.7 = (bf16[256,2048]{1,0:T(8,128)(2,1)}, bf16[256,2048]{1,0:T(8,128)(2,1)}, u32[]{:S(2)}, u32[]{:S(2)}) collective-permute-start(bf16[256,2048]{1,0:T(8,128)(2,1)} %get-tuple-element.106.refs_3_), channel_id=1, source_target_pairs={{0,2},{2,0},{4,6},{6,4},{8,10},{10,8},{12,14},{14,12},{16,18},{18,... | collective-permute-start | bytes 3145736 | tf_op jit(solution)/shard_map/ppermute | solution.py:476
  36.0 36.0 %collective-permute-start.6 = (bf16[256,2048]{1,0:T(8,128)(2,1)}, bf16[256,2048]{1,0:T(8,128)(2,1)}, u32[]{:S(2)}, u32[]{:S(2)}) collective-permute-start(bf16[256,2048]{1,0:T(8,128)(2,1)} %get-tuple-element.105.refs_0_), channel_id=1, source_target_pairs={{8,0},{10,2},{12,4},{14,6},{16,24},{18,26},{20,28},{22,30},{9,1},{... | collective-permute-start | bytes 3145736 | tf_op jit(solution)/shard_map/ppermute | solution.py:537
  43.1 26.1 %collective-permute-start.9 = (bf16[144,2048]{1,0:T(8,128)(2,1)}, bf16[144,2048]{1,0:T(8,128)(2,1)}, u32[]{:S(2)}, u32[]{:S(2)}) collective-permute-start(bf16[144,2048]{1,0:T(8,128)(2,1)} %get-tuple-element.109.mine_ref), channel_id=1, source_target_pairs={{0,4},{2,6},{4,0},{6,2},{8,12},{10,14},{12,8},{14,10},{16,20},{18,... | collective-permute-start | bytes 1769480 | tf_op jit(solution)/shard_map/ppermute | solution.py:476
  72.0 6.5 %copy-start = (bf16[144,2048]{1,0:T(8,128)(2,1)S(1)}, bf16[144,2048]{1,0:T(8,128)(2,1)}, u32[]{:S(2)}) copy-start(bf16[144,2048]{1,0:T(8,128)(2,1)} %get-tuple-element.123.mine_ref) | copy-start | bytes 1769476
  75.0 43.6 %collective-permute-start.12 = (bf16[256,2048]{1,0:T(8,128)(2,1)}, bf16[256,2048]{1,0:T(8,128)(2,1)}, u32[]{:S(2)}, u32[]{:S(2)}) collective-permute-start(bf16[256,2048]{1,0:T(8,128)(2,1)} %add.123.refs_6_), channel_id=1, source_target_pairs={{0,4},{2,6},{4,0},{6,2},{8,12},{10,14},{12,8},{14,10},{16,20},{18,... | collective-permute-start | bytes 3145736 | tf_op jit(solution)/shard_map/ppermute | solution.py:476
  76.5 42.0 %collective-permute-start.13 = (bf16[256,2048]{1,0:T(8,128)(2,1)}, bf16[256,2048]{1,0:T(8,128)(2,1)}, u32[]{:S(2)}, u32[]{:S(2)}) collective-permute-start(bf16[256,2048]{1,0:T(8,128)(2,1)} %add.123.refs_6_), channel_id=1, source_target_pairs={{0,2},{2,0},{4,6},{6,4},{8,10},{10,8},{12,14},{14,12},{16,18},{18,... | collective-permute-start | bytes 3145736 | tf_op jit(solution)/shard_map/ppermute | solution.py:476
  77.0 41.5 %collective-permute-start.11 = (bf16[256,2048]{1,0:T(8,128)(2,1)}, bf16[256,2048]{1,0:T(8,128)(2,1)}, u32[]{:S(2)}, u32[]{:S(2)}) collective-permute-start(bf16[256,2048]{1,0:T(8,128)(2,1)} %get-tuple-element.116.refs_0_), channel_id=1, source_target_pairs={{8,0},{10,2},{12,4},{14,6},{16,24},{18,26},{20,28},{22,30},{9,1},{... | collective-permute-start | bytes 3145736 | tf_op jit(solution)/shard_map/ppermute | solution.py:537
  78.5 36.1 %collective-permute-start.15 = (bf16[144,2048]{1,0:T(8,128)(2,1)S(1)}, bf16[144,2048]{1,0:T(8,128)(2,1)S(1)}, u32[]{:S(2)}, u32[]{:S(2)}) collective-permute-start(bf16[144,2048]{1,0:T(8,128)(2,1)S(1)} %copy-done), channel_id=1, source_target_pairs={{0,8},{2,10},{4,12},{6,14},{8,0},{10,2},{12,4},{14,6},{16,24},{18,... | collective-permute-start | bytes 1769480 | tf_op jit(solution)/shard_map/ppermute | solution.py:476
  114.6 0.8 copy-start.1
  118.1 25.4 %collective-permute-start.16 = (bf16[144,2048]{1,0:T(8,128)(2,1)}, bf16[144,2048]{1,0:T(8,128)(2,1)}, u32[]{:S(2)}, u32[]{:S(2)}) collective-permute-start(bf16[144,2048]{1,0:T(8,128)(2,1)} %get-tuple-element.126.mine_ref), channel_id=1, source_target_pairs={{0,16},{2,18},{4,20},{6,22},{8,24},{10,26},{12,28},{14,30},{16,0},... | collective-permute-start | bytes 1769480 | tf_op jit(solution)/shard_map/ppermute | solution.py:476
  121.1 25.0 %collective-permute-start.14 = (bf16[256,1024]{1,0:T(8,128)(2,1)}, bf16[256,1024]{1,0:T(8,128)(2,1)}, u32[]{:S(2)}, u32[]{:S(2)}) collective-permute-start(bf16[256,1024]{1,0:T(8,128)(2,1)} %get-tuple-element.201.refs_3_.refs_6_), channel_id=1, source_target_pairs={{0,2},{2,0},{4,6},{6,4},{8,10},{10,8},{12,14},{14,12},{16,18},{18,... | collective-permute-start | bytes 1572872 | tf_op jit(solution)/shard_map/ppermute | solution.py:476
  122.6 23.6 %collective-permute-start.17 = (bf16[256,1024]{1,0:T(8,128)(2,1)}, bf16[256,1024]{1,0:T(8,128)(2,1)}, u32[]{:S(2)}, u32[]{:S(2)}) collective-permute-start(bf16[256,1024]{1,0:T(8,128)(2,1)} %get-tuple-element.201.refs_3_.refs_6_), channel_id=1, source_target_pairs={{0,4},{2,6},{4,0},{6,2},{8,12},{10,14},{12,8},{14,10},{16,20},{18,... | collective-permute-start | bytes 1572872 | tf_op jit(solution)/shard_map/ppermute | solution.py:476
  125.4 20.8 %collective-permute-start.18 = (bf16[256,1024]{1,0:T(8,128)(2,1)}, bf16[256,1024]{1,0:T(8,128)(2,1)}, u32[]{:S(2)}, u32[]{:S(2)}) collective-permute-start(bf16[256,1024]{1,0:T(8,128)(2,1)} %get-tuple-element.203), channel_id=1, source_target_pairs={{0,2},{2,0},{4,6},{6,4},{8,10},{10,8},{12,14},{14,12},{16,18},{18,... | collective-permute-start | bytes 1572872 | tf_op jit(solution)/shard_map/ppermute | solution.py:476
  125.9 20.3 %collective-permute-start.19 = (bf16[256,1024]{1,0:T(8,128)(2,1)}, bf16[256,1024]{1,0:T(8,128)(2,1)}, u32[]{:S(2)}, u32[]{:S(2)}) collective-permute-start(bf16[256,1024]{1,0:T(8,128)(2,1)} %get-tuple-element.130), channel_id=1, source_target_pairs={{0,4},{2,6},{4,0},{6,2},{8,12},{10,14},{12,8},{14,10},{16,20},{18,... | collective-permute-start | bytes 1572872 | tf_op jit(solution)/shard_map/ppermute | solution.py:476
  146.2 19.1 %collective-permute-start.22 = (bf16[256,1024]{1,0:T(8,128)(2,1)}, bf16[256,1024]{1,0:T(8,128)(2,1)}, u32[]{:S(2)}, u32[]{:S(2)}) collective-permute-start(bf16[256,1024]{1,0:T(8,128)(2,1)} %get-tuple-element.137), channel_id=1, source_target_pairs={{0,2},{2,0},{4,6},{6,4},{8,10},{10,8},{12,14},{14,12},{16,18},{18,... | collective-permute-start | bytes 1572872 | tf_op jit(solution)/shard_map/ppermute | solution.py:476
  147.8 17.5 %collective-permute-start.23 = (bf16[256,1024]{1,0:T(8,128)(2,1)}, bf16[256,1024]{1,0:T(8,128)(2,1)}, u32[]{:S(2)}, u32[]{:S(2)}) collective-permute-start(bf16[256,1024]{1,0:T(8,128)(2,1)} %get-tuple-element.138.refs_4_.refs_8_), channel_id=1, source_target_pairs={{0,4},{2,6},{4,0},{6,2},{8,12},{10,14},{12,8},{14,10},{16,20},{18,... | collective-permute-start | bytes 1572872 | tf_op jit(solution)/shard_map/ppermute | solution.py:476
  151.4 20.3 %collective-permute-start.20 = (bf16[256,1024]{1,0:T(8,128)(2,1)}, bf16[256,1024]{1,0:T(8,128)(2,1)}, u32[]{:S(2)}, u32[]{:S(2)}) collective-permute-start(bf16[256,1024]{1,0:T(8,128)(2,1)} %shard_map.124.refs_3_.refs_7_), channel_id=1, source_target_pairs={{0,2},{2,0},{4,6},{6,4},{8,10},{10,8},{12,14},{14,12},{16,18},{18,... | collective-permute-start | bytes 1572872 | tf_op jit(solution)/shard_map/ppermute | solution.py:476
  152.0 20.9 %collective-permute-start.21 = (bf16[256,1024]{1,0:T(8,128)(2,1)}, bf16[256,1024]{1,0:T(8,128)(2,1)}, u32[]{:S(2)}, u32[]{:S(2)}) collective-permute-start(bf16[256,1024]{1,0:T(8,128)(2,1)} %shard_map.124.refs_3_.refs_7_), channel_id=1, source_target_pairs={{0,4},{2,6},{4,0},{6,2},{8,12},{10,14},{12,8},{14,10},{16,20},{18,... | collective-permute-start | bytes 1572872 | tf_op jit(solution)/shard_map/ppermute | solution.py:476
  172.9 15.2 %collective-permute-start.24 = (bf16[256,1024]{1,0:T(8,128)(2,1)}, bf16[256,1024]{1,0:T(8,128)(2,1)}, u32[]{:S(2)}, u32[]{:S(2)}) collective-permute-start(bf16[256,1024]{1,0:T(8,128)(2,1)} %get-tuple-element.141), channel_id=1, source_target_pairs={{0,2},{2,0},{4,6},{6,4},{8,10},{10,8},{12,14},{14,12},{16,18},{18,... | collective-permute-start | bytes 1572872 | tf_op jit(solution)/shard_map/ppermute | solution.py:476
  173.4 15.2 %collective-permute-start.25 = (bf16[256,1024]{1,0:T(8,128)(2,1)}, bf16[256,1024]{1,0:T(8,128)(2,1)}, u32[]{:S(2)}, u32[]{:S(2)}) collective-permute-start(bf16[256,1024]{1,0:T(8,128)(2,1)} %get-tuple-element.142.refs_4_.refs_9_), channel_id=1, source_target_pairs={{0,4},{2,6},{4,0},{6,2},{8,12},{10,14},{12,8},{14,10},{16,20},{18,... | collective-permute-start | bytes 1572872 | tf_op jit(solution)/shard_map/ppermute | solution.py:476
  173.9 23.2 %collective-permute-start.26 = (bf16[256,1024]{1,0:T(8,128)(2,1)}, bf16[256,1024]{1,0:T(8,128)(2,1)}, u32[]{:S(2)}, u32[]{:S(2)}) collective-permute-start(bf16[256,1024]{1,0:T(8,128)(2,1)} %get-tuple-element.143), channel_id=1, source_target_pairs={{0,2},{2,0},{4,6},{6,4},{8,10},{10,8},{12,14},{14,12},{16,18},{18,... | collective-permute-start | bytes 1572872 | tf_op jit(solution)/shard_map/ppermute | solution.py:476
  175.4 22.0 %collective-permute-start.27 = (bf16[256,1024]{1,0:T(8,128)(2,1)}, bf16[256,1024]{1,0:T(8,128)(2,1)}, u32[]{:S(2)}, u32[]{:S(2)}) collective-permute-start(bf16[256,1024]{1,0:T(8,128)(2,1)} %get-tuple-element.144), channel_id=1, source_target_pairs={{0,4},{2,6},{4,0},{6,2},{8,12},{10,14},{12,8},{14,10},{16,20},{18,... | collective-permute-start | bytes 1572872 | tf_op jit(solution)/shard_map/ppermute | solution.py:476
  197.5 9.2 %collective-permute-start.28 = (bf16[128,1024]{1,0:T(8,128)(2,1)}, bf16[128,1024]{1,0:T(8,128)(2,1)}, u32[]{:S(2)}, u32[]{:S(2)}) collective-permute-start(bf16[128,1024]{1,0:T(8,128)(2,1)} %get-tuple-element.149.mine_ref), channel_id=1, source_target_pairs={{0,2},{2,0},{4,6},{6,4},{8,10},{10,8},{12,14},{14,12},{16,18},{18,... | collective-permute-start | bytes 786440 | tf_op jit(solution)/shard_map/ppermute | solution.py:476
  208.7 10.0 %collective-permute-start.29 = (bf16[128,1024]{1,0:T(8,128)(2,1)}, bf16[128,1024]{1,0:T(8,128)(2,1)}, u32[]{:S(2)}, u32[]{:S(2)}) collective-permute-start(bf16[128,1024]{1,0:T(8,128)(2,1)} %get-tuple-element.158.refs_1_), channel_id=1, source_target_pairs={{0,2},{2,0},{4,6},{6,4},{8,10},{10,8},{12,14},{14,12},{16,18},{18,... | collective-permute-start | bytes 786440 | tf_op jit(solution)/shard_map/ppermute | solution.py:476
  209.3 9.4 %collective-permute-start.30 = (bf16[128,1024]{1,0:T(8,128)(2,1)}, bf16[128,1024]{1,0:T(8,128)(2,1)}, u32[]{:S(2)}, u32[]{:S(2)}) collective-permute-start(bf16[128,1024]{1,0:T(8,128)(2,1)} %get-tuple-element.159.refs_4_), channel_id=1, source_target_pairs={{0,4},{2,6},{4,0},{6,2},{8,12},{10,14},{12,8},{14,10},{16,20},{18,... | collective-permute-start | bytes 786440 | tf_op jit(solution)/shard_map/ppermute | solution.py:476
  221.4 32.7 %collective-permute-start.35 = (bf16[512,2048]{1,0:T(8,128)(2,1)}, bf16[512,2048]{1,0:T(8,128)(2,1)}, u32[]{:S(2)}, u32[]{:S(2)}) collective-permute-start(bf16[512,2048]{1,0:T(8,128)(2,1)} %get-tuple-element.181), channel_id=1, source_target_pairs={{0,1},{1,0},{2,3},{3,2},{4,5},{5,4},{6,7},{7,6},{8,9},{9,8},{10,11... | collective-permute-start | bytes 6291464 | tf_op jit(solution)/shard_map/ppermute | solution.py:476
  221.4 10.4 %collective-permute-start.31 = (bf16[128,1024]{1,0:T(8,128)(2,1)}, bf16[128,1024]{1,0:T(8,128)(2,1)}, u32[]{:S(2)}, u32[]{:S(2)}) collective-permute-start(bf16[128,1024]{1,0:T(8,128)(2,1)} %get-tuple-element.165.refs_1_), channel_id=1, source_target_pairs={{0,4},{2,6},{4,0},{6,2},{8,12},{10,14},{12,8},{14,10},{16,20},{18,... | collective-permute-start | bytes 786440 | tf_op jit(solution)/shard_map/ppermute | solution.py:476
  223.0 8.8 %collective-permute-start.32 = (bf16[128,1024]{1,0:T(8,128)(2,1)}, bf16[128,1024]{1,0:T(8,128)(2,1)}, u32[]{:S(2)}, u32[]{:S(2)}) collective-permute-start(bf16[128,1024]{1,0:T(8,128)(2,1)} %get-tuple-element.167.refs_5_), channel_id=1, source_target_pairs={{0,8},{2,10},{4,12},{6,14},{8,0},{10,2},{12,4},{14,6},{16,24},{18,... | collective-permute-start | bytes 786440 | tf_op jit(solution)/shard_map/ppermute | solution.py:476
  234.6 13.4 %collective-permute-start.33 = (bf16[128,1024]{1,0:T(8,128)(2,1)}, bf16[128,1024]{1,0:T(8,128)(2,1)}, u32[]{:S(2)}, u32[]{:S(2)}) collective-permute-start(bf16[128,1024]{1,0:T(8,128)(2,1)} %get-tuple-element.174.refs_1_), channel_id=1, source_target_pairs={{0,8},{2,10},{4,12},{6,14},{8,0},{10,2},{12,4},{14,6},{16,24},{18,... | collective-permute-start | bytes 786440 | tf_op jit(solution)/shard_map/ppermute | solution.py:476
  236.6 14.7 %collective-permute-start.34 = (bf16[128,1024]{1,0:T(8,128)(2,1)}, bf16[128,1024]{1,0:T(8,128)(2,1)}, u32[]{:S(2)}, u32[]{:S(2)}) collective-permute-start(bf16[128,1024]{1,0:T(8,128)(2,1)} %get-tuple-element.177.refs_5_), channel_id=1, source_target_pairs={{0,16},{2,18},{4,20},{6,22},{8,24},{10,26},{12,28},{14,30},{16,0},... | collective-permute-start | bytes 786440 | tf_op jit(solution)/shard_map/ppermute | solution.py:476
  254.0 11.9 %collective-permute-start.37 = (bf16[128,1024]{1,0:T(8,128)(2,1)}, bf16[128,1024]{1,0:T(8,128)(2,1)}, u32[]{:S(2)}, u32[]{:S(2)}) collective-permute-start(bf16[128,1024]{1,0:T(8,128)(2,1)} %get-tuple-element.188.mine_ref), channel_id=1, source_target_pairs={{0,16},{2,18},{4,20},{6,22},{8,24},{10,26},{12,28},{14,30},{16,0},... | collective-permute-start | bytes 786440 | tf_op jit(solution)/shard_map/ppermute | solution.py:476
  256.0 19.1 %collective-permute-start.36 = (bf16[512,128]{1,0:T(8,128)(2,1)}, bf16[512,128]{1,0:T(8,128)(2,1)}, u32[]{:S(2)}, u32[]{:S(2)}) collective-permute-start(bf16[512,128]{1,0:T(8,128)(2,1)} %convert_element_type.38), channel_id=1, source_target_pairs={{0,1},{1,0},{2,3},{3,2},{4,5},{5,4},{6,7},{7,6},{8,9},{9,8},{10,11... | collective-permute-start | bytes 393224 | tf_op jit(solution)/shard_map/ppermute | solution.py:476
  274.5 2.3 collective-permute-start.38

commit v12 on v11

--- a/solution.py
+++ b/solution.py
@@ -919,6 +919,7 @@
     x1, y1 = swap_x(z1), swap_y(z1)
     inner3, outer2 = along_z(z1, MIDDLE), along_z(inner2, OUTWARD)
     own_y_a, own_y_b = own_y[:, :half], own_y[:, half:]
+    inner3_a, inner3_b = inner3[:, :half], inner3[:, half:]
     leaving, sent, log, factors_2 = back_step(spot, log, sent, (leaving,), 2)
     order_own = (order + place * (blocks // 2)) % blocks
     cut = len(EARLY) * w_in.shape[0]
@@ -933,18 +934,20 @@
         [pltpu.VMEM((length, width), BF16)],
     )(order_own, inputs, other)
 
-    inner2, inner3, outer2, x1, sent, own_y_a, own_y_b = after(
-        [inner2, inner3, outer2, x1, sent, own_y_a, own_y_b], y1, early_features
+    inner2, inner3_a, inner3_b, outer2, x1, sent, own_y_a, own_y_b = after(
+        [inner2, inner3_a, inner3_b, outer2, x1, sent, own_y_a, own_y_b], y1, early_features
     )
     z3 = inner2 + outer2
     x3, y3 = swap_x(z3), swap_y(z3)
-    outer3 = along_z(inner3, OUTWARD)
+    outer3_a = along_z(inner3_a, OUTWARD)
     x1_a, x1_b = x1[:, :half], x1[:, half:]
     leaving, sent, log, factors_4 = back_step(spot, log, sent, (leaving,), 4)
 
-    inner3, outer3, y3, x1_a, x1_b = after([inner3, outer3, y3, x1_a, x1_b], x3)
-    z2a = inner3[:, :half] + outer3[:, :half]
-    z2b = inner3[:, half:] + outer3[:, half:]
+    inner3_a, inner3_b, outer3_a, y3, x1_a, x1_b = after(
+        [inner3_a, inner3_b, outer3_a, y3, x1_a, x1_b], x3
+    )
+    z2a = inner3_a + outer3_a
+    outer3_b = along_z(inner3_b, OUTWARD)
     y3_a, y3_b = y3[:, :half], y3[:, half:]
     x2a, y2a = swap_x(z2a), swap_y(z2a)
     d3a, d1a = swap_x(y3_a), swap_y(x1_a)
@@ -952,13 +955,13 @@
     early = [w_in, own_x, own_y, z1, x1, y1, z3, x3, y3]
     part = early_forward(early_features, early)
 
-    own_y_a, x2a, z2b, leaving = after([own_y_a, x2a, z2b, leaving], y2a, d3a, d1a, part)
+    own_y_a, x2a, leaving = after([own_y_a, x2a, leaving], y2a, d3a, d1a, part)
     d0a, d2a = swap_x(own_y_a), swap_y(x2a)
     leaving_all = [leaving]
     for k in range(spans - 1, 0, -1):
         leaving_all.insert(0, own_grads[k] + kept[k, :1] * leaving_all[0])
     leaving_all = jnp.stack([value.astype(BF16) for value in leaving_all])
-    (z2b,) = after([z2b], leaving_all)
+    (z2b,) = after([inner3_b + outer3_b], leaving_all)
     x2b, y2b = swap_x(z2b), swap_y(z2b)
     skip = jnp.repeat(skip_gain, P_SIZE)[None]
     grad_x = grad_rows(running, running_t, grad_out, b_rows, c_rows, leaving_all, skip, True)

time: 280 us -> 265 us (0.946)
  waiting for transfers between devices: 76.5 us -> 57.1 us
    ppermute x35, waiting for transfers between devices: 76.5 us -> 48.7 us  [swap(): return lax.ppermute(value, axis, [(i, i ^ bit) for i in range(count)])]
    ppermute x4 -> x5, waiting for transfers between devices: 0.01 us -> 8.39 us  [along_z(): return lax.ppermute(value, 'ctx', pairs)]
    ppermute x4 -> x5, starting transfers between devices: 6.12 us -> 7.34 us  [along_z(): return lax.ppermute(value, 'ctx', pairs)]
  transfers between devices with their start and end apart: 39 -> 40, of which waited for: 14 -> 14; matrix products, arithmetic and copies ran while one was open for 10% -> 12% of each run, Pallas kernels for 42% -> 44%
where the time goes in v12:
time: 265 us; the launch traced here: 263 us
  Pallas kernels  122 us (46%)
  waiting for transfers between devices  57.1 us (22%)
  starting transfers between devices  42.9 us (16%)
  other arithmetic  22.1 us (8%)
  local copies, waits for them, and re-layouts  16.1 us (6%)
  between operations  3.52 us (1%)
    ppermute x35, waiting for transfers between devices, swap(): return lax.ppermute(value, axis, [(i, i ^ bit) for i in range(count)])  48.7 us
    ppermute x35, starting transfers between devices, swap(): return lax.ppermute(value, axis, [(i, i ^ bit) for i in range(count)])  35.6 us
    pallas_call x2, Pallas kernels, multiply_blocks(): pl.pallas_call(functools.partial(blocks_kernel, [len(piece) for piece in...  18.9 us
    pallas_call x2, Pallas kernels, inner(): call(inner_kernel, grid, specs + [SHARED] * len(so_far), [run_spec(), SHA...  17.8 us
    pallas_call x2, Pallas kernels, late_forward(): call(functools.partial(late_forward_kernel, len(pieces)), (columns // WID...  13 us
    pallas_call x2, Pallas kernels, state_terms(): pl.pallas_call(state_kernel, grid=grid, in_specs=[run_t_spec(here), rows_...  11 us
    pallas_call x4, Pallas kernels, back_step(): call(functools.partial(back_kernel, bit), (columns // (2 * WIDE),), [SCAL...  10.5 us
    pallas_call x1, Pallas kernels, grad_rows(): call(functools.partial(grad_x_kernel, transposed), (length // SPAN, runni...  10.4 us
  transfers between devices with their start and end apart: 40, of which 14 were waited for; matrix products, arithmetic and copies ran while one was open for 12% of the time, Pallas kernels for 44%

profile of v12, /device:TPU:0, one launch (start us, length us, event | category | flops | bytes accessed | tf_op | source)
XLA Modules:
  0.0 263.5 jit_solution(5151882360171102517)
XLA Ops:
  1.1 2.6 collective-permute-start.3
  3.7 1.6 collective-permute-start
  5.3 1.7 collective-permute-start.1
  7.0 1.5 collective-permute-start.2
  8.5 9.1 %shard_map.111 = (f32[32,512]{1,0:T(8,128)}, f32[4,512,8]{2,1,0:T(8,128)}, f32[2,8,2048]{2,1,0:T(8,128)}, f32[2,128,2048]{2,1,0:T(8,128)}) custom-call(f32[32,512]{1,0:T(8,128)} %d_ref.1, bf16[512,2048]{1,0:T(8,128)(2,1)} %g_ref.11, bf16[512,128]{1,0:T(8,128)(2,1)} %c_ref.11), custom_call_target="tpu_custom_call" | custom-call | flops 268435456 | bytes 6291456 | tf_op jit(solution)/shard_map/pallas_call | solution.py:823
  17.6 3.5 %shard_map.112 = (f32[8,2048]{1,0:T(8,128)}, bf16[144,2048]{1,0:T(8,128)(2,1)}) custom-call(f32[2,128,2048]{2,1,0:T(8,128)} %get-tuple-element.103.own_ref, f32[2,8,2048]{2,1,0:T(8,128)} %get-tuple-element.104.kept_ref.a_ref), custom_call_target="tpu_custom_call" | custom-call | bytes 3670016 | tf_op jit(solution)/shard_map/pallas_call | solution.py:732
  21.7 6.3 %collective-permute-done.3.refs_3_.refs_1_ = bf16[256,2048]{1,0:T(8,128)(2,1)} collective-permute-done((bf16[256,2048]{1,0:T(8,128)(2,1)}, bf16[256,2048]{1,0:T(8,128)(2,1)}, u32[]{:S(2)}, u32[]{:S(2)}) %collective-permute-start.3) | collective-permute-done | bytes 1048608 | tf_op jit(solution)/shard_map/ppermute | solution.py:476
  29.3 3.0 %collective-permute-done.2.refs_2_ = bf16[256,2048]{1,0:T(8,128)(2,1)} collective-permute-done((bf16[256,2048]{1,0:T(8,128)(2,1)}, bf16[256,2048]{1,0:T(8,128)(2,1)}, u32[]{:S(2)}, u32[]{:S(2)}) %collective-permute-start.2) | collective-permute-done | bytes 1048608 | tf_op jit(solution)/shard_map/ppermute | solution.py:476
  32.2 1.6 collective-permute-start.5
  33.9 1.5 collective-permute-start.10
  35.9 1.3 collective-permute-start.6
  41.9 2.4 shard_map.115
  46.4 5.1 %shard_map.117 = (bf16[512,2304]{1,0:T(8,128)(2,1)}, bf16[512,1792]{1,0:T(8,128)(2,1)}) custom-call(s32[16]{0:T(128)} %get-tuple-element.217.order_ref, bf16[512,2048]{1,0:T(8,128)(2,1)} %own_ref.1, bf16[512,2048]{1,0:T(8,128)(2,1)} %collective-permute-done.4.refs_1_.other_ref), custom_call_target="tpu_custom_call" | custom-call | bytes 8388608 | tf_op jit(solution)/shard_map/pallas_call | solution.py:926
  51.5 2.3 fusion.6
  53.8 2.3 fusion.7
  56.1 14.8 %collective-permute-done.9.got_ref = bf16[144,2048]{1,0:T(8,128)(2,1)} collective-permute-done((bf16[144,2048]{1,0:T(8,128)(2,1)}, bf16[144,2048]{1,0:T(8,128)(2,1)}, u32[]{:S(2)}, u32[]{:S(2)}) %collective-permute-start.9) | collective-permute-done | bytes 589856 | tf_op jit(solution)/shard_map/ppermute | solution.py:476
  70.9 2.7 %shard_map.116 = (f32[128,2048]{1,0:T(8,128)}, bf16[144,2048]{1,0:T(8,128)(2,1)}, f32[8,2048]{1,0:T(8,128)}, f32[8,2048]{1,0:T(8,128)}) custom-call(s32[1]{0:T(128)} %bitcast.20.place_ref, f32[8,2048]{1,0:T(8,128)} %get-tuple-element.109.log_ref, bf16[144,2048]{1,0:T(8,128)(2,1)} %get-tuple-element.110.mine_ref, ...), custom_call_target="tpu_custom_call" | custom-call | bytes 3670016 | tf_op jit(solution)/shard_map/pallas_call | solution.py:753
  73.6 3.0 %add.123.refs_6_ = bf16[256,2048]{1,0:T(8,128)(2,1)} add(bf16[256,2048]{1,0:T(8,128)(2,1)} %get-tuple-element.118, bf16[256,2048]{1,0:T(8,128)(2,1)} %get-tuple-element.119) | non-fusion elementwise | flops 524288 | bytes 3145728 | tf_op jit(solution)/shard_map/add | solution.py:940
  76.6 1.5 collective-permute-start.12
  78.7 3.5 %collective-permute-start.16 = (bf16[144,2048]{1,0:T(8,128)(2,1)S(1)}, bf16[144,2048]{1,0:T(8,128)(2,1)S(1)}, u32[]{:S(2)}, u32[]{:S(2)}) collective-permute-start(bf16[144,2048]{1,0:T(8,128)(2,1)S(1)} %copy-done.1), channel_id=1, source_target_pairs={{0,8},{2,10},{4,12},{6,14},{8,0},{10,2},{12,4},{14,6},{16,24},{18,... | collective-permute-start | bytes 1769480 | tf_op jit(solution)/shard_map/ppermute | solution.py:476
  82.2 1.3 collective-permute-start.11
  83.5 2.2 fusion.5
  85.8 10.7 %collective-permute-done.16.got_ref = bf16[144,2048]{1,0:T(8,128)(2,1)S(1)} collective-permute-done((bf16[144,2048]{1,0:T(8,128)(2,1)S(1)}, bf16[144,2048]{1,0:T(8,128)(2,1)S(1)}, u32[]{:S(2)}, u32[]{:S(2)}) %collective-permute-start.16) | collective-permute-done | bytes 589856 | tf_op jit(solution)/shard_map/ppermute | solution.py:476
  97.3 2.7 %shard_map.120 = (f32[128,2048]{1,0:T(8,128)}, bf16[144,2048]{1,0:T(8,128)(2,1)}, f32[8,2048]{1,0:T(8,128)}, f32[8,2048]{1,0:T(8,128)}) custom-call(s32[1]{0:T(128)} %bitcast.20.place_ref, f32[8,2048]{1,0:T(8,128)} %get-tuple-element.125.log_ref, bf16[144,2048]{1,0:T(8,128)(2,1)} %get-tuple-element.126.mine_ref, bf16[144,2048]{1,0:T(8,128)(2,1)} %copy-done.2, ...), custom_call_target="tpu_custom_call" | custom-call | bytes 3670016 | tf_op jit(solution)/shard_map/pallas_call | solution.py:753
  100.5 5.7 %collective-permute-done.11.refs_2_ = bf16[256,1024]{1,0:T(8,128)(2,1)} collective-permute-done((bf16[256,1024]{1,0:T(8,128)(2,1)}, bf16[256,1024]{1,0:T(8,128)(2,1)}, u32[]{:S(2)}, u32[]{:S(2)}) %collective-permute-start.11) | collective-permute-done | bytes 524320 | tf_op jit(solution)/shard_map/ppermute | solution.py:537
  106.2 2.2 add.125.refs_3_.refs_6_
  108.4 1.5 collective-permute-start.15
  110.4 2.3 fusion.4
  113.3 1.5 collective-permute-start.20
  114.8 1.4 slice.76
  116.2 10.2 %shard_map.122.refs_6_.part_ref = f32[512,2048]{1,0:T(8,128)} custom-call(bf16[512,2304]{1,0:T(8,128)(2,1)} %get-tuple-element.114.refs_9_.f_ref, bf16[256,2048]{1,0:T(8,128)(2,1)} %refs_0_.3, bf16[256,2048]{1,0:T(8,128)(2,1)} %collective-permute-done.3.refs_3_.refs_1_, bf16[256,2048]{1,0:T(8,128)(2,1)} %get-tuple-element.113.refs_2_, ...), custom_call_target="tpu_custom_call" | custom-call | flops 4831838208 | bytes 9437184 | tf_op jit(solution)/shard_map/pallas_call | solution.py:651
  126.4 1.5 collective-permute-start.14
  127.9 2.7 %shard_map.121 = (f32[128,2048]{1,0:T(8,128)}, bf16[144,2048]{1,0:T(8,128)(2,1)}, f32[8,2048]{1,0:T(8,128)}, f32[8,2048]{1,0:T(8,128)}) custom-call(s32[1]{0:T(128)} %bitcast.20.place_ref, f32[8,2048]{1,0:T(8,128)} %get-tuple-element.128.log_ref, bf16[144,2048]{1,0:T(8,128)(2,1)} %get-tuple-element.129.mine_ref, ...), custom_call_target="tpu_custom_call" | custom-call | bytes 3670016 | tf_op jit(solution)/shard_map/pallas_call | solution.py:753
  133.0 2.1 fusion.1
  135.1 2.7 %collective-permute-done.14 = bf16[256,1024]{1,0:T(8,128)(2,1)} collective-permute-done((bf16[256,1024]{1,0:T(8,128)(2,1)}, bf16[256,1024]{1,0:T(8,128)(2,1)}, u32[]{:S(2)}, u32[]{:S(2)}) %collective-permute-start.14) | collective-permute-done | bytes 524320 | tf_op jit(solution)/shard_map/ppermute | solution.py:537
  137.8 2.0 add.124.refs_0_
  140.9 1.5 collective-permute-start.21
  144.3 10.4 %shard_map.125.refs_4_ = bf16[2048,512]{1,0:T(8,128)(2,1)} custom-call(f32[32,512]{1,0:T(8,128)} %get-tuple-element.136.r_ref, f32[4,512,8]{2,1,0:T(8,128)} %get-tuple-element.137.rt_ref, bf16[512,2048]{1,0:T(8,128)(2,1)} %g_ref.11, bf16[512,128]{1,0:T(8,128)(2,1)} %b_ref.9, bf16[512,128]{1,0:T(8,128)(2,1)} %c_ref.11, ...), custom_call_target="tpu_custom_call" | custom-call | flops 2147483648 | bytes 6291456 | tf_op jit(solution)/shard_map/pallas_call | solution.py:1031
  154.7 6.5 %shard_map.126 = (bf16[512,1024]{1,0:T(8,128)(2,1)}, f32[2,128,1024]{2,1,0:T(8,128)}, bf16[128,1024]{1,0:T(8,128)(2,1)}) custom-call(bf16[512,1792]{1,0:T(8,128)(2,1)} %get-tuple-element.138.f_ref, f32[512,2048]{1,0:T(8,128)} %shard_map.122.refs_6_.part_ref, f32[4,512,8]{2,1,0:T(8,128)} %get-tuple-element.137.rt_ref, bf16[512,128]{1,0:T(8,128)(2,1)} %b_ref.9, ...), custom_call_target="tpu_custom_call" | custom-call | flops 1879048192 | bytes 3670016 | tf_op jit(solution)/shard_map/pallas_call | solution.py:671
  161.8 1.5 collective-permute-start.26
  163.3 1.5 collective-permute-start.27
  165.3 10.0 %shard_map.128 = (bf16[512,2048]{1,0:T(8,128)(2,1)}, bf16[512,2048]{1,0:T(8,128)(2,1)}) custom-call(s32[9]{0:T(128)} %bitcast.34, bf16[2048,512]{1,0:T(8,128)(2,1)} %get-tuple-element.142.g_ref, bf16[256,2048]{1,0:T(8,128)(2,1)} %refs_0_.3, bf16[256,2048]{1,0:T(8,128)(2,1)} %collective-permute-done.3.refs_3_.refs_1_, ...), custom_call_target="tpu_custom_call" | custom-call | flops 4831838208 | bytes 9437184 | tf_op jit(solution)/shard_map/pallas_call | solution.py:705
  175.3 7.0 %collective-permute-done.27.refs_3_.refs_2_.refs_5_ = bf16[256,1024]{1,0:T(8,128)(2,1)} collective-permute-done((bf16[256,1024]{1,0:T(8,128)(2,1)}, bf16[256,1024]{1,0:T(8,128)(2,1)}, u32[]{:S(2)}, u32[]{:S(2)}) %collective-permute-start.27) | collective-permute-done | bytes 524320 | tf_op jit(solution)/shard_map/ppermute | solution.py:476
  183.1 1.3 slice.68.order_ref
  184.4 6.5 %shard_map.131 = (bf16[512,1024]{1,0:T(8,128)(2,1)}, f32[2,128,1024]{2,1,0:T(8,128)}, bf16[128,1024]{1,0:T(8,128)(2,1)}) custom-call(bf16[512,1792]{1,0:T(8,128)(2,1)} %get-tuple-element.138.f_ref, f32[512,2048]{1,0:T(8,128)} %shard_map.122.refs_6_.part_ref, f32[4,512,8]{2,1,0:T(8,128)} %get-tuple-element.137.rt_ref, bf16[512,128]{1,0:T(8,128)(2,1)} %b_ref.9, ...), custom_call_target="tpu_custom_call" | custom-call | flops 1879048192 | bytes 3670016 | tf_op jit(solution)/shard_map/pallas_call | solution.py:671
  191.3 2.0 shard_map.130
  194.2 1.5 collective-permute-start.31
  195.7 8.9 %shard_map.133 = (bf16[512,2048]{1,0:T(8,128)(2,1)}, bf16[512,2048]{1,0:T(8,128)(2,1)}) custom-call(s32[7]{0:T(128)} %slice.68.order_ref, bf16[2048,512]{1,0:T(8,128)(2,1)} %get-tuple-element.142.g_ref, bf16[256,1024]{1,0:T(8,128)(2,1)} %collective-permute-done.23.refs_0_, ...), custom_call_target="tpu_custom_call", output_to_operand_aliasing={{0}: (16, {}), {1}: (17, {})} | custom-call | flops 3758096384 | bytes 7340032 | tf_op jit(solution)/shard_map/pallas_call | solution.py:705
  204.7 2.6 %shard_map.134 = (f32[128,1024]{1,0:T(8,128)}, bf16[128,1024]{1,0:T(8,128)(2,1)}, f32[128,1024]{1,0:T(8,128)}, bf16[128,1024]{1,0:T(8,128)(2,1)}) custom-call(f32[8,2048]{1,0:T(8,128)} %get-tuple-element.150.factor_ref.refs_0_, bf16[128,1024]{1,0:T(8,128)(2,1)} %get-tuple-element.160.refs_1_, bf16[128,1024]{1,0:T(8,128)(2,1)} %collective-permute-done.30.refs_2_, ...), custom_call_target="tpu_custom_call" | custom-call | bytes 2621440 | tf_op jit(solution)/shard_map/pallas_call | solution.py:798
  207.9 1.3 collective-permute-start.33
  209.2 8.8 %shard_map.137 = (f32[16,512]{1,0:T(8,128)}, f32[512,128]{1,0:T(8,128)}, f32[512,128]{1,0:T(8,128)}) custom-call(f32[32,512]{1,0:T(8,128)} %get-tuple-element.136.r_ref, f32[4,512,8]{2,1,0:T(8,128)} %get-tuple-element.137.rt_ref, bf16[512,2048]{1,0:T(8,128)(2,1)} %g_ref.11, bf16[512,1024]{1,0:T(8,128)(2,1)} %get-tuple-element.174.x_ref, ...), custom_call_target="tpu_custom_call" | custom-call | flops 1610612736 | bytes 3145728 | tf_op jit(solution)/shard_map/pallas_call | solution.py:851
  218.0 2.8 %shard_map.136 = (f32[128,1024]{1,0:T(8,128)}, bf16[128,1024]{1,0:T(8,128)(2,1)}, f32[128,1024]{1,0:T(8,128)}, bf16[128,1024]{1,0:T(8,128)(2,1)}) custom-call(f32[8,2048]{1,0:T(8,128)} %get-tuple-element.159.refs_3_.refs_0_, bf16[128,1024]{1,0:T(8,128)(2,1)} %get-tuple-element.167.refs_1_, bf16[128,1024]{1,0:T(8,128)(2,1)} %collective-permute-done.32.refs_2_, ...), custom_call_target="tpu_custom_call" | custom-call | bytes 2621440 | tf_op jit(solution)/shard_map/pallas_call | solution.py:798
  221.5 2.1 collective-permute-start.35
  223.6 9.0 %shard_map.140 = (f32[16,512]{1,0:T(8,128)}, f32[512,128]{1,0:T(8,128)}, f32[512,128]{1,0:T(8,128)}) custom-call(f32[32,512]{1,0:T(8,128)} %get-tuple-element.136.r_ref, f32[4,512,8]{2,1,0:T(8,128)} %get-tuple-element.137.rt_ref, bf16[512,2048]{1,0:T(8,128)(2,1)} %g_ref.11, bf16[512,1024]{1,0:T(8,128)(2,1)} %get-tuple-element.184.x_ref, ...), custom_call_target="tpu_custom_call" | custom-call | flops 1610612736 | bytes 3145728 | tf_op jit(solution)/shard_map/pallas_call | solution.py:851
  232.6 1.8 collective-permute-done.34.refs_2_
  234.4 1.9 collective-permute-done.35.refs_6_
  236.3 2.7 %shard_map.139 = (f32[128,1024]{1,0:T(8,128)}, bf16[128,1024]{1,0:T(8,128)(2,1)}, f32[128,1024]{1,0:T(8,128)}) custom-call(f32[8,2048]{1,0:T(8,128)} %get-tuple-element.158.refs_4_.refs_0_, bf16[128,1024]{1,0:T(8,128)(2,1)} %get-tuple-element.176.refs_1_, bf16[128,1024]{1,0:T(8,128)(2,1)} %collective-permute-done.34.refs_2_, ...), custom_call_target="tpu_custom_call" | custom-call | bytes 2621440 | tf_op jit(solution)/shard_map/pallas_call | solution.py:798
  239.3 1.6 convert_element_type.38
  240.9 4.4 %add_convert_fusion.refs_1_ = bf16[512,2048]{1,0:T(8,128)(2,1)} fusion(bf16[512,2048]{1,0:T(8,128)(2,1)} %get-tuple-element.188, bf16[512,2048]{1,0:T(8,128)(2,1)} %get-tuple-element.157), kind=kLoop, calls=%fused_computation | loop fusion | flops 4194304 | bytes 6291456 | tf_op jit(solution)/shard_map/convert_element_type | solution.py:1015
  245.4 5.5 %shard_map.143 = (f32[32,512]{1,0:T(8,128)}, f32[512,128]{1,0:T(8,128)}) custom-call(f32[4,512,8]{2,1,0:T(8,128)} %get-tuple-element.137.rt_ref, bf16[512,2048]{1,0:T(8,128)(2,1)} %g_ref.11, bf16[512,128]{1,0:T(8,128)(2,1)} %c_ref.11, f32[128,1024]{1,0:T(8,128)} %get-tuple-element.192.s_ref, f32[2,128,1024]{2,1,0:T(8,128)} %get-tuple-element.193.e_ref, ...), custom_call_target="tpu_custom_call" | custom-call | flops 268435456 | bytes 3145728 | tf_op jit(solution)/shard_map/pallas_call | solution.py:869
  251.2 2.1 shard_map.142.refs_0_
  253.2 5.5 %shard_map.145 = (f32[32,512]{1,0:T(8,128)}, f32[512,128]{1,0:T(8,128)}) custom-call(f32[4,512,8]{2,1,0:T(8,128)} %get-tuple-element.137.rt_ref, bf16[512,2048]{1,0:T(8,128)(2,1)} %g_ref.11, bf16[512,128]{1,0:T(8,128)(2,1)} %c_ref.11, f32[128,1024]{1,0:T(8,128)} %shard_map.144.s_ref, ...), custom_call_target="tpu_custom_call", output_to_operand_aliasing={{0}: (9, {})} | custom-call | flops 268435456 | bytes 3145728 | tf_op jit(solution)/shard_map/pallas_call | solution.py:869
  260.0 1.7 convert_add_fusion.1
  261.8 1.7 convert_add_fusion
  (79 shorter events, 21.9 us)
Async XLA Ops:
  0.6 20.5 %collective-permute-start.4 = (bf16[512,2048]{1,0:T(8,128)(2,1)}, bf16[512,2048]{1,0:T(8,128)(2,1)}, u32[]{:S(2)}, u32[]{:S(2)}) collective-permute-start(bf16[512,2048]{1,0:T(8,128)(2,1)} %own_ref.1), channel_id=1, source_target_pairs={{0,1},{1,0},{2,3},{3,2},{4,5},{5,4},{6,7},{7,6},{8,9},{9,8},{10,11... | collective-permute-start | bytes 6291464 | tf_op jit(solution)/shard_map/ppermute | solution.py:476
  1.1 26.9 %collective-permute-start.3 = (bf16[256,2048]{1,0:T(8,128)(2,1)}, bf16[256,2048]{1,0:T(8,128)(2,1)}, u32[]{:S(2)}, u32[]{:S(2)}) collective-permute-start(bf16[256,2048]{1,0:T(8,128)(2,1)} %refs_0_.3), channel_id=1, source_target_pairs={{0,2},{2,0},{4,6},{6,4},{8,10},{10,8},{12,14},{14,12},{16,18},{18,... | collective-permute-start | bytes 3145736 | tf_op jit(solution)/shard_map/ppermute | solution.py:476
  3.7 25.5 %collective-permute-start = (bf16[256,2048]{1,0:T(8,128)(2,1)}, bf16[256,2048]{1,0:T(8,128)(2,1)}, u32[]{:S(2)}, u32[]{:S(2)}) collective-permute-start(bf16[256,2048]{1,0:T(8,128)(2,1)} %refs_0_.3), channel_id=1, source_target_pairs={{0,8},{2,10},{4,12},{6,14},{8,0},{10,2},{12,4},{14,6},{16,24},{18,... | collective-permute-start | bytes 3145736 | tf_op jit(solution)/shard_map/ppermute | solution.py:476
  5.3 24.0 %collective-permute-start.1 = (bf16[256,2048]{1,0:T(8,128)(2,1)}, bf16[256,2048]{1,0:T(8,128)(2,1)}, u32[]{:S(2)}, u32[]{:S(2)}) collective-permute-start(bf16[256,2048]{1,0:T(8,128)(2,1)} %refs_0_.3), channel_id=1, source_target_pairs={{8,16},{10,18},{12,20},{14,22},{16,8},{18,10},{20,12},{22,14},{9,1... | collective-permute-start | bytes 3145736 | tf_op jit(solution)/shard_map/ppermute | solution.py:537
  7.0 25.3 %collective-permute-start.2 = (bf16[256,2048]{1,0:T(8,128)(2,1)}, bf16[256,2048]{1,0:T(8,128)(2,1)}, u32[]{:S(2)}, u32[]{:S(2)}) collective-permute-start(bf16[256,2048]{1,0:T(8,128)(2,1)} %refs_0_.3), channel_id=1, source_target_pairs={{0,4},{2,6},{4,0},{6,2},{8,12},{10,14},{12,8},{14,10},{16,20},{18,... | collective-permute-start | bytes 3145736 | tf_op jit(solution)/shard_map/ppermute | solution.py:476
  21.1 20.8 %collective-permute-start.8 = (bf16[144,2048]{1,0:T(8,128)(2,1)}, bf16[144,2048]{1,0:T(8,128)(2,1)}, u32[]{:S(2)}, u32[]{:S(2)}) collective-permute-start(bf16[144,2048]{1,0:T(8,128)(2,1)} %shard_map.113.refs_4_.mine_ref), channel_id=1, source_target_pairs={{0,2},{2,0},{4,6},{6,4},{8,10},{10,8},{12,14},{14,12},{16,18},{18,... | collective-permute-start | bytes 1769480 | tf_op jit(solution)/shard_map/ppermute | solution.py:476
  32.2 21.6 %collective-permute-start.5 = (bf16[256,2048]{1,0:T(8,128)(2,1)}, bf16[256,2048]{1,0:T(8,128)(2,1)}, u32[]{:S(2)}, u32[]{:S(2)}) collective-permute-start(bf16[256,2048]{1,0:T(8,128)(2,1)} %get-tuple-element.107.refs_3_), channel_id=1, source_target_pairs={{8,16},{10,18},{12,20},{14,22},{16,8},{18,10},{20,12},{22,14},{9,1... | collective-permute-start | bytes 3145736 | tf_op jit(solution)/shard_map/ppermute | solution.py:537
  33.9 39.7 %collective-permute-start.10 = (bf16[256,2048]{1,0:T(8,128)(2,1)}, bf16[256,2048]{1,0:T(8,128)(2,1)}, u32[]{:S(2)}, u32[]{:S(2)}) collective-permute-start(bf16[256,2048]{1,0:T(8,128)(2,1)} %get-tuple-element.107.refs_3_), channel_id=1, source_target_pairs={{0,4},{2,6},{4,0},{6,2},{8,12},{10,14},{12,8},{14,10},{16,20},{18,... | collective-permute-start | bytes 3145736 | tf_op jit(solution)/shard_map/ppermute | solution.py:476
  35.4 38.2 %collective-permute-start.7 = (bf16[256,2048]{1,0:T(8,128)(2,1)}, bf16[256,2048]{1,0:T(8,128)(2,1)}, u32[]{:S(2)}, u32[]{:S(2)}) collective-permute-start(bf16[256,2048]{1,0:T(8,128)(2,1)} %get-tuple-element.107.refs_3_), channel_id=1, source_target_pairs={{0,2},{2,0},{4,6},{6,4},{8,10},{10,8},{12,14},{14,12},{16,18},{18,... | collective-permute-start | bytes 3145736 | tf_op jit(solution)/shard_map/ppermute | solution.py:476
  35.9 37.7 %collective-permute-start.6 = (bf16[256,2048]{1,0:T(8,128)(2,1)}, bf16[256,2048]{1,0:T(8,128)(2,1)}, u32[]{:S(2)}, u32[]{:S(2)}) collective-permute-start(bf16[256,2048]{1,0:T(8,128)(2,1)} %get-tuple-element.106.refs_0_), channel_id=1, source_target_pairs={{8,0},{10,2},{12,4},{14,6},{16,24},{18,26},{20,28},{22,30},{9,1},{... | collective-permute-start | bytes 3145736 | tf_op jit(solution)/shard_map/ppermute | solution.py:537
  44.3 26.6 %collective-permute-start.9 = (bf16[144,2048]{1,0:T(8,128)(2,1)}, bf16[144,2048]{1,0:T(8,128)(2,1)}, u32[]{:S(2)}, u32[]{:S(2)}) collective-permute-start(bf16[144,2048]{1,0:T(8,128)(2,1)} %get-tuple-element.110.mine_ref), channel_id=1, source_target_pairs={{0,4},{2,6},{4,0},{6,2},{8,12},{10,14},{12,8},{14,10},{16,20},{18,... | collective-permute-start | bytes 1769480 | tf_op jit(solution)/shard_map/ppermute | solution.py:476
  73.6 5.1 %copy-start.1 = (bf16[144,2048]{1,0:T(8,128)(2,1)S(1)}, bf16[144,2048]{1,0:T(8,128)(2,1)}, u32[]{:S(2)}) copy-start(bf16[144,2048]{1,0:T(8,128)(2,1)} %get-tuple-element.126.mine_ref) | copy-start | bytes 1769476
  76.6 29.6 %collective-permute-start.12 = (bf16[256,2048]{1,0:T(8,128)(2,1)}, bf16[256,2048]{1,0:T(8,128)(2,1)}, u32[]{:S(2)}, u32[]{:S(2)}) collective-permute-start(bf16[256,2048]{1,0:T(8,128)(2,1)} %add.123.refs_6_), channel_id=1, source_target_pairs={{0,4},{2,6},{4,0},{6,2},{8,12},{10,14},{12,8},{14,10},{16,20},{18,... | collective-permute-start | bytes 3145736 | tf_op jit(solution)/shard_map/ppermute | solution.py:476
  78.2 28.1 %collective-permute-start.13 = (bf16[256,2048]{1,0:T(8,128)(2,1)}, bf16[256,2048]{1,0:T(8,128)(2,1)}, u32[]{:S(2)}, u32[]{:S(2)}) collective-permute-start(bf16[256,2048]{1,0:T(8,128)(2,1)} %add.123.refs_6_), channel_id=1, source_target_pairs={{0,2},{2,0},{4,6},{6,4},{8,10},{10,8},{12,14},{14,12},{16,18},{18,... | collective-permute-start | bytes 3145736 | tf_op jit(solution)/shard_map/ppermute | solution.py:476
  78.7 17.8 %collective-permute-start.16 = (bf16[144,2048]{1,0:T(8,128)(2,1)S(1)}, bf16[144,2048]{1,0:T(8,128)(2,1)S(1)}, u32[]{:S(2)}, u32[]{:S(2)}) collective-permute-start(bf16[144,2048]{1,0:T(8,128)(2,1)S(1)} %copy-done.1), channel_id=1, source_target_pairs={{0,8},{2,10},{4,12},{6,14},{8,0},{10,2},{12,4},{14,6},{16,24},{18,... | collective-permute-start | bytes 1769480 | tf_op jit(solution)/shard_map/ppermute | solution.py:476
  82.2 24.0 %collective-permute-start.11 = (bf16[256,1024]{1,0:T(8,128)(2,1)}, bf16[256,1024]{1,0:T(8,128)(2,1)}, u32[]{:S(2)}, u32[]{:S(2)}) collective-permute-start(bf16[256,1024]{1,0:T(8,128)(2,1)} %get-tuple-element.116.refs_0_), channel_id=1, source_target_pairs={{8,0},{10,2},{12,4},{14,6},{16,24},{18,26},{20,28},{22,30},{9,1},{... | collective-permute-start | bytes 1572872 | tf_op jit(solution)/shard_map/ppermute | solution.py:537
  96.5 0.9 copy-start.2
  100.0 26.4 %collective-permute-start.17 = (bf16[144,2048]{1,0:T(8,128)(2,1)}, bf16[144,2048]{1,0:T(8,128)(2,1)}, u32[]{:S(2)}, u32[]{:S(2)}) collective-permute-start(bf16[144,2048]{1,0:T(8,128)(2,1)} %get-tuple-element.129.mine_ref), channel_id=1, source_target_pairs={{0,16},{2,18},{4,20},{6,22},{8,24},{10,26},{12,28},{14,30},{16,0},... | collective-permute-start | bytes 1769480 | tf_op jit(solution)/shard_map/ppermute | solution.py:476
  108.4 22.1 %collective-permute-start.15 = (bf16[256,1024]{1,0:T(8,128)(2,1)}, bf16[256,1024]{1,0:T(8,128)(2,1)}, u32[]{:S(2)}, u32[]{:S(2)}) collective-permute-start(bf16[256,1024]{1,0:T(8,128)(2,1)} %add.125.refs_3_.refs_6_), channel_id=1, source_target_pairs={{0,2},{2,0},{4,6},{6,4},{8,10},{10,8},{12,14},{14,12},{16,18},{18,... | collective-permute-start | bytes 1572872 | tf_op jit(solution)/shard_map/ppermute | solution.py:476
  109.9 20.6 %collective-permute-start.18 = (bf16[256,1024]{1,0:T(8,128)(2,1)}, bf16[256,1024]{1,0:T(8,128)(2,1)}, u32[]{:S(2)}, u32[]{:S(2)}) collective-permute-start(bf16[256,1024]{1,0:T(8,128)(2,1)} %add.125.refs_3_.refs_6_), channel_id=1, source_target_pairs={{0,4},{2,6},{4,0},{6,2},{8,12},{10,14},{12,8},{14,10},{16,20},{18,... | collective-permute-start | bytes 1572872 | tf_op jit(solution)/shard_map/ppermute | solution.py:476
  112.7 18.0 %collective-permute-start.19 = (bf16[256,1024]{1,0:T(8,128)(2,1)}, bf16[256,1024]{1,0:T(8,128)(2,1)}, u32[]{:S(2)}, u32[]{:S(2)}) collective-permute-start(bf16[256,1024]{1,0:T(8,128)(2,1)} %get-tuple-element.203), channel_id=1, source_target_pairs={{0,2},{2,0},{4,6},{6,4},{8,10},{10,8},{12,14},{14,12},{16,18},{18,... | collective-permute-start | bytes 1572872 | tf_op jit(solution)/shard_map/ppermute | solution.py:476
  113.3 18.7 %collective-permute-start.20 = (bf16[256,1024]{1,0:T(8,128)(2,1)}, bf16[256,1024]{1,0:T(8,128)(2,1)}, u32[]{:S(2)}, u32[]{:S(2)}) collective-permute-start(bf16[256,1024]{1,0:T(8,128)(2,1)} %get-tuple-element.133), channel_id=1, source_target_pairs={{0,4},{2,6},{4,0},{6,2},{8,12},{10,14},{12,8},{14,10},{16,20},{18,... | collective-permute-start | bytes 1572872 | tf_op jit(solution)/shard_map/ppermute | solution.py:476
  126.4 11.4 %collective-permute-start.14 = (bf16[256,1024]{1,0:T(8,128)(2,1)}, bf16[256,1024]{1,0:T(8,128)(2,1)}, u32[]{:S(2)}, u32[]{:S(2)}) collective-permute-start(bf16[256,1024]{1,0:T(8,128)(2,1)} %get-tuple-element.121), channel_id=1, source_target_pairs={{8,0},{10,2},{12,4},{14,6},{16,24},{18,26},{20,28},{22,30},{9,1},{... | collective-permute-start | bytes 1572872 | tf_op jit(solution)/shard_map/ppermute | solution.py:537
  132.0 5.8 %copy-start = (bf16[256,1024]{1,0:T(8,128)(2,1)S(1)}, bf16[256,1024]{1,0:T(8,128)(2,1)}, u32[]{:S(2)}) copy-start(bf16[256,1024]{1,0:T(8,128)(2,1)} %get-tuple-element.121) | copy-start | bytes 1572868
  132.0 22.7 %collective-permute-start.23 = (bf16[256,1024]{1,0:T(8,128)(2,1)}, bf16[256,1024]{1,0:T(8,128)(2,1)}, u32[]{:S(2)}, u32[]{:S(2)}) collective-permute-start(bf16[256,1024]{1,0:T(8,128)(2,1)} %get-tuple-element.139), channel_id=1, source_target_pairs={{0,2},{2,0},{4,6},{6,4},{8,10},{10,8},{12,14},{14,12},{16,18},{18,... | collective-permute-start | bytes 1572872 | tf_op jit(solution)/shard_map/ppermute | solution.py:476
  132.5 22.2 %collective-permute-start.24 = (bf16[256,1024]{1,0:T(8,128)(2,1)}, bf16[256,1024]{1,0:T(8,128)(2,1)}, u32[]{:S(2)}, u32[]{:S(2)}) collective-permute-start(bf16[256,1024]{1,0:T(8,128)(2,1)} %get-tuple-element.140.refs_4_.refs_8_), channel_id=1, source_target_pairs={{0,4},{2,6},{4,0},{6,2},{8,12},{10,14},{12,8},{14,10},{16,20},{18,... | collective-permute-start | bytes 1572872 | tf_op jit(solution)/shard_map/ppermute | solution.py:476
  140.9 20.3 %collective-permute-start.21 = (bf16[256,1024]{1,0:T(8,128)(2,1)}, bf16[256,1024]{1,0:T(8,128)(2,1)}, u32[]{:S(2)}, u32[]{:S(2)}) collective-permute-start(bf16[256,1024]{1,0:T(8,128)(2,1)} %shard_map.124.refs_3_.refs_7_), channel_id=1, source_target_pairs={{0,2},{2,0},{4,6},{6,4},{8,10},{10,8},{12,14},{14,12},{16,18},{18,... | collective-permute-start | bytes 1572872 | tf_op jit(solution)/shard_map/ppermute | solution.py:476
  142.4 18.8 %collective-permute-start.22 = (bf16[256,1024]{1,0:T(8,128)(2,1)}, bf16[256,1024]{1,0:T(8,128)(2,1)}, u32[]{:S(2)}, u32[]{:S(2)}) collective-permute-start(bf16[256,1024]{1,0:T(8,128)(2,1)} %shard_map.124.refs_3_.refs_7_), channel_id=1, source_target_pairs={{0,4},{2,6},{4,0},{6,2},{8,12},{10,14},{12,8},{14,10},{16,20},{18,... | collective-permute-start | bytes 1572872 | tf_op jit(solution)/shard_map/ppermute | solution.py:476
  161.2 14.1 %collective-permute-start.25 = (bf16[256,1024]{1,0:T(8,128)(2,1)}, bf16[256,1024]{1,0:T(8,128)(2,1)}, u32[]{:S(2)}, u32[]{:S(2)}) collective-permute-start(bf16[256,1024]{1,0:T(8,128)(2,1)} %get-tuple-element.143), channel_id=1, source_target_pairs={{0,2},{2,0},{4,6},{6,4},{8,10},{10,8},{12,14},{14,12},{16,18},{18,... | collective-permute-start | bytes 1572872 | tf_op jit(solution)/shard_map/ppermute | solution.py:476
  161.8 13.5 %collective-permute-start.26 = (bf16[256,1024]{1,0:T(8,128)(2,1)}, bf16[256,1024]{1,0:T(8,128)(2,1)}, u32[]{:S(2)}, u32[]{:S(2)}) collective-permute-start(bf16[256,1024]{1,0:T(8,128)(2,1)} %get-tuple-element.144.refs_4_.refs_9_), channel_id=1, source_target_pairs={{0,4},{2,6},{4,0},{6,2},{8,12},{10,14},{12,8},{14,10},{16,20},{18,... | collective-permute-start | bytes 1572872 | tf_op jit(solution)/shard_map/ppermute | solution.py:476
  163.3 19.0 %collective-permute-start.27 = (bf16[256,1024]{1,0:T(8,128)(2,1)}, bf16[256,1024]{1,0:T(8,128)(2,1)}, u32[]{:S(2)}, u32[]{:S(2)}) collective-permute-start(bf16[256,1024]{1,0:T(8,128)(2,1)} %get-tuple-element.145), channel_id=1, source_target_pairs={{0,2},{2,0},{4,6},{6,4},{8,10},{10,8},{12,14},{14,12},{16,18},{18,... | collective-permute-start | bytes 1572872 | tf_op jit(solution)/shard_map/ppermute | solution.py:476
  164.8 17.5 %collective-permute-start.28 = (bf16[256,1024]{1,0:T(8,128)(2,1)}, bf16[256,1024]{1,0:T(8,128)(2,1)}, u32[]{:S(2)}, u32[]{:S(2)}) collective-permute-start(bf16[256,1024]{1,0:T(8,128)(2,1)} %get-tuple-element.146), channel_id=1, source_target_pairs={{0,4},{2,6},{4,0},{6,2},{8,12},{10,14},{12,8},{14,10},{16,20},{18,... | collective-permute-start | bytes 1572872 | tf_op jit(solution)/shard_map/ppermute | solution.py:476
  182.3 9.0 %collective-permute-start.29 = (bf16[128,1024]{1,0:T(8,128)(2,1)}, bf16[128,1024]{1,0:T(8,128)(2,1)}, u32[]{:S(2)}, u32[]{:S(2)}) collective-permute-start(bf16[128,1024]{1,0:T(8,128)(2,1)} %get-tuple-element.151.mine_ref), channel_id=1, source_target_pairs={{0,2},{2,0},{4,6},{6,4},{8,10},{10,8},{12,14},{14,12},{16,18},{18,... | collective-permute-start | bytes 786440 | tf_op jit(solution)/shard_map/ppermute | solution.py:476
  193.3 11.4 %collective-permute-start.30 = (bf16[128,1024]{1,0:T(8,128)(2,1)}, bf16[128,1024]{1,0:T(8,128)(2,1)}, u32[]{:S(2)}, u32[]{:S(2)}) collective-permute-start(bf16[128,1024]{1,0:T(8,128)(2,1)} %get-tuple-element.160.refs_1_), channel_id=1, source_target_pairs={{0,2},{2,0},{4,6},{6,4},{8,10},{10,8},{12,14},{14,12},{16,18},{18,... | collective-permute-start | bytes 786440 | tf_op jit(solution)/shard_map/ppermute | solution.py:476
  194.2 10.5 %collective-permute-start.31 = (bf16[128,1024]{1,0:T(8,128)(2,1)}, bf16[128,1024]{1,0:T(8,128)(2,1)}, u32[]{:S(2)}, u32[]{:S(2)}) collective-permute-start(bf16[128,1024]{1,0:T(8,128)(2,1)} %get-tuple-element.161.refs_4_), channel_id=1, source_target_pairs={{0,4},{2,6},{4,0},{6,2},{8,12},{10,14},{12,8},{14,10},{16,20},{18,... | collective-permute-start | bytes 786440 | tf_op jit(solution)/shard_map/ppermute | solution.py:476
  207.3 31.6 %collective-permute-start.36 = (bf16[512,2048]{1,0:T(8,128)(2,1)}, bf16[512,2048]{1,0:T(8,128)(2,1)}, u32[]{:S(2)}, u32[]{:S(2)}) collective-permute-start(bf16[512,2048]{1,0:T(8,128)(2,1)} %get-tuple-element.183), channel_id=1, source_target_pairs={{0,1},{1,0},{2,3},{3,2},{4,5},{5,4},{6,7},{7,6},{8,9},{9,8},{10,11... | collective-permute-start | bytes 6291464 | tf_op jit(solution)/shard_map/ppermute | solution.py:476
  207.3 10.7 %collective-permute-start.32 = (bf16[128,1024]{1,0:T(8,128)(2,1)}, bf16[128,1024]{1,0:T(8,128)(2,1)}, u32[]{:S(2)}, u32[]{:S(2)}) collective-permute-start(bf16[128,1024]{1,0:T(8,128)(2,1)} %get-tuple-element.167.refs_1_), channel_id=1, source_target_pairs={{0,4},{2,6},{4,0},{6,2},{8,12},{10,14},{12,8},{14,10},{16,20},{18,... | collective-permute-start | bytes 786440 | tf_op jit(solution)/shard_map/ppermute | solution.py:476
  207.9 10.1 %collective-permute-start.33 = (bf16[128,1024]{1,0:T(8,128)(2,1)}, bf16[128,1024]{1,0:T(8,128)(2,1)}, u32[]{:S(2)}, u32[]{:S(2)}) collective-permute-start(bf16[128,1024]{1,0:T(8,128)(2,1)} %get-tuple-element.169.refs_5_), channel_id=1, source_target_pairs={{0,8},{2,10},{4,12},{6,14},{8,0},{10,2},{12,4},{14,6},{16,24},{18,... | collective-permute-start | bytes 786440 | tf_op jit(solution)/shard_map/ppermute | solution.py:476
  220.8 13.6 %collective-permute-start.34 = (bf16[128,1024]{1,0:T(8,128)(2,1)}, bf16[128,1024]{1,0:T(8,128)(2,1)}, u32[]{:S(2)}, u32[]{:S(2)}) collective-permute-start(bf16[128,1024]{1,0:T(8,128)(2,1)} %get-tuple-element.176.refs_1_), channel_id=1, source_target_pairs={{0,8},{2,10},{4,12},{6,14},{8,0},{10,2},{12,4},{14,6},{16,24},{18,... | collective-permute-start | bytes 786440 | tf_op jit(solution)/shard_map/ppermute | solution.py:476
  221.5 14.7 %collective-permute-start.35 = (bf16[128,1024]{1,0:T(8,128)(2,1)}, bf16[128,1024]{1,0:T(8,128)(2,1)}, u32[]{:S(2)}, u32[]{:S(2)}) collective-permute-start(bf16[128,1024]{1,0:T(8,128)(2,1)} %get-tuple-element.179.refs_5_), channel_id=1, source_target_pairs={{0,16},{2,18},{4,20},{6,22},{8,24},{10,26},{12,28},{14,30},{16,0},... | collective-permute-start | bytes 786440 | tf_op jit(solution)/shard_map/ppermute | solution.py:476
  239.0 12.2 %collective-permute-start.38 = (bf16[128,1024]{1,0:T(8,128)(2,1)}, bf16[128,1024]{1,0:T(8,128)(2,1)}, u32[]{:S(2)}, u32[]{:S(2)}) collective-permute-start(bf16[128,1024]{1,0:T(8,128)(2,1)} %get-tuple-element.190.mine_ref), channel_id=1, source_target_pairs={{0,16},{2,18},{4,20},{6,22},{8,24},{10,26},{12,28},{14,30},{16,0},... | collective-permute-start | bytes 786440 | tf_op jit(solution)/shard_map/ppermute | solution.py:476
  240.9 19.1 %collective-permute-start.37 = (bf16[512,128]{1,0:T(8,128)(2,1)}, bf16[512,128]{1,0:T(8,128)(2,1)}, u32[]{:S(2)}, u32[]{:S(2)}) collective-permute-start(bf16[512,128]{1,0:T(8,128)(2,1)} %convert_element_type.38), channel_id=1, source_target_pairs={{0,1},{1,0},{2,3},{3,2},{4,5},{5,4},{6,7},{7,6},{8,9},{9,8},{10,11... | collective-permute-start | bytes 393224 | tf_op jit(solution)/shard_map/ppermute | solution.py:476
  259.7 2.1 collective-permute-start.39

commit v13 on v12

--- a/solution.py
+++ b/solution.py
@@ -96,8 +96,10 @@
     columns = rt_ref[0]
     top_keep = iota((HALF, SPAN), 1) >= iota((HALF, SPAN), 0)
     low_keep = iota((HALF, HALF), 1) >= iota((HALF, HALF), 0)
-    to_end = jnp.exp2(spread_columns(columns[SPAN - 1 : SPAN] - columns))
-    from_state = mm(b, q_ref[0]) * to_end
+    from_state = None
+    if q_ref is not None:
+        to_end = jnp.exp2(spread_columns(columns[SPAN - 1 : SPAN] - columns))
+        from_state = mm(b, q_ref[0]) * to_end
     for pair in range(GROUP // 2):
         lanes = slice(pair * 2 * P_SIZE, (pair + 1) * 2 * P_SIZE)
         g = g_ref[:, lanes]
@@ -112,9 +114,11 @@
         product = mm(jnp.concatenate(parts, axis=0), g)
         parts = [product[:SPAN], product[SPAN:]]
         inner = jnp.where(first_head(), parts[0], parts[1])
-        total = inner + skip_ref[:, lanes] * g.astype(F32) + from_state[:, lanes]
+        total = inner + skip_ref[:, lanes] * g.astype(F32)
+        if from_state is not None:
+            total = total + from_state[:, lanes]
         if transposed:
-            out_ref[lanes, :] = total.T.astype(BF16)
+            out_ref[lanes, :] = total.T.astype(out_ref.dtype)
         else:
             out_ref[:, lanes] = total.astype(BF16)
 
@@ -232,6 +236,17 @@
         refs[1][...] = total.astype(BF16)
     passed = factors[2:3] * got
     refs[0][...] = passed if entering_ref is None else entering_ref[...] + passed
+
+
+def inner_rows_kernel(r_ref, rt_ref, g_ref, b_ref, c_ref, skip_ref, out_ref):
+    grad_x_kernel(True, r_ref, rt_ref, g_ref, b_ref, c_ref, None, skip_ref, out_ref)
+
+
+def state_rows_kernel(rt_ref, b_ref, q_ref, part_ref, out_ref):
+    columns = rt_ref[0]
+    to_end = jnp.exp2(spread_columns(columns[SPAN - 1 : SPAN] - columns))
+    from_state = mm(b_ref[...], q_ref[0]) * to_end
+    out_ref[...] = (part_ref[...] + from_state.T).astype(BF16)
 
 
 def scan_pair_kernel(number, last, *refs):
@@ -940,11 +955,14 @@
     z3 = inner2 + outer2
     x3, y3 = swap_x(z3), swap_y(z3)
     outer3_a = along_z(inner3_a, OUTWARD)
+    skip = jnp.repeat(skip_gain, P_SIZE)[None]
+    (running,) = after([running], z3)
+    rows_part = inner_rows(running, running_t, grad_out, b_rows, c_rows, skip)
     x1_a, x1_b = x1[:, :half], x1[:, half:]
     leaving, sent, log, factors_4 = back_step(spot, log, sent, (leaving,), 4)
 
     inner3_a, inner3_b, outer3_a, y3, x1_a, x1_b = after(
-        [inner3_a, inner3_b, outer3_a, y3, x1_a, x1_b], x3
+        [inner3_a, inner3_b, outer3_a, y3, x1_a, x1_b], x3, rows_part
     )
     z2a = inner3_a + outer3_a
     outer3_b = along_z(inner3_b, OUTWARD)
@@ -963,8 +981,7 @@
     leaving_all = jnp.stack([value.astype(BF16) for value in leaving_all])
     (z2b,) = after([inner3_b + outer3_b], leaving_all)
     x2b, y2b = swap_x(z2b), swap_y(z2b)
-    skip = jnp.repeat(skip_gain, P_SIZE)[None]
-    grad_x = grad_rows(running, running_t, grad_out, b_rows, c_rows, leaving_all, skip, True)
+    grad_x = state_rows(running_t, b_rows, leaving_all, rows_part)
     order_away = (order + (1 - place) * (blocks // 2)) % blocks
     early_order, late_order = order_away[: len(EARLY)], order_away[len(EARLY) :]
     late_a = [d0a, d1a, d3a, z2a, x2a, y2a, d2a]
@@ -1021,6 +1038,35 @@
     state_b = common + (entering_b, states_b, leaving_all, kept, decay_b, grad_c)
     decays, grad_c = state_terms(grid, here, half, state_b, heads, decays)
     return (grad_inputs, grad_b, head_sum(grad_c), decays)
+
+
+TURNED = pl.BlockSpec((WIDE, SPAN), lambda k, h: (h, k))
+
+
+def inner_rows(running, running_t, grad_out, b_rows, c_rows, skip):
+    length, columns = grad_out.shape
+    return call(
+        inner_rows_kernel,
+        (length // SPAN, running_t.shape[0]),
+        [run_spec(), run_t_spec(), rows_spec(), SHARED, SHARED, GAIN],
+        TURNED,
+        shape(columns, length),
+        8 * length * columns * SPAN,
+        6 * length * columns,
+    )(running, running_t, grad_out, b_rows, c_rows, skip)
+
+
+def state_rows(running_t, b_rows, leaving, part):
+    columns, length = part.shape
+    return call(
+        state_rows_kernel,
+        (length // SPAN, running_t.shape[0]),
+        [run_t_spec(), SHARED, state_spec(), TURNED],
+        TURNED,
+        shape(columns, length, dtype=BF16),
+        2 * length * columns * SPAN,
+        8 * length * columns,
+    )(running_t, b_rows, leaving, part)
 
 
 def grad_rows(running, running_t, grad_out, b_rows, c_rows, leaving, skip, transposed):

time: 265 us -> 272 us (1.026)
  Pallas kernels: 122 us -> 130 us
  starting transfers between devices: 42.9 us -> 46 us
    pallas_call x1 -> x2, Pallas kernels: 10.4 us -> 17.8 us  [the longest x1 9.28 us: inner_rows(): call(inner_rows_kernel, (length // SPAN, running_t.shape[0]), [run_spec()...]
    ppermute x35, starting transfers between devices: 35.6 us -> 38.7 us  [swap(): return lax.ppermute(value, axis, [(i, i ^ bit) for i in range(count)])]
  transfers between devices with their start and end apart: 40 -> 40, of which waited for: 14 -> 14; matrix products, arithmetic and copies ran while one was open for 12% -> 11% of each run, Pallas kernels for 44% -> 46%
where the time goes in v13:
time: 272 us; the launch traced here: 271 us
  Pallas kernels  130 us (48%)
  waiting for transfers between devices  55.3 us (20%)
  starting transfers between devices  46 us (17%)
  other arithmetic  21.9 us (8%)
  local copies, waits for them, and re-layouts  14.3 us (5%)
  between operations  3.44 us (1%)
    ppermute x35, waiting for transfers between devices, swap(): return lax.ppermute(value, axis, [(i, i ^ bit) for i in range(count)])  47.5 us
    ppermute x35, starting transfers between devices, swap(): return lax.ppermute(value, axis, [(i, i ^ bit) for i in range(count)])  38.7 us
    pallas_call x2, Pallas kernels, multiply_blocks(): pl.pallas_call(functools.partial(blocks_kernel, [len(piece) for piece in...  18.9 us
    pallas_call x2, Pallas kernels, inner(): call(inner_kernel, grid, specs + [SHARED] * len(so_far), [run_spec(), SHA...  18.1 us
    pallas_call x2, Pallas kernels, late_forward(): call(functools.partial(late_forward_kernel, len(pieces)), (columns // WID...  13 us
    pallas_call x2, Pallas kernels, state_terms(): pl.pallas_call(state_kernel, grid=grid, in_specs=[run_t_spec(here), rows_...  11 us
    pallas_call x4, Pallas kernels, back_step(): call(functools.partial(back_kernel, bit), (columns // (2 * WIDE),), [SCAL...  10.4 us
    pallas_call x1, Pallas kernels, early_forward(): call(functools.partial(early_forward_kernel, len(pieces)), (columns // WI...  10.3 us
  transfers between devices with their start and end apart: 40, of which 14 were waited for; matrix products, arithmetic and copies ran while one was open for 11% of the time, Pallas kernels for 46%

profile of v13, /device:TPU:0, one launch (start us, length us, event | category | flops | bytes accessed | tf_op | source)
XLA Modules:
  0.0 270.5 jit_solution(519456346587176573)
XLA Ops:
  1.1 2.6 collective-permute-start.3
  3.7 1.5 collective-permute-start.2
  5.2 1.6 collective-permute-start.1
  6.9 3.5 %collective-permute-start = (bf16[256,2048]{1,0:T(8,128)(2,1)}, bf16[256,2048]{1,0:T(8,128)(2,1)}, u32[]{:S(2)}, u32[]{:S(2)}) collective-permute-start(bf16[256,2048]{1,0:T(8,128)(2,1)} %refs_0_.3), channel_id=1, source_target_pairs={{0,8},{2,10},{4,12},{6,14},{8,0},{10,2},{12,4},{14,6},{16,24},{18,... | collective-permute-start | bytes 3145736 | tf_op jit(solution)/shard_map/ppermute | solution.py:491
  10.4 9.1 %shard_map.111 = (f32[32,512]{1,0:T(8,128)}, f32[4,512,8]{2,1,0:T(8,128)}, f32[2,8,2048]{2,1,0:T(8,128)}, f32[2,128,2048]{2,1,0:T(8,128)}) custom-call(f32[32,512]{1,0:T(8,128)} %d_ref.1, bf16[512,2048]{1,0:T(8,128)(2,1)} %g_ref.11, bf16[512,128]{1,0:T(8,128)(2,1)} %c_ref.11), custom_call_target="tpu_custom_call" | custom-call | flops 268435456 | bytes 6291456 | tf_op jit(solution)/shard_map/pallas_call | solution.py:838
  19.4 3.6 %shard_map.112 = (f32[8,2048]{1,0:T(8,128)}, bf16[144,2048]{1,0:T(8,128)(2,1)}) custom-call(f32[2,128,2048]{2,1,0:T(8,128)} %get-tuple-element.103.own_ref, f32[2,8,2048]{2,1,0:T(8,128)} %get-tuple-element.104.kept_ref.a_ref), custom_call_target="tpu_custom_call" | custom-call | bytes 3670016 | tf_op jit(solution)/shard_map/pallas_call | solution.py:747
  23.6 4.4 %collective-permute-done.3.refs_3_.refs_1_ = bf16[256,2048]{1,0:T(8,128)(2,1)} collective-permute-done((bf16[256,2048]{1,0:T(8,128)(2,1)}, bf16[256,2048]{1,0:T(8,128)(2,1)}, u32[]{:S(2)}, u32[]{:S(2)}) %collective-permute-start.3) | collective-permute-done | bytes 1048608 | tf_op jit(solution)/shard_map/ppermute | solution.py:491
  29.3 4.3 %collective-permute-done.refs_0_ = bf16[256,2048]{1,0:T(8,128)(2,1)} collective-permute-done((bf16[256,2048]{1,0:T(8,128)(2,1)}, bf16[256,2048]{1,0:T(8,128)(2,1)}, u32[]{:S(2)}, u32[]{:S(2)}) %collective-permute-start) | collective-permute-done | bytes 1048608 | tf_op jit(solution)/shard_map/ppermute | solution.py:491
  33.6 1.6 collective-permute-start.5
  42.2 2.4 shard_map.115
  44.6 1.6 collective-permute-start.9
  47.3 5.2 %shard_map.117 = (bf16[512,2304]{1,0:T(8,128)(2,1)}, bf16[512,1792]{1,0:T(8,128)(2,1)}) custom-call(s32[16]{0:T(128)} %get-tuple-element.217.order_ref, bf16[512,2048]{1,0:T(8,128)(2,1)} %own_ref.1, bf16[512,2048]{1,0:T(8,128)(2,1)} %collective-permute-done.4.refs_1_.other_ref), custom_call_target="tpu_custom_call" | custom-call | bytes 8388608 | tf_op jit(solution)/shard_map/pallas_call | solution.py:941
  52.5 2.2 fusion.6
  54.7 2.2 fusion.7
  57.0 16.7 %collective-permute-done.9.got_ref = bf16[144,2048]{1,0:T(8,128)(2,1)} collective-permute-done((bf16[144,2048]{1,0:T(8,128)(2,1)}, bf16[144,2048]{1,0:T(8,128)(2,1)}, u32[]{:S(2)}, u32[]{:S(2)}) %collective-permute-start.9) | collective-permute-done | bytes 589856 | tf_op jit(solution)/shard_map/ppermute | solution.py:491
  73.6 2.7 shard_map.116
  76.3 2.9 %add.123.refs_1_.refs_6_ = bf16[256,2048]{1,0:T(8,128)(2,1)} add(bf16[256,2048]{1,0:T(8,128)(2,1)} %get-tuple-element.118, bf16[256,2048]{1,0:T(8,128)(2,1)} %get-tuple-element.119) | non-fusion elementwise | flops 524288 | bytes 3145728 | tf_op jit(solution)/shard_map/add | solution.py:955
  80.3 3.3 %collective-permute-start.16 = (bf16[144,2048]{1,0:T(8,128)(2,1)}, bf16[144,2048]{1,0:T(8,128)(2,1)}, u32[]{:S(2)}, u32[]{:S(2)}) collective-permute-start(bf16[144,2048]{1,0:T(8,128)(2,1)} %get-tuple-element.128.mine_ref), channel_id=1, source_target_pairs={{0,8},{2,10},{4,12},{6,14},{8,0},{10,2},{12,4},{14,6},{16,24},{18,... | collective-permute-start | bytes 1769480 | tf_op jit(solution)/shard_map/ppermute | solution.py:491
  85.6 9.3 %shard_map.120.refs_7_.part_ref = f32[2048,512]{1,0:T(8,128)} custom-call(f32[32,512]{1,0:T(8,128)} %shard_map.119.r_ref, f32[4,512,8]{2,1,0:T(8,128)} %get-tuple-element.122.rt_ref, bf16[512,2048]{1,0:T(8,128)(2,1)} %g_ref.11, bf16[512,128]{1,0:T(8,128)(2,1)} %b_ref.11, bf16[512,128]{1,0:T(8,128)(2,1)} %c_ref.11, f32[1,2048]{1,0:T(1,128)} %broadcast_in_dim_reshape.3.skip_ref), custom_call_target="tpu_custom_call" | custom-call | flops 2147483648 | bytes 6291456 | tf_op jit(solution)/shard_map/pallas_call | solution.py:1048
  94.9 2.3 fusion.5
  98.1 2.7 shard_map.122
  100.8 3.2 %collective-permute-start.17 = (bf16[144,2048]{1,0:T(8,128)(2,1)}, bf16[144,2048]{1,0:T(8,128)(2,1)}, u32[]{:S(2)}, u32[]{:S(2)}) collective-permute-start(bf16[144,2048]{1,0:T(8,128)(2,1)} %get-tuple-element.131.mine_ref), channel_id=1, source_target_pairs={{0,16},{2,18},{4,20},{6,22},{8,24},{10,26},{12,28},{14,30},{16,0},... | collective-permute-start | bytes 1769480 | tf_op jit(solution)/shard_map/ppermute | solution.py:491
  104.0 3.5 %collective-permute-done.11.refs_2_ = bf16[256,1024]{1,0:T(8,128)(2,1)} collective-permute-done((bf16[256,1024]{1,0:T(8,128)(2,1)}, bf16[256,1024]{1,0:T(8,128)(2,1)}, u32[]{:S(2)}, u32[]{:S(2)}) %collective-permute-start.11) | collective-permute-done | bytes 524320 | tf_op jit(solution)/shard_map/ppermute | solution.py:552
  107.5 2.2 add.125.refs_3_.refs_6_
  109.8 1.5 collective-permute-start.18
  111.3 1.5 collective-permute-start.15
  113.3 2.3 fusion.4
  116.1 1.4 slice.76
  117.5 10.3 %shard_map.124.refs_6_.part_ref = f32[512,2048]{1,0:T(8,128)} custom-call(bf16[512,2304]{1,0:T(8,128)(2,1)} %get-tuple-element.114.refs_9_.f_ref, bf16[256,2048]{1,0:T(8,128)(2,1)} %refs_0_.3, bf16[256,2048]{1,0:T(8,128)(2,1)} %collective-permute-done.3.refs_3_.refs_1_, bf16[256,2048]{1,0:T(8,128)(2,1)} %get-tuple-element.113.refs_2_, ...), custom_call_target="tpu_custom_call" | custom-call | flops 4831838208 | bytes 9437184 | tf_op jit(solution)/shard_map/pallas_call | solution.py:666
  127.8 1.5 collective-permute-start.14
  129.3 2.7 shard_map.123
  133.4 1.5 collective-permute-start.23
  135.1 2.1 fusion.1
  137.2 4.2 %collective-permute-done.14 = bf16[256,1024]{1,0:T(8,128)(2,1)} collective-permute-done((bf16[256,1024]{1,0:T(8,128)(2,1)}, bf16[256,1024]{1,0:T(8,128)(2,1)}, u32[]{:S(2)}, u32[]{:S(2)}) %collective-permute-start.14) | collective-permute-done | bytes 524320 | tf_op jit(solution)/shard_map/ppermute | solution.py:552
  141.4 2.0 add.124.refs_0_
  144.5 1.5 collective-permute-start.22
  146.1 1.5 collective-permute-start.21
  147.5 8.5 %shard_map.127.refs_4_ = bf16[2048,512]{1,0:T(8,128)(2,1)} custom-call(f32[4,512,8]{2,1,0:T(8,128)} %get-tuple-element.122.rt_ref, bf16[512,128]{1,0:T(8,128)(2,1)} %b_ref.11, bf16[2,128,2048]{2,1,0:T(8,128)(2,1)} %pad_maximum_fusion.refs_1_.q_ref, f32[2048,512]{1,0:T(8,128)} %shard_map.120.refs_7_.part_ref), custom_call_target="tpu_custom_call" | custom-call | flops 536870912 | bytes 8388608 | tf_op jit(solution)/shard_map/pallas_call | solution.py:1061
  156.1 6.5 %shard_map.128 = (bf16[512,1024]{1,0:T(8,128)(2,1)}, f32[2,128,1024]{2,1,0:T(8,128)}, bf16[128,1024]{1,0:T(8,128)(2,1)}) custom-call(bf16[512,1792]{1,0:T(8,128)(2,1)} %get-tuple-element.138.f_ref, f32[512,2048]{1,0:T(8,128)} %shard_map.124.refs_6_.part_ref, f32[4,512,8]{2,1,0:T(8,128)} %get-tuple-element.122.rt_ref, bf16[512,128]{1,0:T(8,128)(2,1)} %b_ref.11, ...), custom_call_target="tpu_custom_call" | custom-call | flops 1879048192 | bytes 3670016 | tf_op jit(solution)/shard_map/pallas_call | solution.py:686
  163.2 1.5 collective-permute-start.27
  165.2 1.5 collective-permute-start.26
  166.7 10.0 %shard_map.130 = (bf16[512,2048]{1,0:T(8,128)(2,1)}, bf16[512,2048]{1,0:T(8,128)(2,1)}) custom-call(s32[9]{0:T(128)} %bitcast.34, bf16[2048,512]{1,0:T(8,128)(2,1)} %get-tuple-element.142.g_ref, bf16[256,2048]{1,0:T(8,128)(2,1)} %refs_0_.3, bf16[256,2048]{1,0:T(8,128)(2,1)} %collective-permute-done.3.refs_3_.refs_1_, ...), custom_call_target="tpu_custom_call" | custom-call | flops 4831838208 | bytes 9437184 | tf_op jit(solution)/shard_map/pallas_call | solution.py:720
  177.8 7.2 %collective-permute-done.27.refs_3_.refs_2_.refs_5_ = bf16[256,1024]{1,0:T(8,128)(2,1)} collective-permute-done((bf16[256,1024]{1,0:T(8,128)(2,1)}, bf16[256,1024]{1,0:T(8,128)(2,1)}, u32[]{:S(2)}, u32[]{:S(2)}) %collective-permute-start.27) | collective-permute-done | bytes 524320 | tf_op jit(solution)/shard_map/ppermute | solution.py:491
  187.3 6.5 %shard_map.133 = (bf16[512,1024]{1,0:T(8,128)(2,1)}, f32[2,128,1024]{2,1,0:T(8,128)}, bf16[128,1024]{1,0:T(8,128)(2,1)}) custom-call(bf16[512,1792]{1,0:T(8,128)(2,1)} %get-tuple-element.138.f_ref, f32[512,2048]{1,0:T(8,128)} %shard_map.124.refs_6_.part_ref, f32[4,512,8]{2,1,0:T(8,128)} %get-tuple-element.122.rt_ref, bf16[512,128]{1,0:T(8,128)(2,1)} %b_ref.11, ...), custom_call_target="tpu_custom_call" | custom-call | flops 1879048192 | bytes 3670016 | tf_op jit(solution)/shard_map/pallas_call | solution.py:686
  193.8 2.0 shard_map.132
  195.8 1.5 collective-permute-start.30
  197.8 8.9 %shard_map.135 = (bf16[512,2048]{1,0:T(8,128)(2,1)}, bf16[512,2048]{1,0:T(8,128)(2,1)}) custom-call(s32[7]{0:T(128)} %slice.68.order_ref, bf16[2048,512]{1,0:T(8,128)(2,1)} %get-tuple-element.142.g_ref, bf16[256,1024]{1,0:T(8,128)(2,1)} %collective-permute-done.23.refs_0_, ...), custom_call_target="tpu_custom_call", output_to_operand_aliasing={{0}: (16, {}), {1}: (17, {})} | custom-call | flops 3758096384 | bytes 7340032 | tf_op jit(solution)/shard_map/pallas_call | solution.py:720
  206.8 2.7 shard_map.136
  209.4 1.6 collective-permute-start.32
  211.0 9.0 %shard_map.139 = (f32[16,512]{1,0:T(8,128)}, f32[512,128]{1,0:T(8,128)}, f32[512,128]{1,0:T(8,128)}) custom-call(f32[32,512]{1,0:T(8,128)} %shard_map.119.r_ref, f32[4,512,8]{2,1,0:T(8,128)} %get-tuple-element.122.rt_ref, bf16[512,2048]{1,0:T(8,128)(2,1)} %g_ref.11, bf16[512,1024]{1,0:T(8,128)(2,1)} %get-tuple-element.174.x_ref, bf16[512,128]{1,0:T(8,128)(2,1)} %b_ref.11, ...), custom_call_target="tpu_custom_call" | custom-call | flops 1610612736 | bytes 3145728 | tf_op jit(solution)/shard_map/pallas_call | solution.py:866
  220.1 2.8 %shard_map.138 = (f32[128,1024]{1,0:T(8,128)}, bf16[128,1024]{1,0:T(8,128)(2,1)}, f32[128,1024]{1,0:T(8,128)}, bf16[128,1024]{1,0:T(8,128)(2,1)}) custom-call(f32[8,2048]{1,0:T(8,128)} %get-tuple-element.159.refs_3_.refs_0_, bf16[128,1024]{1,0:T(8,128)(2,1)} %get-tuple-element.167.refs_1_, bf16[128,1024]{1,0:T(8,128)(2,1)} %collective-permute-done.32.refs_2_, ...), custom_call_target="tpu_custom_call" | custom-call | bytes 2621440 | tf_op jit(solution)/shard_map/pallas_call | solution.py:813
  222.9 1.8 collective-permute-start.34
  225.2 9.0 %shard_map.142 = (f32[16,512]{1,0:T(8,128)}, f32[512,128]{1,0:T(8,128)}, f32[512,128]{1,0:T(8,128)}) custom-call(f32[32,512]{1,0:T(8,128)} %shard_map.119.r_ref, f32[4,512,8]{2,1,0:T(8,128)} %get-tuple-element.122.rt_ref, bf16[512,2048]{1,0:T(8,128)(2,1)} %g_ref.11, bf16[512,1024]{1,0:T(8,128)(2,1)} %get-tuple-element.184.x_ref, bf16[512,128]{1,0:T(8,128)(2,1)} %b_ref.11, ...), custom_call_target="tpu_custom_call" | custom-call | flops 1610612736 | bytes 3145728 | tf_op jit(solution)/shard_map/pallas_call | solution.py:866
  234.2 2.1 collective-permute-done.34.refs_2_
  236.3 3.0 %collective-permute-done.35.refs_6_ = bf16[128,1024]{1,0:T(8,128)(2,1)} collective-permute-done((bf16[128,1024]{1,0:T(8,128)(2,1)}, bf16[128,1024]{1,0:T(8,128)(2,1)}, u32[]{:S(2)}, u32[]{:S(2)}) %collective-permute-start.35) | collective-permute-done | bytes 262176 | tf_op jit(solution)/shard_map/ppermute | solution.py:491
  239.3 2.7 shard_map.141
  242.0 1.6 convert_element_type.38
  244.0 4.4 %add_convert_fusion.refs_1_ = bf16[512,2048]{1,0:T(8,128)(2,1)} fusion(bf16[512,2048]{1,0:T(8,128)(2,1)} %get-tuple-element.188, bf16[512,2048]{1,0:T(8,128)(2,1)} %get-tuple-element.157), kind=kLoop, calls=%fused_computation | loop fusion | flops 4194304 | bytes 6291456 | tf_op jit(solution)/shard_map/convert_element_type | solution.py:1032
  248.4 5.5 %shard_map.145 = (f32[32,512]{1,0:T(8,128)}, f32[512,128]{1,0:T(8,128)}) custom-call(f32[4,512,8]{2,1,0:T(8,128)} %get-tuple-element.122.rt_ref, bf16[512,2048]{1,0:T(8,128)(2,1)} %g_ref.11, bf16[512,128]{1,0:T(8,128)(2,1)} %c_ref.11, f32[128,1024]{1,0:T(8,128)} %get-tuple-element.192.s_ref, f32[2,128,1024]{2,1,0:T(8,128)} %get-tuple-element.193.e_ref, ...), custom_call_target="tpu_custom_call" | custom-call | flops 268435456 | bytes 3145728 | tf_op jit(solution)/shard_map/pallas_call | solution.py:884
  253.9 4.4 %collective-permute-done.38.got_ref = bf16[128,1024]{1,0:T(8,128)(2,1)} collective-permute-done((bf16[128,1024]{1,0:T(8,128)(2,1)}, bf16[128,1024]{1,0:T(8,128)(2,1)}, u32[]{:S(2)}, u32[]{:S(2)}) %collective-permute-start.38) | collective-permute-done | bytes 262176 | tf_op jit(solution)/shard_map/ppermute | solution.py:491
  258.3 2.1 shard_map.144.refs_0_
  260.4 5.5 %shard_map.147 = (f32[32,512]{1,0:T(8,128)}, f32[512,128]{1,0:T(8,128)}) custom-call(f32[4,512,8]{2,1,0:T(8,128)} %get-tuple-element.122.rt_ref, bf16[512,2048]{1,0:T(8,128)(2,1)} %g_ref.11, bf16[512,128]{1,0:T(8,128)(2,1)} %c_ref.11, f32[128,1024]{1,0:T(8,128)} %shard_map.146.s_ref, ...), custom_call_target="tpu_custom_call", output_to_operand_aliasing={{0}: (9, {})} | custom-call | flops 268435456 | bytes 3145728 | tf_op jit(solution)/shard_map/pallas_call | solution.py:884
  267.1 1.7 convert_add_fusion.1
  268.8 1.7 convert_add_fusion
  (79 shorter events, 22.6 us)
Async XLA Ops:
  0.6 22.4 %collective-permute-start.4 = (bf16[512,2048]{1,0:T(8,128)(2,1)}, bf16[512,2048]{1,0:T(8,128)(2,1)}, u32[]{:S(2)}, u32[]{:S(2)}) collective-permute-start(bf16[512,2048]{1,0:T(8,128)(2,1)} %own_ref.1), channel_id=1, source_target_pairs={{0,1},{1,0},{2,3},{3,2},{4,5},{5,4},{6,7},{7,6},{8,9},{9,8},{10,11... | collective-permute-start | bytes 6291464 | tf_op jit(solution)/shard_map/ppermute | solution.py:491
  1.1 26.9 %collective-permute-start.3 = (bf16[256,2048]{1,0:T(8,128)(2,1)}, bf16[256,2048]{1,0:T(8,128)(2,1)}, u32[]{:S(2)}, u32[]{:S(2)}) collective-permute-start(bf16[256,2048]{1,0:T(8,128)(2,1)} %refs_0_.3), channel_id=1, source_target_pairs={{0,2},{2,0},{4,6},{6,4},{8,10},{10,8},{12,14},{14,12},{16,18},{18,... | collective-permute-start | bytes 3145736 | tf_op jit(solution)/shard_map/ppermute | solution.py:491
  3.7 25.5 %collective-permute-start.2 = (bf16[256,2048]{1,0:T(8,128)(2,1)}, bf16[256,2048]{1,0:T(8,128)(2,1)}, u32[]{:S(2)}, u32[]{:S(2)}) collective-permute-start(bf16[256,2048]{1,0:T(8,128)(2,1)} %refs_0_.3), channel_id=1, source_target_pairs={{0,4},{2,6},{4,0},{6,2},{8,12},{10,14},{12,8},{14,10},{16,20},{18,... | collective-permute-start | bytes 3145736 | tf_op jit(solution)/shard_map/ppermute | solution.py:491
  5.2 24.0 %collective-permute-start.1 = (bf16[256,2048]{1,0:T(8,128)(2,1)}, bf16[256,2048]{1,0:T(8,128)(2,1)}, u32[]{:S(2)}, u32[]{:S(2)}) collective-permute-start(bf16[256,2048]{1,0:T(8,128)(2,1)} %refs_0_.3), channel_id=1, source_target_pairs={{8,16},{10,18},{12,20},{14,22},{16,8},{18,10},{20,12},{22,14},{9,1... | collective-permute-start | bytes 3145736 | tf_op jit(solution)/shard_map/ppermute | solution.py:552
  6.9 26.7 %collective-permute-start = (bf16[256,2048]{1,0:T(8,128)(2,1)}, bf16[256,2048]{1,0:T(8,128)(2,1)}, u32[]{:S(2)}, u32[]{:S(2)}) collective-permute-start(bf16[256,2048]{1,0:T(8,128)(2,1)} %refs_0_.3), channel_id=1, source_target_pairs={{0,8},{2,10},{4,12},{6,14},{8,0},{10,2},{12,4},{14,6},{16,24},{18,... | collective-permute-start | bytes 3145736 | tf_op jit(solution)/shard_map/ppermute | solution.py:491
  23.0 19.1 %collective-permute-start.8 = (bf16[144,2048]{1,0:T(8,128)(2,1)}, bf16[144,2048]{1,0:T(8,128)(2,1)}, u32[]{:S(2)}, u32[]{:S(2)}) collective-permute-start(bf16[144,2048]{1,0:T(8,128)(2,1)} %shard_map.113.refs_4_.mine_ref), channel_id=1, source_target_pairs={{0,2},{2,0},{4,6},{6,4},{8,10},{10,8},{12,14},{14,12},{16,18},{18,... | collective-permute-start | bytes 1769480 | tf_op jit(solution)/shard_map/ppermute | solution.py:491
  33.6 21.1 %collective-permute-start.5 = (bf16[256,2048]{1,0:T(8,128)(2,1)}, bf16[256,2048]{1,0:T(8,128)(2,1)}, u32[]{:S(2)}, u32[]{:S(2)}) collective-permute-start(bf16[256,2048]{1,0:T(8,128)(2,1)} %get-tuple-element.107.refs_3_), channel_id=1, source_target_pairs={{8,16},{10,18},{12,20},{14,22},{16,8},{18,10},{20,12},{22,14},{9,1... | collective-permute-start | bytes 3145736 | tf_op jit(solution)/shard_map/ppermute | solution.py:552
  35.2 41.0 %collective-permute-start.6 = (bf16[256,2048]{1,0:T(8,128)(2,1)}, bf16[256,2048]{1,0:T(8,128)(2,1)}, u32[]{:S(2)}, u32[]{:S(2)}) collective-permute-start(bf16[256,2048]{1,0:T(8,128)(2,1)} %get-tuple-element.106.refs_0_), channel_id=1, source_target_pairs={{8,0},{10,2},{12,4},{14,6},{16,24},{18,26},{20,28},{22,30},{9,1},{... | collective-permute-start | bytes 3145736 | tf_op jit(solution)/shard_map/ppermute | solution.py:552
  36.5 39.8 %collective-permute-start.10 = (bf16[256,2048]{1,0:T(8,128)(2,1)}, bf16[256,2048]{1,0:T(8,128)(2,1)}, u32[]{:S(2)}, u32[]{:S(2)}) collective-permute-start(bf16[256,2048]{1,0:T(8,128)(2,1)} %get-tuple-element.107.refs_3_), channel_id=1, source_target_pairs={{0,4},{2,6},{4,0},{6,2},{8,12},{10,14},{12,8},{14,10},{16,20},{18,... | collective-permute-start | bytes 3145736 | tf_op jit(solution)/shard_map/ppermute | solution.py:491
  37.1 39.2 %collective-permute-start.7 = (bf16[256,2048]{1,0:T(8,128)(2,1)}, bf16[256,2048]{1,0:T(8,128)(2,1)}, u32[]{:S(2)}, u32[]{:S(2)}) collective-permute-start(bf16[256,2048]{1,0:T(8,128)(2,1)} %get-tuple-element.107.refs_3_), channel_id=1, source_target_pairs={{0,2},{2,0},{4,6},{6,4},{8,10},{10,8},{12,14},{14,12},{16,18},{18,... | collective-permute-start | bytes 3145736 | tf_op jit(solution)/shard_map/ppermute | solution.py:491
  44.6 29.0 %collective-permute-start.9 = (bf16[144,2048]{1,0:T(8,128)(2,1)}, bf16[144,2048]{1,0:T(8,128)(2,1)}, u32[]{:S(2)}, u32[]{:S(2)}) collective-permute-start(bf16[144,2048]{1,0:T(8,128)(2,1)} %get-tuple-element.110.mine_ref), channel_id=1, source_target_pairs={{0,4},{2,6},{4,0},{6,2},{8,12},{10,14},{12,8},{14,10},{16,20},{18,... | collective-permute-start | bytes 1769480 | tf_op jit(solution)/shard_map/ppermute | solution.py:491
  76.3 8.6 %copy-start.1 = (f32[32]{0:T(128)S(1)}, f32[32]{0:T(128)}, u32[]{:S(2)}) copy-start(f32[32]{0:T(128)} %param.13) | copy-start | bytes 388
  79.3 28.3 %collective-permute-start.13 = (bf16[256,2048]{1,0:T(8,128)(2,1)}, bf16[256,2048]{1,0:T(8,128)(2,1)}, u32[]{:S(2)}, u32[]{:S(2)}) collective-permute-start(bf16[256,2048]{1,0:T(8,128)(2,1)} %add.123.refs_1_.refs_6_), channel_id=1, source_target_pairs={{0,2},{2,0},{4,6},{6,4},{8,10},{10,8},{12,14},{14,12},{16,18},{18,... | collective-permute-start | bytes 3145736 | tf_op jit(solution)/shard_map/ppermute | solution.py:491
  79.8 27.7 %collective-permute-start.12 = (bf16[256,2048]{1,0:T(8,128)(2,1)}, bf16[256,2048]{1,0:T(8,128)(2,1)}, u32[]{:S(2)}, u32[]{:S(2)}) collective-permute-start(bf16[256,2048]{1,0:T(8,128)(2,1)} %add.123.refs_1_.refs_6_), channel_id=1, source_target_pairs={{0,4},{2,6},{4,0},{6,2},{8,12},{10,14},{12,8},{14,10},{16,20},{18,... | collective-permute-start | bytes 3145736 | tf_op jit(solution)/shard_map/ppermute | solution.py:491
  80.3 17.8 %collective-permute-start.16 = (bf16[144,2048]{1,0:T(8,128)(2,1)}, bf16[144,2048]{1,0:T(8,128)(2,1)}, u32[]{:S(2)}, u32[]{:S(2)}) collective-permute-start(bf16[144,2048]{1,0:T(8,128)(2,1)} %get-tuple-element.128.mine_ref), channel_id=1, source_target_pairs={{0,8},{2,10},{4,12},{6,14},{8,0},{10,2},{12,4},{14,6},{16,24},{18,... | collective-permute-start | bytes 1769480 | tf_op jit(solution)/shard_map/ppermute | solution.py:491
  83.6 23.9 %collective-permute-start.11 = (bf16[256,1024]{1,0:T(8,128)(2,1)}, bf16[256,1024]{1,0:T(8,128)(2,1)}, u32[]{:S(2)}, u32[]{:S(2)}) collective-permute-start(bf16[256,1024]{1,0:T(8,128)(2,1)} %get-tuple-element.116.refs_0_), channel_id=1, source_target_pairs={{8,0},{10,2},{12,4},{14,6},{16,24},{18,26},{20,28},{22,30},{9,1},{... | collective-permute-start | bytes 1572872 | tf_op jit(solution)/shard_map/ppermute | solution.py:552
  100.8 27.0 %collective-permute-start.17 = (bf16[144,2048]{1,0:T(8,128)(2,1)}, bf16[144,2048]{1,0:T(8,128)(2,1)}, u32[]{:S(2)}, u32[]{:S(2)}) collective-permute-start(bf16[144,2048]{1,0:T(8,128)(2,1)} %get-tuple-element.131.mine_ref), channel_id=1, source_target_pairs={{0,16},{2,18},{4,20},{6,22},{8,24},{10,26},{12,28},{14,30},{16,0},... | collective-permute-start | bytes 1769480 | tf_op jit(solution)/shard_map/ppermute | solution.py:491
  109.8 22.2 %collective-permute-start.18 = (bf16[256,1024]{1,0:T(8,128)(2,1)}, bf16[256,1024]{1,0:T(8,128)(2,1)}, u32[]{:S(2)}, u32[]{:S(2)}) collective-permute-start(bf16[256,1024]{1,0:T(8,128)(2,1)} %add.125.refs_3_.refs_6_), channel_id=1, source_target_pairs={{0,4},{2,6},{4,0},{6,2},{8,12},{10,14},{12,8},{14,10},{16,20},{18,... | collective-permute-start | bytes 1572872 | tf_op jit(solution)/shard_map/ppermute | solution.py:491
  111.3 20.7 %collective-permute-start.15 = (bf16[256,1024]{1,0:T(8,128)(2,1)}, bf16[256,1024]{1,0:T(8,128)(2,1)}, u32[]{:S(2)}, u32[]{:S(2)}) collective-permute-start(bf16[256,1024]{1,0:T(8,128)(2,1)} %add.125.refs_3_.refs_6_), channel_id=1, source_target_pairs={{0,2},{2,0},{4,6},{6,4},{8,10},{10,8},{12,14},{14,12},{16,18},{18,... | collective-permute-start | bytes 1572872 | tf_op jit(solution)/shard_map/ppermute | solution.py:491
  112.8 19.2 %collective-permute-start.20 = (bf16[256,1024]{1,0:T(8,128)(2,1)}, bf16[256,1024]{1,0:T(8,128)(2,1)}, u32[]{:S(2)}, u32[]{:S(2)}) collective-permute-start(bf16[256,1024]{1,0:T(8,128)(2,1)} %get-tuple-element.135), channel_id=1, source_target_pairs={{0,4},{2,6},{4,0},{6,2},{8,12},{10,14},{12,8},{14,10},{16,20},{18,... | collective-permute-start | bytes 1572872 | tf_op jit(solution)/shard_map/ppermute | solution.py:491
  115.6 17.8 %collective-permute-start.19 = (bf16[256,1024]{1,0:T(8,128)(2,1)}, bf16[256,1024]{1,0:T(8,128)(2,1)}, u32[]{:S(2)}, u32[]{:S(2)}) collective-permute-start(bf16[256,1024]{1,0:T(8,128)(2,1)} %get-tuple-element.203), channel_id=1, source_target_pairs={{0,2},{2,0},{4,6},{6,4},{8,10},{10,8},{12,14},{14,12},{16,18},{18,... | collective-permute-start | bytes 1572872 | tf_op jit(solution)/shard_map/ppermute | solution.py:491
  127.8 13.6 %collective-permute-start.14 = (bf16[256,1024]{1,0:T(8,128)(2,1)}, bf16[256,1024]{1,0:T(8,128)(2,1)}, u32[]{:S(2)}, u32[]{:S(2)}) collective-permute-start(bf16[256,1024]{1,0:T(8,128)(2,1)} %get-tuple-element.123), channel_id=1, source_target_pairs={{8,0},{10,2},{12,4},{14,6},{16,24},{18,26},{20,28},{22,30},{9,1},{... | collective-permute-start | bytes 1572872 | tf_op jit(solution)/shard_map/ppermute | solution.py:552
  133.4 8.1 %copy-start = (bf16[256,1024]{1,0:T(8,128)(2,1)S(1)}, bf16[256,1024]{1,0:T(8,128)(2,1)}, u32[]{:S(2)}) copy-start(bf16[256,1024]{1,0:T(8,128)(2,1)} %get-tuple-element.123) | copy-start | bytes 1572868
  133.4 22.7 %collective-permute-start.23 = (bf16[256,1024]{1,0:T(8,128)(2,1)}, bf16[256,1024]{1,0:T(8,128)(2,1)}, u32[]{:S(2)}, u32[]{:S(2)}) collective-permute-start(bf16[256,1024]{1,0:T(8,128)(2,1)} %get-tuple-element.139), channel_id=1, source_target_pairs={{0,2},{2,0},{4,6},{6,4},{8,10},{10,8},{12,14},{14,12},{16,18},{18,... | collective-permute-start | bytes 1572872 | tf_op jit(solution)/shard_map/ppermute | solution.py:491
  134.9 21.2 %collective-permute-start.24 = (bf16[256,1024]{1,0:T(8,128)(2,1)}, bf16[256,1024]{1,0:T(8,128)(2,1)}, u32[]{:S(2)}, u32[]{:S(2)}) collective-permute-start(bf16[256,1024]{1,0:T(8,128)(2,1)} %get-tuple-element.140.refs_4_.refs_8_), channel_id=1, source_target_pairs={{0,4},{2,6},{4,0},{6,2},{8,12},{10,14},{12,8},{14,10},{16,20},{18,... | collective-permute-start | bytes 1572872 | tf_op jit(solution)/shard_map/ppermute | solution.py:491
  144.5 18.0 %collective-permute-start.22 = (bf16[256,1024]{1,0:T(8,128)(2,1)}, bf16[256,1024]{1,0:T(8,128)(2,1)}, u32[]{:S(2)}, u32[]{:S(2)}) collective-permute-start(bf16[256,1024]{1,0:T(8,128)(2,1)} %shard_map.126.refs_3_.refs_7_), channel_id=1, source_target_pairs={{0,4},{2,6},{4,0},{6,2},{8,12},{10,14},{12,8},{14,10},{16,20},{18,... | collective-permute-start | bytes 1572872 | tf_op jit(solution)/shard_map/ppermute | solution.py:491
  146.1 16.5 %collective-permute-start.21 = (bf16[256,1024]{1,0:T(8,128)(2,1)}, bf16[256,1024]{1,0:T(8,128)(2,1)}, u32[]{:S(2)}, u32[]{:S(2)}) collective-permute-start(bf16[256,1024]{1,0:T(8,128)(2,1)} %shard_map.126.refs_3_.refs_7_), channel_id=1, source_target_pairs={{0,2},{2,0},{4,6},{6,4},{8,10},{10,8},{12,14},{14,12},{16,18},{18,... | collective-permute-start | bytes 1572872 | tf_op jit(solution)/shard_map/ppermute | solution.py:491
  162.6 15.2 %collective-permute-start.25 = (bf16[256,1024]{1,0:T(8,128)(2,1)}, bf16[256,1024]{1,0:T(8,128)(2,1)}, u32[]{:S(2)}, u32[]{:S(2)}) collective-permute-start(bf16[256,1024]{1,0:T(8,128)(2,1)} %get-tuple-element.143), channel_id=1, source_target_pairs={{0,2},{2,0},{4,6},{6,4},{8,10},{10,8},{12,14},{14,12},{16,18},{18,... | collective-permute-start | bytes 1572872 | tf_op jit(solution)/shard_map/ppermute | solution.py:491
  163.2 21.9 %collective-permute-start.27 = (bf16[256,1024]{1,0:T(8,128)(2,1)}, bf16[256,1024]{1,0:T(8,128)(2,1)}, u32[]{:S(2)}, u32[]{:S(2)}) collective-permute-start(bf16[256,1024]{1,0:T(8,128)(2,1)} %get-tuple-element.145), channel_id=1, source_target_pairs={{0,2},{2,0},{4,6},{6,4},{8,10},{10,8},{12,14},{14,12},{16,18},{18,... | collective-permute-start | bytes 1572872 | tf_op jit(solution)/shard_map/ppermute | solution.py:491
  164.7 20.4 %collective-permute-start.28 = (bf16[256,1024]{1,0:T(8,128)(2,1)}, bf16[256,1024]{1,0:T(8,128)(2,1)}, u32[]{:S(2)}, u32[]{:S(2)}) collective-permute-start(bf16[256,1024]{1,0:T(8,128)(2,1)} %get-tuple-element.146), channel_id=1, source_target_pairs={{0,4},{2,6},{4,0},{6,2},{8,12},{10,14},{12,8},{14,10},{16,20},{18,... | collective-permute-start | bytes 1572872 | tf_op jit(solution)/shard_map/ppermute | solution.py:491
  165.2 20.4 %collective-permute-start.26 = (bf16[256,1024]{1,0:T(8,128)(2,1)}, bf16[256,1024]{1,0:T(8,128)(2,1)}, u32[]{:S(2)}, u32[]{:S(2)}) collective-permute-start(bf16[256,1024]{1,0:T(8,128)(2,1)} %get-tuple-element.144.refs_4_.refs_9_), channel_id=1, source_target_pairs={{0,4},{2,6},{4,0},{6,2},{8,12},{10,14},{12,8},{14,10},{16,20},{18,... | collective-permute-start | bytes 1572872 | tf_op jit(solution)/shard_map/ppermute | solution.py:491
  185.6 8.2 %collective-permute-start.29 = (bf16[128,1024]{1,0:T(8,128)(2,1)}, bf16[128,1024]{1,0:T(8,128)(2,1)}, u32[]{:S(2)}, u32[]{:S(2)}) collective-permute-start(bf16[128,1024]{1,0:T(8,128)(2,1)} %get-tuple-element.151.mine_ref), channel_id=1, source_target_pairs={{0,2},{2,0},{4,6},{6,4},{8,10},{10,8},{12,14},{14,12},{16,18},{18,... | collective-permute-start | bytes 786440 | tf_op jit(solution)/shard_map/ppermute | solution.py:491
  195.8 10.9 %collective-permute-start.30 = (bf16[128,1024]{1,0:T(8,128)(2,1)}, bf16[128,1024]{1,0:T(8,128)(2,1)}, u32[]{:S(2)}, u32[]{:S(2)}) collective-permute-start(bf16[128,1024]{1,0:T(8,128)(2,1)} %get-tuple-element.160.refs_1_), channel_id=1, source_target_pairs={{0,2},{2,0},{4,6},{6,4},{8,10},{10,8},{12,14},{14,12},{16,18},{18,... | collective-permute-start | bytes 786440 | tf_op jit(solution)/shard_map/ppermute | solution.py:491
  197.3 9.4 %collective-permute-start.31 = (bf16[128,1024]{1,0:T(8,128)(2,1)}, bf16[128,1024]{1,0:T(8,128)(2,1)}, u32[]{:S(2)}, u32[]{:S(2)}) collective-permute-start(bf16[128,1024]{1,0:T(8,128)(2,1)} %get-tuple-element.161.refs_4_), channel_id=1, source_target_pairs={{0,4},{2,6},{4,0},{6,2},{8,12},{10,14},{12,8},{14,10},{16,20},{18,... | collective-permute-start | bytes 786440 | tf_op jit(solution)/shard_map/ppermute | solution.py:491
  209.4 32.6 %collective-permute-start.36 = (bf16[512,2048]{1,0:T(8,128)(2,1)}, bf16[512,2048]{1,0:T(8,128)(2,1)}, u32[]{:S(2)}, u32[]{:S(2)}) collective-permute-start(bf16[512,2048]{1,0:T(8,128)(2,1)} %get-tuple-element.183), channel_id=1, source_target_pairs={{0,1},{1,0},{2,3},{3,2},{4,5},{5,4},{6,7},{7,6},{8,9},{9,8},{10,11... | collective-permute-start | bytes 6291464 | tf_op jit(solution)/shard_map/ppermute | solution.py:491
  209.4 10.6 %collective-permute-start.32 = (bf16[128,1024]{1,0:T(8,128)(2,1)}, bf16[128,1024]{1,0:T(8,128)(2,1)}, u32[]{:S(2)}, u32[]{:S(2)}) collective-permute-start(bf16[128,1024]{1,0:T(8,128)(2,1)} %get-tuple-element.167.refs_1_), channel_id=1, source_target_pairs={{0,4},{2,6},{4,0},{6,2},{8,12},{10,14},{12,8},{14,10},{16,20},{18,... | collective-permute-start | bytes 786440 | tf_op jit(solution)/shard_map/ppermute | solution.py:491
  211.0 9.1 %collective-permute-start.33 = (bf16[128,1024]{1,0:T(8,128)(2,1)}, bf16[128,1024]{1,0:T(8,128)(2,1)}, u32[]{:S(2)}, u32[]{:S(2)}) collective-permute-start(bf16[128,1024]{1,0:T(8,128)(2,1)} %get-tuple-element.169.refs_5_), channel_id=1, source_target_pairs={{0,8},{2,10},{4,12},{6,14},{8,0},{10,2},{12,4},{14,6},{16,24},{18,... | collective-permute-start | bytes 786440 | tf_op jit(solution)/shard_map/ppermute | solution.py:491
  222.9 13.4 %collective-permute-start.34 = (bf16[128,1024]{1,0:T(8,128)(2,1)}, bf16[128,1024]{1,0:T(8,128)(2,1)}, u32[]{:S(2)}, u32[]{:S(2)}) collective-permute-start(bf16[128,1024]{1,0:T(8,128)(2,1)} %get-tuple-element.176.refs_1_), channel_id=1, source_target_pairs={{0,8},{2,10},{4,12},{6,14},{8,0},{10,2},{12,4},{14,6},{16,24},{18,... | collective-permute-start | bytes 786440 | tf_op jit(solution)/shard_map/ppermute | solution.py:491
  224.6 14.7 %collective-permute-start.35 = (bf16[128,1024]{1,0:T(8,128)(2,1)}, bf16[128,1024]{1,0:T(8,128)(2,1)}, u32[]{:S(2)}, u32[]{:S(2)}) collective-permute-start(bf16[128,1024]{1,0:T(8,128)(2,1)} %get-tuple-element.179.refs_5_), channel_id=1, source_target_pairs={{0,16},{2,18},{4,20},{6,22},{8,24},{10,26},{12,28},{14,30},{16,0},... | collective-permute-start | bytes 786440 | tf_op jit(solution)/shard_map/ppermute | solution.py:491
  243.6 23.4 %collective-permute-start.37 = (bf16[512,128]{1,0:T(8,128)(2,1)}, bf16[512,128]{1,0:T(8,128)(2,1)}, u32[]{:S(2)}, u32[]{:S(2)}) collective-permute-start(bf16[512,128]{1,0:T(8,128)(2,1)} %convert_element_type.38), channel_id=1, source_target_pairs={{0,1},{1,0},{2,3},{3,2},{4,5},{5,4},{6,7},{7,6},{8,9},{9,8},{10,11... | collective-permute-start | bytes 393224 | tf_op jit(solution)/shard_map/ppermute | solution.py:491
  243.6 14.7 %collective-permute-start.38 = (bf16[128,1024]{1,0:T(8,128)(2,1)}, bf16[128,1024]{1,0:T(8,128)(2,1)}, u32[]{:S(2)}, u32[]{:S(2)}) collective-permute-start(bf16[128,1024]{1,0:T(8,128)(2,1)} %get-tuple-element.190.mine_ref), channel_id=1, source_target_pairs={{0,16},{2,18},{4,20},{6,22},{8,24},{10,26},{12,28},{14,30},{16,0},... | collective-permute-start | bytes 786440 | tf_op jit(solution)/shard_map/ppermute | solution.py:491
  266.9 1.9 collective-permute-start.39

commit v14 on v12

--- a/solution.py
+++ b/solution.py
@@ -972,7 +972,9 @@
         late_features, part, late_a, running_t, b_rows, kept, 0
     )
 
-    own_y_b, x2b, y3_b, x1_b, grad_x = after([own_y_b, x2b, y3_b, x1_b, grad_x], y2b, sent_a)
+    own_y_b, x2b, y3_b, x1_b, grad_x, x_a = after(
+        [own_y_b, x2b, y3_b, x1_b, grad_x, x_a], y2b, sent_a
+    )
     d0b, d2b = swap_x(own_y_b), swap_y(x2b)
     d3b, d1b = swap_x(y3_b), swap_y(x1_b)
     product = multiply_blocks(early_order, grad_x, [[piece] for piece in early], ())
@@ -980,7 +982,9 @@
     here = groups // 2
     grid = (spans, here)
 
-    d0b, d2b, sent_a = after([d0b, d2b, sent_a], d3b, d1b, product[0])
+    inner_a = shared + (x_a, b_rows, c_rows, leaving_all)
+    decay_a, grad_b, grad_c = inner(grid, 0, half, inner_a, ())
+    d0b, d2b, sent_a = after([d0b, d2b, sent_a], d3b, d1b, product[0], grad_b)
     entering_a, sent_a = scan_step(factors_1, 0, sent_a, (), 1)
     late_b = [d0b, d1b, d3b, z2b, x2b, y2b, d2b]
     x_b, states_b, sent_b = late_forward(
@@ -993,15 +997,13 @@
     )
     away, own = multiply_blocks(late_order, grad_x, pairs, product)
 
-    sent_a, sent_b, x_a, away = after([sent_a, sent_b, x_a, away])
+    sent_a, sent_b, away = after([sent_a, sent_b, away])
     entering_b, sent_b, entering_a, sent_a = scan_pair(
         (factors_2, here, sent_b, (entering_b,), 2), (factors_4, 0, sent_a, (entering_a,), 4)
     )
     got = swap(away, "head", 1)
-    inner_a = shared + (x_a, b_rows, c_rows, leaving_all)
-    decay_a, grad_b, grad_c = inner(grid, 0, half, inner_a, ())
-
-    sent_a, sent_b, x_b, grad_b = after([sent_a, sent_b, x_b, grad_b])
+
+    sent_a, sent_b, x_b = after([sent_a, sent_b, x_b])
     entering_b, sent_b, entering_a = scan_pair(
         (factors_4, here, sent_b, (entering_b,), 4),
         (factors_8, 0, sent_a, (entering_a,), 8),

time: 265 us -> 275 us (1.038)
  waiting for transfers between devices: 57.1 us -> 64.7 us
    ppermute x35, waiting for transfers between devices: 48.7 us -> 56.7 us  [swap(): return lax.ppermute(value, axis, [(i, i ^ bit) for i in range(count)])]
  transfers between devices with their start and end apart: 40 -> 40, of which waited for: 14 -> 13; matrix products, arithmetic and copies ran while one was open for 12% -> 11% of each run, Pallas kernels for 44% -> 43%
where the time goes in v14:
time: 275 us; the launch traced here: 273 us
  Pallas kernels  122 us (44%)
  waiting for transfers between devices  64.7 us (24%)
  starting transfers between devices  44.6 us (16%)
  other arithmetic  22 us (8%)
  local copies, waits for them, and re-layouts  16.1 us (6%)
  between operations  3.49 us (1%)
    ppermute x35, waiting for transfers between devices, swap(): return lax.ppermute(value, axis, [(i, i ^ bit) for i in range(count)])  56.7 us
    ppermute x35, starting transfers between devices, swap(): return lax.ppermute(value, axis, [(i, i ^ bit) for i in range(count)])  37.3 us
    pallas_call x2, Pallas kernels, multiply_blocks(): pl.pallas_call(functools.partial(blocks_kernel, [len(piece) for piece in...  18.9 us
    pallas_call x2, Pallas kernels, inner(): call(inner_kernel, grid, specs + [SHARED] * len(so_far), [run_spec(), SHA...  17.8 us
    pallas_call x2, Pallas kernels, late_forward(): call(functools.partial(late_forward_kernel, len(pieces)), (columns // WID...  13 us
    pallas_call x2, Pallas kernels, state_terms(): pl.pallas_call(state_kernel, grid=grid, in_specs=[run_t_spec(here), rows_...  11 us
    pallas_call x4, Pallas kernels, back_step(): call(functools.partial(back_kernel, bit), (columns // (2 * WIDE),), [SCAL...  10.5 us
    pallas_call x1, Pallas kernels, grad_rows(): call(functools.partial(grad_x_kernel, transposed), (length // SPAN, runni...  10.4 us
  transfers between devices with their start and end apart: 40, of which 13 were waited for; matrix products, arithmetic and copies ran while one was open for 11% of the time, Pallas kernels for 43%

profile of v14, /device:TPU:0, one launch (start us, length us, event | category | flops | bytes accessed | tf_op | source)
XLA Modules:
  0.0 272.9 jit_solution(3271773357771202842)
XLA Ops:
  1.1 2.7 collective-permute-start
  3.8 1.7 collective-permute-start.1
  5.5 1.5 collective-permute-start.2
  7.0 1.5 collective-permute-start.3
  8.5 9.1 %shard_map.111 = (f32[32,512]{1,0:T(8,128)}, f32[4,512,8]{2,1,0:T(8,128)}, f32[2,8,2048]{2,1,0:T(8,128)}, f32[2,128,2048]{2,1,0:T(8,128)}) custom-call(f32[32,512]{1,0:T(8,128)} %d_ref.1, bf16[512,2048]{1,0:T(8,128)(2,1)} %g_ref.11, bf16[512,128]{1,0:T(8,128)(2,1)} %c_ref.11), custom_call_target="tpu_custom_call" | custom-call | flops 268435456 | bytes 6291456 | tf_op jit(solution)/shard_map/pallas_call | solution.py:823
  17.6 3.6 %shard_map.112 = (f32[8,2048]{1,0:T(8,128)}, bf16[144,2048]{1,0:T(8,128)(2,1)}) custom-call(f32[2,128,2048]{2,1,0:T(8,128)} %get-tuple-element.102.own_ref, f32[2,8,2048]{2,1,0:T(8,128)} %get-tuple-element.103.kept_ref.a_ref), custom_call_target="tpu_custom_call" | custom-call | bytes 3670016 | tf_op jit(solution)/shard_map/pallas_call | solution.py:732
  21.7 6.1 %collective-permute-done.refs_0_ = bf16[256,2048]{1,0:T(8,128)(2,1)} collective-permute-done((bf16[256,2048]{1,0:T(8,128)(2,1)}, bf16[256,2048]{1,0:T(8,128)(2,1)}, u32[]{:S(2)}, u32[]{:S(2)}) %collective-permute-start) | collective-permute-done | bytes 1048608 | tf_op jit(solution)/shard_map/ppermute | solution.py:476
  27.9 3.1 %collective-permute-done.2.refs_2_ = bf16[256,2048]{1,0:T(8,128)(2,1)} collective-permute-done((bf16[256,2048]{1,0:T(8,128)(2,1)}, bf16[256,2048]{1,0:T(8,128)(2,1)}, u32[]{:S(2)}, u32[]{:S(2)}) %collective-permute-start.2) | collective-permute-done | bytes 1048608 | tf_op jit(solution)/shard_map/ppermute | solution.py:476
  31.0 2.3 collective-permute-done.3.refs_3_.refs_1_
  33.3 1.6 collective-permute-start.5
  36.3 1.6 collective-permute-start.7
  42.9 3.1 %collective-permute-done.8.got_ref = bf16[144,2048]{1,0:T(8,128)(2,1)} collective-permute-done((bf16[144,2048]{1,0:T(8,128)(2,1)}, bf16[144,2048]{1,0:T(8,128)(2,1)}, u32[]{:S(2)}, u32[]{:S(2)}) %collective-permute-start.8) | collective-permute-done | bytes 589856 | tf_op jit(solution)/shard_map/ppermute | solution.py:476
  46.0 2.4 shard_map.115
  50.1 5.1 %shard_map.117 = (bf16[512,2304]{1,0:T(8,128)(2,1)}, bf16[512,1792]{1,0:T(8,128)(2,1)}) custom-call(s32[16]{0:T(128)} %get-tuple-element.215.order_ref, bf16[512,2048]{1,0:T(8,128)(2,1)} %own_ref.1, bf16[512,2048]{1,0:T(8,128)(2,1)} %collective-permute-done.4.refs_1_.other_ref), custom_call_target="tpu_custom_call" | custom-call | bytes 8388608 | tf_op jit(solution)/shard_map/pallas_call | solution.py:926
  55.2 2.3 fusion.6
  57.5 2.2 fusion.7
  59.7 13.7 %collective-permute-done.9.got_ref = bf16[144,2048]{1,0:T(8,128)(2,1)} collective-permute-done((bf16[144,2048]{1,0:T(8,128)(2,1)}, bf16[144,2048]{1,0:T(8,128)(2,1)}, u32[]{:S(2)}, u32[]{:S(2)}) %collective-permute-start.9) | collective-permute-done | bytes 589856 | tf_op jit(solution)/shard_map/ppermute | solution.py:476
  73.5 2.7 shard_map.116
  76.2 3.0 %add.123.refs_6_ = bf16[256,2048]{1,0:T(8,128)(2,1)} add(bf16[256,2048]{1,0:T(8,128)(2,1)} %get-tuple-element.117, bf16[256,2048]{1,0:T(8,128)(2,1)} %get-tuple-element.118) | non-fusion elementwise | flops 524288 | bytes 3145728 | tf_op jit(solution)/shard_map/add | solution.py:940
  80.4 4.5 %collective-permute-start.16 = (bf16[144,2048]{1,0:T(8,128)(2,1)S(1)}, bf16[144,2048]{1,0:T(8,128)(2,1)S(1)}, u32[]{:S(2)}, u32[]{:S(2)}) collective-permute-start(bf16[144,2048]{1,0:T(8,128)(2,1)S(1)} %copy-done.1), channel_id=1, source_target_pairs={{0,8},{2,10},{4,12},{6,14},{8,0},{10,2},{12,4},{14,6},{16,24},{18,... | collective-permute-start | bytes 1769480 | tf_op jit(solution)/shard_map/ppermute | solution.py:476
  86.1 2.3 fusion.5
  88.4 11.7 %collective-permute-done.16.got_ref = bf16[144,2048]{1,0:T(8,128)(2,1)S(1)} collective-permute-done((bf16[144,2048]{1,0:T(8,128)(2,1)S(1)}, bf16[144,2048]{1,0:T(8,128)(2,1)S(1)}, u32[]{:S(2)}, u32[]{:S(2)}) %collective-permute-start.16) | collective-permute-done | bytes 589856 | tf_op jit(solution)/shard_map/ppermute | solution.py:476
  100.9 2.7 shard_map.120
  104.0 6.1 %collective-permute-done.11.refs_2_ = bf16[256,1024]{1,0:T(8,128)(2,1)} collective-permute-done((bf16[256,1024]{1,0:T(8,128)(2,1)}, bf16[256,1024]{1,0:T(8,128)(2,1)}, u32[]{:S(2)}, u32[]{:S(2)}) %collective-permute-start.11) | collective-permute-done | bytes 524320 | tf_op jit(solution)/shard_map/ppermute | solution.py:537
  110.1 2.2 add.125.refs_3_.refs_6_
  112.3 1.5 collective-permute-start.15
  113.8 1.5 collective-permute-start.18
  115.3 2.4 fusion.4
  120.1 10.2 %shard_map.122.refs_6_.part_ref = f32[512,2048]{1,0:T(8,128)} custom-call(bf16[512,2304]{1,0:T(8,128)(2,1)} %get-tuple-element.113.refs_9_.f_ref, bf16[256,2048]{1,0:T(8,128)(2,1)} %refs_0_.3, bf16[256,2048]{1,0:T(8,128)(2,1)} %collective-permute-done.3.refs_3_.refs_1_, bf16[256,2048]{1,0:T(8,128)(2,1)} %get-tuple-element.112.refs_2_, ...), custom_call_target="tpu_custom_call" | custom-call | flops 4831838208 | bytes 9437184 | tf_op jit(solution)/shard_map/pallas_call | solution.py:651
  130.3 1.5 collective-permute-start.14
  131.8 2.7 shard_map.121
  134.6 1.6 collective-permute-start.22
  136.1 1.5 collective-permute-start.23
  137.7 2.1 fusion.1
  139.8 2.0 collective-permute-done.14
  141.7 2.1 add.124.refs_0_
  144.9 1.5 collective-permute-start.21
  146.3 1.5 collective-permute-start.24
  149.3 10.4 %shard_map.125.refs_4_ = bf16[2048,512]{1,0:T(8,128)(2,1)} custom-call(f32[32,512]{1,0:T(8,128)} %get-tuple-element.135.r_ref, f32[4,512,8]{2,1,0:T(8,128)} %get-tuple-element.136.rt_ref, bf16[512,2048]{1,0:T(8,128)(2,1)} %g_ref.11, bf16[512,128]{1,0:T(8,128)(2,1)} %b_ref.9, bf16[512,128]{1,0:T(8,128)(2,1)} %c_ref.11, ...), custom_call_target="tpu_custom_call" | custom-call | flops 2147483648 | bytes 6291456 | tf_op jit(solution)/shard_map/pallas_call | solution.py:1033
  159.6 6.5 %shard_map.126 = (bf16[512,1024]{1,0:T(8,128)(2,1)}, f32[2,128,1024]{2,1,0:T(8,128)}, bf16[128,1024]{1,0:T(8,128)(2,1)}) custom-call(bf16[512,1792]{1,0:T(8,128)(2,1)} %get-tuple-element.137.f_ref, f32[512,2048]{1,0:T(8,128)} %shard_map.122.refs_6_.part_ref, f32[4,512,8]{2,1,0:T(8,128)} %get-tuple-element.136.rt_ref, bf16[512,128]{1,0:T(8,128)(2,1)} %b_ref.9, ...), custom_call_target="tpu_custom_call" | custom-call | flops 1879048192 | bytes 3670016 | tf_op jit(solution)/shard_map/pallas_call | solution.py:671
  167.3 1.5 collective-permute-start.27
  168.8 1.5 collective-permute-start.28
  170.3 8.8 %shard_map.129 = (f32[16,512]{1,0:T(8,128)}, f32[512,128]{1,0:T(8,128)}, f32[512,128]{1,0:T(8,128)}) custom-call(f32[32,512]{1,0:T(8,128)} %get-tuple-element.135.r_ref, f32[4,512,8]{2,1,0:T(8,128)} %get-tuple-element.136.rt_ref, bf16[512,2048]{1,0:T(8,128)(2,1)} %g_ref.11, bf16[512,1024]{1,0:T(8,128)(2,1)} %get-tuple-element.148.x_ref, ...), custom_call_target="tpu_custom_call" | custom-call | flops 1610612736 | bytes 3145728 | tf_op jit(solution)/shard_map/pallas_call | solution.py:851
  179.1 10.0 %shard_map.128 = (bf16[512,2048]{1,0:T(8,128)(2,1)}, bf16[512,2048]{1,0:T(8,128)(2,1)}) custom-call(s32[9]{0:T(128)} %bitcast.34, bf16[2048,512]{1,0:T(8,128)(2,1)} %get-tuple-element.142.g_ref, bf16[256,2048]{1,0:T(8,128)(2,1)} %refs_0_.3, bf16[256,2048]{1,0:T(8,128)(2,1)} %collective-permute-done.3.refs_3_.refs_1_, ...), custom_call_target="tpu_custom_call" | custom-call | flops 4831838208 | bytes 9437184 | tf_op jit(solution)/shard_map/pallas_call | solution.py:705
  191.0 6.5 %shard_map.132 = (bf16[512,1024]{1,0:T(8,128)(2,1)}, f32[2,128,1024]{2,1,0:T(8,128)}, bf16[128,1024]{1,0:T(8,128)(2,1)}) custom-call(bf16[512,1792]{1,0:T(8,128)(2,1)} %get-tuple-element.137.f_ref, f32[512,2048]{1,0:T(8,128)} %shard_map.122.refs_6_.part_ref, f32[4,512,8]{2,1,0:T(8,128)} %get-tuple-element.136.rt_ref, bf16[512,128]{1,0:T(8,128)(2,1)} %b_ref.9, ...), custom_call_target="tpu_custom_call" | custom-call | flops 1879048192 | bytes 3670016 | tf_op jit(solution)/shard_map/pallas_call | solution.py:671
  197.5 2.0 shard_map.131
  199.6 1.5 collective-permute-start.30
  201.6 8.9 %shard_map.134 = (bf16[512,2048]{1,0:T(8,128)(2,1)}, bf16[512,2048]{1,0:T(8,128)(2,1)}) custom-call(s32[7]{0:T(128)} %slice.68.order_ref, bf16[2048,512]{1,0:T(8,128)(2,1)} %get-tuple-element.142.g_ref, bf16[256,1024]{1,0:T(8,128)(2,1)} %collective-permute-done.22.refs_0_, ...), custom_call_target="tpu_custom_call", output_to_operand_aliasing={{0}: (16, {}), {1}: (17, {})} | custom-call | flops 3758096384 | bytes 7340032 | tf_op jit(solution)/shard_map/pallas_call | solution.py:705
  210.6 2.6 shard_map.135
  213.2 1.6 collective-permute-start.32
  214.8 7.5 %collective-permute-done.32.refs_2_ = bf16[128,1024]{1,0:T(8,128)(2,1)} collective-permute-done((bf16[128,1024]{1,0:T(8,128)(2,1)}, bf16[128,1024]{1,0:T(8,128)(2,1)}, u32[]{:S(2)}, u32[]{:S(2)}) %collective-permute-start.32) | collective-permute-done | bytes 262176 | tf_op jit(solution)/shard_map/ppermute | solution.py:476
  223.5 2.8 %shard_map.137 = (f32[128,1024]{1,0:T(8,128)}, bf16[128,1024]{1,0:T(8,128)(2,1)}, f32[128,1024]{1,0:T(8,128)}, bf16[128,1024]{1,0:T(8,128)(2,1)}) custom-call(f32[8,2048]{1,0:T(8,128)} %get-tuple-element.161.refs_3_.refs_0_, bf16[128,1024]{1,0:T(8,128)(2,1)} %get-tuple-element.168.refs_1_, bf16[128,1024]{1,0:T(8,128)(2,1)} %collective-permute-done.32.refs_2_, ...), custom_call_target="tpu_custom_call" | custom-call | bytes 2621440 | tf_op jit(solution)/shard_map/pallas_call | solution.py:798
  226.6 2.7 collective-permute-start.35
  229.3 9.0 %shard_map.140 = (f32[16,512]{1,0:T(8,128)}, f32[512,128]{1,0:T(8,128)}, f32[512,128]{1,0:T(8,128)}) custom-call(f32[32,512]{1,0:T(8,128)} %get-tuple-element.135.r_ref, f32[4,512,8]{2,1,0:T(8,128)} %get-tuple-element.136.rt_ref, bf16[512,2048]{1,0:T(8,128)(2,1)} %g_ref.11, bf16[512,1024]{1,0:T(8,128)(2,1)} %get-tuple-element.183.x_ref, ...), custom_call_target="tpu_custom_call" | custom-call | flops 1610612736 | bytes 3145728 | tf_op jit(solution)/shard_map/pallas_call | solution.py:851
  239.6 1.4 collective-permute-done.35.refs_6_
  241.0 2.7 shard_map.139
  243.7 1.6 convert_element_type.38
  245.7 4.4 %add_convert_fusion.refs_1_ = bf16[512,2048]{1,0:T(8,128)(2,1)} fusion(bf16[512,2048]{1,0:T(8,128)(2,1)} %get-tuple-element.186, bf16[512,2048]{1,0:T(8,128)(2,1)} %get-tuple-element.159), kind=kLoop, calls=%fused_computation | loop fusion | flops 4194304 | bytes 6291456 | tf_op jit(solution)/shard_map/convert_element_type | solution.py:1017
  250.2 5.5 %shard_map.143 = (f32[32,512]{1,0:T(8,128)}, f32[512,128]{1,0:T(8,128)}) custom-call(f32[4,512,8]{2,1,0:T(8,128)} %get-tuple-element.136.rt_ref, bf16[512,2048]{1,0:T(8,128)(2,1)} %g_ref.11, bf16[512,128]{1,0:T(8,128)(2,1)} %c_ref.11, f32[128,1024]{1,0:T(8,128)} %get-tuple-element.190.s_ref, f32[2,128,1024]{2,1,0:T(8,128)} %get-tuple-element.191.e_ref, ...), custom_call_target="tpu_custom_call" | custom-call | flops 268435456 | bytes 3145728 | tf_op jit(solution)/shard_map/pallas_call | solution.py:869
  255.7 5.1 %collective-permute-done.38.got_ref = bf16[128,1024]{1,0:T(8,128)(2,1)} collective-permute-done((bf16[128,1024]{1,0:T(8,128)(2,1)}, bf16[128,1024]{1,0:T(8,128)(2,1)}, u32[]{:S(2)}, u32[]{:S(2)}) %collective-permute-start.38) | collective-permute-done | bytes 262176 | tf_op jit(solution)/shard_map/ppermute | solution.py:476
  260.8 2.1 shard_map.142.refs_0_
  262.8 5.5 %shard_map.145 = (f32[32,512]{1,0:T(8,128)}, f32[512,128]{1,0:T(8,128)}) custom-call(f32[4,512,8]{2,1,0:T(8,128)} %get-tuple-element.136.rt_ref, bf16[512,2048]{1,0:T(8,128)(2,1)} %g_ref.11, bf16[512,128]{1,0:T(8,128)(2,1)} %c_ref.11, f32[128,1024]{1,0:T(8,128)} %shard_map.144.s_ref, ...), custom_call_target="tpu_custom_call", output_to_operand_aliasing={{0}: (9, {})} | custom-call | flops 268435456 | bytes 3145728 | tf_op jit(solution)/shard_map/pallas_call | solution.py:869
  269.5 1.7 convert_add_fusion.1
  271.2 1.7 convert_add_fusion
  (79 shorter events, 23.0 us)
Async XLA Ops:
  0.6 20.5 %collective-permute-start.4 = (bf16[512,2048]{1,0:T(8,128)(2,1)}, bf16[512,2048]{1,0:T(8,128)(2,1)}, u32[]{:S(2)}, u32[]{:S(2)}) collective-permute-start(bf16[512,2048]{1,0:T(8,128)(2,1)} %own_ref.1), channel_id=1, source_target_pairs={{0,1},{1,0},{2,3},{3,2},{4,5},{5,4},{6,7},{7,6},{8,9},{9,8},{10,11... | collective-permute-start | bytes 6291464 | tf_op jit(solution)/shard_map/ppermute | solution.py:476
  1.1 26.7 %collective-permute-start = (bf16[256,2048]{1,0:T(8,128)(2,1)}, bf16[256,2048]{1,0:T(8,128)(2,1)}, u32[]{:S(2)}, u32[]{:S(2)}) collective-permute-start(bf16[256,2048]{1,0:T(8,128)(2,1)} %refs_0_.3), channel_id=1, source_target_pairs={{0,8},{2,10},{4,12},{6,14},{8,0},{10,2},{12,4},{14,6},{16,24},{18,... | collective-permute-start | bytes 3145736 | tf_op jit(solution)/shard_map/ppermute | solution.py:476
  3.8 24.1 %collective-permute-start.1 = (bf16[256,2048]{1,0:T(8,128)(2,1)}, bf16[256,2048]{1,0:T(8,128)(2,1)}, u32[]{:S(2)}, u32[]{:S(2)}) collective-permute-start(bf16[256,2048]{1,0:T(8,128)(2,1)} %refs_0_.3), channel_id=1, source_target_pairs={{8,16},{10,18},{12,20},{14,22},{16,8},{18,10},{20,12},{22,14},{9,1... | collective-permute-start | bytes 3145736 | tf_op jit(solution)/shard_map/ppermute | solution.py:537
  5.5 25.5 %collective-permute-start.2 = (bf16[256,2048]{1,0:T(8,128)(2,1)}, bf16[256,2048]{1,0:T(8,128)(2,1)}, u32[]{:S(2)}, u32[]{:S(2)}) collective-permute-start(bf16[256,2048]{1,0:T(8,128)(2,1)} %refs_0_.3), channel_id=1, source_target_pairs={{0,4},{2,6},{4,0},{6,2},{8,12},{10,14},{12,8},{14,10},{16,20},{18,... | collective-permute-start | bytes 3145736 | tf_op jit(solution)/shard_map/ppermute | solution.py:476
  7.0 26.4 %collective-permute-start.3 = (bf16[256,2048]{1,0:T(8,128)(2,1)}, bf16[256,2048]{1,0:T(8,128)(2,1)}, u32[]{:S(2)}, u32[]{:S(2)}) collective-permute-start(bf16[256,2048]{1,0:T(8,128)(2,1)} %refs_0_.3), channel_id=1, source_target_pairs={{0,2},{2,0},{4,6},{6,4},{8,10},{10,8},{12,14},{14,12},{16,18},{18,... | collective-permute-start | bytes 3145736 | tf_op jit(solution)/shard_map/ppermute | solution.py:476
  21.1 24.8 %collective-permute-start.8 = (bf16[144,2048]{1,0:T(8,128)(2,1)}, bf16[144,2048]{1,0:T(8,128)(2,1)}, u32[]{:S(2)}, u32[]{:S(2)}) collective-permute-start(bf16[144,2048]{1,0:T(8,128)(2,1)} %shard_map.113.refs_4_.mine_ref), channel_id=1, source_target_pairs={{0,2},{2,0},{4,6},{6,4},{8,10},{10,8},{12,14},{14,12},{16,18},{18,... | collective-permute-start | bytes 1769480 | tf_op jit(solution)/shard_map/ppermute | solution.py:476
  33.3 24.2 %collective-permute-start.5 = (bf16[256,2048]{1,0:T(8,128)(2,1)}, bf16[256,2048]{1,0:T(8,128)(2,1)}, u32[]{:S(2)}, u32[]{:S(2)}) collective-permute-start(bf16[256,2048]{1,0:T(8,128)(2,1)} %get-tuple-element.106.refs_3_), channel_id=1, source_target_pairs={{8,16},{10,18},{12,20},{14,22},{16,8},{18,10},{20,12},{22,14},{9,1... | collective-permute-start | bytes 3145736 | tf_op jit(solution)/shard_map/ppermute | solution.py:537
  35.0 41.2 %collective-permute-start.6 = (bf16[256,2048]{1,0:T(8,128)(2,1)}, bf16[256,2048]{1,0:T(8,128)(2,1)}, u32[]{:S(2)}, u32[]{:S(2)}) collective-permute-start(bf16[256,2048]{1,0:T(8,128)(2,1)} %get-tuple-element.105.refs_0_), channel_id=1, source_target_pairs={{8,0},{10,2},{12,4},{14,6},{16,24},{18,26},{20,28},{22,30},{9,1},{... | collective-permute-start | bytes 3145736 | tf_op jit(solution)/shard_map/ppermute | solution.py:537
  36.3 39.9 %collective-permute-start.7 = (bf16[256,2048]{1,0:T(8,128)(2,1)}, bf16[256,2048]{1,0:T(8,128)(2,1)}, u32[]{:S(2)}, u32[]{:S(2)}) collective-permute-start(bf16[256,2048]{1,0:T(8,128)(2,1)} %get-tuple-element.106.refs_3_), channel_id=1, source_target_pairs={{0,2},{2,0},{4,6},{6,4},{8,10},{10,8},{12,14},{14,12},{16,18},{18,... | collective-permute-start | bytes 3145736 | tf_op jit(solution)/shard_map/ppermute | solution.py:476
  37.8 38.4 %collective-permute-start.10 = (bf16[256,2048]{1,0:T(8,128)(2,1)}, bf16[256,2048]{1,0:T(8,128)(2,1)}, u32[]{:S(2)}, u32[]{:S(2)}) collective-permute-start(bf16[256,2048]{1,0:T(8,128)(2,1)} %get-tuple-element.106.refs_3_), channel_id=1, source_target_pairs={{0,4},{2,6},{4,0},{6,2},{8,12},{10,14},{12,8},{14,10},{16,20},{18,... | collective-permute-start | bytes 3145736 | tf_op jit(solution)/shard_map/ppermute | solution.py:476
  48.4 25.1 %collective-permute-start.9 = (bf16[144,2048]{1,0:T(8,128)(2,1)}, bf16[144,2048]{1,0:T(8,128)(2,1)}, u32[]{:S(2)}, u32[]{:S(2)}) collective-permute-start(bf16[144,2048]{1,0:T(8,128)(2,1)} %get-tuple-element.109.mine_ref), channel_id=1, source_target_pairs={{0,4},{2,6},{4,0},{6,2},{8,12},{10,14},{12,8},{14,10},{16,20},{18,... | collective-permute-start | bytes 1769480 | tf_op jit(solution)/shard_map/ppermute | solution.py:476
  76.2 4.1 %copy-start.1 = (bf16[144,2048]{1,0:T(8,128)(2,1)S(1)}, bf16[144,2048]{1,0:T(8,128)(2,1)}, u32[]{:S(2)}) copy-start(bf16[144,2048]{1,0:T(8,128)(2,1)} %get-tuple-element.125.mine_ref) | copy-start | bytes 1769476
  79.2 30.8 %collective-permute-start.12 = (bf16[256,2048]{1,0:T(8,128)(2,1)}, bf16[256,2048]{1,0:T(8,128)(2,1)}, u32[]{:S(2)}, u32[]{:S(2)}) collective-permute-start(bf16[256,2048]{1,0:T(8,128)(2,1)} %add.123.refs_6_), channel_id=1, source_target_pairs={{0,4},{2,6},{4,0},{6,2},{8,12},{10,14},{12,8},{14,10},{16,20},{18,... | collective-permute-start | bytes 3145736 | tf_op jit(solution)/shard_map/ppermute | solution.py:476
  79.8 30.2 %collective-permute-start.13 = (bf16[256,2048]{1,0:T(8,128)(2,1)}, bf16[256,2048]{1,0:T(8,128)(2,1)}, u32[]{:S(2)}, u32[]{:S(2)}) collective-permute-start(bf16[256,2048]{1,0:T(8,128)(2,1)} %add.123.refs_6_), channel_id=1, source_target_pairs={{0,2},{2,0},{4,6},{6,4},{8,10},{10,8},{12,14},{14,12},{16,18},{18,... | collective-permute-start | bytes 3145736 | tf_op jit(solution)/shard_map/ppermute | solution.py:476
  80.4 19.7 %collective-permute-start.16 = (bf16[144,2048]{1,0:T(8,128)(2,1)S(1)}, bf16[144,2048]{1,0:T(8,128)(2,1)S(1)}, u32[]{:S(2)}, u32[]{:S(2)}) collective-permute-start(bf16[144,2048]{1,0:T(8,128)(2,1)S(1)} %copy-done.1), channel_id=1, source_target_pairs={{0,8},{2,10},{4,12},{6,14},{8,0},{10,2},{12,4},{14,6},{16,24},{18,... | collective-permute-start | bytes 1769480 | tf_op jit(solution)/shard_map/ppermute | solution.py:476
  84.9 25.2 %collective-permute-start.11 = (bf16[256,1024]{1,0:T(8,128)(2,1)}, bf16[256,1024]{1,0:T(8,128)(2,1)}, u32[]{:S(2)}, u32[]{:S(2)}) collective-permute-start(bf16[256,1024]{1,0:T(8,128)(2,1)} %get-tuple-element.115.refs_0_), channel_id=1, source_target_pairs={{8,0},{10,2},{12,4},{14,6},{16,24},{18,26},{20,28},{22,30},{9,1},{... | collective-permute-start | bytes 1572872 | tf_op jit(solution)/shard_map/ppermute | solution.py:537
  100.1 0.8 copy-start.2
  103.6 26.7 %collective-permute-start.17 = (bf16[144,2048]{1,0:T(8,128)(2,1)}, bf16[144,2048]{1,0:T(8,128)(2,1)}, u32[]{:S(2)}, u32[]{:S(2)}) collective-permute-start(bf16[144,2048]{1,0:T(8,128)(2,1)} %get-tuple-element.128.mine_ref), channel_id=1, source_target_pairs={{0,16},{2,18},{4,20},{6,22},{8,24},{10,26},{12,28},{14,30},{16,0},... | collective-permute-start | bytes 1769480 | tf_op jit(solution)/shard_map/ppermute | solution.py:476
  112.3 22.2 %collective-permute-start.15 = (bf16[256,1024]{1,0:T(8,128)(2,1)}, bf16[256,1024]{1,0:T(8,128)(2,1)}, u32[]{:S(2)}, u32[]{:S(2)}) collective-permute-start(bf16[256,1024]{1,0:T(8,128)(2,1)} %add.125.refs_3_.refs_6_), channel_id=1, source_target_pairs={{0,2},{2,0},{4,6},{6,4},{8,10},{10,8},{12,14},{14,12},{16,18},{18,... | collective-permute-start | bytes 1572872 | tf_op jit(solution)/shard_map/ppermute | solution.py:476
  113.8 20.7 %collective-permute-start.18 = (bf16[256,1024]{1,0:T(8,128)(2,1)}, bf16[256,1024]{1,0:T(8,128)(2,1)}, u32[]{:S(2)}, u32[]{:S(2)}) collective-permute-start(bf16[256,1024]{1,0:T(8,128)(2,1)} %add.125.refs_3_.refs_6_), channel_id=1, source_target_pairs={{0,4},{2,6},{4,0},{6,2},{8,12},{10,14},{12,8},{14,10},{16,20},{18,... | collective-permute-start | bytes 1572872 | tf_op jit(solution)/shard_map/ppermute | solution.py:476
  117.7 16.9 %collective-permute-start.19 = (bf16[256,1024]{1,0:T(8,128)(2,1)}, bf16[256,1024]{1,0:T(8,128)(2,1)}, u32[]{:S(2)}, u32[]{:S(2)}) collective-permute-start(bf16[256,1024]{1,0:T(8,128)(2,1)} %get-tuple-element.201), channel_id=1, source_target_pairs={{0,2},{2,0},{4,6},{6,4},{8,10},{10,8},{12,14},{14,12},{16,18},{18,... | collective-permute-start | bytes 1572872 | tf_op jit(solution)/shard_map/ppermute | solution.py:476
  118.2 16.4 %collective-permute-start.20 = (bf16[256,1024]{1,0:T(8,128)(2,1)}, bf16[256,1024]{1,0:T(8,128)(2,1)}, u32[]{:S(2)}, u32[]{:S(2)}) collective-permute-start(bf16[256,1024]{1,0:T(8,128)(2,1)} %get-tuple-element.132), channel_id=1, source_target_pairs={{0,4},{2,6},{4,0},{6,2},{8,12},{10,14},{12,8},{14,10},{16,20},{18,... | collective-permute-start | bytes 1572872 | tf_op jit(solution)/shard_map/ppermute | solution.py:476
  130.3 11.4 %collective-permute-start.14 = (bf16[256,1024]{1,0:T(8,128)(2,1)}, bf16[256,1024]{1,0:T(8,128)(2,1)}, u32[]{:S(2)}, u32[]{:S(2)}) collective-permute-start(bf16[256,1024]{1,0:T(8,128)(2,1)} %get-tuple-element.120), channel_id=1, source_target_pairs={{8,0},{10,2},{12,4},{14,6},{16,24},{18,26},{20,28},{22,30},{9,1},{... | collective-permute-start | bytes 1572872 | tf_op jit(solution)/shard_map/ppermute | solution.py:537
  134.6 7.1 %copy-start = (bf16[256,1024]{1,0:T(8,128)(2,1)S(1)}, bf16[256,1024]{1,0:T(8,128)(2,1)}, u32[]{:S(2)}) copy-start(bf16[256,1024]{1,0:T(8,128)(2,1)} %get-tuple-element.120) | copy-start | bytes 1572868
  134.6 25.0 %collective-permute-start.22 = (bf16[256,1024]{1,0:T(8,128)(2,1)}, bf16[256,1024]{1,0:T(8,128)(2,1)}, u32[]{:S(2)}, u32[]{:S(2)}) collective-permute-start(bf16[256,1024]{1,0:T(8,128)(2,1)} %get-tuple-element.138), channel_id=1, source_target_pairs={{0,2},{2,0},{4,6},{6,4},{8,10},{10,8},{12,14},{14,12},{16,18},{18,... | collective-permute-start | bytes 1572872 | tf_op jit(solution)/shard_map/ppermute | solution.py:476
  136.1 23.5 %collective-permute-start.23 = (bf16[256,1024]{1,0:T(8,128)(2,1)}, bf16[256,1024]{1,0:T(8,128)(2,1)}, u32[]{:S(2)}, u32[]{:S(2)}) collective-permute-start(bf16[256,1024]{1,0:T(8,128)(2,1)} %get-tuple-element.139.refs_4_.refs_8_), channel_id=1, source_target_pairs={{0,4},{2,6},{4,0},{6,2},{8,12},{10,14},{12,8},{14,10},{16,20},{18,... | collective-permute-start | bytes 1572872 | tf_op jit(solution)/shard_map/ppermute | solution.py:476
  144.9 21.3 %collective-permute-start.21 = (bf16[256,1024]{1,0:T(8,128)(2,1)}, bf16[256,1024]{1,0:T(8,128)(2,1)}, u32[]{:S(2)}, u32[]{:S(2)}) collective-permute-start(bf16[256,1024]{1,0:T(8,128)(2,1)} %shard_map.124.refs_3_.refs_7_), channel_id=1, source_target_pairs={{0,2},{2,0},{4,6},{6,4},{8,10},{10,8},{12,14},{14,12},{16,18},{18,... | collective-permute-start | bytes 1572872 | tf_op jit(solution)/shard_map/ppermute | solution.py:476
  146.3 19.8 %collective-permute-start.24 = (bf16[256,1024]{1,0:T(8,128)(2,1)}, bf16[256,1024]{1,0:T(8,128)(2,1)}, u32[]{:S(2)}, u32[]{:S(2)}) collective-permute-start(bf16[256,1024]{1,0:T(8,128)(2,1)} %shard_map.124.refs_3_.refs_7_), channel_id=1, source_target_pairs={{0,4},{2,6},{4,0},{6,2},{8,12},{10,14},{12,8},{14,10},{16,20},{18,... | collective-permute-start | bytes 1572872 | tf_op jit(solution)/shard_map/ppermute | solution.py:476
  166.2 22.9 %collective-permute-start.25 = (bf16[256,1024]{1,0:T(8,128)(2,1)}, bf16[256,1024]{1,0:T(8,128)(2,1)}, u32[]{:S(2)}, u32[]{:S(2)}) collective-permute-start(bf16[256,1024]{1,0:T(8,128)(2,1)} %get-tuple-element.143), channel_id=1, source_target_pairs={{0,2},{2,0},{4,6},{6,4},{8,10},{10,8},{12,14},{14,12},{16,18},{18,... | collective-permute-start | bytes 1572872 | tf_op jit(solution)/shard_map/ppermute | solution.py:476
  166.8 22.3 %collective-permute-start.26 = (bf16[256,1024]{1,0:T(8,128)(2,1)}, bf16[256,1024]{1,0:T(8,128)(2,1)}, u32[]{:S(2)}, u32[]{:S(2)}) collective-permute-start(bf16[256,1024]{1,0:T(8,128)(2,1)} %get-tuple-element.144.refs_4_.refs_9_), channel_id=1, source_target_pairs={{0,4},{2,6},{4,0},{6,2},{8,12},{10,14},{12,8},{14,10},{16,20},{18,... | collective-permute-start | bytes 1572872 | tf_op jit(solution)/shard_map/ppermute | solution.py:476
  167.3 21.8 %collective-permute-start.27 = (bf16[256,1024]{1,0:T(8,128)(2,1)}, bf16[256,1024]{1,0:T(8,128)(2,1)}, u32[]{:S(2)}, u32[]{:S(2)}) collective-permute-start(bf16[256,1024]{1,0:T(8,128)(2,1)} %get-tuple-element.145), channel_id=1, source_target_pairs={{0,2},{2,0},{4,6},{6,4},{8,10},{10,8},{12,14},{14,12},{16,18},{18,... | collective-permute-start | bytes 1572872 | tf_op jit(solution)/shard_map/ppermute | solution.py:476
  168.8 20.4 %collective-permute-start.28 = (bf16[256,1024]{1,0:T(8,128)(2,1)}, bf16[256,1024]{1,0:T(8,128)(2,1)}, u32[]{:S(2)}, u32[]{:S(2)}) collective-permute-start(bf16[256,1024]{1,0:T(8,128)(2,1)} %get-tuple-element.146), channel_id=1, source_target_pairs={{0,4},{2,6},{4,0},{6,2},{8,12},{10,14},{12,8},{14,10},{16,20},{18,... | collective-permute-start | bytes 1572872 | tf_op jit(solution)/shard_map/ppermute | solution.py:476
  189.2 8.3 %collective-permute-start.29 = (bf16[128,1024]{1,0:T(8,128)(2,1)}, bf16[128,1024]{1,0:T(8,128)(2,1)}, u32[]{:S(2)}, u32[]{:S(2)}) collective-permute-start(bf16[128,1024]{1,0:T(8,128)(2,1)} %get-tuple-element.153.mine_ref), channel_id=1, source_target_pairs={{0,2},{2,0},{4,6},{6,4},{8,10},{10,8},{12,14},{14,12},{16,18},{18,... | collective-permute-start | bytes 786440 | tf_op jit(solution)/shard_map/ppermute | solution.py:476
  199.6 11.0 %collective-permute-start.30 = (bf16[128,1024]{1,0:T(8,128)(2,1)}, bf16[128,1024]{1,0:T(8,128)(2,1)}, u32[]{:S(2)}, u32[]{:S(2)}) collective-permute-start(bf16[128,1024]{1,0:T(8,128)(2,1)} %get-tuple-element.162.refs_1_), channel_id=1, source_target_pairs={{0,2},{2,0},{4,6},{6,4},{8,10},{10,8},{12,14},{14,12},{16,18},{18,... | collective-permute-start | bytes 786440 | tf_op jit(solution)/shard_map/ppermute | solution.py:476
  201.1 9.5 %collective-permute-start.31 = (bf16[128,1024]{1,0:T(8,128)(2,1)}, bf16[128,1024]{1,0:T(8,128)(2,1)}, u32[]{:S(2)}, u32[]{:S(2)}) collective-permute-start(bf16[128,1024]{1,0:T(8,128)(2,1)} %get-tuple-element.163.refs_4_), channel_id=1, source_target_pairs={{0,4},{2,6},{4,0},{6,2},{8,12},{10,14},{12,8},{14,10},{16,20},{18,... | collective-permute-start | bytes 786440 | tf_op jit(solution)/shard_map/ppermute | solution.py:476
  213.2 30.5 %collective-permute-start.36 = (bf16[512,2048]{1,0:T(8,128)(2,1)}, bf16[512,2048]{1,0:T(8,128)(2,1)}, u32[]{:S(2)}, u32[]{:S(2)}) collective-permute-start(bf16[512,2048]{1,0:T(8,128)(2,1)} %get-tuple-element.182), channel_id=1, source_target_pairs={{0,1},{1,0},{2,3},{3,2},{4,5},{5,4},{6,7},{7,6},{8,9},{9,8},{10,11... | collective-permute-start | bytes 6291464 | tf_op jit(solution)/shard_map/ppermute | solution.py:476
  213.2 9.0 %collective-permute-start.32 = (bf16[128,1024]{1,0:T(8,128)(2,1)}, bf16[128,1024]{1,0:T(8,128)(2,1)}, u32[]{:S(2)}, u32[]{:S(2)}) collective-permute-start(bf16[128,1024]{1,0:T(8,128)(2,1)} %get-tuple-element.168.refs_1_), channel_id=1, source_target_pairs={{0,4},{2,6},{4,0},{6,2},{8,12},{10,14},{12,8},{14,10},{16,20},{18,... | collective-permute-start | bytes 786440 | tf_op jit(solution)/shard_map/ppermute | solution.py:476
  214.8 8.7 %collective-permute-start.33 = (bf16[128,1024]{1,0:T(8,128)(2,1)}, bf16[128,1024]{1,0:T(8,128)(2,1)}, u32[]{:S(2)}, u32[]{:S(2)}) collective-permute-start(bf16[128,1024]{1,0:T(8,128)(2,1)} %get-tuple-element.170.refs_5_), channel_id=1, source_target_pairs={{0,8},{2,10},{4,12},{6,14},{8,0},{10,2},{12,4},{14,6},{16,24},{18,... | collective-permute-start | bytes 786440 | tf_op jit(solution)/shard_map/ppermute | solution.py:476
  226.3 13.3 %collective-permute-start.34 = (bf16[128,1024]{1,0:T(8,128)(2,1)}, bf16[128,1024]{1,0:T(8,128)(2,1)}, u32[]{:S(2)}, u32[]{:S(2)}) collective-permute-start(bf16[128,1024]{1,0:T(8,128)(2,1)} %get-tuple-element.175.refs_1_), channel_id=1, source_target_pairs={{0,8},{2,10},{4,12},{6,14},{8,0},{10,2},{12,4},{14,6},{16,24},{18,... | collective-permute-start | bytes 786440 | tf_op jit(solution)/shard_map/ppermute | solution.py:476
  226.6 14.5 %collective-permute-start.35 = (bf16[128,1024]{1,0:T(8,128)(2,1)}, bf16[128,1024]{1,0:T(8,128)(2,1)}, u32[]{:S(2)}, u32[]{:S(2)}) collective-permute-start(bf16[128,1024]{1,0:T(8,128)(2,1)} %get-tuple-element.178.refs_5_), channel_id=1, source_target_pairs={{0,16},{2,18},{4,20},{6,22},{8,24},{10,26},{12,28},{14,30},{16,0},... | collective-permute-start | bytes 786440 | tf_op jit(solution)/shard_map/ppermute | solution.py:476
  245.4 24.1 %collective-permute-start.37 = (bf16[512,128]{1,0:T(8,128)(2,1)}, bf16[512,128]{1,0:T(8,128)(2,1)}, u32[]{:S(2)}, u32[]{:S(2)}) collective-permute-start(bf16[512,128]{1,0:T(8,128)(2,1)} %convert_element_type.38), channel_id=1, source_target_pairs={{0,1},{1,0},{2,3},{3,2},{4,5},{5,4},{6,7},{7,6},{8,9},{9,8},{10,11... | collective-permute-start | bytes 393224 | tf_op jit(solution)/shard_map/ppermute | solution.py:476
  245.4 15.4 %collective-permute-start.38 = (bf16[128,1024]{1,0:T(8,128)(2,1)}, bf16[128,1024]{1,0:T(8,128)(2,1)}, u32[]{:S(2)}, u32[]{:S(2)}) collective-permute-start(bf16[128,1024]{1,0:T(8,128)(2,1)} %get-tuple-element.188.mine_ref), channel_id=1, source_target_pairs={{0,16},{2,18},{4,20},{6,22},{8,24},{10,26},{12,28},{14,30},{16,0},... | collective-permute-start | bytes 786440 | tf_op jit(solution)/shard_map/ppermute | solution.py:476
  269.3 1.9 collective-permute-start.39
